TPU v7x, 32 devices: a whole 2x2x4 slice. The times are simulated.
32 devices in a mesh: dp: 4 (over z), expert: 8 (over y, x, core).
Axes of the slice: x: 2, y: 2, z: 4, core: 2. Of those that a mesh axis runs over, the one named last changes fastest.
Arguments:
- tokens: bfloat16 [1024, 2048], P('dp'), may hold values from -6 to 6
- expert_ids: int32 [1024, 8], P('dp', 'expert'), may hold values from 0 to 15, as said below
- gates: float32 [1024, 8], P('dp', 'expert'), may hold values from 0.05 to 0.25
- positives: int32 [16], P('dp'), may hold values from 0 to 15, as said below
- gate_up: bfloat16 [32, 2048, 768], P(('dp', 'expert')), may hold values from -0.125 to 0.125
- down: bfloat16 [32, 384, 2048], P(('dp', 'expert')), may hold values from -0.21875 to 0.21875
Outputs:
- layer_out: bfloat16 [1024, 2048], P('dp')
- grad_gate_up: bfloat16 [32, 2048, 768], P(('dp', 'expert'))
- grad_down: bfloat16 [32, 384, 2048], P(('dp', 'expert'))
Inputs may be any that keep to these rules, and one draw needn't show every extreme that they name: `expert_ids`: each row names 8 different experts. In the 256 rows of one index of dp no expert is named more than 32 times in one column, and in each column one expert is named exactly 32 times in the rows of every index of dp. positives[i] != i and positives[positives[i]] = i.
All inputs are finite; a program needn't handle non-finite values.
Results may differ from a plain program's by a relative error of at most 0.015.
Values may be sent and summed in bfloat16 or wider, within the bound.
No kernel may reach another device: no remote copies, remote signals or barrier semaphores. Data moves between devices by JAX's collectives and lax.ppermute only.
A program may use at most 128 MiB of HBM per device.

v0:
```python
import jax
import jax.numpy as jnp
from jax import lax
from jax.sharding import PartitionSpec as P

logit_divisor = 0.05
grad_scale = 256.0
epsilon = 1e-06


def dispatch(outgoing):
    at_owners = lax.all_to_all(outgoing, "dp", split_axis=0, concat_axis=0, tiled=True)
    doubled = jnp.repeat(at_owners, 2, axis=1)
    arrived = lax.all_to_all(doubled, "expert", split_axis=1, concat_axis=1, tiled=True)
    return arrived


def contract_rows(left_side, right_side):
    return lax.dot_general(
        left_side, right_side, (((0,), (0,)), ((), ())), preferred_element_type=jnp.float32
    )


def body(tokens, expert_ids, gates, positives, gate_up, down):
    dp_count = lax.axis_size("dp")
    expert_count = lax.axis_size("expert")
    experts = dp_count * expert_count // 2
    owners = expert_count // 2
    tok_dev, model_width = tokens.shape
    routes = expert_ids.shape[1]
    capacity = 2 * tok_dev // experts
    half_width = down.shape[1]
    seq_dev = positives.shape[0]
    seq_length = tok_dev // seq_dev
    lane_rows = routes * capacity
    slot_count = experts * lane_rows
    labels = jnp.arange(experts, dtype=jnp.int32)
    onehot = (expert_ids[:, :, None] == labels).astype(jnp.int32)
    before = jnp.cumsum(onehot, axis=0) - onehot
    position = jnp.sum(before * onehot, axis=2)
    column = jnp.arange(routes, dtype=jnp.int32)[None, :]
    slot_of = (expert_ids * routes + column) * capacity + position
    spread = tokens[:, None, :].reshape(tok_dev * routes, model_width)
    outgoing = (
        jnp.zeros((slot_count, model_width), jnp.bfloat16).at[slot_of.reshape(-1)].set(spread)
    )
    arrived = dispatch(outgoing.reshape(dp_count, owners, lane_rows, model_width))
    expert_rows = arrived.reshape(-1, model_width)
    weight_in = gate_up[0]
    weight_out = down[0]
    projected = jnp.dot(expert_rows, weight_in, preferred_element_type=jnp.float32)
    gate_part = projected[:, :half_width]
    up_part = projected[:, half_width:]
    sigmoid_gate = jax.nn.sigmoid(gate_part)
    activated = gate_part * sigmoid_gate
    hidden = (activated * up_part).astype(jnp.bfloat16)
    half_out = jnp.dot(hidden, weight_out, preferred_element_type=jnp.float32).astype(jnp.bfloat16)
    returned = lax.all_to_all(
        lax.all_to_all(
            half_out.reshape(dp_count, expert_count, lane_rows, model_width),
            "dp",
            split_axis=0,
            concat_axis=0,
            tiled=True,
        ),
        "expert",
        split_axis=1,
        concat_axis=1,
        tiled=True,
    )
    paired = returned.reshape(dp_count, owners, 2, lane_rows, model_width)
    route_out = (paired[:, :, 0].astype(jnp.float32) + paired[:, :, 1].astype(jnp.float32)).reshape(
        slot_count, model_width
    )
    picked = route_out[slot_of.reshape(-1)].reshape(tok_dev, routes, model_width)
    contrib = jnp.sum(gates[:, :, None] * picked, axis=1)
    summed = lax.psum(contrib.astype(jnp.bfloat16), "expert").astype(jnp.float32)
    layer_out = (tokens.astype(jnp.float32) + summed).astype(jnp.bfloat16)
    last_rows = layer_out[seq_length - 1 :: seq_length]
    gathered = lax.all_gather(last_rows, "dp", axis=0, tiled=True)
    gathered_values = gathered.astype(jnp.float32)
    norms_every_row = jnp.sqrt(jnp.sum(gathered_values * gathered_values, axis=1) + epsilon)
    last_values = last_rows.astype(jnp.float32)
    norms_local_rows = jnp.sqrt(jnp.sum(last_values * last_values, axis=1) + epsilon)
    row_start = lax.axis_index("dp") * seq_dev
    columns_all = jnp.arange(gathered.shape[0], dtype=jnp.int32)
    own_index = row_start + jnp.arange(seq_dev, dtype=jnp.int32)
    target = (columns_all[None, :] == positives[:, None]).astype(jnp.float32)
    unit_all = gathered_values / norms_every_row[:, None]
    unit_own = last_values / norms_local_rows[:, None]
    pairwise_dots = lax.dot_general(
        last_rows, gathered, (((1,), (1,)), ((), ())), preferred_element_type=jnp.float32
    )
    cosine_logits = (
        pairwise_dots / (norms_local_rows[:, None] * norms_every_row[None, :]) / logit_divisor
    )
    keep_mask = columns_all[None, :] != own_index[:, None]
    exp_scores = jnp.where(keep_mask, jnp.exp(cosine_logits), 0.0)
    probabilities = exp_scores / jnp.sum(exp_scores, axis=1, keepdims=True)
    objective_multiplier = grad_scale * (probabilities - target)
    forward_terms = (
        jnp.dot(
            objective_multiplier,
            unit_all,
            precision=lax.Precision.HIGHEST,
            preferred_element_type=jnp.float32,
        )
        / logit_divisor
    )
    reverse_local = (
        lax.dot_general(
            objective_multiplier,
            unit_own,
            (((0,), (0,)), ((), ())),
            precision=lax.Precision.HIGHEST,
            preferred_element_type=jnp.float32,
        )
        / logit_divisor
    )
    reverse_own = lax.psum_scatter(
        reverse_local.astype(jnp.bfloat16), "dp", scatter_dimension=0, tiled=True
    ).astype(jnp.float32)
    slope_wrt_unit_embedding = forward_terms + reverse_own
    projection = jnp.sum(unit_own * slope_wrt_unit_embedding, axis=1, keepdims=True)
    grad_last = (slope_wrt_unit_embedding - unit_own * projection) / norms_local_rows[:, None]
    slot_last = slot_of[seq_length - 1 :: seq_length]
    gates_last = gates[seq_length - 1 :: seq_length]
    route_grad = (gates_last[:, :, None] * grad_last[:, None, :]).astype(jnp.bfloat16)
    backward_out = (
        jnp.zeros((slot_count, model_width), jnp.bfloat16)
        .at[slot_last.reshape(-1)]
        .set(route_grad.reshape(-1, model_width))
    )
    grad_rows = dispatch(backward_out.reshape(dp_count, owners, lane_rows, model_width)).reshape(
        -1, model_width
    )
    grad_hidden = lax.dot_general(
        grad_rows, weight_out, (((1,), (1,)), ((), ())), preferred_element_type=jnp.float32
    )
    grad_down = contract_rows(hidden, grad_rows).astype(jnp.bfloat16)
    gate_slope = sigmoid_gate * (1.0 + gate_part * (1.0 - sigmoid_gate))
    grad_projected = jnp.concatenate(
        [grad_hidden * up_part * gate_slope, grad_hidden * activated], axis=1
    ).astype(jnp.bfloat16)
    grad_gate_up = contract_rows(expert_rows, grad_projected).astype(jnp.bfloat16)
    return (layer_out, grad_gate_up[None], grad_down[None])


def solution(mesh):
    return jax.shard_map(
        body,
        mesh=mesh,
        in_specs=(
            P("dp", None),
            P("dp", "expert"),
            P("dp", "expert"),
            P("dp"),
            P(("dp", "expert"), None, None),
            P(("dp", "expert"), None, None),
        ),
        out_specs=(P("dp", None), P(("dp", "expert"), None, None), P(("dp", "expert"), None, None)),
        check_vma=False,
    )
```

profile of v0, /device:TPU:0, one launch (start us, length us, event | category | flops | bytes accessed | tf_op | source)
XLA Modules:
  0.0 523.0 jit_solution(3511101328871937188)
XLA Ops:
  7.2 0.8 compare_convert_fusion
  8.0 0.6 reduce-window.6
  9.0 0.7 fusion.26
  9.8 0.7 compare_select_fusion.1
  10.5 4.4 scatter_custom_fusion
  14.9 54.5 %all_to_all.30 = bf16[4,4,32,2048]{3,2,1,0:T(8,128)(2,1)S(1)} all-to-all(bf16[4,4,32,2048]{3,2,1,0:T(8,128)(2,1)} %bitcast.60), channel_id=1, replica_groups=mesh['dp'=4,'expert'=8] {'dp'}, dimensions={0} | all-to-all | bytes 4194304 | tf_op jit(solution)/shard_map/all_to_all | solution.py:12
  70.1 52.6 %all_to_all.31 = bf16[4,8,32,2048]{3,2,0,1:T(8,128)(2,1)S(1)} all-to-all(bf16[4,8,32,2048]{3,2,0,1:T(8,128)(2,1)S(1)} %bitcast.57), channel_id=1, replica_groups=mesh['dp'=4,'expert'=8] {'expert'}, dimensions={1} | all-to-all | bytes 8388608 | tf_op jit(solution)/shard_map/all_to_all | solution.py:14
  123.3 3.6 fusion
  127.4 2.0 copy-done.11
  129.4 2.4 convolution_convert_fusion
  131.9 95.3 %all_to_all.32 = bf16[4,8,32,2048]{3,2,1,0:T(8,128)(2,1)S(1)} all-to-all(bf16[4,8,32,2048]{3,2,1,0:T(8,128)(2,1)S(1)} %bitcast.65), channel_id=1, replica_groups=mesh['dp'=4,'expert'=8] {'dp'}, dimensions={0} | all-to-all | bytes 8388608 | tf_op jit(solution)/shard_map/all_to_all | solution.py:59
  227.2 2.3 copy.39
  229.5 4.5 all-to-all-start.3
  234.3 48.9 %all-to-all-done.3 = bf16[4,8,32,2048]{3,2,0,1:T(8,128)(2,1)} async-done(((bf16[4,8,32,2048]{3,2,0,1:T(8,128)(2,1)}), bf16[4,8,32,2048]{3,2,0,1:T(8,128)(2,1)}, u32[]{:S(2)}, u32[]{:S(2)}) %all-to-all-start.3) | async-done | bytes 4194336 | tf_op jit(solution)/shard_map/all_to_all | solution.py:58
  283.1 2.8 fusion.32
  285.9 2.7 convert_add_fusion
  288.6 4.6 gather_fusion
  293.3 1.1 multiply_convert_fusion
  294.6 53.9 %all-reduce.4.cloned.1.call-done = bf16[256,2048]{1,0:T(8,128)(2,1)} async-done(((bf16[256,2048]{1,0:T(8,128)(2,1)}), bf16[256,2048]{1,0:T(8,128)(2,1)}) %all-reduce.4.cloned.1.call-update) | async-done | bytes 1048592 | tf_op jit(solution)/shard_map/psum | solution.py:77
  348.5 1.6 add_convert_fusion
  350.3 13.1 %all-gather = bf16[4,4,2048]{2,1,0:T(4,128)(2,1)S(1)} all-gather(bf16[1,4,2048]{2,1,0:T(4,128)(2,1)S(1)} %bitcast.66), channel_id=1, replica_groups=mesh['dp'=4,'expert'=8] {'dp'}, dimensions={0}, use_global_device_ids=true | all-gather | bytes 81920 | tf_op jit(solution)/shard_map/all_gather | solution.py:80
  363.9 1.0 fusion.4
  365.1 0.6 dynamic-slice
  366.3 31.9 %all-reduce.6.cloned.1.call-done = bf16[16,2048]{1,0:T(8,128)(2,1)} async-done(((bf16[16,2048]{1,0:T(8,128)(2,1)}), bf16[16,2048]{1,0:T(8,128)(2,1)}) %all-reduce.6.cloned.1.call-update) | async-done | bytes 65552
  398.2 1.1 multiply_reduce_fusion
  399.3 1.6 scatter_custom_fusion.1
  400.9 49.6 %all_to_all.33 = bf16[4,4,32,2048]{3,2,1,0:T(8,128)(2,1)S(1)} all-to-all(bf16[4,4,32,2048]{3,2,1,0:T(8,128)(2,1)S(1)} %bitcast.59), channel_id=1, replica_groups=mesh['dp'=4,'expert'=8] {'dp'}, dimensions={0} | all-to-all | bytes 4194304 | tf_op jit(solution)/shard_map/all_to_all | solution.py:12
  451.1 52.5 %all_to_all.34 = bf16[4,8,32,2048]{3,2,0,1:T(8,128)(2,1)S(1)} all-to-all(bf16[4,8,32,2048]{3,2,0,1:T(8,128)(2,1)S(1)} %bitcast.58), channel_id=1, replica_groups=mesh['dp'=4,'expert'=8] {'expert'}, dimensions={1} | all-to-all | bytes 8388608 | tf_op jit(solution)/shard_map/all_to_all | solution.py:14
  504.2 1.3 copy-done.5
  506.0 2.3 multiply_convert_fusion.2
  508.3 3.0 fusion.3
  511.3 4.9 fusion.2
  (58 shorter events, 5.1 us)
Async XLA Ops:
  7.2 116.1 %copy-start = (bf16[1,2048,768]{2,1,0:T(8,128)(2,1)S(1)}, bf16[1,2048,768]{2,1,0:T(8,128)(2,1)}, u32[]{:S(2)}) copy-start(bf16[1,2048,768]{2,1,0:T(8,128)(2,1)} %param.10) | copy-start | bytes 9437188
  123.2 3.6 copy-start.2
  126.9 5.0 copy-start.4
  126.9 2.5 copy-start.11
  129.4 2.4 copy-start.8
  229.5 53.7 %all-to-all-start.3 = ((bf16[4,8,32,2048]{3,2,0,1:T(8,128)(2,1)}), bf16[4,8,32,2048]{3,2,0,1:T(8,128)(2,1)}, u32[]{:S(2)}, u32[]{:S(2)}) async-start(bf16[4,8,32,2048]{3,2,0,1:T(8,128)(2,1)} %copy.39), calls=%async_computation.3 | async-start | bytes 8388608 | tf_op jit(solution)/shard_map/all_to_all | solution.py:58
  234.0 114.4 %all-reduce.4.cloned.1.call-start = ((), (), s32[]{:S(2)}) async-start(), calls=%async_computation.6 | async-start | bytes 2097152 | tf_op jit(solution)/shard_map/psum | solution.py:77
  288.6 4.6 copy-start.10
  293.2 55.2 %copy-start.7 = (bf16[256,2048]{1,0:T(8,128)(2,1)S(1)}, bf16[256,2048]{1,0:T(8,128)(2,1)}, u32[]{:S(2)}) copy-start(bf16[256,2048]{1,0:T(8,128)(2,1)} %param.6) | copy-start | bytes 3145732
  294.4 69.5 %copy-start.13 = (s32[4]{0:T(128)S(1)}, s32[4]{0:T(128)}, u32[]{:S(2)}) copy-start(s32[4]{0:T(128)} %param.9) | copy-start | bytes 52
  294.4 70.6 %copy-start.14 = (u32[32]{0:T(128)S(1)}, u32[32]{0:T(128)}, u32[]{:S(2)}) copy-start(u32[32]{0:T(128)} %constant.44) | copy-start | bytes 388
  294.4 103.7 %all-reduce.6.cloned.1.call-start = ((), (), s32[]{:S(2)}) async-start(), calls=%async_computation.7 | async-start | bytes 131072
  350.1 49.2 %copy-start.6 = (bf16[256,2048]{1,0:T(8,128)(2,1)}, bf16[256,2048]{1,0:T(8,128)(2,1)S(1)}, u32[]{:S(2)}) copy-start(bf16[256,2048]{1,0:T(8,128)(2,1)S(1)} %add_convert_fusion) | copy-start | bytes 3145732
  503.6 1.9 copy-start.5
  503.6 2.4 copy-start.12
  506.0 2.3 copy-start.9
  508.3 3.0 copy-start.3
  511.3 4.9 copy-start.1
Sparse Core Ops, SparseCore 0:
  294.5 53.8 all-reduce.3
  365.1 33.0 all-reduce.5
where the time goes:
time: 524 us; the launch traced here: 523 us
  blocking collectives  318 us (61%)
  waiting for transfers between devices  135 us (26%)
  local copies, waits for them, and re-layouts  21.7 us (4%)
  matrix products  18.6 us (4%)
  between operations  14.9 us (3%)
  other arithmetic  10.7 us (2%)
    all_to_all x2, blocking collectives, dispatch(): lax.all_to_all(doubled, 'expert', split_axis=1, concat_axis=1, tiled=True)  105 us
    all_to_all x2, blocking collectives, dispatch(): lax.all_to_all(outgoing, 'dp', split_axis=0, concat_axis=0, tiled=True)  104 us
    all_to_all x1, blocking collectives, body(): lax.all_to_all(half_out.reshape(dp_count, expert_count, lane_rows, model_...  95.3 us
    psum x1, waiting for transfers between devices, body(): lax.psum(contrib.astype(jnp.bfloat16), 'expert').astype(jnp.float32)  53.9 us
    all_to_all x1, waiting for transfers between devices, body(): lax.all_to_all(lax.all_to_all(half_out.reshape(dp_count, expert_count, la...  48.9 us
    unnamed x3, waiting for transfers between devices  31.9 us
    all_gather x1, blocking collectives, body(): gathered = lax.all_gather(last_rows, 'dp', axis=0, tiled=True)  13.1 us
  transfers between devices with their start and end apart: 3, of which 3 were waited for; matrix products, arithmetic and copies ran while one was open for 0% of the time, Pallas kernels for 0%

commit v1 on v0

v1 whole, which is shorter than its diff:
```python
import jax
import jax.numpy as jnp
from jax import lax
from jax.sharding import PartitionSpec as P

logit_divisor = 0.05
grad_scale = 256.0
epsilon = 1e-06


def contract_rows(left_side, right_side):
    return lax.dot_general(
        left_side, right_side, (((0,), (0,)), ((), ())), preferred_element_type=jnp.float32
    )


def matmul(left_side, right_side):
    return jnp.dot(left_side, right_side, preferred_element_type=jnp.float32)


def gated(rows, weight_in):
    projected = matmul(rows, weight_in)
    half_width = weight_in.shape[1] // 2
    gate_part = projected[:, :half_width]
    up_part = projected[:, half_width:]
    sigmoid_gate = jax.nn.sigmoid(gate_part)
    activated = gate_part * sigmoid_gate
    hidden = (activated * up_part).astype(jnp.bfloat16)
    return gate_part, up_part, sigmoid_gate, activated, hidden


def weighted_rows(rows, weight, pairs):
    total = sum(matmul(gated(rows, w_in)[4], w_out) for w_in, w_out in pairs)
    return (weight[:, None] * total).astype(jnp.bfloat16)


def loss_gradient(last_rows, positives):
    values = last_rows.astype(jnp.float32)
    norms = jnp.sqrt(jnp.sum(values * values, axis=1) + epsilon)
    unit = values / norms[:, None]
    dots = lax.dot_general(
        last_rows, last_rows, (((1,), (1,)), ((), ())), preferred_element_type=jnp.float32
    )
    scores = dots / (norms[:, None] * norms[None, :]) / logit_divisor
    index = jnp.arange(last_rows.shape[0], dtype=jnp.int32)
    exp_scores = jnp.where(index[:, None] != index[None, :], jnp.exp(scores), 0.0)
    probabilities = exp_scores / jnp.sum(exp_scores, axis=1, keepdims=True)
    target = (index[None, :] == positives[:, None]).astype(jnp.float32)
    coefficient = grad_scale * (probabilities - target)
    grad_unit = (
        jnp.dot(
            coefficient + coefficient.T,
            unit,
            precision=lax.Precision.HIGHEST,
            preferred_element_type=jnp.float32,
        )
        / logit_divisor
    )
    projection = jnp.sum(unit * grad_unit, axis=1, keepdims=True)
    return (grad_unit - unit * projection) / norms[:, None]


def body(tokens, expert_ids, gates, positives, gate_up, down):
    dp_count = lax.axis_size("dp")
    expert_count = lax.axis_size("expert")
    chips = expert_count // 2
    tok_dev, width = tokens.shape
    seq_dev = positives.shape[0]
    seq_length = tok_dev // seq_dev
    part_rows = tok_dev // expert_count
    plane = lax.axis_index("dp")
    lane = lax.axis_index("expert")
    chip = lane // 2
    core = lane % 2
    own_expert = plane * chips + chip
    hops = range(1, dp_count)

    def partner(place, step):
        return place ^ step if chips & (chips - 1) == 0 else (place + step) % chips

    def giver(place, step):
        return place ^ step if chips & (chips - 1) == 0 else (place - step) % chips

    def to_chip(value, step):
        pairs = [
            (2 * place + side, 2 * partner(place, step) + side)
            for place in range(chips)
            for side in range(2)
        ]
        return lax.ppermute(value, "expert", pairs)

    def from_chip(value, step):
        pairs = [
            (2 * place + side, 2 * giver(place, step) + side)
            for place in range(chips)
            for side in range(2)
        ]
        return lax.ppermute(value, "expert", pairs)

    def swap_cores(value):
        return lax.ppermute(value, "expert", [(j, j ^ 1) for j in range(expert_count)])

    def up_planes(value, hop):
        return lax.ppermute(value, "dp", [(p, (p + hop) % dp_count) for p in range(dp_count)])

    own_part = lax.dynamic_slice_in_dim(tokens, lane * part_rows, part_rows, 0)
    far_parts = [up_planes(own_part, hop) for hop in hops]

    last_tokens = tokens[seq_length - 1 :: seq_length]
    last_width = width // expert_count
    last_share = lax.dynamic_slice_in_dim(last_tokens, lane * last_width, last_width, 1)
    notes = [
        expert_ids[:, 0].astype(jnp.float32),
        gates[:, 0],
        positives.astype(jnp.float32),
        last_share.astype(jnp.float32).reshape(-1),
    ]
    note_size = sum(note.shape[0] for note in notes)
    notes.append(jnp.zeros((-note_size % 1024,), jnp.float32))
    noted = lax.all_gather(jnp.concatenate(notes), ("dp", "expert"), axis=0, tiled=False)
    noted = noted.reshape(dp_count, expert_count, -1)

    other_in = swap_cores(gate_up[0])
    other_out = swap_cores(down[0])
    pairs = [(gate_up[0], down[0]), (other_in, other_out)]

    far_own = jnp.concatenate(far_parts, axis=0)
    far_rows = jnp.concatenate(
        [far_own] + [from_chip(far_own, step) for step in range(1, chips)], axis=0
    )

    all_ids = noted[:, :, :tok_dev].astype(jnp.int32)
    all_gates = noted[:, :, tok_dev : 2 * tok_dev]
    weight = jnp.sum(jnp.where(all_ids == own_expert, all_gates, 0.0), axis=1)
    all_positives = noted[:, 0, 2 * tok_dev : 2 * tok_dev + seq_dev].astype(jnp.int32).reshape(-1)
    last_all = noted[:, :, 2 * tok_dev + seq_dev : note_size]
    last_all = last_all.reshape(dp_count, expert_count, seq_dev, last_width)
    last_all = last_all.transpose(0, 2, 1, 3).reshape(dp_count * seq_dev, width)

    def part_weight(hop, step):
        source = (plane - hop) % dp_count
        place = partner(chip, step) * 2 + core
        return lax.dynamic_slice(weight, (source, place * part_rows), (1, part_rows))[0]

    last_rows_in = last_all.astype(jnp.bfloat16)
    gate_part, up_part, sigmoid_gate, activated, hidden = gated(last_rows_in, gate_up[0])
    last_weight = weight[:, seq_length - 1 :: seq_length].reshape(-1)
    last_half = matmul(hidden, down[0]).astype(jnp.bfloat16).astype(jnp.float32)
    last_sum = lax.psum(last_weight[:, None] * last_half, ("dp", "expert"))

    def own_rows(step):
        place = partner(chip, step) * 2 + core
        return lax.dynamic_slice_in_dim(tokens, place * part_rows, part_rows, 0)

    near_rows = jnp.concatenate([own_rows(step) for step in range(chips)], axis=0)
    near_weight = jnp.concatenate([part_weight(0, step) for step in range(chips)])
    near_out = weighted_rows(near_rows, near_weight, pairs).reshape(chips, 1, part_rows, width)
    far_weight = jnp.concatenate(
        [part_weight(hop, step) for step in range(chips) for hop in hops]
    )
    far_out = weighted_rows(far_rows, far_weight, pairs)
    far_out = far_out.reshape(chips, dp_count - 1, part_rows, width)

    def over_chips(parts):
        total = parts[0].astype(jnp.float32)
        for step in range(1, chips):
            total = total + to_chip(parts[step], step).astype(jnp.float32)
        return total

    far_sum = over_chips(far_out).astype(jnp.bfloat16)
    near_sum = over_chips(near_out)[0]
    total = near_sum + own_part.astype(jnp.float32)
    for hop in hops:
        total = total + up_planes(far_sum[hop - 1], dp_count - hop).astype(jnp.float32)
    layer_out = lax.all_gather(total.astype(jnp.bfloat16), "expert", axis=0, tiled=True)

    last_out = (last_all + last_sum).astype(jnp.bfloat16)
    grad_last = loss_gradient(last_out, all_positives)
    route_grad = (last_weight[:, None] * grad_last).astype(jnp.bfloat16)
    grad_hidden = lax.dot_general(
        route_grad, down[0], (((1,), (1,)), ((), ())), preferred_element_type=jnp.float32
    )
    grad_down = contract_rows(hidden, route_grad).astype(jnp.bfloat16)
    gate_slope = sigmoid_gate * (1.0 + gate_part * (1.0 - sigmoid_gate))
    grad_projected = jnp.concatenate(
        [grad_hidden * up_part * gate_slope, grad_hidden * activated], axis=1
    ).astype(jnp.bfloat16)
    grad_gate_up = contract_rows(last_rows_in, grad_projected).astype(jnp.bfloat16)
    return (layer_out, grad_gate_up[None], grad_down[None])


def solution(mesh):
    return jax.shard_map(
        body,
        mesh=mesh,
        in_specs=(
            P("dp", None),
            P("dp", "expert"),
            P("dp", "expert"),
            P("dp"),
            P(("dp", "expert"), None, None),
            P(("dp", "expert"), None, None),
        ),
        out_specs=(P("dp", None), P(("dp", "expert"), None, None), P(("dp", "expert"), None, None)),
        check_vma=False,
    )
```

time: 524 us -> 269 us (0.51)
  blocking collectives: 318 us -> 39.3 us
  starting transfers between devices: 4.81 us -> 21.6 us
  waiting for transfers between devices: 135 us -> 146 us
  other arithmetic: 10.7 us -> 3.8 us
  matrix products: 18.6 us -> 25.1 us
    all_to_all x5 -> x0, blocking collectives: 305 us -> none  [the longest x2 105 us: dispatch(): lax.all_to_all(doubled, 'expert', split_axis=1, concat_axis=1, tiled=True)]
    psum x1, waiting for transfers between devices: 53.9 us -> 112 us  [body(): last_sum = lax.psum(last_weight[:, None] * last_half, ('dp', 'expert'))]
    all_to_all x1 -> x0, waiting for transfers between devices: 48.9 us -> none  [body(): lax.all_to_all(lax.all_to_all(half_out.reshape(dp_count, expert_count, la...]
    ppermute x0 -> x17, waiting for transfers between devices: none -> 33.2 us  [the longest x3 15.4 us: from_chip(): return lax.ppermute(value, 'expert', pairs)]
    unnamed x3 -> x2, waiting for transfers between devices: 31.9 us -> 0.03 us
    all_gather x1, blocking collectives: 13.1 us -> 39.3 us  [body(): lax.all_gather(jnp.concatenate(notes), ('dp', 'expert'), axis=0, tiled=Fa...]
    ppermute x0 -> x17, starting transfers between devices: none -> 21.6 us  [the longest x6 9.01 us: up_planes(): lax.ppermute(value, 'dp', [(p, (p + hop) % dp_count) for p in range(dp_co...]
    dot_general x6 -> x13, matrix products: 10.7 us -> 20.6 us  [the longest x10 19.5 us: matmul(): return jnp.dot(left_side, right_side, preferred_element_type=jnp.float32)]
  transfers between devices with their start and end apart: 3 -> 19, of which waited for: 3 -> 8; matrix products, arithmetic and copies ran while one was open for 0% -> 14% of each run, Pallas kernels for 0% -> 0%
where the time goes in v1:
time: 269 us
  waiting for transfers between devices  146 us (54%)
  blocking collectives  39.3 us (15%)
  matrix products  25.1 us (9%)
  starting transfers between devices  21.6 us (8%)
  local copies, waits for them, and re-layouts  17.4 us (6%)
  between operations  15.9 us (6%)
  other arithmetic  3.8 us (1%)
    psum x1, waiting for transfers between devices, body(): last_sum = lax.psum(last_weight[:, None] * last_half, ('dp', 'expert'))  112 us
    all_gather x1, blocking collectives, body(): lax.all_gather(jnp.concatenate(notes), ('dp', 'expert'), axis=0, tiled=Fa...  39.3 us
    dot_general x10, matrix products, matmul(): return jnp.dot(left_side, right_side, preferred_element_type=jnp.float32)  19.5 us
    ppermute x3, waiting for transfers between devices, from_chip(): return lax.ppermute(value, 'expert', pairs)  15.4 us
    ppermute x6, waiting for transfers between devices, to_chip(): return lax.ppermute(value, 'expert', pairs)  9.72 us
    unnamed x38, local copies, waits for them, and re-layouts  9.62 us
    ppermute x6, starting transfers between devices, up_planes(): lax.ppermute(value, 'dp', [(p, (p + hop) % dp_count) for p in range(dp_co...  9.01 us
    ppermute x6, starting transfers between devices, to_chip(): return lax.ppermute(value, 'expert', pairs)  8.5 us
  transfers between devices with their start and end apart: 19, of which 8 were waited for; matrix products, arithmetic and copies ran while one was open for 14% of the time, Pallas kernels for 0%

profile of v1, /device:TPU:0, one launch (start us, length us, event | category | flops | bytes accessed | tf_op | source)
XLA Modules:
  0.0 268.8 jit_solution(5341596506553566317)
XLA Ops:
  8.1 1.2 constant_dynamic-slice_fusion.4
  9.4 3.1 %collective-permute-start.5 = (bf16[32,2048]{1,0:T(8,128)(2,1)S(1)}, bf16[32,2048]{1,0:T(8,128)(2,1)}, u32[]{:S(2)}, u32[]{:S(2)}) collective-permute-start(bf16[32,2048]{1,0:T(8,128)(2,1)S(1)} %get-tuple-element.12), channel_id=1, source_target_pairs={{0,8},{8,16},{16,24},{24,0},{1,9},{9,17},{17,25},{25,1},{2,10},{10... | collective-permute-start | bytes 393224 | tf_op jit(solution)/shard_map/ppermute | solution.py:104
  12.4 2.6 collective-permute-start.6
  15.0 1.3 collective-permute-start.7
  20.2 39.3 %all-gather = f32[65536]{0:T(1024)S(1)} all-gather(f32[2048]{0:T(1024)S(1)} %concatenate.23), channel_id=2, replica_groups=mesh['dp'=4,'expert'=8] {'dp','expert'}, dimensions={0}, use_global_device_ids=true | all-gather | bytes 270336 | tf_op jit(solution)/shard_map/all_gather | solution.py:120
  59.7 2.6 fusion.33
  64.4 1.6 constant_dynamic-update-slice_fusion.2
  66.0 1.6 constant_dynamic-update-slice_fusion.1
  67.7 1.6 constant_dynamic-update-slice_fusion
  69.9 3.5 %collective-permute-start.10 = (bf16[96,2048]{1,0:T(8,128)(2,1)}, bf16[96,2048]{1,0:T(8,128)(2,1)S(1)}, u32[]{:S(2)}, u32[]{:S(2)}) collective-permute-start(bf16[96,2048]{1,0:T(8,128)(2,1)} %get-tuple-element.20), channel_id=1, source_target_pairs={{0,6},{1,7},{2,4},{3,5},{4,2},{5,3},{6,0},{7,1},{8,14},{9,15},{10,... | collective-permute-start | bytes 1179656 | tf_op jit(solution)/shard_map/ppermute | solution.py:98
  73.4 8.0 %collective-permute-done.8 = bf16[96,2048]{1,0:T(8,128)(2,1)S(1)} collective-permute-done((bf16[96,2048]{1,0:T(8,128)(2,1)}, bf16[96,2048]{1,0:T(8,128)(2,1)S(1)}, u32[]{:S(2)}, u32[]{:S(2)}) %collective-permute-start.8) | collective-permute-done | bytes 393248 | tf_op jit(solution)/shard_map/ppermute | solution.py:98
  82.2 7.4 %collective-permute-done.9 = bf16[96,2048]{1,0:T(8,128)(2,1)} collective-permute-done((bf16[96,2048]{1,0:T(8,128)(2,1)}, bf16[96,2048]{1,0:T(8,128)(2,1)}, u32[]{:S(2)}, u32[]{:S(2)}) %collective-permute-start.9) | collective-permute-done | bytes 393248 | tf_op jit(solution)/shard_map/ppermute | solution.py:98
  89.6 1.8 constant_dynamic-update-slice_fusion.4
  92.1 3.7 %fusion.75 = f32[384,768]{1,0:T(8,128)S(1)} fusion(bf16[384,2048]{1,0:T(8,128)(2,1)} %constant_dynamic-update-slice_fusion.3, bf16[1,2048,768]{2,1,0:T(8,128)(2,1)} %param.10), kind=kOutput, calls=%fused_computation.141 | convolution fusion | flops 1207959552 | bytes 5898240 | tf_op jit(solution)/shard_map/dot_general | solution.py:18
  97.3 3.3 %fusion.88 = f32[384,768]{1,0:T(8,128)S(1)} fusion(bf16[384,2048]{1,0:T(8,128)(2,1)S(1)} %copy-done.14, bf16[2048,768]{1,0:T(8,128)(2,1)} %collective-permute-done), kind=kOutput, calls=%fused_computation.153 | convolution fusion | flops 1207959552 | bytes 5898240 | tf_op jit(solution)/shard_map/dot_general | solution.py:18
  100.6 2.5 multiply_convert_fusion
  103.2 1.5 collective-permute-start.13
  104.8 1.7 collective-permute-start.12
  106.8 2.5 fusion.32
  109.3 1.9 fusion.3
  111.9 1.5 collective-permute-start.4
  113.3 1.7 collective-permute-start.3
  116.3 1.7 collective-permute-start.2
  118.0 6.7 %collective-permute-done.12 = bf16[3,32,2048]{2,1,0:T(8,128)(2,1)S(1)} collective-permute-done((bf16[3,32,2048]{2,1,0:T(8,128)(2,1)S(1)}, bf16[3,32,2048]{2,1,0:T(8,128)(2,1)S(1)}, u32[]{:S(2)}, u32[]{:S(2)}) %collective-permute-start.12) | collective-permute-done | bytes 393248 | tf_op jit(solution)/shard_map/ppermute | solution.py:90
  125.7 1.8 collective-permute-done.4
  127.5 2.0 collective-permute-start.14
  130.6 3.6 %collective-permute-done.16 = bf16[32,2048]{1,0:T(8,128)(2,1)S(1)} collective-permute-done((bf16[32,2048]{1,0:T(8,128)(2,1)}, bf16[32,2048]{1,0:T(8,128)(2,1)S(1)}, u32[]{:S(2)}, u32[]{:S(2)}) %collective-permute-start.16) | collective-permute-done | bytes 131104 | tf_op jit(solution)/shard_map/ppermute | solution.py:104
  134.2 4.5 %collective-permute-done.15 = bf16[32,2048]{1,0:T(8,128)(2,1)S(1)} collective-permute-done((bf16[32,2048]{1,0:T(8,128)(2,1)}, bf16[32,2048]{1,0:T(8,128)(2,1)S(1)}, u32[]{:S(2)}, u32[]{:S(2)}) %collective-permute-start.15) | collective-permute-done | bytes 131104 | tf_op jit(solution)/shard_map/ppermute | solution.py:104
  139.6 112.5 %all-reduce.2.cloned.1.call-done = f32[16,2048]{1,0:T(8,128)} async-done(((f32[16,2048]{1,0:T(8,128)}), f32[16,2048]{1,0:T(8,128)}) %all-reduce.2.cloned.1.call-update) | async-done | bytes 131088 | tf_op jit(solution)/shard_map/psum | solution.py:149
  254.1 1.8 fusion.1
  256.4 2.7 %fusion = bf16[1,2048,768]{2,1,0:T(8,128)(2,1)} fusion(f32[16,2048]{1,0:T(8,128)S(1)} %bitcast.124, bf16[16,384]{1,0:T(8,128)(2,1)S(1)} %get-tuple-element.27, bf16[16,384]{1,0:T(8,128)(2,1)S(1)} %get-tuple-element.26), kind=kOutput, calls=%fused_computation.2 | convolution fusion | flops 51986432 | bytes 3301376 | tf_op jit(solution)/shard_map/dot_general | solution.py:12
  259.1 2.3 copy.25
  (92 shorter events, 17.3 us)
Async XLA Ops:
  8.0 244.1 %all-reduce.2.cloned.1.call-start = ((), (), s32[]{:S(2)}) async-start(), calls=%async_computation.1 | async-start | bytes 262144 | tf_op jit(solution)/shard_map/psum | solution.py:149
  9.3 53.0 %copy-start.2 = (bf16[32,2048]{1,0:T(8,128)(2,1)}, bf16[32,2048]{1,0:T(8,128)(2,1)S(1)}, u32[]{:S(2)}) copy-start(bf16[32,2048]{1,0:T(8,128)(2,1)S(1)} %get-tuple-element.12) | copy-start | bytes 393220
  9.3 53.0 %copy-start.6 = (bf16[32,2048]{1,0:T(8,128)(2,1)}, bf16[32,2048]{1,0:T(8,128)(2,1)S(1)}, u32[]{:S(2)}) copy-start(bf16[32,2048]{1,0:T(8,128)(2,1)S(1)} %get-tuple-element.9) | copy-start | bytes 393220
  9.3 53.0 %copy-start.8 = (bf16[32,2048]{1,0:T(8,128)(2,1)}, bf16[32,2048]{1,0:T(8,128)(2,1)S(1)}, u32[]{:S(2)}) copy-start(bf16[32,2048]{1,0:T(8,128)(2,1)S(1)} %get-tuple-element.10) | copy-start | bytes 393220
  9.3 53.0 %copy-start.10 = (bf16[32,2048]{1,0:T(8,128)(2,1)}, bf16[32,2048]{1,0:T(8,128)(2,1)S(1)}, u32[]{:S(2)}) copy-start(bf16[32,2048]{1,0:T(8,128)(2,1)S(1)} %get-tuple-element.11) | copy-start | bytes 393220
  9.4 53.0 %copy-start.12 = (bf16[32,2048]{1,0:T(8,128)(2,1)}, bf16[32,2048]{1,0:T(8,128)(2,1)S(1)}, u32[]{:S(2)}) copy-start(bf16[32,2048]{1,0:T(8,128)(2,1)S(1)} %get-tuple-element.13) | copy-start | bytes 393220
  9.4 55.0 %collective-permute-start.5 = (bf16[32,2048]{1,0:T(8,128)(2,1)S(1)}, bf16[32,2048]{1,0:T(8,128)(2,1)}, u32[]{:S(2)}, u32[]{:S(2)}) collective-permute-start(bf16[32,2048]{1,0:T(8,128)(2,1)S(1)} %get-tuple-element.12), channel_id=1, source_target_pairs={{0,8},{8,16},{16,24},{24,0},{1,9},{9,17},{17,25},{25,1},{2,10},{10... | collective-permute-start | bytes 393224 | tf_op jit(solution)/shard_map/ppermute | solution.py:104
  12.4 53.6 %collective-permute-start.6 = (bf16[32,2048]{1,0:T(8,128)(2,1)S(1)}, bf16[32,2048]{1,0:T(8,128)(2,1)}, u32[]{:S(2)}, u32[]{:S(2)}) collective-permute-start(bf16[32,2048]{1,0:T(8,128)(2,1)S(1)} %get-tuple-element.12), channel_id=1, source_target_pairs={{0,16},{8,24},{16,0},{24,8},{1,17},{9,25},{17,1},{25,9},{2,18},{10... | collective-permute-start | bytes 393224 | tf_op jit(solution)/shard_map/ppermute | solution.py:104
  15.0 52.6 %collective-permute-start.7 = (bf16[32,2048]{1,0:T(8,128)(2,1)S(1)}, bf16[32,2048]{1,0:T(8,128)(2,1)}, u32[]{:S(2)}, u32[]{:S(2)}) collective-permute-start(bf16[32,2048]{1,0:T(8,128)(2,1)S(1)} %get-tuple-element.12), channel_id=1, source_target_pairs={{0,24},{8,0},{16,8},{24,16},{1,25},{9,1},{17,9},{25,17},{2,26},{10... | collective-permute-start | bytes 393224 | tf_op jit(solution)/shard_map/ppermute | solution.py:104
  16.4 84.2 %collective-permute-start.1 = (bf16[384,2048]{1,0:T(8,128)(2,1)}, bf16[384,2048]{1,0:T(8,128)(2,1)}, u32[]{:S(2)}, u32[]{:S(2)}) collective-permute-start(bf16[384,2048]{1,0:T(8,128)(2,1)} %bitcast.120), channel_id=1, source_target_pairs={{0,1},{1,0},{2,3},{3,2},{4,5},{5,4},{6,7},{7,6},{8,9},{9,8},{10,11... | collective-permute-start | bytes 4718600 | tf_op jit(solution)/shard_map/ppermute | solution.py:101
  16.4 80.5 %collective-permute-start = (bf16[2048,768]{1,0:T(8,128)(2,1)}, bf16[2048,768]{1,0:T(8,128)(2,1)}, u32[]{:S(2)}, u32[]{:S(2)}) collective-permute-start(bf16[2048,768]{1,0:T(8,128)(2,1)} %bitcast.121), channel_id=1, source_target_pairs={{0,1},{1,0},{2,3},{3,2},{4,5},{5,4},{6,7},{7,6},{8,9},{9,8},{10,11... | collective-permute-start | bytes 9437192 | tf_op jit(solution)/shard_map/ppermute | solution.py:101
  59.7 2.8 %copy-start.1 = (bf16[1,2048,768]{2,1,0:T(8,128)(2,1)S(1)}, bf16[1,2048,768]{2,1,0:T(8,128)(2,1)}, u32[]{:S(2)}) copy-start(bf16[1,2048,768]{2,1,0:T(8,128)(2,1)} %param.10) | copy-start | bytes 9437188
  63.9 5.4 %copy-start.4 = (f32[16,768]{1,0:T(8,128)}, f32[16,768]{1,0:T(8,128)S(1)}, u32[]{:S(2)}) copy-start(f32[16,768]{1,0:T(8,128)S(1)} %fusion.73) | copy-start | bytes 147460
  69.3 12.1 %collective-permute-start.8 = (bf16[96,2048]{1,0:T(8,128)(2,1)}, bf16[96,2048]{1,0:T(8,128)(2,1)S(1)}, u32[]{:S(2)}, u32[]{:S(2)}) collective-permute-start(bf16[96,2048]{1,0:T(8,128)(2,1)} %get-tuple-element.20), channel_id=1, source_target_pairs={{0,2},{1,3},{2,0},{3,1},{4,6},{5,7},{6,4},{7,5},{8,10},{9,11},{10,... | collective-permute-start | bytes 1179656 | tf_op jit(solution)/shard_map/ppermute | solution.py:98
  69.4 20.2 %collective-permute-start.9 = (bf16[96,2048]{1,0:T(8,128)(2,1)}, bf16[96,2048]{1,0:T(8,128)(2,1)}, u32[]{:S(2)}, u32[]{:S(2)}) collective-permute-start(bf16[96,2048]{1,0:T(8,128)(2,1)} %get-tuple-element.20), channel_id=1, source_target_pairs={{0,4},{1,5},{2,6},{3,7},{4,0},{5,1},{6,2},{7,3},{8,12},{9,13},{10,... | collective-permute-start | bytes 1179656 | tf_op jit(solution)/shard_map/ppermute | solution.py:98
  69.9 21.4 %collective-permute-start.10 = (bf16[96,2048]{1,0:T(8,128)(2,1)}, bf16[96,2048]{1,0:T(8,128)(2,1)S(1)}, u32[]{:S(2)}, u32[]{:S(2)}) collective-permute-start(bf16[96,2048]{1,0:T(8,128)(2,1)} %get-tuple-element.20), channel_id=1, source_target_pairs={{0,6},{1,7},{2,4},{3,5},{4,2},{5,3},{6,0},{7,1},{8,14},{9,15},{10,... | collective-permute-start | bytes 1179656 | tf_op jit(solution)/shard_map/ppermute | solution.py:98
  103.1 3.7 %copy-start.7 = (bf16[32,2048]{1,0:T(8,128)(2,1)S(1)}, bf16[32,2048]{1,0:T(8,128)(2,1)}, u32[]{:S(2)}) copy-start(bf16[32,2048]{1,0:T(8,128)(2,1)} %copy-done.6) | copy-start | bytes 393220
  103.1 3.7 %copy-start.9 = (bf16[32,2048]{1,0:T(8,128)(2,1)S(1)}, bf16[32,2048]{1,0:T(8,128)(2,1)}, u32[]{:S(2)}) copy-start(bf16[32,2048]{1,0:T(8,128)(2,1)} %copy-done.8) | copy-start | bytes 393220
  103.1 3.7 %copy-start.11 = (bf16[32,2048]{1,0:T(8,128)(2,1)S(1)}, bf16[32,2048]{1,0:T(8,128)(2,1)}, u32[]{:S(2)}) copy-start(bf16[32,2048]{1,0:T(8,128)(2,1)} %copy-done.10) | copy-start | bytes 393220
  103.1 3.7 %copy-start.13 = (bf16[32,2048]{1,0:T(8,128)(2,1)S(1)}, bf16[32,2048]{1,0:T(8,128)(2,1)}, u32[]{:S(2)}) copy-start(bf16[32,2048]{1,0:T(8,128)(2,1)} %copy-done.12) | copy-start | bytes 393220
  103.2 13.0 %collective-permute-start.13 = (bf16[3,32,2048]{2,1,0:T(8,128)(2,1)S(1)}, bf16[3,32,2048]{2,1,0:T(8,128)(2,1)S(1)}, u32[]{:S(2)}, u32[]{:S(2)}) collective-permute-start(bf16[3,32,2048]{2,1,0:T(8,128)(2,1)S(1)} %bitcast.129), channel_id=1, source_target_pairs={{0,6},{1,7},{2,4},{3,5},{4,2},{5,3},{6,0},{7,1},{8,14},{9,15},{10,... | collective-permute-start | bytes 1179656 | tf_op jit(solution)/shard_map/ppermute | solution.py:90
  104.8 19.9 %collective-permute-start.12 = (bf16[3,32,2048]{2,1,0:T(8,128)(2,1)S(1)}, bf16[3,32,2048]{2,1,0:T(8,128)(2,1)S(1)}, u32[]{:S(2)}, u32[]{:S(2)}) collective-permute-start(bf16[3,32,2048]{2,1,0:T(8,128)(2,1)S(1)} %bitcast.128), channel_id=1, source_target_pairs={{0,4},{1,5},{2,6},{3,7},{4,0},{5,1},{6,2},{7,3},{8,12},{9,13},{10,... | collective-permute-start | bytes 1179656 | tf_op jit(solution)/shard_map/ppermute | solution.py:90
  106.5 18.2 %collective-permute-start.11 = (bf16[3,32,2048]{2,1,0:T(8,128)(2,1)S(1)}, bf16[3,32,2048]{2,1,0:T(8,128)(2,1)S(1)}, u32[]{:S(2)}, u32[]{:S(2)}) collective-permute-start(bf16[3,32,2048]{2,1,0:T(8,128)(2,1)S(1)} %bitcast.127), channel_id=1, source_target_pairs={{0,2},{1,3},{2,0},{3,1},{4,6},{5,7},{6,4},{7,5},{8,10},{9,11},{10,... | collective-permute-start | bytes 1179656 | tf_op jit(solution)/shard_map/ppermute | solution.py:90
  111.9 15.7 %collective-permute-start.4 = (bf16[1,32,2048]{2,1,0:T(8,128)(2,1)S(1)}, bf16[1,32,2048]{2,1,0:T(8,128)(2,1)S(1)}, u32[]{:S(2)}, u32[]{:S(2)}) collective-permute-start(bf16[1,32,2048]{2,1,0:T(8,128)(2,1)S(1)} %get-tuple-element.15), channel_id=1, source_target_pairs={{0,6},{1,7},{2,4},{3,5},{4,2},{5,3},{6,0},{7,1},{8,14},{9,15},{10,... | collective-permute-start | bytes 393224 | tf_op jit(solution)/shard_map/ppermute | solution.py:90
  113.3 17.3 %collective-permute-start.3 = (bf16[1,32,2048]{2,1,0:T(8,128)(2,1)}, bf16[1,32,2048]{2,1,0:T(8,128)(2,1)S(1)}, u32[]{:S(2)}, u32[]{:S(2)}) collective-permute-start(bf16[1,32,2048]{2,1,0:T(8,128)(2,1)} %get-tuple-element.16), channel_id=1, source_target_pairs={{0,4},{1,5},{2,6},{3,7},{4,0},{5,1},{6,2},{7,3},{8,12},{9,13},{10,... | collective-permute-start | bytes 393224 | tf_op jit(solution)/shard_map/ppermute | solution.py:90
  116.3 14.3 %collective-permute-start.2 = (bf16[1,32,2048]{2,1,0:T(8,128)(2,1)S(1)}, bf16[1,32,2048]{2,1,0:T(8,128)(2,1)S(1)}, u32[]{:S(2)}, u32[]{:S(2)}) collective-permute-start(bf16[1,32,2048]{2,1,0:T(8,128)(2,1)S(1)} %get-tuple-element.14), channel_id=1, source_target_pairs={{0,2},{1,3},{2,0},{3,1},{4,6},{5,7},{6,4},{7,5},{8,10},{9,11},{10,... | collective-permute-start | bytes 393224 | tf_op jit(solution)/shard_map/ppermute | solution.py:90
  124.9 13.7 %copy-start.3 = (bf16[32,2048]{1,0:T(8,128)(2,1)S(1)}, bf16[32,2048]{1,0:T(8,128)(2,1)}, u32[]{:S(2)}) copy-start(bf16[32,2048]{1,0:T(8,128)(2,1)} %copy-done.2) | copy-start | bytes 393220
  125.7 8.5 %collective-permute-start.16 = (bf16[32,2048]{1,0:T(8,128)(2,1)}, bf16[32,2048]{1,0:T(8,128)(2,1)S(1)}, u32[]{:S(2)}, u32[]{:S(2)}) collective-permute-start(bf16[32,2048]{1,0:T(8,128)(2,1)} %get-tuple-element.18), channel_id=1, source_target_pairs={{0,8},{8,16},{16,24},{24,0},{1,9},{9,17},{17,25},{25,1},{2,10},{10... | collective-permute-start | bytes 393224 | tf_op jit(solution)/shard_map/ppermute | solution.py:104
  125.7 12.9 %collective-permute-start.15 = (bf16[32,2048]{1,0:T(8,128)(2,1)}, bf16[32,2048]{1,0:T(8,128)(2,1)S(1)}, u32[]{:S(2)}, u32[]{:S(2)}) collective-permute-start(bf16[32,2048]{1,0:T(8,128)(2,1)} %get-tuple-element.19), channel_id=1, source_target_pairs={{0,16},{8,24},{16,0},{24,8},{1,17},{9,25},{17,1},{25,9},{2,18},{10... | collective-permute-start | bytes 393224 | tf_op jit(solution)/shard_map/ppermute | solution.py:104
  127.5 11.1 %collective-permute-start.14 = (bf16[32,2048]{1,0:T(8,128)(2,1)}, bf16[32,2048]{1,0:T(8,128)(2,1)S(1)}, u32[]{:S(2)}, u32[]{:S(2)}) collective-permute-start(bf16[32,2048]{1,0:T(8,128)(2,1)} %get-tuple-element.17), channel_id=1, source_target_pairs={{0,24},{8,0},{16,8},{24,16},{1,25},{9,1},{17,9},{25,17},{2,26},{10... | collective-permute-start | bytes 393224 | tf_op jit(solution)/shard_map/ppermute | solution.py:104
  130.5 128.6 %all-gather.3.cloned.1.call-start = ((), (), s32[]{:S(2)}) async-start(), calls=%async_computation | async-start | bytes 1179648 | tf_op jit(solution)/shard_map/all_gather | solution.py:175
  253.2 2.7 copy-start.5
  (2 other events, 2.8 us)
Sparse Core Ops, SparseCore 0:
  130.7 121.4 all-reduce.1
Sparse Core Ops, SparseCore 1:
  139.6 21.5 all-gather.2

commit v2 on v1

v2 whole, which is shorter than its diff:
```python
import jax
import jax.numpy as jnp
from jax import lax
from jax.sharding import PartitionSpec as P

logit_divisor = 0.05
grad_scale = 256.0
epsilon = 1e-06


def contract_rows(left_side, right_side):
    return lax.dot_general(
        left_side, right_side, (((0,), (0,)), ((), ())), preferred_element_type=jnp.float32
    )


def matmul(left_side, right_side):
    return jnp.dot(left_side, right_side, preferred_element_type=jnp.float32)


def gated(rows, weight_in):
    projected = matmul(rows, weight_in)
    half_width = weight_in.shape[1] // 2
    gate_part = projected[:, :half_width]
    up_part = projected[:, half_width:]
    sigmoid_gate = jax.nn.sigmoid(gate_part)
    activated = gate_part * sigmoid_gate
    hidden = (activated * up_part).astype(jnp.bfloat16)
    return gate_part, up_part, sigmoid_gate, activated, hidden


def weighted_rows(rows, weight, pairs):
    total = sum(matmul(gated(rows, w_in)[4], w_out) for w_in, w_out in pairs)
    return (weight[:, None] * total).astype(jnp.bfloat16)


def loss_gradient(last_rows, positives):
    values = last_rows.astype(jnp.float32)
    norms = jnp.sqrt(jnp.sum(values * values, axis=1) + epsilon)
    unit = values / norms[:, None]
    dots = lax.dot_general(
        last_rows, last_rows, (((1,), (1,)), ((), ())), preferred_element_type=jnp.float32
    )
    scores = dots / (norms[:, None] * norms[None, :]) / logit_divisor
    index = jnp.arange(last_rows.shape[0], dtype=jnp.int32)
    exp_scores = jnp.where(index[:, None] != index[None, :], jnp.exp(scores), 0.0)
    probabilities = exp_scores / jnp.sum(exp_scores, axis=1, keepdims=True)
    target = (index[None, :] == positives[:, None]).astype(jnp.float32)
    coefficient = grad_scale * (probabilities - target)
    grad_unit = (
        jnp.dot(
            coefficient + coefficient.T,
            unit,
            precision=lax.Precision.HIGHEST,
            preferred_element_type=jnp.float32,
        )
        / logit_divisor
    )
    projection = jnp.sum(unit * grad_unit, axis=1, keepdims=True)
    return (grad_unit - unit * projection) / norms[:, None]


def doublings(count):
    steps = [1 << bit for bit in range((count - 1).bit_length())]
    assert 1 << len(steps) == count
    return steps


def body(tokens, expert_ids, gates, positives, gate_up, down):
    dp_count = lax.axis_size("dp")
    expert_count = lax.axis_size("expert")
    chips = expert_count // 2
    tok_dev, width = tokens.shape
    seq_dev = positives.shape[0]
    seq_length = tok_dev // seq_dev
    part_rows = tok_dev // expert_count
    plane = lax.axis_index("dp")
    lane = lax.axis_index("expert")
    own_expert = plane * chips + lane // 2

    def to_lane(value, step):
        return lax.ppermute(value, "expert", [(j, j ^ step) for j in range(expert_count)])

    def to_plane(value, step):
        return lax.ppermute(value, "dp", [(p, p ^ step) for p in range(dp_count)])

    chip_steps = [2 * step for step in range(1, chips)]
    hop_groups = [range(first, 2 * first) for first in doublings(dp_count)]

    own_part = lax.dynamic_slice_in_dim(tokens, lane * part_rows, part_rows, 0)
    far_parts = [[to_plane(own_part, hop) for hop in group] for group in hop_groups]

    last_tokens = tokens[seq_length - 1 :: seq_length]
    last_width = width // expert_count
    last_share = lax.dynamic_slice_in_dim(last_tokens, lane * last_width, last_width, 1)
    gates_high = gates[:, 0].astype(jnp.bfloat16)
    gates_low = (gates[:, 0] - gates_high.astype(jnp.float32)).astype(jnp.bfloat16)
    notes = [
        expert_ids[:, 0].astype(jnp.bfloat16),
        gates_high,
        gates_low,
        last_share.reshape(-1),
        positives.astype(jnp.bfloat16),
    ]
    note_size = sum(note.shape[0] for note in notes)
    notes.append(jnp.zeros((-note_size % width,), jnp.bfloat16))
    noted = jnp.concatenate(notes).reshape(1, 1, -1)

    def joined(value, other, upper, axis):
        return jnp.where(
            upper,
            jnp.concatenate([other, value], axis=axis),
            jnp.concatenate([value, other], axis=axis),
        )

    for step in doublings(dp_count):
        noted = joined(noted, to_plane(noted, step), plane & step != 0, 0)
    for step in doublings(expert_count):
        noted = joined(noted, to_lane(noted, step), lane & step != 0, 1)

    other_in = to_lane(gate_up[0], 1)
    other_out = to_lane(down[0], 1)
    pairs = [(gate_up[0], down[0]), (other_in, other_out)]

    far_rows = []
    for parts in far_parts:
        own = jnp.concatenate(parts, axis=0)
        far_rows.append(
            jnp.concatenate([own] + [to_lane(own, step) for step in chip_steps], axis=0)
        )

    all_ids = noted[:, :, :tok_dev].astype(jnp.int32)
    all_gates = noted[:, :, tok_dev : 2 * tok_dev].astype(jnp.float32)
    all_gates = all_gates + noted[:, :, 2 * tok_dev : 3 * tok_dev].astype(jnp.float32)
    weight = jnp.sum(jnp.where(all_ids == own_expert, all_gates, 0.0), axis=1)
    last_start = 3 * tok_dev
    last_end = last_start + seq_dev * last_width
    all_positives = noted[:, 0, last_end : last_end + seq_dev].astype(jnp.int32).reshape(-1)
    last_all = noted[:, :, last_start:last_end]
    last_all = last_all.reshape(dp_count, expert_count, seq_dev, last_width)
    last_all = last_all.transpose(0, 2, 1, 3).reshape(dp_count * seq_dev, width)

    def part_weight(hop, step):
        source = plane ^ hop
        start = (lane ^ step) * part_rows
        return lax.dynamic_slice(weight, (source, start), (1, part_rows))[0]

    def group_weight(group):
        return jnp.concatenate(
            [part_weight(hop, step) for step in [0] + chip_steps for hop in group]
        )

    gate_part, up_part, sigmoid_gate, activated, hidden = gated(last_all, gate_up[0])
    last_weight = weight[:, seq_length - 1 :: seq_length].reshape(-1)
    last_half = matmul(hidden, down[0]).astype(jnp.bfloat16).astype(jnp.float32)
    last_sum = last_weight[:, None] * last_half
    for step in doublings(expert_count):
        last_sum = last_sum + to_lane(last_sum, step)
    for step in doublings(dp_count):
        last_sum = last_sum + to_plane(last_sum, step)

    def over_chips(parts):
        total = parts[0].astype(jnp.float32)
        for index, step in enumerate(chip_steps):
            total = total + to_lane(parts[index + 1], step).astype(jnp.float32)
        return total

    near_rows = jnp.concatenate(
        [
            lax.dynamic_slice_in_dim(tokens, (lane ^ step) * part_rows, part_rows, 0)
            for step in [0] + chip_steps
        ],
        axis=0,
    )
    near_out = weighted_rows(near_rows, group_weight([0]), pairs)
    total = over_chips(near_out.reshape(chips, part_rows, width)) + own_part.astype(jnp.float32)
    for group, rows in zip(hop_groups, far_rows):
        out = weighted_rows(rows, group_weight(group), pairs)
        out = over_chips(out.reshape(chips, len(group), part_rows, width)).astype(jnp.bfloat16)
        for index, hop in enumerate(group):
            total = total + to_plane(out[index], hop).astype(jnp.float32)

    own_out = total.astype(jnp.bfloat16)
    layer_out = jnp.zeros((tok_dev, width), jnp.bfloat16)
    pieces = [own_out] + [to_lane(own_out, step) for step in chip_steps]
    stacked = jnp.concatenate(pieces, axis=0)
    mirrored = to_lane(stacked, 1)
    for index, step in enumerate([0] + chip_steps):
        rows = slice(index * part_rows, (index + 1) * part_rows)
        for source, value in ((lane ^ step, stacked[rows]), (lane ^ step ^ 1, mirrored[rows])):
            layer_out = lax.dynamic_update_slice(layer_out, value, (source * part_rows, 0))

    last_out = (last_all.astype(jnp.float32) + last_sum).astype(jnp.bfloat16)
    grad_last = loss_gradient(last_out, all_positives)
    route_grad = (last_weight[:, None] * grad_last).astype(jnp.bfloat16)
    grad_hidden = lax.dot_general(
        route_grad, down[0], (((1,), (1,)), ((), ())), preferred_element_type=jnp.float32
    )
    grad_down = contract_rows(hidden, route_grad).astype(jnp.bfloat16)
    gate_slope = sigmoid_gate * (1.0 + gate_part * (1.0 - sigmoid_gate))
    grad_projected = jnp.concatenate(
        [grad_hidden * up_part * gate_slope, grad_hidden * activated], axis=1
    ).astype(jnp.bfloat16)
    grad_gate_up = contract_rows(last_all, grad_projected).astype(jnp.bfloat16)
    return (layer_out, grad_gate_up[None], grad_down[None])


def solution(mesh):
    return jax.shard_map(
        body,
        mesh=mesh,
        in_specs=(
            P("dp", None),
            P("dp", "expert"),
            P("dp", "expert"),
            P("dp"),
            P(("dp", "expert"), None, None),
            P(("dp", "expert"), None, None),
        ),
        out_specs=(P("dp", None), P(("dp", "expert"), None, None), P(("dp", "expert"), None, None)),
        check_vma=False,
    )
```

time: 269 us -> 139 us (0.52)
  waiting for transfers between devices: 146 us -> 41.3 us
  blocking collectives: 39.3 us -> 0 us
  starting transfers between devices: 21.6 us -> 49.4 us
  between operations: 15.9 us -> 1.17 us
  local copies, waits for them, and re-layouts: 17.4 us -> 11.4 us
  matrix products: 25.1 us -> 29.8 us
    psum x1 -> x0, waiting for transfers between devices: 112 us -> none  [body(): last_sum = lax.psum(last_weight[:, None] * last_half, ('dp', 'expert'))]
    all_gather x1 -> x0, blocking collectives: 39.3 us -> none  [body(): lax.all_gather(jnp.concatenate(notes), ('dp', 'expert'), axis=0, tiled=Fa...]
    ppermute x17 -> x37, starting transfers between devices: 21.6 us -> 49.4 us  [the longest x27 29.7 us: to_lane(): lax.ppermute(value, 'expert', [(j, j ^ step) for j in range(expert_count)])]
    ppermute x17 -> x37, waiting for transfers between devices: 33.2 us -> 41.3 us  [the longest x27 27.7 us: to_lane(): lax.ppermute(value, 'expert', [(j, j ^ step) for j in range(expert_count)])]
    unnamed x38 -> x45, local copies, waits for them, and re-layouts: 9.62 us -> 4.42 us
    dot_general x10 -> x14, matrix products: 19.5 us -> 22.8 us  [matmul(): return jnp.dot(left_side, right_side, preferred_element_type=jnp.float32)]
  transfers between devices with their start and end apart: 19 -> 37, of which waited for: 8 -> 18; matrix products, arithmetic and copies ran while one was open for 14% -> 28% of each run, Pallas kernels for 0% -> 0%
where the time goes in v2:
time: 139 us
  starting transfers between devices  49.4 us (36%)
  waiting for transfers between devices  41.3 us (30%)
  matrix products  29.8 us (21%)
  local copies, waits for them, and re-layouts  11.4 us (8%)
  other arithmetic  5.74 us (4%)
    ppermute x27, starting transfers between devices, to_lane(): lax.ppermute(value, 'expert', [(j, j ^ step) for j in range(expert_count)])  29.7 us
    ppermute x27, waiting for transfers between devices, to_lane(): lax.ppermute(value, 'expert', [(j, j ^ step) for j in range(expert_count)])  27.7 us
    dot_general x14, matrix products, matmul(): return jnp.dot(left_side, right_side, preferred_element_type=jnp.float32)  22.8 us
    ppermute x10, starting transfers between devices, to_plane(): return lax.ppermute(value, 'dp', [(p, p ^ step) for p in range(dp_count)])  19.7 us
    ppermute x10, waiting for transfers between devices, to_plane(): return lax.ppermute(value, 'dp', [(p, p ^ step) for p in range(dp_count)])  13.6 us
    dot_general x2, matrix products, contract_rows(): lax.dot_general(left_side, right_side, (((0,), (0,)), ((), ())), preferre...  4.47 us
    unnamed x45, local copies, waits for them, and re-layouts  4.42 us
  transfers between devices with their start and end apart: 37, of which 18 were waited for; matrix products, arithmetic and copies ran while one was open for 28% of the time, Pallas kernels for 0%

profile of v2, /device:TPU:0, one launch (start us, length us, event | category | flops | bytes accessed | tf_op | source)
XLA Modules:
  0.0 138.7 jit_solution(13533895309957007755)
XLA Ops:
  4.1 3.1 %collective-permute-start = (bf16[1,1,2048]{2,0,1:T(2,128)(2,1)S(1)}, bf16[1,1,2048]{2,0,1:T(2,128)(2,1)S(1)}, u32[]{:S(2)}, u32[]{:S(2)}) collective-permute-start(bf16[1,1,2048]{2,0,1:T(2,128)(2,1)S(1)} %reshape.254), channel_id=1, source_target_pairs={{0,8},{8,0},{16,24},{24,16},{1,9},{9,1},{17,25},{25,17},{2,10},{10... | collective-permute-start | bytes 12296 | tf_op jit(solution)/shard_map/ppermute | solution.py:85
  7.2 1.6 %collective-permute-done = bf16[1,1,2048]{2,0,1:T(2,128)(2,1)S(1)} collective-permute-done((bf16[1,1,2048]{2,0,1:T(2,128)(2,1)S(1)}, bf16[1,1,2048]{2,0,1:T(2,128)(2,1)S(1)}, u32[]{:S(2)}, u32[]{:S(2)}) %collective-permute-start) | collective-permute-done | bytes 4128 | tf_op jit(solution)/shard_map/ppermute | solution.py:85
  8.8 3.1 %collective-permute-start.1 = (bf16[2,1,2048]{2,0,1:T(2,128)(2,1)S(1)}, bf16[2,1,2048]{2,0,1:T(2,128)(2,1)S(1)}, u32[]{:S(2)}, u32[]{:S(2)}) collective-permute-start(bf16[2,1,2048]{2,0,1:T(2,128)(2,1)S(1)} %broadcast_select_fusion.1), channel_id=1, source_target_pairs={{0,16},{8,24},{16,0},{24,8},{1,17},{9,25},{17,1},{25,9},{2,18},{10... | collective-permute-start | bytes 24584 | tf_op jit(solution)/shard_map/ppermute | solution.py:85
  13.7 1.8 %constant_dynamic-slice_fusion.2 = (bf16[32,2048]{1,0:T(8,128)(2,1)S(1)}, bf16[32,2048]{1,0:T(8,128)(2,1)S(1)}, bf16[32,2048]{1,0:T(8,128)(2,1)}, bf16[32,2048]{1,0:T(8,128)(2,1)}) fusion(bf16[256,2048]{1,0:T(8,128)(2,1)} %param.6, s32[]{:T(128)S(6)} %select_n.176, s32[]{:T(128)S(6)} %select_n.175, s32[]{:T(128)S(6)} %select_n.178, s32[]{:T(128)S(6)} %select_n.177), kind=kLoop, calls=%fused_computation.130 | loop fusion | bytes 1048592 | tf_op jit(solution)/shard_map/dynamic_slice | solution.py:170
  15.5 2.9 %collective-permute-start.18 = (bf16[32,2048]{1,0:T(8,128)(2,1)S(1)}, bf16[32,2048]{1,0:T(8,128)(2,1)}, u32[]{:S(2)}, u32[]{:S(2)}) collective-permute-start(bf16[32,2048]{1,0:T(8,128)(2,1)S(1)} %get-tuple-element.10), channel_id=1, source_target_pairs={{0,16},{8,24},{16,0},{24,8},{1,17},{9,25},{17,1},{25,9},{2,18},{10... | collective-permute-start | bytes 393224 | tf_op jit(solution)/shard_map/ppermute | solution.py:85
  21.6 3.5 %fusion.40 = f32[128,768]{1,0:T(8,128)} fusion(bf16[32,2048]{1,0:T(8,128)(2,1)} %get-tuple-element.11, bf16[32,2048]{1,0:T(8,128)(2,1)} %get-tuple-element.12, bf16[32,2048]{1,0:T(8,128)(2,1)S(1)} %get-tuple-element.9, bf16[32,2048]{1,0:T(8,128)(2,1)S(1)} %get-tuple-element.10, bf16[1,2048,768]{2,1,0:T(8,128)(2,1)} %param.10), kind=kOutput, calls=%fused_computation.68 | convolution fusion | flops 404750336 | bytes 4063232 | tf_op jit(solution)/shard_map/dot_general | solution.py:18
  26.7 2.4 %fusion.29 = f32[128,2048]{1,0:T(8,128)} fusion(f32[128,768]{1,0:T(8,128)} %fusion.40, bf16[1,384,2048]{2,1,0:T(8,128)(2,1)S(1)} %copy-done), kind=kOutput, calls=%fused_computation.61 | convolution fusion | flops 201621504 | bytes 3014656 | tf_op jit(solution)/shard_map/dot_general | solution.py:18
  29.8 2.4 %fusion.79 = f32[16,768]{1,0:T(8,128)S(1)} fusion(bf16[16,2048]{1,0:T(8,128)(2,1)S(1)} %bitcast.120, bf16[1,2048,768]{2,1,0:T(8,128)(2,1)} %param.10), kind=kOutput, calls=%fused_computation.165 | convolution fusion | flops 50331648 | bytes 3260416 | tf_op jit(solution)/shard_map/dot_general | solution.py:18
  43.3 6.4 %collective-permute-done.11 = bf16[32,2048]{1,0:T(8,128)(2,1)S(1)} collective-permute-done((bf16[32,2048]{1,0:T(8,128)(2,1)}, bf16[32,2048]{1,0:T(8,128)(2,1)S(1)}, u32[]{:S(2)}, u32[]{:S(2)}) %collective-permute-start.11) | collective-permute-done | bytes 131104 | tf_op jit(solution)/shard_map/ppermute | solution.py:82
  51.3 3.6 %collective-permute-done.12 = bf16[32,2048]{1,0:T(8,128)(2,1)S(1)} collective-permute-done((bf16[32,2048]{1,0:T(8,128)(2,1)}, bf16[32,2048]{1,0:T(8,128)(2,1)S(1)}, u32[]{:S(2)}, u32[]{:S(2)}) %collective-permute-start.12) | collective-permute-done | bytes 131104 | tf_op jit(solution)/shard_map/ppermute | solution.py:82
  56.4 4.6 %collective-permute-done.13 = bf16[32,2048]{1,0:T(8,128)(2,1)S(1)} collective-permute-done((bf16[32,2048]{1,0:T(8,128)(2,1)}, bf16[32,2048]{1,0:T(8,128)(2,1)S(1)}, u32[]{:S(2)}, u32[]{:S(2)}) %collective-permute-start.13) | collective-permute-done | bytes 131104 | tf_op jit(solution)/shard_map/ppermute | solution.py:82
  61.5 2.5 %fusion.83 = f32[128,768]{1,0:T(8,128)S(1)} fusion(bf16[128,2048]{1,0:T(8,128)(2,1)S(1)} %constant_dynamic-update-slice_fusion, bf16[1,2048,768]{2,1,0:T(8,128)(2,1)} %param.10), kind=kOutput, calls=%fused_computation.169 | convolution fusion | flops 402653184 | bytes 4063232 | tf_op jit(solution)/shard_map/dot_general | solution.py:18
  64.5 2.2 %collective-permute-done.33 = f32[16,2048]{1,0:T(8,128)S(1)} collective-permute-done((f32[16,2048]{1,0:T(8,128)S(1)}, f32[16,2048]{1,0:T(8,128)S(1)}, u32[]{:S(2)}, u32[]{:S(2)}) %collective-permute-start.33) | collective-permute-done | bytes 131104 | tf_op jit(solution)/shard_map/ppermute | solution.py:82
  66.7 2.7 %collective-permute-start.22 = (bf16[64,2048]{1,0:T(8,128)(2,1)S(1)}, bf16[64,2048]{1,0:T(8,128)(2,1)S(1)}, u32[]{:S(2)}, u32[]{:S(2)}) collective-permute-start(bf16[64,2048]{1,0:T(8,128)(2,1)S(1)} %get-tuple-element.25), channel_id=1, source_target_pairs={{0,6},{1,7},{2,4},{3,5},{4,2},{5,3},{6,0},{7,1},{8,14},{9,15},{10,... | collective-permute-start | bytes 786440 | tf_op jit(solution)/shard_map/ppermute | solution.py:82
  69.6 4.5 %collective-permute-done.22 = bf16[64,2048]{1,0:T(8,128)(2,1)S(1)} collective-permute-done((bf16[64,2048]{1,0:T(8,128)(2,1)S(1)}, bf16[64,2048]{1,0:T(8,128)(2,1)S(1)}, u32[]{:S(2)}, u32[]{:S(2)}) %collective-permute-start.22) | collective-permute-done | bytes 262176 | tf_op jit(solution)/shard_map/ppermute | solution.py:82
  75.4 1.9 %collective-permute-start.35 = (f32[16,2048]{1,0:T(8,128)S(1)}, f32[16,2048]{1,0:T(8,128)S(1)}, u32[]{:S(2)}, u32[]{:S(2)}) collective-permute-start(f32[16,2048]{1,0:T(8,128)S(1)} %add.224), channel_id=1, source_target_pairs={{0,8},{8,0},{16,24},{24,16},{1,9},{9,1},{17,25},{25,17},{2,10},{10... | collective-permute-start | bytes 393224 | tf_op jit(solution)/shard_map/ppermute | solution.py:85
  78.2 2.2 %collective-permute-done.35 = f32[16,2048]{1,0:T(8,128)S(1)} collective-permute-done((f32[16,2048]{1,0:T(8,128)S(1)}, f32[16,2048]{1,0:T(8,128)S(1)}, u32[]{:S(2)}, u32[]{:S(2)}) %collective-permute-start.35) | collective-permute-done | bytes 131104 | tf_op jit(solution)/shard_map/ppermute | solution.py:85
  80.5 2.9 %collective-permute-start.36 = (f32[16,2048]{1,0:T(8,128)S(1)}, f32[16,2048]{1,0:T(8,128)S(1)}, u32[]{:S(2)}, u32[]{:S(2)}) collective-permute-start(f32[16,2048]{1,0:T(8,128)S(1)} %add.225), channel_id=1, source_target_pairs={{0,16},{8,24},{16,0},{24,8},{1,17},{9,25},{17,1},{25,9},{2,18},{10... | collective-permute-start | bytes 393224 | tf_op jit(solution)/shard_map/ppermute | solution.py:85
  84.0 2.4 %collective-permute-done.36 = f32[16,2048]{1,0:T(8,128)S(1)} collective-permute-done((f32[16,2048]{1,0:T(8,128)S(1)}, f32[16,2048]{1,0:T(8,128)S(1)}, u32[]{:S(2)}, u32[]{:S(2)}) %collective-permute-start.36) | collective-permute-done | bytes 131104 | tf_op jit(solution)/shard_map/ppermute | solution.py:85
  87.3 2.9 %fusion.100 = f32[256,768]{1,0:T(8,128)S(1)} fusion(bf16[256,2048]{1,0:T(8,128)(2,1)S(1)} %constant_dynamic-update-slice_fusion.6, bf16[2048,768]{1,0:T(8,128)(2,1)} %collective-permute-done.5), kind=kOutput, calls=%fused_computation.185 | convolution fusion | flops 805306368 | bytes 4980736 | tf_op jit(solution)/shard_map/dot_general | solution.py:18
  91.1 4.4 %collective-permute-start.25 = (bf16[2,32,2048]{2,1,0:T(8,128)(2,1)S(1)}, bf16[2,32,2048]{2,1,0:T(8,128)(2,1)S(1)}, u32[]{:S(2)}, u32[]{:S(2)}) collective-permute-start(bf16[2,32,2048]{2,1,0:T(8,128)(2,1)S(1)} %bitcast.127), channel_id=1, source_target_pairs={{0,6},{1,7},{2,4},{3,5},{4,2},{5,3},{6,0},{7,1},{8,14},{9,15},{10,... | collective-permute-start | bytes 786440 | tf_op jit(solution)/shard_map/ppermute | solution.py:82
  95.5 2.5 %fusion.99 = f32[128,768]{1,0:T(8,128)S(1)} fusion(bf16[128,2048]{1,0:T(8,128)(2,1)S(1)} %constant_dynamic-update-slice_fusion, bf16[2048,768]{1,0:T(8,128)(2,1)} %collective-permute-done.5), kind=kOutput, calls=%fused_computation.184 | convolution fusion | flops 402653184 | bytes 4063232 | tf_op jit(solution)/shard_map/dot_general | solution.py:18
  98.5 2.2 %collective-permute-start.16 = (bf16[1,32,2048]{2,1,0:T(8,128)(2,1)S(1)}, bf16[1,32,2048]{2,1,0:T(8,128)(2,1)S(1)}, u32[]{:S(2)}, u32[]{:S(2)}) collective-permute-start(bf16[1,32,2048]{2,1,0:T(8,128)(2,1)S(1)} %get-tuple-element.21), channel_id=1, source_target_pairs={{0,6},{1,7},{2,4},{3,5},{4,2},{5,3},{6,0},{7,1},{8,14},{9,15},{10,... | collective-permute-start | bytes 393224 | tf_op jit(solution)/shard_map/ppermute | solution.py:82
  102.1 2.5 %fusion.39 = f32[128,768]{1,0:T(8,128)S(1)} fusion(bf16[2048,768]{1,0:T(8,128)(2,1)} %collective-permute-done.5, bf16[32,2048]{1,0:T(8,128)(2,1)S(1)} %copy-done.10, bf16[32,2048]{1,0:T(8,128)(2,1)S(1)} %copy-done.11, bf16[32,2048]{1,0:T(8,128)(2,1)S(1)} %copy-done.9, bf16[32,2048]{1,0:T(8,128)(2,1)S(1)} %get-tuple-element.10), kind=kOutput, calls=%fused_computation.67 | convolution fusion | flops 404750336 | bytes 4063232 | tf_op jit(solution)/shard_map/dot_general | solution.py:18
  106.7 1.7 %collective-permute-done.15 = bf16[1,32,2048]{2,1,0:T(8,128)(2,1)S(1)} collective-permute-done((bf16[1,32,2048]{2,1,0:T(8,128)(2,1)S(1)}, bf16[1,32,2048]{2,1,0:T(8,128)(2,1)S(1)}, u32[]{:S(2)}, u32[]{:S(2)}) %collective-permute-start.15) | collective-permute-done | bytes 131104 | tf_op jit(solution)/shard_map/ppermute | solution.py:82
  108.4 2.2 %collective-permute-start.9 = (bf16[32,2048]{1,0:T(8,128)(2,1)S(1)}, bf16[32,2048]{1,0:T(8,128)(2,1)S(1)}, u32[]{:S(2)}, u32[]{:S(2)}) collective-permute-start(bf16[32,2048]{1,0:T(8,128)(2,1)S(1)} %get-tuple-element.18), channel_id=1, source_target_pairs={{0,6},{1,7},{2,4},{3,5},{4,2},{5,3},{6,0},{7,1},{8,14},{9,15},{10,... | collective-permute-start | bytes 393224 | tf_op jit(solution)/shard_map/ppermute | solution.py:82
  112.7 3.1 %collective-permute-start.27 = (bf16[32,2048]{1,0:T(8,128)(2,1)S(1)}, bf16[32,2048]{1,0:T(8,128)(2,1)S(1)}, u32[]{:S(2)}, u32[]{:S(2)}) collective-permute-start(bf16[32,2048]{1,0:T(8,128)(2,1)S(1)} %get-tuple-element.24), channel_id=1, source_target_pairs={{0,24},{8,16},{16,8},{24,0},{1,25},{9,17},{17,9},{25,1},{2,26},{10... | collective-permute-start | bytes 393224 | tf_op jit(solution)/shard_map/ppermute | solution.py:85
  117.0 2.8 %collective-permute-done.27 = bf16[32,2048]{1,0:T(8,128)(2,1)S(1)} collective-permute-done((bf16[32,2048]{1,0:T(8,128)(2,1)S(1)}, bf16[32,2048]{1,0:T(8,128)(2,1)S(1)}, u32[]{:S(2)}, u32[]{:S(2)}) %collective-permute-start.27) | collective-permute-done | bytes 131104 | tf_op jit(solution)/shard_map/ppermute | solution.py:85
  120.4 2.9 %collective-permute-done.26 = bf16[32,2048]{1,0:T(8,128)(2,1)} collective-permute-done((bf16[32,2048]{1,0:T(8,128)(2,1)S(1)}, bf16[32,2048]{1,0:T(8,128)(2,1)}, u32[]{:S(2)}, u32[]{:S(2)}) %collective-permute-start.26) | collective-permute-done | bytes 131104 | tf_op jit(solution)/shard_map/ppermute | solution.py:85
  124.7 2.1 %collective-permute-start.30 = (bf16[32,2048]{1,0:T(8,128)(2,1)S(1)}, bf16[32,2048]{1,0:T(8,128)(2,1)S(1)}, u32[]{:S(2)}, u32[]{:S(2)}) collective-permute-start(bf16[32,2048]{1,0:T(8,128)(2,1)S(1)} %get-tuple-element.6), channel_id=1, source_target_pairs={{0,6},{1,7},{2,4},{3,5},{4,2},{5,3},{6,0},{7,1},{8,14},{9,15},{10,... | collective-permute-start | bytes 393224 | tf_op jit(solution)/shard_map/ppermute | solution.py:82
  132.6 1.8 %fusion.3 = bf16[1,384,2048]{2,1,0:T(8,128)(2,1)} fusion(bf16[16,384]{1,0:T(8,128)(2,1)S(1)} %multiply_convert_fusion.3, f32[16,2048]{1,0:T(8,128)S(1)} %get-tuple-element.48, f32[16]{0:T(128)S(1)} %get-tuple-element.47, f32[16]{0:T(128)S(1)} %copy-done.16, f32[16]{0:T(128)S(1)} %mul.211, bf16[16,2048]{1,0:T(8,128)(2,1)S(1)} %get-tuple-element.4), kind=kOutput, calls=%fused_computation.6 | convolution fusion | flops 26181632 | bytes 1781952 | tf_op jit(solution)/shard_map/dot_general | solution.py:12
  134.9 2.7 %fusion = bf16[1,2048,768]{2,1,0:T(8,128)(2,1)} fusion(bf16[16,2048]{1,0:T(8,128)(2,1)S(1)} %bitcast.122, bf16[16,384]{1,0:T(8,128)(2,1)S(1)} %get-tuple-element.30, bf16[16,384]{1,0:T(8,128)(2,1)S(1)} %get-tuple-element.29), kind=kOutput, calls=%fused_computation.1 | convolution fusion | flops 51953664 | bytes 3235840 | tf_op jit(solution)/shard_map/dot_general | solution.py:12
  (161 shorter events, 47.3 us)
Async XLA Ops:
  13.6 6.4 %collective-permute-start.2 = (bf16[4,1,2048]{2,0,1:T(4,128)(2,1)S(1)}, bf16[4,1,2048]{2,0,1:T(4,128)(2,1)S(1)}, u32[]{:S(2)}, u32[]{:S(2)}) collective-permute-start(bf16[4,1,2048]{2,0,1:T(4,128)(2,1)S(1)} %maximum_select_fusion.3), channel_id=1, source_target_pairs={{0,1},{1,0},{2,3},{3,2},{4,5},{5,4},{6,7},{7,6},{8,9},{9,8},{10,11... | collective-permute-start | bytes 49160 | tf_op jit(solution)/shard_map/ppermute | solution.py:82
  15.5 20.7 %collective-permute-start.18 = (bf16[32,2048]{1,0:T(8,128)(2,1)S(1)}, bf16[32,2048]{1,0:T(8,128)(2,1)}, u32[]{:S(2)}, u32[]{:S(2)}) collective-permute-start(bf16[32,2048]{1,0:T(8,128)(2,1)S(1)} %get-tuple-element.10), channel_id=1, source_target_pairs={{0,16},{8,24},{16,0},{24,8},{1,17},{9,25},{17,1},{25,9},{2,18},{10... | collective-permute-start | bytes 393224 | tf_op jit(solution)/shard_map/ppermute | solution.py:85
  18.5 19.3 %collective-permute-start.19 = (bf16[32,2048]{1,0:T(8,128)(2,1)S(1)}, bf16[32,2048]{1,0:T(8,128)(2,1)}, u32[]{:S(2)}, u32[]{:S(2)}) collective-permute-start(bf16[32,2048]{1,0:T(8,128)(2,1)S(1)} %get-tuple-element.10), channel_id=1, source_target_pairs={{0,24},{8,16},{16,8},{24,0},{1,25},{9,17},{17,9},{25,1},{2,26},{10... | collective-permute-start | bytes 393224 | tf_op jit(solution)/shard_map/ppermute | solution.py:85
  19.8 19.4 %collective-permute-start.10 = (bf16[32,2048]{1,0:T(8,128)(2,1)S(1)}, bf16[32,2048]{1,0:T(8,128)(2,1)}, u32[]{:S(2)}, u32[]{:S(2)}) collective-permute-start(bf16[32,2048]{1,0:T(8,128)(2,1)S(1)} %get-tuple-element.10), channel_id=1, source_target_pairs={{0,8},{8,0},{16,24},{24,16},{1,9},{9,1},{17,25},{25,17},{2,10},{10... | collective-permute-start | bytes 393224 | tf_op jit(solution)/shard_map/ppermute | solution.py:85
  20.0 70.1 %collective-permute-start.6 = (bf16[384,2048]{1,0:T(8,128)(2,1)}, bf16[384,2048]{1,0:T(8,128)(2,1)S(1)}, u32[]{:S(2)}, u32[]{:S(2)}) collective-permute-start(bf16[384,2048]{1,0:T(8,128)(2,1)} %bitcast.118), channel_id=1, source_target_pairs={{0,1},{1,0},{2,3},{3,2},{4,5},{5,4},{6,7},{7,6},{8,9},{9,8},{10,11... | collective-permute-start | bytes 4718600 | tf_op jit(solution)/shard_map/ppermute | solution.py:82
  20.1 5.0 %collective-permute-start.3 = (bf16[4,2,2048]{2,0,1:T(4,128)(2,1)S(1)}, bf16[4,2,2048]{2,0,1:T(4,128)(2,1)S(1)}, u32[]{:S(2)}, u32[]{:S(2)}) collective-permute-start(bf16[4,2,2048]{2,0,1:T(4,128)(2,1)S(1)} %maximum_select_fusion.2), channel_id=1, source_target_pairs={{0,2},{1,3},{2,0},{3,1},{4,6},{5,7},{6,4},{7,5},{8,10},{9,11},{10,... | collective-permute-start | bytes 98312 | tf_op jit(solution)/shard_map/ppermute | solution.py:82
  29.5 57.8 %collective-permute-start.5 = (bf16[2048,768]{1,0:T(8,128)(2,1)}, bf16[2048,768]{1,0:T(8,128)(2,1)}, u32[]{:S(2)}, u32[]{:S(2)}) collective-permute-start(bf16[2048,768]{1,0:T(8,128)(2,1)} %bitcast.119), channel_id=1, source_target_pairs={{0,1},{1,0},{2,3},{3,2},{4,5},{5,4},{6,7},{7,6},{8,9},{9,8},{10,11... | collective-permute-start | bytes 9437192 | tf_op jit(solution)/shard_map/ppermute | solution.py:82
  36.3 5.4 %collective-permute-start.32 = (f32[16,2048]{1,0:T(8,128)S(1)}, f32[16,2048]{1,0:T(8,128)S(1)}, u32[]{:S(2)}, u32[]{:S(2)}) collective-permute-start(f32[16,2048]{1,0:T(8,128)S(1)} %fusion.9), channel_id=1, source_target_pairs={{0,1},{1,0},{2,3},{3,2},{4,5},{5,4},{6,7},{7,6},{8,9},{9,8},{10,11... | collective-permute-start | bytes 393224 | tf_op jit(solution)/shard_map/ppermute | solution.py:82
  38.6 30.8 %collective-permute-start.20 = (bf16[64,2048]{1,0:T(8,128)(2,1)S(1)}, bf16[64,2048]{1,0:T(8,128)(2,1)S(1)}, u32[]{:S(2)}, u32[]{:S(2)}) collective-permute-start(bf16[64,2048]{1,0:T(8,128)(2,1)S(1)} %get-tuple-element.25), channel_id=1, source_target_pairs={{0,2},{1,3},{2,0},{3,1},{4,6},{5,7},{6,4},{7,5},{8,10},{9,11},{10,... | collective-permute-start | bytes 786440 | tf_op jit(solution)/shard_map/ppermute | solution.py:82
  39.2 10.5 %collective-permute-start.11 = (bf16[32,2048]{1,0:T(8,128)(2,1)}, bf16[32,2048]{1,0:T(8,128)(2,1)S(1)}, u32[]{:S(2)}, u32[]{:S(2)}) collective-permute-start(bf16[32,2048]{1,0:T(8,128)(2,1)} %collective-permute-done.10), channel_id=1, source_target_pairs={{0,2},{1,3},{2,0},{3,1},{4,6},{5,7},{6,4},{7,5},{8,10},{9,11},{10,... | collective-permute-start | bytes 393224 | tf_op jit(solution)/shard_map/ppermute | solution.py:82
  41.7 27.8 %collective-permute-start.21 = (bf16[64,2048]{1,0:T(8,128)(2,1)S(1)}, bf16[64,2048]{1,0:T(8,128)(2,1)S(1)}, u32[]{:S(2)}, u32[]{:S(2)}) collective-permute-start(bf16[64,2048]{1,0:T(8,128)(2,1)S(1)} %get-tuple-element.25), channel_id=1, source_target_pairs={{0,4},{1,5},{2,6},{3,7},{4,0},{5,1},{6,2},{7,3},{8,12},{9,13},{10,... | collective-permute-start | bytes 786440 | tf_op jit(solution)/shard_map/ppermute | solution.py:82
  49.7 5.2 %collective-permute-start.12 = (bf16[32,2048]{1,0:T(8,128)(2,1)}, bf16[32,2048]{1,0:T(8,128)(2,1)S(1)}, u32[]{:S(2)}, u32[]{:S(2)}) collective-permute-start(bf16[32,2048]{1,0:T(8,128)(2,1)} %collective-permute-done.10), channel_id=1, source_target_pairs={{0,4},{1,5},{2,6},{3,7},{4,0},{5,1},{6,2},{7,3},{8,12},{9,13},{10,... | collective-permute-start | bytes 393224 | tf_op jit(solution)/shard_map/ppermute | solution.py:82
  54.9 6.1 %collective-permute-start.13 = (bf16[32,2048]{1,0:T(8,128)(2,1)}, bf16[32,2048]{1,0:T(8,128)(2,1)S(1)}, u32[]{:S(2)}, u32[]{:S(2)}) collective-permute-start(bf16[32,2048]{1,0:T(8,128)(2,1)} %collective-permute-done.10), channel_id=1, source_target_pairs={{0,6},{1,7},{2,4},{3,5},{4,2},{5,3},{6,0},{7,1},{8,14},{9,15},{10,... | collective-permute-start | bytes 393224 | tf_op jit(solution)/shard_map/ppermute | solution.py:82
  61.0 5.7 %collective-permute-start.33 = (f32[16,2048]{1,0:T(8,128)S(1)}, f32[16,2048]{1,0:T(8,128)S(1)}, u32[]{:S(2)}, u32[]{:S(2)}) collective-permute-start(f32[16,2048]{1,0:T(8,128)S(1)} %add.222), channel_id=1, source_target_pairs={{0,2},{1,3},{2,0},{3,1},{4,6},{5,7},{6,4},{7,5},{8,10},{9,11},{10,... | collective-permute-start | bytes 393224 | tf_op jit(solution)/shard_map/ppermute | solution.py:82
  66.7 7.4 %collective-permute-start.22 = (bf16[64,2048]{1,0:T(8,128)(2,1)S(1)}, bf16[64,2048]{1,0:T(8,128)(2,1)S(1)}, u32[]{:S(2)}, u32[]{:S(2)}) collective-permute-start(bf16[64,2048]{1,0:T(8,128)(2,1)S(1)} %get-tuple-element.25), channel_id=1, source_target_pairs={{0,6},{1,7},{2,4},{3,5},{4,2},{5,3},{6,0},{7,1},{8,14},{9,15},{10,... | collective-permute-start | bytes 786440 | tf_op jit(solution)/shard_map/ppermute | solution.py:82
  69.4 6.0 %collective-permute-start.34 = (f32[16,2048]{1,0:T(8,128)S(1)}, f32[16,2048]{1,0:T(8,128)S(1)}, u32[]{:S(2)}, u32[]{:S(2)}) collective-permute-start(f32[16,2048]{1,0:T(8,128)S(1)} %add.223), channel_id=1, source_target_pairs={{0,4},{1,5},{2,6},{3,7},{4,0},{5,1},{6,2},{7,3},{8,12},{9,13},{10,... | collective-permute-start | bytes 393224 | tf_op jit(solution)/shard_map/ppermute | solution.py:82
  75.4 5.0 %collective-permute-start.35 = (f32[16,2048]{1,0:T(8,128)S(1)}, f32[16,2048]{1,0:T(8,128)S(1)}, u32[]{:S(2)}, u32[]{:S(2)}) collective-permute-start(f32[16,2048]{1,0:T(8,128)S(1)} %add.224), channel_id=1, source_target_pairs={{0,8},{8,0},{16,24},{24,16},{1,9},{9,1},{17,25},{25,17},{2,10},{10... | collective-permute-start | bytes 393224 | tf_op jit(solution)/shard_map/ppermute | solution.py:85
  80.5 5.9 %collective-permute-start.36 = (f32[16,2048]{1,0:T(8,128)S(1)}, f32[16,2048]{1,0:T(8,128)S(1)}, u32[]{:S(2)}, u32[]{:S(2)}) collective-permute-start(f32[16,2048]{1,0:T(8,128)S(1)} %add.225), channel_id=1, source_target_pairs={{0,16},{8,24},{16,0},{24,8},{1,17},{9,25},{17,1},{25,9},{2,18},{10... | collective-permute-start | bytes 393224 | tf_op jit(solution)/shard_map/ppermute | solution.py:85
  91.1 20.2 %collective-permute-start.25 = (bf16[2,32,2048]{2,1,0:T(8,128)(2,1)S(1)}, bf16[2,32,2048]{2,1,0:T(8,128)(2,1)S(1)}, u32[]{:S(2)}, u32[]{:S(2)}) collective-permute-start(bf16[2,32,2048]{2,1,0:T(8,128)(2,1)S(1)} %bitcast.127), channel_id=1, source_target_pairs={{0,6},{1,7},{2,4},{3,5},{4,2},{5,3},{6,0},{7,1},{8,14},{9,15},{10,... | collective-permute-start | bytes 786440 | tf_op jit(solution)/shard_map/ppermute | solution.py:82
  95.5 16.6 %collective-permute-start.24 = (bf16[2,32,2048]{2,1,0:T(8,128)(2,1)S(1)}, bf16[2,32,2048]{2,1,0:T(8,128)(2,1)S(1)}, u32[]{:S(2)}, u32[]{:S(2)}) collective-permute-start(bf16[2,32,2048]{2,1,0:T(8,128)(2,1)S(1)} %bitcast.126), channel_id=1, source_target_pairs={{0,4},{1,5},{2,6},{3,7},{4,0},{5,1},{6,2},{7,3},{8,12},{9,13},{10,... | collective-permute-start | bytes 786440 | tf_op jit(solution)/shard_map/ppermute | solution.py:82
  98.5 7.4 %collective-permute-start.16 = (bf16[1,32,2048]{2,1,0:T(8,128)(2,1)S(1)}, bf16[1,32,2048]{2,1,0:T(8,128)(2,1)S(1)}, u32[]{:S(2)}, u32[]{:S(2)}) collective-permute-start(bf16[1,32,2048]{2,1,0:T(8,128)(2,1)S(1)} %get-tuple-element.21), channel_id=1, source_target_pairs={{0,6},{1,7},{2,4},{3,5},{4,2},{5,3},{6,0},{7,1},{8,14},{9,15},{10,... | collective-permute-start | bytes 393224 | tf_op jit(solution)/shard_map/ppermute | solution.py:82
  100.7 7.7 %collective-permute-start.15 = (bf16[1,32,2048]{2,1,0:T(8,128)(2,1)S(1)}, bf16[1,32,2048]{2,1,0:T(8,128)(2,1)S(1)}, u32[]{:S(2)}, u32[]{:S(2)}) collective-permute-start(bf16[1,32,2048]{2,1,0:T(8,128)(2,1)S(1)} %get-tuple-element.22), channel_id=1, source_target_pairs={{0,4},{1,5},{2,6},{3,7},{4,0},{5,1},{6,2},{7,3},{8,12},{9,13},{10,... | collective-permute-start | bytes 393224 | tf_op jit(solution)/shard_map/ppermute | solution.py:82
  100.7 9.8 %collective-permute-start.14 = (bf16[1,32,2048]{2,1,0:T(8,128)(2,1)S(1)}, bf16[1,32,2048]{2,1,0:T(8,128)(2,1)S(1)}, u32[]{:S(2)}, u32[]{:S(2)}) collective-permute-start(bf16[1,32,2048]{2,1,0:T(8,128)(2,1)S(1)} %get-tuple-element.20), channel_id=1, source_target_pairs={{0,2},{1,3},{2,0},{3,1},{4,6},{5,7},{6,4},{7,5},{8,10},{9,11},{10,... | collective-permute-start | bytes 393224 | tf_op jit(solution)/shard_map/ppermute | solution.py:82
  105.9 6.6 %collective-permute-start.23 = (bf16[2,32,2048]{2,1,0:T(8,128)(2,1)S(1)}, bf16[2,32,2048]{2,1,0:T(8,128)(2,1)S(1)}, u32[]{:S(2)}, u32[]{:S(2)}) collective-permute-start(bf16[2,32,2048]{2,1,0:T(8,128)(2,1)S(1)} %bitcast.125), channel_id=1, source_target_pairs={{0,2},{1,3},{2,0},{3,1},{4,6},{5,7},{6,4},{7,5},{8,10},{9,11},{10,... | collective-permute-start | bytes 786440 | tf_op jit(solution)/shard_map/ppermute | solution.py:82
  108.4 7.4 %collective-permute-start.9 = (bf16[32,2048]{1,0:T(8,128)(2,1)S(1)}, bf16[32,2048]{1,0:T(8,128)(2,1)S(1)}, u32[]{:S(2)}, u32[]{:S(2)}) collective-permute-start(bf16[32,2048]{1,0:T(8,128)(2,1)S(1)} %get-tuple-element.18), channel_id=1, source_target_pairs={{0,6},{1,7},{2,4},{3,5},{4,2},{5,3},{6,0},{7,1},{8,14},{9,15},{10,... | collective-permute-start | bytes 393224 | tf_op jit(solution)/shard_map/ppermute | solution.py:82
  110.6 6.3 %collective-permute-start.8 = (bf16[32,2048]{1,0:T(8,128)(2,1)S(1)}, bf16[32,2048]{1,0:T(8,128)(2,1)S(1)}, u32[]{:S(2)}, u32[]{:S(2)}) collective-permute-start(bf16[32,2048]{1,0:T(8,128)(2,1)S(1)} %get-tuple-element.19), channel_id=1, source_target_pairs={{0,4},{1,5},{2,6},{3,7},{4,0},{5,1},{6,2},{7,3},{8,12},{9,13},{10,... | collective-permute-start | bytes 393224 | tf_op jit(solution)/shard_map/ppermute | solution.py:82
  111.3 5.6 %collective-permute-start.7 = (bf16[32,2048]{1,0:T(8,128)(2,1)S(1)}, bf16[32,2048]{1,0:T(8,128)(2,1)S(1)}, u32[]{:S(2)}, u32[]{:S(2)}) collective-permute-start(bf16[32,2048]{1,0:T(8,128)(2,1)S(1)} %get-tuple-element.17), channel_id=1, source_target_pairs={{0,2},{1,3},{2,0},{3,1},{4,6},{5,7},{6,4},{7,5},{8,10},{9,11},{10,... | collective-permute-start | bytes 393224 | tf_op jit(solution)/shard_map/ppermute | solution.py:82
  112.7 7.1 %collective-permute-start.27 = (bf16[32,2048]{1,0:T(8,128)(2,1)S(1)}, bf16[32,2048]{1,0:T(8,128)(2,1)S(1)}, u32[]{:S(2)}, u32[]{:S(2)}) collective-permute-start(bf16[32,2048]{1,0:T(8,128)(2,1)S(1)} %get-tuple-element.24), channel_id=1, source_target_pairs={{0,24},{8,16},{16,8},{24,0},{1,25},{9,17},{17,9},{25,1},{2,26},{10... | collective-permute-start | bytes 393224 | tf_op jit(solution)/shard_map/ppermute | solution.py:85
  115.8 7.6 %collective-permute-start.26 = (bf16[32,2048]{1,0:T(8,128)(2,1)S(1)}, bf16[32,2048]{1,0:T(8,128)(2,1)}, u32[]{:S(2)}, u32[]{:S(2)}) collective-permute-start(bf16[32,2048]{1,0:T(8,128)(2,1)S(1)} %get-tuple-element.23), channel_id=1, source_target_pairs={{0,16},{8,24},{16,0},{24,8},{1,17},{9,25},{17,1},{25,9},{2,18},{10... | collective-permute-start | bytes 393224 | tf_op jit(solution)/shard_map/ppermute | solution.py:85
  124.7 6.0 %collective-permute-start.30 = (bf16[32,2048]{1,0:T(8,128)(2,1)S(1)}, bf16[32,2048]{1,0:T(8,128)(2,1)S(1)}, u32[]{:S(2)}, u32[]{:S(2)}) collective-permute-start(bf16[32,2048]{1,0:T(8,128)(2,1)S(1)} %get-tuple-element.6), channel_id=1, source_target_pairs={{0,6},{1,7},{2,4},{3,5},{4,2},{5,3},{6,0},{7,1},{8,14},{9,15},{10,... | collective-permute-start | bytes 393224 | tf_op jit(solution)/shard_map/ppermute | solution.py:82
  126.8 5.2 %collective-permute-start.29 = (bf16[32,2048]{1,0:T(8,128)(2,1)S(1)}, bf16[32,2048]{1,0:T(8,128)(2,1)S(1)}, u32[]{:S(2)}, u32[]{:S(2)}) collective-permute-start(bf16[32,2048]{1,0:T(8,128)(2,1)S(1)} %get-tuple-element.6), channel_id=1, source_target_pairs={{0,4},{1,5},{2,6},{3,7},{4,0},{5,1},{6,2},{7,3},{8,12},{9,13},{10,... | collective-permute-start | bytes 393224 | tf_op jit(solution)/shard_map/ppermute | solution.py:82
  132.5 5.1 %collective-permute-start.31 = (bf16[128,2048]{1,0:T(8,128)(2,1)S(1)}, bf16[128,2048]{1,0:T(8,128)(2,1)S(1)}, u32[]{:S(2)}, u32[]{:S(2)}) collective-permute-start(bf16[128,2048]{1,0:T(8,128)(2,1)S(1)} %pad_maximum_fusion.1), channel_id=1, source_target_pairs={{0,1},{1,0},{2,3},{3,2},{4,5},{5,4},{6,7},{7,6},{8,9},{9,8},{10,11... | collective-permute-start | bytes 1572872 | tf_op jit(solution)/shard_map/ppermute | solution.py:82
  (23 other events, 145.3 us)

commit v3 on v0

v3 whole, which is shorter than its diff:
```python
import functools

import jax
import jax.numpy as jnp
from jax import lax
from jax.experimental import pallas as pl
from jax.experimental.pallas import tpu as pltpu
from jax.sharding import PartitionSpec as P

logit_divisor = 0.05
grad_scale = 256.0
epsilon = 1e-06
lanes = 128
tail = 16
bf16 = jnp.bfloat16
f32 = jnp.float32

anywhere = pl.BlockSpec(memory_space=pl.ANY)
in_vmem = pl.BlockSpec(memory_space=pltpu.VMEM)
in_smem = pl.BlockSpec(memory_space=pltpu.SMEM)


def params(mebibytes):
    return pltpu.CompilerParams(vmem_limit_bytes=mebibytes << 20)


def cost(flops, moved):
    return pl.CostEstimate(flops=flops, transcendentals=0, bytes_accessed=moved)


def dot(left, right, dims=((1,), (0,)), precision=None):
    return lax.dot_general(
        left, right, (dims, ((), ())), precision=precision, preferred_element_type=f32
    )


def doublings(count):
    steps = [1 << bit for bit in range((count - 1).bit_length())]
    assert 1 << len(steps) == count
    return steps


def column(table, wanted):
    index = lax.broadcasted_iota(jnp.int32, table.shape, 1)
    return jnp.sum(jnp.where(index == wanted, table, 0.0), axis=1, keepdims=True)


def note_kernel(seq_dev, part_rows, place, positives, dense, tokens, out, wide, table, rows, sems):
    seq_length = tokens.shape[0] // seq_dev
    copies = [
        pltpu.make_async_copy(
            tokens.at[pl.ds((seq + 1) * seq_length - tail, tail)], rows.at[seq], sems.at[seq]
        )
        for seq in range(seq_dev)
    ]
    for copy in copies:
        copy.start()
    table[...] = dense[...].astype(f32)
    start = pl.multiple_of(place[1] * part_rows, part_rows)
    wide[:part_rows, :] = table[pl.ds(start, part_rows), :]
    base = part_rows + 2 * seq_dev
    for seq in range(seq_dev):
        last = (seq + 1) * seq_length - 1
        wide[part_rows + seq : part_rows + seq + 1, :] = table[last : last + 1, :]
        own = jnp.full((1, wide.shape[1]), positives[seq], jnp.int32).astype(f32)
        wide[part_rows + seq_dev + seq : part_rows + seq_dev + seq + 1, :] = own
    for seq in range(seq_dev):
        copies[seq].wait()
        values = rows[seq].astype(f32)
        for chunk in range(tokens.shape[1] // lanes):
            row = base + chunk * seq_dev + seq
            wide[row : row + 1, :] = values[tail - 1 : tail, chunk * lanes : (chunk + 1) * lanes]
    out[...] = wide[...].astype(bf16)


def expert_kernel(layout, *refs):
    chips, part_rows, seq_dev, near, with_last, n_parts = layout
    refs = list(refs)
    place = refs.pop(0)
    tokens = refs.pop(0) if near else None
    noted = refs.pop(0) if with_last else None
    parts, refs = refs[:n_parts], refs[n_parts:]
    weights, refs = refs[:4], refs[4:]
    outs, refs = refs[:chips], refs[chips:]
    if with_last:
        last_rows, last_projected, last_out, last_marks, *refs = refs
        floats, joined, marks, *refs = refs
    rows, w_in, w_out, sems, weight_sems = refs
    targets = [w_in.at[0], w_out.at[0], w_in.at[1], w_out.at[1]]
    weight_copies = [
        pltpu.make_async_copy(source.at[0], target, weight_sems.at[index])
        for index, (source, target) in enumerate(zip(weights, targets))
    ]
    count = outs[0].shape[0] // part_rows
    copies = []

    def place_rows(source, start):
        target = rows.at[pl.ds(start, source.shape[0])]
        copies.append(pltpu.make_async_copy(source, target, sems.at[len(copies)]))

    block = count * part_rows
    if near:
        for chip in range(chips):
            start = pl.multiple_of((place[1] ^ (2 * chip)) * part_rows, part_rows)
            place_rows(tokens.at[pl.ds(start, part_rows)], chip * block)
    own_parts = count - 1 if near else count
    for index in range(own_parts):
        place_rows(parts[index], (index + count - own_parts) * part_rows)
    for chip in range(1, chips):
        place_rows(parts[own_parts + chip - 1], chip * block + (count - own_parts) * part_rows)
    for copy in copies:
        copy.start()
    for copy in weight_copies:
        copy.start()
    total = chips * block
    if with_last:
        base = part_rows + 2 * seq_dev
        floats[...] = noted[...].astype(f32)
        for plane in range(noted.shape[0]):
            own = slice(plane * seq_dev, (plane + 1) * seq_dev)
            marks[0, own, :] = floats[plane, part_rows : part_rows + seq_dev, :]
            marks[1, own, :] = floats[plane, part_rows + seq_dev : base, :]
            for chunk in range(rows.shape[1] // lanes):
                start = base + chunk * seq_dev
                joined[own, chunk * lanes : (chunk + 1) * lanes] = floats[
                    plane, start : start + seq_dev, :
                ]
        last_rows[...] = joined[...].astype(bf16)
        rows[total:, :] = joined[...].astype(bf16)
    for copy in copies:
        copy.wait()
    half_width = w_out.shape[1]
    result = None
    for half in range(2):
        weight_copies[2 * half].wait()
        used = rows[...] if half == 0 else rows[:total, :]
        projected = dot(used, w_in[half])
        gate, up = projected[:, :half_width], projected[:, half_width:]
        hidden = (gate * jax.nn.sigmoid(gate) * up).astype(bf16)
        weight_copies[2 * half + 1].wait()
        if half == 0 and with_last:
            last_projected[...] = projected[total:]
            weight = column(marks[0], place[2])
            own_last = dot(hidden[total:], w_out[0]).astype(bf16).astype(f32)
            last_out[...] = (weight * own_last).astype(bf16)
            last_marks[0, :, :] = jnp.broadcast_to(weight, marks.shape[1:])
            last_marks[1, :, :] = marks[1]
        part = dot(hidden[:total], w_out[half])
        result = part if half == 0 else result + part
    for chip in range(chips):
        outs[chip][...] = result[chip * block : (chip + 1) * block].astype(bf16)


def combine_kernel(layout, place, noted, own, *refs):
    chips, part_rows, group, n_outs = layout
    parts, outs = refs[:chips], refs[chips : chips + n_outs]
    first_expert = place[2] - place[1] // 2
    for index, hop in enumerate(group):
        table = noted[place[0] ^ hop, :part_rows, :].astype(f32)
        rows = slice(index * part_rows, (index + 1) * part_rows)
        total = own[...].astype(f32) if hop == 0 else None
        for chip in range(chips):
            weight = column(table, first_expert + ((place[1] // 2) ^ chip))
            term = weight * parts[chip][rows, :].astype(f32)
            total = term if total is None else total + term
        outs[index][...] = total.astype(outs[index].dtype)


def gather_kernel(chips, place, *refs):
    pieces, mirrored, out, sems = refs[:chips], refs[chips], refs[chips + 1], refs[chips + 2]
    part_rows = pieces[0].shape[0]
    copies = []
    for chip in range(chips):
        lane = place[1] ^ (2 * chip)
        for source, at in (
            (pieces[chip], lane),
            (mirrored.at[pl.ds(chip * part_rows, part_rows)], lane ^ 1),
        ):
            start = pl.multiple_of(at * part_rows, part_rows)
            target = out.at[pl.ds(start, part_rows)]
            copies.append(pltpu.make_async_copy(source, target, sems.at[len(copies)]))
    for copy in copies:
        copy.start()
    for copy in copies:
        copy.wait()


def gradient_kernel(
    last_all, last_block, last_sum, projected, marks, down, grad_in, grad_out, route, hidden, slope
):
    step = pl.program_id(0)
    half_width = down.shape[1]
    block = grad_out.shape[2]

    @pl.when(step == 0)
    def _():
        layer_last = (last_all[...].astype(f32) + last_sum[...].astype(f32)).astype(bf16)
        values = layer_last.astype(f32)
        count = values.shape[0]
        norms = jnp.sqrt(jnp.sum(values * values, axis=1, keepdims=True) + epsilon)
        unit = values / norms
        scores = dot(unit, unit, ((1,), (1,)), lax.Precision.HIGHEST) / logit_divisor
        row = lax.broadcasted_iota(jnp.int32, (count, count), 0)
        col = lax.broadcasted_iota(jnp.int32, (count, count), 1)
        exp_scores = jnp.where(row != col, jnp.exp(scores), 0.0)
        probabilities = exp_scores / jnp.sum(exp_scores, axis=1, keepdims=True)
        partner = marks[1][:, :1].astype(jnp.int32)
        coefficient = grad_scale * (probabilities - jnp.where(col == partner, 1.0, 0.0))
        high = lax.Precision.HIGHEST
        grad_unit = (
            dot(coefficient, unit, ((1,), (0,)), high) + dot(coefficient, unit, ((0,), (0,)), high)
        ) / logit_divisor
        projection = jnp.sum(unit * grad_unit, axis=1, keepdims=True)
        grad_last = (grad_unit - unit * projection) / norms
        route_grad = (marks[0][:, :1] * grad_last).astype(bf16)
        for index in range(route.shape[0]):
            route[index] = route_grad[:, index * block : (index + 1) * block]
        grad_hidden = dot(route_grad, down[0], ((1,), (1,)))
        gate, up = projected[:, :half_width], projected[:, half_width:]
        sigmoid_gate = jax.nn.sigmoid(gate)
        activated = gate * sigmoid_gate
        hidden[...] = (activated * up).astype(bf16)
        gate_slope = sigmoid_gate * (1.0 + gate * (1.0 - sigmoid_gate))
        slope[:, :half_width] = (grad_hidden * up * gate_slope).astype(bf16)
        slope[:, half_width:] = (grad_hidden * activated).astype(bf16)

    grad_in[0] = dot(last_block[...], slope[...], ((0,), (0,))).astype(bf16)
    grad_out[0] = dot(hidden[...], route[step], ((0,), (0,))).astype(bf16)


def body(tokens, expert_ids, gates, positives, gate_up, down):
    dp_count = lax.axis_size("dp")
    expert_count = lax.axis_size("expert")
    chips = expert_count // 2
    experts = dp_count * chips
    tok_dev, width = tokens.shape
    half_width = down.shape[1]
    seq_dev = positives.shape[0]
    seqs = dp_count * seq_dev
    seq_length = tok_dev // seq_dev
    part_rows = tok_dev // expert_count
    plane = lax.axis_index("dp")
    lane = lax.axis_index("expert")
    place = jnp.stack([plane, lane, plane * chips + lane // 2]).astype(jnp.int32)
    assert experts <= lanes and seq_length % tail == 0

    def to_lane(value, step):
        return lax.ppermute(value, "expert", [(j, j ^ step) for j in range(expert_count)])

    def to_plane(value, step):
        return lax.ppermute(value, "dp", [(p, p ^ step) for p in range(dp_count)])

    chip_steps = [2 * step for step in range(1, chips)]
    groups = [range(first, min(first + 2, dp_count)) for first in range(0, dp_count, 2)]

    own_part = lax.dynamic_slice_in_dim(tokens, lane * part_rows, part_rows, 0)
    arrivals = {hop: to_plane(own_part, hop) for hop in range(1, dp_count)}
    mate_in = to_lane(gate_up, 1)
    mate_out = to_lane(down, 1)
    weights = (gate_up, down, mate_in, mate_out)

    dense = jnp.where(
        expert_ids == jnp.arange(lanes, dtype=jnp.int32)[None, :], gates, 0.0
    ).astype(bf16)
    dense, _ = lax.optimization_barrier((dense, arrivals[1]))
    for step in doublings(expert_count):
        dense = dense + to_lane(dense, step)
    note_rows = part_rows + 2 * seq_dev + seq_dev * (width // lanes)
    noted = pl.pallas_call(
        functools.partial(note_kernel, seq_dev, part_rows),
        out_shape=jax.ShapeDtypeStruct((note_rows, lanes), bf16),
        in_specs=[in_smem, in_smem, in_vmem, anywhere],
        out_specs=in_vmem,
        scratch_shapes=[
            pltpu.VMEM((note_rows, lanes), f32),
            pltpu.VMEM((tok_dev, lanes), f32),
            pltpu.VMEM((seq_dev, tail, width), bf16),
            pltpu.SemaphoreType.DMA((seq_dev,)),
        ],
        cost_estimate=cost(0, 1 << 20),
        name="notes",
    )(place, positives, dense, tokens)[None]

    for step in doublings(dp_count):
        other = to_plane(noted, step)
        noted = jnp.where(
            plane & step != 0,
            jnp.concatenate([other, noted], axis=0),
            jnp.concatenate([noted, other], axis=0),
        )

    def expert(group, with_last):
        near = group[0] == 0
        own = [arrivals[hop] for hop in group if hop]
        joined = own[0] if len(own) == 1 else jnp.concatenate(own, axis=0)
        parts = own + [to_lane(joined, step) for step in chip_steps]
        block = len(group) * part_rows
        total = chips * block
        extra = seqs if with_last else 0
        out_shape = [jax.ShapeDtypeStruct((block, width), bf16)] * chips
        scratch = []
        if with_last:
            out_shape += [
                jax.ShapeDtypeStruct((seqs, width), bf16),
                jax.ShapeDtypeStruct((seqs, 2 * half_width), f32),
                jax.ShapeDtypeStruct((seqs, width), bf16),
                jax.ShapeDtypeStruct((2, seqs, lanes), f32),
            ]
            scratch += [
                pltpu.VMEM(noted.shape, f32),
                pltpu.VMEM((seqs, width), f32),
                pltpu.VMEM((2, seqs, lanes), f32),
            ]
        scratch += [
            pltpu.VMEM((total + extra, width), bf16),
            pltpu.VMEM((2, width, 2 * half_width), bf16),
            pltpu.VMEM((2, half_width, width), bf16),
            pltpu.SemaphoreType.DMA((2 * chips + len(group),)),
            pltpu.SemaphoreType.DMA((4,)),
        ]
        operands = [place] + [tokens] * near + [noted] * with_last + parts + list(weights)
        specs = [in_smem] + [anywhere] * near + [in_vmem] * with_last
        specs += [anywhere] * (len(parts) + 4)
        layout = (chips, part_rows, seq_dev, near, with_last, len(parts))
        return pl.pallas_call(
            functools.partial(expert_kernel, layout),
            out_shape=out_shape,
            in_specs=specs,
            out_specs=[in_vmem] * len(out_shape),
            scratch_shapes=scratch,
            compiler_params=params(32),
            cost_estimate=cost(2 * total * width * 6 * half_width, 12 << 20),
            name="experts",
        )(*operands)

    def combine(group, out):
        parts = [out[0]] + [to_lane(out[index + 1], step) for index, step in enumerate(chip_steps)]
        out_shape = [
            jax.ShapeDtypeStruct((part_rows, width), bf16 if hop else f32) for hop in group
        ]
        layout = (chips, part_rows, tuple(group), len(group))
        return pl.pallas_call(
            functools.partial(combine_kernel, layout),
            out_shape=out_shape,
            in_specs=[in_smem] + [in_vmem] * (2 + chips),
            out_specs=[in_vmem] * len(group),
            cost_estimate=cost(0, 3 << 20),
            name="combine",
        )(place, noted, own_part, *parts)

    last_group = min(1, len(groups) - 1)
    sums = {}
    for index, group in enumerate(groups):
        out = expert(group, index == last_group)
        if index == last_group:
            last_all, last_projected, last_sum, last_marks = out[chips:]
        for hop, value in zip(group, combine(group, out[:chips])):
            sums[hop] = value

    for step in doublings(expert_count):
        last_sum = (last_sum.astype(f32) + to_lane(last_sum, step).astype(f32)).astype(bf16)
    for step in doublings(dp_count):
        last_sum = (last_sum.astype(f32) + to_plane(last_sum, step).astype(f32)).astype(bf16)

    total = sums[0]
    for hop in range(1, dp_count):
        total = total + to_plane(sums[hop], hop).astype(f32)
    own_out = total.astype(bf16)
    pieces = [own_out] + [to_lane(own_out, step) for step in chip_steps]
    mirrored = to_lane(jnp.concatenate(pieces, axis=0), 1)
    layer_out = pl.pallas_call(
        functools.partial(gather_kernel, chips),
        out_shape=jax.ShapeDtypeStruct((tok_dev, width), bf16),
        in_specs=[in_smem] + [anywhere] * (chips + 1),
        out_specs=anywhere,
        scratch_shapes=[pltpu.SemaphoreType.DMA((expert_count,))],
        cost_estimate=cost(0, 2 << 20),
        name="gather",
    )(place, *pieces, mirrored)

    block = min(512, width)
    steps = width // block
    grad_gate_up, grad_down = pl.pallas_call(
        gradient_kernel,
        grid=(steps,),
        out_shape=[
            jax.ShapeDtypeStruct(gate_up.shape, bf16),
            jax.ShapeDtypeStruct(down.shape, bf16),
        ],
        in_specs=[
            pl.BlockSpec((seqs, width), lambda step: (0, 0)),
            pl.BlockSpec((seqs, block), lambda step: (0, step)),
            pl.BlockSpec((seqs, width), lambda step: (0, 0)),
            pl.BlockSpec((seqs, 2 * half_width), lambda step: (0, 0)),
            pl.BlockSpec((2, seqs, lanes), lambda step: (0, 0, 0)),
            pl.BlockSpec((1, half_width, width), lambda step: (0, 0, 0)),
        ],
        out_specs=[
            pl.BlockSpec((1, block, 2 * half_width), lambda step: (0, step, 0)),
            pl.BlockSpec((1, half_width, block), lambda step: (0, 0, step)),
        ],
        scratch_shapes=[
            pltpu.VMEM((steps, seqs, block), bf16),
            pltpu.VMEM((seqs, half_width), bf16),
            pltpu.VMEM((seqs, 2 * half_width), bf16),
        ],
        compiler_params=params(24),
        cost_estimate=cost(2 * seqs * width * 4 * half_width, 7 << 20),
        name="gradients",
    )(last_all, last_all, last_sum, last_projected, last_marks, down)
    return (layer_out, grad_gate_up, grad_down)


def solution(mesh):
    return jax.shard_map(
        body,
        mesh=mesh,
        in_specs=(
            P("dp", None),
            P("dp", "expert"),
            P("dp", "expert"),
            P("dp"),
            P(("dp", "expert"), None, None),
            P(("dp", "expert"), None, None),
        ),
        out_specs=(P("dp", None), P(("dp", "expert"), None, None), P(("dp", "expert"), None, None)),
        check_vma=False,
    )
```

time: 524 us -> 151 us (0.29)
  blocking collectives: 318 us -> 0 us
  waiting for transfers between devices: 135 us -> 35.6 us
  Pallas kernels: 0 us -> 60.6 us
  starting transfers between devices: 4.81 us -> 40.1 us
  matrix products: 18.6 us -> 0 us
  between operations: 14.9 us -> 0.93 us
  local copies, waits for them, and re-layouts: 21.7 us -> 9.07 us
  other arithmetic: 10.7 us -> 4.09 us
    all_to_all x5 -> x0, blocking collectives: 305 us -> none  [the longest x2 105 us: dispatch(): lax.all_to_all(doubled, 'expert', split_axis=1, concat_axis=1, tiled=True)]
    pallas_call x0 -> x7, Pallas kernels: none -> 60.6 us  [the longest x1 33.6 us: body(): pl.pallas_call(functools.partial(gather_kernel, chips), out_shape=jax.Sha...]
    psum x1 -> x0, waiting for transfers between devices: 53.9 us -> none  [body(): lax.psum(contrib.astype(jnp.bfloat16), 'expert').astype(jnp.float32)]
    all_to_all x1 -> x0, waiting for transfers between devices: 48.9 us -> none  [body(): lax.all_to_all(lax.all_to_all(half_out.reshape(dp_count, expert_count, la...]
    ppermute x0 -> x34, starting transfers between devices: none -> 40.1 us  [the longest x24 25.2 us: to_lane(): lax.ppermute(value, 'expert', [(j, j ^ step) for j in range(expert_count)])]
    ppermute x0 -> x34, waiting for transfers between devices: none -> 35.6 us  [the longest x24 23 us: to_lane(): lax.ppermute(value, 'expert', [(j, j ^ step) for j in range(expert_count)])]
    unnamed x3 -> x0, waiting for transfers between devices: 31.9 us -> none
    dot_general x8 -> x0, matrix products: 18.6 us -> none  [the longest x2 7.89 us: contract_rows(): lax.dot_general(left_side, right_side, (((0,), (0,)), ((), ())), preferre...]
  transfers between devices with their start and end apart: 3 -> 34, of which waited for: 3 -> 19; matrix products, arithmetic and copies ran while one was open for 0% -> 5% of each run, Pallas kernels for 0% -> 13%
where the time goes in v3:
time: 151 us; the launch traced here: 150 us
  Pallas kernels  60.6 us (40%)
  starting transfers between devices  40.1 us (27%)
  waiting for transfers between devices  35.6 us (24%)
  local copies, waits for them, and re-layouts  9.07 us (6%)
  other arithmetic  4.09 us (3%)
    pallas_call x1, Pallas kernels, body(): pl.pallas_call(functools.partial(gather_kernel, chips), out_shape=jax.Sha...  33.6 us
    ppermute x24, starting transfers between devices, to_lane(): lax.ppermute(value, 'expert', [(j, j ^ step) for j in range(expert_count)])  25.2 us
    ppermute x24, waiting for transfers between devices, to_lane(): lax.ppermute(value, 'expert', [(j, j ^ step) for j in range(expert_count)])  23 us
    ppermute x10, starting transfers between devices, to_plane(): return lax.ppermute(value, 'dp', [(p, p ^ step) for p in range(dp_count)])  15 us
    pallas_call x2, Pallas kernels, expert(): pl.pallas_call(functools.partial(expert_kernel, layout), out_shape=out_sh...  14.2 us
    ppermute x10, waiting for transfers between devices, to_plane(): return lax.ppermute(value, 'dp', [(p, p ^ step) for p in range(dp_count)])  12.6 us
    unnamed x51, local copies, waits for them, and re-layouts  6.84 us
    pallas_call x1, Pallas kernels, body(): pl.pallas_call(gradient_kernel, grid=(steps,), out_shape=[jax.ShapeDtypeS...  5.75 us
  transfers between devices with their start and end apart: 34, of which 19 were waited for; matrix products, arithmetic and copies ran while one was open for 5% of the time, Pallas kernels for 13%

profile of v3, /device:TPU:0, one launch (start us, length us, event | category | flops | bytes accessed | tf_op | source)
XLA Modules:
  0.0 150.4 jit_solution(16686018508282037741)
XLA Ops:
  2.8 3.0 %collective-permute-start = (bf16[32,2048]{1,0:T(8,128)(2,1)}, bf16[32,2048]{1,0:T(8,128)(2,1)S(1)}, u32[]{:S(2)}, u32[]{:S(2)}) collective-permute-start(bf16[32,2048]{1,0:T(8,128)(2,1)} %constant_dynamic-slice_fusion.own), channel_id=1, source_target_pairs={{0,8},{8,0},{16,24},{24,16},{1,9},{9,1},{17,25},{25,17},{2,10},{10... | collective-permute-start | bytes 393224 | tf_op jit(solution)/shard_map/ppermute | solution.py:251
  6.6 3.1 %collective-permute-done.refs_2_ = bf16[32,2048]{1,0:T(8,128)(2,1)S(1)} collective-permute-done((bf16[32,2048]{1,0:T(8,128)(2,1)}, bf16[32,2048]{1,0:T(8,128)(2,1)S(1)}, u32[]{:S(2)}, u32[]{:S(2)}) %collective-permute-start) | collective-permute-done | bytes 131104 | tf_op jit(solution)/shard_map/ppermute | solution.py:251
  11.0 1.7 %collective-permute-start.2 = (bf16[256,128]{1,0:T(8,128)(2,1)S(1)}, bf16[256,128]{1,0:T(8,128)(2,1)S(1)}, u32[]{:S(2)}, u32[]{:S(2)}) collective-permute-start(bf16[256,128]{1,0:T(8,128)(2,1)S(1)} %add.42), channel_id=1, source_target_pairs={{0,2},{1,3},{2,0},{3,1},{4,6},{5,7},{6,4},{7,5},{8,10},{9,11},{10,... | collective-permute-start | bytes 196616 | tf_op jit(solution)/shard_map/ppermute | solution.py:248
  12.8 2.6 %collective-permute-start.15 = (bf16[32,2048]{1,0:T(8,128)(2,1)}, bf16[32,2048]{1,0:T(8,128)(2,1)S(1)}, u32[]{:S(2)}, u32[]{:S(2)}) collective-permute-start(bf16[32,2048]{1,0:T(8,128)(2,1)} %constant_dynamic-slice_fusion.own), channel_id=1, source_target_pairs={{0,16},{8,24},{16,0},{24,8},{1,17},{9,25},{17,1},{25,9},{2,18},{10... | collective-permute-start | bytes 393224 | tf_op jit(solution)/shard_map/ppermute | solution.py:251
  16.7 1.6 %collective-permute-start.3 = (bf16[256,128]{1,0:T(8,128)(2,1)S(1)}, bf16[256,128]{1,0:T(8,128)(2,1)S(1)}, u32[]{:S(2)}, u32[]{:S(2)}) collective-permute-start(bf16[256,128]{1,0:T(8,128)(2,1)S(1)} %add.43), channel_id=1, source_target_pairs={{0,4},{1,5},{2,6},{3,7},{4,0},{5,1},{6,2},{7,3},{8,12},{9,13},{10,... | collective-permute-start | bytes 196616 | tf_op jit(solution)/shard_map/ppermute | solution.py:248
  18.9 2.2 %collective-permute-done.3 = bf16[256,128]{1,0:T(8,128)(2,1)S(1)} collective-permute-done((bf16[256,128]{1,0:T(8,128)(2,1)S(1)}, bf16[256,128]{1,0:T(8,128)(2,1)S(1)}, u32[]{:S(2)}, u32[]{:S(2)}) %collective-permute-start.3) | collective-permute-done | bytes 65568 | tf_op jit(solution)/shard_map/ppermute | solution.py:248
  21.7 2.4 %notes.1 = bf16[104,128]{1,0:T(8,128)(2,1)} custom-call(s32[3]{0:T(128)} %pad_add_fusion.place.refs_0_, s32[4]{0:T(128)} %positives.1, bf16[256,128]{1,0:T(8,128)(2,1)} %add.44.dense, bf16[256,2048]{1,0:T(8,128)(2,1)} %refs_1_.1), custom_call_target="tpu_custom_call" | custom-call | bytes 1048576 | tf_op jit(solution)/shard_map/notes/pallas_call | solution.py:269
  26.5 1.8 %collective-permute-done.4 = bf16[1,104,128]{2,1,0:T(8,128)(2,1)S(1)} collective-permute-done((bf16[1,104,128]{2,1,0:T(8,128)(2,1)}, bf16[1,104,128]{2,1,0:T(8,128)(2,1)S(1)}, u32[]{:S(2)}, u32[]{:S(2)}) %collective-permute-start.4) | collective-permute-done | bytes 26656 | tf_op jit(solution)/shard_map/ppermute | solution.py:251
  29.1 1.8 %collective-permute-start.5 = (bf16[2,104,128]{2,1,0:T(8,128)(2,1)S(1)}, bf16[2,104,128]{2,1,0:T(8,128)(2,1)S(1)}, u32[]{:S(2)}, u32[]{:S(2)}) collective-permute-start(bf16[2,104,128]{2,1,0:T(8,128)(2,1)S(1)} %maximum_select_fusion.1), channel_id=1, source_target_pairs={{0,16},{8,24},{16,0},{24,8},{1,17},{9,25},{17,1},{25,9},{2,18},{10... | collective-permute-start | bytes 159752 | tf_op jit(solution)/shard_map/ppermute | solution.py:251
  35.7 5.1 %collective-permute-done.17.refs_4_ = bf16[64,2048]{1,0:T(8,128)(2,1)} collective-permute-done((bf16[64,2048]{1,0:T(8,128)(2,1)}, bf16[64,2048]{1,0:T(8,128)(2,1)}, u32[]{:S(2)}, u32[]{:S(2)}) %collective-permute-start.17) | collective-permute-done | bytes 262176 | tf_op jit(solution)/shard_map/ppermute | solution.py:248
  40.8 2.5 %collective-permute-done.18.refs_5_ = bf16[64,2048]{1,0:T(8,128)(2,1)} collective-permute-done((bf16[64,2048]{1,0:T(8,128)(2,1)}, bf16[64,2048]{1,0:T(8,128)(2,1)}, u32[]{:S(2)}, u32[]{:S(2)}) %collective-permute-start.18) | collective-permute-done | bytes 262176 | tf_op jit(solution)/shard_map/ppermute | solution.py:248
  44.1 1.9 %copy-done.1 = bf16[1,2048,768]{2,1,0:T(8,128)(2,1)S(1)} copy-done((bf16[1,2048,768]{2,1,0:T(8,128)(2,1)S(1)}, bf16[1,2048,768]{2,1,0:T(8,128)(2,1)}, u32[]{:S(2)}) %copy-start.1) | copy-done | bytes 3145752
  46.6 6.7 %experts.3 = (bf16[64,2048]{1,0:T(8,128)(2,1)S(1)}, bf16[64,2048]{1,0:T(8,128)(2,1)S(1)}, bf16[64,2048]{1,0:T(8,128)(2,1)S(1)}, bf16[64,2048]{1,0:T(8,128)(2,1)S...) custom-call(s32[3]{0:T(128)S(1)} %copy-done.12, ...), custom_call_target="tpu_custom_call" | custom-call | flops 2415919104 | bytes 12582912 | tf_op jit(solution)/shard_map/experts/pallas_call | solution.py:325
  60.3 1.6 %collective-permute-start.22 = (bf16[64,2048]{1,0:T(8,128)(2,1)S(1)}, bf16[64,2048]{1,0:T(8,128)(2,1)S(1)}, u32[]{:S(2)}, u32[]{:S(2)}) collective-permute-start(bf16[64,2048]{1,0:T(8,128)(2,1)S(1)} %get-tuple-element.32), channel_id=1, source_target_pairs={{0,6},{1,7},{2,4},{3,5},{4,2},{5,3},{6,0},{7,1},{8,14},{9,15},{10,... | collective-permute-start | bytes 786440 | tf_op jit(solution)/shard_map/ppermute | solution.py:248
  62.5 1.9 %collective-permute-start.30 = (bf16[16,2048]{1,0:T(8,128)(2,1)S(1)}, bf16[16,2048]{1,0:T(8,128)(2,1)S(1)}, u32[]{:S(2)}, u32[]{:S(2)}) collective-permute-start(bf16[16,2048]{1,0:T(8,128)(2,1)S(1)} %add_convert_fusion.5), channel_id=1, source_target_pairs={{0,2},{1,3},{2,0},{3,1},{4,6},{5,7},{6,4},{7,5},{8,10},{9,11},{10,... | collective-permute-start | bytes 196616 | tf_op jit(solution)/shard_map/ppermute | solution.py:248
  64.4 7.5 %experts.2 = (bf16[64,2048]{1,0:T(8,128)(2,1)S(1)}, bf16[64,2048]{1,0:T(8,128)(2,1)}, bf16[64,2048]{1,0:T(8,128)(2,1)}, bf16[64,2048]{1,0:T(8,128)(2,1)S(1)}) custom-call(s32[3]{0:T(128)S(1)} %copy-done.13, bf16[256,2048]{1,0:T(8,128)(2,1)S(1)} %copy-done.2, bf16[32,2048]{1,0:T(8,128)(2,1)S(1)} %copy-done.9, ...), custom_call_target="tpu_custom_call" | custom-call | flops 2415919104 | bytes 12582912 | tf_op jit(solution)/shard_map/experts/pallas_call | solution.py:325
  73.3 2.6 %collective-permute-done.30 = bf16[16,2048]{1,0:T(8,128)(2,1)S(1)} collective-permute-done((bf16[16,2048]{1,0:T(8,128)(2,1)S(1)}, bf16[16,2048]{1,0:T(8,128)(2,1)S(1)}, u32[]{:S(2)}, u32[]{:S(2)}) %collective-permute-start.30) | collective-permute-done | bytes 65568 | tf_op jit(solution)/shard_map/ppermute | solution.py:248
  75.9 1.6 %collective-permute-start.12 = (bf16[64,2048]{1,0:T(8,128)(2,1)}, bf16[64,2048]{1,0:T(8,128)(2,1)S(1)}, u32[]{:S(2)}, u32[]{:S(2)}) collective-permute-start(bf16[64,2048]{1,0:T(8,128)(2,1)} %get-tuple-element.25), channel_id=1, source_target_pairs={{0,4},{1,5},{2,6},{3,7},{4,0},{5,1},{6,2},{7,3},{8,12},{9,13},{10,... | collective-permute-start | bytes 786440 | tf_op jit(solution)/shard_map/ppermute | solution.py:248
  78.2 1.6 %collective-permute-start.31 = (bf16[16,2048]{1,0:T(8,128)(2,1)S(1)}, bf16[16,2048]{1,0:T(8,128)(2,1)S(1)}, u32[]{:S(2)}, u32[]{:S(2)}) collective-permute-start(bf16[16,2048]{1,0:T(8,128)(2,1)S(1)} %add_convert_fusion.4), channel_id=1, source_target_pairs={{0,4},{1,5},{2,6},{3,7},{4,0},{5,1},{6,2},{7,3},{8,12},{9,13},{10,... | collective-permute-start | bytes 196616 | tf_op jit(solution)/shard_map/ppermute | solution.py:248
  80.6 2.2 %combine.3 = (bf16[32,2048]{1,0:T(8,128)(2,1)}, bf16[32,2048]{1,0:T(8,128)(2,1)}) custom-call(s32[3]{0:T(128)} %pad_add_fusion.place.refs_0_, bf16[4,104,128]{2,1,0:T(8,128)(2,1)} %copy-done.3, bf16[32,2048]{1,0:T(8,128)(2,1)} %constant_dynamic-slice_fusion.own, bf16[64,2048]{1,0:T(8,128)(2,1)} %copy-done.6, bf16[64,2048]{1,0:T(8,128)(2,1)} %copy-done.19, ...), custom_call_target="tpu_custom_call" | custom-call | bytes 3145728 | tf_op jit(solution)/shard_map/combine/pallas_call | solution.py:342
  82.8 2.1 %collective-permute-start.24 = (bf16[32,2048]{1,0:T(8,128)(2,1)}, bf16[32,2048]{1,0:T(8,128)(2,1)S(1)}, u32[]{:S(2)}, u32[]{:S(2)}) collective-permute-start(bf16[32,2048]{1,0:T(8,128)(2,1)} %get-tuple-element.34), channel_id=1, source_target_pairs={{0,24},{8,16},{16,8},{24,0},{1,25},{9,17},{17,9},{25,1},{2,26},{10... | collective-permute-start | bytes 393224 | tf_op jit(solution)/shard_map/ppermute | solution.py:251
  86.1 3.8 %collective-permute-done.12.refs_2_ = bf16[64,2048]{1,0:T(8,128)(2,1)S(1)} collective-permute-done((bf16[64,2048]{1,0:T(8,128)(2,1)}, bf16[64,2048]{1,0:T(8,128)(2,1)S(1)}, u32[]{:S(2)}, u32[]{:S(2)}) %collective-permute-start.12) | collective-permute-done | bytes 262176 | tf_op jit(solution)/shard_map/ppermute | solution.py:248
  90.6 2.3 %combine.2 = (f32[32,2048]{1,0:T(8,128)}, bf16[32,2048]{1,0:T(8,128)(2,1)}) custom-call(s32[3]{0:T(128)} %pad_add_fusion.place.refs_0_, bf16[4,104,128]{2,1,0:T(8,128)(2,1)} %copy-done.3, bf16[32,2048]{1,0:T(8,128)(2,1)} %constant_dynamic-slice_fusion.own, bf16[64,2048]{1,0:T(8,128)(2,1)} %copy-done.7, bf16[64,2048]{1,0:T(8,128)(2,1)} %copy-done.21, ...), custom_call_target="tpu_custom_call" | custom-call | bytes 3145728 | tf_op jit(solution)/shard_map/combine/pallas_call | solution.py:342
  92.9 2.0 %collective-permute-start.14 = (bf16[32,2048]{1,0:T(8,128)(2,1)}, bf16[32,2048]{1,0:T(8,128)(2,1)S(1)}, u32[]{:S(2)}, u32[]{:S(2)}) collective-permute-start(bf16[32,2048]{1,0:T(8,128)(2,1)} %get-tuple-element.28), channel_id=1, source_target_pairs={{0,8},{8,0},{16,24},{24,16},{1,9},{9,1},{17,25},{25,17},{2,10},{10... | collective-permute-start | bytes 393224 | tf_op jit(solution)/shard_map/ppermute | solution.py:251
  96.5 3.1 %collective-permute-done.14 = bf16[32,2048]{1,0:T(8,128)(2,1)S(1)} collective-permute-done((bf16[32,2048]{1,0:T(8,128)(2,1)}, bf16[32,2048]{1,0:T(8,128)(2,1)S(1)}, u32[]{:S(2)}, u32[]{:S(2)}) %collective-permute-start.14) | collective-permute-done | bytes 131104 | tf_op jit(solution)/shard_map/ppermute | solution.py:251
  100.7 1.8 %collective-permute-start.26 = (bf16[32,2048]{1,0:T(8,128)(2,1)S(1)}, bf16[32,2048]{1,0:T(8,128)(2,1)S(1)}, u32[]{:S(2)}, u32[]{:S(2)}) collective-permute-start(bf16[32,2048]{1,0:T(8,128)(2,1)S(1)} %add_convert_fusion.refs_0_), channel_id=1, source_target_pairs={{0,4},{1,5},{2,6},{3,7},{4,0},{5,1},{6,2},{7,3},{8,12},{9,13},{10,... | collective-permute-start | bytes 393224 | tf_op jit(solution)/shard_map/ppermute | solution.py:248
  102.6 1.6 %collective-permute-start.27 = (bf16[32,2048]{1,0:T(8,128)(2,1)S(1)}, bf16[32,2048]{1,0:T(8,128)(2,1)S(1)}, u32[]{:S(2)}, u32[]{:S(2)}) collective-permute-start(bf16[32,2048]{1,0:T(8,128)(2,1)S(1)} %add_convert_fusion.refs_0_), channel_id=1, source_target_pairs={{0,6},{1,7},{2,4},{3,5},{4,2},{5,3},{6,0},{7,1},{8,14},{9,15},{10,... | collective-permute-start | bytes 393224 | tf_op jit(solution)/shard_map/ppermute | solution.py:248
  104.7 1.9 %collective-permute-done.25.refs_1_ = bf16[32,2048]{1,0:T(8,128)(2,1)S(1)} collective-permute-done((bf16[32,2048]{1,0:T(8,128)(2,1)S(1)}, bf16[32,2048]{1,0:T(8,128)(2,1)S(1)}, u32[]{:S(2)}, u32[]{:S(2)}) %collective-permute-start.25) | collective-permute-done | bytes 131104 | tf_op jit(solution)/shard_map/ppermute | solution.py:248
  106.8 1.7 %collective-permute-done.27.refs_3_ = bf16[32,2048]{1,0:T(8,128)(2,1)S(1)} collective-permute-done((bf16[32,2048]{1,0:T(8,128)(2,1)S(1)}, bf16[32,2048]{1,0:T(8,128)(2,1)S(1)}, u32[]{:S(2)}, u32[]{:S(2)}) %collective-permute-start.27) | collective-permute-done | bytes 131104 | tf_op jit(solution)/shard_map/ppermute | solution.py:248
  108.5 1.6 %collective-permute-done.33 = bf16[16,2048]{1,0:T(8,128)(2,1)S(1)} collective-permute-done((bf16[16,2048]{1,0:T(8,128)(2,1)S(1)}, bf16[16,2048]{1,0:T(8,128)(2,1)S(1)}, u32[]{:S(2)}, u32[]{:S(2)}) %collective-permute-start.33) | collective-permute-done | bytes 65568 | tf_op jit(solution)/shard_map/ppermute | solution.py:251
  110.2 5.7 %gradients.1 = (bf16[1,2048,768]{2,1,0:T(8,128)(2,1)}, bf16[1,384,2048]{2,1,0:T(8,128)(2,1)}) custom-call(bf16[16,2048]{1,0:T(8,128)(2,1)S(1)} %copy-done.5, bf16[16,2048]{1,0:T(8,128)(2,1)S(1)} %copy-done.5, bf16[16,2048]{1,0:T(8,128)(2,1)S(1)} %add_convert_fusion.1.last_sum, f32[16,768]{1,0:T(8,128)S(1)} %copy-done.11, ...), custom_call_target="tpu_custom_call" | custom-call | flops 100663296 | bytes 7340032 | tf_op jit(solution)/shard_map/gradients/pallas_call | solution.py:383
  116.8 33.6 %gather.1 = bf16[256,2048]{1,0:T(8,128)(2,1)} custom-call(s32[3]{0:T(128)} %pad_add_fusion.place.refs_0_, bf16[32,2048]{1,0:T(8,128)(2,1)} %copy-done.14, bf16[32,2048]{1,0:T(8,128)(2,1)} %copy-done.16, bf16[32,2048]{1,0:T(8,128)(2,1)} %copy-done.17, bf16[32,2048]{1,0:T(8,128)(2,1)} %copy-done.18, bf16[128,2048]{1,0:T(8,128)(2,1)} %copy-done.15), custom_call_target="tpu_custom_call" | custom-call | bytes 2097152 | tf_op jit(solution)/shard_map/gather/pallas_call | solution.py:371
  (110 shorter events, 32.8 us)
Async XLA Ops:
  0.6 43.4 %collective-permute-start.9 = (bf16[1,2048,768]{2,1,0:T(8,128)(2,1)}, bf16[1,2048,768]{2,1,0:T(8,128)(2,1)}, u32[]{:S(2)}, u32[]{:S(2)}) collective-permute-start(bf16[1,2048,768]{2,1,0:T(8,128)(2,1)} %refs_7_.3), channel_id=1, source_target_pairs={{0,1},{1,0},{2,3},{3,2},{4,5},{5,4},{6,7},{7,6},{8,9},{9,8},{10,11... | collective-permute-start | bytes 9437192 | tf_op jit(solution)/shard_map/ppermute | solution.py:248
  1.2 42.9 %collective-permute-start.10 = (bf16[1,384,2048]{2,1,0:T(8,128)(2,1)}, bf16[1,384,2048]{2,1,0:T(8,128)(2,1)S(1)}, u32[]{:S(2)}, u32[]{:S(2)}) collective-permute-start(bf16[1,384,2048]{2,1,0:T(8,128)(2,1)} %down.1), channel_id=1, source_target_pairs={{0,1},{1,0},{2,3},{3,2},{4,5},{5,4},{6,7},{7,6},{8,9},{9,8},{10,11... | collective-permute-start | bytes 4718600 | tf_op jit(solution)/shard_map/ppermute | solution.py:248
  2.8 7.0 %collective-permute-start = (bf16[32,2048]{1,0:T(8,128)(2,1)}, bf16[32,2048]{1,0:T(8,128)(2,1)S(1)}, u32[]{:S(2)}, u32[]{:S(2)}) collective-permute-start(bf16[32,2048]{1,0:T(8,128)(2,1)} %constant_dynamic-slice_fusion.own), channel_id=1, source_target_pairs={{0,8},{8,0},{16,24},{24,16},{1,9},{9,1},{17,25},{25,17},{2,10},{10... | collective-permute-start | bytes 393224 | tf_op jit(solution)/shard_map/ppermute | solution.py:251
  11.0 5.7 %collective-permute-start.2 = (bf16[256,128]{1,0:T(8,128)(2,1)S(1)}, bf16[256,128]{1,0:T(8,128)(2,1)S(1)}, u32[]{:S(2)}, u32[]{:S(2)}) collective-permute-start(bf16[256,128]{1,0:T(8,128)(2,1)S(1)} %add.42), channel_id=1, source_target_pairs={{0,2},{1,3},{2,0},{3,1},{4,6},{5,7},{6,4},{7,5},{8,10},{9,11},{10,... | collective-permute-start | bytes 196616 | tf_op jit(solution)/shard_map/ppermute | solution.py:248
  12.8 13.1 %collective-permute-start.15 = (bf16[32,2048]{1,0:T(8,128)(2,1)}, bf16[32,2048]{1,0:T(8,128)(2,1)S(1)}, u32[]{:S(2)}, u32[]{:S(2)}) collective-permute-start(bf16[32,2048]{1,0:T(8,128)(2,1)} %constant_dynamic-slice_fusion.own), channel_id=1, source_target_pairs={{0,16},{8,24},{16,0},{24,8},{1,17},{9,25},{17,1},{25,9},{2,18},{10... | collective-permute-start | bytes 393224 | tf_op jit(solution)/shard_map/ppermute | solution.py:251
  15.4 15.5 %collective-permute-start.16 = (bf16[32,2048]{1,0:T(8,128)(2,1)}, bf16[32,2048]{1,0:T(8,128)(2,1)S(1)}, u32[]{:S(2)}, u32[]{:S(2)}) collective-permute-start(bf16[32,2048]{1,0:T(8,128)(2,1)} %constant_dynamic-slice_fusion.own), channel_id=1, source_target_pairs={{0,24},{8,16},{16,8},{24,0},{1,25},{9,17},{17,9},{25,1},{2,26},{10... | collective-permute-start | bytes 393224 | tf_op jit(solution)/shard_map/ppermute | solution.py:251
  16.7 4.3 %collective-permute-start.3 = (bf16[256,128]{1,0:T(8,128)(2,1)S(1)}, bf16[256,128]{1,0:T(8,128)(2,1)S(1)}, u32[]{:S(2)}, u32[]{:S(2)}) collective-permute-start(bf16[256,128]{1,0:T(8,128)(2,1)S(1)} %add.43), channel_id=1, source_target_pairs={{0,4},{1,5},{2,6},{3,7},{4,0},{5,1},{6,2},{7,3},{8,12},{9,13},{10,... | collective-permute-start | bytes 196616 | tf_op jit(solution)/shard_map/ppermute | solution.py:248
  29.1 5.5 %collective-permute-start.5 = (bf16[2,104,128]{2,1,0:T(8,128)(2,1)S(1)}, bf16[2,104,128]{2,1,0:T(8,128)(2,1)S(1)}, u32[]{:S(2)}, u32[]{:S(2)}) collective-permute-start(bf16[2,104,128]{2,1,0:T(8,128)(2,1)S(1)} %maximum_select_fusion.1), channel_id=1, source_target_pairs={{0,16},{8,24},{16,0},{24,8},{1,17},{9,25},{17,1},{25,9},{2,18},{10... | collective-permute-start | bytes 159752 | tf_op jit(solution)/shard_map/ppermute | solution.py:251
  31.5 9.3 %collective-permute-start.17 = (bf16[64,2048]{1,0:T(8,128)(2,1)}, bf16[64,2048]{1,0:T(8,128)(2,1)}, u32[]{:S(2)}, u32[]{:S(2)}) collective-permute-start(bf16[64,2048]{1,0:T(8,128)(2,1)} %constant_dynamic-update-slice_fusion), channel_id=1, source_target_pairs={{0,2},{1,3},{2,0},{3,1},{4,6},{5,7},{6,4},{7,5},{8,10},{9,11},{10,... | collective-permute-start | bytes 786440 | tf_op jit(solution)/shard_map/ppermute | solution.py:248
  32.8 10.5 %collective-permute-start.18 = (bf16[64,2048]{1,0:T(8,128)(2,1)}, bf16[64,2048]{1,0:T(8,128)(2,1)}, u32[]{:S(2)}, u32[]{:S(2)}) collective-permute-start(bf16[64,2048]{1,0:T(8,128)(2,1)} %constant_dynamic-update-slice_fusion), channel_id=1, source_target_pairs={{0,4},{1,5},{2,6},{3,7},{4,0},{5,1},{6,2},{7,3},{8,12},{9,13},{10,... | collective-permute-start | bytes 786440 | tf_op jit(solution)/shard_map/ppermute | solution.py:248
  34.6 9.4 %collective-permute-start.19 = (bf16[64,2048]{1,0:T(8,128)(2,1)}, bf16[64,2048]{1,0:T(8,128)(2,1)}, u32[]{:S(2)}, u32[]{:S(2)}) collective-permute-start(bf16[64,2048]{1,0:T(8,128)(2,1)} %constant_dynamic-update-slice_fusion), channel_id=1, source_target_pairs={{0,6},{1,7},{2,4},{3,5},{4,2},{5,3},{6,0},{7,1},{8,14},{9,15},{10,... | collective-permute-start | bytes 786440 | tf_op jit(solution)/shard_map/ppermute | solution.py:248
  54.0 4.4 %collective-permute-start.29 = (bf16[16,2048]{1,0:T(8,128)(2,1)S(1)}, bf16[16,2048]{1,0:T(8,128)(2,1)S(1)}, u32[]{:S(2)}, u32[]{:S(2)}) collective-permute-start(bf16[16,2048]{1,0:T(8,128)(2,1)S(1)} %get-tuple-element.36), channel_id=1, source_target_pairs={{0,1},{1,0},{2,3},{3,2},{4,5},{5,4},{6,7},{7,6},{8,9},{9,8},{10,11... | collective-permute-start | bytes 196616 | tf_op jit(solution)/shard_map/ppermute | solution.py:248
  54.0 6.4 %collective-permute-start.6 = (bf16[32,2048]{1,0:T(8,128)(2,1)S(1)}, bf16[32,2048]{1,0:T(8,128)(2,1)S(1)}, u32[]{:S(2)}, u32[]{:S(2)}) collective-permute-start(bf16[32,2048]{1,0:T(8,128)(2,1)S(1)} %copy-done.9), channel_id=1, source_target_pairs={{0,2},{1,3},{2,0},{3,1},{4,6},{5,7},{6,4},{7,5},{8,10},{9,11},{10,... | collective-permute-start | bytes 393224 | tf_op jit(solution)/shard_map/ppermute | solution.py:248
  54.9 7.6 %collective-permute-start.7 = (bf16[32,2048]{1,0:T(8,128)(2,1)S(1)}, bf16[32,2048]{1,0:T(8,128)(2,1)S(1)}, u32[]{:S(2)}, u32[]{:S(2)}) collective-permute-start(bf16[32,2048]{1,0:T(8,128)(2,1)S(1)} %copy-done.9), channel_id=1, source_target_pairs={{0,4},{1,5},{2,6},{3,7},{4,0},{5,1},{6,2},{7,3},{8,12},{9,13},{10,... | collective-permute-start | bytes 393224 | tf_op jit(solution)/shard_map/ppermute | solution.py:248
  56.3 8.1 %collective-permute-start.8 = (bf16[32,2048]{1,0:T(8,128)(2,1)S(1)}, bf16[32,2048]{1,0:T(8,128)(2,1)S(1)}, u32[]{:S(2)}, u32[]{:S(2)}) collective-permute-start(bf16[32,2048]{1,0:T(8,128)(2,1)S(1)} %copy-done.9), channel_id=1, source_target_pairs={{0,6},{1,7},{2,4},{3,5},{4,2},{5,3},{6,0},{7,1},{8,14},{9,15},{10,... | collective-permute-start | bytes 393224 | tf_op jit(solution)/shard_map/ppermute | solution.py:248
  57.5 20.0 %collective-permute-start.20 = (bf16[64,2048]{1,0:T(8,128)(2,1)S(1)}, bf16[64,2048]{1,0:T(8,128)(2,1)S(1)}, u32[]{:S(2)}, u32[]{:S(2)}) collective-permute-start(bf16[64,2048]{1,0:T(8,128)(2,1)S(1)} %get-tuple-element.30), channel_id=1, source_target_pairs={{0,2},{1,3},{2,0},{3,1},{4,6},{5,7},{6,4},{7,5},{8,10},{9,11},{10,... | collective-permute-start | bytes 786440 | tf_op jit(solution)/shard_map/ppermute | solution.py:248
  58.3 19.8 %collective-permute-start.21 = (bf16[64,2048]{1,0:T(8,128)(2,1)S(1)}, bf16[64,2048]{1,0:T(8,128)(2,1)S(1)}, u32[]{:S(2)}, u32[]{:S(2)}) collective-permute-start(bf16[64,2048]{1,0:T(8,128)(2,1)S(1)} %get-tuple-element.31), channel_id=1, source_target_pairs={{0,4},{1,5},{2,6},{3,7},{4,0},{5,1},{6,2},{7,3},{8,12},{9,13},{10,... | collective-permute-start | bytes 786440 | tf_op jit(solution)/shard_map/ppermute | solution.py:248
  60.3 19.5 %collective-permute-start.22 = (bf16[64,2048]{1,0:T(8,128)(2,1)S(1)}, bf16[64,2048]{1,0:T(8,128)(2,1)S(1)}, u32[]{:S(2)}, u32[]{:S(2)}) collective-permute-start(bf16[64,2048]{1,0:T(8,128)(2,1)S(1)} %get-tuple-element.32), channel_id=1, source_target_pairs={{0,6},{1,7},{2,4},{3,5},{4,2},{5,3},{6,0},{7,1},{8,14},{9,15},{10,... | collective-permute-start | bytes 786440 | tf_op jit(solution)/shard_map/ppermute | solution.py:248
  62.5 13.4 %collective-permute-start.30 = (bf16[16,2048]{1,0:T(8,128)(2,1)S(1)}, bf16[16,2048]{1,0:T(8,128)(2,1)S(1)}, u32[]{:S(2)}, u32[]{:S(2)}) collective-permute-start(bf16[16,2048]{1,0:T(8,128)(2,1)S(1)} %add_convert_fusion.5), channel_id=1, source_target_pairs={{0,2},{1,3},{2,0},{3,1},{4,6},{5,7},{6,4},{7,5},{8,10},{9,11},{10,... | collective-permute-start | bytes 196616 | tf_op jit(solution)/shard_map/ppermute | solution.py:248
  72.7 12.3 %collective-permute-start.11 = (bf16[64,2048]{1,0:T(8,128)(2,1)}, bf16[64,2048]{1,0:T(8,128)(2,1)S(1)}, u32[]{:S(2)}, u32[]{:S(2)}) collective-permute-start(bf16[64,2048]{1,0:T(8,128)(2,1)} %get-tuple-element.24), channel_id=1, source_target_pairs={{0,2},{1,3},{2,0},{3,1},{4,6},{5,7},{6,4},{7,5},{8,10},{9,11},{10,... | collective-permute-start | bytes 786440 | tf_op jit(solution)/shard_map/ppermute | solution.py:248
  75.9 13.9 %collective-permute-start.12 = (bf16[64,2048]{1,0:T(8,128)(2,1)}, bf16[64,2048]{1,0:T(8,128)(2,1)S(1)}, u32[]{:S(2)}, u32[]{:S(2)}) collective-permute-start(bf16[64,2048]{1,0:T(8,128)(2,1)} %get-tuple-element.25), channel_id=1, source_target_pairs={{0,4},{1,5},{2,6},{3,7},{4,0},{5,1},{6,2},{7,3},{8,12},{9,13},{10,... | collective-permute-start | bytes 786440 | tf_op jit(solution)/shard_map/ppermute | solution.py:248
  77.5 12.3 %collective-permute-start.13 = (bf16[64,2048]{1,0:T(8,128)(2,1)S(1)}, bf16[64,2048]{1,0:T(8,128)(2,1)S(1)}, u32[]{:S(2)}, u32[]{:S(2)}) collective-permute-start(bf16[64,2048]{1,0:T(8,128)(2,1)S(1)} %get-tuple-element.26), channel_id=1, source_target_pairs={{0,6},{1,7},{2,4},{3,5},{4,2},{5,3},{6,0},{7,1},{8,14},{9,15},{10,... | collective-permute-start | bytes 786440 | tf_op jit(solution)/shard_map/ppermute | solution.py:248
  78.2 16.8 %collective-permute-start.31 = (bf16[16,2048]{1,0:T(8,128)(2,1)S(1)}, bf16[16,2048]{1,0:T(8,128)(2,1)S(1)}, u32[]{:S(2)}, u32[]{:S(2)}) collective-permute-start(bf16[16,2048]{1,0:T(8,128)(2,1)S(1)} %add_convert_fusion.4), channel_id=1, source_target_pairs={{0,4},{1,5},{2,6},{3,7},{4,0},{5,1},{6,2},{7,3},{8,12},{9,13},{10,... | collective-permute-start | bytes 196616 | tf_op jit(solution)/shard_map/ppermute | solution.py:248
  82.8 12.3 %collective-permute-start.24 = (bf16[32,2048]{1,0:T(8,128)(2,1)}, bf16[32,2048]{1,0:T(8,128)(2,1)S(1)}, u32[]{:S(2)}, u32[]{:S(2)}) collective-permute-start(bf16[32,2048]{1,0:T(8,128)(2,1)} %get-tuple-element.34), channel_id=1, source_target_pairs={{0,24},{8,16},{16,8},{24,0},{1,25},{9,17},{17,9},{25,1},{2,26},{10... | collective-permute-start | bytes 393224 | tf_op jit(solution)/shard_map/ppermute | solution.py:251
  84.9 11.6 %collective-permute-start.23 = (bf16[32,2048]{1,0:T(8,128)(2,1)}, bf16[32,2048]{1,0:T(8,128)(2,1)S(1)}, u32[]{:S(2)}, u32[]{:S(2)}) collective-permute-start(bf16[32,2048]{1,0:T(8,128)(2,1)} %get-tuple-element.33), channel_id=1, source_target_pairs={{0,16},{8,24},{16,0},{24,8},{1,17},{9,25},{17,1},{25,9},{2,18},{10... | collective-permute-start | bytes 393224 | tf_op jit(solution)/shard_map/ppermute | solution.py:251
  92.9 6.7 %collective-permute-start.14 = (bf16[32,2048]{1,0:T(8,128)(2,1)}, bf16[32,2048]{1,0:T(8,128)(2,1)S(1)}, u32[]{:S(2)}, u32[]{:S(2)}) collective-permute-start(bf16[32,2048]{1,0:T(8,128)(2,1)} %get-tuple-element.28), channel_id=1, source_target_pairs={{0,8},{8,0},{16,24},{24,16},{1,9},{9,1},{17,25},{25,17},{2,10},{10... | collective-permute-start | bytes 393224 | tf_op jit(solution)/shard_map/ppermute | solution.py:251
  95.0 9.2 %collective-permute-start.32 = (bf16[16,2048]{1,0:T(8,128)(2,1)S(1)}, bf16[16,2048]{1,0:T(8,128)(2,1)S(1)}, u32[]{:S(2)}, u32[]{:S(2)}) collective-permute-start(bf16[16,2048]{1,0:T(8,128)(2,1)S(1)} %add_convert_fusion.3), channel_id=1, source_target_pairs={{0,8},{8,0},{16,24},{24,16},{1,9},{9,1},{17,25},{25,17},{2,10},{10... | collective-permute-start | bytes 196616 | tf_op jit(solution)/shard_map/ppermute | solution.py:251
  100.6 5.9 %collective-permute-start.25 = (bf16[32,2048]{1,0:T(8,128)(2,1)S(1)}, bf16[32,2048]{1,0:T(8,128)(2,1)S(1)}, u32[]{:S(2)}, u32[]{:S(2)}) collective-permute-start(bf16[32,2048]{1,0:T(8,128)(2,1)S(1)} %add_convert_fusion.refs_0_), channel_id=1, source_target_pairs={{0,2},{1,3},{2,0},{3,1},{4,6},{5,7},{6,4},{7,5},{8,10},{9,11},{10,... | collective-permute-start | bytes 393224 | tf_op jit(solution)/shard_map/ppermute | solution.py:248
  100.7 6.0 %collective-permute-start.26 = (bf16[32,2048]{1,0:T(8,128)(2,1)S(1)}, bf16[32,2048]{1,0:T(8,128)(2,1)S(1)}, u32[]{:S(2)}, u32[]{:S(2)}) collective-permute-start(bf16[32,2048]{1,0:T(8,128)(2,1)S(1)} %add_convert_fusion.refs_0_), channel_id=1, source_target_pairs={{0,4},{1,5},{2,6},{3,7},{4,0},{5,1},{6,2},{7,3},{8,12},{9,13},{10,... | collective-permute-start | bytes 393224 | tf_op jit(solution)/shard_map/ppermute | solution.py:248
  102.6 5.9 %collective-permute-start.27 = (bf16[32,2048]{1,0:T(8,128)(2,1)S(1)}, bf16[32,2048]{1,0:T(8,128)(2,1)S(1)}, u32[]{:S(2)}, u32[]{:S(2)}) collective-permute-start(bf16[32,2048]{1,0:T(8,128)(2,1)S(1)} %add_convert_fusion.refs_0_), channel_id=1, source_target_pairs={{0,6},{1,7},{2,4},{3,5},{4,2},{5,3},{6,0},{7,1},{8,14},{9,15},{10,... | collective-permute-start | bytes 393224 | tf_op jit(solution)/shard_map/ppermute | solution.py:248
  104.2 5.9 %collective-permute-start.33 = (bf16[16,2048]{1,0:T(8,128)(2,1)S(1)}, bf16[16,2048]{1,0:T(8,128)(2,1)S(1)}, u32[]{:S(2)}, u32[]{:S(2)}) collective-permute-start(bf16[16,2048]{1,0:T(8,128)(2,1)S(1)} %add_convert_fusion.2), channel_id=1, source_target_pairs={{0,16},{8,24},{16,0},{24,8},{1,17},{9,25},{17,1},{25,9},{2,18},{10... | collective-permute-start | bytes 196616 | tf_op jit(solution)/shard_map/ppermute | solution.py:251
  108.5 7.5 %collective-permute-start.28 = (bf16[128,2048]{1,0:T(8,128)(2,1)S(1)}, bf16[128,2048]{1,0:T(8,128)(2,1)S(1)}, u32[]{:S(2)}, u32[]{:S(2)}) collective-permute-start(bf16[128,2048]{1,0:T(8,128)(2,1)S(1)} %pad_maximum_fusion), channel_id=1, source_target_pairs={{0,1},{1,0},{2,3},{3,2},{4,5},{5,4},{6,7},{7,6},{8,9},{9,8},{10,11... | collective-permute-start | bytes 1572872 | tf_op jit(solution)/shard_map/ppermute | solution.py:248
  (27 other events, 302.3 us)

commit v4 on v3

v4 whole, which is shorter than its diff:
```python
import functools

import jax
import jax.numpy as jnp
from jax import lax
from jax.experimental import pallas as pl
from jax.experimental.pallas import tpu as pltpu
from jax.sharding import PartitionSpec as P

logit_divisor = 0.05
grad_scale = 256.0
epsilon = 1e-06
lanes = 128
tail = 16
bf16 = jnp.bfloat16
f32 = jnp.float32

anywhere = pl.BlockSpec(memory_space=pl.ANY)
in_vmem = pl.BlockSpec(memory_space=pltpu.VMEM)
in_smem = pl.BlockSpec(memory_space=pltpu.SMEM)


def params(mebibytes):
    return pltpu.CompilerParams(vmem_limit_bytes=mebibytes << 20)


def cost(flops, moved):
    return pl.CostEstimate(flops=flops, transcendentals=0, bytes_accessed=moved)


def dot(left, right, dims=((1,), (0,)), precision=None):
    return lax.dot_general(
        left, right, (dims, ((), ())), precision=precision, preferred_element_type=f32
    )


def doublings(count):
    steps = [1 << bit for bit in range((count - 1).bit_length())]
    assert 1 << len(steps) == count
    return steps


def column(table, wanted):
    index = lax.broadcasted_iota(jnp.int32, table.shape, 1)
    return jnp.sum(jnp.where(index == wanted, table, 0.0), axis=1, keepdims=True)


def pack_kernel(seq_dev, place, positives, ids, gates, tokens, out, tile, rows, sems):
    part_rows, width = out.shape[0], tokens.shape[1]
    tok_dev = tokens.shape[0]
    seq_length = tok_dev // seq_dev
    share = rows.shape[2]
    column_at = pl.multiple_of(place[1] // 2 * share, lanes)
    start = pl.multiple_of(place[1] * part_rows, part_rows)
    copies = [
        pltpu.make_async_copy(
            tokens.at[pl.ds((seq + 1) * seq_length - tail, tail), pl.ds(column_at, share)],
            rows.at[seq],
            sems.at[seq],
        )
        for seq in range(seq_dev)
    ]
    own = pltpu.make_async_copy(
        tokens.at[pl.ds(start, part_rows)], out.at[:, pl.ds(0, width)], sems.at[seq_dev]
    )
    own.start()
    for copy in copies:
        copy.start()
    row_index = lax.broadcasted_iota(jnp.int32, (lanes, lanes), 0)
    diagonal = row_index == lax.broadcasted_iota(jnp.int32, (lanes, lanes), 1)
    note_rows = tok_dev // lanes
    tile[...] = jnp.zeros_like(tile)
    for index in range(note_rows):
        block = slice(index * lanes, (index + 1) * lanes)
        for offset, values in ((0, ids[block, :].astype(f32)), (note_rows, gates[block, :])):
            line = jnp.sum(jnp.where(diagonal, values, 0.0), axis=0, keepdims=True)
            tile[offset + index : offset + index + 1, :] = line
    for seq in range(seq_dev):
        row = 2 * note_rows + seq
        tile[row : row + 1, :] = jnp.full((1, lanes), positives[seq], jnp.int32).astype(f32)
    base = part_rows - seq_dev * (share // lanes)
    for seq in range(seq_dev):
        copies[seq].wait()
        values = rows[seq].astype(f32)
        for chunk in range(share // lanes):
            row = base + chunk * seq_dev + seq
            tile[row : row + 1, :] = values[tail - 1 : tail, chunk * lanes : (chunk + 1) * lanes]
    out[:, width:] = tile[...].astype(bf16)
    own.wait()


def table_kernel(layout, place, *refs):
    seq_dev, tok_dev, where_tiles, n_parts = layout
    parts = refs[:n_parts]
    kept, sent, last_rows, partners, tokens, routes, marks = refs[n_parts:]
    part_rows = parts[0].shape[0]
    dp_count, chunks = tokens.shape[:2]
    note_rows = tok_dev // lanes
    seq_length = tok_dev // seq_dev
    chips = len(where_tiles[0])
    share_chunks = chunks // chips
    base = part_rows - seq_dev * share_chunks
    lane_index = lax.broadcasted_iota(jnp.int32, (part_rows, lanes), 1)
    row_index = lax.broadcasted_iota(jnp.int32, (part_rows, lanes), 0)

    def dense_rows(tile, lane):
        start = lane * part_rows
        picked = lane_index == row_index + start % lanes
        found = []
        for offset in (0, note_rows):
            line = tile[offset : offset + 1, :]
            for index in range(1, note_rows):
                other = tile[offset + index : offset + index + 1, :]
                line = jnp.where(start // lanes == index, other, line)
            found.append(jnp.sum(jnp.where(picked, line, 0.0), axis=1, keepdims=True))
        return jnp.where(lane_index.astype(f32) == found[0], found[1], 0.0)

    for hop in range(dp_count):
        plane = place[0] ^ hop
        sums = [None, None]
        for chip in range(chips):
            source, row, at = where_tiles[hop][chip]
            tile = parts[source][row : row + part_rows, at : at + lanes].astype(f32)
            for index, lane in enumerate((place[1], place[1] ^ 1)):
                value = dense_rows(tile, lane)
                sums[index] = value if chip == 0 else sums[index] + value
            for seq in range(seq_dev):
                at_token = (seq + 1) * seq_length - 1
                row = at_token // lanes
                here = lane_index[:1] == at_token % lanes
                expert, gate = [
                    jnp.sum(
                        jnp.where(here, tile[offset + row : offset + row + 1, :], 0.0),
                        axis=1,
                        keepdims=True,
                    )
                    for offset in (0, note_rows)
                ]
                value = jnp.where(lane_index[:1].astype(f32) == expert, gate, 0.0)
                if chip:
                    value = value + routes[plane, seq : seq + 1, :]
                routes[plane, seq : seq + 1, :] = value
            if chip == 0:
                marks[plane, 0:seq_dev, :] = tile[2 * note_rows : 2 * note_rows + seq_dev, :]
            first = ((place[1] // 2) ^ chip) * share_chunks
            for chunk in range(share_chunks):
                row = base + chunk * seq_dev
                tokens[plane, first + chunk, 0:seq_dev, :] = tile[row : row + seq_dev, :]
        at = slice(hop * part_rows, (hop + 1) * part_rows)
        kept[at, :] = sums[0].astype(bf16)
        sent[at, :] = sums[1].astype(bf16)
    last = dp_count * part_rows
    joined, shared = [], []
    for plane in range(dp_count):
        shared.append(routes[plane, 0:seq_dev, :])
        partners[plane * seq_dev : (plane + 1) * seq_dev, :] = marks[plane, 0:seq_dev, :]
        lines = [tokens[plane, chunk, 0:seq_dev, :] for chunk in range(chunks)]
        joined.append(jnp.concatenate(lines, axis=1))
    last_rows[...] = jnp.concatenate(joined, axis=0).astype(bf16)
    seqs = dp_count * seq_dev
    value = jnp.concatenate(shared, axis=0).astype(bf16)
    kept[last : last + seqs, :] = value
    sent[last : last + seqs, :] = value


def hidden_parts(projected):
    half_width = projected.shape[1] // 2
    gate, up = projected[:, :half_width], projected[:, half_width:]
    sigmoid_gate = jax.nn.sigmoid(gate)
    return gate, up, sigmoid_gate, gate * sigmoid_gate


def expert_kernel(layout, *refs):
    chips, part_rows, near, n_parts = layout
    refs = list(refs)
    place = refs.pop(0)
    tokens = refs.pop(0) if near else None
    parts, refs = refs[:n_parts], refs[n_parts:]
    weights, refs = refs[:4], refs[4:]
    outs, (rows,) = refs[:chips], refs[chips:]
    count, width = outs[0].shape[0] // part_rows, outs[0].shape[1]
    block = count * part_rows
    if near:
        for chip in range(chips):
            start = pl.multiple_of((place[1] ^ (2 * chip)) * part_rows, part_rows)
            at = chip * block
            rows[at : at + part_rows, :] = tokens[pl.ds(start, part_rows), :]
    own_parts = count - 1 if near else count
    for index in range(own_parts):
        at = (index + count - own_parts) * part_rows
        rows[at : at + part_rows, :] = parts[index][:, :width]
    for chip in range(1, chips):
        at = chip * block + (count - own_parts) * part_rows
        rows[at : at + own_parts * part_rows, :] = parts[own_parts + chip - 1][:, :width]
    result = None
    for half in range(2):
        w_in, w_out = weights[2 * half], weights[2 * half + 1]
        _, up, _, activated = hidden_parts(dot(rows[...], w_in[0]))
        part = dot((activated * up).astype(bf16), w_out[0])
        result = part if half == 0 else result + part
    for chip in range(chips):
        outs[chip][...] = result[chip * block : (chip + 1) * block].astype(bf16)


def last_kernel(place, rows, kept, found, w_in, w_out, projected, out, weights):
    seqs = rows.shape[0]
    last = kept.shape[0] - seqs
    values = dot(rows[...], w_in[0])
    projected[...] = values
    _, up, _, activated = hidden_parts(values)
    half_out = dot((activated * up).astype(bf16), w_out[0]).astype(bf16).astype(f32)
    weight = column(kept[last:, :].astype(f32) + found[last:, :].astype(f32), place[2])
    out[...] = (weight * half_out).astype(bf16)
    weights[...] = jnp.broadcast_to(weight, weights.shape)


def combine_kernel(layout, place, kept, found, own, *refs):
    chips, part_rows, group, n_outs = layout
    parts, outs = refs[:chips], refs[chips : chips + n_outs]
    first_expert = place[2] - place[1] // 2
    width = parts[0].shape[1]
    for index, hop in enumerate(group):
        at = slice(hop * part_rows, (hop + 1) * part_rows)
        table = kept[at, :].astype(f32) + found[at, :].astype(f32)
        rows = slice(index * part_rows, (index + 1) * part_rows)
        total = own[:, :width].astype(f32) if hop == 0 else None
        for chip in range(chips):
            weight = column(table, first_expert + ((place[1] // 2) ^ chip))
            term = weight * parts[chip][rows, :].astype(f32)
            total = term if total is None else total + term
        outs[index][...] = total.astype(outs[index].dtype)


def gather_kernel(chips, place, *refs):
    out = refs[-1]
    part_rows = refs[0].shape[0]
    for chip in range(chips):
        lane = place[1] ^ (2 * chip)
        own = pl.multiple_of(lane * part_rows, part_rows)
        out[pl.ds(own, part_rows), :] = refs[chip][...]
        other = pl.multiple_of((lane ^ 1) * part_rows, part_rows)
        out[pl.ds(other, part_rows), :] = refs[chips + chip][...]


def gradient_kernel(
    last_all,
    last_block,
    last_sum,
    projected,
    weights,
    partners,
    down,
    grad_in,
    grad_out,
    route,
    hidden,
    slope,
):
    step = pl.program_id(0)
    half_width = down.shape[1]
    block = grad_out.shape[2]

    @pl.when(step == 0)
    def _():
        layer_last = (last_all[...].astype(f32) + last_sum[...].astype(f32)).astype(bf16)
        values = layer_last.astype(f32)
        count = values.shape[0]
        norms = jnp.sqrt(jnp.sum(values * values, axis=1, keepdims=True) + epsilon)
        unit = values / norms
        scores = dot(unit, unit, ((1,), (1,)), lax.Precision.HIGHEST) / logit_divisor
        row = lax.broadcasted_iota(jnp.int32, (count, count), 0)
        col = lax.broadcasted_iota(jnp.int32, (count, count), 1)
        exp_scores = jnp.where(row != col, jnp.exp(scores), 0.0)
        probabilities = exp_scores / jnp.sum(exp_scores, axis=1, keepdims=True)
        partner = partners[:, :1].astype(jnp.int32)
        coefficient = grad_scale * (probabilities - jnp.where(col == partner, 1.0, 0.0))
        high = lax.Precision.HIGHEST
        grad_unit = (
            dot(coefficient, unit, ((1,), (0,)), high) + dot(coefficient, unit, ((0,), (0,)), high)
        ) / logit_divisor
        projection = jnp.sum(unit * grad_unit, axis=1, keepdims=True)
        grad_last = (grad_unit - unit * projection) / norms
        route_grad = (weights[:, :1] * grad_last).astype(bf16)
        for index in range(route.shape[0]):
            route[index] = route_grad[:, index * block : (index + 1) * block]
        grad_hidden = dot(route_grad, down[0], ((1,), (1,)))
        gate, up, sigmoid_gate, activated = hidden_parts(projected[...])
        hidden[...] = (activated * up).astype(bf16)
        gate_slope = sigmoid_gate * (1.0 + gate * (1.0 - sigmoid_gate))
        slope[:, :half_width] = (grad_hidden * up * gate_slope).astype(bf16)
        slope[:, half_width:] = (grad_hidden * activated).astype(bf16)

    grad_in[0] = dot(last_block[...], slope[...], ((0,), (0,))).astype(bf16)
    grad_out[0] = dot(hidden[...], route[step], ((0,), (0,))).astype(bf16)


def body(tokens, expert_ids, gates, positives, gate_up, down):
    dp_count = lax.axis_size("dp")
    expert_count = lax.axis_size("expert")
    chips = expert_count // 2
    experts = dp_count * chips
    tok_dev, width = tokens.shape
    half_width = down.shape[1]
    seq_dev = positives.shape[0]
    seqs = dp_count * seq_dev
    seq_length = tok_dev // seq_dev
    part_rows = tok_dev // expert_count
    plane = lax.axis_index("dp")
    lane = lax.axis_index("expert")
    place = jnp.stack([plane, lane, plane * chips + lane // 2]).astype(jnp.int32)
    assert experts <= lanes and seq_length % tail == 0

    def to_lane(value, step):
        return lax.ppermute(value, "expert", [(j, j ^ step) for j in range(expert_count)])

    def to_plane(value, step):
        return lax.ppermute(value, "dp", [(p, p ^ step) for p in range(dp_count)])

    chip_steps = [2 * step for step in range(1, chips)]
    groups = [range(first, min(first + 2, dp_count)) for first in range(0, dp_count, 2)]

    share = width // chips
    packed = pl.pallas_call(
        functools.partial(pack_kernel, seq_dev),
        out_shape=jax.ShapeDtypeStruct((part_rows, width + lanes), bf16),
        in_specs=[in_smem, in_smem, in_vmem, in_vmem, anywhere],
        out_specs=in_vmem,
        scratch_shapes=[
            pltpu.VMEM((part_rows, lanes), f32),
            pltpu.VMEM((seq_dev, tail, share), bf16),
            pltpu.SemaphoreType.DMA((seq_dev + 1,)),
        ],
        compiler_params=params(4),
        cost_estimate=cost(0, 1 << 19),
        name="pack",
    )(place, positives, expert_ids, gates, tokens)
    arrivals = {hop: to_plane(packed, hop) for hop in range(1, dp_count)}
    mate_in = to_lane(gate_up, 1)
    mate_out = to_lane(down, 1)
    weights = (gate_up, down, mate_in, mate_out)

    groups.reverse()
    far_parts = []
    tiles = []
    where_tiles = [[None] * chips for _ in range(dp_count)]
    for group in groups:
        own = [arrivals[hop] for hop in group if hop]
        if group[0] == 0:
            joined = jnp.concatenate(own + [packed[:, width:]], axis=1)
        else:
            joined = jnp.concatenate(own, axis=0)
        received = [to_lane(joined, step) for step in chip_steps]
        far_parts.append(own + received)
        for index, hop in enumerate(group):
            tiles.append(packed if hop == 0 else arrivals[hop])
            where_tiles[hop][0] = (len(tiles) - 1, 0, width)
            for chip in range(1, chips):
                if group[0] == 0:
                    spot = (0, width if hop else width + lanes)
                else:
                    spot = (index * part_rows, width)
                where_tiles[hop][chip] = (chip,) + spot
        first = len(tiles)
        tiles += received
        for hop in group:
            for chip in range(1, chips):
                where_tiles[hop][chip] = (first + chip - 1,) + where_tiles[hop][chip][1:]

    def expert(group, parts, place):
        near = group[0] == 0
        block = len(group) * part_rows
        total = chips * block
        operands = [place] + [tokens] * near + parts + list(weights)
        return pl.pallas_call(
            functools.partial(expert_kernel, (chips, part_rows, near, len(parts))),
            out_shape=[jax.ShapeDtypeStruct((block, width), bf16)] * chips,
            in_specs=[in_smem] + [in_vmem] * (len(operands) - 1),
            out_specs=[in_vmem] * chips,
            scratch_shapes=[pltpu.VMEM((total, width), bf16)],
            compiler_params=params(32),
            cost_estimate=cost(2 * total * width * 6 * half_width, 12 << 20),
            name="experts",
        )(*operands)

    outs = []
    after = place
    for group, parts in zip(groups, far_parts):
        outs.append(expert(group, parts, after))
        after, _ = lax.optimization_barrier((place, outs[-1][0]))
    table_place, _ = lax.optimization_barrier((place, outs[0][0]))

    table_rows = dp_count * part_rows + seqs
    chunks = width // lanes
    sublanes = -(-seq_dev // 8) * 8
    kept, sent, last_all, partners = pl.pallas_call(
        functools.partial(table_kernel, (seq_dev, tok_dev, where_tiles, len(tiles))),
        out_shape=[
            jax.ShapeDtypeStruct((table_rows, lanes), bf16),
            jax.ShapeDtypeStruct((table_rows, lanes), bf16),
            jax.ShapeDtypeStruct((seqs, width), bf16),
            jax.ShapeDtypeStruct((seqs, lanes), f32),
        ],
        in_specs=[in_smem] + [in_vmem] * len(tiles),
        out_specs=[in_vmem] * 4,
        scratch_shapes=[
            pltpu.VMEM((dp_count, chunks, sublanes, lanes), f32),
            pltpu.VMEM((dp_count, sublanes, lanes), f32),
            pltpu.VMEM((dp_count, sublanes, lanes), f32),
        ],
        compiler_params=params(48 if dp_count > 8 else 12),
        cost_estimate=cost(0, 1 << 20),
        name="tables",
    )(table_place, *tiles)
    found = to_lane(sent, 1)

    last_projected, last_sum, last_weights = pl.pallas_call(
        last_kernel,
        out_shape=[
            jax.ShapeDtypeStruct((seqs, 2 * half_width), f32),
            jax.ShapeDtypeStruct((seqs, width), bf16),
            jax.ShapeDtypeStruct((seqs, lanes), f32),
        ],
        in_specs=[in_smem] + [in_vmem] * 5,
        out_specs=[in_vmem] * 3,
        compiler_params=params(16),
        cost_estimate=cost(2 * seqs * width * 3 * half_width, 5 << 20),
        name="last_rows",
    )(place, last_all, kept, found, gate_up, down)

    def combine(group, parts):
        out_shape = [
            jax.ShapeDtypeStruct((part_rows, width), bf16 if hop else f32) for hop in group
        ]
        layout = (chips, part_rows, tuple(group), len(group))
        return pl.pallas_call(
            functools.partial(combine_kernel, layout),
            out_shape=out_shape,
            in_specs=[in_smem] + [in_vmem] * (3 + chips),
            out_specs=[in_vmem] * len(group),
            compiler_params=params(8),
            cost_estimate=cost(0, 3 << 20),
            name="combine",
        )(place, kept, found, packed, *parts)

    sums = {}
    for group, out in zip(groups, outs):
        returned = [to_lane(out[index + 1], step) for index, step in enumerate(chip_steps)]
        for hop, value in zip(group, combine(group, [out[0]] + returned)):
            sums[hop] = value

    for step in doublings(expert_count):
        last_sum = (last_sum.astype(f32) + to_lane(last_sum, step).astype(f32)).astype(bf16)
    for step in doublings(dp_count):
        last_sum = (last_sum.astype(f32) + to_plane(last_sum, step).astype(f32)).astype(bf16)

    total = sums[0]
    for hop in range(1, dp_count):
        total = total + to_plane(sums[hop], hop).astype(f32)
    own_out = total.astype(bf16)
    pieces = [own_out] + [to_lane(own_out, step) for step in chip_steps]
    pieces += [to_lane(piece, 1) for piece in pieces]
    layer_out = pl.pallas_call(
        functools.partial(gather_kernel, chips),
        out_shape=jax.ShapeDtypeStruct((tok_dev, width), bf16),
        in_specs=[in_smem] + [in_vmem] * len(pieces),
        out_specs=in_vmem,
        compiler_params=params(4),
        cost_estimate=cost(0, 2 << 20),
        name="gather",
    )(place, *pieces)

    block = min(512, width)
    steps = width // block
    grad_gate_up, grad_down = pl.pallas_call(
        gradient_kernel,
        grid=(steps,),
        out_shape=[
            jax.ShapeDtypeStruct(gate_up.shape, bf16),
            jax.ShapeDtypeStruct(down.shape, bf16),
        ],
        in_specs=[
            pl.BlockSpec((seqs, width), lambda step: (0, 0)),
            pl.BlockSpec((seqs, block), lambda step: (0, step)),
            pl.BlockSpec((seqs, width), lambda step: (0, 0)),
            pl.BlockSpec((seqs, 2 * half_width), lambda step: (0, 0)),
            pl.BlockSpec((seqs, lanes), lambda step: (0, 0)),
            pl.BlockSpec((seqs, lanes), lambda step: (0, 0)),
            pl.BlockSpec((1, half_width, width), lambda step: (0, 0, 0)),
        ],
        out_specs=[
            pl.BlockSpec((1, block, 2 * half_width), lambda step: (0, step, 0)),
            pl.BlockSpec((1, half_width, block), lambda step: (0, 0, step)),
        ],
        scratch_shapes=[
            pltpu.VMEM((steps, seqs, block), bf16),
            pltpu.VMEM((seqs, half_width), bf16),
            pltpu.VMEM((seqs, 2 * half_width), bf16),
        ],
        compiler_params=params(24),
        cost_estimate=cost(2 * seqs * width * 4 * half_width, 7 << 20),
        name="gradients",
    )(last_all, last_all, last_sum, last_projected, last_weights, partners, down)
    return (layer_out, grad_gate_up, grad_down)


def solution(mesh):
    return jax.shard_map(
        body,
        mesh=mesh,
        in_specs=(
            P("dp", None),
            P("dp", "expert"),
            P("dp", "expert"),
            P("dp"),
            P(("dp", "expert"), None, None),
            P(("dp", "expert"), None, None),
        ),
        out_specs=(P("dp", None), P(("dp", "expert"), None, None), P(("dp", "expert"), None, None)),
        check_vma=False,
    )
```

time: 151 us -> 106 us (0.70)
  Pallas kernels: 60.6 us -> 22.3 us
  other arithmetic: 4.09 us -> 0.24 us
  local copies, waits for them, and re-layouts: 9.07 us -> 5.43 us
    pallas_call x1, Pallas kernels: 33.6 us -> 1.58 us  [body(): pl.pallas_call(functools.partial(gather_kernel, chips), out_shape=jax.Sha...]
    pallas_call x3 -> x5, Pallas kernels: 16.7 us -> 13.3 us  [the longest x2 9.8 us: expert(): pl.pallas_call(functools.partial(expert_kernel, (chips, part_rows, near,...]
    pallas_call x2, Pallas kernels: 4.58 us -> 1.66 us  [combine(): pl.pallas_call(functools.partial(combine_kernel, layout), out_shape=out_s...]
    ppermute x24 -> x25, waiting for transfers between devices: 23 us -> 20.3 us  [to_lane(): lax.ppermute(value, 'expert', [(j, j ^ step) for j in range(expert_count)])]
    ppermute x10 -> x8, waiting for transfers between devices: 12.6 us -> 15 us  [to_plane(): return lax.ppermute(value, 'dp', [(p, p ^ step) for p in range(dp_count)])]
    ppermute x10 -> x8, starting transfers between devices: 15 us -> 17.1 us  [to_plane(): return lax.ppermute(value, 'dp', [(p, p ^ step) for p in range(dp_count)])]
    dynamic_slice x1 -> x0, local copies, waits for them, and re-layouts: 1.56 us -> none  [body(): own_part = lax.dynamic_slice_in_dim(tokens, lane * part_rows, part_rows, 0)]
    unnamed x51 -> x15, local copies, waits for them, and re-layouts: 6.84 us -> 5.41 us
  transfers between devices with their start and end apart: 34 -> 33, of which waited for: 19 -> 11; matrix products, arithmetic and copies ran while one was open for 5% -> 2% of each run, Pallas kernels for 13% -> 17%
where the time goes in v4:
time: 106 us; the launch traced here: 105 us
  starting transfers between devices  41.1 us (39%)
  waiting for transfers between devices  35.3 us (33%)
  Pallas kernels  22.3 us (21%)
  local copies, waits for them, and re-layouts  5.43 us (5%)
    ppermute x25, starting transfers between devices, to_lane(): lax.ppermute(value, 'expert', [(j, j ^ step) for j in range(expert_count)])  23.9 us
    ppermute x25, waiting for transfers between devices, to_lane(): lax.ppermute(value, 'expert', [(j, j ^ step) for j in range(expert_count)])  20.3 us
    ppermute x8, starting transfers between devices, to_plane(): return lax.ppermute(value, 'dp', [(p, p ^ step) for p in range(dp_count)])  17.1 us
    ppermute x8, waiting for transfers between devices, to_plane(): return lax.ppermute(value, 'dp', [(p, p ^ step) for p in range(dp_count)])  15 us
    pallas_call x2, Pallas kernels, expert(): pl.pallas_call(functools.partial(expert_kernel, (chips, part_rows, near,...  9.8 us
    pallas_call x1, Pallas kernels, body(): pl.pallas_call(gradient_kernel, grid=(steps,), out_shape=[jax.ShapeDtypeS...  5.75 us
    unnamed x15, local copies, waits for them, and re-layouts  5.41 us
  transfers between devices with their start and end apart: 33, of which 11 were waited for; matrix products, arithmetic and copies ran while one was open for 2% of the time, Pallas kernels for 17%

profile of v4, /device:TPU:0, one launch (start us, length us, event | category | flops | bytes accessed | tf_op | source)
XLA Modules:
  0.0 105.2 jit_solution(18186968738085181527)
XLA Ops:
  3.0 1.2 %copy-done.3 = bf16[256,2048]{1,0:T(8,128)(2,1)S(1)} copy-done((bf16[256,2048]{1,0:T(8,128)(2,1)S(1)}, bf16[256,2048]{1,0:T(8,128)(2,1)}, u32[]{:S(2)}) %copy-start.3) | copy-done | bytes 1048600
  5.7 4.1 %collective-permute-start = (bf16[32,2176]{1,0:T(8,128)(2,1)S(1)}, bf16[32,2176]{1,0:T(8,128)(2,1)S(1)}, u32[]{:S(2)}, u32[]{:S(2)}) collective-permute-start(bf16[32,2176]{1,0:T(8,128)(2,1)S(1)} %pack.1.refs_5_.own), channel_id=1, source_target_pairs={{0,16},{8,24},{16,0},{24,8},{1,17},{9,25},{17,1},{25,9},{2,18},{10... | collective-permute-start | bytes 417800 | tf_op jit(solution)/shard_map/ppermute | solution.py:317
  9.8 1.3 %collective-permute-start.1 = (bf16[32,2176]{1,0:T(8,128)(2,1)S(1)}, bf16[32,2176]{1,0:T(8,128)(2,1)S(1)}, u32[]{:S(2)}, u32[]{:S(2)}) collective-permute-start(bf16[32,2176]{1,0:T(8,128)(2,1)S(1)} %pack.1.refs_5_.own), channel_id=1, source_target_pairs={{0,24},{8,16},{16,8},{24,0},{1,25},{9,17},{17,9},{25,1},{2,26},{10... | collective-permute-start | bytes 417800 | tf_op jit(solution)/shard_map/ppermute | solution.py:317
  11.4 8.9 %collective-permute-done.refs_1_.refs_0_ = bf16[32,2176]{1,0:T(8,128)(2,1)S(1)} collective-permute-done((bf16[32,2176]{1,0:T(8,128)(2,1)S(1)}, bf16[32,2176]{1,0:T(8,128)(2,1)S(1)}, u32[]{:S(2)}, u32[]{:S(2)}) %collective-permute-start) | collective-permute-done | bytes 139296 | tf_op jit(solution)/shard_map/ppermute | solution.py:317
  20.3 1.9 %collective-permute-start.2 = (bf16[64,2176]{1,0:T(8,128)(2,1)S(1)}, bf16[64,2176]{1,0:T(8,128)(2,1)S(1)}, u32[]{:S(2)}, u32[]{:S(2)}) collective-permute-start(bf16[64,2176]{1,0:T(8,128)(2,1)S(1)} %constant_dynamic-update-slice_fusion), channel_id=1, source_target_pairs={{0,2},{1,3},{2,0},{3,1},{4,6},{5,7},{6,4},{7,5},{8,10},{9,11},{10,... | collective-permute-start | bytes 835592 | tf_op jit(solution)/shard_map/ppermute | solution.py:314
  22.2 1.5 %collective-permute-start.3 = (bf16[64,2176]{1,0:T(8,128)(2,1)S(1)}, bf16[64,2176]{1,0:T(8,128)(2,1)S(1)}, u32[]{:S(2)}, u32[]{:S(2)}) collective-permute-start(bf16[64,2176]{1,0:T(8,128)(2,1)S(1)} %constant_dynamic-update-slice_fusion), channel_id=1, source_target_pairs={{0,4},{1,5},{2,6},{3,7},{4,0},{5,1},{6,2},{7,3},{8,12},{9,13},{10,... | collective-permute-start | bytes 835592 | tf_op jit(solution)/shard_map/ppermute | solution.py:314
  23.9 6.1 %collective-permute-done.2.refs_3_.refs_2_ = bf16[64,2176]{1,0:T(8,128)(2,1)S(1)} collective-permute-done((bf16[64,2176]{1,0:T(8,128)(2,1)S(1)}, bf16[64,2176]{1,0:T(8,128)(2,1)S(1)}, u32[]{:S(2)}, u32[]{:S(2)}) %collective-permute-start.2) | collective-permute-done | bytes 278560 | tf_op jit(solution)/shard_map/ppermute | solution.py:314
  30.0 1.9 %collective-permute-start.8 = (bf16[32,2304]{1,0:T(8,128)(2,1)S(1)}, bf16[32,2304]{1,0:T(8,128)(2,1)S(1)}, u32[]{:S(2)}, u32[]{:S(2)}) collective-permute-start(bf16[32,2304]{1,0:T(8,128)(2,1)S(1)} %pad_maximum_fusion), channel_id=1, source_target_pairs={{0,2},{1,3},{2,0},{3,1},{4,6},{5,7},{6,4},{7,5},{8,10},{9,11},{10,... | collective-permute-start | bytes 442376 | tf_op jit(solution)/shard_map/ppermute | solution.py:314
  31.8 3.7 %collective-permute-done.3.refs_4_.refs_3_ = bf16[64,2176]{1,0:T(8,128)(2,1)S(1)} collective-permute-done((bf16[64,2176]{1,0:T(8,128)(2,1)S(1)}, bf16[64,2176]{1,0:T(8,128)(2,1)S(1)}, u32[]{:S(2)}, u32[]{:S(2)}) %collective-permute-start.3) | collective-permute-done | bytes 278560 | tf_op jit(solution)/shard_map/ppermute | solution.py:314
  35.5 3.0 %collective-permute-start.9 = (bf16[32,2304]{1,0:T(8,128)(2,1)S(1)}, bf16[32,2304]{1,0:T(8,128)(2,1)S(1)}, u32[]{:S(2)}, u32[]{:S(2)}) collective-permute-start(bf16[32,2304]{1,0:T(8,128)(2,1)S(1)} %pad_maximum_fusion), channel_id=1, source_target_pairs={{0,4},{1,5},{2,6},{3,7},{4,0},{5,1},{6,2},{7,3},{8,12},{9,13},{10,... | collective-permute-start | bytes 442376 | tf_op jit(solution)/shard_map/ppermute | solution.py:314
  38.6 1.9 %copy-done = bf16[1,2048,768]{2,1,0:T(8,128)(2,1)S(1)} copy-done((bf16[1,2048,768]{2,1,0:T(8,128)(2,1)S(1)}, bf16[1,2048,768]{2,1,0:T(8,128)(2,1)}, u32[]{:S(2)}) %copy-start) | copy-done | bytes 3145752
  40.4 4.9 %experts.2 = (bf16[64,2048]{1,0:T(8,128)(2,1)S(1)}, bf16[64,2048]{1,0:T(8,128)(2,1)S(1)}, bf16[64,2048]{1,0:T(8,128)(2,1)S(1)}, bf16[64,2048]{1,0:T(8,128)(2,1)S(1)}) custom-call(s32[3]{0:T(128)S(1)} %pad_add_fusion.place.refs_0_, bf16[32,2176]{1,0:T(8,128)(2,1)S(1)} %collective-permute-done.refs_1_.refs_0_, ...), custom_call_target="tpu_custom_call" | custom-call | flops 2415919104 | bytes 12582912 | tf_op jit(solution)/shard_map/experts/pallas_call | solution.py:374
  47.8 1.6 %last_rows.1 = (f32[16,768]{1,0:T(8,128)S(1)}, bf16[16,2048]{1,0:T(8,128)(2,1)S(1)}, f32[16,128]{1,0:T(8,128)S(1)}) custom-call(s32[3]{0:T(128)S(1)} %pad_add_fusion.place.refs_0_, bf16[16,2048]{1,0:T(8,128)(2,1)S(1)} %get-tuple-element.40.rows.last_all.last_block, bf16[144,128]{1,0:T(8,128)(2,1)S(1)} %get-tuple-element.27.kept, ...), custom_call_target="tpu_custom_call" | custom-call | flops 75497472 | bytes 5242880 | tf_op jit(solution)/shard_map/last_rows/pallas_call | solution.py:416
  49.6 1.5 %collective-permute-start.16 = (bf16[64,2048]{1,0:T(8,128)(2,1)S(1)}, bf16[64,2048]{1,0:T(8,128)(2,1)S(1)}, u32[]{:S(2)}, u32[]{:S(2)}) collective-permute-start(bf16[64,2048]{1,0:T(8,128)(2,1)S(1)} %get-tuple-element.35), channel_id=1, source_target_pairs={{0,2},{1,3},{2,0},{3,1},{4,6},{5,7},{6,4},{7,5},{8,10},{9,11},{10,... | collective-permute-start | bytes 786440 | tf_op jit(solution)/shard_map/ppermute | solution.py:314
  51.0 2.0 %collective-permute-start.17 = (bf16[64,2048]{1,0:T(8,128)(2,1)S(1)}, bf16[64,2048]{1,0:T(8,128)(2,1)S(1)}, u32[]{:S(2)}, u32[]{:S(2)}) collective-permute-start(bf16[64,2048]{1,0:T(8,128)(2,1)S(1)} %get-tuple-element.36), channel_id=1, source_target_pairs={{0,4},{1,5},{2,6},{3,7},{4,0},{5,1},{6,2},{7,3},{8,12},{9,13},{10,... | collective-permute-start | bytes 786440 | tf_op jit(solution)/shard_map/ppermute | solution.py:314
  53.1 1.5 %collective-permute-start.29 = (bf16[16,2048]{1,0:T(8,128)(2,1)S(1)}, bf16[16,2048]{1,0:T(8,128)(2,1)S(1)}, u32[]{:S(2)}, u32[]{:S(2)}) collective-permute-start(bf16[16,2048]{1,0:T(8,128)(2,1)S(1)} %add_convert_fusion.5), channel_id=1, source_target_pairs={{0,2},{1,3},{2,0},{3,1},{4,6},{5,7},{6,4},{7,5},{8,10},{9,11},{10,... | collective-permute-start | bytes 196616 | tf_op jit(solution)/shard_map/ppermute | solution.py:314
  54.6 4.9 %experts.3 = (bf16[64,2048]{1,0:T(8,128)(2,1)S(1)}, bf16[64,2048]{1,0:T(8,128)(2,1)S(1)}, bf16[64,2048]{1,0:T(8,128)(2,1)S(1)}, bf16[64,2048]{1,0:T(8,128)(2,1)S(1)}) custom-call(s32[3]{0:T(128)S(1)} %pad_add_fusion.place.refs_0_, bf16[256,2048]{1,0:T(8,128)(2,1)S(1)} %copy-done.4, bf16[32,2176]{1,0:T(8,128)(2,1)S(1)} %collective-permute-done.7.refs_6_.refs_2_, ...), custom_call_target="tpu_custom_call" | custom-call | flops 2415919104 | bytes 12582912 | tf_op jit(solution)/shard_map/experts/pallas_call | solution.py:374
  60.2 5.6 %collective-permute-done.29 = bf16[16,2048]{1,0:T(8,128)(2,1)S(1)} collective-permute-done((bf16[16,2048]{1,0:T(8,128)(2,1)S(1)}, bf16[16,2048]{1,0:T(8,128)(2,1)S(1)}, u32[]{:S(2)}, u32[]{:S(2)}) %collective-permute-start.29) | collective-permute-done | bytes 65568 | tf_op jit(solution)/shard_map/ppermute | solution.py:314
  65.8 1.9 %collective-permute-start.13 = (bf16[64,2048]{1,0:T(8,128)(2,1)S(1)}, bf16[64,2048]{1,0:T(8,128)(2,1)S(1)}, u32[]{:S(2)}, u32[]{:S(2)}) collective-permute-start(bf16[64,2048]{1,0:T(8,128)(2,1)S(1)} %get-tuple-element.31), channel_id=1, source_target_pairs={{0,4},{1,5},{2,6},{3,7},{4,0},{5,1},{6,2},{7,3},{8,12},{9,13},{10,... | collective-permute-start | bytes 786440 | tf_op jit(solution)/shard_map/ppermute | solution.py:314
  68.7 2.0 %collective-permute-start.30 = (bf16[16,2048]{1,0:T(8,128)(2,1)S(1)}, bf16[16,2048]{1,0:T(8,128)(2,1)S(1)}, u32[]{:S(2)}, u32[]{:S(2)}) collective-permute-start(bf16[16,2048]{1,0:T(8,128)(2,1)S(1)} %add_convert_fusion.4), channel_id=1, source_target_pairs={{0,4},{1,5},{2,6},{3,7},{4,0},{5,1},{6,2},{7,3},{8,12},{9,13},{10,... | collective-permute-start | bytes 196616 | tf_op jit(solution)/shard_map/ppermute | solution.py:314
  71.6 3.3 %collective-permute-start.20 = (bf16[32,2048]{1,0:T(8,128)(2,1)S(1)}, bf16[32,2048]{1,0:T(8,128)(2,1)S(1)}, u32[]{:S(2)}, u32[]{:S(2)}) collective-permute-start(bf16[32,2048]{1,0:T(8,128)(2,1)S(1)} %get-tuple-element.39), channel_id=1, source_target_pairs={{0,24},{8,16},{16,8},{24,0},{1,25},{9,17},{17,9},{25,1},{2,26},{10... | collective-permute-start | bytes 393224 | tf_op jit(solution)/shard_map/ppermute | solution.py:317
  74.9 2.1 %collective-permute-start.19 = (bf16[32,2048]{1,0:T(8,128)(2,1)S(1)}, bf16[32,2048]{1,0:T(8,128)(2,1)S(1)}, u32[]{:S(2)}, u32[]{:S(2)}) collective-permute-start(bf16[32,2048]{1,0:T(8,128)(2,1)S(1)} %get-tuple-element.38), channel_id=1, source_target_pairs={{0,16},{8,24},{16,0},{24,8},{1,17},{9,25},{17,1},{25,9},{2,18},{10... | collective-permute-start | bytes 393224 | tf_op jit(solution)/shard_map/ppermute | solution.py:317
  77.0 2.4 %collective-permute-done.13.refs_2_ = bf16[64,2048]{1,0:T(8,128)(2,1)S(1)} collective-permute-done((bf16[64,2048]{1,0:T(8,128)(2,1)S(1)}, bf16[64,2048]{1,0:T(8,128)(2,1)S(1)}, u32[]{:S(2)}, u32[]{:S(2)}) %collective-permute-start.13) | collective-permute-done | bytes 262176 | tf_op jit(solution)/shard_map/ppermute | solution.py:314
  80.3 3.5 %collective-permute-start.15 = (bf16[32,2048]{1,0:T(8,128)(2,1)S(1)}, bf16[32,2048]{1,0:T(8,128)(2,1)S(1)}, u32[]{:S(2)}, u32[]{:S(2)}) collective-permute-start(bf16[32,2048]{1,0:T(8,128)(2,1)S(1)} %get-tuple-element.34), channel_id=1, source_target_pairs={{0,8},{8,0},{16,24},{24,16},{1,9},{9,1},{17,25},{25,17},{2,10},{10... | collective-permute-start | bytes 393224 | tf_op jit(solution)/shard_map/ppermute | solution.py:317
  83.9 2.0 %collective-permute-done.19 = bf16[32,2048]{1,0:T(8,128)(2,1)S(1)} collective-permute-done((bf16[32,2048]{1,0:T(8,128)(2,1)S(1)}, bf16[32,2048]{1,0:T(8,128)(2,1)S(1)}, u32[]{:S(2)}, u32[]{:S(2)}) %collective-permute-start.19) | collective-permute-done | bytes 131104 | tf_op jit(solution)/shard_map/ppermute | solution.py:317
  85.9 2.4 %collective-permute-done.15 = bf16[32,2048]{1,0:T(8,128)(2,1)S(1)} collective-permute-done((bf16[32,2048]{1,0:T(8,128)(2,1)S(1)}, bf16[32,2048]{1,0:T(8,128)(2,1)S(1)}, u32[]{:S(2)}, u32[]{:S(2)}) %collective-permute-start.15) | collective-permute-done | bytes 131104 | tf_op jit(solution)/shard_map/ppermute | solution.py:317
  88.4 1.3 %collective-permute-start.21 = (bf16[32,2048]{1,0:T(8,128)(2,1)S(1)}, bf16[32,2048]{1,0:T(8,128)(2,1)S(1)}, u32[]{:S(2)}, u32[]{:S(2)}) collective-permute-start(bf16[32,2048]{1,0:T(8,128)(2,1)S(1)} %add_convert_fusion.refs_0_), channel_id=1, source_target_pairs={{0,2},{1,3},{2,0},{3,1},{4,6},{5,7},{6,4},{7,5},{8,10},{9,11},{10,... | collective-permute-start | bytes 393224 | tf_op jit(solution)/shard_map/ppermute | solution.py:314
  90.3 1.6 %collective-permute-start.23 = (bf16[32,2048]{1,0:T(8,128)(2,1)S(1)}, bf16[32,2048]{1,0:T(8,128)(2,1)S(1)}, u32[]{:S(2)}, u32[]{:S(2)}) collective-permute-start(bf16[32,2048]{1,0:T(8,128)(2,1)S(1)} %add_convert_fusion.refs_0_), channel_id=1, source_target_pairs={{0,6},{1,7},{2,4},{3,5},{4,2},{5,3},{6,0},{7,1},{8,14},{9,15},{10,... | collective-permute-start | bytes 393224 | tf_op jit(solution)/shard_map/ppermute | solution.py:314
  91.9 2.4 %collective-permute-start.32 = (bf16[16,2048]{1,0:T(8,128)(2,1)S(1)}, bf16[16,2048]{1,0:T(8,128)(2,1)S(1)}, u32[]{:S(2)}, u32[]{:S(2)}) collective-permute-start(bf16[16,2048]{1,0:T(8,128)(2,1)S(1)} %add_convert_fusion.2), channel_id=1, source_target_pairs={{0,16},{8,24},{16,0},{24,8},{1,17},{9,25},{17,1},{25,9},{2,18},{10... | collective-permute-start | bytes 196616 | tf_op jit(solution)/shard_map/ppermute | solution.py:317
  96.1 1.7 %collective-permute-done.32 = bf16[16,2048]{1,0:T(8,128)(2,1)S(1)} collective-permute-done((bf16[16,2048]{1,0:T(8,128)(2,1)S(1)}, bf16[16,2048]{1,0:T(8,128)(2,1)S(1)}, u32[]{:S(2)}, u32[]{:S(2)}) %collective-permute-start.32) | collective-permute-done | bytes 65568 | tf_op jit(solution)/shard_map/ppermute | solution.py:317
  97.9 5.8 %gradients.1 = (bf16[1,2048,768]{2,1,0:T(8,128)(2,1)}, bf16[1,384,2048]{2,1,0:T(8,128)(2,1)}) custom-call(bf16[16,2048]{1,0:T(8,128)(2,1)S(1)} %get-tuple-element.40.rows.last_all.last_block, bf16[16,2048]{1,0:T(8,128)(2,1)S(1)} %get-tuple-element.40.rows.last_all.last_block, bf16[16,2048]{1,0:T(8,128)(2,1)S(1)} %add_convert_fusion.1.last_sum, ...), custom_call_target="tpu_custom_call" | custom-call | flops 100663296 | bytes 7340032 | tf_op jit(solution)/shard_map/gradients/pallas_call | solution.py:474
  103.7 1.6 %gather.1 = bf16[256,2048]{1,0:T(8,128)(2,1)} custom-call(s32[3]{0:T(128)S(1)} %pad_add_fusion.place.refs_0_, bf16[32,2048]{1,0:T(8,128)(2,1)S(1)} %add_convert_fusion.refs_0_, bf16[32,2048]{1,0:T(8,128)(2,1)S(1)} %collective-permute-done.21.refs_1_, bf16[32,2048]{1,0:T(8,128)(2,1)S(1)} %collective-permute-done.22.refs_2_, ...), custom_call_target="tpu_custom_call" | custom-call | bytes 2097152 | tf_op jit(solution)/shard_map/gather/pallas_call | solution.py:462
  (68 shorter events, 12.8 us)
Async XLA Ops:
  0.6 37.9 %collective-permute-start.5 = (bf16[1,2048,768]{2,1,0:T(8,128)(2,1)}, bf16[1,2048,768]{2,1,0:T(8,128)(2,1)}, u32[]{:S(2)}, u32[]{:S(2)}) collective-permute-start(bf16[1,2048,768]{2,1,0:T(8,128)(2,1)} %w_in.1), channel_id=1, source_target_pairs={{0,1},{1,0},{2,3},{3,2},{4,5},{5,4},{6,7},{7,6},{8,9},{9,8},{10,11... | collective-permute-start | bytes 9437192 | tf_op jit(solution)/shard_map/ppermute | solution.py:314
  1.2 37.4 %collective-permute-start.6 = (bf16[1,384,2048]{2,1,0:T(8,128)(2,1)}, bf16[1,384,2048]{2,1,0:T(8,128)(2,1)S(1)}, u32[]{:S(2)}, u32[]{:S(2)}) collective-permute-start(bf16[1,384,2048]{2,1,0:T(8,128)(2,1)} %down.1), channel_id=1, source_target_pairs={{0,1},{1,0},{2,3},{3,2},{4,5},{5,4},{6,7},{7,6},{8,9},{9,8},{10,11... | collective-permute-start | bytes 4718600 | tf_op jit(solution)/shard_map/ppermute | solution.py:314
  5.7 14.6 %collective-permute-start = (bf16[32,2176]{1,0:T(8,128)(2,1)S(1)}, bf16[32,2176]{1,0:T(8,128)(2,1)S(1)}, u32[]{:S(2)}, u32[]{:S(2)}) collective-permute-start(bf16[32,2176]{1,0:T(8,128)(2,1)S(1)} %pack.1.refs_5_.own), channel_id=1, source_target_pairs={{0,16},{8,24},{16,0},{24,8},{1,17},{9,25},{17,1},{25,9},{2,18},{10... | collective-permute-start | bytes 417800 | tf_op jit(solution)/shard_map/ppermute | solution.py:317
  9.8 10.5 %collective-permute-start.1 = (bf16[32,2176]{1,0:T(8,128)(2,1)S(1)}, bf16[32,2176]{1,0:T(8,128)(2,1)S(1)}, u32[]{:S(2)}, u32[]{:S(2)}) collective-permute-start(bf16[32,2176]{1,0:T(8,128)(2,1)S(1)} %pack.1.refs_5_.own), channel_id=1, source_target_pairs={{0,24},{8,16},{16,8},{24,0},{1,25},{9,17},{17,9},{25,1},{2,26},{10... | collective-permute-start | bytes 417800 | tf_op jit(solution)/shard_map/ppermute | solution.py:317
  11.1 12.6 %collective-permute-start.7 = (bf16[32,2176]{1,0:T(8,128)(2,1)S(1)}, bf16[32,2176]{1,0:T(8,128)(2,1)S(1)}, u32[]{:S(2)}, u32[]{:S(2)}) collective-permute-start(bf16[32,2176]{1,0:T(8,128)(2,1)S(1)} %pack.1.refs_5_.own), channel_id=1, source_target_pairs={{0,8},{8,0},{16,24},{24,16},{1,9},{9,1},{17,25},{25,17},{2,10},{10... | collective-permute-start | bytes 417800 | tf_op jit(solution)/shard_map/ppermute | solution.py:317
  20.3 9.7 %collective-permute-start.2 = (bf16[64,2176]{1,0:T(8,128)(2,1)S(1)}, bf16[64,2176]{1,0:T(8,128)(2,1)S(1)}, u32[]{:S(2)}, u32[]{:S(2)}) collective-permute-start(bf16[64,2176]{1,0:T(8,128)(2,1)S(1)} %constant_dynamic-update-slice_fusion), channel_id=1, source_target_pairs={{0,2},{1,3},{2,0},{3,1},{4,6},{5,7},{6,4},{7,5},{8,10},{9,11},{10,... | collective-permute-start | bytes 835592 | tf_op jit(solution)/shard_map/ppermute | solution.py:314
  22.2 13.3 %collective-permute-start.3 = (bf16[64,2176]{1,0:T(8,128)(2,1)S(1)}, bf16[64,2176]{1,0:T(8,128)(2,1)S(1)}, u32[]{:S(2)}, u32[]{:S(2)}) collective-permute-start(bf16[64,2176]{1,0:T(8,128)(2,1)S(1)} %constant_dynamic-update-slice_fusion), channel_id=1, source_target_pairs={{0,4},{1,5},{2,6},{3,7},{4,0},{5,1},{6,2},{7,3},{8,12},{9,13},{10,... | collective-permute-start | bytes 835592 | tf_op jit(solution)/shard_map/ppermute | solution.py:314
  23.8 14.8 %collective-permute-start.4 = (bf16[64,2176]{1,0:T(8,128)(2,1)S(1)}, bf16[64,2176]{1,0:T(8,128)(2,1)S(1)}, u32[]{:S(2)}, u32[]{:S(2)}) collective-permute-start(bf16[64,2176]{1,0:T(8,128)(2,1)S(1)} %constant_dynamic-update-slice_fusion), channel_id=1, source_target_pairs={{0,6},{1,7},{2,4},{3,5},{4,2},{5,3},{6,0},{7,1},{8,14},{9,15},{10,... | collective-permute-start | bytes 835592 | tf_op jit(solution)/shard_map/ppermute | solution.py:314
  30.0 15.4 %collective-permute-start.8 = (bf16[32,2304]{1,0:T(8,128)(2,1)S(1)}, bf16[32,2304]{1,0:T(8,128)(2,1)S(1)}, u32[]{:S(2)}, u32[]{:S(2)}) collective-permute-start(bf16[32,2304]{1,0:T(8,128)(2,1)S(1)} %pad_maximum_fusion), channel_id=1, source_target_pairs={{0,2},{1,3},{2,0},{3,1},{4,6},{5,7},{6,4},{7,5},{8,10},{9,11},{10,... | collective-permute-start | bytes 442376 | tf_op jit(solution)/shard_map/ppermute | solution.py:314
  35.5 9.8 %collective-permute-start.9 = (bf16[32,2304]{1,0:T(8,128)(2,1)S(1)}, bf16[32,2304]{1,0:T(8,128)(2,1)S(1)}, u32[]{:S(2)}, u32[]{:S(2)}) collective-permute-start(bf16[32,2304]{1,0:T(8,128)(2,1)S(1)} %pad_maximum_fusion), channel_id=1, source_target_pairs={{0,4},{1,5},{2,6},{3,7},{4,0},{5,1},{6,2},{7,3},{8,12},{9,13},{10,... | collective-permute-start | bytes 442376 | tf_op jit(solution)/shard_map/ppermute | solution.py:314
  38.5 6.9 %collective-permute-start.10 = (bf16[32,2304]{1,0:T(8,128)(2,1)S(1)}, bf16[32,2304]{1,0:T(8,128)(2,1)S(1)}, u32[]{:S(2)}, u32[]{:S(2)}) collective-permute-start(bf16[32,2304]{1,0:T(8,128)(2,1)S(1)} %pad_maximum_fusion), channel_id=1, source_target_pairs={{0,6},{1,7},{2,4},{3,5},{4,2},{5,3},{6,0},{7,1},{8,14},{9,15},{10,... | collective-permute-start | bytes 442376 | tf_op jit(solution)/shard_map/ppermute | solution.py:314
  49.4 3.7 %collective-permute-start.28 = (bf16[16,2048]{1,0:T(8,128)(2,1)S(1)}, bf16[16,2048]{1,0:T(8,128)(2,1)S(1)}, u32[]{:S(2)}, u32[]{:S(2)}) collective-permute-start(bf16[16,2048]{1,0:T(8,128)(2,1)S(1)} %get-tuple-element.41), channel_id=1, source_target_pairs={{0,1},{1,0},{2,3},{3,2},{4,5},{5,4},{6,7},{7,6},{8,9},{9,8},{10,11... | collective-permute-start | bytes 196616 | tf_op jit(solution)/shard_map/ppermute | solution.py:314
  49.6 18.1 %collective-permute-start.16 = (bf16[64,2048]{1,0:T(8,128)(2,1)S(1)}, bf16[64,2048]{1,0:T(8,128)(2,1)S(1)}, u32[]{:S(2)}, u32[]{:S(2)}) collective-permute-start(bf16[64,2048]{1,0:T(8,128)(2,1)S(1)} %get-tuple-element.35), channel_id=1, source_target_pairs={{0,2},{1,3},{2,0},{3,1},{4,6},{5,7},{6,4},{7,5},{8,10},{9,11},{10,... | collective-permute-start | bytes 786440 | tf_op jit(solution)/shard_map/ppermute | solution.py:314
  51.0 17.7 %collective-permute-start.17 = (bf16[64,2048]{1,0:T(8,128)(2,1)S(1)}, bf16[64,2048]{1,0:T(8,128)(2,1)S(1)}, u32[]{:S(2)}, u32[]{:S(2)}) collective-permute-start(bf16[64,2048]{1,0:T(8,128)(2,1)S(1)} %get-tuple-element.36), channel_id=1, source_target_pairs={{0,4},{1,5},{2,6},{3,7},{4,0},{5,1},{6,2},{7,3},{8,12},{9,13},{10,... | collective-permute-start | bytes 786440 | tf_op jit(solution)/shard_map/ppermute | solution.py:314
  53.0 17.7 %collective-permute-start.18 = (bf16[64,2048]{1,0:T(8,128)(2,1)S(1)}, bf16[64,2048]{1,0:T(8,128)(2,1)S(1)}, u32[]{:S(2)}, u32[]{:S(2)}) collective-permute-start(bf16[64,2048]{1,0:T(8,128)(2,1)S(1)} %get-tuple-element.37), channel_id=1, source_target_pairs={{0,6},{1,7},{2,4},{3,5},{4,2},{5,3},{6,0},{7,1},{8,14},{9,15},{10,... | collective-permute-start | bytes 786440 | tf_op jit(solution)/shard_map/ppermute | solution.py:314
  53.1 12.7 %collective-permute-start.29 = (bf16[16,2048]{1,0:T(8,128)(2,1)S(1)}, bf16[16,2048]{1,0:T(8,128)(2,1)S(1)}, u32[]{:S(2)}, u32[]{:S(2)}) collective-permute-start(bf16[16,2048]{1,0:T(8,128)(2,1)S(1)} %add_convert_fusion.5), channel_id=1, source_target_pairs={{0,2},{1,3},{2,0},{3,1},{4,6},{5,7},{6,4},{7,5},{8,10},{9,11},{10,... | collective-permute-start | bytes 196616 | tf_op jit(solution)/shard_map/ppermute | solution.py:314
  59.5 15.4 %collective-permute-start.12 = (bf16[64,2048]{1,0:T(8,128)(2,1)S(1)}, bf16[64,2048]{1,0:T(8,128)(2,1)S(1)}, u32[]{:S(2)}, u32[]{:S(2)}) collective-permute-start(bf16[64,2048]{1,0:T(8,128)(2,1)S(1)} %get-tuple-element.30), channel_id=1, source_target_pairs={{0,2},{1,3},{2,0},{3,1},{4,6},{5,7},{6,4},{7,5},{8,10},{9,11},{10,... | collective-permute-start | bytes 786440 | tf_op jit(solution)/shard_map/ppermute | solution.py:314
  65.8 13.7 %collective-permute-start.13 = (bf16[64,2048]{1,0:T(8,128)(2,1)S(1)}, bf16[64,2048]{1,0:T(8,128)(2,1)S(1)}, u32[]{:S(2)}, u32[]{:S(2)}) collective-permute-start(bf16[64,2048]{1,0:T(8,128)(2,1)S(1)} %get-tuple-element.31), channel_id=1, source_target_pairs={{0,4},{1,5},{2,6},{3,7},{4,0},{5,1},{6,2},{7,3},{8,12},{9,13},{10,... | collective-permute-start | bytes 786440 | tf_op jit(solution)/shard_map/ppermute | solution.py:314
  67.7 11.8 %collective-permute-start.14 = (bf16[64,2048]{1,0:T(8,128)(2,1)S(1)}, bf16[64,2048]{1,0:T(8,128)(2,1)S(1)}, u32[]{:S(2)}, u32[]{:S(2)}) collective-permute-start(bf16[64,2048]{1,0:T(8,128)(2,1)S(1)} %get-tuple-element.32), channel_id=1, source_target_pairs={{0,6},{1,7},{2,4},{3,5},{4,2},{5,3},{6,0},{7,1},{8,14},{9,15},{10,... | collective-permute-start | bytes 786440 | tf_op jit(solution)/shard_map/ppermute | solution.py:314
  68.7 15.1 %collective-permute-start.30 = (bf16[16,2048]{1,0:T(8,128)(2,1)S(1)}, bf16[16,2048]{1,0:T(8,128)(2,1)S(1)}, u32[]{:S(2)}, u32[]{:S(2)}) collective-permute-start(bf16[16,2048]{1,0:T(8,128)(2,1)S(1)} %add_convert_fusion.4), channel_id=1, source_target_pairs={{0,4},{1,5},{2,6},{3,7},{4,0},{5,1},{6,2},{7,3},{8,12},{9,13},{10,... | collective-permute-start | bytes 196616 | tf_op jit(solution)/shard_map/ppermute | solution.py:314
  71.6 12.3 %collective-permute-start.20 = (bf16[32,2048]{1,0:T(8,128)(2,1)S(1)}, bf16[32,2048]{1,0:T(8,128)(2,1)S(1)}, u32[]{:S(2)}, u32[]{:S(2)}) collective-permute-start(bf16[32,2048]{1,0:T(8,128)(2,1)S(1)} %get-tuple-element.39), channel_id=1, source_target_pairs={{0,24},{8,16},{16,8},{24,0},{1,25},{9,17},{17,9},{25,1},{2,26},{10... | collective-permute-start | bytes 393224 | tf_op jit(solution)/shard_map/ppermute | solution.py:317
  74.9 11.0 %collective-permute-start.19 = (bf16[32,2048]{1,0:T(8,128)(2,1)S(1)}, bf16[32,2048]{1,0:T(8,128)(2,1)S(1)}, u32[]{:S(2)}, u32[]{:S(2)}) collective-permute-start(bf16[32,2048]{1,0:T(8,128)(2,1)S(1)} %get-tuple-element.38), channel_id=1, source_target_pairs={{0,16},{8,24},{16,0},{24,8},{1,17},{9,25},{17,1},{25,9},{2,18},{10... | collective-permute-start | bytes 393224 | tf_op jit(solution)/shard_map/ppermute | solution.py:317
  80.3 8.0 %collective-permute-start.15 = (bf16[32,2048]{1,0:T(8,128)(2,1)S(1)}, bf16[32,2048]{1,0:T(8,128)(2,1)S(1)}, u32[]{:S(2)}, u32[]{:S(2)}) collective-permute-start(bf16[32,2048]{1,0:T(8,128)(2,1)S(1)} %get-tuple-element.34), channel_id=1, source_target_pairs={{0,8},{8,0},{16,24},{24,16},{1,9},{9,1},{17,25},{25,17},{2,10},{10... | collective-permute-start | bytes 393224 | tf_op jit(solution)/shard_map/ppermute | solution.py:317
  83.8 8.1 %collective-permute-start.31 = (bf16[16,2048]{1,0:T(8,128)(2,1)S(1)}, bf16[16,2048]{1,0:T(8,128)(2,1)S(1)}, u32[]{:S(2)}, u32[]{:S(2)}) collective-permute-start(bf16[16,2048]{1,0:T(8,128)(2,1)S(1)} %add_convert_fusion.3), channel_id=1, source_target_pairs={{0,8},{8,0},{16,24},{24,16},{1,9},{9,1},{17,25},{25,17},{2,10},{10... | collective-permute-start | bytes 196616 | tf_op jit(solution)/shard_map/ppermute | solution.py:317
  88.4 6.1 %collective-permute-start.21 = (bf16[32,2048]{1,0:T(8,128)(2,1)S(1)}, bf16[32,2048]{1,0:T(8,128)(2,1)S(1)}, u32[]{:S(2)}, u32[]{:S(2)}) collective-permute-start(bf16[32,2048]{1,0:T(8,128)(2,1)S(1)} %add_convert_fusion.refs_0_), channel_id=1, source_target_pairs={{0,2},{1,3},{2,0},{3,1},{4,6},{5,7},{6,4},{7,5},{8,10},{9,11},{10,... | collective-permute-start | bytes 393224 | tf_op jit(solution)/shard_map/ppermute | solution.py:314
  89.6 5.3 %collective-permute-start.22 = (bf16[32,2048]{1,0:T(8,128)(2,1)S(1)}, bf16[32,2048]{1,0:T(8,128)(2,1)S(1)}, u32[]{:S(2)}, u32[]{:S(2)}) collective-permute-start(bf16[32,2048]{1,0:T(8,128)(2,1)S(1)} %add_convert_fusion.refs_0_), channel_id=1, source_target_pairs={{0,4},{1,5},{2,6},{3,7},{4,0},{5,1},{6,2},{7,3},{8,12},{9,13},{10,... | collective-permute-start | bytes 393224 | tf_op jit(solution)/shard_map/ppermute | solution.py:314
  90.3 5.9 %collective-permute-start.23 = (bf16[32,2048]{1,0:T(8,128)(2,1)S(1)}, bf16[32,2048]{1,0:T(8,128)(2,1)S(1)}, u32[]{:S(2)}, u32[]{:S(2)}) collective-permute-start(bf16[32,2048]{1,0:T(8,128)(2,1)S(1)} %add_convert_fusion.refs_0_), channel_id=1, source_target_pairs={{0,6},{1,7},{2,4},{3,5},{4,2},{5,3},{6,0},{7,1},{8,14},{9,15},{10,... | collective-permute-start | bytes 393224 | tf_op jit(solution)/shard_map/ppermute | solution.py:314
  91.9 5.9 %collective-permute-start.32 = (bf16[16,2048]{1,0:T(8,128)(2,1)S(1)}, bf16[16,2048]{1,0:T(8,128)(2,1)S(1)}, u32[]{:S(2)}, u32[]{:S(2)}) collective-permute-start(bf16[16,2048]{1,0:T(8,128)(2,1)S(1)} %add_convert_fusion.2), channel_id=1, source_target_pairs={{0,16},{8,24},{16,0},{24,8},{1,17},{9,25},{17,1},{25,9},{2,18},{10... | collective-permute-start | bytes 196616 | tf_op jit(solution)/shard_map/ppermute | solution.py:317
  94.4 9.3 %collective-permute-start.24 = (bf16[32,2048]{1,0:T(8,128)(2,1)S(1)}, bf16[32,2048]{1,0:T(8,128)(2,1)S(1)}, u32[]{:S(2)}, u32[]{:S(2)}) collective-permute-start(bf16[32,2048]{1,0:T(8,128)(2,1)S(1)} %add_convert_fusion.refs_0_), channel_id=1, source_target_pairs={{0,1},{1,0},{2,3},{3,2},{4,5},{5,4},{6,7},{7,6},{8,9},{9,8},{10,11... | collective-permute-start | bytes 393224 | tf_op jit(solution)/shard_map/ppermute | solution.py:314
  94.5 9.2 %collective-permute-start.25 = (bf16[32,2048]{1,0:T(8,128)(2,1)S(1)}, bf16[32,2048]{1,0:T(8,128)(2,1)S(1)}, u32[]{:S(2)}, u32[]{:S(2)}) collective-permute-start(bf16[32,2048]{1,0:T(8,128)(2,1)S(1)} %collective-permute-done.21.refs_1_), channel_id=1, source_target_pairs={{0,1},{1,0},{2,3},{3,2},{4,5},{5,4},{6,7},{7,6},{8,9},{9,8},{10,11... | collective-permute-start | bytes 393224 | tf_op jit(solution)/shard_map/ppermute | solution.py:314
  94.9 8.8 %collective-permute-start.26 = (bf16[32,2048]{1,0:T(8,128)(2,1)S(1)}, bf16[32,2048]{1,0:T(8,128)(2,1)S(1)}, u32[]{:S(2)}, u32[]{:S(2)}) collective-permute-start(bf16[32,2048]{1,0:T(8,128)(2,1)S(1)} %collective-permute-done.22.refs_2_), channel_id=1, source_target_pairs={{0,1},{1,0},{2,3},{3,2},{4,5},{5,4},{6,7},{7,6},{8,9},{9,8},{10,11... | collective-permute-start | bytes 393224 | tf_op jit(solution)/shard_map/ppermute | solution.py:314
  96.1 7.5 %collective-permute-start.27 = (bf16[32,2048]{1,0:T(8,128)(2,1)S(1)}, bf16[32,2048]{1,0:T(8,128)(2,1)S(1)}, u32[]{:S(2)}, u32[]{:S(2)}) collective-permute-start(bf16[32,2048]{1,0:T(8,128)(2,1)S(1)} %collective-permute-done.23.refs_3_), channel_id=1, source_target_pairs={{0,1},{1,0},{2,3},{3,2},{4,5},{5,4},{6,7},{7,6},{8,9},{9,8},{10,11... | collective-permute-start | bytes 393224 | tf_op jit(solution)/shard_map/ppermute | solution.py:314
  (7 other events, 61.4 us)

commit v5 on v4

--- a/solution.py
+++ b/solution.py
@@ -45,7 +45,7 @@
     return jnp.sum(jnp.where(index == wanted, table, 0.0), axis=1, keepdims=True)
 
 
-def pack_kernel(seq_dev, place, positives, ids, gates, tokens, out, tile, rows, sems):
+def pack_kernel(seq_dev, place, ids, gates, tokens, out, tile, rows, sems):
     part_rows, width = out.shape[0], tokens.shape[1]
     tok_dev = tokens.shape[0]
     seq_length = tok_dev // seq_dev
@@ -66,18 +66,15 @@
     own.start()
     for copy in copies:
         copy.start()
-    row_index = lax.broadcasted_iota(jnp.int32, (lanes, lanes), 0)
-    diagonal = row_index == lax.broadcasted_iota(jnp.int32, (lanes, lanes), 1)
     note_rows = tok_dev // lanes
     tile[...] = jnp.zeros_like(tile)
     for index in range(note_rows):
         block = slice(index * lanes, (index + 1) * lanes)
-        for offset, values in ((0, ids[block, :].astype(f32)), (note_rows, gates[block, :])):
-            line = jnp.sum(jnp.where(diagonal, values, 0.0), axis=0, keepdims=True)
-            tile[offset + index : offset + index + 1, :] = line
+        tile[index : index + 1, :] = ids[:, block].astype(f32)
+        tile[note_rows + index : note_rows + index + 1, :] = gates[:, block]
     for seq in range(seq_dev):
         row = 2 * note_rows + seq
-        tile[row : row + 1, :] = jnp.full((1, lanes), positives[seq], jnp.int32).astype(f32)
+        tile[row : row + 1, :] = jnp.full((1, lanes), place[3 + seq], jnp.int32).astype(f32)
     base = part_rows - seq_dev * (share // lanes)
     for seq in range(seq_dev):
         copies[seq].wait()
@@ -170,16 +167,31 @@
     return gate, up, sigmoid_gate, gate * sigmoid_gate
 
 
+def spread_rows(values, rows, blocks):
+    chunks = values.shape[1] // lanes
+    for index in range(values.shape[0] * chunks):
+        row, chunk = index // chunks, index % chunks
+        spot = slice(index % rows, index % rows + 1)
+        block = slice(index // rows * lanes, (index // rows + 1) * lanes)
+        blocks[spot, block] = values[row : row + 1, chunk * lanes : (chunk + 1) * lanes]
+
+
 def expert_kernel(layout, *refs):
-    chips, part_rows, near, n_parts = layout
+    chips, part_rows, near, with_last, n_parts = layout
     refs = list(refs)
     place = refs.pop(0)
     tokens = refs.pop(0) if near else None
+    last_rows = refs.pop(0) if with_last else None
     parts, refs = refs[:n_parts], refs[n_parts:]
     weights, refs = refs[:4], refs[4:]
-    outs, (rows,) = refs[:chips], refs[chips:]
-    count, width = outs[0].shape[0] // part_rows, outs[0].shape[1]
+    outs, refs = refs[:chips], refs[chips:]
+    if with_last:
+        last_projected, own_last, by_lane, tile, *refs = refs
+    (rows,) = refs
+    count = outs[0].shape[0] // part_rows
+    width = weights[0].shape[1]
     block = count * part_rows
+    total = chips * block
     if near:
         for chip in range(chips):
             start = pl.multiple_of((place[1] ^ (2 * chip)) * part_rows, part_rows)
@@ -192,62 +204,115 @@
     for chip in range(1, chips):
         at = chip * block + (count - own_parts) * part_rows
         rows[at : at + own_parts * part_rows, :] = parts[own_parts + chip - 1][:, :width]
+    if with_last:
+        rows[total:, :] = last_rows[...]
     result = None
     for half in range(2):
         w_in, w_out = weights[2 * half], weights[2 * half + 1]
-        _, up, _, activated = hidden_parts(dot(rows[...], w_in[0]))
+        projected = dot(rows[...], w_in[0])
+        if half == 0 and with_last:
+            last_projected[...] = projected[total:]
+        _, up, _, activated = hidden_parts(projected)
         part = dot((activated * up).astype(bf16), w_out[0])
         result = part if half == 0 else result + part
     for chip in range(chips):
-        outs[chip][...] = result[chip * block : (chip + 1) * block].astype(bf16)
-
-
-def last_kernel(place, rows, kept, found, w_in, w_out, projected, out, weights):
-    seqs = rows.shape[0]
-    last = kept.shape[0] - seqs
-    values = dot(rows[...], w_in[0])
-    projected[...] = values
-    _, up, _, activated = hidden_parts(values)
-    half_out = dot((activated * up).astype(bf16), w_out[0]).astype(bf16).astype(f32)
-    weight = column(kept[last:, :].astype(f32) + found[last:, :].astype(f32), place[2])
-    out[...] = (weight * half_out).astype(bf16)
-    weights[...] = jnp.broadcast_to(weight, weights.shape)
-
-
-def combine_kernel(layout, place, kept, found, own, *refs):
-    chips, part_rows, group, n_outs = layout
-    parts, outs = refs[:chips], refs[chips : chips + n_outs]
+        outs[chip][:, :width] = result[chip * block : (chip + 1) * block].astype(bf16)
+    if with_last:
+        each = last_rows.shape[0] // by_lane.shape[0]
+        floats = last_rows[...].astype(f32)
+        for lane in range(by_lane.shape[0]):
+            by_lane[lane, 0:each, :] = floats[lane * each : (lane + 1) * each]
+        spread_rows(by_lane[place[1], 0:each, :], part_rows, tile)
+        own_last[...] = tile[...]
+        for lane in range(by_lane.shape[0]):
+            first = total + lane * each
+            by_lane[lane, 0:each, :] = result[first : first + each]
+        for chip in range(chips):
+            spread_rows(by_lane[place[1] ^ (2 * chip), 0:each, :], part_rows, tile)
+            outs[chip][:part_rows, width:] = tile[...].astype(bf16)
+            outs[chip][part_rows:, width:] = jnp.zeros((block - part_rows, tile.shape[1]), bf16)
+
+
+def combine_kernel(layout, place, kept, found, *refs):
+    chips, part_rows, group, with_last, width, each = layout
+    own, refs = (refs[0], refs[1:]) if group[0] == 0 else (None, refs)
+    last_in, refs = (None, refs) if with_last else (refs[0], refs[1:])
+    parts, outs = refs[:chips], refs[chips : chips + len(group)]
     first_expert = place[2] - place[1] // 2
-    width = parts[0].shape[1]
+    experts = [first_expert + ((place[1] // 2) ^ chip) for chip in range(chips)]
+    if with_last:
+        last_out = refs[-1]
+        last = kept.shape[0] - 2 * chips * each
+        table = kept[last:, :].astype(f32) + found[last:, :].astype(f32)
+        row_index = lax.broadcasted_iota(jnp.int32, table.shape, 0)
+        chunks = width // lanes
+        for row in range(each):
+            mine = jnp.where(row_index == place[1] * each + row, table, 0.0)
+            mine = jnp.sum(mine, axis=0, keepdims=True)
+            first = row * chunks % part_rows
+            spot = slice(first, first + chunks)
+            at = row * chunks // part_rows * lanes
+            total = None
+            for chip in range(chips):
+                values = parts[chip][spot, width + at : width + at + lanes].astype(f32)
+                term = column(mine, experts[chip]) * values
+                total = term if total is None else total + term
+            last_out[spot, at : at + lanes] = total.astype(bf16)
+        last_in = last_out
     for index, hop in enumerate(group):
         at = slice(hop * part_rows, (hop + 1) * part_rows)
         table = kept[at, :].astype(f32) + found[at, :].astype(f32)
         rows = slice(index * part_rows, (index + 1) * part_rows)
         total = own[:, :width].astype(f32) if hop == 0 else None
         for chip in range(chips):
-            weight = column(table, first_expert + ((place[1] // 2) ^ chip))
-            term = weight * parts[chip][rows, :].astype(f32)
+            weight = column(table, experts[chip])
+            term = weight * parts[chip][rows, :width].astype(f32)
             total = term if total is None else total + term
-        outs[index][...] = total.astype(outs[index].dtype)
-
-
-def gather_kernel(chips, place, *refs):
-    out = refs[-1]
-    part_rows = refs[0].shape[0]
-    for chip in range(chips):
-        lane = place[1] ^ (2 * chip)
-        own = pl.multiple_of(lane * part_rows, part_rows)
-        out[pl.ds(own, part_rows), :] = refs[chip][...]
-        other = pl.multiple_of((lane ^ 1) * part_rows, part_rows)
-        out[pl.ds(other, part_rows), :] = refs[chips + chip][...]
+        outs[index][:, :width] = total.astype(outs[index].dtype)
+        if hop:
+            outs[index][:, width:] = last_in[...]
+
+
+def finish_kernel(near, own_last, last_sum, *refs):
+    parts, out = refs[:-1], refs[-1]
+    width = near.shape[1]
+    total = near[...]
+    last = last_sum[...].astype(f32)
+    for part in parts:
+        total = total + part[:, :width].astype(f32)
+        last = last + part[:, width:].astype(f32)
+    out[:, :width] = total.astype(bf16)
+    out[:, width:] = (own_last[...] + last).astype(bf16)
+
+
+def gather_kernel(chips, each, place, *refs):
+    pieces, (out, last_rows, by_lane) = refs[: 2 * chips], refs[2 * chips :]
+    part_rows, width = pieces[0].shape[0], out.shape[1]
+    chunks = width // lanes
+    for index in range(2 * chips):
+        lane = place[1] ^ (2 * (index % chips)) ^ (index // chips)
+        piece = pieces[index]
+        start = pl.multiple_of(lane * part_rows, part_rows)
+        out[pl.ds(start, part_rows), :] = piece[:, :width]
+        values = piece[:, width:].astype(f32)
+        for spot in range(each * chunks):
+            row, chunk = spot // chunks, spot % chunks
+            at = spot // part_rows * lanes
+            from_row = spot % part_rows
+            by_lane[lane, row : row + 1, chunk * lanes : (chunk + 1) * lanes] = values[
+                from_row : from_row + 1, at : at + lanes
+            ]
+    ordered = [by_lane[lane, 0:each, :] for lane in range(2 * chips)]
+    last_rows[...] = jnp.concatenate(ordered, axis=0).astype(bf16)
 
 
 def gradient_kernel(
-    last_all,
     last_block,
-    last_sum,
+    layer_last,
     projected,
-    weights,
+    place,
+    kept,
+    found,
     partners,
     down,
     grad_in,
@@ -262,9 +327,10 @@
 
     @pl.when(step == 0)
     def _():
-        layer_last = (last_all[...].astype(f32) + last_sum[...].astype(f32)).astype(bf16)
-        values = layer_last.astype(f32)
+        values = layer_last[...].astype(f32)
         count = values.shape[0]
+        last = kept.shape[0] - count
+        table = kept[last:, :].astype(f32) + found[last:, :].astype(f32)
         norms = jnp.sqrt(jnp.sum(values * values, axis=1, keepdims=True) + epsilon)
         unit = values / norms
         scores = dot(unit, unit, ((1,), (1,)), lax.Precision.HIGHEST) / logit_divisor
@@ -280,7 +346,7 @@
         ) / logit_divisor
         projection = jnp.sum(unit * grad_unit, axis=1, keepdims=True)
         grad_last = (grad_unit - unit * projection) / norms
-        route_grad = (weights[:, :1] * grad_last).astype(bf16)
+        route_grad = (column(table, place[2]) * grad_last).astype(bf16)
         for index in range(route.shape[0]):
             route[index] = route_grad[:, index * block : (index + 1) * block]
         grad_hidden = dot(route_grad, down[0], ((1,), (1,)))
@@ -308,6 +374,7 @@
     plane = lax.axis_index("dp")
     lane = lax.axis_index("expert")
     place = jnp.stack([plane, lane, plane * chips + lane // 2]).astype(jnp.int32)
+    place = jnp.concatenate([place, positives])
     assert experts <= lanes and seq_length % tail == 0
 
     def to_lane(value, step):
@@ -323,7 +390,7 @@
     packed = pl.pallas_call(
         functools.partial(pack_kernel, seq_dev),
         out_shape=jax.ShapeDtypeStruct((part_rows, width + lanes), bf16),
-        in_specs=[in_smem, in_smem, in_vmem, in_vmem, anywhere],
+        in_specs=[in_smem, in_vmem, in_vmem, pl.BlockSpec(memory_space=pltpu.HBM)],
         out_specs=in_vmem,
         scratch_shapes=[
             pltpu.VMEM((part_rows, lanes), f32),
@@ -333,13 +400,12 @@
         compiler_params=params(4),
         cost_estimate=cost(0, 1 << 19),
         name="pack",
-    )(place, positives, expert_ids, gates, tokens)
+    )(place, expert_ids.T, gates.T, tokens)
     arrivals = {hop: to_plane(packed, hop) for hop in range(1, dp_count)}
     mate_in = to_lane(gate_up, 1)
     mate_out = to_lane(down, 1)
     weights = (gate_up, down, mate_in, mate_out)
 
-    groups.reverse()
     far_parts = []
     tiles = []
     where_tiles = [[None] * chips for _ in range(dp_count)]
@@ -347,8 +413,12 @@
         own = [arrivals[hop] for hop in group if hop]
         if group[0] == 0:
             joined = jnp.concatenate(own + [packed[:, width:]], axis=1)
+            joined, weights = lax.optimization_barrier((joined, weights))
         else:
             joined = jnp.concatenate(own, axis=0)
+            joined, received = lax.optimization_barrier((joined, received))
+            tiles[-len(received) :] = received
+            far_parts[-1][-len(received) :] = received
         received = [to_lane(joined, step) for step in chip_steps]
         far_parts.append(own + received)
         for index, hop in enumerate(group):
@@ -366,29 +436,6 @@
             for chip in range(1, chips):
                 where_tiles[hop][chip] = (first + chip - 1,) + where_tiles[hop][chip][1:]
 
-    def expert(group, parts, place):
-        near = group[0] == 0
-        block = len(group) * part_rows
-        total = chips * block
-        operands = [place] + [tokens] * near + parts + list(weights)
-        return pl.pallas_call(
-            functools.partial(expert_kernel, (chips, part_rows, near, len(parts))),
-            out_shape=[jax.ShapeDtypeStruct((block, width), bf16)] * chips,
-            in_specs=[in_smem] + [in_vmem] * (len(operands) - 1),
-            out_specs=[in_vmem] * chips,
-            scratch_shapes=[pltpu.VMEM((total, width), bf16)],
-            compiler_params=params(32),
-            cost_estimate=cost(2 * total * width * 6 * half_width, 12 << 20),
-            name="experts",
-        )(*operands)
-
-    outs = []
-    after = place
-    for group, parts in zip(groups, far_parts):
-        outs.append(expert(group, parts, after))
-        after, _ = lax.optimization_barrier((place, outs[-1][0]))
-    table_place, _ = lax.optimization_barrier((place, outs[0][0]))
-
     table_rows = dp_count * part_rows + seqs
     chunks = width // lanes
     sublanes = -(-seq_dev // 8) * 8
@@ -410,61 +457,113 @@
         compiler_params=params(48 if dp_count > 8 else 12),
         cost_estimate=cost(0, 1 << 20),
         name="tables",
-    )(table_place, *tiles)
+    )(place, *tiles)
     found = to_lane(sent, 1)
 
-    last_projected, last_sum, last_weights = pl.pallas_call(
-        last_kernel,
-        out_shape=[
-            jax.ShapeDtypeStruct((seqs, 2 * half_width), f32),
-            jax.ShapeDtypeStruct((seqs, width), bf16),
-            jax.ShapeDtypeStruct((seqs, lanes), f32),
-        ],
-        in_specs=[in_smem] + [in_vmem] * 5,
-        out_specs=[in_vmem] * 3,
-        compiler_params=params(16),
-        cost_estimate=cost(2 * seqs * width * 3 * half_width, 5 << 20),
-        name="last_rows",
-    )(place, last_all, kept, found, gate_up, down)
-
-    def combine(group, parts):
+    each = seqs // expert_count
+    extra = each * width // part_rows
+    assert extra % lanes == 0 and part_rows % (width // lanes) == 0
+
+    def expert(group, parts, place, with_last):
+        near = group[0] == 0
+        block = len(group) * part_rows
+        total = chips * block + (seqs if with_last else 0)
+        out_width = width + (extra if with_last else 0)
+        out_shape = [jax.ShapeDtypeStruct((block, out_width), bf16)] * chips
+        scratch = [pltpu.VMEM((total, width), bf16)]
+        if with_last:
+            out_shape += [
+                jax.ShapeDtypeStruct((seqs, 2 * half_width), f32),
+                jax.ShapeDtypeStruct((part_rows, extra), f32),
+            ]
+            scratch = [
+                pltpu.VMEM((expert_count, -(-each // 8) * 8, width), f32),
+                pltpu.VMEM((part_rows, extra), f32),
+            ] + scratch
+        operands = [place] + [tokens] * near + [last_all] * with_last + parts + list(weights)
+        return pl.pallas_call(
+            functools.partial(expert_kernel, (chips, part_rows, near, with_last, len(parts))),
+            out_shape=out_shape,
+            in_specs=[in_smem] + [in_vmem] * (len(operands) - 1),
+            out_specs=[in_vmem] * len(out_shape),
+            scratch_shapes=scratch,
+            compiler_params=params(32),
+            cost_estimate=cost(2 * total * width * 6 * half_width, 12 << 20),
+            name="experts",
+        )(*operands)
+
+    def combine(group, parts, last_sum):
+        with_last = last_sum is None
         out_shape = [
-            jax.ShapeDtypeStruct((part_rows, width), bf16 if hop else f32) for hop in group
+            jax.ShapeDtypeStruct((part_rows, width + extra), bf16)
+            if hop
+            else jax.ShapeDtypeStruct((part_rows, width), f32)
+            for hop in group
         ]
-        layout = (chips, part_rows, tuple(group), len(group))
+        if with_last:
+            out_shape.append(jax.ShapeDtypeStruct((part_rows, extra), bf16))
+        layout = (chips, part_rows, tuple(group), with_last, width, each)
+        operands = [place, kept, found]
+        operands += [packed] * (group[0] == 0) + [last_sum] * (not with_last) + parts
         return pl.pallas_call(
             functools.partial(combine_kernel, layout),
             out_shape=out_shape,
-            in_specs=[in_smem] + [in_vmem] * (3 + chips),
-            out_specs=[in_vmem] * len(group),
+            in_specs=[in_smem] + [in_vmem] * (len(operands) - 1),
+            out_specs=[in_vmem] * len(out_shape),
             compiler_params=params(8),
             cost_estimate=cost(0, 3 << 20),
             name="combine",
-        )(place, kept, found, packed, *parts)
+        )(*operands)
+
+    outs = []
+    after = place
+    for group, parts in zip(groups, far_parts):
+        outs.append(expert(group, parts, after, group is groups[-1]))
+        after, _ = lax.optimization_barrier((place, outs[-1][0]))
+    last_projected, own_last = outs[-1][chips:]
 
     sums = {}
-    for group, out in zip(groups, outs):
-        returned = [to_lane(out[index + 1], step) for index, step in enumerate(chip_steps)]
-        for hop, value in zip(group, combine(group, [out[0]] + returned)):
-            sums[hop] = value
-
-    for step in doublings(expert_count):
-        last_sum = (last_sum.astype(f32) + to_lane(last_sum, step).astype(f32)).astype(bf16)
-    for step in doublings(dp_count):
-        last_sum = (last_sum.astype(f32) + to_plane(last_sum, step).astype(f32)).astype(bf16)
-
-    total = sums[0]
-    for hop in range(1, dp_count):
-        total = total + to_plane(sums[hop], hop).astype(f32)
-    own_out = total.astype(bf16)
+    last_sum = None
+    returned = None
+    for index in [len(groups) - 1] + list(range(len(groups) - 2, -1, -1)):
+        group, sent_back = groups[index], list(outs[index][1:chips])
+        if returned is None:
+            sent_back, found = lax.optimization_barrier((sent_back, found))
+        else:
+            result = combine(before, [first] + returned, last_sum)
+            sums.update(zip(before, result))
+            last_sum = result[-1] if last_sum is None else last_sum
+            sent_back, _ = lax.optimization_barrier((sent_back, result[0]))
+        returned = [to_lane(value, step) for value, step in zip(sent_back, chip_steps)]
+        before, first = group, outs[index][0]
+    homeward = {hop: to_plane(value, hop) for hop, value in sums.items()}
+    returned, homeward = lax.optimization_barrier((returned, homeward))
+    result = combine(before, [first] + returned, last_sum)
+    last_sum = result[-1] if last_sum is None else last_sum
+    sums.update(zip(before, result))
+    homeward.update({hop: to_plane(sums[hop], hop) for hop in before if hop})
+
+    own_out = pl.pallas_call(
+        finish_kernel,
+        out_shape=jax.ShapeDtypeStruct((part_rows, width + extra), bf16),
+        in_specs=[in_vmem] * (2 + dp_count),
+        out_specs=in_vmem,
+        compiler_params=params(16 if dp_count > 8 else 4),
+        cost_estimate=cost(0, 1 << 20),
+        name="finish",
+    )(sums[0], own_last, last_sum, *homeward.values())
     pieces = [own_out] + [to_lane(own_out, step) for step in chip_steps]
     pieces += [to_lane(piece, 1) for piece in pieces]
-    layer_out = pl.pallas_call(
-        functools.partial(gather_kernel, chips),
-        out_shape=jax.ShapeDtypeStruct((tok_dev, width), bf16),
+    layer_out, layer_last = pl.pallas_call(
+        functools.partial(gather_kernel, chips, each),
+        out_shape=[
+            jax.ShapeDtypeStruct((tok_dev, width), bf16),
+            jax.ShapeDtypeStruct((seqs, width), bf16),
+        ],
         in_specs=[in_smem] + [in_vmem] * len(pieces),
-        out_specs=in_vmem,
-        compiler_params=params(4),
+        out_specs=[in_vmem] * 2,
+        scratch_shapes=[pltpu.VMEM((expert_count, -(-each // 8) * 8, width), f32)],
+        compiler_params=params(8),
         cost_estimate=cost(0, 2 << 20),
         name="gather",
     )(place, *pieces)
@@ -479,11 +578,12 @@
             jax.ShapeDtypeStruct(down.shape, bf16),
         ],
         in_specs=[
-            pl.BlockSpec((seqs, width), lambda step: (0, 0)),
             pl.BlockSpec((seqs, block), lambda step: (0, step)),
             pl.BlockSpec((seqs, width), lambda step: (0, 0)),
             pl.BlockSpec((seqs, 2 * half_width), lambda step: (0, 0)),
-            pl.BlockSpec((seqs, lanes), lambda step: (0, 0)),
+            in_smem,
+            pl.BlockSpec((table_rows, lanes), lambda step: (0, 0)),
+            pl.BlockSpec((table_rows, lanes), lambda step: (0, 0)),
             pl.BlockSpec((seqs, lanes), lambda step: (0, 0)),
             pl.BlockSpec((1, half_width, width), lambda step: (0, 0, 0)),
         ],
@@ -499,7 +599,7 @@
         compiler_params=params(24),
         cost_estimate=cost(2 * seqs * width * 4 * half_width, 7 << 20),
         name="gradients",
-    )(last_all, last_all, last_sum, last_projected, last_weights, partners, down)
+    )(last_all, layer_last, last_projected, place, kept, found, partners, down)
     return (layer_out, grad_gate_up, grad_down)
 
 

time: 106 us -> 102 us (0.962)
  starting transfers between devices: 41.1 us -> 27.1 us
  waiting for transfers between devices: 35.3 us -> 45.7 us
    ppermute x8 -> x6, waiting for transfers between devices: 15 us -> 24.7 us  [to_plane(): return lax.ppermute(value, 'dp', [(p, p ^ step) for p in range(dp_count)])]
    ppermute x8 -> x6, starting transfers between devices: 17.1 us -> 8.17 us  [to_plane(): return lax.ppermute(value, 'dp', [(p, p ^ step) for p in range(dp_count)])]
    ppermute x25 -> x22, starting transfers between devices: 23.9 us -> 19 us  [to_lane(): lax.ppermute(value, 'expert', [(j, j ^ step) for j in range(expert_count)])]
    pallas_call x2, Pallas kernels: 3.19 us -> 1.72 us  [the longest x1 1.64 us: body(): pl.pallas_call(functools.partial(gather_kernel, chips, each), out_shape=[...]
    ppermute x25 -> x22, waiting for transfers between devices: 20.3 us -> 21.1 us  [to_lane(): lax.ppermute(value, 'expert', [(j, j ^ step) for j in range(expert_count)])]
    unnamed x15 -> x12, local copies, waits for them, and re-layouts: 5.41 us -> 5.7 us
  transfers between devices with their start and end apart: 33 -> 28, of which waited for: 11 -> 14; matrix products, arithmetic and copies ran while one was open for 2% -> 1% of each run, Pallas kernels for 17% -> 11%
where the time goes in v5:
time: 102 us
  waiting for transfers between devices  45.7 us (45%)
  starting transfers between devices  27.1 us (27%)
  Pallas kernels  21.5 us (21%)
  local copies, waits for them, and re-layouts  5.7 us (6%)
    ppermute x6, waiting for transfers between devices, to_plane(): return lax.ppermute(value, 'dp', [(p, p ^ step) for p in range(dp_count)])  24.7 us
    ppermute x22, waiting for transfers between devices, to_lane(): lax.ppermute(value, 'expert', [(j, j ^ step) for j in range(expert_count)])  21.1 us
    ppermute x22, starting transfers between devices, to_lane(): lax.ppermute(value, 'expert', [(j, j ^ step) for j in range(expert_count)])  19 us
    pallas_call x2, Pallas kernels, expert(): pl.pallas_call(functools.partial(expert_kernel, (chips, part_rows, near,...  10.1 us
    ppermute x6, starting transfers between devices, to_plane(): return lax.ppermute(value, 'dp', [(p, p ^ step) for p in range(dp_count)])  8.17 us
    pallas_call x1, Pallas kernels, body(): pl.pallas_call(gradient_kernel, grid=(steps,), out_shape=[jax.ShapeDtypeS...  6.26 us
    unnamed x12, local copies, waits for them, and re-layouts  5.7 us
  transfers between devices with their start and end apart: 28, of which 14 were waited for; matrix products, arithmetic and copies ran while one was open for 1% of the time, Pallas kernels for 11%

profile of v5, /device:TPU:0, one launch (start us, length us, event | category | flops | bytes accessed | tf_op | source)
XLA Modules:
  0.0 101.6 jit_solution(14088415189863820648)
XLA Ops:
  2.0 1.2 %copy-done.2 = bf16[256,2048]{1,0:T(8,128)(2,1)S(1)} copy-done((bf16[256,2048]{1,0:T(8,128)(2,1)S(1)}, bf16[256,2048]{1,0:T(8,128)(2,1)}, u32[]{:S(2)}) %copy-start.2) | copy-done | bytes 1048600
  5.3 3.1 %collective-permute-start = (bf16[32,2176]{1,0:T(8,128)(2,1)S(1)}, bf16[32,2176]{1,0:T(8,128)(2,1)S(1)}, u32[]{:S(2)}, u32[]{:S(2)}) collective-permute-start(bf16[32,2176]{1,0:T(8,128)(2,1)S(1)} %pack.1.refs_0_), channel_id=1, source_target_pairs={{0,8},{8,0},{16,24},{24,16},{1,9},{9,1},{17,25},{25,17},{2,10},{10... | collective-permute-start | bytes 417800 | tf_op jit(solution)/shard_map/ppermute | solution.py:384
  8.3 2.5 %collective-permute-start.2 = (bf16[32,2176]{1,0:T(8,128)(2,1)S(1)}, bf16[32,2176]{1,0:T(8,128)(2,1)S(1)}, u32[]{:S(2)}, u32[]{:S(2)}) collective-permute-start(bf16[32,2176]{1,0:T(8,128)(2,1)S(1)} %pack.1.refs_0_), channel_id=1, source_target_pairs={{0,24},{8,16},{16,8},{24,0},{1,25},{9,17},{17,9},{25,1},{2,26},{10... | collective-permute-start | bytes 417800 | tf_op jit(solution)/shard_map/ppermute | solution.py:384
  10.9 1.3 %collective-permute-done.refs_1_.refs_2_ = bf16[32,2176]{1,0:T(8,128)(2,1)S(1)} collective-permute-done((bf16[32,2176]{1,0:T(8,128)(2,1)S(1)}, bf16[32,2176]{1,0:T(8,128)(2,1)S(1)}, u32[]{:S(2)}, u32[]{:S(2)}) %collective-permute-start) | collective-permute-done | bytes 139296 | tf_op jit(solution)/shard_map/ppermute | solution.py:384
  12.3 2.7 %collective-permute-start.7 = (bf16[32,2304]{1,0:T(8,128)(2,1)S(1)}, bf16[32,2304]{1,0:T(8,128)(2,1)S(1)}, u32[]{:S(2)}, u32[]{:S(2)}) collective-permute-start(bf16[32,2304]{1,0:T(8,128)(2,1)S(1)} %pad_maximum_fusion.1), channel_id=1, source_target_pairs={{0,6},{1,7},{2,4},{3,5},{4,2},{5,3},{6,0},{7,1},{8,14},{9,15},{10,... | collective-permute-start | bytes 442376 | tf_op jit(solution)/shard_map/ppermute | solution.py:381
  15.9 2.5 %collective-permute-done.2.refs_6_.refs_3_ = bf16[32,2176]{1,0:T(8,128)(2,1)S(1)} collective-permute-done((bf16[32,2176]{1,0:T(8,128)(2,1)S(1)}, bf16[32,2176]{1,0:T(8,128)(2,1)S(1)}, u32[]{:S(2)}, u32[]{:S(2)}) %collective-permute-start.2) | collective-permute-done | bytes 139296 | tf_op jit(solution)/shard_map/ppermute | solution.py:384
  18.4 5.1 %collective-permute-done.1.refs_5_.refs_2_ = bf16[32,2176]{1,0:T(8,128)(2,1)S(1)} collective-permute-done((bf16[32,2176]{1,0:T(8,128)(2,1)S(1)}, bf16[32,2176]{1,0:T(8,128)(2,1)S(1)}, u32[]{:S(2)}, u32[]{:S(2)}) %collective-permute-start.1) | collective-permute-done | bytes 139296 | tf_op jit(solution)/shard_map/ppermute | solution.py:384
  23.6 2.5 %collective-permute-start.10 = (bf16[64,2176]{1,0:T(8,128)(2,1)S(1)}, bf16[64,2176]{1,0:T(8,128)(2,1)S(1)}, u32[]{:S(2)}, u32[]{:S(2)}) collective-permute-start(bf16[64,2176]{1,0:T(8,128)(2,1)S(1)} %pad_maximum_fusion), channel_id=1, source_target_pairs={{0,6},{1,7},{2,4},{3,5},{4,2},{5,3},{6,0},{7,1},{8,14},{9,15},{10,... | collective-permute-start | bytes 835592 | tf_op jit(solution)/shard_map/ppermute | solution.py:381
  27.1 1.9 %copy-done.1 = bf16[1,2048,768]{2,1,0:T(8,128)(2,1)S(1)} copy-done((bf16[1,2048,768]{2,1,0:T(8,128)(2,1)S(1)}, bf16[1,2048,768]{2,1,0:T(8,128)(2,1)}, u32[]{:S(2)}) %copy-start.1) | copy-done | bytes 3145752
  29.0 1.2 %copy-done.3 = bf16[256,2048]{1,0:T(8,128)(2,1)S(1)} copy-done((bf16[256,2048]{1,0:T(8,128)(2,1)S(1)}, bf16[256,2048]{1,0:T(8,128)(2,1)}, u32[]{:S(2)}) %copy-start.3) | copy-done | bytes 1048600
  30.2 4.9 %experts.2 = (bf16[64,2048]{1,0:T(8,128)(2,1)S(1)}, bf16[64,2048]{1,0:T(8,128)(2,1)S(1)}, bf16[64,2048]{1,0:T(8,128)(2,1)S(1)}, bf16[64,2048]{1,0:T(8,128)(2,1)S(1)}) custom-call(s32[7]{0:T(128)S(1)} %pad_add_fusion.place.refs_0_, bf16[256,2048]{1,0:T(8,128)(2,1)S(1)} %copy-done.3, bf16[32,2176]{1,0:T(8,128)(2,1)S(1)} %collective-permute-done.refs_1_.refs_2_, ...), custom_call_target="tpu_custom_call" | custom-call | flops 2415919104 | bytes 12582912 | tf_op jit(solution)/shard_map/experts/pallas_call | solution.py:484
  35.2 3.2 %collective-permute-done.9.refs_8_.refs_5_ = bf16[64,2176]{1,0:T(8,128)(2,1)S(1)} collective-permute-done((bf16[64,2176]{1,0:T(8,128)(2,1)S(1)}, bf16[64,2176]{1,0:T(8,128)(2,1)S(1)}, u32[]{:S(2)}, u32[]{:S(2)}) %collective-permute-start.9) | collective-permute-done | bytes 278560 | tf_op jit(solution)/shard_map/ppermute | solution.py:381
  38.5 1.1 %tables.1 = (bf16[144,128]{1,0:T(8,128)(2,1)S(1)}, bf16[144,128]{1,0:T(8,128)(2,1)S(1)}, bf16[16,2048]{1,0:T(8,128)(2,1)S(1)}, f32[16,128]{1,0:T(8,128)S(1)}) custom-call(s32[7]{0:T(128)S(1)} %pad_add_fusion.place.refs_0_, bf16[32,2176]{1,0:T(8,128)(2,1)S(1)} %pack.1.refs_0_, bf16[32,2176]{1,0:T(8,128)(2,1)S(1)} %collective-permute-done.refs_1_.refs_2_, ...), custom_call_target="tpu_custom_call" | custom-call | bytes 1048576 | tf_op jit(solution)/shard_map/tables/pallas_call | solution.py:442
  39.6 5.2 %experts.3 = (bf16[64,2176]{1,0:T(8,128)(2,1)S(1)}, bf16[64,2176]{1,0:T(8,128)(2,1)S(1)}, bf16[64,2176]{1,0:T(8,128)(2,1)S(1)}, bf16[64,2176]{1,0:T(8,128)(2,1)S...) custom-call(s32[7]{0:T(128)S(1)} %pad_add_fusion.place.refs_0_, ...), custom_call_target="tpu_custom_call" | custom-call | flops 2566914048 | bytes 12582912 | tf_op jit(solution)/shard_map/experts/pallas_call | solution.py:484
  44.8 1.6 %collective-permute-start.12 = (bf16[64,2176]{1,0:T(8,128)(2,1)S(1)}, bf16[64,2176]{1,0:T(8,128)(2,1)S(1)}, u32[]{:S(2)}, u32[]{:S(2)}) collective-permute-start(bf16[64,2176]{1,0:T(8,128)(2,1)S(1)} %get-tuple-element.67), channel_id=1, source_target_pairs={{0,2},{1,3},{2,0},{3,1},{4,6},{5,7},{6,4},{7,5},{8,10},{9,11},{10,... | collective-permute-start | bytes 835592 | tf_op jit(solution)/shard_map/ppermute | solution.py:381
  47.1 1.3 %collective-permute-start.14 = (bf16[64,2176]{1,0:T(8,128)(2,1)S(1)}, bf16[64,2176]{1,0:T(8,128)(2,1)S(1)}, u32[]{:S(2)}, u32[]{:S(2)}) collective-permute-start(bf16[64,2176]{1,0:T(8,128)(2,1)S(1)} %get-tuple-element.69), channel_id=1, source_target_pairs={{0,6},{1,7},{2,4},{3,5},{4,2},{5,3},{6,0},{7,1},{8,14},{9,15},{10,... | collective-permute-start | bytes 835592 | tf_op jit(solution)/shard_map/ppermute | solution.py:381
  48.3 6.0 %collective-permute-done.12.refs_1_ = bf16[64,2176]{1,0:T(8,128)(2,1)S(1)} collective-permute-done((bf16[64,2176]{1,0:T(8,128)(2,1)S(1)}, bf16[64,2176]{1,0:T(8,128)(2,1)S(1)}, u32[]{:S(2)}, u32[]{:S(2)}) %collective-permute-start.12) | collective-permute-done | bytes 278560 | tf_op jit(solution)/shard_map/ppermute | solution.py:381
  54.3 6.8 %collective-permute-done.13.refs_2_ = bf16[64,2176]{1,0:T(8,128)(2,1)S(1)} collective-permute-done((bf16[64,2176]{1,0:T(8,128)(2,1)S(1)}, bf16[64,2176]{1,0:T(8,128)(2,1)S(1)}, u32[]{:S(2)}, u32[]{:S(2)}) %collective-permute-start.13) | collective-permute-done | bytes 278560 | tf_op jit(solution)/shard_map/ppermute | solution.py:381
  62.5 1.4 %collective-permute-start.16 = (bf16[64,2048]{1,0:T(8,128)(2,1)S(1)}, bf16[64,2048]{1,0:T(8,128)(2,1)S(1)}, u32[]{:S(2)}, u32[]{:S(2)}) collective-permute-start(bf16[64,2048]{1,0:T(8,128)(2,1)S(1)} %get-tuple-element.76), channel_id=1, source_target_pairs={{0,4},{1,5},{2,6},{3,7},{4,0},{5,1},{6,2},{7,3},{8,12},{9,13},{10,... | collective-permute-start | bytes 786440 | tf_op jit(solution)/shard_map/ppermute | solution.py:381
  63.9 1.5 %collective-permute-start.17 = (bf16[64,2048]{1,0:T(8,128)(2,1)S(1)}, bf16[64,2048]{1,0:T(8,128)(2,1)S(1)}, u32[]{:S(2)}, u32[]{:S(2)}) collective-permute-start(bf16[64,2048]{1,0:T(8,128)(2,1)S(1)} %get-tuple-element.77), channel_id=1, source_target_pairs={{0,6},{1,7},{2,4},{3,5},{4,2},{5,3},{6,0},{7,1},{8,14},{9,15},{10,... | collective-permute-start | bytes 786440 | tf_op jit(solution)/shard_map/ppermute | solution.py:381
  65.5 2.4 %collective-permute-start.19 = (bf16[32,2176]{1,0:T(8,128)(2,1)S(1)}, bf16[32,2176]{1,0:T(8,128)(2,1)S(1)}, u32[]{:S(2)}, u32[]{:S(2)}) collective-permute-start(bf16[32,2176]{1,0:T(8,128)(2,1)S(1)} %get-tuple-element.78), channel_id=1, source_target_pairs={{0,24},{8,16},{16,8},{24,0},{1,25},{9,17},{17,9},{25,1},{2,26},{10... | collective-permute-start | bytes 417800 | tf_op jit(solution)/shard_map/ppermute | solution.py:384
  67.9 5.1 %collective-permute-done.19.refs_1_ = bf16[32,2176]{1,0:T(8,128)(2,1)S(1)} collective-permute-done((bf16[32,2176]{1,0:T(8,128)(2,1)S(1)}, bf16[32,2176]{1,0:T(8,128)(2,1)S(1)}, u32[]{:S(2)}, u32[]{:S(2)}) %collective-permute-start.19) | collective-permute-done | bytes 139296 | tf_op jit(solution)/shard_map/ppermute | solution.py:384
  73.0 5.5 %collective-permute-done.18.refs_0_ = bf16[32,2176]{1,0:T(8,128)(2,1)S(1)} collective-permute-done((bf16[32,2176]{1,0:T(8,128)(2,1)S(1)}, bf16[32,2176]{1,0:T(8,128)(2,1)S(1)}, u32[]{:S(2)}, u32[]{:S(2)}) %collective-permute-start.18) | collective-permute-done | bytes 139296 | tf_op jit(solution)/shard_map/ppermute | solution.py:384
  78.5 0.8 combine.3
  79.5 5.0 %collective-permute-done.20.refs_2_ = bf16[32,2176]{1,0:T(8,128)(2,1)S(1)} collective-permute-done((bf16[32,2176]{1,0:T(8,128)(2,1)S(1)}, bf16[32,2176]{1,0:T(8,128)(2,1)S(1)}, u32[]{:S(2)}, u32[]{:S(2)}) %collective-permute-start.20) | collective-permute-done | bytes 139296 | tf_op jit(solution)/shard_map/ppermute | solution.py:384
  84.6 1.5 %collective-permute-start.23 = (bf16[32,2176]{1,0:T(8,128)(2,1)S(1)}, bf16[32,2176]{1,0:T(8,128)(2,1)S(1)}, u32[]{:S(2)}, u32[]{:S(2)}) collective-permute-start(bf16[32,2176]{1,0:T(8,128)(2,1)S(1)} %finish.1.refs_0_), channel_id=1, source_target_pairs={{0,6},{1,7},{2,4},{3,5},{4,2},{5,3},{6,0},{7,1},{8,14},{9,15},{10,... | collective-permute-start | bytes 417800 | tf_op jit(solution)/shard_map/ppermute | solution.py:381
  86.7 1.5 %collective-permute-start.21 = (bf16[32,2176]{1,0:T(8,128)(2,1)S(1)}, bf16[32,2176]{1,0:T(8,128)(2,1)S(1)}, u32[]{:S(2)}, u32[]{:S(2)}) collective-permute-start(bf16[32,2176]{1,0:T(8,128)(2,1)S(1)} %finish.1.refs_0_), channel_id=1, source_target_pairs={{0,2},{1,3},{2,0},{3,1},{4,6},{5,7},{6,4},{7,5},{8,10},{9,11},{10,... | collective-permute-start | bytes 417800 | tf_op jit(solution)/shard_map/ppermute | solution.py:381
  88.2 2.6 %collective-permute-done.23.refs_3_ = bf16[32,2176]{1,0:T(8,128)(2,1)S(1)} collective-permute-done((bf16[32,2176]{1,0:T(8,128)(2,1)S(1)}, bf16[32,2176]{1,0:T(8,128)(2,1)S(1)}, u32[]{:S(2)}, u32[]{:S(2)}) %collective-permute-start.23) | collective-permute-done | bytes 139296 | tf_op jit(solution)/shard_map/ppermute | solution.py:381
  90.7 1.4 %collective-permute-done.22.refs_2_ = bf16[32,2176]{1,0:T(8,128)(2,1)S(1)} collective-permute-done((bf16[32,2176]{1,0:T(8,128)(2,1)S(1)}, bf16[32,2176]{1,0:T(8,128)(2,1)S(1)}, u32[]{:S(2)}, u32[]{:S(2)}) %collective-permute-start.22) | collective-permute-done | bytes 139296 | tf_op jit(solution)/shard_map/ppermute | solution.py:381
  92.6 0.8 collective-permute-done.26.refs_6_
  93.7 1.6 %gather.1 = (bf16[256,2048]{1,0:T(8,128)(2,1)}, bf16[16,2048]{1,0:T(8,128)(2,1)S(1)}) custom-call(s32[7]{0:T(128)S(1)} %pad_add_fusion.place.refs_0_, bf16[32,2176]{1,0:T(8,128)(2,1)S(1)} %finish.1.refs_0_, bf16[32,2176]{1,0:T(8,128)(2,1)S(1)} %collective-permute-done.21.refs_1_, bf16[32,2176]{1,0:T(8,128)(2,1)S(1)} %collective-permute-done.22.refs_2_, ...), custom_call_target="tpu_custom_call" | custom-call | bytes 2097152 | tf_op jit(solution)/shard_map/gather/pallas_call | solution.py:557
  95.3 6.3 %gradients.1 = (bf16[1,2048,768]{2,1,0:T(8,128)(2,1)}, bf16[1,384,2048]{2,1,0:T(8,128)(2,1)}) custom-call(bf16[16,2048]{1,0:T(8,128)(2,1)S(1)} %get-tuple-element.60.refs_1_.last_block, bf16[16,2048]{1,0:T(8,128)(2,1)S(1)} %get-tuple-element.88.layer_last, f32[16,768]{1,0:T(8,128)S(1)} %get-tuple-element.89.projected, s32[7]{0:T(128)S(1)} %pad_add_fusion.place.refs_0_, ...), custom_call_target="tpu_custom_call" | custom-call | flops 100663296 | bytes 7340032 | tf_op jit(solution)/shard_map/gradients/pallas_call | solution.py:573
  (49 shorter events, 9.3 us)
Async XLA Ops:
  0.6 26.5 %copy-start = (bf16[1,384,2048]{2,1,0:T(8,128)(2,1)S(1)}, bf16[1,384,2048]{2,1,0:T(8,128)(2,1)}, u32[]{:S(2)}) copy-start(bf16[1,384,2048]{2,1,0:T(8,128)(2,1)} %down.1) | copy-start | bytes 4718596
  0.6 11.7 %collective-permute-start.3 = (bf16[1,2048,768]{2,1,0:T(8,128)(2,1)}, bf16[1,2048,768]{2,1,0:T(8,128)(2,1)}, u32[]{:S(2)}, u32[]{:S(2)}) collective-permute-start(bf16[1,2048,768]{2,1,0:T(8,128)(2,1)} %refs_7_.1), channel_id=1, source_target_pairs={{0,1},{1,0},{2,3},{3,2},{4,5},{5,4},{6,7},{7,6},{8,9},{9,8},{10,11... | collective-permute-start | bytes 9437192 | tf_op jit(solution)/shard_map/ppermute | solution.py:381
  1.2 11.1 %collective-permute-start.4 = (bf16[1,384,2048]{2,1,0:T(8,128)(2,1)}, bf16[1,384,2048]{2,1,0:T(8,128)(2,1)S(1)}, u32[]{:S(2)}, u32[]{:S(2)}) collective-permute-start(bf16[1,384,2048]{2,1,0:T(8,128)(2,1)} %down.1), channel_id=1, source_target_pairs={{0,1},{1,0},{2,3},{3,2},{4,5},{5,4},{6,7},{7,6},{8,9},{9,8},{10,11... | collective-permute-start | bytes 4718600 | tf_op jit(solution)/shard_map/ppermute | solution.py:381
  2.0 1.2 %copy-start.2 = (bf16[256,2048]{1,0:T(8,128)(2,1)S(1)}, bf16[256,2048]{1,0:T(8,128)(2,1)}, u32[]{:S(2)}) copy-start(bf16[256,2048]{1,0:T(8,128)(2,1)} %refs_1_.1) | copy-start | bytes 3145732
  5.3 7.0 %collective-permute-start = (bf16[32,2176]{1,0:T(8,128)(2,1)S(1)}, bf16[32,2176]{1,0:T(8,128)(2,1)S(1)}, u32[]{:S(2)}, u32[]{:S(2)}) collective-permute-start(bf16[32,2176]{1,0:T(8,128)(2,1)S(1)} %pack.1.refs_0_), channel_id=1, source_target_pairs={{0,8},{8,0},{16,24},{24,16},{1,9},{9,1},{17,25},{25,17},{2,10},{10... | collective-permute-start | bytes 417800 | tf_op jit(solution)/shard_map/ppermute | solution.py:384
  8.3 10.1 %collective-permute-start.2 = (bf16[32,2176]{1,0:T(8,128)(2,1)S(1)}, bf16[32,2176]{1,0:T(8,128)(2,1)S(1)}, u32[]{:S(2)}, u32[]{:S(2)}) collective-permute-start(bf16[32,2176]{1,0:T(8,128)(2,1)S(1)} %pack.1.refs_0_), channel_id=1, source_target_pairs={{0,24},{8,16},{16,8},{24,0},{1,25},{9,17},{17,9},{25,1},{2,26},{10... | collective-permute-start | bytes 417800 | tf_op jit(solution)/shard_map/ppermute | solution.py:384
  10.8 12.7 %collective-permute-start.1 = (bf16[32,2176]{1,0:T(8,128)(2,1)S(1)}, bf16[32,2176]{1,0:T(8,128)(2,1)S(1)}, u32[]{:S(2)}, u32[]{:S(2)}) collective-permute-start(bf16[32,2176]{1,0:T(8,128)(2,1)S(1)} %pack.1.refs_0_), channel_id=1, source_target_pairs={{0,16},{8,24},{16,0},{24,8},{1,17},{9,25},{17,1},{25,9},{2,18},{10... | collective-permute-start | bytes 417800 | tf_op jit(solution)/shard_map/ppermute | solution.py:384
  12.3 11.2 %collective-permute-start.7 = (bf16[32,2304]{1,0:T(8,128)(2,1)S(1)}, bf16[32,2304]{1,0:T(8,128)(2,1)S(1)}, u32[]{:S(2)}, u32[]{:S(2)}) collective-permute-start(bf16[32,2304]{1,0:T(8,128)(2,1)S(1)} %pad_maximum_fusion.1), channel_id=1, source_target_pairs={{0,6},{1,7},{2,4},{3,5},{4,2},{5,3},{6,0},{7,1},{8,14},{9,15},{10,... | collective-permute-start | bytes 442376 | tf_op jit(solution)/shard_map/ppermute | solution.py:381
  15.0 8.6 %collective-permute-start.6 = (bf16[32,2304]{1,0:T(8,128)(2,1)S(1)}, bf16[32,2304]{1,0:T(8,128)(2,1)S(1)}, u32[]{:S(2)}, u32[]{:S(2)}) collective-permute-start(bf16[32,2304]{1,0:T(8,128)(2,1)S(1)} %pad_maximum_fusion.1), channel_id=1, source_target_pairs={{0,4},{1,5},{2,6},{3,7},{4,0},{5,1},{6,2},{7,3},{8,12},{9,13},{10,... | collective-permute-start | bytes 442376 | tf_op jit(solution)/shard_map/ppermute | solution.py:381
  15.5 8.1 %collective-permute-start.5 = (bf16[32,2304]{1,0:T(8,128)(2,1)S(1)}, bf16[32,2304]{1,0:T(8,128)(2,1)S(1)}, u32[]{:S(2)}, u32[]{:S(2)}) collective-permute-start(bf16[32,2304]{1,0:T(8,128)(2,1)S(1)} %pad_maximum_fusion.1), channel_id=1, source_target_pairs={{0,2},{1,3},{2,0},{3,1},{4,6},{5,7},{6,4},{7,5},{8,10},{9,11},{10,... | collective-permute-start | bytes 442376 | tf_op jit(solution)/shard_map/ppermute | solution.py:381
  23.6 11.6 %collective-permute-start.10 = (bf16[64,2176]{1,0:T(8,128)(2,1)S(1)}, bf16[64,2176]{1,0:T(8,128)(2,1)S(1)}, u32[]{:S(2)}, u32[]{:S(2)}) collective-permute-start(bf16[64,2176]{1,0:T(8,128)(2,1)S(1)} %pad_maximum_fusion), channel_id=1, source_target_pairs={{0,6},{1,7},{2,4},{3,5},{4,2},{5,3},{6,0},{7,1},{8,14},{9,15},{10,... | collective-permute-start | bytes 835592 | tf_op jit(solution)/shard_map/ppermute | solution.py:381
  26.1 12.3 %collective-permute-start.9 = (bf16[64,2176]{1,0:T(8,128)(2,1)S(1)}, bf16[64,2176]{1,0:T(8,128)(2,1)S(1)}, u32[]{:S(2)}, u32[]{:S(2)}) collective-permute-start(bf16[64,2176]{1,0:T(8,128)(2,1)S(1)} %pad_maximum_fusion), channel_id=1, source_target_pairs={{0,4},{1,5},{2,6},{3,7},{4,0},{5,1},{6,2},{7,3},{8,12},{9,13},{10,... | collective-permute-start | bytes 835592 | tf_op jit(solution)/shard_map/ppermute | solution.py:381
  26.6 11.9 %collective-permute-start.8 = (bf16[64,2176]{1,0:T(8,128)(2,1)S(1)}, bf16[64,2176]{1,0:T(8,128)(2,1)S(1)}, u32[]{:S(2)}, u32[]{:S(2)}) collective-permute-start(bf16[64,2176]{1,0:T(8,128)(2,1)S(1)} %pad_maximum_fusion), channel_id=1, source_target_pairs={{0,2},{1,3},{2,0},{3,1},{4,6},{5,7},{6,4},{7,5},{8,10},{9,11},{10,... | collective-permute-start | bytes 835592 | tf_op jit(solution)/shard_map/ppermute | solution.py:381
  27.1 1.9 %copy-start.1 = (bf16[1,2048,768]{2,1,0:T(8,128)(2,1)S(1)}, bf16[1,2048,768]{2,1,0:T(8,128)(2,1)}, u32[]{:S(2)}) copy-start(bf16[1,2048,768]{2,1,0:T(8,128)(2,1)} %refs_7_.1) | copy-start | bytes 9437188
  29.0 1.2 %copy-start.3 = (bf16[256,2048]{1,0:T(8,128)(2,1)S(1)}, bf16[256,2048]{1,0:T(8,128)(2,1)}, u32[]{:S(2)}) copy-start(bf16[256,2048]{1,0:T(8,128)(2,1)} %refs_1_.1) | copy-start | bytes 3145732
  39.5 5.2 %collective-permute-start.11 = (bf16[144,128]{1,0:T(8,128)(2,1)S(1)}, bf16[144,128]{1,0:T(8,128)(2,1)S(1)}, u32[]{:S(2)}, u32[]{:S(2)}) collective-permute-start(bf16[144,128]{1,0:T(8,128)(2,1)S(1)} %get-tuple-element.64), channel_id=1, source_target_pairs={{0,1},{1,0},{2,3},{3,2},{4,5},{5,4},{6,7},{7,6},{8,9},{9,8},{10,11... | collective-permute-start | bytes 110600 | tf_op jit(solution)/shard_map/ppermute | solution.py:381
  44.8 9.5 %collective-permute-start.12 = (bf16[64,2176]{1,0:T(8,128)(2,1)S(1)}, bf16[64,2176]{1,0:T(8,128)(2,1)S(1)}, u32[]{:S(2)}, u32[]{:S(2)}) collective-permute-start(bf16[64,2176]{1,0:T(8,128)(2,1)S(1)} %get-tuple-element.67), channel_id=1, source_target_pairs={{0,2},{1,3},{2,0},{3,1},{4,6},{5,7},{6,4},{7,5},{8,10},{9,11},{10,... | collective-permute-start | bytes 835592 | tf_op jit(solution)/shard_map/ppermute | solution.py:381
  46.3 14.7 %collective-permute-start.13 = (bf16[64,2176]{1,0:T(8,128)(2,1)S(1)}, bf16[64,2176]{1,0:T(8,128)(2,1)S(1)}, u32[]{:S(2)}, u32[]{:S(2)}) collective-permute-start(bf16[64,2176]{1,0:T(8,128)(2,1)S(1)} %get-tuple-element.68), channel_id=1, source_target_pairs={{0,4},{1,5},{2,6},{3,7},{4,0},{5,1},{6,2},{7,3},{8,12},{9,13},{10,... | collective-permute-start | bytes 835592 | tf_op jit(solution)/shard_map/ppermute | solution.py:381
  47.1 14.0 %collective-permute-start.14 = (bf16[64,2176]{1,0:T(8,128)(2,1)S(1)}, bf16[64,2176]{1,0:T(8,128)(2,1)S(1)}, u32[]{:S(2)}, u32[]{:S(2)}) collective-permute-start(bf16[64,2176]{1,0:T(8,128)(2,1)S(1)} %get-tuple-element.69), channel_id=1, source_target_pairs={{0,6},{1,7},{2,4},{3,5},{4,2},{5,3},{6,0},{7,1},{8,14},{9,15},{10,... | collective-permute-start | bytes 835592 | tf_op jit(solution)/shard_map/ppermute | solution.py:381
  61.9 16.6 %collective-permute-start.15 = (bf16[64,2048]{1,0:T(8,128)(2,1)S(1)}, bf16[64,2048]{1,0:T(8,128)(2,1)S(1)}, u32[]{:S(2)}, u32[]{:S(2)}) collective-permute-start(bf16[64,2048]{1,0:T(8,128)(2,1)S(1)} %get-tuple-element.75), channel_id=1, source_target_pairs={{0,2},{1,3},{2,0},{3,1},{4,6},{5,7},{6,4},{7,5},{8,10},{9,11},{10,... | collective-permute-start | bytes 786440 | tf_op jit(solution)/shard_map/ppermute | solution.py:381
  62.5 16.0 %collective-permute-start.16 = (bf16[64,2048]{1,0:T(8,128)(2,1)S(1)}, bf16[64,2048]{1,0:T(8,128)(2,1)S(1)}, u32[]{:S(2)}, u32[]{:S(2)}) collective-permute-start(bf16[64,2048]{1,0:T(8,128)(2,1)S(1)} %get-tuple-element.76), channel_id=1, source_target_pairs={{0,4},{1,5},{2,6},{3,7},{4,0},{5,1},{6,2},{7,3},{8,12},{9,13},{10,... | collective-permute-start | bytes 786440 | tf_op jit(solution)/shard_map/ppermute | solution.py:381
  63.9 14.6 %collective-permute-start.17 = (bf16[64,2048]{1,0:T(8,128)(2,1)S(1)}, bf16[64,2048]{1,0:T(8,128)(2,1)S(1)}, u32[]{:S(2)}, u32[]{:S(2)}) collective-permute-start(bf16[64,2048]{1,0:T(8,128)(2,1)S(1)} %get-tuple-element.77), channel_id=1, source_target_pairs={{0,6},{1,7},{2,4},{3,5},{4,2},{5,3},{6,0},{7,1},{8,14},{9,15},{10,... | collective-permute-start | bytes 786440 | tf_op jit(solution)/shard_map/ppermute | solution.py:381
  65.5 7.5 %collective-permute-start.19 = (bf16[32,2176]{1,0:T(8,128)(2,1)S(1)}, bf16[32,2176]{1,0:T(8,128)(2,1)S(1)}, u32[]{:S(2)}, u32[]{:S(2)}) collective-permute-start(bf16[32,2176]{1,0:T(8,128)(2,1)S(1)} %get-tuple-element.78), channel_id=1, source_target_pairs={{0,24},{8,16},{16,8},{24,0},{1,25},{9,17},{17,9},{25,1},{2,26},{10... | collective-permute-start | bytes 417800 | tf_op jit(solution)/shard_map/ppermute | solution.py:384
  67.9 10.6 %collective-permute-start.18 = (bf16[32,2176]{1,0:T(8,128)(2,1)S(1)}, bf16[32,2176]{1,0:T(8,128)(2,1)S(1)}, u32[]{:S(2)}, u32[]{:S(2)}) collective-permute-start(bf16[32,2176]{1,0:T(8,128)(2,1)S(1)} %get-tuple-element.74), channel_id=1, source_target_pairs={{0,16},{8,24},{16,0},{24,8},{1,17},{9,25},{17,1},{25,9},{2,18},{10... | collective-permute-start | bytes 417800 | tf_op jit(solution)/shard_map/ppermute | solution.py:384
  79.4 5.1 %collective-permute-start.20 = (bf16[32,2176]{1,0:T(8,128)(2,1)S(1)}, bf16[32,2176]{1,0:T(8,128)(2,1)S(1)}, u32[]{:S(2)}, u32[]{:S(2)}) collective-permute-start(bf16[32,2176]{1,0:T(8,128)(2,1)S(1)} %get-tuple-element.86), channel_id=1, source_target_pairs={{0,8},{8,0},{16,24},{24,16},{1,9},{9,1},{17,25},{25,17},{2,10},{10... | collective-permute-start | bytes 417800 | tf_op jit(solution)/shard_map/ppermute | solution.py:384
  84.6 6.1 %collective-permute-start.23 = (bf16[32,2176]{1,0:T(8,128)(2,1)S(1)}, bf16[32,2176]{1,0:T(8,128)(2,1)S(1)}, u32[]{:S(2)}, u32[]{:S(2)}) collective-permute-start(bf16[32,2176]{1,0:T(8,128)(2,1)S(1)} %finish.1.refs_0_), channel_id=1, source_target_pairs={{0,6},{1,7},{2,4},{3,5},{4,2},{5,3},{6,0},{7,1},{8,14},{9,15},{10,... | collective-permute-start | bytes 417800 | tf_op jit(solution)/shard_map/ppermute | solution.py:381
  86.1 6.1 %collective-permute-start.22 = (bf16[32,2176]{1,0:T(8,128)(2,1)S(1)}, bf16[32,2176]{1,0:T(8,128)(2,1)S(1)}, u32[]{:S(2)}, u32[]{:S(2)}) collective-permute-start(bf16[32,2176]{1,0:T(8,128)(2,1)S(1)} %finish.1.refs_0_), channel_id=1, source_target_pairs={{0,4},{1,5},{2,6},{3,7},{4,0},{5,1},{6,2},{7,3},{8,12},{9,13},{10,... | collective-permute-start | bytes 417800 | tf_op jit(solution)/shard_map/ppermute | solution.py:381
  86.7 5.5 %collective-permute-start.21 = (bf16[32,2176]{1,0:T(8,128)(2,1)S(1)}, bf16[32,2176]{1,0:T(8,128)(2,1)S(1)}, u32[]{:S(2)}, u32[]{:S(2)}) collective-permute-start(bf16[32,2176]{1,0:T(8,128)(2,1)S(1)} %finish.1.refs_0_), channel_id=1, source_target_pairs={{0,2},{1,3},{2,0},{3,1},{4,6},{5,7},{6,4},{7,5},{8,10},{9,11},{10,... | collective-permute-start | bytes 417800 | tf_op jit(solution)/shard_map/ppermute | solution.py:381
  88.1 4.5 %collective-permute-start.24 = (bf16[32,2176]{1,0:T(8,128)(2,1)S(1)}, bf16[32,2176]{1,0:T(8,128)(2,1)S(1)}, u32[]{:S(2)}, u32[]{:S(2)}) collective-permute-start(bf16[32,2176]{1,0:T(8,128)(2,1)S(1)} %finish.1.refs_0_), channel_id=1, source_target_pairs={{0,1},{1,0},{2,3},{3,2},{4,5},{5,4},{6,7},{7,6},{8,9},{9,8},{10,11... | collective-permute-start | bytes 417800 | tf_op jit(solution)/shard_map/ppermute | solution.py:381
  90.7 1.9 %collective-permute-start.27 = (bf16[32,2176]{1,0:T(8,128)(2,1)S(1)}, bf16[32,2176]{1,0:T(8,128)(2,1)S(1)}, u32[]{:S(2)}, u32[]{:S(2)}) collective-permute-start(bf16[32,2176]{1,0:T(8,128)(2,1)S(1)} %collective-permute-done.23.refs_3_), channel_id=1, source_target_pairs={{0,1},{1,0},{2,3},{3,2},{4,5},{5,4},{6,7},{7,6},{8,9},{9,8},{10,11... | collective-permute-start | bytes 417800 | tf_op jit(solution)/shard_map/ppermute | solution.py:381
  92.1 1.4 %collective-permute-start.26 = (bf16[32,2176]{1,0:T(8,128)(2,1)S(1)}, bf16[32,2176]{1,0:T(8,128)(2,1)S(1)}, u32[]{:S(2)}, u32[]{:S(2)}) collective-permute-start(bf16[32,2176]{1,0:T(8,128)(2,1)S(1)} %collective-permute-done.22.refs_2_), channel_id=1, source_target_pairs={{0,1},{1,0},{2,3},{3,2},{4,5},{5,4},{6,7},{7,6},{8,9},{9,8},{10,11... | collective-permute-start | bytes 417800 | tf_op jit(solution)/shard_map/ppermute | solution.py:381
  92.1 1.6 %collective-permute-start.25 = (bf16[32,2176]{1,0:T(8,128)(2,1)S(1)}, bf16[32,2176]{1,0:T(8,128)(2,1)S(1)}, u32[]{:S(2)}, u32[]{:S(2)}) collective-permute-start(bf16[32,2176]{1,0:T(8,128)(2,1)S(1)} %collective-permute-done.21.refs_1_), channel_id=1, source_target_pairs={{0,1},{1,0},{2,3},{3,2},{4,5},{5,4},{6,7},{7,6},{8,9},{9,8},{10,11... | collective-permute-start | bytes 417800 | tf_op jit(solution)/shard_map/ppermute | solution.py:381
  (2 other events, 1.4 us)

commit v6 on v5

--- a/solution.py
+++ b/solution.py
@@ -45,13 +45,14 @@
     return jnp.sum(jnp.where(index == wanted, table, 0.0), axis=1, keepdims=True)
 
 
-def pack_kernel(seq_dev, place, ids, gates, tokens, out, tile, rows, sems):
+def pack_kernel(seq_dev, positives, ids, gates, tokens, out, tile, rows, sems):
     part_rows, width = out.shape[0], tokens.shape[1]
     tok_dev = tokens.shape[0]
     seq_length = tok_dev // seq_dev
     share = rows.shape[2]
-    column_at = pl.multiple_of(place[1] // 2 * share, lanes)
-    start = pl.multiple_of(place[1] * part_rows, part_rows)
+    lane = lax.axis_index("expert")
+    column_at = pl.multiple_of(lane // 2 * share, lanes)
+    start = pl.multiple_of(lane * part_rows, part_rows)
     copies = [
         pltpu.make_async_copy(
             tokens.at[pl.ds((seq + 1) * seq_length - tail, tail), pl.ds(column_at, share)],
@@ -74,7 +75,7 @@
         tile[note_rows + index : note_rows + index + 1, :] = gates[:, block]
     for seq in range(seq_dev):
         row = 2 * note_rows + seq
-        tile[row : row + 1, :] = jnp.full((1, lanes), place[3 + seq], jnp.int32).astype(f32)
+        tile[row : row + 1, :] = jnp.full((1, lanes), positives[seq], jnp.int32).astype(f32)
     base = part_rows - seq_dev * (share // lanes)
     for seq in range(seq_dev):
         copies[seq].wait()
@@ -177,33 +178,28 @@
 
 
 def expert_kernel(layout, *refs):
-    chips, part_rows, near, with_last, n_parts = layout
+    group, chips, part_rows, with_last, sources, n_parts = layout
     refs = list(refs)
     place = refs.pop(0)
+    near = 0 in group
     tokens = refs.pop(0) if near else None
     last_rows = refs.pop(0) if with_last else None
     parts, refs = refs[:n_parts], refs[n_parts:]
     weights, refs = refs[:4], refs[4:]
-    outs, refs = refs[:chips], refs[chips:]
+    n_outs = chips * len(group)
+    outs, refs = refs[:n_outs], refs[n_outs:]
     if with_last:
         last_projected, own_last, by_lane, tile, *refs = refs
     (rows,) = refs
-    count = outs[0].shape[0] // part_rows
     width = weights[0].shape[1]
-    block = count * part_rows
-    total = chips * block
+    total = n_outs * part_rows
+    spots = [slice(index * part_rows, (index + 1) * part_rows) for index in range(n_outs)]
     if near:
         for chip in range(chips):
             start = pl.multiple_of((place[1] ^ (2 * chip)) * part_rows, part_rows)
-            at = chip * block
-            rows[at : at + part_rows, :] = tokens[pl.ds(start, part_rows), :]
-    own_parts = count - 1 if near else count
-    for index in range(own_parts):
-        at = (index + count - own_parts) * part_rows
-        rows[at : at + part_rows, :] = parts[index][:, :width]
-    for chip in range(1, chips):
-        at = chip * block + (count - own_parts) * part_rows
-        rows[at : at + own_parts * part_rows, :] = parts[own_parts + chip - 1][:, :width]
+            rows[spots[chip], :] = tokens[pl.ds(start, part_rows), :]
+    for (index, row), spot in zip(sources, spots[n_outs - len(sources) :]):
+        rows[spot, :] = parts[index][row : row + part_rows, :width]
     if with_last:
         rows[total:, :] = last_rows[...]
     result = None
@@ -215,8 +211,8 @@
         _, up, _, activated = hidden_parts(projected)
         part = dot((activated * up).astype(bf16), w_out[0])
         result = part if half == 0 else result + part
-    for chip in range(chips):
-        outs[chip][:, :width] = result[chip * block : (chip + 1) * block].astype(bf16)
+    for out, spot in zip(outs, spots):
+        out[:, :width] = result[spot].astype(bf16)
     if with_last:
         each = last_rows.shape[0] // by_lane.shape[0]
         floats = last_rows[...].astype(f32)
@@ -229,21 +225,20 @@
             by_lane[lane, 0:each, :] = result[first : first + each]
         for chip in range(chips):
             spread_rows(by_lane[place[1] ^ (2 * chip), 0:each, :], part_rows, tile)
-            outs[chip][:part_rows, width:] = tile[...].astype(bf16)
-            outs[chip][part_rows:, width:] = jnp.zeros((block - part_rows, tile.shape[1]), bf16)
+            outs[n_outs - chips + chip][:, width:] = tile[...].astype(bf16)
 
 
 def combine_kernel(layout, place, kept, found, *refs):
-    chips, part_rows, group, with_last, width, each = layout
-    own, refs = (refs[0], refs[1:]) if group[0] == 0 else (None, refs)
-    last_in, refs = (None, refs) if with_last else (refs[0], refs[1:])
-    parts, outs = refs[:chips], refs[chips : chips + len(group)]
+    hop, chips, with_last, width, each = layout
+    own, refs = (refs[0], refs[1:]) if hop == 0 else (None, refs)
+    last_in, refs = (refs[0], refs[1:]) if hop and not with_last else (None, refs)
+    parts, out = refs[:chips], refs[chips]
+    part_rows = out.shape[0]
     first_expert = place[2] - place[1] // 2
     experts = [first_expert + ((place[1] // 2) ^ chip) for chip in range(chips)]
     if with_last:
-        last_out = refs[-1]
-        last = kept.shape[0] - 2 * chips * each
-        table = kept[last:, :].astype(f32) + found[last:, :].astype(f32)
+        last_in = refs[-1]
+        table = kept[-2 * chips * each :, :].astype(f32) + found[-2 * chips * each :, :].astype(f32)
         row_index = lax.broadcasted_iota(jnp.int32, table.shape, 0)
         chunks = width // lanes
         for row in range(each):
@@ -257,20 +252,16 @@
                 values = parts[chip][spot, width + at : width + at + lanes].astype(f32)
                 term = column(mine, experts[chip]) * values
                 total = term if total is None else total + term
-            last_out[spot, at : at + lanes] = total.astype(bf16)
-        last_in = last_out
-    for index, hop in enumerate(group):
-        at = slice(hop * part_rows, (hop + 1) * part_rows)
-        table = kept[at, :].astype(f32) + found[at, :].astype(f32)
-        rows = slice(index * part_rows, (index + 1) * part_rows)
-        total = own[:, :width].astype(f32) if hop == 0 else None
-        for chip in range(chips):
-            weight = column(table, experts[chip])
-            term = weight * parts[chip][rows, :width].astype(f32)
-            total = term if total is None else total + term
-        outs[index][:, :width] = total.astype(outs[index].dtype)
-        if hop:
-            outs[index][:, width:] = last_in[...]
+            last_in[spot, at : at + lanes] = total.astype(bf16)
+    at = slice(hop * part_rows, (hop + 1) * part_rows)
+    table = kept[at, :].astype(f32) + found[at, :].astype(f32)
+    total = None if hop else own[:, :width].astype(f32)
+    for chip in range(chips):
+        term = column(table, experts[chip]) * parts[chip][:, :width].astype(f32)
+        total = term if total is None else total + term
+    out[:, :width] = total.astype(out.dtype)
+    if hop:
+        out[:, width:] = last_in[...]
 
 
 def finish_kernel(near, own_last, last_sum, *refs):
@@ -374,7 +365,6 @@
     plane = lax.axis_index("dp")
     lane = lax.axis_index("expert")
     place = jnp.stack([plane, lane, plane * chips + lane // 2]).astype(jnp.int32)
-    place = jnp.concatenate([place, positives])
     assert experts <= lanes and seq_length % tail == 0
 
     def to_lane(value, step):
@@ -397,18 +387,17 @@
             pltpu.VMEM((seq_dev, tail, share), bf16),
             pltpu.SemaphoreType.DMA((seq_dev + 1,)),
         ],
-        compiler_params=params(4),
         cost_estimate=cost(0, 1 << 19),
         name="pack",
-    )(place, expert_ids.T, gates.T, tokens)
+    )(positives, expert_ids.T, gates.T, tokens)
     arrivals = {hop: to_plane(packed, hop) for hop in range(1, dp_count)}
     mate_in = to_lane(gate_up, 1)
     mate_out = to_lane(down, 1)
     weights = (gate_up, down, mate_in, mate_out)
 
-    far_parts = []
-    tiles = []
-    where_tiles = [[None] * chips for _ in range(dp_count)]
+    tiles = [packed]
+    spots = {}
+    received = None
     for group in groups:
         own = [arrivals[hop] for hop in group if hop]
         if group[0] == 0:
@@ -418,23 +407,20 @@
             joined = jnp.concatenate(own, axis=0)
             joined, received = lax.optimization_barrier((joined, received))
             tiles[-len(received) :] = received
-            far_parts[-1][-len(received) :] = received
+        first = len(tiles)
         received = [to_lane(joined, step) for step in chip_steps]
-        far_parts.append(own + received)
+        tiles += own + received
         for index, hop in enumerate(group):
-            tiles.append(packed if hop == 0 else arrivals[hop])
-            where_tiles[hop][0] = (len(tiles) - 1, 0, width)
-            for chip in range(1, chips):
-                if group[0] == 0:
-                    spot = (0, width if hop else width + lanes)
-                else:
-                    spot = (index * part_rows, width)
-                where_tiles[hop][chip] = (chip,) + spot
-        first = len(tiles)
-        tiles += received
-        for hop in group:
-            for chip in range(1, chips):
-                where_tiles[hop][chip] = (first + chip - 1,) + where_tiles[hop][chip][1:]
+            if group[0] == 0:
+                place_of = (first, 0, width) if hop else (0, 0, width)
+                row, at = 0, width if hop else width + lanes
+            else:
+                place_of = (first + index, 0, width)
+                row, at = index * part_rows, width
+            spots[hop] = [place_of] + [
+                (first + len(own) + chip, row, at) for chip in range(chips - 1)
+            ]
+    where_tiles = [spots[hop] for hop in range(dp_count)]
 
     table_rows = dp_count * part_rows + seqs
     chunks = width // lanes
@@ -464,14 +450,19 @@
     extra = each * width // part_rows
     assert extra % lanes == 0 and part_rows % (width // lanes) == 0
 
-    def expert(group, parts, place, with_last):
-        near = group[0] == 0
-        block = len(group) * part_rows
-        total = chips * block + (seqs if with_last else 0)
-        out_width = width + (extra if with_last else 0)
-        out_shape = [jax.ShapeDtypeStruct((block, out_width), bf16)] * chips
+    def expert(group, place, with_last):
+        near = 0 in group
+        wanted = [spot for hop in group if hop for spot in where_tiles[hop]]
+        used = sorted({spot[0] for spot in wanted})
+        sources = tuple((used.index(spot[0]), spot[1]) for spot in wanted)
+        parts = [tiles[index] for index in used]
+        n_outs = chips * len(group)
+        total = n_outs * part_rows + (seqs if with_last else 0)
+        out_shape = [jax.ShapeDtypeStruct((part_rows, width), bf16)] * n_outs
         scratch = [pltpu.VMEM((total, width), bf16)]
         if with_last:
+            wider = jax.ShapeDtypeStruct((part_rows, width + extra), bf16)
+            out_shape[n_outs - chips :] = [wider] * chips
             out_shape += [
                 jax.ShapeDtypeStruct((seqs, 2 * half_width), f32),
                 jax.ShapeDtypeStruct((part_rows, extra), f32),
@@ -482,7 +473,10 @@
             ] + scratch
         operands = [place] + [tokens] * near + [last_all] * with_last + parts + list(weights)
         return pl.pallas_call(
-            functools.partial(expert_kernel, (chips, part_rows, near, with_last, len(parts))),
+            functools.partial(
+                expert_kernel,
+                (tuple(group), chips, part_rows, with_last, sources, len(parts)),
+            ),
             out_shape=out_shape,
             in_specs=[in_smem] + [in_vmem] * (len(operands) - 1),
             out_specs=[in_vmem] * len(out_shape),
@@ -492,56 +486,47 @@
             name="experts",
         )(*operands)
 
-    def combine(group, parts, last_sum):
+    def combine(hop, parts, last_sum):
         with_last = last_sum is None
-        out_shape = [
-            jax.ShapeDtypeStruct((part_rows, width + extra), bf16)
-            if hop
-            else jax.ShapeDtypeStruct((part_rows, width), f32)
-            for hop in group
-        ]
+        out_shape = [jax.ShapeDtypeStruct((part_rows, width), f32)]
+        if hop:
+            out_shape = [jax.ShapeDtypeStruct((part_rows, width + extra), bf16)]
         if with_last:
             out_shape.append(jax.ShapeDtypeStruct((part_rows, extra), bf16))
-        layout = (chips, part_rows, tuple(group), with_last, width, each)
-        operands = [place, kept, found]
-        operands += [packed] * (group[0] == 0) + [last_sum] * (not with_last) + parts
+        operands = [place, kept, found] + [packed] * (hop == 0)
+        operands += [last_sum] * (hop > 0 and not with_last) + parts
         return pl.pallas_call(
-            functools.partial(combine_kernel, layout),
+            functools.partial(combine_kernel, (hop, chips, with_last, width, each)),
             out_shape=out_shape,
             in_specs=[in_smem] + [in_vmem] * (len(operands) - 1),
             out_specs=[in_vmem] * len(out_shape),
             compiler_params=params(8),
-            cost_estimate=cost(0, 3 << 20),
+            cost_estimate=cost(0, 2 << 20),
             name="combine",
         )(*operands)
 
-    outs = []
+    outs = {}
     after = place
-    for group, parts in zip(groups, far_parts):
-        outs.append(expert(group, parts, after, group is groups[-1]))
-        after, _ = lax.optimization_barrier((place, outs[-1][0]))
-    last_projected, own_last = outs[-1][chips:]
-
-    sums = {}
+    for group in groups:
+        out = expert(group, after, group is groups[-1])
+        after, _ = lax.optimization_barrier((place, out[0]))
+        for index, hop in enumerate(group):
+            outs[hop] = out[index * chips : (index + 1) * chips]
+    last_projected, own_last = out[-2:]
+
+    returned = {}
+    for hop in range(dp_count - 1, -1, -1):
+        first, *sent_back = outs[hop]
+        if hop == dp_count - 1:
+            sent_back, found = lax.optimization_barrier((sent_back, found))
+        returned[hop] = [first] + [to_lane(value, step) for value, step in zip(sent_back, chip_steps)]
+    homeward = []
     last_sum = None
-    returned = None
-    for index in [len(groups) - 1] + list(range(len(groups) - 2, -1, -1)):
-        group, sent_back = groups[index], list(outs[index][1:chips])
-        if returned is None:
-            sent_back, found = lax.optimization_barrier((sent_back, found))
-        else:
-            result = combine(before, [first] + returned, last_sum)
-            sums.update(zip(before, result))
-            last_sum = result[-1] if last_sum is None else last_sum
-            sent_back, _ = lax.optimization_barrier((sent_back, result[0]))
-        returned = [to_lane(value, step) for value, step in zip(sent_back, chip_steps)]
-        before, first = group, outs[index][0]
-    homeward = {hop: to_plane(value, hop) for hop, value in sums.items()}
-    returned, homeward = lax.optimization_barrier((returned, homeward))
-    result = combine(before, [first] + returned, last_sum)
-    last_sum = result[-1] if last_sum is None else last_sum
-    sums.update(zip(before, result))
-    homeward.update({hop: to_plane(sums[hop], hop) for hop in before if hop})
+    for hop in range(dp_count - 1, 0, -1):
+        result = combine(hop, returned[hop], last_sum)
+        last_sum = result[1] if last_sum is None else last_sum
+        homeward.append(to_plane(result[0], hop))
+    near_sum = combine(0, returned[0], last_sum)[0]
 
     own_out = pl.pallas_call(
         finish_kernel,
@@ -551,7 +536,7 @@
         compiler_params=params(16 if dp_count > 8 else 4),
         cost_estimate=cost(0, 1 << 20),
         name="finish",
-    )(sums[0], own_last, last_sum, *homeward.values())
+    )(near_sum, own_last, last_sum, *homeward)
     pieces = [own_out] + [to_lane(own_out, step) for step in chip_steps]
     pieces += [to_lane(piece, 1) for piece in pieces]
     layer_out, layer_last = pl.pallas_call(

time: 102 us -> 98.3 us (0.964)
  waiting for transfers between devices: 45.7 us -> 31.3 us
  starting transfers between devices: 27.1 us -> 36.4 us
  Pallas kernels: 21.5 us -> 24.7 us
  local copies, waits for them, and re-layouts: 5.7 us -> 3.85 us
    ppermute x6, waiting for transfers between devices: 24.7 us -> 8.62 us  [to_plane(): return lax.ppermute(value, 'dp', [(p, p ^ step) for p in range(dp_count)])]
    ppermute x22 -> x28, starting transfers between devices: 19 us -> 26.2 us  [to_lane(): lax.ppermute(value, 'expert', [(j, j ^ step) for j in range(expert_count)])]
    unnamed x12 -> x8, local copies, waits for them, and re-layouts: 5.7 us -> 3.12 us
    ppermute x6, starting transfers between devices: 8.17 us -> 10.2 us  [to_plane(): return lax.ppermute(value, 'dp', [(p, p ^ step) for p in range(dp_count)])]
    pallas_call x1, Pallas kernels: 0.71 us -> 2.32 us  [body(): pl.pallas_call(functools.partial(pack_kernel, seq_dev), out_shape=jax.Sha...]
    ppermute x22 -> x28, waiting for transfers between devices: 21.1 us -> 22.6 us  [to_lane(): lax.ppermute(value, 'expert', [(j, j ^ step) for j in range(expert_count)])]
    pallas_call x4 -> x6, Pallas kernels: 11.7 us -> 12.9 us  [the longest x2 10 us: expert(): pl.pallas_call(functools.partial(expert_kernel, (tuple(group), chips, par...]
  transfers between devices with their start and end apart: 28 -> 34, of which waited for: 14 -> 12; matrix products, arithmetic and copies ran while one was open for 1% -> 2% of each run, Pallas kernels for 11% -> 16%
where the time goes in v6:
time: 98.3 us; the launch traced here: 98 us
  starting transfers between devices  36.4 us (37%)
  waiting for transfers between devices  31.3 us (32%)
  Pallas kernels  24.7 us (25%)
  local copies, waits for them, and re-layouts  3.85 us (4%)
  other arithmetic  1.01 us (1%)
    ppermute x28, starting transfers between devices, to_lane(): lax.ppermute(value, 'expert', [(j, j ^ step) for j in range(expert_count)])  26.2 us
    ppermute x28, waiting for transfers between devices, to_lane(): lax.ppermute(value, 'expert', [(j, j ^ step) for j in range(expert_count)])  22.6 us
    ppermute x6, starting transfers between devices, to_plane(): return lax.ppermute(value, 'dp', [(p, p ^ step) for p in range(dp_count)])  10.2 us
    pallas_call x2, Pallas kernels, expert(): pl.pallas_call(functools.partial(expert_kernel, (tuple(group), chips, par...  10 us
    ppermute x6, waiting for transfers between devices, to_plane(): return lax.ppermute(value, 'dp', [(p, p ^ step) for p in range(dp_count)])  8.62 us
    pallas_call x1, Pallas kernels, body(): pl.pallas_call(gradient_kernel, grid=(steps,), out_shape=[jax.ShapeDtypeS...  6.26 us
    unnamed x8, local copies, waits for them, and re-layouts  3.12 us
    pallas_call x4, Pallas kernels, combine(): pl.pallas_call(functools.partial(combine_kernel, (hop, chips, with_last,...  2.9 us
  transfers between devices with their start and end apart: 34, of which 12 were waited for; matrix products, arithmetic and copies ran while one was open for 2% of the time, Pallas kernels for 16%

profile of v6, /device:TPU:0, one launch (start us, length us, event | category | flops | bytes accessed | tf_op | source)
XLA Modules:
  0.0 98.0 jit_solution(14844018635364143598)
XLA Ops:
  1.2 2.3 %pack.1.refs_0_ = bf16[32,2176]{1,0:T(8,128)(2,1)} custom-call(s32[4]{0:T(128)} %positives.1, s32[1,256]{1,0:T(1,128)} %bitcast.5, f32[1,256]{1,0:T(1,128)} %bitcast.6, bf16[256,2048]{1,0:T(8,128)(2,1)} %refs_1_.1), custom_call_target="tpu_custom_call" | custom-call | bytes 524288 | tf_op jit(solution)/shard_map/pack/pallas_call | solution.py:380
  3.6 3.1 %collective-permute-start = (bf16[32,2176]{1,0:T(8,128)(2,1)}, bf16[32,2176]{1,0:T(8,128)(2,1)S(1)}, u32[]{:S(2)}, u32[]{:S(2)}) collective-permute-start(bf16[32,2176]{1,0:T(8,128)(2,1)} %pack.1.refs_0_), channel_id=1, source_target_pairs={{0,8},{8,0},{16,24},{24,16},{1,9},{9,1},{17,25},{25,17},{2,10},{10... | collective-permute-start | bytes 417800 | tf_op jit(solution)/shard_map/ppermute | solution.py:374
  6.6 2.5 %collective-permute-start.2 = (bf16[32,2176]{1,0:T(8,128)(2,1)}, bf16[32,2176]{1,0:T(8,128)(2,1)S(1)}, u32[]{:S(2)}, u32[]{:S(2)}) collective-permute-start(bf16[32,2176]{1,0:T(8,128)(2,1)} %pack.1.refs_0_), channel_id=1, source_target_pairs={{0,24},{8,16},{16,8},{24,0},{1,25},{9,17},{17,9},{25,1},{2,26},{10... | collective-permute-start | bytes 417800 | tf_op jit(solution)/shard_map/ppermute | solution.py:374
  10.9 2.6 %collective-permute-start.7 = (bf16[32,2304]{1,0:T(8,128)(2,1)S(1)}, bf16[32,2304]{1,0:T(8,128)(2,1)S(1)}, u32[]{:S(2)}, u32[]{:S(2)}) collective-permute-start(bf16[32,2304]{1,0:T(8,128)(2,1)S(1)} %pad_maximum_fusion.1), channel_id=1, source_target_pairs={{0,6},{1,7},{2,4},{3,5},{4,2},{5,3},{6,0},{7,1},{8,14},{9,15},{10,... | collective-permute-start | bytes 442376 | tf_op jit(solution)/shard_map/ppermute | solution.py:371
  14.5 2.4 %collective-permute-done.2.refs_6_.refs_3_ = bf16[32,2176]{1,0:T(8,128)(2,1)S(1)} collective-permute-done((bf16[32,2176]{1,0:T(8,128)(2,1)}, bf16[32,2176]{1,0:T(8,128)(2,1)S(1)}, u32[]{:S(2)}, u32[]{:S(2)}) %collective-permute-start.2) | collective-permute-done | bytes 139296 | tf_op jit(solution)/shard_map/ppermute | solution.py:374
  16.9 5.3 %collective-permute-done.1.refs_5_.refs_2_ = bf16[32,2176]{1,0:T(8,128)(2,1)} collective-permute-done((bf16[32,2176]{1,0:T(8,128)(2,1)}, bf16[32,2176]{1,0:T(8,128)(2,1)}, u32[]{:S(2)}, u32[]{:S(2)}) %collective-permute-start.1) | collective-permute-done | bytes 139296 | tf_op jit(solution)/shard_map/ppermute | solution.py:374
  23.1 2.5 %collective-permute-start.10 = (bf16[64,2176]{1,0:T(8,128)(2,1)S(1)}, bf16[64,2176]{1,0:T(8,128)(2,1)S(1)}, u32[]{:S(2)}, u32[]{:S(2)}) collective-permute-start(bf16[64,2176]{1,0:T(8,128)(2,1)S(1)} %pad_maximum_fusion), channel_id=1, source_target_pairs={{0,6},{1,7},{2,4},{3,5},{4,2},{5,3},{6,0},{7,1},{8,14},{9,15},{10,... | collective-permute-start | bytes 835592 | tf_op jit(solution)/shard_map/ppermute | solution.py:371
  26.8 1.9 %copy-done.1 = bf16[1,2048,768]{2,1,0:T(8,128)(2,1)S(1)} copy-done((bf16[1,2048,768]{2,1,0:T(8,128)(2,1)S(1)}, bf16[1,2048,768]{2,1,0:T(8,128)(2,1)}, u32[]{:S(2)}) %copy-start.1) | copy-done | bytes 3145752
  29.9 4.9 %experts.2 = (bf16[32,2048]{1,0:T(8,128)(2,1)S(1)}, bf16[32,2048]{1,0:T(8,128)(2,1)S(1)}, bf16[32,2048]{1,0:T(8,128)(2,1)S(1)}, bf16[32,2048]{1,0:T(8,128)(2,1)S...) custom-call(s32[3]{0:T(128)S(1)} %pad_add_fusion.place.refs_0_, ...), custom_call_target="tpu_custom_call" | custom-call | flops 2415919104 | bytes 12582912 | tf_op jit(solution)/shard_map/experts/pallas_call | solution.py:475
  34.8 3.1 %collective-permute-done.9.refs_8_.refs_5_ = bf16[64,2176]{1,0:T(8,128)(2,1)S(1)} collective-permute-done((bf16[64,2176]{1,0:T(8,128)(2,1)S(1)}, bf16[64,2176]{1,0:T(8,128)(2,1)S(1)}, u32[]{:S(2)}, u32[]{:S(2)}) %collective-permute-start.9) | collective-permute-done | bytes 278560 | tf_op jit(solution)/shard_map/ppermute | solution.py:371
  38.0 1.4 %tables.1 = (bf16[144,128]{1,0:T(8,128)(2,1)S(1)}, bf16[144,128]{1,0:T(8,128)(2,1)S(1)}, bf16[16,2048]{1,0:T(8,128)(2,1)S(1)}, f32[16,128]{1,0:T(8,128)S(1)}) custom-call(s32[3]{0:T(128)S(1)} %pad_add_fusion.place.refs_0_, bf16[32,2176]{1,0:T(8,128)(2,1)S(1)} %copy-done.3, bf16[32,2176]{1,0:T(8,128)(2,1)S(1)} %collective-permute-done.refs_1_.refs_2_, ...), custom_call_target="tpu_custom_call" | custom-call | bytes 1048576 | tf_op jit(solution)/shard_map/tables/pallas_call | solution.py:428
  39.5 5.1 %experts.3 = (bf16[32,2048]{1,0:T(8,128)(2,1)S(1)}, bf16[32,2048]{1,0:T(8,128)(2,1)S(1)}, bf16[32,2048]{1,0:T(8,128)(2,1)S(1)}, bf16[32,2048]{1,0:T(8,128)(2,1)S...) custom-call(s32[3]{0:T(128)S(1)} %pad_add_fusion.place.refs_0_, ...), custom_call_target="tpu_custom_call" | custom-call | flops 2566914048 | bytes 12582912 | tf_op jit(solution)/shard_map/experts/pallas_call | solution.py:475
  44.6 1.6 %collective-permute-start.15 = (bf16[32,2176]{1,0:T(8,128)(2,1)S(1)}, bf16[32,2176]{1,0:T(8,128)(2,1)S(1)}, u32[]{:S(2)}, u32[]{:S(2)}) collective-permute-start(bf16[32,2176]{1,0:T(8,128)(2,1)S(1)} %get-tuple-element.68), channel_id=1, source_target_pairs={{0,2},{1,3},{2,0},{3,1},{4,6},{5,7},{6,4},{7,5},{8,10},{9,11},{10,... | collective-permute-start | bytes 417800 | tf_op jit(solution)/shard_map/ppermute | solution.py:371
  48.8 1.6 %collective-permute-start.17 = (bf16[32,2176]{1,0:T(8,128)(2,1)S(1)}, bf16[32,2176]{1,0:T(8,128)(2,1)S(1)}, u32[]{:S(2)}, u32[]{:S(2)}) collective-permute-start(bf16[32,2176]{1,0:T(8,128)(2,1)S(1)} %get-tuple-element.70), channel_id=1, source_target_pairs={{0,6},{1,7},{2,4},{3,5},{4,2},{5,3},{6,0},{7,1},{8,14},{9,15},{10,... | collective-permute-start | bytes 417800 | tf_op jit(solution)/shard_map/ppermute | solution.py:371
  50.4 3.6 %collective-permute-done.19.refs_2_ = bf16[32,2048]{1,0:T(8,128)(2,1)S(1)} collective-permute-done((bf16[32,2048]{1,0:T(8,128)(2,1)S(1)}, bf16[32,2048]{1,0:T(8,128)(2,1)S(1)}, u32[]{:S(2)}, u32[]{:S(2)}) %collective-permute-start.19) | collective-permute-done | bytes 131104 | tf_op jit(solution)/shard_map/ppermute | solution.py:371
  54.0 1.6 %collective-permute-start.21 = (bf16[32,2048]{1,0:T(8,128)(2,1)S(1)}, bf16[32,2048]{1,0:T(8,128)(2,1)S(1)}, u32[]{:S(2)}, u32[]{:S(2)}) collective-permute-start(bf16[32,2048]{1,0:T(8,128)(2,1)S(1)} %get-tuple-element.76), channel_id=1, source_target_pairs={{0,6},{1,7},{2,4},{3,5},{4,2},{5,3},{6,0},{7,1},{8,14},{9,15},{10,... | collective-permute-start | bytes 393224 | tf_op jit(solution)/shard_map/ppermute | solution.py:371
  55.6 4.6 %collective-permute-done.20.refs_3_ = bf16[32,2048]{1,0:T(8,128)(2,1)S(1)} collective-permute-done((bf16[32,2048]{1,0:T(8,128)(2,1)S(1)}, bf16[32,2048]{1,0:T(8,128)(2,1)S(1)}, u32[]{:S(2)}, u32[]{:S(2)}) %collective-permute-start.20) | collective-permute-done | bytes 131104 | tf_op jit(solution)/shard_map/ppermute | solution.py:371
  60.2 1.4 %collective-permute-start.24 = (bf16[32,2048]{1,0:T(8,128)(2,1)S(1)}, bf16[32,2048]{1,0:T(8,128)(2,1)S(1)}, u32[]{:S(2)}, u32[]{:S(2)}) collective-permute-start(bf16[32,2048]{1,0:T(8,128)(2,1)S(1)} %get-tuple-element.79), channel_id=1, source_target_pairs={{0,4},{1,5},{2,6},{3,7},{4,0},{5,1},{6,2},{7,3},{8,12},{9,13},{10,... | collective-permute-start | bytes 393224 | tf_op jit(solution)/shard_map/ppermute | solution.py:371
  61.6 2.1 %collective-permute-start.25 = (bf16[32,2048]{1,0:T(8,128)(2,1)S(1)}, bf16[32,2048]{1,0:T(8,128)(2,1)S(1)}, u32[]{:S(2)}, u32[]{:S(2)}) collective-permute-start(bf16[32,2048]{1,0:T(8,128)(2,1)S(1)} %get-tuple-element.80), channel_id=1, source_target_pairs={{0,6},{1,7},{2,4},{3,5},{4,2},{5,3},{6,0},{7,1},{8,14},{9,15},{10,... | collective-permute-start | bytes 393224 | tf_op jit(solution)/shard_map/ppermute | solution.py:371
  64.5 2.5 %collective-permute-start.18 = (bf16[32,2176]{1,0:T(8,128)(2,1)S(1)}, bf16[32,2176]{1,0:T(8,128)(2,1)S(1)}, u32[]{:S(2)}, u32[]{:S(2)}) collective-permute-start(bf16[32,2176]{1,0:T(8,128)(2,1)S(1)} %get-tuple-element.72), channel_id=1, source_target_pairs={{0,24},{8,16},{16,8},{24,0},{1,25},{9,17},{17,9},{25,1},{2,26},{10... | collective-permute-start | bytes 417800 | tf_op jit(solution)/shard_map/ppermute | solution.py:374
  68.5 2.0 %collective-permute-start.26 = (bf16[32,2176]{1,0:T(8,128)(2,1)S(1)}, bf16[32,2176]{1,0:T(8,128)(2,1)S(1)}, u32[]{:S(2)}, u32[]{:S(2)}) collective-permute-start(bf16[32,2176]{1,0:T(8,128)(2,1)S(1)} %combine.7), channel_id=1, source_target_pairs={{0,8},{8,0},{16,24},{24,16},{1,9},{9,1},{17,25},{25,17},{2,10},{10... | collective-permute-start | bytes 417800 | tf_op jit(solution)/shard_map/ppermute | solution.py:374
  70.5 1.4 %collective-permute-start.13 = (bf16[32,2048]{1,0:T(8,128)(2,1)S(1)}, bf16[32,2048]{1,0:T(8,128)(2,1)S(1)}, u32[]{:S(2)}, u32[]{:S(2)}) collective-permute-start(bf16[32,2048]{1,0:T(8,128)(2,1)S(1)} %get-tuple-element.64), channel_id=1, source_target_pairs={{0,4},{1,5},{2,6},{3,7},{4,0},{5,1},{6,2},{7,3},{8,12},{9,13},{10,... | collective-permute-start | bytes 393224 | tf_op jit(solution)/shard_map/ppermute | solution.py:371
  71.9 2.1 %collective-permute-start.14 = (bf16[32,2048]{1,0:T(8,128)(2,1)S(1)}, bf16[32,2048]{1,0:T(8,128)(2,1)S(1)}, u32[]{:S(2)}, u32[]{:S(2)}) collective-permute-start(bf16[32,2048]{1,0:T(8,128)(2,1)S(1)} %get-tuple-element.65), channel_id=1, source_target_pairs={{0,6},{1,7},{2,4},{3,5},{4,2},{5,3},{6,0},{7,1},{8,14},{9,15},{10,... | collective-permute-start | bytes 393224 | tf_op jit(solution)/shard_map/ppermute | solution.py:371
  74.0 4.8 %collective-permute-done.13.refs_3_ = bf16[32,2048]{1,0:T(8,128)(2,1)S(1)} collective-permute-done((bf16[32,2048]{1,0:T(8,128)(2,1)S(1)}, bf16[32,2048]{1,0:T(8,128)(2,1)S(1)}, u32[]{:S(2)}, u32[]{:S(2)}) %collective-permute-start.13) | collective-permute-done | bytes 131104 | tf_op jit(solution)/shard_map/ppermute | solution.py:371
  79.7 2.5 %collective-permute-start.29 = (bf16[32,2176]{1,0:T(8,128)(2,1)S(1)}, bf16[32,2176]{1,0:T(8,128)(2,1)S(1)}, u32[]{:S(2)}, u32[]{:S(2)}) collective-permute-start(bf16[32,2176]{1,0:T(8,128)(2,1)S(1)} %finish.1.refs_0_), channel_id=1, source_target_pairs={{0,6},{1,7},{2,4},{3,5},{4,2},{5,3},{6,0},{7,1},{8,14},{9,15},{10,... | collective-permute-start | bytes 417800 | tf_op jit(solution)/shard_map/ppermute | solution.py:371
  82.2 1.5 %collective-permute-start.28 = (bf16[32,2176]{1,0:T(8,128)(2,1)S(1)}, bf16[32,2176]{1,0:T(8,128)(2,1)S(1)}, u32[]{:S(2)}, u32[]{:S(2)}) collective-permute-start(bf16[32,2176]{1,0:T(8,128)(2,1)S(1)} %finish.1.refs_0_), channel_id=1, source_target_pairs={{0,4},{1,5},{2,6},{3,7},{4,0},{5,1},{6,2},{7,3},{8,12},{9,13},{10,... | collective-permute-start | bytes 417800 | tf_op jit(solution)/shard_map/ppermute | solution.py:371
  83.7 2.0 %collective-permute-done.29.refs_3_ = bf16[32,2176]{1,0:T(8,128)(2,1)S(1)} collective-permute-done((bf16[32,2176]{1,0:T(8,128)(2,1)S(1)}, bf16[32,2176]{1,0:T(8,128)(2,1)S(1)}, u32[]{:S(2)}, u32[]{:S(2)}) %collective-permute-start.29) | collective-permute-done | bytes 139296 | tf_op jit(solution)/shard_map/ppermute | solution.py:371
  85.7 1.6 %collective-permute-done.28.refs_2_ = bf16[32,2176]{1,0:T(8,128)(2,1)S(1)} collective-permute-done((bf16[32,2176]{1,0:T(8,128)(2,1)S(1)}, bf16[32,2176]{1,0:T(8,128)(2,1)S(1)}, u32[]{:S(2)}, u32[]{:S(2)}) %collective-permute-start.28) | collective-permute-done | bytes 139296 | tf_op jit(solution)/shard_map/ppermute | solution.py:371
  87.3 1.5 %collective-permute-done.27.refs_1_ = bf16[32,2176]{1,0:T(8,128)(2,1)S(1)} collective-permute-done((bf16[32,2176]{1,0:T(8,128)(2,1)S(1)}, bf16[32,2176]{1,0:T(8,128)(2,1)S(1)}, u32[]{:S(2)}, u32[]{:S(2)}) %collective-permute-start.27) | collective-permute-done | bytes 139296 | tf_op jit(solution)/shard_map/ppermute | solution.py:371
  88.8 1.3 %collective-permute-done.31.refs_5_ = bf16[32,2176]{1,0:T(8,128)(2,1)S(1)} collective-permute-done((bf16[32,2176]{1,0:T(8,128)(2,1)S(1)}, bf16[32,2176]{1,0:T(8,128)(2,1)S(1)}, u32[]{:S(2)}, u32[]{:S(2)}) %collective-permute-start.31) | collective-permute-done | bytes 139296 | tf_op jit(solution)/shard_map/ppermute | solution.py:371
  90.1 1.6 %gather.1 = (bf16[256,2048]{1,0:T(8,128)(2,1)}, bf16[16,2048]{1,0:T(8,128)(2,1)S(1)}) custom-call(s32[3]{0:T(128)S(1)} %pad_add_fusion.place.refs_0_, bf16[32,2176]{1,0:T(8,128)(2,1)S(1)} %finish.1.refs_0_, bf16[32,2176]{1,0:T(8,128)(2,1)S(1)} %collective-permute-done.27.refs_1_, bf16[32,2176]{1,0:T(8,128)(2,1)S(1)} %collective-permute-done.28.refs_2_, ...), custom_call_target="tpu_custom_call" | custom-call | bytes 2097152 | tf_op jit(solution)/shard_map/gather/pallas_call | solution.py:542
  91.8 6.3 %gradients.1 = (bf16[1,2048,768]{2,1,0:T(8,128)(2,1)}, bf16[1,384,2048]{2,1,0:T(8,128)(2,1)}) custom-call(bf16[16,2048]{1,0:T(8,128)(2,1)S(1)} %get-tuple-element.57.refs_1_.last_block, bf16[16,2048]{1,0:T(8,128)(2,1)S(1)} %get-tuple-element.82.layer_last, f32[16,768]{1,0:T(8,128)S(1)} %get-tuple-element.83.projected, s32[3]{0:T(128)S(1)} %pad_add_fusion.place.refs_0_, ...), custom_call_target="tpu_custom_call" | custom-call | flops 100663296 | bytes 7340032 | tf_op jit(solution)/shard_map/gradients/pallas_call | solution.py:558
  (59 shorter events, 12.5 us)
Async XLA Ops:
  0.6 10.3 %collective-permute-start.3 = (bf16[1,2048,768]{2,1,0:T(8,128)(2,1)}, bf16[1,2048,768]{2,1,0:T(8,128)(2,1)}, u32[]{:S(2)}, u32[]{:S(2)}) collective-permute-start(bf16[1,2048,768]{2,1,0:T(8,128)(2,1)} %refs_7_.1), channel_id=1, source_target_pairs={{0,1},{1,0},{2,3},{3,2},{4,5},{5,4},{6,7},{7,6},{8,9},{9,8},{10,11... | collective-permute-start | bytes 9437192 | tf_op jit(solution)/shard_map/ppermute | solution.py:371
  1.2 9.7 %collective-permute-start.4 = (bf16[1,384,2048]{2,1,0:T(8,128)(2,1)}, bf16[1,384,2048]{2,1,0:T(8,128)(2,1)S(1)}, u32[]{:S(2)}, u32[]{:S(2)}) collective-permute-start(bf16[1,384,2048]{2,1,0:T(8,128)(2,1)} %down.1), channel_id=1, source_target_pairs={{0,1},{1,0},{2,3},{3,2},{4,5},{5,4},{6,7},{7,6},{8,9},{9,8},{10,11... | collective-permute-start | bytes 4718600 | tf_op jit(solution)/shard_map/ppermute | solution.py:371
  3.6 7.3 %collective-permute-start = (bf16[32,2176]{1,0:T(8,128)(2,1)}, bf16[32,2176]{1,0:T(8,128)(2,1)S(1)}, u32[]{:S(2)}, u32[]{:S(2)}) collective-permute-start(bf16[32,2176]{1,0:T(8,128)(2,1)} %pack.1.refs_0_), channel_id=1, source_target_pairs={{0,8},{8,0},{16,24},{24,16},{1,9},{9,1},{17,25},{25,17},{2,10},{10... | collective-permute-start | bytes 417800 | tf_op jit(solution)/shard_map/ppermute | solution.py:374
  6.6 10.3 %collective-permute-start.2 = (bf16[32,2176]{1,0:T(8,128)(2,1)}, bf16[32,2176]{1,0:T(8,128)(2,1)S(1)}, u32[]{:S(2)}, u32[]{:S(2)}) collective-permute-start(bf16[32,2176]{1,0:T(8,128)(2,1)} %pack.1.refs_0_), channel_id=1, source_target_pairs={{0,24},{8,16},{16,8},{24,0},{1,25},{9,17},{17,9},{25,1},{2,26},{10... | collective-permute-start | bytes 417800 | tf_op jit(solution)/shard_map/ppermute | solution.py:374
  9.1 13.1 %collective-permute-start.1 = (bf16[32,2176]{1,0:T(8,128)(2,1)}, bf16[32,2176]{1,0:T(8,128)(2,1)}, u32[]{:S(2)}, u32[]{:S(2)}) collective-permute-start(bf16[32,2176]{1,0:T(8,128)(2,1)} %pack.1.refs_0_), channel_id=1, source_target_pairs={{0,16},{8,24},{16,0},{24,8},{1,17},{9,25},{17,1},{25,9},{2,18},{10... | collective-permute-start | bytes 417800 | tf_op jit(solution)/shard_map/ppermute | solution.py:374
  10.9 12.2 %collective-permute-start.7 = (bf16[32,2304]{1,0:T(8,128)(2,1)S(1)}, bf16[32,2304]{1,0:T(8,128)(2,1)S(1)}, u32[]{:S(2)}, u32[]{:S(2)}) collective-permute-start(bf16[32,2304]{1,0:T(8,128)(2,1)S(1)} %pad_maximum_fusion.1), channel_id=1, source_target_pairs={{0,6},{1,7},{2,4},{3,5},{4,2},{5,3},{6,0},{7,1},{8,14},{9,15},{10,... | collective-permute-start | bytes 442376 | tf_op jit(solution)/shard_map/ppermute | solution.py:371
  13.5 9.6 %collective-permute-start.6 = (bf16[32,2304]{1,0:T(8,128)(2,1)S(1)}, bf16[32,2304]{1,0:T(8,128)(2,1)S(1)}, u32[]{:S(2)}, u32[]{:S(2)}) collective-permute-start(bf16[32,2304]{1,0:T(8,128)(2,1)S(1)} %pad_maximum_fusion.1), channel_id=1, source_target_pairs={{0,4},{1,5},{2,6},{3,7},{4,0},{5,1},{6,2},{7,3},{8,12},{9,13},{10,... | collective-permute-start | bytes 442376 | tf_op jit(solution)/shard_map/ppermute | solution.py:371
  14.0 9.1 %collective-permute-start.5 = (bf16[32,2304]{1,0:T(8,128)(2,1)S(1)}, bf16[32,2304]{1,0:T(8,128)(2,1)S(1)}, u32[]{:S(2)}, u32[]{:S(2)}) collective-permute-start(bf16[32,2304]{1,0:T(8,128)(2,1)S(1)} %pad_maximum_fusion.1), channel_id=1, source_target_pairs={{0,2},{1,3},{2,0},{3,1},{4,6},{5,7},{6,4},{7,5},{8,10},{9,11},{10,... | collective-permute-start | bytes 442376 | tf_op jit(solution)/shard_map/ppermute | solution.py:371
  23.1 11.6 %collective-permute-start.10 = (bf16[64,2176]{1,0:T(8,128)(2,1)S(1)}, bf16[64,2176]{1,0:T(8,128)(2,1)S(1)}, u32[]{:S(2)}, u32[]{:S(2)}) collective-permute-start(bf16[64,2176]{1,0:T(8,128)(2,1)S(1)} %pad_maximum_fusion), channel_id=1, source_target_pairs={{0,6},{1,7},{2,4},{3,5},{4,2},{5,3},{6,0},{7,1},{8,14},{9,15},{10,... | collective-permute-start | bytes 835592 | tf_op jit(solution)/shard_map/ppermute | solution.py:371
  25.6 12.2 %collective-permute-start.9 = (bf16[64,2176]{1,0:T(8,128)(2,1)S(1)}, bf16[64,2176]{1,0:T(8,128)(2,1)S(1)}, u32[]{:S(2)}, u32[]{:S(2)}) collective-permute-start(bf16[64,2176]{1,0:T(8,128)(2,1)S(1)} %pad_maximum_fusion), channel_id=1, source_target_pairs={{0,4},{1,5},{2,6},{3,7},{4,0},{5,1},{6,2},{7,3},{8,12},{9,13},{10,... | collective-permute-start | bytes 835592 | tf_op jit(solution)/shard_map/ppermute | solution.py:371
  26.1 11.8 %collective-permute-start.8 = (bf16[64,2176]{1,0:T(8,128)(2,1)S(1)}, bf16[64,2176]{1,0:T(8,128)(2,1)S(1)}, u32[]{:S(2)}, u32[]{:S(2)}) collective-permute-start(bf16[64,2176]{1,0:T(8,128)(2,1)S(1)} %pad_maximum_fusion), channel_id=1, source_target_pairs={{0,2},{1,3},{2,0},{3,1},{4,6},{5,7},{6,4},{7,5},{8,10},{9,11},{10,... | collective-permute-start | bytes 835592 | tf_op jit(solution)/shard_map/ppermute | solution.py:371
  39.4 5.2 %collective-permute-start.11 = (bf16[144,128]{1,0:T(8,128)(2,1)S(1)}, bf16[144,128]{1,0:T(8,128)(2,1)S(1)}, u32[]{:S(2)}, u32[]{:S(2)}) collective-permute-start(bf16[144,128]{1,0:T(8,128)(2,1)S(1)} %get-tuple-element.61), channel_id=1, source_target_pairs={{0,1},{1,0},{2,3},{3,2},{4,5},{5,4},{6,7},{7,6},{8,9},{9,8},{10,11... | collective-permute-start | bytes 110600 | tf_op jit(solution)/shard_map/ppermute | solution.py:371
  44.6 15.6 %collective-permute-start.15 = (bf16[32,2176]{1,0:T(8,128)(2,1)S(1)}, bf16[32,2176]{1,0:T(8,128)(2,1)S(1)}, u32[]{:S(2)}, u32[]{:S(2)}) collective-permute-start(bf16[32,2176]{1,0:T(8,128)(2,1)S(1)} %get-tuple-element.68), channel_id=1, source_target_pairs={{0,2},{1,3},{2,0},{3,1},{4,6},{5,7},{6,4},{7,5},{8,10},{9,11},{10,... | collective-permute-start | bytes 417800 | tf_op jit(solution)/shard_map/ppermute | solution.py:371
  46.2 15.4 %collective-permute-start.16 = (bf16[32,2176]{1,0:T(8,128)(2,1)S(1)}, bf16[32,2176]{1,0:T(8,128)(2,1)S(1)}, u32[]{:S(2)}, u32[]{:S(2)}) collective-permute-start(bf16[32,2176]{1,0:T(8,128)(2,1)S(1)} %get-tuple-element.69), channel_id=1, source_target_pairs={{0,4},{1,5},{2,6},{3,7},{4,0},{5,1},{6,2},{7,3},{8,12},{9,13},{10,... | collective-permute-start | bytes 417800 | tf_op jit(solution)/shard_map/ppermute | solution.py:371
  46.9 7.1 %collective-permute-start.19 = (bf16[32,2048]{1,0:T(8,128)(2,1)S(1)}, bf16[32,2048]{1,0:T(8,128)(2,1)S(1)}, u32[]{:S(2)}, u32[]{:S(2)}) collective-permute-start(bf16[32,2048]{1,0:T(8,128)(2,1)S(1)} %get-tuple-element.74), channel_id=1, source_target_pairs={{0,2},{1,3},{2,0},{3,1},{4,6},{5,7},{6,4},{7,5},{8,10},{9,11},{10,... | collective-permute-start | bytes 393224 | tf_op jit(solution)/shard_map/ppermute | solution.py:371
  48.1 12.1 %collective-permute-start.20 = (bf16[32,2048]{1,0:T(8,128)(2,1)S(1)}, bf16[32,2048]{1,0:T(8,128)(2,1)S(1)}, u32[]{:S(2)}, u32[]{:S(2)}) collective-permute-start(bf16[32,2048]{1,0:T(8,128)(2,1)S(1)} %get-tuple-element.75), channel_id=1, source_target_pairs={{0,4},{1,5},{2,6},{3,7},{4,0},{5,1},{6,2},{7,3},{8,12},{9,13},{10,... | collective-permute-start | bytes 393224 | tf_op jit(solution)/shard_map/ppermute | solution.py:371
  48.8 15.0 %collective-permute-start.17 = (bf16[32,2176]{1,0:T(8,128)(2,1)S(1)}, bf16[32,2176]{1,0:T(8,128)(2,1)S(1)}, u32[]{:S(2)}, u32[]{:S(2)}) collective-permute-start(bf16[32,2176]{1,0:T(8,128)(2,1)S(1)} %get-tuple-element.70), channel_id=1, source_target_pairs={{0,6},{1,7},{2,4},{3,5},{4,2},{5,3},{6,0},{7,1},{8,14},{9,15},{10,... | collective-permute-start | bytes 417800 | tf_op jit(solution)/shard_map/ppermute | solution.py:371
  54.0 10.5 %collective-permute-start.21 = (bf16[32,2048]{1,0:T(8,128)(2,1)S(1)}, bf16[32,2048]{1,0:T(8,128)(2,1)S(1)}, u32[]{:S(2)}, u32[]{:S(2)}) collective-permute-start(bf16[32,2048]{1,0:T(8,128)(2,1)S(1)} %get-tuple-element.76), channel_id=1, source_target_pairs={{0,6},{1,7},{2,4},{3,5},{4,2},{5,3},{6,0},{7,1},{8,14},{9,15},{10,... | collective-permute-start | bytes 393224 | tf_op jit(solution)/shard_map/ppermute | solution.py:371
  60.2 7.5 %collective-permute-start.23 = (bf16[32,2048]{1,0:T(8,128)(2,1)S(1)}, bf16[32,2048]{1,0:T(8,128)(2,1)S(1)}, u32[]{:S(2)}, u32[]{:S(2)}) collective-permute-start(bf16[32,2048]{1,0:T(8,128)(2,1)S(1)} %get-tuple-element.78), channel_id=1, source_target_pairs={{0,2},{1,3},{2,0},{3,1},{4,6},{5,7},{6,4},{7,5},{8,10},{9,11},{10,... | collective-permute-start | bytes 393224 | tf_op jit(solution)/shard_map/ppermute | solution.py:371
  60.2 7.6 %collective-permute-start.24 = (bf16[32,2048]{1,0:T(8,128)(2,1)S(1)}, bf16[32,2048]{1,0:T(8,128)(2,1)S(1)}, u32[]{:S(2)}, u32[]{:S(2)}) collective-permute-start(bf16[32,2048]{1,0:T(8,128)(2,1)S(1)} %get-tuple-element.79), channel_id=1, source_target_pairs={{0,4},{1,5},{2,6},{3,7},{4,0},{5,1},{6,2},{7,3},{8,12},{9,13},{10,... | collective-permute-start | bytes 393224 | tf_op jit(solution)/shard_map/ppermute | solution.py:371
  61.6 6.2 %collective-permute-start.25 = (bf16[32,2048]{1,0:T(8,128)(2,1)S(1)}, bf16[32,2048]{1,0:T(8,128)(2,1)S(1)}, u32[]{:S(2)}, u32[]{:S(2)}) collective-permute-start(bf16[32,2048]{1,0:T(8,128)(2,1)S(1)} %get-tuple-element.80), channel_id=1, source_target_pairs={{0,6},{1,7},{2,4},{3,5},{4,2},{5,3},{6,0},{7,1},{8,14},{9,15},{10,... | collective-permute-start | bytes 393224 | tf_op jit(solution)/shard_map/ppermute | solution.py:371
  63.7 8.2 %collective-permute-start.12 = (bf16[32,2048]{1,0:T(8,128)(2,1)S(1)}, bf16[32,2048]{1,0:T(8,128)(2,1)S(1)}, u32[]{:S(2)}, u32[]{:S(2)}) collective-permute-start(bf16[32,2048]{1,0:T(8,128)(2,1)S(1)} %get-tuple-element.63), channel_id=1, source_target_pairs={{0,2},{1,3},{2,0},{3,1},{4,6},{5,7},{6,4},{7,5},{8,10},{9,11},{10,... | collective-permute-start | bytes 393224 | tf_op jit(solution)/shard_map/ppermute | solution.py:371
  64.5 15.1 %collective-permute-start.18 = (bf16[32,2176]{1,0:T(8,128)(2,1)S(1)}, bf16[32,2176]{1,0:T(8,128)(2,1)S(1)}, u32[]{:S(2)}, u32[]{:S(2)}) collective-permute-start(bf16[32,2176]{1,0:T(8,128)(2,1)S(1)} %get-tuple-element.72), channel_id=1, source_target_pairs={{0,24},{8,16},{16,8},{24,0},{1,25},{9,17},{17,9},{25,1},{2,26},{10... | collective-permute-start | bytes 417800 | tf_op jit(solution)/shard_map/ppermute | solution.py:374
  67.7 11.9 %collective-permute-start.22 = (bf16[32,2176]{1,0:T(8,128)(2,1)S(1)}, bf16[32,2176]{1,0:T(8,128)(2,1)S(1)}, u32[]{:S(2)}, u32[]{:S(2)}) collective-permute-start(bf16[32,2176]{1,0:T(8,128)(2,1)S(1)} %combine.6), channel_id=1, source_target_pairs={{0,16},{8,24},{16,0},{24,8},{1,17},{9,25},{17,1},{25,9},{2,18},{10... | collective-permute-start | bytes 417800 | tf_op jit(solution)/shard_map/ppermute | solution.py:374
  68.5 11.1 %collective-permute-start.26 = (bf16[32,2176]{1,0:T(8,128)(2,1)S(1)}, bf16[32,2176]{1,0:T(8,128)(2,1)S(1)}, u32[]{:S(2)}, u32[]{:S(2)}) collective-permute-start(bf16[32,2176]{1,0:T(8,128)(2,1)S(1)} %combine.7), channel_id=1, source_target_pairs={{0,8},{8,0},{16,24},{24,16},{1,9},{9,1},{17,25},{25,17},{2,10},{10... | collective-permute-start | bytes 417800 | tf_op jit(solution)/shard_map/ppermute | solution.py:374
  70.5 8.3 %collective-permute-start.13 = (bf16[32,2048]{1,0:T(8,128)(2,1)S(1)}, bf16[32,2048]{1,0:T(8,128)(2,1)S(1)}, u32[]{:S(2)}, u32[]{:S(2)}) collective-permute-start(bf16[32,2048]{1,0:T(8,128)(2,1)S(1)} %get-tuple-element.64), channel_id=1, source_target_pairs={{0,4},{1,5},{2,6},{3,7},{4,0},{5,1},{6,2},{7,3},{8,12},{9,13},{10,... | collective-permute-start | bytes 393224 | tf_op jit(solution)/shard_map/ppermute | solution.py:371
  71.9 6.9 %collective-permute-start.14 = (bf16[32,2048]{1,0:T(8,128)(2,1)S(1)}, bf16[32,2048]{1,0:T(8,128)(2,1)S(1)}, u32[]{:S(2)}, u32[]{:S(2)}) collective-permute-start(bf16[32,2048]{1,0:T(8,128)(2,1)S(1)} %get-tuple-element.65), channel_id=1, source_target_pairs={{0,6},{1,7},{2,4},{3,5},{4,2},{5,3},{6,0},{7,1},{8,14},{9,15},{10,... | collective-permute-start | bytes 393224 | tf_op jit(solution)/shard_map/ppermute | solution.py:371
  79.7 6.0 %collective-permute-start.29 = (bf16[32,2176]{1,0:T(8,128)(2,1)S(1)}, bf16[32,2176]{1,0:T(8,128)(2,1)S(1)}, u32[]{:S(2)}, u32[]{:S(2)}) collective-permute-start(bf16[32,2176]{1,0:T(8,128)(2,1)S(1)} %finish.1.refs_0_), channel_id=1, source_target_pairs={{0,6},{1,7},{2,4},{3,5},{4,2},{5,3},{6,0},{7,1},{8,14},{9,15},{10,... | collective-permute-start | bytes 417800 | tf_op jit(solution)/shard_map/ppermute | solution.py:371
  82.2 5.1 %collective-permute-start.28 = (bf16[32,2176]{1,0:T(8,128)(2,1)S(1)}, bf16[32,2176]{1,0:T(8,128)(2,1)S(1)}, u32[]{:S(2)}, u32[]{:S(2)}) collective-permute-start(bf16[32,2176]{1,0:T(8,128)(2,1)S(1)} %finish.1.refs_0_), channel_id=1, source_target_pairs={{0,4},{1,5},{2,6},{3,7},{4,0},{5,1},{6,2},{7,3},{8,12},{9,13},{10,... | collective-permute-start | bytes 417800 | tf_op jit(solution)/shard_map/ppermute | solution.py:371
  83.7 5.1 %collective-permute-start.27 = (bf16[32,2176]{1,0:T(8,128)(2,1)S(1)}, bf16[32,2176]{1,0:T(8,128)(2,1)S(1)}, u32[]{:S(2)}, u32[]{:S(2)}) collective-permute-start(bf16[32,2176]{1,0:T(8,128)(2,1)S(1)} %finish.1.refs_0_), channel_id=1, source_target_pairs={{0,2},{1,3},{2,0},{3,1},{4,6},{5,7},{6,4},{7,5},{8,10},{9,11},{10,... | collective-permute-start | bytes 417800 | tf_op jit(solution)/shard_map/ppermute | solution.py:371
  83.7 5.1 %collective-permute-start.30 = (bf16[32,2176]{1,0:T(8,128)(2,1)S(1)}, bf16[32,2176]{1,0:T(8,128)(2,1)S(1)}, u32[]{:S(2)}, u32[]{:S(2)}) collective-permute-start(bf16[32,2176]{1,0:T(8,128)(2,1)S(1)} %finish.1.refs_0_), channel_id=1, source_target_pairs={{0,1},{1,0},{2,3},{3,2},{4,5},{5,4},{6,7},{7,6},{8,9},{9,8},{10,11... | collective-permute-start | bytes 417800 | tf_op jit(solution)/shard_map/ppermute | solution.py:371
  85.7 3.1 %collective-permute-start.33 = (bf16[32,2176]{1,0:T(8,128)(2,1)S(1)}, bf16[32,2176]{1,0:T(8,128)(2,1)S(1)}, u32[]{:S(2)}, u32[]{:S(2)}) collective-permute-start(bf16[32,2176]{1,0:T(8,128)(2,1)S(1)} %collective-permute-done.29.refs_3_), channel_id=1, source_target_pairs={{0,1},{1,0},{2,3},{3,2},{4,5},{5,4},{6,7},{7,6},{8,9},{9,8},{10,11... | collective-permute-start | bytes 417800 | tf_op jit(solution)/shard_map/ppermute | solution.py:371
  (6 other events, 40.2 us)

commit v7 on v6

--- a/solution.py
+++ b/solution.py
@@ -265,60 +265,56 @@
 
 
 def finish_kernel(near, own_last, last_sum, *refs):
-    parts, out = refs[:-1], refs[-1]
+    parts, (out, last_out) = refs[:-2], refs[-2:]
     width = near.shape[1]
     total = near[...]
     last = last_sum[...].astype(f32)
     for part in parts:
         total = total + part[:, :width].astype(f32)
         last = last + part[:, width:].astype(f32)
-    out[:, :width] = total.astype(bf16)
-    out[:, width:] = (own_last[...] + last).astype(bf16)
-
-
-def gather_kernel(chips, each, place, *refs):
-    pieces, (out, last_rows, by_lane) = refs[: 2 * chips], refs[2 * chips :]
-    part_rows, width = pieces[0].shape[0], out.shape[1]
-    chunks = width // lanes
+    out[...] = total.astype(bf16)
+    last_out[...] = (own_last[...] + last).astype(bf16)
+
+
+def gather_kernel(chips, place, *refs):
+    pieces, out = refs[: 2 * chips], refs[-1]
+    part_rows = pieces[0].shape[0]
     for index in range(2 * chips):
         lane = place[1] ^ (2 * (index % chips)) ^ (index // chips)
-        piece = pieces[index]
         start = pl.multiple_of(lane * part_rows, part_rows)
-        out[pl.ds(start, part_rows), :] = piece[:, :width]
-        values = piece[:, width:].astype(f32)
+        out[pl.ds(start, part_rows), :] = pieces[index][...]
+
+
+def collect_rows(lane, shares, by_lane, each):
+    chunks = by_lane.shape[2] // lanes
+    part_rows = shares[0].shape[0] // 2
+    for index in range(2 * len(shares)):
+        source = lane ^ index
+        first = index % 2 * part_rows
+        values = shares[index // 2][first : first + part_rows, :].astype(f32)
         for spot in range(each * chunks):
             row, chunk = spot // chunks, spot % chunks
             at = spot // part_rows * lanes
             from_row = spot % part_rows
-            by_lane[lane, row : row + 1, chunk * lanes : (chunk + 1) * lanes] = values[
+            by_lane[source, row : row + 1, chunk * lanes : (chunk + 1) * lanes] = values[
                 from_row : from_row + 1, at : at + lanes
             ]
-    ordered = [by_lane[lane, 0:each, :] for lane in range(2 * chips)]
-    last_rows[...] = jnp.concatenate(ordered, axis=0).astype(bf16)
-
-
-def gradient_kernel(
-    last_block,
-    layer_last,
-    projected,
-    place,
-    kept,
-    found,
-    partners,
-    down,
-    grad_in,
-    grad_out,
-    route,
-    hidden,
-    slope,
-):
+    ordered = [by_lane[index, 0:each, :] for index in range(2 * len(shares))]
+    return jnp.concatenate(ordered, axis=0)
+
+
+def gradient_kernel(chips, *refs):
+    shares, refs = refs[:chips], refs[chips:]
+    last_block, projected, place, kept, found, partners, down, *refs = refs
+    grad_in, grad_out, route, hidden, slope, by_lane = refs
     step = pl.program_id(0)
     half_width = down.shape[1]
     block = grad_out.shape[2]
 
     @pl.when(step == 0)
     def _():
-        values = layer_last[...].astype(f32)
+        each = projected.shape[0] // by_lane.shape[0]
+        values = collect_rows(place[1], shares, by_lane, each)
         count = values.shape[0]
         last = kept.shape[0] - count
         table = kept[last:, :].astype(f32) + found[last:, :].astype(f32)
@@ -515,10 +511,12 @@
     last_projected, own_last = out[-2:]
 
     returned = {}
-    for hop in range(dp_count - 1, -1, -1):
+    for hop in [0] + list(range(dp_count - 1, 0, -1)):
         first, *sent_back = outs[hop]
         if hop == dp_count - 1:
-            sent_back, found = lax.optimization_barrier((sent_back, found))
+            sent_back, found, returned[0][1:] = lax.optimization_barrier(
+                (sent_back, found, returned[0][1:])
+            )
         returned[hop] = [first] + [to_lane(value, step) for value, step in zip(sent_back, chip_steps)]
     homeward = []
     last_sum = None
@@ -528,27 +526,28 @@
         homeward.append(to_plane(result[0], hop))
     near_sum = combine(0, returned[0], last_sum)[0]
 
-    own_out = pl.pallas_call(
+    own_out, share = pl.pallas_call(
         finish_kernel,
-        out_shape=jax.ShapeDtypeStruct((part_rows, width + extra), bf16),
+        out_shape=[
+            jax.ShapeDtypeStruct((part_rows, width), bf16),
+            jax.ShapeDtypeStruct((part_rows, extra), bf16),
+        ],
         in_specs=[in_vmem] * (2 + dp_count),
-        out_specs=in_vmem,
+        out_specs=[in_vmem] * 2,
         compiler_params=params(16 if dp_count > 8 else 4),
         cost_estimate=cost(0, 1 << 20),
         name="finish",
     )(near_sum, own_last, last_sum, *homeward)
+    shares = [jnp.concatenate([share, to_lane(share, 1)], axis=0)]
+    shares += [to_lane(shares[0], step) for step in chip_steps]
     pieces = [own_out] + [to_lane(own_out, step) for step in chip_steps]
     pieces += [to_lane(piece, 1) for piece in pieces]
-    layer_out, layer_last = pl.pallas_call(
-        functools.partial(gather_kernel, chips, each),
-        out_shape=[
-            jax.ShapeDtypeStruct((tok_dev, width), bf16),
-            jax.ShapeDtypeStruct((seqs, width), bf16),
-        ],
+    layer_out = pl.pallas_call(
+        functools.partial(gather_kernel, chips),
+        out_shape=jax.ShapeDtypeStruct((tok_dev, width), bf16),
         in_specs=[in_smem] + [in_vmem] * len(pieces),
-        out_specs=[in_vmem] * 2,
-        scratch_shapes=[pltpu.VMEM((expert_count, -(-each // 8) * 8, width), f32)],
-        compiler_params=params(8),
+        out_specs=in_vmem,
+        compiler_params=params(4),
         cost_estimate=cost(0, 2 << 20),
         name="gather",
     )(place, *pieces)
@@ -556,15 +555,15 @@
     block = min(512, width)
     steps = width // block
     grad_gate_up, grad_down = pl.pallas_call(
-        gradient_kernel,
+        functools.partial(gradient_kernel, chips),
         grid=(steps,),
         out_shape=[
             jax.ShapeDtypeStruct(gate_up.shape, bf16),
             jax.ShapeDtypeStruct(down.shape, bf16),
         ],
         in_specs=[
+            *[pl.BlockSpec((2 * part_rows, extra), lambda step: (0, 0))] * chips,
             pl.BlockSpec((seqs, block), lambda step: (0, step)),
-            pl.BlockSpec((seqs, width), lambda step: (0, 0)),
             pl.BlockSpec((seqs, 2 * half_width), lambda step: (0, 0)),
             in_smem,
             pl.BlockSpec((table_rows, lanes), lambda step: (0, 0)),
@@ -580,11 +579,12 @@
             pltpu.VMEM((steps, seqs, block), bf16),
             pltpu.VMEM((seqs, half_width), bf16),
             pltpu.VMEM((seqs, 2 * half_width), bf16),
+            pltpu.VMEM((expert_count, -(-each // 8) * 8, width), f32),
         ],
         compiler_params=params(24),
         cost_estimate=cost(2 * seqs * width * 4 * half_width, 7 << 20),
         name="gradients",
-    )(last_all, layer_last, last_projected, place, kept, found, partners, down)
+    )(*shares, last_all, last_projected, place, kept, found, partners, down)
     return (layer_out, grad_gate_up, grad_down)
 
 

time: 98.3 us -> 107 us (1.089)
  waiting for transfers between devices: 31.3 us -> 38.8 us
    ppermute x6, waiting for transfers between devices: 8.62 us -> 15.3 us  [to_plane(): return lax.ppermute(value, 'dp', [(p, p ^ step) for p in range(dp_count)])]
    ppermute x28 -> x32, starting transfers between devices: 26.2 us -> 28.9 us  [to_lane(): lax.ppermute(value, 'expert', [(j, j ^ step) for j in range(expert_count)])]
    ppermute x6, starting transfers between devices: 10.2 us -> 8.48 us  [to_plane(): return lax.ppermute(value, 'dp', [(p, p ^ step) for p in range(dp_count)])]
    ppermute x28 -> x32, waiting for transfers between devices: 22.6 us -> 23.6 us  [to_lane(): lax.ppermute(value, 'expert', [(j, j ^ step) for j in range(expert_count)])]
    unnamed x8 -> x9, local copies, waits for them, and re-layouts: 3.12 us -> 3.12 us
  transfers between devices with their start and end apart: 34 -> 38, of which waited for: 12 -> 15; matrix products, arithmetic and copies ran while one was open for 2% -> 2% of each run, Pallas kernels for 16% -> 22%
where the time goes in v7:
time: 107 us
  waiting for transfers between devices  38.8 us (36%)
  starting transfers between devices  37.4 us (35%)
  Pallas kernels  24.7 us (23%)
  local copies, waits for them, and re-layouts  3.86 us (4%)
    ppermute x32, starting transfers between devices, to_lane(): lax.ppermute(value, 'expert', [(j, j ^ step) for j in range(expert_count)])  28.9 us
    ppermute x32, waiting for transfers between devices, to_lane(): lax.ppermute(value, 'expert', [(j, j ^ step) for j in range(expert_count)])  23.6 us
    ppermute x6, waiting for transfers between devices, to_plane(): return lax.ppermute(value, 'dp', [(p, p ^ step) for p in range(dp_count)])  15.3 us
    pallas_call x2, Pallas kernels, expert(): pl.pallas_call(functools.partial(expert_kernel, (tuple(group), chips, par...  10 us
    ppermute x6, starting transfers between devices, to_plane(): return lax.ppermute(value, 'dp', [(p, p ^ step) for p in range(dp_count)])  8.48 us
    pallas_call x1, Pallas kernels, body(): pl.pallas_call(functools.partial(gradient_kernel, chips), grid=(steps,),...  6.36 us
    unnamed x9, local copies, waits for them, and re-layouts  3.12 us
    pallas_call x4, Pallas kernels, combine(): pl.pallas_call(functools.partial(combine_kernel, (hop, chips, with_last,...  2.89 us
  transfers between devices with their start and end apart: 38, of which 15 were waited for; matrix products, arithmetic and copies ran while one was open for 2% of the time, Pallas kernels for 22%

profile of v7, /device:TPU:0, one launch (start us, length us, event | category | flops | bytes accessed | tf_op | source)
XLA Modules:
  0.0 106.6 jit_solution(2031749208069891873)
XLA Ops:
  1.2 2.3 %pack.1.refs_0_ = bf16[32,2176]{1,0:T(8,128)(2,1)} custom-call(s32[4]{0:T(128)} %positives.1, s32[1,256]{1,0:T(1,128)} %bitcast.5, f32[1,256]{1,0:T(1,128)} %bitcast.6, bf16[256,2048]{1,0:T(8,128)(2,1)} %refs_1_.1), custom_call_target="tpu_custom_call" | custom-call | bytes 524288 | tf_op jit(solution)/shard_map/pack/pallas_call | solution.py:376
  3.6 3.1 %collective-permute-start = (bf16[32,2176]{1,0:T(8,128)(2,1)}, bf16[32,2176]{1,0:T(8,128)(2,1)S(1)}, u32[]{:S(2)}, u32[]{:S(2)}) collective-permute-start(bf16[32,2176]{1,0:T(8,128)(2,1)} %pack.1.refs_0_), channel_id=1, source_target_pairs={{0,8},{8,0},{16,24},{24,16},{1,9},{9,1},{17,25},{25,17},{2,10},{10... | collective-permute-start | bytes 417800 | tf_op jit(solution)/shard_map/ppermute | solution.py:370
  6.6 2.5 %collective-permute-start.2 = (bf16[32,2176]{1,0:T(8,128)(2,1)}, bf16[32,2176]{1,0:T(8,128)(2,1)S(1)}, u32[]{:S(2)}, u32[]{:S(2)}) collective-permute-start(bf16[32,2176]{1,0:T(8,128)(2,1)} %pack.1.refs_0_), channel_id=1, source_target_pairs={{0,24},{8,16},{16,8},{24,0},{1,25},{9,17},{17,9},{25,1},{2,26},{10... | collective-permute-start | bytes 417800 | tf_op jit(solution)/shard_map/ppermute | solution.py:370
  10.9 2.6 %collective-permute-start.7 = (bf16[32,2304]{1,0:T(8,128)(2,1)S(1)}, bf16[32,2304]{1,0:T(8,128)(2,1)S(1)}, u32[]{:S(2)}, u32[]{:S(2)}) collective-permute-start(bf16[32,2304]{1,0:T(8,128)(2,1)S(1)} %pad_maximum_fusion.1), channel_id=1, source_target_pairs={{0,6},{1,7},{2,4},{3,5},{4,2},{5,3},{6,0},{7,1},{8,14},{9,15},{10,... | collective-permute-start | bytes 442376 | tf_op jit(solution)/shard_map/ppermute | solution.py:367
  14.5 2.4 %collective-permute-done.2.refs_6_.refs_3_ = bf16[32,2176]{1,0:T(8,128)(2,1)S(1)} collective-permute-done((bf16[32,2176]{1,0:T(8,128)(2,1)}, bf16[32,2176]{1,0:T(8,128)(2,1)S(1)}, u32[]{:S(2)}, u32[]{:S(2)}) %collective-permute-start.2) | collective-permute-done | bytes 139296 | tf_op jit(solution)/shard_map/ppermute | solution.py:370
  16.9 5.3 %collective-permute-done.1.refs_5_.refs_2_ = bf16[32,2176]{1,0:T(8,128)(2,1)} collective-permute-done((bf16[32,2176]{1,0:T(8,128)(2,1)}, bf16[32,2176]{1,0:T(8,128)(2,1)}, u32[]{:S(2)}, u32[]{:S(2)}) %collective-permute-start.1) | collective-permute-done | bytes 139296 | tf_op jit(solution)/shard_map/ppermute | solution.py:370
  23.1 2.5 %collective-permute-start.10 = (bf16[64,2176]{1,0:T(8,128)(2,1)S(1)}, bf16[64,2176]{1,0:T(8,128)(2,1)S(1)}, u32[]{:S(2)}, u32[]{:S(2)}) collective-permute-start(bf16[64,2176]{1,0:T(8,128)(2,1)S(1)} %pad_maximum_fusion), channel_id=1, source_target_pairs={{0,6},{1,7},{2,4},{3,5},{4,2},{5,3},{6,0},{7,1},{8,14},{9,15},{10,... | collective-permute-start | bytes 835592 | tf_op jit(solution)/shard_map/ppermute | solution.py:367
  26.8 1.9 %copy-done.1 = bf16[1,2048,768]{2,1,0:T(8,128)(2,1)S(1)} copy-done((bf16[1,2048,768]{2,1,0:T(8,128)(2,1)S(1)}, bf16[1,2048,768]{2,1,0:T(8,128)(2,1)}, u32[]{:S(2)}) %copy-start.1) | copy-done | bytes 3145752
  29.9 4.9 %experts.2 = (bf16[32,2048]{1,0:T(8,128)(2,1)S(1)}, bf16[32,2048]{1,0:T(8,128)(2,1)S(1)}, bf16[32,2048]{1,0:T(8,128)(2,1)S(1)}, bf16[32,2048]{1,0:T(8,128)(2,1)S...) custom-call(s32[3]{0:T(128)S(1)} %pad_add_fusion.place.refs_0_.refs_, ...), custom_call_target="tpu_custom_call" | custom-call | flops 2415919104 | bytes 12582912 | tf_op jit(solution)/shard_map/experts/pallas_call | solution.py:471
  34.8 1.6 %collective-permute-start.12 = (bf16[32,2048]{1,0:T(8,128)(2,1)S(1)}, bf16[32,2048]{1,0:T(8,128)(2,1)S(1)}, u32[]{:S(2)}, u32[]{:S(2)}) collective-permute-start(bf16[32,2048]{1,0:T(8,128)(2,1)S(1)} %get-tuple-element.65), channel_id=1, source_target_pairs={{0,2},{1,3},{2,0},{3,1},{4,6},{5,7},{6,4},{7,5},{8,10},{9,11},{10,... | collective-permute-start | bytes 393224 | tf_op jit(solution)/shard_map/ppermute | solution.py:367
  36.3 1.5 %collective-permute-start.13 = (bf16[32,2048]{1,0:T(8,128)(2,1)S(1)}, bf16[32,2048]{1,0:T(8,128)(2,1)S(1)}, u32[]{:S(2)}, u32[]{:S(2)}) collective-permute-start(bf16[32,2048]{1,0:T(8,128)(2,1)S(1)} %get-tuple-element.66), channel_id=1, source_target_pairs={{0,4},{1,5},{2,6},{3,7},{4,0},{5,1},{6,2},{7,3},{8,12},{9,13},{10,... | collective-permute-start | bytes 393224 | tf_op jit(solution)/shard_map/ppermute | solution.py:367
  38.3 1.4 %collective-permute-done.8.refs_7_.refs_4_ = bf16[64,2176]{1,0:T(8,128)(2,1)S(1)} collective-permute-done((bf16[64,2176]{1,0:T(8,128)(2,1)S(1)}, bf16[64,2176]{1,0:T(8,128)(2,1)S(1)}, u32[]{:S(2)}, u32[]{:S(2)}) %collective-permute-start.8) | collective-permute-done | bytes 278560 | tf_op jit(solution)/shard_map/ppermute | solution.py:367
  39.8 1.4 %tables.1 = (bf16[144,128]{1,0:T(8,128)(2,1)S(1)}, bf16[144,128]{1,0:T(8,128)(2,1)S(1)}, bf16[16,2048]{1,0:T(8,128)(2,1)S(1)}, f32[16,128]{1,0:T(8,128)S(1)}) custom-call(s32[3]{0:T(128)S(1)} %pad_add_fusion.place.refs_0_.refs_6_, bf16[32,2176]{1,0:T(8,128)(2,1)S(1)} %copy-done.3, bf16[32,2176]{1,0:T(8,128)(2,1)S(1)} %collective-permute-done.refs_1_.refs_2_, ...), custom_call_target="tpu_custom_call" | custom-call | bytes 1048576 | tf_op jit(solution)/shard_map/tables/pallas_call | solution.py:424
  41.3 5.1 %experts.3 = (bf16[32,2048]{1,0:T(8,128)(2,1)S(1)}, bf16[32,2048]{1,0:T(8,128)(2,1)S(1)}, bf16[32,2048]{1,0:T(8,128)(2,1)S(1)}, bf16[32,2048]{1,0:T(8,128)(2,1)S...) custom-call(s32[3]{0:T(128)S(1)} %pad_add_fusion.place.refs_0_.refs_, ...), custom_call_target="tpu_custom_call" | custom-call | flops 2566914048 | bytes 12582912 | tf_op jit(solution)/shard_map/experts/pallas_call | solution.py:471
  46.5 1.5 %collective-permute-start.15 = (bf16[32,2176]{1,0:T(8,128)(2,1)S(1)}, bf16[32,2176]{1,0:T(8,128)(2,1)S(1)}, u32[]{:S(2)}, u32[]{:S(2)}) collective-permute-start(bf16[32,2176]{1,0:T(8,128)(2,1)S(1)} %get-tuple-element.74), channel_id=1, source_target_pairs={{0,2},{1,3},{2,0},{3,1},{4,6},{5,7},{6,4},{7,5},{8,10},{9,11},{10,... | collective-permute-start | bytes 417800 | tf_op jit(solution)/shard_map/ppermute | solution.py:367
  48.1 1.9 %collective-permute-start.17 = (bf16[32,2176]{1,0:T(8,128)(2,1)S(1)}, bf16[32,2176]{1,0:T(8,128)(2,1)S(1)}, u32[]{:S(2)}, u32[]{:S(2)}) collective-permute-start(bf16[32,2176]{1,0:T(8,128)(2,1)S(1)} %get-tuple-element.76), channel_id=1, source_target_pairs={{0,6},{1,7},{2,4},{3,5},{4,2},{5,3},{6,0},{7,1},{8,14},{9,15},{10,... | collective-permute-start | bytes 417800 | tf_op jit(solution)/shard_map/ppermute | solution.py:367
  50.0 1.4 %collective-permute-start.19 = (bf16[32,2048]{1,0:T(8,128)(2,1)S(1)}, bf16[32,2048]{1,0:T(8,128)(2,1)S(1)}, u32[]{:S(2)}, u32[]{:S(2)}) collective-permute-start(bf16[32,2048]{1,0:T(8,128)(2,1)S(1)} %get-tuple-element.80), channel_id=1, source_target_pairs={{0,2},{1,3},{2,0},{3,1},{4,6},{5,7},{6,4},{7,5},{8,10},{9,11},{10,... | collective-permute-start | bytes 393224 | tf_op jit(solution)/shard_map/ppermute | solution.py:367
  51.6 6.8 %collective-permute-done.19.refs_2_ = bf16[32,2048]{1,0:T(8,128)(2,1)S(1)} collective-permute-done((bf16[32,2048]{1,0:T(8,128)(2,1)S(1)}, bf16[32,2048]{1,0:T(8,128)(2,1)S(1)}, u32[]{:S(2)}, u32[]{:S(2)}) %collective-permute-start.19) | collective-permute-done | bytes 131104 | tf_op jit(solution)/shard_map/ppermute | solution.py:367
  60.0 1.9 %collective-permute-start.24 = (bf16[32,2048]{1,0:T(8,128)(2,1)S(1)}, bf16[32,2048]{1,0:T(8,128)(2,1)S(1)}, u32[]{:S(2)}, u32[]{:S(2)}) collective-permute-start(bf16[32,2048]{1,0:T(8,128)(2,1)S(1)} %get-tuple-element.85), channel_id=1, source_target_pairs={{0,4},{1,5},{2,6},{3,7},{4,0},{5,1},{6,2},{7,3},{8,12},{9,13},{10,... | collective-permute-start | bytes 393224 | tf_op jit(solution)/shard_map/ppermute | solution.py:367
  63.7 2.7 %collective-permute-start.18 = (bf16[32,2176]{1,0:T(8,128)(2,1)S(1)}, bf16[32,2176]{1,0:T(8,128)(2,1)S(1)}, u32[]{:S(2)}, u32[]{:S(2)}) collective-permute-start(bf16[32,2176]{1,0:T(8,128)(2,1)S(1)} %get-tuple-element.78), channel_id=1, source_target_pairs={{0,24},{8,16},{16,8},{24,0},{1,25},{9,17},{17,9},{25,1},{2,26},{10... | collective-permute-start | bytes 417800 | tf_op jit(solution)/shard_map/ppermute | solution.py:370
  67.2 1.4 %collective-permute-done.24.refs_3_ = bf16[32,2048]{1,0:T(8,128)(2,1)S(1)} collective-permute-done((bf16[32,2048]{1,0:T(8,128)(2,1)S(1)}, bf16[32,2048]{1,0:T(8,128)(2,1)S(1)}, u32[]{:S(2)}, u32[]{:S(2)}) %collective-permute-start.24) | collective-permute-done | bytes 131104 | tf_op jit(solution)/shard_map/ppermute | solution.py:367
  68.5 1.4 %collective-permute-done.25.refs_4_ = bf16[32,2048]{1,0:T(8,128)(2,1)S(1)} collective-permute-done((bf16[32,2048]{1,0:T(8,128)(2,1)S(1)}, bf16[32,2048]{1,0:T(8,128)(2,1)S(1)}, u32[]{:S(2)}, u32[]{:S(2)}) %collective-permute-start.25) | collective-permute-done | bytes 131104 | tf_op jit(solution)/shard_map/ppermute | solution.py:367
  71.5 5.6 %collective-permute-done.22.refs_1_ = bf16[32,2176]{1,0:T(8,128)(2,1)S(1)} collective-permute-done((bf16[32,2176]{1,0:T(8,128)(2,1)S(1)}, bf16[32,2176]{1,0:T(8,128)(2,1)S(1)}, u32[]{:S(2)}, u32[]{:S(2)}) %collective-permute-start.22) | collective-permute-done | bytes 139296 | tf_op jit(solution)/shard_map/ppermute | solution.py:370
  78.2 1.5 %collective-permute-start.29 = (bf16[32,2048]{1,0:T(8,128)(2,1)S(1)}, bf16[32,2048]{1,0:T(8,128)(2,1)S(1)}, u32[]{:S(2)}, u32[]{:S(2)}) collective-permute-start(bf16[32,2048]{1,0:T(8,128)(2,1)S(1)} %get-tuple-element.87.refs_0_), channel_id=1, source_target_pairs={{0,6},{1,7},{2,4},{3,5},{4,2},{5,3},{6,0},{7,1},{8,14},{9,15},{10,... | collective-permute-start | bytes 393224 | tf_op jit(solution)/shard_map/ppermute | solution.py:367
  79.7 1.5 %collective-permute-start.28 = (bf16[32,2048]{1,0:T(8,128)(2,1)S(1)}, bf16[32,2048]{1,0:T(8,128)(2,1)S(1)}, u32[]{:S(2)}, u32[]{:S(2)}) collective-permute-start(bf16[32,2048]{1,0:T(8,128)(2,1)S(1)} %get-tuple-element.87.refs_0_), channel_id=1, source_target_pairs={{0,4},{1,5},{2,6},{3,7},{4,0},{5,1},{6,2},{7,3},{8,12},{9,13},{10,... | collective-permute-start | bytes 393224 | tf_op jit(solution)/shard_map/ppermute | solution.py:367
  82.3 2.6 %collective-permute-done.29.refs_3_ = bf16[32,2048]{1,0:T(8,128)(2,1)S(1)} collective-permute-done((bf16[32,2048]{1,0:T(8,128)(2,1)S(1)}, bf16[32,2048]{1,0:T(8,128)(2,1)S(1)}, u32[]{:S(2)}, u32[]{:S(2)}) %collective-permute-start.29) | collective-permute-done | bytes 131104 | tf_op jit(solution)/shard_map/ppermute | solution.py:367
  86.5 1.5 %collective-permute-start.37 = (bf16[64,128]{1,0:T(8,128)(2,1)S(1)}, bf16[64,128]{1,0:T(8,128)(2,1)S(1)}, u32[]{:S(2)}, u32[]{:S(2)}) collective-permute-start(bf16[64,128]{1,0:T(8,128)(2,1)S(1)} %constant_dynamic-update-slice_fusion.refs_0_), channel_id=1, source_target_pairs={{0,6},{1,7},{2,4},{3,5},{4,2},{5,3},{6,0},{7,1},{8,14},{9,15},{10,... | collective-permute-start | bytes 49160 | tf_op jit(solution)/shard_map/ppermute | solution.py:367
  88.0 3.2 %collective-permute-done.37.refs_3_ = bf16[64,128]{1,0:T(8,128)(2,1)S(1)} collective-permute-done((bf16[64,128]{1,0:T(8,128)(2,1)S(1)}, bf16[64,128]{1,0:T(8,128)(2,1)S(1)}, u32[]{:S(2)}, u32[]{:S(2)}) %collective-permute-start.37) | collective-permute-done | bytes 16416 | tf_op jit(solution)/shard_map/ppermute | solution.py:367
  92.2 2.7 %collective-permute-done.36.refs_2_ = bf16[64,128]{1,0:T(8,128)(2,1)S(1)} collective-permute-done((bf16[64,128]{1,0:T(8,128)(2,1)S(1)}, bf16[64,128]{1,0:T(8,128)(2,1)S(1)}, u32[]{:S(2)}, u32[]{:S(2)}) %collective-permute-start.36) | collective-permute-done | bytes 16416 | tf_op jit(solution)/shard_map/ppermute | solution.py:367
  96.2 2.4 %collective-permute-done.35.refs_1_ = bf16[64,128]{1,0:T(8,128)(2,1)S(1)} collective-permute-done((bf16[64,128]{1,0:T(8,128)(2,1)S(1)}, bf16[64,128]{1,0:T(8,128)(2,1)S(1)}, u32[]{:S(2)}, u32[]{:S(2)}) %collective-permute-start.35) | collective-permute-done | bytes 16416 | tf_op jit(solution)/shard_map/ppermute | solution.py:367
  98.7 6.4 %gradients.1 = (bf16[1,2048,768]{2,1,0:T(8,128)(2,1)}, bf16[1,384,2048]{2,1,0:T(8,128)(2,1)}) custom-call(bf16[64,128]{1,0:T(8,128)(2,1)S(1)} %constant_dynamic-update-slice_fusion.refs_0_, bf16[64,128]{1,0:T(8,128)(2,1)S(1)} %collective-permute-done.35.refs_1_, bf16[64,128]{1,0:T(8,128)(2,1)S(1)} %collective-permute-done.36.refs_2_, ...), custom_call_target="tpu_custom_call" | custom-call | flops 100663296 | bytes 7340032 | tf_op jit(solution)/shard_map/gradients/pallas_call | solution.py:557
  105.0 1.6 %gather.1 = bf16[256,2048]{1,0:T(8,128)(2,1)} custom-call(s32[3]{0:T(128)S(1)} %pad_add_fusion.place.refs_0_.refs_6_, bf16[32,2048]{1,0:T(8,128)(2,1)S(1)} %get-tuple-element.87.refs_0_, bf16[32,2048]{1,0:T(8,128)(2,1)S(1)} %collective-permute-done.27.refs_1_, bf16[32,2048]{1,0:T(8,128)(2,1)S(1)} %collective-permute-done.28.refs_2_, ...), custom_call_target="tpu_custom_call" | custom-call | bytes 2097152 | tf_op jit(solution)/shard_map/gather/pallas_call | solution.py:545
  (69 shorter events, 19.4 us)
Async XLA Ops:
  0.6 10.3 %collective-permute-start.3 = (bf16[1,2048,768]{2,1,0:T(8,128)(2,1)}, bf16[1,2048,768]{2,1,0:T(8,128)(2,1)}, u32[]{:S(2)}, u32[]{:S(2)}) collective-permute-start(bf16[1,2048,768]{2,1,0:T(8,128)(2,1)} %refs_7_.1), channel_id=1, source_target_pairs={{0,1},{1,0},{2,3},{3,2},{4,5},{5,4},{6,7},{7,6},{8,9},{9,8},{10,11... | collective-permute-start | bytes 9437192 | tf_op jit(solution)/shard_map/ppermute | solution.py:367
  1.2 9.7 %collective-permute-start.4 = (bf16[1,384,2048]{2,1,0:T(8,128)(2,1)}, bf16[1,384,2048]{2,1,0:T(8,128)(2,1)S(1)}, u32[]{:S(2)}, u32[]{:S(2)}) collective-permute-start(bf16[1,384,2048]{2,1,0:T(8,128)(2,1)} %refs_10_.1), channel_id=1, source_target_pairs={{0,1},{1,0},{2,3},{3,2},{4,5},{5,4},{6,7},{7,6},{8,9},{9,8},{10,11... | collective-permute-start | bytes 4718600 | tf_op jit(solution)/shard_map/ppermute | solution.py:367
  3.6 7.3 %collective-permute-start = (bf16[32,2176]{1,0:T(8,128)(2,1)}, bf16[32,2176]{1,0:T(8,128)(2,1)S(1)}, u32[]{:S(2)}, u32[]{:S(2)}) collective-permute-start(bf16[32,2176]{1,0:T(8,128)(2,1)} %pack.1.refs_0_), channel_id=1, source_target_pairs={{0,8},{8,0},{16,24},{24,16},{1,9},{9,1},{17,25},{25,17},{2,10},{10... | collective-permute-start | bytes 417800 | tf_op jit(solution)/shard_map/ppermute | solution.py:370
  6.6 10.3 %collective-permute-start.2 = (bf16[32,2176]{1,0:T(8,128)(2,1)}, bf16[32,2176]{1,0:T(8,128)(2,1)S(1)}, u32[]{:S(2)}, u32[]{:S(2)}) collective-permute-start(bf16[32,2176]{1,0:T(8,128)(2,1)} %pack.1.refs_0_), channel_id=1, source_target_pairs={{0,24},{8,16},{16,8},{24,0},{1,25},{9,17},{17,9},{25,1},{2,26},{10... | collective-permute-start | bytes 417800 | tf_op jit(solution)/shard_map/ppermute | solution.py:370
  9.1 13.1 %collective-permute-start.1 = (bf16[32,2176]{1,0:T(8,128)(2,1)}, bf16[32,2176]{1,0:T(8,128)(2,1)}, u32[]{:S(2)}, u32[]{:S(2)}) collective-permute-start(bf16[32,2176]{1,0:T(8,128)(2,1)} %pack.1.refs_0_), channel_id=1, source_target_pairs={{0,16},{8,24},{16,0},{24,8},{1,17},{9,25},{17,1},{25,9},{2,18},{10... | collective-permute-start | bytes 417800 | tf_op jit(solution)/shard_map/ppermute | solution.py:370
  10.9 12.2 %collective-permute-start.7 = (bf16[32,2304]{1,0:T(8,128)(2,1)S(1)}, bf16[32,2304]{1,0:T(8,128)(2,1)S(1)}, u32[]{:S(2)}, u32[]{:S(2)}) collective-permute-start(bf16[32,2304]{1,0:T(8,128)(2,1)S(1)} %pad_maximum_fusion.1), channel_id=1, source_target_pairs={{0,6},{1,7},{2,4},{3,5},{4,2},{5,3},{6,0},{7,1},{8,14},{9,15},{10,... | collective-permute-start | bytes 442376 | tf_op jit(solution)/shard_map/ppermute | solution.py:367
  13.5 9.6 %collective-permute-start.6 = (bf16[32,2304]{1,0:T(8,128)(2,1)S(1)}, bf16[32,2304]{1,0:T(8,128)(2,1)S(1)}, u32[]{:S(2)}, u32[]{:S(2)}) collective-permute-start(bf16[32,2304]{1,0:T(8,128)(2,1)S(1)} %pad_maximum_fusion.1), channel_id=1, source_target_pairs={{0,4},{1,5},{2,6},{3,7},{4,0},{5,1},{6,2},{7,3},{8,12},{9,13},{10,... | collective-permute-start | bytes 442376 | tf_op jit(solution)/shard_map/ppermute | solution.py:367
  14.0 9.1 %collective-permute-start.5 = (bf16[32,2304]{1,0:T(8,128)(2,1)S(1)}, bf16[32,2304]{1,0:T(8,128)(2,1)S(1)}, u32[]{:S(2)}, u32[]{:S(2)}) collective-permute-start(bf16[32,2304]{1,0:T(8,128)(2,1)S(1)} %pad_maximum_fusion.1), channel_id=1, source_target_pairs={{0,2},{1,3},{2,0},{3,1},{4,6},{5,7},{6,4},{7,5},{8,10},{9,11},{10,... | collective-permute-start | bytes 442376 | tf_op jit(solution)/shard_map/ppermute | solution.py:367
  23.1 14.7 %collective-permute-start.10 = (bf16[64,2176]{1,0:T(8,128)(2,1)S(1)}, bf16[64,2176]{1,0:T(8,128)(2,1)S(1)}, u32[]{:S(2)}, u32[]{:S(2)}) collective-permute-start(bf16[64,2176]{1,0:T(8,128)(2,1)S(1)} %pad_maximum_fusion), channel_id=1, source_target_pairs={{0,6},{1,7},{2,4},{3,5},{4,2},{5,3},{6,0},{7,1},{8,14},{9,15},{10,... | collective-permute-start | bytes 835592 | tf_op jit(solution)/shard_map/ppermute | solution.py:367
  25.6 12.7 %collective-permute-start.9 = (bf16[64,2176]{1,0:T(8,128)(2,1)S(1)}, bf16[64,2176]{1,0:T(8,128)(2,1)S(1)}, u32[]{:S(2)}, u32[]{:S(2)}) collective-permute-start(bf16[64,2176]{1,0:T(8,128)(2,1)S(1)} %pad_maximum_fusion), channel_id=1, source_target_pairs={{0,4},{1,5},{2,6},{3,7},{4,0},{5,1},{6,2},{7,3},{8,12},{9,13},{10,... | collective-permute-start | bytes 835592 | tf_op jit(solution)/shard_map/ppermute | solution.py:367
  26.1 13.6 %collective-permute-start.8 = (bf16[64,2176]{1,0:T(8,128)(2,1)S(1)}, bf16[64,2176]{1,0:T(8,128)(2,1)S(1)}, u32[]{:S(2)}, u32[]{:S(2)}) collective-permute-start(bf16[64,2176]{1,0:T(8,128)(2,1)S(1)} %pad_maximum_fusion), channel_id=1, source_target_pairs={{0,2},{1,3},{2,0},{3,1},{4,6},{5,7},{6,4},{7,5},{8,10},{9,11},{10,... | collective-permute-start | bytes 835592 | tf_op jit(solution)/shard_map/ppermute | solution.py:367
  34.8 11.6 %collective-permute-start.12 = (bf16[32,2048]{1,0:T(8,128)(2,1)S(1)}, bf16[32,2048]{1,0:T(8,128)(2,1)S(1)}, u32[]{:S(2)}, u32[]{:S(2)}) collective-permute-start(bf16[32,2048]{1,0:T(8,128)(2,1)S(1)} %get-tuple-element.65), channel_id=1, source_target_pairs={{0,2},{1,3},{2,0},{3,1},{4,6},{5,7},{6,4},{7,5},{8,10},{9,11},{10,... | collective-permute-start | bytes 393224 | tf_op jit(solution)/shard_map/ppermute | solution.py:367
  36.3 10.1 %collective-permute-start.13 = (bf16[32,2048]{1,0:T(8,128)(2,1)S(1)}, bf16[32,2048]{1,0:T(8,128)(2,1)S(1)}, u32[]{:S(2)}, u32[]{:S(2)}) collective-permute-start(bf16[32,2048]{1,0:T(8,128)(2,1)S(1)} %get-tuple-element.66), channel_id=1, source_target_pairs={{0,4},{1,5},{2,6},{3,7},{4,0},{5,1},{6,2},{7,3},{8,12},{9,13},{10,... | collective-permute-start | bytes 393224 | tf_op jit(solution)/shard_map/ppermute | solution.py:367
  37.8 8.6 %collective-permute-start.14 = (bf16[32,2048]{1,0:T(8,128)(2,1)S(1)}, bf16[32,2048]{1,0:T(8,128)(2,1)S(1)}, u32[]{:S(2)}, u32[]{:S(2)}) collective-permute-start(bf16[32,2048]{1,0:T(8,128)(2,1)S(1)} %get-tuple-element.67), channel_id=1, source_target_pairs={{0,6},{1,7},{2,4},{3,5},{4,2},{5,3},{6,0},{7,1},{8,14},{9,15},{10,... | collective-permute-start | bytes 393224 | tf_op jit(solution)/shard_map/ppermute | solution.py:367
  46.5 13.0 %collective-permute-start.15 = (bf16[32,2176]{1,0:T(8,128)(2,1)S(1)}, bf16[32,2176]{1,0:T(8,128)(2,1)S(1)}, u32[]{:S(2)}, u32[]{:S(2)}) collective-permute-start(bf16[32,2176]{1,0:T(8,128)(2,1)S(1)} %get-tuple-element.74), channel_id=1, source_target_pairs={{0,2},{1,3},{2,0},{3,1},{4,6},{5,7},{6,4},{7,5},{8,10},{9,11},{10,... | collective-permute-start | bytes 417800 | tf_op jit(solution)/shard_map/ppermute | solution.py:367
  48.0 12.0 %collective-permute-start.16 = (bf16[32,2176]{1,0:T(8,128)(2,1)S(1)}, bf16[32,2176]{1,0:T(8,128)(2,1)S(1)}, u32[]{:S(2)}, u32[]{:S(2)}) collective-permute-start(bf16[32,2176]{1,0:T(8,128)(2,1)S(1)} %get-tuple-element.75), channel_id=1, source_target_pairs={{0,4},{1,5},{2,6},{3,7},{4,0},{5,1},{6,2},{7,3},{8,12},{9,13},{10,... | collective-permute-start | bytes 417800 | tf_op jit(solution)/shard_map/ppermute | solution.py:367
  48.1 13.8 %collective-permute-start.17 = (bf16[32,2176]{1,0:T(8,128)(2,1)S(1)}, bf16[32,2176]{1,0:T(8,128)(2,1)S(1)}, u32[]{:S(2)}, u32[]{:S(2)}) collective-permute-start(bf16[32,2176]{1,0:T(8,128)(2,1)S(1)} %get-tuple-element.76), channel_id=1, source_target_pairs={{0,6},{1,7},{2,4},{3,5},{4,2},{5,3},{6,0},{7,1},{8,14},{9,15},{10,... | collective-permute-start | bytes 417800 | tf_op jit(solution)/shard_map/ppermute | solution.py:367
  50.0 8.4 %collective-permute-start.19 = (bf16[32,2048]{1,0:T(8,128)(2,1)S(1)}, bf16[32,2048]{1,0:T(8,128)(2,1)S(1)}, u32[]{:S(2)}, u32[]{:S(2)}) collective-permute-start(bf16[32,2048]{1,0:T(8,128)(2,1)S(1)} %get-tuple-element.80), channel_id=1, source_target_pairs={{0,2},{1,3},{2,0},{3,1},{4,6},{5,7},{6,4},{7,5},{8,10},{9,11},{10,... | collective-permute-start | bytes 393224 | tf_op jit(solution)/shard_map/ppermute | solution.py:367
  51.5 12.2 %collective-permute-start.20 = (bf16[32,2048]{1,0:T(8,128)(2,1)S(1)}, bf16[32,2048]{1,0:T(8,128)(2,1)S(1)}, u32[]{:S(2)}, u32[]{:S(2)}) collective-permute-start(bf16[32,2048]{1,0:T(8,128)(2,1)S(1)} %get-tuple-element.81), channel_id=1, source_target_pairs={{0,4},{1,5},{2,6},{3,7},{4,0},{5,1},{6,2},{7,3},{8,12},{9,13},{10,... | collective-permute-start | bytes 393224 | tf_op jit(solution)/shard_map/ppermute | solution.py:367
  58.4 7.9 %collective-permute-start.21 = (bf16[32,2048]{1,0:T(8,128)(2,1)S(1)}, bf16[32,2048]{1,0:T(8,128)(2,1)S(1)}, u32[]{:S(2)}, u32[]{:S(2)}) collective-permute-start(bf16[32,2048]{1,0:T(8,128)(2,1)S(1)} %get-tuple-element.82), channel_id=1, source_target_pairs={{0,6},{1,7},{2,4},{3,5},{4,2},{5,3},{6,0},{7,1},{8,14},{9,15},{10,... | collective-permute-start | bytes 393224 | tf_op jit(solution)/shard_map/ppermute | solution.py:367
  59.4 7.7 %collective-permute-start.23 = (bf16[32,2048]{1,0:T(8,128)(2,1)S(1)}, bf16[32,2048]{1,0:T(8,128)(2,1)S(1)}, u32[]{:S(2)}, u32[]{:S(2)}) collective-permute-start(bf16[32,2048]{1,0:T(8,128)(2,1)S(1)} %get-tuple-element.84), channel_id=1, source_target_pairs={{0,2},{1,3},{2,0},{3,1},{4,6},{5,7},{6,4},{7,5},{8,10},{9,11},{10,... | collective-permute-start | bytes 393224 | tf_op jit(solution)/shard_map/ppermute | solution.py:367
  60.0 8.5 %collective-permute-start.24 = (bf16[32,2048]{1,0:T(8,128)(2,1)S(1)}, bf16[32,2048]{1,0:T(8,128)(2,1)S(1)}, u32[]{:S(2)}, u32[]{:S(2)}) collective-permute-start(bf16[32,2048]{1,0:T(8,128)(2,1)S(1)} %get-tuple-element.85), channel_id=1, source_target_pairs={{0,4},{1,5},{2,6},{3,7},{4,0},{5,1},{6,2},{7,3},{8,12},{9,13},{10,... | collective-permute-start | bytes 393224 | tf_op jit(solution)/shard_map/ppermute | solution.py:367
  61.9 8.1 %collective-permute-start.25 = (bf16[32,2048]{1,0:T(8,128)(2,1)S(1)}, bf16[32,2048]{1,0:T(8,128)(2,1)S(1)}, u32[]{:S(2)}, u32[]{:S(2)}) collective-permute-start(bf16[32,2048]{1,0:T(8,128)(2,1)S(1)} %get-tuple-element.86), channel_id=1, source_target_pairs={{0,6},{1,7},{2,4},{3,5},{4,2},{5,3},{6,0},{7,1},{8,14},{9,15},{10,... | collective-permute-start | bytes 393224 | tf_op jit(solution)/shard_map/ppermute | solution.py:367
  63.7 7.8 %collective-permute-start.18 = (bf16[32,2176]{1,0:T(8,128)(2,1)S(1)}, bf16[32,2176]{1,0:T(8,128)(2,1)S(1)}, u32[]{:S(2)}, u32[]{:S(2)}) collective-permute-start(bf16[32,2176]{1,0:T(8,128)(2,1)S(1)} %get-tuple-element.78), channel_id=1, source_target_pairs={{0,24},{8,16},{16,8},{24,0},{1,25},{9,17},{17,9},{25,1},{2,26},{10... | collective-permute-start | bytes 417800 | tf_op jit(solution)/shard_map/ppermute | solution.py:370
  67.1 10.0 %collective-permute-start.22 = (bf16[32,2176]{1,0:T(8,128)(2,1)S(1)}, bf16[32,2176]{1,0:T(8,128)(2,1)S(1)}, u32[]{:S(2)}, u32[]{:S(2)}) collective-permute-start(bf16[32,2176]{1,0:T(8,128)(2,1)S(1)} %combine.6), channel_id=1, source_target_pairs={{0,16},{8,24},{16,0},{24,8},{1,17},{9,25},{17,1},{25,9},{2,18},{10... | collective-permute-start | bytes 417800 | tf_op jit(solution)/shard_map/ppermute | solution.py:370
  70.7 7.5 %collective-permute-start.26 = (bf16[32,2176]{1,0:T(8,128)(2,1)S(1)}, bf16[32,2176]{1,0:T(8,128)(2,1)S(1)}, u32[]{:S(2)}, u32[]{:S(2)}) collective-permute-start(bf16[32,2176]{1,0:T(8,128)(2,1)S(1)} %combine.7), channel_id=1, source_target_pairs={{0,8},{8,0},{16,24},{24,16},{1,9},{9,1},{17,25},{25,17},{2,10},{10... | collective-permute-start | bytes 417800 | tf_op jit(solution)/shard_map/ppermute | solution.py:370
  78.2 6.6 %collective-permute-start.29 = (bf16[32,2048]{1,0:T(8,128)(2,1)S(1)}, bf16[32,2048]{1,0:T(8,128)(2,1)S(1)}, u32[]{:S(2)}, u32[]{:S(2)}) collective-permute-start(bf16[32,2048]{1,0:T(8,128)(2,1)S(1)} %get-tuple-element.87.refs_0_), channel_id=1, source_target_pairs={{0,6},{1,7},{2,4},{3,5},{4,2},{5,3},{6,0},{7,1},{8,14},{9,15},{10,... | collective-permute-start | bytes 393224 | tf_op jit(solution)/shard_map/ppermute | solution.py:367
  79.7 6.1 %collective-permute-start.28 = (bf16[32,2048]{1,0:T(8,128)(2,1)S(1)}, bf16[32,2048]{1,0:T(8,128)(2,1)S(1)}, u32[]{:S(2)}, u32[]{:S(2)}) collective-permute-start(bf16[32,2048]{1,0:T(8,128)(2,1)S(1)} %get-tuple-element.87.refs_0_), channel_id=1, source_target_pairs={{0,4},{1,5},{2,6},{3,7},{4,0},{5,1},{6,2},{7,3},{8,12},{9,13},{10,... | collective-permute-start | bytes 393224 | tf_op jit(solution)/shard_map/ppermute | solution.py:367
  81.8 23.2 %collective-permute-start.30 = (bf16[32,2048]{1,0:T(8,128)(2,1)S(1)}, bf16[32,2048]{1,0:T(8,128)(2,1)S(1)}, u32[]{:S(2)}, u32[]{:S(2)}) collective-permute-start(bf16[32,2048]{1,0:T(8,128)(2,1)S(1)} %get-tuple-element.87.refs_0_), channel_id=1, source_target_pairs={{0,1},{1,0},{2,3},{3,2},{4,5},{5,4},{6,7},{7,6},{8,9},{9,8},{10,11... | collective-permute-start | bytes 393224 | tf_op jit(solution)/shard_map/ppermute | solution.py:367
  84.9 20.1 %collective-permute-start.33 = (bf16[32,2048]{1,0:T(8,128)(2,1)S(1)}, bf16[32,2048]{1,0:T(8,128)(2,1)S(1)}, u32[]{:S(2)}, u32[]{:S(2)}) collective-permute-start(bf16[32,2048]{1,0:T(8,128)(2,1)S(1)} %collective-permute-done.29.refs_3_), channel_id=1, source_target_pairs={{0,1},{1,0},{2,3},{3,2},{4,5},{5,4},{6,7},{7,6},{8,9},{9,8},{10,11... | collective-permute-start | bytes 393224 | tf_op jit(solution)/shard_map/ppermute | solution.py:367
  85.8 19.2 %collective-permute-start.32 = (bf16[32,2048]{1,0:T(8,128)(2,1)S(1)}, bf16[32,2048]{1,0:T(8,128)(2,1)S(1)}, u32[]{:S(2)}, u32[]{:S(2)}) collective-permute-start(bf16[32,2048]{1,0:T(8,128)(2,1)S(1)} %collective-permute-done.28.refs_2_), channel_id=1, source_target_pairs={{0,1},{1,0},{2,3},{3,2},{4,5},{5,4},{6,7},{7,6},{8,9},{9,8},{10,11... | collective-permute-start | bytes 393224 | tf_op jit(solution)/shard_map/ppermute | solution.py:367
  86.5 18.6 %collective-permute-start.31 = (bf16[32,2048]{1,0:T(8,128)(2,1)S(1)}, bf16[32,2048]{1,0:T(8,128)(2,1)S(1)}, u32[]{:S(2)}, u32[]{:S(2)}) collective-permute-start(bf16[32,2048]{1,0:T(8,128)(2,1)S(1)} %collective-permute-done.27.refs_1_), channel_id=1, source_target_pairs={{0,1},{1,0},{2,3},{3,2},{4,5},{5,4},{6,7},{7,6},{8,9},{9,8},{10,11... | collective-permute-start | bytes 393224 | tf_op jit(solution)/shard_map/ppermute | solution.py:367
  (10 other events, 66.5 us)

commit v8 on v6

--- a/solution.py
+++ b/solution.py
@@ -276,65 +276,67 @@
     out[:, width:] = (own_last[...] + last).astype(bf16)
 
 
-def gather_kernel(chips, each, place, *refs):
-    pieces, (out, last_rows, by_lane) = refs[: 2 * chips], refs[2 * chips :]
+def gather_rows(lane, pieces, out, by_lane, each):
     part_rows, width = pieces[0].shape[0], out.shape[1]
     chunks = width // lanes
-    for index in range(2 * chips):
-        lane = place[1] ^ (2 * (index % chips)) ^ (index // chips)
-        piece = pieces[index]
-        start = pl.multiple_of(lane * part_rows, part_rows)
-        out[pl.ds(start, part_rows), :] = piece[:, :width]
-        values = piece[:, width:].astype(f32)
+    count = len(pieces)
+    for index in range(count):
+        source = lane ^ (2 * (index % (count // 2))) ^ (index // (count // 2))
+        start = pl.multiple_of(source * part_rows, part_rows)
+        out[pl.ds(start, part_rows), :] = pieces[index][:, :width]
+        values = pieces[index][:, width:].astype(f32)
         for spot in range(each * chunks):
             row, chunk = spot // chunks, spot % chunks
             at = spot // part_rows * lanes
             from_row = spot % part_rows
-            by_lane[lane, row : row + 1, chunk * lanes : (chunk + 1) * lanes] = values[
+            by_lane[source, row : row + 1, chunk * lanes : (chunk + 1) * lanes] = values[
                 from_row : from_row + 1, at : at + lanes
             ]
-    ordered = [by_lane[lane, 0:each, :] for lane in range(2 * chips)]
-    last_rows[...] = jnp.concatenate(ordered, axis=0).astype(bf16)
-
-
-def gradient_kernel(
-    last_block,
-    layer_last,
-    projected,
-    place,
-    kept,
-    found,
-    partners,
-    down,
-    grad_in,
-    grad_out,
-    route,
-    hidden,
-    slope,
-):
+    return jnp.concatenate([by_lane[index, 0:each, :] for index in range(count)], axis=0)
+
+
+def both_ways(coefficient, unit, diagonal):
+    count = unit.shape[0]
+    if count > 32:
+        high = lax.Precision.HIGHEST
+        there = dot(coefficient, unit, ((1,), (0,)), high)
+        return there + dot(coefficient, unit, ((0,), (0,)), high)
+    total = None
+    for index in range(count):
+        line = jnp.where(diagonal, coefficient[index : index + 1, :], 0.0)
+        factor = coefficient[:, index : index + 1] + jnp.sum(line, axis=1, keepdims=True)
+        term = factor * unit[index : index + 1, :]
+        total = term if total is None else total + term
+    return total
+
+
+def final_kernel(n_pieces, *refs):
+    pieces, refs = refs[:n_pieces], refs[n_pieces:]
+    last_block, projected, place, kept, found, partners, down, *refs = refs
+    layer_out, grad_in, grad_out, route, hidden, slope, by_lane = refs
     step = pl.program_id(0)
     half_width = down.shape[1]
     block = grad_out.shape[2]
 
     @pl.when(step == 0)
     def _():
-        values = layer_last[...].astype(f32)
+        each = projected.shape[0] // by_lane.shape[0]
+        values = gather_rows(place[1], pieces, layer_out, by_lane, each)
         count = values.shape[0]
         last = kept.shape[0] - count
         table = kept[last:, :].astype(f32) + found[last:, :].astype(f32)
-        norms = jnp.sqrt(jnp.sum(values * values, axis=1, keepdims=True) + epsilon)
-        unit = values / norms
-        scores = dot(unit, unit, ((1,), (1,)), lax.Precision.HIGHEST) / logit_divisor
         row = lax.broadcasted_iota(jnp.int32, (count, count), 0)
         col = lax.broadcasted_iota(jnp.int32, (count, count), 1)
+        norms = jnp.sqrt(jnp.sum(values * values, axis=1, keepdims=True) + epsilon)
+        norms_line = jnp.sum(jnp.where(row == col, norms, 0.0), axis=0, keepdims=True)
+        unit = values / norms
+        rows = values.astype(bf16)
+        scores = dot(rows, rows, ((1,), (1,))) / (norms * norms_line) / logit_divisor
         exp_scores = jnp.where(row != col, jnp.exp(scores), 0.0)
         probabilities = exp_scores / jnp.sum(exp_scores, axis=1, keepdims=True)
         partner = partners[:, :1].astype(jnp.int32)
         coefficient = grad_scale * (probabilities - jnp.where(col == partner, 1.0, 0.0))
-        high = lax.Precision.HIGHEST
-        grad_unit = (
-            dot(coefficient, unit, ((1,), (0,)), high) + dot(coefficient, unit, ((0,), (0,)), high)
-        ) / logit_divisor
+        grad_unit = both_ways(coefficient, unit, row == col) / logit_divisor
         projection = jnp.sum(unit * grad_unit, axis=1, keepdims=True)
         grad_last = (grad_unit - unit * projection) / norms
         route_grad = (column(table, place[2]) * grad_last).astype(bf16)
@@ -515,11 +517,19 @@
     last_projected, own_last = out[-2:]
 
     returned = {}
-    for hop in range(dp_count - 1, -1, -1):
-        first, *sent_back = outs[hop]
-        if hop == dp_count - 1:
-            sent_back, found = lax.optimization_barrier((sent_back, found))
-        returned[hop] = [first] + [to_lane(value, step) for value, step in zip(sent_back, chip_steps)]
+
+    def send_back(hop, after):
+        first, *parts = outs[hop]
+        parts, after = lax.optimization_barrier((parts, after))
+        returned[hop] = [first] + [to_lane(value, step) for value, step in zip(parts, chip_steps)]
+        return after
+
+    send_back(0, [])
+    send_back(1, [])
+    before = 1
+    for hop in range(dp_count - 1, 1, -1):
+        returned[before][1:], found = send_back(hop, (returned[before][1:], found))
+        before = hop
     homeward = []
     last_sum = None
     for hop in range(dp_count - 1, 0, -1):
@@ -539,32 +549,20 @@
     )(near_sum, own_last, last_sum, *homeward)
     pieces = [own_out] + [to_lane(own_out, step) for step in chip_steps]
     pieces += [to_lane(piece, 1) for piece in pieces]
-    layer_out, layer_last = pl.pallas_call(
-        functools.partial(gather_kernel, chips, each),
+
+    block = min(512, width)
+    steps = width // block
+    layer_out, grad_gate_up, grad_down = pl.pallas_call(
+        functools.partial(final_kernel, len(pieces)),
+        grid=(steps,),
         out_shape=[
             jax.ShapeDtypeStruct((tok_dev, width), bf16),
-            jax.ShapeDtypeStruct((seqs, width), bf16),
-        ],
-        in_specs=[in_smem] + [in_vmem] * len(pieces),
-        out_specs=[in_vmem] * 2,
-        scratch_shapes=[pltpu.VMEM((expert_count, -(-each // 8) * 8, width), f32)],
-        compiler_params=params(8),
-        cost_estimate=cost(0, 2 << 20),
-        name="gather",
-    )(place, *pieces)
-
-    block = min(512, width)
-    steps = width // block
-    grad_gate_up, grad_down = pl.pallas_call(
-        gradient_kernel,
-        grid=(steps,),
-        out_shape=[
             jax.ShapeDtypeStruct(gate_up.shape, bf16),
             jax.ShapeDtypeStruct(down.shape, bf16),
         ],
         in_specs=[
+            *[pl.BlockSpec((part_rows, width + extra), lambda step: (0, 0))] * len(pieces),
             pl.BlockSpec((seqs, block), lambda step: (0, step)),
-            pl.BlockSpec((seqs, width), lambda step: (0, 0)),
             pl.BlockSpec((seqs, 2 * half_width), lambda step: (0, 0)),
             in_smem,
             pl.BlockSpec((table_rows, lanes), lambda step: (0, 0)),
@@ -573,6 +571,7 @@
             pl.BlockSpec((1, half_width, width), lambda step: (0, 0, 0)),
         ],
         out_specs=[
+            pl.BlockSpec((tok_dev, width), lambda step: (0, 0)),
             pl.BlockSpec((1, block, 2 * half_width), lambda step: (0, step, 0)),
             pl.BlockSpec((1, half_width, block), lambda step: (0, 0, step)),
         ],
@@ -580,11 +579,12 @@
             pltpu.VMEM((steps, seqs, block), bf16),
             pltpu.VMEM((seqs, half_width), bf16),
             pltpu.VMEM((seqs, 2 * half_width), bf16),
+            pltpu.VMEM((expert_count, -(-each // 8) * 8, width), f32),
         ],
         compiler_params=params(24),
         cost_estimate=cost(2 * seqs * width * 4 * half_width, 7 << 20),
-        name="gradients",
-    )(last_all, layer_last, last_projected, place, kept, found, partners, down)
+        name="final",
+    )(*pieces, last_all, last_projected, place, kept, found, partners, down)
     return (layer_out, grad_gate_up, grad_down)
 
 

time: 98.3 us -> 90.6 us (0.922)
  waiting for transfers between devices: 31.3 us -> 27.1 us
  Pallas kernels: 24.7 us -> 22.3 us
  starting transfers between devices: 36.4 us -> 35.1 us
    ppermute x28, waiting for transfers between devices: 22.6 us -> 18.5 us  [to_lane(): lax.ppermute(value, 'expert', [(j, j ^ step) for j in range(expert_count)])]
    pallas_call x2 -> x1, Pallas kernels: 7.9 us -> 5.55 us  [body(): pl.pallas_call(functools.partial(final_kernel, len(pieces)), grid=(steps,...]
  transfers between devices with their start and end apart: 34 -> 34, of which waited for: 12 -> 14; matrix products, arithmetic and copies ran while one was open for 2% -> 2% of each run, Pallas kernels for 16% -> 18%
where the time goes in v8:
time: 90.6 us; the launch traced here: 90.3 us
  starting transfers between devices  35.1 us (39%)
  waiting for transfers between devices  27.1 us (30%)
  Pallas kernels  22.3 us (25%)
  local copies, waits for them, and re-layouts  3.85 us (4%)
  other arithmetic  1.01 us (1%)
    ppermute x28, starting transfers between devices, to_lane(): lax.ppermute(value, 'expert', [(j, j ^ step) for j in range(expert_count)])  25.7 us
    ppermute x28, waiting for transfers between devices, to_lane(): lax.ppermute(value, 'expert', [(j, j ^ step) for j in range(expert_count)])  18.5 us
    pallas_call x2, Pallas kernels, expert(): pl.pallas_call(functools.partial(expert_kernel, (tuple(group), chips, par...  10 us
    ppermute x6, starting transfers between devices, to_plane(): return lax.ppermute(value, 'dp', [(p, p ^ step) for p in range(dp_count)])  9.49 us
    ppermute x6, waiting for transfers between devices, to_plane(): return lax.ppermute(value, 'dp', [(p, p ^ step) for p in range(dp_count)])  8.62 us
    pallas_call x1, Pallas kernels, body(): pl.pallas_call(functools.partial(final_kernel, len(pieces)), grid=(steps,...  5.55 us
    unnamed x8, local copies, waits for them, and re-layouts  3.12 us
    pallas_call x4, Pallas kernels, combine(): pl.pallas_call(functools.partial(combine_kernel, (hop, chips, with_last,...  2.89 us
  transfers between devices with their start and end apart: 34, of which 14 were waited for; matrix products, arithmetic and copies ran while one was open for 2% of the time, Pallas kernels for 18%

profile of v8, /device:TPU:0, one launch (start us, length us, event | category | flops | bytes accessed | tf_op | source)
XLA Modules:
  0.0 90.3 jit_solution(6237147121895135156)
XLA Ops:
  1.2 2.3 %pack.1.refs_0_ = bf16[32,2176]{1,0:T(8,128)(2,1)} custom-call(s32[4]{0:T(128)} %positives.1, s32[1,256]{1,0:T(1,128)} %bitcast.5, f32[1,256]{1,0:T(1,128)} %bitcast.6, bf16[256,2048]{1,0:T(8,128)(2,1)} %refs_1_.1), custom_call_target="tpu_custom_call" | custom-call | bytes 524288 | tf_op jit(solution)/shard_map/pack/pallas_call | solution.py:382
  3.6 3.1 %collective-permute-start = (bf16[32,2176]{1,0:T(8,128)(2,1)}, bf16[32,2176]{1,0:T(8,128)(2,1)S(1)}, u32[]{:S(2)}, u32[]{:S(2)}) collective-permute-start(bf16[32,2176]{1,0:T(8,128)(2,1)} %pack.1.refs_0_), channel_id=1, source_target_pairs={{0,8},{8,0},{16,24},{24,16},{1,9},{9,1},{17,25},{25,17},{2,10},{10... | collective-permute-start | bytes 417800 | tf_op jit(solution)/shard_map/ppermute | solution.py:376
  6.6 2.5 %collective-permute-start.2 = (bf16[32,2176]{1,0:T(8,128)(2,1)}, bf16[32,2176]{1,0:T(8,128)(2,1)S(1)}, u32[]{:S(2)}, u32[]{:S(2)}) collective-permute-start(bf16[32,2176]{1,0:T(8,128)(2,1)} %pack.1.refs_0_), channel_id=1, source_target_pairs={{0,24},{8,16},{16,8},{24,0},{1,25},{9,17},{17,9},{25,1},{2,26},{10... | collective-permute-start | bytes 417800 | tf_op jit(solution)/shard_map/ppermute | solution.py:376
  10.9 2.6 %collective-permute-start.7 = (bf16[32,2304]{1,0:T(8,128)(2,1)S(1)}, bf16[32,2304]{1,0:T(8,128)(2,1)S(1)}, u32[]{:S(2)}, u32[]{:S(2)}) collective-permute-start(bf16[32,2304]{1,0:T(8,128)(2,1)S(1)} %pad_maximum_fusion.1), channel_id=1, source_target_pairs={{0,6},{1,7},{2,4},{3,5},{4,2},{5,3},{6,0},{7,1},{8,14},{9,15},{10,... | collective-permute-start | bytes 442376 | tf_op jit(solution)/shard_map/ppermute | solution.py:373
  14.5 2.4 %collective-permute-done.2.refs_6_.refs_3_ = bf16[32,2176]{1,0:T(8,128)(2,1)S(1)} collective-permute-done((bf16[32,2176]{1,0:T(8,128)(2,1)}, bf16[32,2176]{1,0:T(8,128)(2,1)S(1)}, u32[]{:S(2)}, u32[]{:S(2)}) %collective-permute-start.2) | collective-permute-done | bytes 139296 | tf_op jit(solution)/shard_map/ppermute | solution.py:376
  16.9 5.3 %collective-permute-done.1.refs_5_.refs_2_ = bf16[32,2176]{1,0:T(8,128)(2,1)} collective-permute-done((bf16[32,2176]{1,0:T(8,128)(2,1)}, bf16[32,2176]{1,0:T(8,128)(2,1)}, u32[]{:S(2)}, u32[]{:S(2)}) %collective-permute-start.1) | collective-permute-done | bytes 139296 | tf_op jit(solution)/shard_map/ppermute | solution.py:376
  23.1 2.5 %collective-permute-start.10 = (bf16[64,2176]{1,0:T(8,128)(2,1)S(1)}, bf16[64,2176]{1,0:T(8,128)(2,1)S(1)}, u32[]{:S(2)}, u32[]{:S(2)}) collective-permute-start(bf16[64,2176]{1,0:T(8,128)(2,1)S(1)} %pad_maximum_fusion), channel_id=1, source_target_pairs={{0,6},{1,7},{2,4},{3,5},{4,2},{5,3},{6,0},{7,1},{8,14},{9,15},{10,... | collective-permute-start | bytes 835592 | tf_op jit(solution)/shard_map/ppermute | solution.py:373
  26.8 1.9 %copy-done.1 = bf16[1,2048,768]{2,1,0:T(8,128)(2,1)S(1)} copy-done((bf16[1,2048,768]{2,1,0:T(8,128)(2,1)S(1)}, bf16[1,2048,768]{2,1,0:T(8,128)(2,1)}, u32[]{:S(2)}) %copy-start.1) | copy-done | bytes 3145752
  28.6 1.2 %copy-done.2 = bf16[256,2048]{1,0:T(8,128)(2,1)S(1)} copy-done((bf16[256,2048]{1,0:T(8,128)(2,1)S(1)}, bf16[256,2048]{1,0:T(8,128)(2,1)}, u32[]{:S(2)}) %copy-start.2) | copy-done | bytes 1048600
  29.9 4.9 %experts.2 = (bf16[32,2048]{1,0:T(8,128)(2,1)S(1)}, bf16[32,2048]{1,0:T(8,128)(2,1)S(1)}, bf16[32,2048]{1,0:T(8,128)(2,1)S(1)}, bf16[32,2048]{1,0:T(8,128)(2,1)S...) custom-call(s32[3]{0:T(128)S(1)} %pad_add_fusion.place.refs_0_.refs_, ...), custom_call_target="tpu_custom_call" | custom-call | flops 2415919104 | bytes 12582912 | tf_op jit(solution)/shard_map/experts/pallas_call | solution.py:477
  34.8 1.6 %collective-permute-start.11 = (bf16[32,2048]{1,0:T(8,128)(2,1)S(1)}, bf16[32,2048]{1,0:T(8,128)(2,1)S(1)}, u32[]{:S(2)}, u32[]{:S(2)}) collective-permute-start(bf16[32,2048]{1,0:T(8,128)(2,1)S(1)} %get-tuple-element.79), channel_id=1, source_target_pairs={{0,2},{1,3},{2,0},{3,1},{4,6},{5,7},{6,4},{7,5},{8,10},{9,11},{10,... | collective-permute-start | bytes 393224 | tf_op jit(solution)/shard_map/ppermute | solution.py:373
  36.3 1.5 %collective-permute-start.12 = (bf16[32,2048]{1,0:T(8,128)(2,1)S(1)}, bf16[32,2048]{1,0:T(8,128)(2,1)S(1)}, u32[]{:S(2)}, u32[]{:S(2)}) collective-permute-start(bf16[32,2048]{1,0:T(8,128)(2,1)S(1)} %get-tuple-element.80), channel_id=1, source_target_pairs={{0,4},{1,5},{2,6},{3,7},{4,0},{5,1},{6,2},{7,3},{8,12},{9,13},{10,... | collective-permute-start | bytes 393224 | tf_op jit(solution)/shard_map/ppermute | solution.py:373
  38.3 1.4 %collective-permute-done.8.refs_7_.refs_4_ = bf16[64,2176]{1,0:T(8,128)(2,1)S(1)} collective-permute-done((bf16[64,2176]{1,0:T(8,128)(2,1)S(1)}, bf16[64,2176]{1,0:T(8,128)(2,1)S(1)}, u32[]{:S(2)}, u32[]{:S(2)}) %collective-permute-start.8) | collective-permute-done | bytes 278560 | tf_op jit(solution)/shard_map/ppermute | solution.py:373
  39.8 1.4 %tables.1 = (bf16[144,128]{1,0:T(8,128)(2,1)S(1)}, bf16[144,128]{1,0:T(8,128)(2,1)S(1)}, bf16[16,2048]{1,0:T(8,128)(2,1)S(1)}, f32[16,128]{1,0:T(8,128)S(1)}) custom-call(s32[3]{0:T(128)S(1)} %pad_add_fusion.place.refs_0_.refs_10_, bf16[32,2176]{1,0:T(8,128)(2,1)S(1)} %copy-done.3, bf16[32,2176]{1,0:T(8,128)(2,1)S(1)} %collective-permute-done.refs_1_.refs_2_, ...), custom_call_target="tpu_custom_call" | custom-call | bytes 1048576 | tf_op jit(solution)/shard_map/tables/pallas_call | solution.py:430
  41.3 5.1 %experts.3 = (bf16[32,2048]{1,0:T(8,128)(2,1)S(1)}, bf16[32,2048]{1,0:T(8,128)(2,1)S(1)}, bf16[32,2048]{1,0:T(8,128)(2,1)S(1)}, bf16[32,2048]{1,0:T(8,128)(2,1)S...) custom-call(s32[3]{0:T(128)S(1)} %pad_add_fusion.place.refs_0_.refs_, ...), custom_call_target="tpu_custom_call" | custom-call | flops 2566914048 | bytes 12582912 | tf_op jit(solution)/shard_map/experts/pallas_call | solution.py:477
  46.5 1.5 %collective-permute-start.15 = (bf16[32,2176]{1,0:T(8,128)(2,1)S(1)}, bf16[32,2176]{1,0:T(8,128)(2,1)S(1)}, u32[]{:S(2)}, u32[]{:S(2)}) collective-permute-start(bf16[32,2176]{1,0:T(8,128)(2,1)S(1)} %get-tuple-element.83), channel_id=1, source_target_pairs={{0,2},{1,3},{2,0},{3,1},{4,6},{5,7},{6,4},{7,5},{8,10},{9,11},{10,... | collective-permute-start | bytes 417800 | tf_op jit(solution)/shard_map/ppermute | solution.py:373
  48.1 1.9 %collective-permute-start.17 = (bf16[32,2176]{1,0:T(8,128)(2,1)S(1)}, bf16[32,2176]{1,0:T(8,128)(2,1)S(1)}, u32[]{:S(2)}, u32[]{:S(2)}) collective-permute-start(bf16[32,2176]{1,0:T(8,128)(2,1)S(1)} %get-tuple-element.85), channel_id=1, source_target_pairs={{0,6},{1,7},{2,4},{3,5},{4,2},{5,3},{6,0},{7,1},{8,14},{9,15},{10,... | collective-permute-start | bytes 417800 | tf_op jit(solution)/shard_map/ppermute | solution.py:373
  50.0 3.0 %collective-permute-done.15.refs_1_ = bf16[32,2176]{1,0:T(8,128)(2,1)S(1)} collective-permute-done((bf16[32,2176]{1,0:T(8,128)(2,1)S(1)}, bf16[32,2176]{1,0:T(8,128)(2,1)S(1)}, u32[]{:S(2)}, u32[]{:S(2)}) %collective-permute-start.15) | collective-permute-done | bytes 139296 | tf_op jit(solution)/shard_map/ppermute | solution.py:373
  53.0 3.7 %collective-permute-done.16.refs_2_ = bf16[32,2176]{1,0:T(8,128)(2,1)S(1)} collective-permute-done((bf16[32,2176]{1,0:T(8,128)(2,1)S(1)}, bf16[32,2176]{1,0:T(8,128)(2,1)S(1)}, u32[]{:S(2)}, u32[]{:S(2)}) %collective-permute-start.16) | collective-permute-done | bytes 139296 | tf_op jit(solution)/shard_map/ppermute | solution.py:373
  57.3 1.2 %collective-permute-start.23 = (bf16[32,2048]{1,0:T(8,128)(2,1)S(1)}, bf16[32,2048]{1,0:T(8,128)(2,1)S(1)}, u32[]{:S(2)}, u32[]{:S(2)}) collective-permute-start(bf16[32,2048]{1,0:T(8,128)(2,1)S(1)} %get-tuple-element.103), channel_id=1, source_target_pairs={{0,4},{1,5},{2,6},{3,7},{4,0},{5,1},{6,2},{7,3},{8,12},{9,13},{10,... | collective-permute-start | bytes 393224 | tf_op jit(solution)/shard_map/ppermute | solution.py:373
  58.5 1.8 %collective-permute-start.24 = (bf16[32,2048]{1,0:T(8,128)(2,1)S(1)}, bf16[32,2048]{1,0:T(8,128)(2,1)S(1)}, u32[]{:S(2)}, u32[]{:S(2)}) collective-permute-start(bf16[32,2048]{1,0:T(8,128)(2,1)S(1)} %get-tuple-element.104), channel_id=1, source_target_pairs={{0,6},{1,7},{2,4},{3,5},{4,2},{5,3},{6,0},{7,1},{8,14},{9,15},{10,... | collective-permute-start | bytes 393224 | tf_op jit(solution)/shard_map/ppermute | solution.py:373
  61.5 2.7 %collective-permute-start.21 = (bf16[32,2176]{1,0:T(8,128)(2,1)S(1)}, bf16[32,2176]{1,0:T(8,128)(2,1)S(1)}, u32[]{:S(2)}, u32[]{:S(2)}) collective-permute-start(bf16[32,2176]{1,0:T(8,128)(2,1)S(1)} %get-tuple-element.100), channel_id=1, source_target_pairs={{0,24},{8,16},{16,8},{24,0},{1,25},{9,17},{17,9},{25,1},{2,26},{10... | collective-permute-start | bytes 417800 | tf_op jit(solution)/shard_map/ppermute | solution.py:376
  66.5 1.1 %collective-permute-start.25 = (bf16[32,2176]{1,0:T(8,128)(2,1)S(1)}, bf16[32,2176]{1,0:T(8,128)(2,1)S(1)}, u32[]{:S(2)}, u32[]{:S(2)}) collective-permute-start(bf16[32,2176]{1,0:T(8,128)(2,1)S(1)} %combine.6), channel_id=1, source_target_pairs={{0,16},{8,24},{16,0},{24,8},{1,17},{9,25},{17,1},{25,9},{2,18},{10... | collective-permute-start | bytes 417800 | tf_op jit(solution)/shard_map/ppermute | solution.py:376
  67.6 1.2 %collective-permute-start.19 = (bf16[32,2048]{1,0:T(8,128)(2,1)S(1)}, bf16[32,2048]{1,0:T(8,128)(2,1)S(1)}, u32[]{:S(2)}, u32[]{:S(2)}) collective-permute-start(bf16[32,2048]{1,0:T(8,128)(2,1)S(1)} %get-tuple-element.92), channel_id=1, source_target_pairs={{0,4},{1,5},{2,6},{3,7},{4,0},{5,1},{6,2},{7,3},{8,12},{9,13},{10,... | collective-permute-start | bytes 393224 | tf_op jit(solution)/shard_map/ppermute | solution.py:373
  68.7 1.8 %collective-permute-start.20 = (bf16[32,2048]{1,0:T(8,128)(2,1)S(1)}, bf16[32,2048]{1,0:T(8,128)(2,1)S(1)}, u32[]{:S(2)}, u32[]{:S(2)}) collective-permute-start(bf16[32,2048]{1,0:T(8,128)(2,1)S(1)} %get-tuple-element.93), channel_id=1, source_target_pairs={{0,6},{1,7},{2,4},{3,5},{4,2},{5,3},{6,0},{7,1},{8,14},{9,15},{10,... | collective-permute-start | bytes 393224 | tf_op jit(solution)/shard_map/ppermute | solution.py:373
  70.5 2.1 %collective-permute-done.19.refs_3_ = bf16[32,2048]{1,0:T(8,128)(2,1)S(1)} collective-permute-done((bf16[32,2048]{1,0:T(8,128)(2,1)S(1)}, bf16[32,2048]{1,0:T(8,128)(2,1)S(1)}, u32[]{:S(2)}, u32[]{:S(2)}) %collective-permute-start.19) | collective-permute-done | bytes 131104 | tf_op jit(solution)/shard_map/ppermute | solution.py:373
  72.5 2.1 %collective-permute-done.20.refs_4_ = bf16[32,2048]{1,0:T(8,128)(2,1)S(1)} collective-permute-done((bf16[32,2048]{1,0:T(8,128)(2,1)S(1)}, bf16[32,2048]{1,0:T(8,128)(2,1)S(1)}, u32[]{:S(2)}, u32[]{:S(2)}) %collective-permute-start.20) | collective-permute-done | bytes 131104 | tf_op jit(solution)/shard_map/ppermute | solution.py:373
  75.4 1.8 %collective-permute-start.29 = (bf16[32,2176]{1,0:T(8,128)(2,1)S(1)}, bf16[32,2176]{1,0:T(8,128)(2,1)S(1)}, u32[]{:S(2)}, u32[]{:S(2)}) collective-permute-start(bf16[32,2176]{1,0:T(8,128)(2,1)S(1)} %finish.1.refs_0_), channel_id=1, source_target_pairs={{0,6},{1,7},{2,4},{3,5},{4,2},{5,3},{6,0},{7,1},{8,14},{9,15},{10,... | collective-permute-start | bytes 417800 | tf_op jit(solution)/shard_map/ppermute | solution.py:373
  77.8 1.2 %collective-permute-start.27 = (bf16[32,2176]{1,0:T(8,128)(2,1)S(1)}, bf16[32,2176]{1,0:T(8,128)(2,1)S(1)}, u32[]{:S(2)}, u32[]{:S(2)}) collective-permute-start(bf16[32,2176]{1,0:T(8,128)(2,1)S(1)} %finish.1.refs_0_), channel_id=1, source_target_pairs={{0,2},{1,3},{2,0},{3,1},{4,6},{5,7},{6,4},{7,5},{8,10},{9,11},{10,... | collective-permute-start | bytes 417800 | tf_op jit(solution)/shard_map/ppermute | solution.py:373
  79.0 2.7 %collective-permute-done.29.refs_3_ = bf16[32,2176]{1,0:T(8,128)(2,1)S(1)} collective-permute-done((bf16[32,2176]{1,0:T(8,128)(2,1)S(1)}, bf16[32,2176]{1,0:T(8,128)(2,1)S(1)}, u32[]{:S(2)}, u32[]{:S(2)}) %collective-permute-start.29) | collective-permute-done | bytes 139296 | tf_op jit(solution)/shard_map/ppermute | solution.py:373
  81.7 1.4 %collective-permute-done.28.refs_2_ = bf16[32,2176]{1,0:T(8,128)(2,1)S(1)} collective-permute-done((bf16[32,2176]{1,0:T(8,128)(2,1)S(1)}, bf16[32,2176]{1,0:T(8,128)(2,1)S(1)}, u32[]{:S(2)}, u32[]{:S(2)}) %collective-permute-start.28) | collective-permute-done | bytes 139296 | tf_op jit(solution)/shard_map/ppermute | solution.py:373
  84.7 5.6 %final.1 = (bf16[256,2048]{1,0:T(8,128)(2,1)}, bf16[1,2048,768]{2,1,0:T(8,128)(2,1)}, bf16[1,384,2048]{2,1,0:T(8,128)(2,1)}) custom-call(bf16[32,2176]{1,0:T(8,128)(2,1)S(1)} %finish.1.refs_0_, bf16[32,2176]{1,0:T(8,128)(2,1)S(1)} %collective-permute-done.27.refs_1_, bf16[32,2176]{1,0:T(8,128)(2,1)S(1)} %collective-permute-done.28.refs_2_, ...), custom_call_target="tpu_custom_call" | custom-call | flops 100663296 | bytes 7340032 | tf_op jit(solution)/shard_map/final/pallas_call | solution.py:555
  (58 shorter events, 13.3 us)
Async XLA Ops:
  0.6 10.3 %collective-permute-start.3 = (bf16[1,2048,768]{2,1,0:T(8,128)(2,1)}, bf16[1,2048,768]{2,1,0:T(8,128)(2,1)}, u32[]{:S(2)}, u32[]{:S(2)}) collective-permute-start(bf16[1,2048,768]{2,1,0:T(8,128)(2,1)} %refs_7_.1), channel_id=1, source_target_pairs={{0,1},{1,0},{2,3},{3,2},{4,5},{5,4},{6,7},{7,6},{8,9},{9,8},{10,11... | collective-permute-start | bytes 9437192 | tf_op jit(solution)/shard_map/ppermute | solution.py:373
  1.2 9.7 %collective-permute-start.4 = (bf16[1,384,2048]{2,1,0:T(8,128)(2,1)}, bf16[1,384,2048]{2,1,0:T(8,128)(2,1)S(1)}, u32[]{:S(2)}, u32[]{:S(2)}) collective-permute-start(bf16[1,384,2048]{2,1,0:T(8,128)(2,1)} %refs_14_.1), channel_id=1, source_target_pairs={{0,1},{1,0},{2,3},{3,2},{4,5},{5,4},{6,7},{7,6},{8,9},{9,8},{10,11... | collective-permute-start | bytes 4718600 | tf_op jit(solution)/shard_map/ppermute | solution.py:373
  3.6 7.3 %collective-permute-start = (bf16[32,2176]{1,0:T(8,128)(2,1)}, bf16[32,2176]{1,0:T(8,128)(2,1)S(1)}, u32[]{:S(2)}, u32[]{:S(2)}) collective-permute-start(bf16[32,2176]{1,0:T(8,128)(2,1)} %pack.1.refs_0_), channel_id=1, source_target_pairs={{0,8},{8,0},{16,24},{24,16},{1,9},{9,1},{17,25},{25,17},{2,10},{10... | collective-permute-start | bytes 417800 | tf_op jit(solution)/shard_map/ppermute | solution.py:376
  6.6 10.3 %collective-permute-start.2 = (bf16[32,2176]{1,0:T(8,128)(2,1)}, bf16[32,2176]{1,0:T(8,128)(2,1)S(1)}, u32[]{:S(2)}, u32[]{:S(2)}) collective-permute-start(bf16[32,2176]{1,0:T(8,128)(2,1)} %pack.1.refs_0_), channel_id=1, source_target_pairs={{0,24},{8,16},{16,8},{24,0},{1,25},{9,17},{17,9},{25,1},{2,26},{10... | collective-permute-start | bytes 417800 | tf_op jit(solution)/shard_map/ppermute | solution.py:376
  9.1 13.1 %collective-permute-start.1 = (bf16[32,2176]{1,0:T(8,128)(2,1)}, bf16[32,2176]{1,0:T(8,128)(2,1)}, u32[]{:S(2)}, u32[]{:S(2)}) collective-permute-start(bf16[32,2176]{1,0:T(8,128)(2,1)} %pack.1.refs_0_), channel_id=1, source_target_pairs={{0,16},{8,24},{16,0},{24,8},{1,17},{9,25},{17,1},{25,9},{2,18},{10... | collective-permute-start | bytes 417800 | tf_op jit(solution)/shard_map/ppermute | solution.py:376
  10.9 12.2 %collective-permute-start.7 = (bf16[32,2304]{1,0:T(8,128)(2,1)S(1)}, bf16[32,2304]{1,0:T(8,128)(2,1)S(1)}, u32[]{:S(2)}, u32[]{:S(2)}) collective-permute-start(bf16[32,2304]{1,0:T(8,128)(2,1)S(1)} %pad_maximum_fusion.1), channel_id=1, source_target_pairs={{0,6},{1,7},{2,4},{3,5},{4,2},{5,3},{6,0},{7,1},{8,14},{9,15},{10,... | collective-permute-start | bytes 442376 | tf_op jit(solution)/shard_map/ppermute | solution.py:373
  13.5 9.6 %collective-permute-start.6 = (bf16[32,2304]{1,0:T(8,128)(2,1)S(1)}, bf16[32,2304]{1,0:T(8,128)(2,1)S(1)}, u32[]{:S(2)}, u32[]{:S(2)}) collective-permute-start(bf16[32,2304]{1,0:T(8,128)(2,1)S(1)} %pad_maximum_fusion.1), channel_id=1, source_target_pairs={{0,4},{1,5},{2,6},{3,7},{4,0},{5,1},{6,2},{7,3},{8,12},{9,13},{10,... | collective-permute-start | bytes 442376 | tf_op jit(solution)/shard_map/ppermute | solution.py:373
  14.0 9.1 %collective-permute-start.5 = (bf16[32,2304]{1,0:T(8,128)(2,1)S(1)}, bf16[32,2304]{1,0:T(8,128)(2,1)S(1)}, u32[]{:S(2)}, u32[]{:S(2)}) collective-permute-start(bf16[32,2304]{1,0:T(8,128)(2,1)S(1)} %pad_maximum_fusion.1), channel_id=1, source_target_pairs={{0,2},{1,3},{2,0},{3,1},{4,6},{5,7},{6,4},{7,5},{8,10},{9,11},{10,... | collective-permute-start | bytes 442376 | tf_op jit(solution)/shard_map/ppermute | solution.py:373
  23.1 14.7 %collective-permute-start.10 = (bf16[64,2176]{1,0:T(8,128)(2,1)S(1)}, bf16[64,2176]{1,0:T(8,128)(2,1)S(1)}, u32[]{:S(2)}, u32[]{:S(2)}) collective-permute-start(bf16[64,2176]{1,0:T(8,128)(2,1)S(1)} %pad_maximum_fusion), channel_id=1, source_target_pairs={{0,6},{1,7},{2,4},{3,5},{4,2},{5,3},{6,0},{7,1},{8,14},{9,15},{10,... | collective-permute-start | bytes 835592 | tf_op jit(solution)/shard_map/ppermute | solution.py:373
  25.6 12.7 %collective-permute-start.9 = (bf16[64,2176]{1,0:T(8,128)(2,1)S(1)}, bf16[64,2176]{1,0:T(8,128)(2,1)S(1)}, u32[]{:S(2)}, u32[]{:S(2)}) collective-permute-start(bf16[64,2176]{1,0:T(8,128)(2,1)S(1)} %pad_maximum_fusion), channel_id=1, source_target_pairs={{0,4},{1,5},{2,6},{3,7},{4,0},{5,1},{6,2},{7,3},{8,12},{9,13},{10,... | collective-permute-start | bytes 835592 | tf_op jit(solution)/shard_map/ppermute | solution.py:373
  26.1 13.6 %collective-permute-start.8 = (bf16[64,2176]{1,0:T(8,128)(2,1)S(1)}, bf16[64,2176]{1,0:T(8,128)(2,1)S(1)}, u32[]{:S(2)}, u32[]{:S(2)}) collective-permute-start(bf16[64,2176]{1,0:T(8,128)(2,1)S(1)} %pad_maximum_fusion), channel_id=1, source_target_pairs={{0,2},{1,3},{2,0},{3,1},{4,6},{5,7},{6,4},{7,5},{8,10},{9,11},{10,... | collective-permute-start | bytes 835592 | tf_op jit(solution)/shard_map/ppermute | solution.py:373
  34.8 11.6 %collective-permute-start.11 = (bf16[32,2048]{1,0:T(8,128)(2,1)S(1)}, bf16[32,2048]{1,0:T(8,128)(2,1)S(1)}, u32[]{:S(2)}, u32[]{:S(2)}) collective-permute-start(bf16[32,2048]{1,0:T(8,128)(2,1)S(1)} %get-tuple-element.79), channel_id=1, source_target_pairs={{0,2},{1,3},{2,0},{3,1},{4,6},{5,7},{6,4},{7,5},{8,10},{9,11},{10,... | collective-permute-start | bytes 393224 | tf_op jit(solution)/shard_map/ppermute | solution.py:373
  36.3 10.1 %collective-permute-start.12 = (bf16[32,2048]{1,0:T(8,128)(2,1)S(1)}, bf16[32,2048]{1,0:T(8,128)(2,1)S(1)}, u32[]{:S(2)}, u32[]{:S(2)}) collective-permute-start(bf16[32,2048]{1,0:T(8,128)(2,1)S(1)} %get-tuple-element.80), channel_id=1, source_target_pairs={{0,4},{1,5},{2,6},{3,7},{4,0},{5,1},{6,2},{7,3},{8,12},{9,13},{10,... | collective-permute-start | bytes 393224 | tf_op jit(solution)/shard_map/ppermute | solution.py:373
  37.8 8.6 %collective-permute-start.13 = (bf16[32,2048]{1,0:T(8,128)(2,1)S(1)}, bf16[32,2048]{1,0:T(8,128)(2,1)S(1)}, u32[]{:S(2)}, u32[]{:S(2)}) collective-permute-start(bf16[32,2048]{1,0:T(8,128)(2,1)S(1)} %get-tuple-element.81), channel_id=1, source_target_pairs={{0,6},{1,7},{2,4},{3,5},{4,2},{5,3},{6,0},{7,1},{8,14},{9,15},{10,... | collective-permute-start | bytes 393224 | tf_op jit(solution)/shard_map/ppermute | solution.py:373
  41.2 5.2 %collective-permute-start.14 = (bf16[144,128]{1,0:T(8,128)(2,1)S(1)}, bf16[144,128]{1,0:T(8,128)(2,1)S(1)}, u32[]{:S(2)}, u32[]{:S(2)}) collective-permute-start(bf16[144,128]{1,0:T(8,128)(2,1)S(1)} %get-tuple-element.82), channel_id=1, source_target_pairs={{0,1},{1,0},{2,3},{3,2},{4,5},{5,4},{6,7},{7,6},{8,9},{9,8},{10,11... | collective-permute-start | bytes 110600 | tf_op jit(solution)/shard_map/ppermute | solution.py:373
  46.5 6.5 %collective-permute-start.15 = (bf16[32,2176]{1,0:T(8,128)(2,1)S(1)}, bf16[32,2176]{1,0:T(8,128)(2,1)S(1)}, u32[]{:S(2)}, u32[]{:S(2)}) collective-permute-start(bf16[32,2176]{1,0:T(8,128)(2,1)S(1)} %get-tuple-element.83), channel_id=1, source_target_pairs={{0,2},{1,3},{2,0},{3,1},{4,6},{5,7},{6,4},{7,5},{8,10},{9,11},{10,... | collective-permute-start | bytes 417800 | tf_op jit(solution)/shard_map/ppermute | solution.py:373
  48.0 8.8 %collective-permute-start.16 = (bf16[32,2176]{1,0:T(8,128)(2,1)S(1)}, bf16[32,2176]{1,0:T(8,128)(2,1)S(1)}, u32[]{:S(2)}, u32[]{:S(2)}) collective-permute-start(bf16[32,2176]{1,0:T(8,128)(2,1)S(1)} %get-tuple-element.84), channel_id=1, source_target_pairs={{0,4},{1,5},{2,6},{3,7},{4,0},{5,1},{6,2},{7,3},{8,12},{9,13},{10,... | collective-permute-start | bytes 417800 | tf_op jit(solution)/shard_map/ppermute | solution.py:373
  48.1 8.6 %collective-permute-start.17 = (bf16[32,2176]{1,0:T(8,128)(2,1)S(1)}, bf16[32,2176]{1,0:T(8,128)(2,1)S(1)}, u32[]{:S(2)}, u32[]{:S(2)}) collective-permute-start(bf16[32,2176]{1,0:T(8,128)(2,1)S(1)} %get-tuple-element.85), channel_id=1, source_target_pairs={{0,6},{1,7},{2,4},{3,5},{4,2},{5,3},{6,0},{7,1},{8,14},{9,15},{10,... | collective-permute-start | bytes 417800 | tf_op jit(solution)/shard_map/ppermute | solution.py:373
  56.7 8.2 %collective-permute-start.22 = (bf16[32,2048]{1,0:T(8,128)(2,1)S(1)}, bf16[32,2048]{1,0:T(8,128)(2,1)S(1)}, u32[]{:S(2)}, u32[]{:S(2)}) collective-permute-start(bf16[32,2048]{1,0:T(8,128)(2,1)S(1)} %get-tuple-element.102), channel_id=1, source_target_pairs={{0,2},{1,3},{2,0},{3,1},{4,6},{5,7},{6,4},{7,5},{8,10},{9,11},{10,... | collective-permute-start | bytes 393224 | tf_op jit(solution)/shard_map/ppermute | solution.py:373
  57.3 7.7 %collective-permute-start.23 = (bf16[32,2048]{1,0:T(8,128)(2,1)S(1)}, bf16[32,2048]{1,0:T(8,128)(2,1)S(1)}, u32[]{:S(2)}, u32[]{:S(2)}) collective-permute-start(bf16[32,2048]{1,0:T(8,128)(2,1)S(1)} %get-tuple-element.103), channel_id=1, source_target_pairs={{0,4},{1,5},{2,6},{3,7},{4,0},{5,1},{6,2},{7,3},{8,12},{9,13},{10,... | collective-permute-start | bytes 393224 | tf_op jit(solution)/shard_map/ppermute | solution.py:373
  58.5 7.3 %collective-permute-start.24 = (bf16[32,2048]{1,0:T(8,128)(2,1)S(1)}, bf16[32,2048]{1,0:T(8,128)(2,1)S(1)}, u32[]{:S(2)}, u32[]{:S(2)}) collective-permute-start(bf16[32,2048]{1,0:T(8,128)(2,1)S(1)} %get-tuple-element.104), channel_id=1, source_target_pairs={{0,6},{1,7},{2,4},{3,5},{4,2},{5,3},{6,0},{7,1},{8,14},{9,15},{10,... | collective-permute-start | bytes 393224 | tf_op jit(solution)/shard_map/ppermute | solution.py:373
  60.2 8.5 %collective-permute-start.18 = (bf16[32,2048]{1,0:T(8,128)(2,1)S(1)}, bf16[32,2048]{1,0:T(8,128)(2,1)S(1)}, u32[]{:S(2)}, u32[]{:S(2)}) collective-permute-start(bf16[32,2048]{1,0:T(8,128)(2,1)S(1)} %get-tuple-element.91), channel_id=1, source_target_pairs={{0,2},{1,3},{2,0},{3,1},{4,6},{5,7},{6,4},{7,5},{8,10},{9,11},{10,... | collective-permute-start | bytes 393224 | tf_op jit(solution)/shard_map/ppermute | solution.py:373
  61.5 13.8 %collective-permute-start.21 = (bf16[32,2176]{1,0:T(8,128)(2,1)S(1)}, bf16[32,2176]{1,0:T(8,128)(2,1)S(1)}, u32[]{:S(2)}, u32[]{:S(2)}) collective-permute-start(bf16[32,2176]{1,0:T(8,128)(2,1)S(1)} %get-tuple-element.100), channel_id=1, source_target_pairs={{0,24},{8,16},{16,8},{24,0},{1,25},{9,17},{17,9},{25,1},{2,26},{10... | collective-permute-start | bytes 417800 | tf_op jit(solution)/shard_map/ppermute | solution.py:376
  64.9 10.4 %collective-permute-start.26 = (bf16[32,2176]{1,0:T(8,128)(2,1)S(1)}, bf16[32,2176]{1,0:T(8,128)(2,1)S(1)}, u32[]{:S(2)}, u32[]{:S(2)}) collective-permute-start(bf16[32,2176]{1,0:T(8,128)(2,1)S(1)} %combine.7), channel_id=1, source_target_pairs={{0,8},{8,0},{16,24},{24,16},{1,9},{9,1},{17,25},{25,17},{2,10},{10... | collective-permute-start | bytes 417800 | tf_op jit(solution)/shard_map/ppermute | solution.py:376
  66.5 8.9 %collective-permute-start.25 = (bf16[32,2176]{1,0:T(8,128)(2,1)S(1)}, bf16[32,2176]{1,0:T(8,128)(2,1)S(1)}, u32[]{:S(2)}, u32[]{:S(2)}) collective-permute-start(bf16[32,2176]{1,0:T(8,128)(2,1)S(1)} %combine.6), channel_id=1, source_target_pairs={{0,16},{8,24},{16,0},{24,8},{1,17},{9,25},{17,1},{25,9},{2,18},{10... | collective-permute-start | bytes 417800 | tf_op jit(solution)/shard_map/ppermute | solution.py:376
  67.6 5.0 %collective-permute-start.19 = (bf16[32,2048]{1,0:T(8,128)(2,1)S(1)}, bf16[32,2048]{1,0:T(8,128)(2,1)S(1)}, u32[]{:S(2)}, u32[]{:S(2)}) collective-permute-start(bf16[32,2048]{1,0:T(8,128)(2,1)S(1)} %get-tuple-element.92), channel_id=1, source_target_pairs={{0,4},{1,5},{2,6},{3,7},{4,0},{5,1},{6,2},{7,3},{8,12},{9,13},{10,... | collective-permute-start | bytes 393224 | tf_op jit(solution)/shard_map/ppermute | solution.py:373
  68.7 5.9 %collective-permute-start.20 = (bf16[32,2048]{1,0:T(8,128)(2,1)S(1)}, bf16[32,2048]{1,0:T(8,128)(2,1)S(1)}, u32[]{:S(2)}, u32[]{:S(2)}) collective-permute-start(bf16[32,2048]{1,0:T(8,128)(2,1)S(1)} %get-tuple-element.93), channel_id=1, source_target_pairs={{0,6},{1,7},{2,4},{3,5},{4,2},{5,3},{6,0},{7,1},{8,14},{9,15},{10,... | collective-permute-start | bytes 393224 | tf_op jit(solution)/shard_map/ppermute | solution.py:373
  75.4 6.2 %collective-permute-start.29 = (bf16[32,2176]{1,0:T(8,128)(2,1)S(1)}, bf16[32,2176]{1,0:T(8,128)(2,1)S(1)}, u32[]{:S(2)}, u32[]{:S(2)}) collective-permute-start(bf16[32,2176]{1,0:T(8,128)(2,1)S(1)} %finish.1.refs_0_), channel_id=1, source_target_pairs={{0,6},{1,7},{2,4},{3,5},{4,2},{5,3},{6,0},{7,1},{8,14},{9,15},{10,... | collective-permute-start | bytes 417800 | tf_op jit(solution)/shard_map/ppermute | solution.py:373
  77.3 5.8 %collective-permute-start.28 = (bf16[32,2176]{1,0:T(8,128)(2,1)S(1)}, bf16[32,2176]{1,0:T(8,128)(2,1)S(1)}, u32[]{:S(2)}, u32[]{:S(2)}) collective-permute-start(bf16[32,2176]{1,0:T(8,128)(2,1)S(1)} %finish.1.refs_0_), channel_id=1, source_target_pairs={{0,4},{1,5},{2,6},{3,7},{4,0},{5,1},{6,2},{7,3},{8,12},{9,13},{10,... | collective-permute-start | bytes 417800 | tf_op jit(solution)/shard_map/ppermute | solution.py:373
  77.8 5.6 %collective-permute-start.27 = (bf16[32,2176]{1,0:T(8,128)(2,1)S(1)}, bf16[32,2176]{1,0:T(8,128)(2,1)S(1)}, u32[]{:S(2)}, u32[]{:S(2)}) collective-permute-start(bf16[32,2176]{1,0:T(8,128)(2,1)S(1)} %finish.1.refs_0_), channel_id=1, source_target_pairs={{0,2},{1,3},{2,0},{3,1},{4,6},{5,7},{6,4},{7,5},{8,10},{9,11},{10,... | collective-permute-start | bytes 417800 | tf_op jit(solution)/shard_map/ppermute | solution.py:373
  79.0 4.6 %collective-permute-start.30 = (bf16[32,2176]{1,0:T(8,128)(2,1)S(1)}, bf16[32,2176]{1,0:T(8,128)(2,1)S(1)}, u32[]{:S(2)}, u32[]{:S(2)}) collective-permute-start(bf16[32,2176]{1,0:T(8,128)(2,1)S(1)} %finish.1.refs_0_), channel_id=1, source_target_pairs={{0,1},{1,0},{2,3},{3,2},{4,5},{5,4},{6,7},{7,6},{8,9},{9,8},{10,11... | collective-permute-start | bytes 417800 | tf_op jit(solution)/shard_map/ppermute | solution.py:373
  81.7 1.9 %collective-permute-start.33 = (bf16[32,2176]{1,0:T(8,128)(2,1)S(1)}, bf16[32,2176]{1,0:T(8,128)(2,1)S(1)}, u32[]{:S(2)}, u32[]{:S(2)}) collective-permute-start(bf16[32,2176]{1,0:T(8,128)(2,1)S(1)} %collective-permute-done.29.refs_3_), channel_id=1, source_target_pairs={{0,1},{1,0},{2,3},{3,2},{4,5},{5,4},{6,7},{7,6},{8,9},{9,8},{10,11... | collective-permute-start | bytes 417800 | tf_op jit(solution)/shard_map/ppermute | solution.py:373
  (6 other events, 41.8 us)

commit v9 on v8

--- a/solution.py
+++ b/solution.py
@@ -90,14 +90,12 @@
 def table_kernel(layout, place, *refs):
     seq_dev, tok_dev, where_tiles, n_parts = layout
     parts = refs[:n_parts]
-    kept, sent, last_rows, partners, tokens, routes, marks = refs[n_parts:]
+    kept, sent, partners, routes, marks = refs[n_parts:]
     part_rows = parts[0].shape[0]
-    dp_count, chunks = tokens.shape[:2]
+    dp_count = len(where_tiles)
     note_rows = tok_dev // lanes
     seq_length = tok_dev // seq_dev
     chips = len(where_tiles[0])
-    share_chunks = chunks // chips
-    base = part_rows - seq_dev * share_chunks
     lane_index = lax.broadcasted_iota(jnp.int32, (part_rows, lanes), 1)
     row_index = lax.broadcasted_iota(jnp.int32, (part_rows, lanes), 0)
 
@@ -140,21 +138,14 @@
                 routes[plane, seq : seq + 1, :] = value
             if chip == 0:
                 marks[plane, 0:seq_dev, :] = tile[2 * note_rows : 2 * note_rows + seq_dev, :]
-            first = ((place[1] // 2) ^ chip) * share_chunks
-            for chunk in range(share_chunks):
-                row = base + chunk * seq_dev
-                tokens[plane, first + chunk, 0:seq_dev, :] = tile[row : row + seq_dev, :]
         at = slice(hop * part_rows, (hop + 1) * part_rows)
         kept[at, :] = sums[0].astype(bf16)
         sent[at, :] = sums[1].astype(bf16)
     last = dp_count * part_rows
-    joined, shared = [], []
+    shared = []
     for plane in range(dp_count):
         shared.append(routes[plane, 0:seq_dev, :])
         partners[plane * seq_dev : (plane + 1) * seq_dev, :] = marks[plane, 0:seq_dev, :]
-        lines = [tokens[plane, chunk, 0:seq_dev, :] for chunk in range(chunks)]
-        joined.append(jnp.concatenate(lines, axis=1))
-    last_rows[...] = jnp.concatenate(joined, axis=0).astype(bf16)
     seqs = dp_count * seq_dev
     value = jnp.concatenate(shared, axis=0).astype(bf16)
     kept[last : last + seqs, :] = value
@@ -177,55 +168,84 @@
         blocks[spot, block] = values[row : row + 1, chunk * lanes : (chunk + 1) * lanes]
 
 
+def last_tokens(place, seq_dev, where_tiles, parts, tokens):
+    part_rows = parts[0].shape[0]
+    dp_count, chunks = tokens.shape[:2]
+    chips = len(where_tiles[0])
+    share_chunks = chunks // chips
+    base = part_rows - seq_dev * share_chunks
+    for hop in range(dp_count):
+        for chip in range(chips):
+            source, row, at = where_tiles[hop][chip]
+            tile = parts[source][row : row + part_rows, at : at + lanes].astype(f32)
+            first = ((place[1] // 2) ^ chip) * share_chunks
+            for chunk in range(share_chunks):
+                row = base + chunk * seq_dev
+                tokens[place[0] ^ hop, first + chunk, 0:seq_dev, :] = tile[row : row + seq_dev, :]
+    joined = []
+    for plane in range(dp_count):
+        lines = [tokens[plane, chunk, 0:seq_dev, :] for chunk in range(chunks)]
+        joined.append(jnp.concatenate(lines, axis=1))
+    return jnp.concatenate(joined, axis=0)
+
+
 def expert_kernel(layout, *refs):
-    group, chips, part_rows, with_last, sources, n_parts = layout
+    group, chips, part_rows, seq_dev, where_tiles, used, with_last = layout
     refs = list(refs)
     place = refs.pop(0)
     near = 0 in group
     tokens = refs.pop(0) if near else None
-    last_rows = refs.pop(0) if with_last else None
-    parts, refs = refs[:n_parts], refs[n_parts:]
+    parts, refs = dict(zip(used, refs)), refs[len(used) :]
     weights, refs = refs[:4], refs[4:]
     n_outs = chips * len(group)
     outs, refs = refs[:n_outs], refs[n_outs:]
     if with_last:
-        last_projected, own_last, by_lane, tile, *refs = refs
+        last_all, last_projected, own_last, by_lane, tile, seq_tokens, *refs = refs
     (rows,) = refs
     width = weights[0].shape[1]
     total = n_outs * part_rows
     spots = [slice(index * part_rows, (index + 1) * part_rows) for index in range(n_outs)]
-    if near:
-        for chip in range(chips):
+    for index, spot in enumerate(spots):
+        hop, chip = group[index // chips], index % chips
+        if hop:
+            source, row, _ = where_tiles[hop][chip]
+            rows[spot, :] = parts[source][row : row + part_rows, :width]
+        else:
             start = pl.multiple_of((place[1] ^ (2 * chip)) * part_rows, part_rows)
-            rows[spots[chip], :] = tokens[pl.ds(start, part_rows), :]
-    for (index, row), spot in zip(sources, spots[n_outs - len(sources) :]):
-        rows[spot, :] = parts[index][row : row + part_rows, :width]
+            rows[spot, :] = tokens[pl.ds(start, part_rows), :]
     if with_last:
-        rows[total:, :] = last_rows[...]
-    result = None
+        floats = last_tokens(place, seq_dev, where_tiles, parts, seq_tokens)
+        last_all[...] = floats.astype(bf16)
+        rows[total:, :] = floats.astype(bf16)
+    hidden = []
     for half in range(2):
-        w_in, w_out = weights[2 * half], weights[2 * half + 1]
-        projected = dot(rows[...], w_in[0])
+        projected = dot(rows[...], weights[2 * half][0])
         if half == 0 and with_last:
             last_projected[...] = projected[total:]
         _, up, _, activated = hidden_parts(projected)
-        part = dot((activated * up).astype(bf16), w_out[0])
-        result = part if half == 0 else result + part
-    for out, spot in zip(outs, spots):
-        out[:, :width] = result[spot].astype(bf16)
+        hidden.append((activated * up).astype(bf16))
+    block = min(512, width)
     if with_last:
-        each = last_rows.shape[0] // by_lane.shape[0]
-        floats = last_rows[...].astype(f32)
+        each = floats.shape[0] // by_lane.shape[0]
+    for first in range(0, width, block):
+        columns = slice(first, first + block)
+        result = dot(hidden[0], weights[1][0, :, columns]) + dot(
+            hidden[1], weights[3][0, :, columns]
+        )
+        for out, spot in zip(outs, spots):
+            out[:, columns] = result[spot].astype(bf16)
+        if with_last:
+            for lane in range(by_lane.shape[0]):
+                at = total + lane * each
+                by_lane[lane, 0:each, columns] = result[at : at + each]
+    if with_last:
+        for chip in range(chips):
+            spread_rows(by_lane[place[1] ^ (2 * chip), 0:each, :], part_rows, tile)
+            outs[n_outs - chips + chip][:, width:] = tile[...].astype(bf16)
         for lane in range(by_lane.shape[0]):
             by_lane[lane, 0:each, :] = floats[lane * each : (lane + 1) * each]
         spread_rows(by_lane[place[1], 0:each, :], part_rows, tile)
         own_last[...] = tile[...]
-        for lane in range(by_lane.shape[0]):
-            first = total + lane * each
-            by_lane[lane, 0:each, :] = result[first : first + each]
-        for chip in range(chips):
-            spread_rows(by_lane[place[1] ^ (2 * chip), 0:each, :], part_rows, tile)
-            outs[n_outs - chips + chip][:, width:] = tile[...].astype(bf16)
 
 
 def combine_kernel(layout, place, kept, found, *refs):
@@ -276,14 +296,12 @@
     out[:, width:] = (own_last[...] + last).astype(bf16)
 
 
-def gather_rows(lane, pieces, out, by_lane, each):
-    part_rows, width = pieces[0].shape[0], out.shape[1]
-    chunks = width // lanes
+def collect_rows(lane, pieces, by_lane, width):
+    part_rows, chunks = pieces[0].shape[0], width // lanes
     count = len(pieces)
+    each = (pieces[0].shape[1] - width) * part_rows // width
     for index in range(count):
         source = lane ^ (2 * (index % (count // 2))) ^ (index // (count // 2))
-        start = pl.multiple_of(source * part_rows, part_rows)
-        out[pl.ds(start, part_rows), :] = pieces[index][:, :width]
         values = pieces[index][:, width:].astype(f32)
         for spot in range(each * chunks):
             row, chunk = spot // chunks, spot % chunks
@@ -310,47 +328,55 @@
     return total
 
 
-def final_kernel(n_pieces, *refs):
+def final_kernel(n_pieces, n_blocks, *refs):
     pieces, refs = refs[:n_pieces], refs[n_pieces:]
-    last_block, projected, place, kept, found, partners, down, *refs = refs
-    layer_out, grad_in, grad_out, route, hidden, slope, by_lane = refs
-    step = pl.program_id(0)
-    half_width = down.shape[1]
-    block = grad_out.shape[2]
-
-    @pl.when(step == 0)
-    def _():
-        each = projected.shape[0] // by_lane.shape[0]
-        values = gather_rows(place[1], pieces, layer_out, by_lane, each)
-        count = values.shape[0]
-        last = kept.shape[0] - count
-        table = kept[last:, :].astype(f32) + found[last:, :].astype(f32)
-        row = lax.broadcasted_iota(jnp.int32, (count, count), 0)
-        col = lax.broadcasted_iota(jnp.int32, (count, count), 1)
-        norms = jnp.sqrt(jnp.sum(values * values, axis=1, keepdims=True) + epsilon)
-        norms_line = jnp.sum(jnp.where(row == col, norms, 0.0), axis=0, keepdims=True)
-        unit = values / norms
-        rows = values.astype(bf16)
-        scores = dot(rows, rows, ((1,), (1,))) / (norms * norms_line) / logit_divisor
-        exp_scores = jnp.where(row != col, jnp.exp(scores), 0.0)
-        probabilities = exp_scores / jnp.sum(exp_scores, axis=1, keepdims=True)
-        partner = partners[:, :1].astype(jnp.int32)
-        coefficient = grad_scale * (probabilities - jnp.where(col == partner, 1.0, 0.0))
-        grad_unit = both_ways(coefficient, unit, row == col) / logit_divisor
-        projection = jnp.sum(unit * grad_unit, axis=1, keepdims=True)
-        grad_last = (grad_unit - unit * projection) / norms
-        route_grad = (column(table, place[2]) * grad_last).astype(bf16)
-        for index in range(route.shape[0]):
-            route[index] = route_grad[:, index * block : (index + 1) * block]
-        grad_hidden = dot(route_grad, down[0], ((1,), (1,)))
-        gate, up, sigmoid_gate, activated = hidden_parts(projected[...])
-        hidden[...] = (activated * up).astype(bf16)
-        gate_slope = sigmoid_gate * (1.0 + gate * (1.0 - sigmoid_gate))
-        slope[:, :half_width] = (grad_hidden * up * gate_slope).astype(bf16)
-        slope[:, half_width:] = (grad_hidden * activated).astype(bf16)
-
-    grad_in[0] = dot(last_block[...], slope[...], ((0,), (0,))).astype(bf16)
-    grad_out[0] = dot(hidden[...], route[step], ((0,), (0,))).astype(bf16)
+    last_all, projected, place, kept, found, partners, down, *refs = refs
+    layer_out, grad_in, grad_out, made_in, made_out, by_lane, sems = refs
+    part_rows, width = pieces[0].shape[0], layer_out.shape[1]
+    copies = []
+
+    def send(source, target):
+        copies.append(pltpu.make_async_copy(source, target, sems.at[len(copies)]))
+        copies[-1].start()
+
+    for index in range(n_pieces):
+        lane = place[1] ^ (2 * (index % (n_pieces // 2))) ^ (index // (n_pieces // 2))
+        start = pl.multiple_of(lane * part_rows, part_rows)
+        send(pieces[index].at[:, pl.ds(0, width)], layer_out.at[pl.ds(start, part_rows)])
+    values = collect_rows(place[1], pieces, by_lane, width)
+    count = values.shape[0]
+    last = kept.shape[0] - count
+    table = kept[last:, :].astype(f32) + found[last:, :].astype(f32)
+    row = lax.broadcasted_iota(jnp.int32, (count, count), 0)
+    col = lax.broadcasted_iota(jnp.int32, (count, count), 1)
+    norms = jnp.sqrt(jnp.sum(values * values, axis=1, keepdims=True) + epsilon)
+    norms_line = jnp.sum(jnp.where(row == col, norms, 0.0), axis=0, keepdims=True)
+    unit = values / norms
+    rows = values.astype(bf16)
+    scores = dot(rows, rows, ((1,), (1,))) / (norms * norms_line) / logit_divisor
+    exp_scores = jnp.where(row != col, jnp.exp(scores), 0.0)
+    probabilities = exp_scores / jnp.sum(exp_scores, axis=1, keepdims=True)
+    partner = partners[:, :1].astype(jnp.int32)
+    coefficient = grad_scale * (probabilities - jnp.where(col == partner, 1.0, 0.0))
+    grad_unit = both_ways(coefficient, unit, row == col) / logit_divisor
+    projection = jnp.sum(unit * grad_unit, axis=1, keepdims=True)
+    grad_last = (grad_unit - unit * projection) / norms
+    route_grad = (column(table, place[2]) * grad_last).astype(bf16)
+    grad_hidden = dot(route_grad, down[0], ((1,), (1,)))
+    gate, up, sigmoid_gate, activated = hidden_parts(projected[...])
+    hidden = (activated * up).astype(bf16)
+    gate_slope = sigmoid_gate * (1.0 + gate * (1.0 - sigmoid_gate))
+    slope = jnp.concatenate([grad_hidden * up * gate_slope, grad_hidden * activated], axis=1)
+    slope = slope.astype(bf16)
+    block = width // n_blocks
+    for index in range(n_blocks):
+        spot = slice(index * block, (index + 1) * block)
+        made_in[spot, :] = dot(last_all[:, spot], slope, ((0,), (0,))).astype(bf16)
+        send(made_in.at[spot], grad_in.at[0, spot])
+    made_out[...] = dot(hidden, route_grad, ((0,), (0,))).astype(bf16)
+    send(made_out, grad_out.at[0])
+    for copy in copies:
+        copy.wait()
 
 
 def body(tokens, expert_ids, gates, positives, gate_up, down):
@@ -424,39 +450,14 @@
             ]
     where_tiles = [spots[hop] for hop in range(dp_count)]
 
-    table_rows = dp_count * part_rows + seqs
-    chunks = width // lanes
-    sublanes = -(-seq_dev // 8) * 8
-    kept, sent, last_all, partners = pl.pallas_call(
-        functools.partial(table_kernel, (seq_dev, tok_dev, where_tiles, len(tiles))),
-        out_shape=[
-            jax.ShapeDtypeStruct((table_rows, lanes), bf16),
-            jax.ShapeDtypeStruct((table_rows, lanes), bf16),
-            jax.ShapeDtypeStruct((seqs, width), bf16),
-            jax.ShapeDtypeStruct((seqs, lanes), f32),
-        ],
-        in_specs=[in_smem] + [in_vmem] * len(tiles),
-        out_specs=[in_vmem] * 4,
-        scratch_shapes=[
-            pltpu.VMEM((dp_count, chunks, sublanes, lanes), f32),
-            pltpu.VMEM((dp_count, sublanes, lanes), f32),
-            pltpu.VMEM((dp_count, sublanes, lanes), f32),
-        ],
-        compiler_params=params(48 if dp_count > 8 else 12),
-        cost_estimate=cost(0, 1 << 20),
-        name="tables",
-    )(place, *tiles)
-    found = to_lane(sent, 1)
-
     each = seqs // expert_count
     extra = each * width // part_rows
     assert extra % lanes == 0 and part_rows % (width // lanes) == 0
 
     def expert(group, place, with_last):
         near = 0 in group
-        wanted = [spot for hop in group if hop for spot in where_tiles[hop]]
-        used = sorted({spot[0] for spot in wanted})
-        sources = tuple((used.index(spot[0]), spot[1]) for spot in wanted)
+        wanted = range(dp_count) if with_last else [hop for hop in group if hop]
+        used = sorted({spot[0] for hop in wanted for spot in where_tiles[hop]})
         parts = [tiles[index] for index in used]
         n_outs = chips * len(group)
         total = n_outs * part_rows + (seqs if with_last else 0)
@@ -466,19 +467,19 @@
             wider = jax.ShapeDtypeStruct((part_rows, width + extra), bf16)
             out_shape[n_outs - chips :] = [wider] * chips
             out_shape += [
+                jax.ShapeDtypeStruct((seqs, width), bf16),
                 jax.ShapeDtypeStruct((seqs, 2 * half_width), f32),
                 jax.ShapeDtypeStruct((part_rows, extra), f32),
             ]
             scratch = [
                 pltpu.VMEM((expert_count, -(-each // 8) * 8, width), f32),
                 pltpu.VMEM((part_rows, extra), f32),
+                pltpu.VMEM((dp_count, width // lanes, -(-seq_dev // 8) * 8, lanes), f32),
             ] + scratch
-        operands = [place] + [tokens] * near + [last_all] * with_last + parts + list(weights)
+        operands = [place] + [tokens] * near + parts + list(weights)
+        layout = (tuple(group), chips, part_rows, seq_dev, where_tiles, used, with_last)
         return pl.pallas_call(
-            functools.partial(
-                expert_kernel,
-                (tuple(group), chips, part_rows, with_last, sources, len(parts)),
-            ),
+            functools.partial(expert_kernel, layout),
             out_shape=out_shape,
             in_specs=[in_smem] + [in_vmem] * (len(operands) - 1),
             out_specs=[in_vmem] * len(out_shape),
@@ -487,6 +488,37 @@
             cost_estimate=cost(2 * total * width * 6 * half_width, 12 << 20),
             name="experts",
         )(*operands)
+
+    outs = {}
+    after = place
+    for group in groups:
+        out = expert(group, after, group is groups[-1])
+        after, _ = lax.optimization_barrier((place, out[0]))
+        for index, hop in enumerate(group):
+            outs[hop] = out[index * chips : (index + 1) * chips]
+    last_all, last_projected, own_last = out[-3:]
+
+    table_rows = dp_count * part_rows + seqs
+    chunks = width // lanes
+    sublanes = -(-seq_dev // 8) * 8
+    kept, sent, partners = pl.pallas_call(
+        functools.partial(table_kernel, (seq_dev, tok_dev, where_tiles, len(tiles))),
+        out_shape=[
+            jax.ShapeDtypeStruct((table_rows, lanes), bf16),
+            jax.ShapeDtypeStruct((table_rows, lanes), bf16),
+            jax.ShapeDtypeStruct((seqs, lanes), f32),
+        ],
+        in_specs=[in_smem] + [in_vmem] * len(tiles),
+        out_specs=[in_vmem] * 3,
+        scratch_shapes=[
+            pltpu.VMEM((dp_count, sublanes, lanes), f32),
+            pltpu.VMEM((dp_count, sublanes, lanes), f32),
+        ],
+        compiler_params=params(48 if dp_count > 8 else 12),
+        cost_estimate=cost(0, 1 << 20),
+        name="tables",
+    )(after, *tiles)
+    found = to_lane(sent, 1)
 
     def combine(hop, parts, last_sum):
         with_last = last_sum is None
@@ -507,15 +539,6 @@
             name="combine",
         )(*operands)
 
-    outs = {}
-    after = place
-    for group in groups:
-        out = expert(group, after, group is groups[-1])
-        after, _ = lax.optimization_barrier((place, out[0]))
-        for index, hop in enumerate(group):
-            outs[hop] = out[index * chips : (index + 1) * chips]
-    last_projected, own_last = out[-2:]
-
     returned = {}
 
     def send_back(hop, after):
@@ -528,7 +551,9 @@
     send_back(1, [])
     before = 1
     for hop in range(dp_count - 1, 1, -1):
-        returned[before][1:], found = send_back(hop, (returned[before][1:], found))
+        returned[before][1:] = send_back(hop, returned[before][1:])
+        if hop == dp_count - 1:
+            returned[hop][1:], found = lax.optimization_barrier((returned[hop][1:], found))
         before = hop
     homeward = []
     last_sum = None
@@ -550,36 +575,22 @@
     pieces = [own_out] + [to_lane(own_out, step) for step in chip_steps]
     pieces += [to_lane(piece, 1) for piece in pieces]
 
-    block = min(512, width)
-    steps = width // block
+    n_blocks = width // min(512, width)
+    in_hbm = pl.BlockSpec(memory_space=pltpu.HBM)
     layer_out, grad_gate_up, grad_down = pl.pallas_call(
-        functools.partial(final_kernel, len(pieces)),
-        grid=(steps,),
+        functools.partial(final_kernel, len(pieces), n_blocks),
         out_shape=[
             jax.ShapeDtypeStruct((tok_dev, width), bf16),
             jax.ShapeDtypeStruct(gate_up.shape, bf16),
             jax.ShapeDtypeStruct(down.shape, bf16),
         ],
-        in_specs=[
-            *[pl.BlockSpec((part_rows, width + extra), lambda step: (0, 0))] * len(pieces),
-            pl.BlockSpec((seqs, block), lambda step: (0, step)),
-            pl.BlockSpec((seqs, 2 * half_width), lambda step: (0, 0)),
-            in_smem,
-            pl.BlockSpec((table_rows, lanes), lambda step: (0, 0)),
-            pl.BlockSpec((table_rows, lanes), lambda step: (0, 0)),
-            pl.BlockSpec((seqs, lanes), lambda step: (0, 0)),
-            pl.BlockSpec((1, half_width, width), lambda step: (0, 0, 0)),
-        ],
-        out_specs=[
-            pl.BlockSpec((tok_dev, width), lambda step: (0, 0)),
-            pl.BlockSpec((1, block, 2 * half_width), lambda step: (0, step, 0)),
-            pl.BlockSpec((1, half_width, block), lambda step: (0, 0, step)),
-        ],
+        in_specs=[in_vmem] * (len(pieces) + 2) + [in_smem] + [in_vmem] * 4,
+        out_specs=[in_hbm] * 3,
         scratch_shapes=[
-            pltpu.VMEM((steps, seqs, block), bf16),
-            pltpu.VMEM((seqs, half_width), bf16),
-            pltpu.VMEM((seqs, 2 * half_width), bf16),
+            pltpu.VMEM((width, 2 * half_width), bf16),
+            pltpu.VMEM((half_width, width), bf16),
             pltpu.VMEM((expert_count, -(-each // 8) * 8, width), f32),
+            pltpu.SemaphoreType.DMA((len(pieces) + n_blocks + 1,)),
         ],
         compiler_params=params(24),
         cost_estimate=cost(2 * seqs * width * 4 * half_width, 7 << 20),

time: 90.6 us -> 86.7 us (0.957)
  waiting for transfers between devices: 27.1 us -> 23.2 us
    ppermute x28, waiting for transfers between devices: 18.5 us -> 14.6 us  [to_lane(): lax.ppermute(value, 'expert', [(j, j ^ step) for j in range(expert_count)])]
    unnamed x8 -> x10, local copies, waits for them, and re-layouts: 3.12 us -> 3.13 us
  transfers between devices with their start and end apart: 34 -> 34, of which waited for: 14 -> 13; matrix products, arithmetic and copies ran while one was open for 2% -> 2% of each run, Pallas kernels for 18% -> 19%
where the time goes in v9:
time: 86.7 us; the launch traced here: 86.4 us
  starting transfers between devices  35.8 us (41%)
  waiting for transfers between devices  23.2 us (27%)
  Pallas kernels  21.6 us (25%)
  local copies, waits for them, and re-layouts  3.86 us (4%)
  other arithmetic  1.01 us (1%)
    ppermute x28, starting transfers between devices, to_lane(): lax.ppermute(value, 'expert', [(j, j ^ step) for j in range(expert_count)])  25.6 us
    ppermute x28, waiting for transfers between devices, to_lane(): lax.ppermute(value, 'expert', [(j, j ^ step) for j in range(expert_count)])  14.6 us
    ppermute x6, starting transfers between devices, to_plane(): return lax.ppermute(value, 'dp', [(p, p ^ step) for p in range(dp_count)])  10.2 us
    pallas_call x2, Pallas kernels, expert(): pl.pallas_call(functools.partial(expert_kernel, layout), out_shape=out_sh...  10.2 us
    ppermute x6, waiting for transfers between devices, to_plane(): return lax.ppermute(value, 'dp', [(p, p ^ step) for p in range(dp_count)])  8.62 us
    pallas_call x1, Pallas kernels, body(): pl.pallas_call(functools.partial(final_kernel, len(pieces), n_blocks), ou...  4.73 us
    unnamed x10, local copies, waits for them, and re-layouts  3.13 us
    pallas_call x4, Pallas kernels, combine(): pl.pallas_call(functools.partial(combine_kernel, (hop, chips, with_last,...  2.89 us
  transfers between devices with their start and end apart: 34, of which 13 were waited for; matrix products, arithmetic and copies ran while one was open for 2% of the time, Pallas kernels for 19%

profile of v9, /device:TPU:0, one launch (start us, length us, event | category | flops | bytes accessed | tf_op | source)
XLA Modules:
  0.0 86.4 jit_solution(15945345485214574934)
XLA Ops:
  1.2 2.3 %pack.1.refs_1_.refs_0_ = bf16[32,2176]{1,0:T(8,128)(2,1)} custom-call(s32[4]{0:T(128)} %positives.1, s32[1,256]{1,0:T(1,128)} %bitcast.5, f32[1,256]{1,0:T(1,128)} %bitcast.6, bf16[256,2048]{1,0:T(8,128)(2,1)} %refs_1_.1), custom_call_target="tpu_custom_call" | custom-call | bytes 524288 | tf_op jit(solution)/shard_map/pack/pallas_call | solution.py:408
  3.6 3.1 %collective-permute-start = (bf16[32,2176]{1,0:T(8,128)(2,1)}, bf16[32,2176]{1,0:T(8,128)(2,1)S(1)}, u32[]{:S(2)}, u32[]{:S(2)}) collective-permute-start(bf16[32,2176]{1,0:T(8,128)(2,1)} %pack.1.refs_1_.refs_0_), channel_id=1, source_target_pairs={{0,8},{8,0},{16,24},{24,16},{1,9},{9,1},{17,25},{25,17},{2,10},{10... | collective-permute-start | bytes 417800 | tf_op jit(solution)/shard_map/ppermute | solution.py:402
  6.6 2.5 %collective-permute-start.2 = (bf16[32,2176]{1,0:T(8,128)(2,1)}, bf16[32,2176]{1,0:T(8,128)(2,1)S(1)}, u32[]{:S(2)}, u32[]{:S(2)}) collective-permute-start(bf16[32,2176]{1,0:T(8,128)(2,1)} %pack.1.refs_1_.refs_0_), channel_id=1, source_target_pairs={{0,24},{8,16},{16,8},{24,0},{1,25},{9,17},{17,9},{25,1},{2,26},{10... | collective-permute-start | bytes 417800 | tf_op jit(solution)/shard_map/ppermute | solution.py:402
  10.9 2.6 %collective-permute-start.7 = (bf16[32,2304]{1,0:T(8,128)(2,1)S(1)}, bf16[32,2304]{1,0:T(8,128)(2,1)S(1)}, u32[]{:S(2)}, u32[]{:S(2)}) collective-permute-start(bf16[32,2304]{1,0:T(8,128)(2,1)S(1)} %pad_maximum_fusion.1), channel_id=1, source_target_pairs={{0,6},{1,7},{2,4},{3,5},{4,2},{5,3},{6,0},{7,1},{8,14},{9,15},{10,... | collective-permute-start | bytes 442376 | tf_op jit(solution)/shard_map/ppermute | solution.py:399
  14.5 2.4 %collective-permute-done.2.refs_7_.refs_6_ = bf16[32,2176]{1,0:T(8,128)(2,1)S(1)} collective-permute-done((bf16[32,2176]{1,0:T(8,128)(2,1)}, bf16[32,2176]{1,0:T(8,128)(2,1)S(1)}, u32[]{:S(2)}, u32[]{:S(2)}) %collective-permute-start.2) | collective-permute-done | bytes 139296 | tf_op jit(solution)/shard_map/ppermute | solution.py:402
  16.9 5.3 %collective-permute-done.1.refs_6_.refs_5_ = bf16[32,2176]{1,0:T(8,128)(2,1)} collective-permute-done((bf16[32,2176]{1,0:T(8,128)(2,1)}, bf16[32,2176]{1,0:T(8,128)(2,1)}, u32[]{:S(2)}, u32[]{:S(2)}) %collective-permute-start.1) | collective-permute-done | bytes 139296 | tf_op jit(solution)/shard_map/ppermute | solution.py:402
  22.2 0.9 %pad_maximum_fusion = bf16[64,2176]{1,0:T(8,128)(2,1)S(1)} fusion(bf16[32,2176]{1,0:T(8,128)(2,1)S(1)} %collective-permute-done.2.refs_7_.refs_6_, bf16[32,2176]{1,0:T(8,128)(2,1)} %collective-permute-done.1.refs_6_.refs_5_), kind=kLoop, calls=%fused_computation | loop fusion | flops 557056 | bytes 557056 | tf_op jit(solution)/shard_map/concatenate | solution.py:435
  23.1 2.5 %collective-permute-start.10 = (bf16[64,2176]{1,0:T(8,128)(2,1)S(1)}, bf16[64,2176]{1,0:T(8,128)(2,1)S(1)}, u32[]{:S(2)}, u32[]{:S(2)}) collective-permute-start(bf16[64,2176]{1,0:T(8,128)(2,1)S(1)} %pad_maximum_fusion), channel_id=1, source_target_pairs={{0,6},{1,7},{2,4},{3,5},{4,2},{5,3},{6,0},{7,1},{8,14},{9,15},{10,... | collective-permute-start | bytes 835592 | tf_op jit(solution)/shard_map/ppermute | solution.py:399
  26.8 1.9 %copy-done.1 = bf16[1,2048,768]{2,1,0:T(8,128)(2,1)S(1)} copy-done((bf16[1,2048,768]{2,1,0:T(8,128)(2,1)S(1)}, bf16[1,2048,768]{2,1,0:T(8,128)(2,1)}, u32[]{:S(2)}) %copy-start.1) | copy-done | bytes 3145752
  28.6 1.2 %copy-done.3 = bf16[256,2048]{1,0:T(8,128)(2,1)S(1)} copy-done((bf16[256,2048]{1,0:T(8,128)(2,1)S(1)}, bf16[256,2048]{1,0:T(8,128)(2,1)}, u32[]{:S(2)}) %copy-start.3) | copy-done | bytes 1048600
  29.9 5.0 %experts.2 = (bf16[32,2048]{1,0:T(8,128)(2,1)S(1)}, bf16[32,2048]{1,0:T(8,128)(2,1)S(1)}, bf16[32,2048]{1,0:T(8,128)(2,1)S(1)}, bf16[32,2048]{1,0:T(8,128)(2,1)S...) custom-call(s32[3]{0:T(128)S(1)} %pad_add_fusion.refs_0_.place.refs_, ...), custom_call_target="tpu_custom_call" | custom-call | flops 2415919104 | bytes 12582912 | tf_op jit(solution)/shard_map/experts/pallas_call | solution.py:481
  34.9 1.6 %collective-permute-start.11 = (bf16[32,2048]{1,0:T(8,128)(2,1)S(1)}, bf16[32,2048]{1,0:T(8,128)(2,1)S(1)}, u32[]{:S(2)}, u32[]{:S(2)}) collective-permute-start(bf16[32,2048]{1,0:T(8,128)(2,1)S(1)} %get-tuple-element.80), channel_id=1, source_target_pairs={{0,2},{1,3},{2,0},{3,1},{4,6},{5,7},{6,4},{7,5},{8,10},{9,11},{10,... | collective-permute-start | bytes 393224 | tf_op jit(solution)/shard_map/ppermute | solution.py:399
  36.4 1.5 %collective-permute-start.12 = (bf16[32,2048]{1,0:T(8,128)(2,1)S(1)}, bf16[32,2048]{1,0:T(8,128)(2,1)S(1)}, u32[]{:S(2)}, u32[]{:S(2)}) collective-permute-start(bf16[32,2048]{1,0:T(8,128)(2,1)S(1)} %get-tuple-element.81), channel_id=1, source_target_pairs={{0,4},{1,5},{2,6},{3,7},{4,0},{5,1},{6,2},{7,3},{8,12},{9,13},{10,... | collective-permute-start | bytes 393224 | tf_op jit(solution)/shard_map/ppermute | solution.py:399
  38.4 1.3 %collective-permute-done.8.refs_8_.refs_7_ = bf16[64,2176]{1,0:T(8,128)(2,1)S(1)} collective-permute-done((bf16[64,2176]{1,0:T(8,128)(2,1)S(1)}, bf16[64,2176]{1,0:T(8,128)(2,1)S(1)}, u32[]{:S(2)}, u32[]{:S(2)}) %collective-permute-start.8) | collective-permute-done | bytes 278560 | tf_op jit(solution)/shard_map/ppermute | solution.py:399
  39.8 5.2 %experts.3 = (bf16[32,2048]{1,0:T(8,128)(2,1)S(1)}, bf16[32,2048]{1,0:T(8,128)(2,1)S(1)}, bf16[32,2048]{1,0:T(8,128)(2,1)S(1)}, bf16[32,2048]{1,0:T(8,128)(2,1)S...) custom-call(s32[3]{0:T(128)S(1)} %pad_add_fusion.refs_0_.place.refs_, ...), custom_call_target="tpu_custom_call" | custom-call | flops 2566914048 | bytes 12582912 | tf_op jit(solution)/shard_map/experts/pallas_call | solution.py:481
  44.9 1.5 %collective-permute-start.14 = (bf16[32,2176]{1,0:T(8,128)(2,1)S(1)}, bf16[32,2176]{1,0:T(8,128)(2,1)S(1)}, u32[]{:S(2)}, u32[]{:S(2)}) collective-permute-start(bf16[32,2176]{1,0:T(8,128)(2,1)S(1)} %get-tuple-element.83), channel_id=1, source_target_pairs={{0,2},{1,3},{2,0},{3,1},{4,6},{5,7},{6,4},{7,5},{8,10},{9,11},{10,... | collective-permute-start | bytes 417800 | tf_op jit(solution)/shard_map/ppermute | solution.py:399
  46.8 1.8 %collective-permute-start.16 = (bf16[32,2176]{1,0:T(8,128)(2,1)S(1)}, bf16[32,2176]{1,0:T(8,128)(2,1)S(1)}, u32[]{:S(2)}, u32[]{:S(2)}) collective-permute-start(bf16[32,2176]{1,0:T(8,128)(2,1)S(1)} %get-tuple-element.85), channel_id=1, source_target_pairs={{0,6},{1,7},{2,4},{3,5},{4,2},{5,3},{6,0},{7,1},{8,14},{9,15},{10,... | collective-permute-start | bytes 417800 | tf_op jit(solution)/shard_map/ppermute | solution.py:399
  48.5 1.4 %tables.1 = (bf16[144,128]{1,0:T(8,128)(2,1)S(1)}, bf16[144,128]{1,0:T(8,128)(2,1)S(1)}, f32[16,128]{1,0:T(8,128)S(1)}) custom-call(s32[3]{0:T(128)S(1)} %pad_add_fusion.refs_0_.place.refs_10_, bf16[32,2176]{1,0:T(8,128)(2,1)S(1)} %copy-done.4, bf16[32,2176]{1,0:T(8,128)(2,1)S(1)} %collective-permute-done.refs_2_.refs_1_, ...), custom_call_target="tpu_custom_call" | custom-call | bytes 1048576 | tf_op jit(solution)/shard_map/tables/pallas_call | solution.py:504
  50.0 1.2 %collective-permute-done.17.found.refs_12_ = bf16[144,128]{1,0:T(8,128)(2,1)S(1)} collective-permute-done((bf16[144,128]{1,0:T(8,128)(2,1)S(1)}, bf16[144,128]{1,0:T(8,128)(2,1)S(1)}, u32[]{:S(2)}, u32[]{:S(2)}) %collective-permute-start.17) | collective-permute-done | bytes 36896 | tf_op jit(solution)/shard_map/ppermute | solution.py:399
  51.2 2.3 %collective-permute-done.15.refs_2_ = bf16[32,2176]{1,0:T(8,128)(2,1)S(1)} collective-permute-done((bf16[32,2176]{1,0:T(8,128)(2,1)S(1)}, bf16[32,2176]{1,0:T(8,128)(2,1)S(1)}, u32[]{:S(2)}, u32[]{:S(2)}) %collective-permute-start.15) | collective-permute-done | bytes 139296 | tf_op jit(solution)/shard_map/ppermute | solution.py:399
  53.5 1.0 %collective-permute-start.22 = (bf16[32,2048]{1,0:T(8,128)(2,1)S(1)}, bf16[32,2048]{1,0:T(8,128)(2,1)S(1)}, u32[]{:S(2)}, u32[]{:S(2)}) collective-permute-start(bf16[32,2048]{1,0:T(8,128)(2,1)S(1)} %get-tuple-element.107), channel_id=1, source_target_pairs={{0,2},{1,3},{2,0},{3,1},{4,6},{5,7},{6,4},{7,5},{8,10},{9,11},{10,... | collective-permute-start | bytes 393224 | tf_op jit(solution)/shard_map/ppermute | solution.py:399
  55.0 2.0 %collective-permute-start.24 = (bf16[32,2048]{1,0:T(8,128)(2,1)S(1)}, bf16[32,2048]{1,0:T(8,128)(2,1)S(1)}, u32[]{:S(2)}, u32[]{:S(2)}) collective-permute-start(bf16[32,2048]{1,0:T(8,128)(2,1)S(1)} %get-tuple-element.109), channel_id=1, source_target_pairs={{0,6},{1,7},{2,4},{3,5},{4,2},{5,3},{6,0},{7,1},{8,14},{9,15},{10,... | collective-permute-start | bytes 393224 | tf_op jit(solution)/shard_map/ppermute | solution.py:399
  57.0 1.0 %collective-permute-start.18 = (bf16[32,2048]{1,0:T(8,128)(2,1)S(1)}, bf16[32,2048]{1,0:T(8,128)(2,1)S(1)}, u32[]{:S(2)}, u32[]{:S(2)}) collective-permute-start(bf16[32,2048]{1,0:T(8,128)(2,1)S(1)} %get-tuple-element.91), channel_id=1, source_target_pairs={{0,2},{1,3},{2,0},{3,1},{4,6},{5,7},{6,4},{7,5},{8,10},{9,11},{10,... | collective-permute-start | bytes 393224 | tf_op jit(solution)/shard_map/ppermute | solution.py:399
  58.8 2.5 %collective-permute-start.21 = (bf16[32,2176]{1,0:T(8,128)(2,1)S(1)}, bf16[32,2176]{1,0:T(8,128)(2,1)S(1)}, u32[]{:S(2)}, u32[]{:S(2)}) collective-permute-start(bf16[32,2176]{1,0:T(8,128)(2,1)S(1)} %get-tuple-element.106), channel_id=1, source_target_pairs={{0,24},{8,16},{16,8},{24,0},{1,25},{9,17},{17,9},{25,1},{2,26},{10... | collective-permute-start | bytes 417800 | tf_op jit(solution)/shard_map/ppermute | solution.py:402
  62.8 2.0 %collective-permute-start.25 = (bf16[32,2176]{1,0:T(8,128)(2,1)S(1)}, bf16[32,2176]{1,0:T(8,128)(2,1)S(1)}, u32[]{:S(2)}, u32[]{:S(2)}) collective-permute-start(bf16[32,2176]{1,0:T(8,128)(2,1)S(1)} %combine.6), channel_id=1, source_target_pairs={{0,16},{8,24},{16,0},{24,8},{1,17},{9,25},{17,1},{25,9},{2,18},{10... | collective-permute-start | bytes 417800 | tf_op jit(solution)/shard_map/ppermute | solution.py:402
  65.3 2.0 %collective-permute-start.20 = (bf16[32,2048]{1,0:T(8,128)(2,1)S(1)}, bf16[32,2048]{1,0:T(8,128)(2,1)S(1)}, u32[]{:S(2)}, u32[]{:S(2)}) collective-permute-start(bf16[32,2048]{1,0:T(8,128)(2,1)S(1)} %get-tuple-element.93), channel_id=1, source_target_pairs={{0,6},{1,7},{2,4},{3,5},{4,2},{5,3},{6,0},{7,1},{8,14},{9,15},{10,... | collective-permute-start | bytes 393224 | tf_op jit(solution)/shard_map/ppermute | solution.py:399
  67.3 2.5 %collective-permute-done.19.refs_3_ = bf16[32,2048]{1,0:T(8,128)(2,1)S(1)} collective-permute-done((bf16[32,2048]{1,0:T(8,128)(2,1)S(1)}, bf16[32,2048]{1,0:T(8,128)(2,1)S(1)}, u32[]{:S(2)}, u32[]{:S(2)}) %collective-permute-start.19) | collective-permute-done | bytes 131104 | tf_op jit(solution)/shard_map/ppermute | solution.py:399
  69.8 1.4 %collective-permute-done.20.refs_4_ = bf16[32,2048]{1,0:T(8,128)(2,1)S(1)} collective-permute-done((bf16[32,2048]{1,0:T(8,128)(2,1)S(1)}, bf16[32,2048]{1,0:T(8,128)(2,1)S(1)}, u32[]{:S(2)}, u32[]{:S(2)}) %collective-permute-start.20) | collective-permute-done | bytes 131104 | tf_op jit(solution)/shard_map/ppermute | solution.py:399
  72.0 2.4 %collective-permute-start.29 = (bf16[32,2176]{1,0:T(8,128)(2,1)S(1)}, bf16[32,2176]{1,0:T(8,128)(2,1)S(1)}, u32[]{:S(2)}, u32[]{:S(2)}) collective-permute-start(bf16[32,2176]{1,0:T(8,128)(2,1)S(1)} %finish.1.refs_0_), channel_id=1, source_target_pairs={{0,6},{1,7},{2,4},{3,5},{4,2},{5,3},{6,0},{7,1},{8,14},{9,15},{10,... | collective-permute-start | bytes 417800 | tf_op jit(solution)/shard_map/ppermute | solution.py:399
  75.8 2.3 %collective-permute-done.29.refs_3_ = bf16[32,2176]{1,0:T(8,128)(2,1)S(1)} collective-permute-done((bf16[32,2176]{1,0:T(8,128)(2,1)S(1)}, bf16[32,2176]{1,0:T(8,128)(2,1)S(1)}, u32[]{:S(2)}, u32[]{:S(2)}) %collective-permute-start.29) | collective-permute-done | bytes 139296 | tf_op jit(solution)/shard_map/ppermute | solution.py:399
  78.1 1.5 %collective-permute-done.28.refs_2_ = bf16[32,2176]{1,0:T(8,128)(2,1)S(1)} collective-permute-done((bf16[32,2176]{1,0:T(8,128)(2,1)S(1)}, bf16[32,2176]{1,0:T(8,128)(2,1)S(1)}, u32[]{:S(2)}, u32[]{:S(2)}) %collective-permute-start.28) | collective-permute-done | bytes 139296 | tf_op jit(solution)/shard_map/ppermute | solution.py:399
  81.6 4.7 %final.1 = (bf16[256,2048]{1,0:T(8,128)(2,1)}, bf16[1,2048,768]{2,1,0:T(8,128)(2,1)}, bf16[1,384,2048]{2,1,0:T(8,128)(2,1)}) custom-call(bf16[32,2176]{1,0:T(8,128)(2,1)S(1)} %finish.1.refs_0_, bf16[32,2176]{1,0:T(8,128)(2,1)S(1)} %collective-permute-done.27.refs_1_, bf16[32,2176]{1,0:T(8,128)(2,1)S(1)} %collective-permute-done.28.refs_2_, ...), custom_call_target="tpu_custom_call" | custom-call | flops 100663296 | bytes 7340032 | tf_op jit(solution)/shard_map/final/pallas_call | solution.py:580
  (60 shorter events, 12.8 us)
Async XLA Ops:
  0.6 10.3 %collective-permute-start.3 = (bf16[1,2048,768]{2,1,0:T(8,128)(2,1)}, bf16[1,2048,768]{2,1,0:T(8,128)(2,1)}, u32[]{:S(2)}, u32[]{:S(2)}) collective-permute-start(bf16[1,2048,768]{2,1,0:T(8,128)(2,1)} %refs_11_), channel_id=1, source_target_pairs={{0,1},{1,0},{2,3},{3,2},{4,5},{5,4},{6,7},{7,6},{8,9},{9,8},{10,11... | collective-permute-start | bytes 9437192 | tf_op jit(solution)/shard_map/ppermute | solution.py:399
  1.2 9.7 %collective-permute-start.4 = (bf16[1,384,2048]{2,1,0:T(8,128)(2,1)}, bf16[1,384,2048]{2,1,0:T(8,128)(2,1)S(1)}, u32[]{:S(2)}, u32[]{:S(2)}) collective-permute-start(bf16[1,384,2048]{2,1,0:T(8,128)(2,1)} %refs_14_.1), channel_id=1, source_target_pairs={{0,1},{1,0},{2,3},{3,2},{4,5},{5,4},{6,7},{7,6},{8,9},{9,8},{10,11... | collective-permute-start | bytes 4718600 | tf_op jit(solution)/shard_map/ppermute | solution.py:399
  3.6 7.3 %collective-permute-start = (bf16[32,2176]{1,0:T(8,128)(2,1)}, bf16[32,2176]{1,0:T(8,128)(2,1)S(1)}, u32[]{:S(2)}, u32[]{:S(2)}) collective-permute-start(bf16[32,2176]{1,0:T(8,128)(2,1)} %pack.1.refs_1_.refs_0_), channel_id=1, source_target_pairs={{0,8},{8,0},{16,24},{24,16},{1,9},{9,1},{17,25},{25,17},{2,10},{10... | collective-permute-start | bytes 417800 | tf_op jit(solution)/shard_map/ppermute | solution.py:402
  6.6 10.3 %collective-permute-start.2 = (bf16[32,2176]{1,0:T(8,128)(2,1)}, bf16[32,2176]{1,0:T(8,128)(2,1)S(1)}, u32[]{:S(2)}, u32[]{:S(2)}) collective-permute-start(bf16[32,2176]{1,0:T(8,128)(2,1)} %pack.1.refs_1_.refs_0_), channel_id=1, source_target_pairs={{0,24},{8,16},{16,8},{24,0},{1,25},{9,17},{17,9},{25,1},{2,26},{10... | collective-permute-start | bytes 417800 | tf_op jit(solution)/shard_map/ppermute | solution.py:402
  9.1 13.1 %collective-permute-start.1 = (bf16[32,2176]{1,0:T(8,128)(2,1)}, bf16[32,2176]{1,0:T(8,128)(2,1)}, u32[]{:S(2)}, u32[]{:S(2)}) collective-permute-start(bf16[32,2176]{1,0:T(8,128)(2,1)} %pack.1.refs_1_.refs_0_), channel_id=1, source_target_pairs={{0,16},{8,24},{16,0},{24,8},{1,17},{9,25},{17,1},{25,9},{2,18},{10... | collective-permute-start | bytes 417800 | tf_op jit(solution)/shard_map/ppermute | solution.py:402
  10.9 12.2 %collective-permute-start.7 = (bf16[32,2304]{1,0:T(8,128)(2,1)S(1)}, bf16[32,2304]{1,0:T(8,128)(2,1)S(1)}, u32[]{:S(2)}, u32[]{:S(2)}) collective-permute-start(bf16[32,2304]{1,0:T(8,128)(2,1)S(1)} %pad_maximum_fusion.1), channel_id=1, source_target_pairs={{0,6},{1,7},{2,4},{3,5},{4,2},{5,3},{6,0},{7,1},{8,14},{9,15},{10,... | collective-permute-start | bytes 442376 | tf_op jit(solution)/shard_map/ppermute | solution.py:399
  13.5 9.6 %collective-permute-start.6 = (bf16[32,2304]{1,0:T(8,128)(2,1)S(1)}, bf16[32,2304]{1,0:T(8,128)(2,1)S(1)}, u32[]{:S(2)}, u32[]{:S(2)}) collective-permute-start(bf16[32,2304]{1,0:T(8,128)(2,1)S(1)} %pad_maximum_fusion.1), channel_id=1, source_target_pairs={{0,4},{1,5},{2,6},{3,7},{4,0},{5,1},{6,2},{7,3},{8,12},{9,13},{10,... | collective-permute-start | bytes 442376 | tf_op jit(solution)/shard_map/ppermute | solution.py:399
  14.0 9.1 %collective-permute-start.5 = (bf16[32,2304]{1,0:T(8,128)(2,1)S(1)}, bf16[32,2304]{1,0:T(8,128)(2,1)S(1)}, u32[]{:S(2)}, u32[]{:S(2)}) collective-permute-start(bf16[32,2304]{1,0:T(8,128)(2,1)S(1)} %pad_maximum_fusion.1), channel_id=1, source_target_pairs={{0,2},{1,3},{2,0},{3,1},{4,6},{5,7},{6,4},{7,5},{8,10},{9,11},{10,... | collective-permute-start | bytes 442376 | tf_op jit(solution)/shard_map/ppermute | solution.py:399
  23.1 14.8 %collective-permute-start.10 = (bf16[64,2176]{1,0:T(8,128)(2,1)S(1)}, bf16[64,2176]{1,0:T(8,128)(2,1)S(1)}, u32[]{:S(2)}, u32[]{:S(2)}) collective-permute-start(bf16[64,2176]{1,0:T(8,128)(2,1)S(1)} %pad_maximum_fusion), channel_id=1, source_target_pairs={{0,6},{1,7},{2,4},{3,5},{4,2},{5,3},{6,0},{7,1},{8,14},{9,15},{10,... | collective-permute-start | bytes 835592 | tf_op jit(solution)/shard_map/ppermute | solution.py:399
  25.6 12.8 %collective-permute-start.9 = (bf16[64,2176]{1,0:T(8,128)(2,1)S(1)}, bf16[64,2176]{1,0:T(8,128)(2,1)S(1)}, u32[]{:S(2)}, u32[]{:S(2)}) collective-permute-start(bf16[64,2176]{1,0:T(8,128)(2,1)S(1)} %pad_maximum_fusion), channel_id=1, source_target_pairs={{0,4},{1,5},{2,6},{3,7},{4,0},{5,1},{6,2},{7,3},{8,12},{9,13},{10,... | collective-permute-start | bytes 835592 | tf_op jit(solution)/shard_map/ppermute | solution.py:399
  26.1 13.6 %collective-permute-start.8 = (bf16[64,2176]{1,0:T(8,128)(2,1)S(1)}, bf16[64,2176]{1,0:T(8,128)(2,1)S(1)}, u32[]{:S(2)}, u32[]{:S(2)}) collective-permute-start(bf16[64,2176]{1,0:T(8,128)(2,1)S(1)} %pad_maximum_fusion), channel_id=1, source_target_pairs={{0,2},{1,3},{2,0},{3,1},{4,6},{5,7},{6,4},{7,5},{8,10},{9,11},{10,... | collective-permute-start | bytes 835592 | tf_op jit(solution)/shard_map/ppermute | solution.py:399
  34.9 10.0 %collective-permute-start.11 = (bf16[32,2048]{1,0:T(8,128)(2,1)S(1)}, bf16[32,2048]{1,0:T(8,128)(2,1)S(1)}, u32[]{:S(2)}, u32[]{:S(2)}) collective-permute-start(bf16[32,2048]{1,0:T(8,128)(2,1)S(1)} %get-tuple-element.80), channel_id=1, source_target_pairs={{0,2},{1,3},{2,0},{3,1},{4,6},{5,7},{6,4},{7,5},{8,10},{9,11},{10,... | collective-permute-start | bytes 393224 | tf_op jit(solution)/shard_map/ppermute | solution.py:399
  36.4 8.5 %collective-permute-start.12 = (bf16[32,2048]{1,0:T(8,128)(2,1)S(1)}, bf16[32,2048]{1,0:T(8,128)(2,1)S(1)}, u32[]{:S(2)}, u32[]{:S(2)}) collective-permute-start(bf16[32,2048]{1,0:T(8,128)(2,1)S(1)} %get-tuple-element.81), channel_id=1, source_target_pairs={{0,4},{1,5},{2,6},{3,7},{4,0},{5,1},{6,2},{7,3},{8,12},{9,13},{10,... | collective-permute-start | bytes 393224 | tf_op jit(solution)/shard_map/ppermute | solution.py:399
  38.0 7.0 %collective-permute-start.13 = (bf16[32,2048]{1,0:T(8,128)(2,1)S(1)}, bf16[32,2048]{1,0:T(8,128)(2,1)S(1)}, u32[]{:S(2)}, u32[]{:S(2)}) collective-permute-start(bf16[32,2048]{1,0:T(8,128)(2,1)S(1)} %get-tuple-element.82), channel_id=1, source_target_pairs={{0,6},{1,7},{2,4},{3,5},{4,2},{5,3},{6,0},{7,1},{8,14},{9,15},{10,... | collective-permute-start | bytes 393224 | tf_op jit(solution)/shard_map/ppermute | solution.py:399
  44.9 6.3 %collective-permute-start.14 = (bf16[32,2176]{1,0:T(8,128)(2,1)S(1)}, bf16[32,2176]{1,0:T(8,128)(2,1)S(1)}, u32[]{:S(2)}, u32[]{:S(2)}) collective-permute-start(bf16[32,2176]{1,0:T(8,128)(2,1)S(1)} %get-tuple-element.83), channel_id=1, source_target_pairs={{0,2},{1,3},{2,0},{3,1},{4,6},{5,7},{6,4},{7,5},{8,10},{9,11},{10,... | collective-permute-start | bytes 417800 | tf_op jit(solution)/shard_map/ppermute | solution.py:399
  46.5 7.1 %collective-permute-start.15 = (bf16[32,2176]{1,0:T(8,128)(2,1)S(1)}, bf16[32,2176]{1,0:T(8,128)(2,1)S(1)}, u32[]{:S(2)}, u32[]{:S(2)}) collective-permute-start(bf16[32,2176]{1,0:T(8,128)(2,1)S(1)} %get-tuple-element.84), channel_id=1, source_target_pairs={{0,4},{1,5},{2,6},{3,7},{4,0},{5,1},{6,2},{7,3},{8,12},{9,13},{10,... | collective-permute-start | bytes 417800 | tf_op jit(solution)/shard_map/ppermute | solution.py:399
  46.8 6.8 %collective-permute-start.16 = (bf16[32,2176]{1,0:T(8,128)(2,1)S(1)}, bf16[32,2176]{1,0:T(8,128)(2,1)S(1)}, u32[]{:S(2)}, u32[]{:S(2)}) collective-permute-start(bf16[32,2176]{1,0:T(8,128)(2,1)S(1)} %get-tuple-element.85), channel_id=1, source_target_pairs={{0,6},{1,7},{2,4},{3,5},{4,2},{5,3},{6,0},{7,1},{8,14},{9,15},{10,... | collective-permute-start | bytes 417800 | tf_op jit(solution)/shard_map/ppermute | solution.py:399
  53.5 8.5 %collective-permute-start.22 = (bf16[32,2048]{1,0:T(8,128)(2,1)S(1)}, bf16[32,2048]{1,0:T(8,128)(2,1)S(1)}, u32[]{:S(2)}, u32[]{:S(2)}) collective-permute-start(bf16[32,2048]{1,0:T(8,128)(2,1)S(1)} %get-tuple-element.107), channel_id=1, source_target_pairs={{0,2},{1,3},{2,0},{3,1},{4,6},{5,7},{6,4},{7,5},{8,10},{9,11},{10,... | collective-permute-start | bytes 393224 | tf_op jit(solution)/shard_map/ppermute | solution.py:399
  54.6 7.6 %collective-permute-start.23 = (bf16[32,2048]{1,0:T(8,128)(2,1)S(1)}, bf16[32,2048]{1,0:T(8,128)(2,1)S(1)}, u32[]{:S(2)}, u32[]{:S(2)}) collective-permute-start(bf16[32,2048]{1,0:T(8,128)(2,1)S(1)} %get-tuple-element.108), channel_id=1, source_target_pairs={{0,4},{1,5},{2,6},{3,7},{4,0},{5,1},{6,2},{7,3},{8,12},{9,13},{10,... | collective-permute-start | bytes 393224 | tf_op jit(solution)/shard_map/ppermute | solution.py:399
  55.0 7.1 %collective-permute-start.24 = (bf16[32,2048]{1,0:T(8,128)(2,1)S(1)}, bf16[32,2048]{1,0:T(8,128)(2,1)S(1)}, u32[]{:S(2)}, u32[]{:S(2)}) collective-permute-start(bf16[32,2048]{1,0:T(8,128)(2,1)S(1)} %get-tuple-element.109), channel_id=1, source_target_pairs={{0,6},{1,7},{2,4},{3,5},{4,2},{5,3},{6,0},{7,1},{8,14},{9,15},{10,... | collective-permute-start | bytes 393224 | tf_op jit(solution)/shard_map/ppermute | solution.py:399
  57.0 8.3 %collective-permute-start.18 = (bf16[32,2048]{1,0:T(8,128)(2,1)S(1)}, bf16[32,2048]{1,0:T(8,128)(2,1)S(1)}, u32[]{:S(2)}, u32[]{:S(2)}) collective-permute-start(bf16[32,2048]{1,0:T(8,128)(2,1)S(1)} %get-tuple-element.91), channel_id=1, source_target_pairs={{0,2},{1,3},{2,0},{3,1},{4,6},{5,7},{6,4},{7,5},{8,10},{9,11},{10,... | collective-permute-start | bytes 393224 | tf_op jit(solution)/shard_map/ppermute | solution.py:399
  58.8 13.2 %collective-permute-start.21 = (bf16[32,2176]{1,0:T(8,128)(2,1)S(1)}, bf16[32,2176]{1,0:T(8,128)(2,1)S(1)}, u32[]{:S(2)}, u32[]{:S(2)}) collective-permute-start(bf16[32,2176]{1,0:T(8,128)(2,1)S(1)} %get-tuple-element.106), channel_id=1, source_target_pairs={{0,24},{8,16},{16,8},{24,0},{1,25},{9,17},{17,9},{25,1},{2,26},{10... | collective-permute-start | bytes 417800 | tf_op jit(solution)/shard_map/ppermute | solution.py:402
  62.0 9.9 %collective-permute-start.26 = (bf16[32,2176]{1,0:T(8,128)(2,1)S(1)}, bf16[32,2176]{1,0:T(8,128)(2,1)S(1)}, u32[]{:S(2)}, u32[]{:S(2)}) collective-permute-start(bf16[32,2176]{1,0:T(8,128)(2,1)S(1)} %combine.7), channel_id=1, source_target_pairs={{0,8},{8,0},{16,24},{24,16},{1,9},{9,1},{17,25},{25,17},{2,10},{10... | collective-permute-start | bytes 417800 | tf_op jit(solution)/shard_map/ppermute | solution.py:402
  62.8 9.1 %collective-permute-start.25 = (bf16[32,2176]{1,0:T(8,128)(2,1)S(1)}, bf16[32,2176]{1,0:T(8,128)(2,1)S(1)}, u32[]{:S(2)}, u32[]{:S(2)}) collective-permute-start(bf16[32,2176]{1,0:T(8,128)(2,1)S(1)} %combine.6), channel_id=1, source_target_pairs={{0,16},{8,24},{16,0},{24,8},{1,17},{9,25},{17,1},{25,9},{2,18},{10... | collective-permute-start | bytes 417800 | tf_op jit(solution)/shard_map/ppermute | solution.py:402
  64.8 5.0 %collective-permute-start.19 = (bf16[32,2048]{1,0:T(8,128)(2,1)S(1)}, bf16[32,2048]{1,0:T(8,128)(2,1)S(1)}, u32[]{:S(2)}, u32[]{:S(2)}) collective-permute-start(bf16[32,2048]{1,0:T(8,128)(2,1)S(1)} %get-tuple-element.92), channel_id=1, source_target_pairs={{0,4},{1,5},{2,6},{3,7},{4,0},{5,1},{6,2},{7,3},{8,12},{9,13},{10,... | collective-permute-start | bytes 393224 | tf_op jit(solution)/shard_map/ppermute | solution.py:399
  65.3 5.9 %collective-permute-start.20 = (bf16[32,2048]{1,0:T(8,128)(2,1)S(1)}, bf16[32,2048]{1,0:T(8,128)(2,1)S(1)}, u32[]{:S(2)}, u32[]{:S(2)}) collective-permute-start(bf16[32,2048]{1,0:T(8,128)(2,1)S(1)} %get-tuple-element.93), channel_id=1, source_target_pairs={{0,6},{1,7},{2,4},{3,5},{4,2},{5,3},{6,0},{7,1},{8,14},{9,15},{10,... | collective-permute-start | bytes 393224 | tf_op jit(solution)/shard_map/ppermute | solution.py:399
  72.0 6.0 %collective-permute-start.29 = (bf16[32,2176]{1,0:T(8,128)(2,1)S(1)}, bf16[32,2176]{1,0:T(8,128)(2,1)S(1)}, u32[]{:S(2)}, u32[]{:S(2)}) collective-permute-start(bf16[32,2176]{1,0:T(8,128)(2,1)S(1)} %finish.1.refs_0_), channel_id=1, source_target_pairs={{0,6},{1,7},{2,4},{3,5},{4,2},{5,3},{6,0},{7,1},{8,14},{9,15},{10,... | collective-permute-start | bytes 417800 | tf_op jit(solution)/shard_map/ppermute | solution.py:399
  74.4 5.1 %collective-permute-start.28 = (bf16[32,2176]{1,0:T(8,128)(2,1)S(1)}, bf16[32,2176]{1,0:T(8,128)(2,1)S(1)}, u32[]{:S(2)}, u32[]{:S(2)}) collective-permute-start(bf16[32,2176]{1,0:T(8,128)(2,1)S(1)} %finish.1.refs_0_), channel_id=1, source_target_pairs={{0,4},{1,5},{2,6},{3,7},{4,0},{5,1},{6,2},{7,3},{8,12},{9,13},{10,... | collective-permute-start | bytes 417800 | tf_op jit(solution)/shard_map/ppermute | solution.py:399
  75.2 5.1 %collective-permute-start.27 = (bf16[32,2176]{1,0:T(8,128)(2,1)S(1)}, bf16[32,2176]{1,0:T(8,128)(2,1)S(1)}, u32[]{:S(2)}, u32[]{:S(2)}) collective-permute-start(bf16[32,2176]{1,0:T(8,128)(2,1)S(1)} %finish.1.refs_0_), channel_id=1, source_target_pairs={{0,2},{1,3},{2,0},{3,1},{4,6},{5,7},{6,4},{7,5},{8,10},{9,11},{10,... | collective-permute-start | bytes 417800 | tf_op jit(solution)/shard_map/ppermute | solution.py:399
  75.8 4.5 %collective-permute-start.30 = (bf16[32,2176]{1,0:T(8,128)(2,1)S(1)}, bf16[32,2176]{1,0:T(8,128)(2,1)S(1)}, u32[]{:S(2)}, u32[]{:S(2)}) collective-permute-start(bf16[32,2176]{1,0:T(8,128)(2,1)S(1)} %finish.1.refs_0_), channel_id=1, source_target_pairs={{0,1},{1,0},{2,3},{3,2},{4,5},{5,4},{6,7},{7,6},{8,9},{9,8},{10,11... | collective-permute-start | bytes 417800 | tf_op jit(solution)/shard_map/ppermute | solution.py:399
  78.0 2.2 %collective-permute-start.33 = (bf16[32,2176]{1,0:T(8,128)(2,1)S(1)}, bf16[32,2176]{1,0:T(8,128)(2,1)S(1)}, u32[]{:S(2)}, u32[]{:S(2)}) collective-permute-start(bf16[32,2176]{1,0:T(8,128)(2,1)S(1)} %collective-permute-done.29.refs_3_), channel_id=1, source_target_pairs={{0,1},{1,0},{2,3},{3,2},{4,5},{5,4},{6,7},{7,6},{8,9},{9,8},{10,11... | collective-permute-start | bytes 417800 | tf_op jit(solution)/shard_map/ppermute | solution.py:399
  79.5 1.4 %collective-permute-start.32 = (bf16[32,2176]{1,0:T(8,128)(2,1)S(1)}, bf16[32,2176]{1,0:T(8,128)(2,1)S(1)}, u32[]{:S(2)}, u32[]{:S(2)}) collective-permute-start(bf16[32,2176]{1,0:T(8,128)(2,1)S(1)} %collective-permute-done.28.refs_2_), channel_id=1, source_target_pairs={{0,1},{1,0},{2,3},{3,2},{4,5},{5,4},{6,7},{7,6},{8,9},{9,8},{10,11... | collective-permute-start | bytes 417800 | tf_op jit(solution)/shard_map/ppermute | solution.py:399
  (7 other events, 51.6 us)

commit v10 on v9

--- a/solution.py
+++ b/solution.py
@@ -15,7 +15,7 @@
 bf16 = jnp.bfloat16
 f32 = jnp.float32
 
-anywhere = pl.BlockSpec(memory_space=pl.ANY)
+in_hbm = pl.BlockSpec(memory_space=pltpu.HBM)
 in_vmem = pl.BlockSpec(memory_space=pltpu.VMEM)
 in_smem = pl.BlockSpec(memory_space=pltpu.SMEM)
 
@@ -45,7 +45,7 @@
     return jnp.sum(jnp.where(index == wanted, table, 0.0), axis=1, keepdims=True)
 
 
-def pack_kernel(seq_dev, positives, ids, gates, tokens, out, tile, rows, sems):
+def pack_kernel(seq_dev, positives, ids_in, gates_in, tokens, out, tile, rows, ids, gates, sems):
     part_rows, width = out.shape[0], tokens.shape[1]
     tok_dev = tokens.shape[0]
     seq_length = tok_dev // seq_dev
@@ -64,11 +64,16 @@
     own = pltpu.make_async_copy(
         tokens.at[pl.ds(start, part_rows)], out.at[:, pl.ds(0, width)], sems.at[seq_dev]
     )
-    own.start()
-    for copy in copies:
+    lines = [
+        pltpu.make_async_copy(ids_in, ids, sems.at[seq_dev + 1]),
+        pltpu.make_async_copy(gates_in, gates, sems.at[seq_dev + 2]),
+    ]
+    for copy in lines + [own] + copies:
         copy.start()
     note_rows = tok_dev // lanes
     tile[...] = jnp.zeros_like(tile)
+    for copy in lines:
+        copy.wait()
     for index in range(note_rows):
         block = slice(index * lanes, (index + 1) * lanes)
         tile[index : index + 1, :] = ids[:, block].astype(f32)
@@ -362,9 +367,11 @@
     projection = jnp.sum(unit * grad_unit, axis=1, keepdims=True)
     grad_last = (grad_unit - unit * projection) / norms
     route_grad = (column(table, place[2]) * grad_last).astype(bf16)
-    grad_hidden = dot(route_grad, down[0], ((1,), (1,)))
     gate, up, sigmoid_gate, activated = hidden_parts(projected[...])
     hidden = (activated * up).astype(bf16)
+    made_out[...] = dot(hidden, route_grad, ((0,), (0,))).astype(bf16)
+    send(made_out, grad_out.at[0])
+    grad_hidden = dot(route_grad, down[0], ((1,), (1,)))
     gate_slope = sigmoid_gate * (1.0 + gate * (1.0 - sigmoid_gate))
     slope = jnp.concatenate([grad_hidden * up * gate_slope, grad_hidden * activated], axis=1)
     slope = slope.astype(bf16)
@@ -373,8 +380,6 @@
         spot = slice(index * block, (index + 1) * block)
         made_in[spot, :] = dot(last_all[:, spot], slope, ((0,), (0,))).astype(bf16)
         send(made_in.at[spot], grad_in.at[0, spot])
-    made_out[...] = dot(hidden, route_grad, ((0,), (0,))).astype(bf16)
-    send(made_out, grad_out.at[0])
     for copy in copies:
         copy.wait()
 
@@ -408,12 +413,14 @@
     packed = pl.pallas_call(
         functools.partial(pack_kernel, seq_dev),
         out_shape=jax.ShapeDtypeStruct((part_rows, width + lanes), bf16),
-        in_specs=[in_smem, in_vmem, in_vmem, pl.BlockSpec(memory_space=pltpu.HBM)],
+        in_specs=[in_smem] + [in_hbm] * 3,
         out_specs=in_vmem,
         scratch_shapes=[
             pltpu.VMEM((part_rows, lanes), f32),
             pltpu.VMEM((seq_dev, tail, share), bf16),
-            pltpu.SemaphoreType.DMA((seq_dev + 1,)),
+            pltpu.VMEM((1, tok_dev), jnp.int32),
+            pltpu.VMEM((1, tok_dev), f32),
+            pltpu.SemaphoreType.DMA((seq_dev + 3,)),
         ],
         cost_estimate=cost(0, 1 << 19),
         name="pack",
@@ -491,12 +498,18 @@
 
     outs = {}
     after = place
-    for group in groups:
-        out = expert(group, after, group is groups[-1])
+    rest = list(range(dp_count - 2, 1, -1))
+    expert_groups = [[0, 1]] + [[dp_count - 1]] * (dp_count > 2)
+    expert_groups += [rest[first : first + 2] for first in range(0, len(rest), 2)]
+    for group in expert_groups:
+        with_last = dp_count - 1 in group
+        out = expert(group, after, with_last)
         after, _ = lax.optimization_barrier((place, out[0]))
         for index, hop in enumerate(group):
             outs[hop] = out[index * chips : (index + 1) * chips]
-    last_all, last_projected, own_last = out[-3:]
+        if with_last:
+            last_all, last_projected, own_last = out[-3:]
+            tables_place = after
 
     table_rows = dp_count * part_rows + seqs
     chunks = width // lanes
@@ -517,7 +530,7 @@
         compiler_params=params(48 if dp_count > 8 else 12),
         cost_estimate=cost(0, 1 << 20),
         name="tables",
-    )(after, *tiles)
+    )(tables_place, *tiles)
     found = to_lane(sent, 1)
 
     def combine(hop, parts, last_sum):
@@ -541,25 +554,27 @@
 
     returned = {}
 
-    def send_back(hop, after):
+    def send_back(hop, gated, after):
         first, *parts = outs[hop]
-        parts, after = lax.optimization_barrier((parts, after))
+        free = len(parts) - gated
+        parts[free:], after = lax.optimization_barrier((parts[free:], after))
         returned[hop] = [first] + [to_lane(value, step) for value, step in zip(parts, chip_steps)]
         return after
 
-    send_back(0, [])
-    send_back(1, [])
-    before = 1
-    for hop in range(dp_count - 1, 1, -1):
-        returned[before][1:] = send_back(hop, returned[before][1:])
-        if hop == dp_count - 1:
-            returned[hop][1:], found = lax.optimization_barrier((returned[hop][1:], found))
+    send_back(1, 0, [])
+    if dp_count > 2:
+        returned[1][1:] = send_back(dp_count - 1, chips - 1, returned[1][1:])
+    before = dp_count - 1
+    for hop in rest:
+        returned[before][1:], found = send_back(hop, 1, (returned[before][1:], found))
         before = hop
     homeward = []
     last_sum = None
     for hop in range(dp_count - 1, 0, -1):
         result = combine(hop, returned[hop], last_sum)
-        last_sum = result[1] if last_sum is None else last_sum
+        if last_sum is None:
+            last_sum = result[1]
+            last_sum = send_back(0, chips - 1, last_sum)
         homeward.append(to_plane(result[0], hop))
     near_sum = combine(0, returned[0], last_sum)[0]
 
@@ -576,7 +591,6 @@
     pieces += [to_lane(piece, 1) for piece in pieces]
 
     n_blocks = width // min(512, width)
-    in_hbm = pl.BlockSpec(memory_space=pltpu.HBM)
     layer_out, grad_gate_up, grad_down = pl.pallas_call(
         functools.partial(final_kernel, len(pieces), n_blocks),
         out_shape=[

time: 86.7 us -> 87 us (level)
  local copies, waits for them, and re-layouts: 3.86 us -> 5.26 us
  waiting for transfers between devices: 23.2 us -> 21.9 us
  Pallas kernels: 21.6 us -> 22.8 us
  starting transfers between devices: 35.8 us -> 34.8 us
    unnamed x10, local copies, waits for them, and re-layouts: 3.13 us -> 4.53 us
    ppermute x28, waiting for transfers between devices: 14.6 us -> 13.4 us  [to_lane(): lax.ppermute(value, 'expert', [(j, j ^ step) for j in range(expert_count)])]
    ppermute x6, starting transfers between devices: 10.2 us -> 9.02 us  [to_plane(): return lax.ppermute(value, 'dp', [(p, p ^ step) for p in range(dp_count)])]
    pallas_call x2 -> x3, Pallas kernels: 10.2 us -> 11.2 us  [expert(): pl.pallas_call(functools.partial(expert_kernel, layout), out_shape=out_sh...]
  transfers between devices with their start and end apart: 34 -> 34, of which waited for: 13 -> 11; matrix products, arithmetic and copies ran while one was open for 2% -> 2% of each run, Pallas kernels for 19% -> 21%
where the time goes in v10:
time: 87 us; the launch traced here: 86.6 us
  starting transfers between devices  34.8 us (40%)
  Pallas kernels  22.8 us (26%)
  waiting for transfers between devices  21.9 us (25%)
  local copies, waits for them, and re-layouts  5.26 us (6%)
  other arithmetic  1.01 us (1%)
    ppermute x28, starting transfers between devices, to_lane(): lax.ppermute(value, 'expert', [(j, j ^ step) for j in range(expert_count)])  25.8 us
    ppermute x28, waiting for transfers between devices, to_lane(): lax.ppermute(value, 'expert', [(j, j ^ step) for j in range(expert_count)])  13.4 us
    pallas_call x3, Pallas kernels, expert(): pl.pallas_call(functools.partial(expert_kernel, layout), out_shape=out_sh...  11.2 us
    ppermute x6, starting transfers between devices, to_plane(): return lax.ppermute(value, 'dp', [(p, p ^ step) for p in range(dp_count)])  9.02 us
    ppermute x6, waiting for transfers between devices, to_plane(): return lax.ppermute(value, 'dp', [(p, p ^ step) for p in range(dp_count)])  8.51 us
    pallas_call x1, Pallas kernels, body(): pl.pallas_call(functools.partial(final_kernel, len(pieces), n_blocks), ou...  4.85 us
    unnamed x10, local copies, waits for them, and re-layouts  4.53 us
    pallas_call x4, Pallas kernels, combine(): pl.pallas_call(functools.partial(combine_kernel, (hop, chips, with_last,...  2.89 us
  transfers between devices with their start and end apart: 34, of which 11 were waited for; matrix products, arithmetic and copies ran while one was open for 2% of the time, Pallas kernels for 21%

profile of v10, /device:TPU:0, one launch (start us, length us, event | category | flops | bytes accessed | tf_op | source)
XLA Modules:
  0.0 86.6 jit_solution(14180452294122720509)
XLA Ops:
  1.2 2.3 %pack.1.refs_1_.refs_0_ = bf16[32,2176]{1,0:T(8,128)(2,1)} custom-call(s32[4]{0:T(128)} %positives.1, s32[1,256]{1,0:T(1,128)} %bitcast.5, f32[1,256]{1,0:T(1,128)} %bitcast.6, bf16[256,2048]{1,0:T(8,128)(2,1)} %refs_1_.1), custom_call_target="tpu_custom_call" | custom-call | bytes 524288 | tf_op jit(solution)/shard_map/pack/pallas_call | solution.py:413
  3.6 3.1 %collective-permute-start = (bf16[32,2176]{1,0:T(8,128)(2,1)}, bf16[32,2176]{1,0:T(8,128)(2,1)S(1)}, u32[]{:S(2)}, u32[]{:S(2)}) collective-permute-start(bf16[32,2176]{1,0:T(8,128)(2,1)} %pack.1.refs_1_.refs_0_), channel_id=1, source_target_pairs={{0,8},{8,0},{16,24},{24,16},{1,9},{9,1},{17,25},{25,17},{2,10},{10... | collective-permute-start | bytes 417800 | tf_op jit(solution)/shard_map/ppermute | solution.py:407
  6.6 2.5 %collective-permute-start.2 = (bf16[32,2176]{1,0:T(8,128)(2,1)}, bf16[32,2176]{1,0:T(8,128)(2,1)}, u32[]{:S(2)}, u32[]{:S(2)}) collective-permute-start(bf16[32,2176]{1,0:T(8,128)(2,1)} %pack.1.refs_1_.refs_0_), channel_id=1, source_target_pairs={{0,24},{8,16},{16,8},{24,0},{1,25},{9,17},{17,9},{25,1},{2,26},{10... | collective-permute-start | bytes 417800 | tf_op jit(solution)/shard_map/ppermute | solution.py:407
  10.9 1.6 %collective-permute-start.5 = (bf16[32,2304]{1,0:T(8,128)(2,1)S(1)}, bf16[32,2304]{1,0:T(8,128)(2,1)S(1)}, u32[]{:S(2)}, u32[]{:S(2)}) collective-permute-start(bf16[32,2304]{1,0:T(8,128)(2,1)S(1)} %pad_maximum_fusion.1), channel_id=1, source_target_pairs={{0,2},{1,3},{2,0},{3,1},{4,6},{5,7},{6,4},{7,5},{8,10},{9,11},{10,... | collective-permute-start | bytes 442376 | tf_op jit(solution)/shard_map/ppermute | solution.py:404
  12.5 1.5 %collective-permute-start.6 = (bf16[32,2304]{1,0:T(8,128)(2,1)S(1)}, bf16[32,2304]{1,0:T(8,128)(2,1)S(1)}, u32[]{:S(2)}, u32[]{:S(2)}) collective-permute-start(bf16[32,2304]{1,0:T(8,128)(2,1)S(1)} %pad_maximum_fusion.1), channel_id=1, source_target_pairs={{0,4},{1,5},{2,6},{3,7},{4,0},{5,1},{6,2},{7,3},{8,12},{9,13},{10,... | collective-permute-start | bytes 442376 | tf_op jit(solution)/shard_map/ppermute | solution.py:404
  14.5 2.5 %collective-permute-done.2.refs_7_.refs_6_ = bf16[32,2176]{1,0:T(8,128)(2,1)} collective-permute-done((bf16[32,2176]{1,0:T(8,128)(2,1)}, bf16[32,2176]{1,0:T(8,128)(2,1)}, u32[]{:S(2)}, u32[]{:S(2)}) %collective-permute-start.2) | collective-permute-done | bytes 139296 | tf_op jit(solution)/shard_map/ppermute | solution.py:407
  17.0 5.0 %collective-permute-done.1.refs_6_.refs_5_.refs_1_ = bf16[32,2176]{1,0:T(8,128)(2,1)S(1)} collective-permute-done((bf16[32,2176]{1,0:T(8,128)(2,1)}, bf16[32,2176]{1,0:T(8,128)(2,1)S(1)}, u32[]{:S(2)}, u32[]{:S(2)}) %collective-permute-start.1) | collective-permute-done | bytes 139296 | tf_op jit(solution)/shard_map/ppermute | solution.py:407
  23.0 1.6 %collective-permute-start.8 = (bf16[64,2176]{1,0:T(8,128)(2,1)S(1)}, bf16[64,2176]{1,0:T(8,128)(2,1)S(1)}, u32[]{:S(2)}, u32[]{:S(2)}) collective-permute-start(bf16[64,2176]{1,0:T(8,128)(2,1)S(1)} %pad_maximum_fusion), channel_id=1, source_target_pairs={{0,2},{1,3},{2,0},{3,1},{4,6},{5,7},{6,4},{7,5},{8,10},{9,11},{10,... | collective-permute-start | bytes 835592 | tf_op jit(solution)/shard_map/ppermute | solution.py:404
  24.6 1.5 %collective-permute-start.9 = (bf16[64,2176]{1,0:T(8,128)(2,1)S(1)}, bf16[64,2176]{1,0:T(8,128)(2,1)S(1)}, u32[]{:S(2)}, u32[]{:S(2)}) collective-permute-start(bf16[64,2176]{1,0:T(8,128)(2,1)S(1)} %pad_maximum_fusion), channel_id=1, source_target_pairs={{0,4},{1,5},{2,6},{3,7},{4,0},{5,1},{6,2},{7,3},{8,12},{9,13},{10,... | collective-permute-start | bytes 835592 | tf_op jit(solution)/shard_map/ppermute | solution.py:404
  26.6 1.9 %copy-done = bf16[1,2048,768]{2,1,0:T(8,128)(2,1)S(1)} copy-done((bf16[1,2048,768]{2,1,0:T(8,128)(2,1)S(1)}, bf16[1,2048,768]{2,1,0:T(8,128)(2,1)}, u32[]{:S(2)}) %copy-start) | copy-done | bytes 3145752
  28.5 1.4 %copy-done.2 = bf16[1,384,2048]{2,1,0:T(8,128)(2,1)S(1)} copy-done((bf16[1,384,2048]{2,1,0:T(8,128)(2,1)S(1)}, bf16[1,384,2048]{2,1,0:T(8,128)(2,1)}, u32[]{:S(2)}) %copy-start.2) | copy-done | bytes 1572888
  29.9 1.2 %copy-done.3 = bf16[256,2048]{1,0:T(8,128)(2,1)S(1)} copy-done((bf16[256,2048]{1,0:T(8,128)(2,1)S(1)}, bf16[256,2048]{1,0:T(8,128)(2,1)}, u32[]{:S(2)}) %copy-start.3) | copy-done | bytes 1048600
  31.2 4.6 %experts.3 = (bf16[32,2048]{1,0:T(8,128)(2,1)S(1)}, bf16[32,2048]{1,0:T(8,128)(2,1)S(1)}, bf16[32,2048]{1,0:T(8,128)(2,1)S(1)}, bf16[32,2048]{1,0:T(8,128)(2,1)S...) custom-call(s32[3]{0:T(128)S(1)} %pad_add_fusion.refs_0_.place.refs_, ...), custom_call_target="tpu_custom_call" | custom-call | flops 2415919104 | bytes 12582912 | tf_op jit(solution)/shard_map/experts/pallas_call | solution.py:488
  35.7 1.6 %collective-permute-start.11 = (bf16[32,2048]{1,0:T(8,128)(2,1)S(1)}, bf16[32,2048]{1,0:T(8,128)(2,1)S(1)}, u32[]{:S(2)}, u32[]{:S(2)}) collective-permute-start(bf16[32,2048]{1,0:T(8,128)(2,1)S(1)} %get-tuple-element.71), channel_id=1, source_target_pairs={{0,2},{1,3},{2,0},{3,1},{4,6},{5,7},{6,4},{7,5},{8,10},{9,11},{10,... | collective-permute-start | bytes 393224 | tf_op jit(solution)/shard_map/ppermute | solution.py:404
  37.3 1.5 %collective-permute-start.12 = (bf16[32,2048]{1,0:T(8,128)(2,1)S(1)}, bf16[32,2048]{1,0:T(8,128)(2,1)S(1)}, u32[]{:S(2)}, u32[]{:S(2)}) collective-permute-start(bf16[32,2048]{1,0:T(8,128)(2,1)S(1)} %get-tuple-element.72), channel_id=1, source_target_pairs={{0,4},{1,5},{2,6},{3,7},{4,0},{5,1},{6,2},{7,3},{8,12},{9,13},{10,... | collective-permute-start | bytes 393224 | tf_op jit(solution)/shard_map/ppermute | solution.py:404
  39.3 3.5 %experts.4 = (bf16[32,2176]{1,0:T(8,128)(2,1)S(1)}, bf16[32,2176]{1,0:T(8,128)(2,1)S(1)}, bf16[32,2176]{1,0:T(8,128)(2,1)S(1)}, bf16[32,2176]{1,0:T(8,128)(2,1)S...) custom-call(s32[3]{0:T(128)S(1)} %pad_add_fusion.refs_0_.place.refs_10_, ...), custom_call_target="tpu_custom_call" | custom-call | flops 1358954496 | bytes 12582912 | tf_op jit(solution)/shard_map/experts/pallas_call | solution.py:488
  43.2 1.5 %collective-permute-done.13.refs_4_ = bf16[32,2048]{1,0:T(8,128)(2,1)S(1)} collective-permute-done((bf16[32,2048]{1,0:T(8,128)(2,1)S(1)}, bf16[32,2048]{1,0:T(8,128)(2,1)S(1)}, u32[]{:S(2)}, u32[]{:S(2)}) %collective-permute-start.13) | collective-permute-done | bytes 131104 | tf_op jit(solution)/shard_map/ppermute | solution.py:404
  45.9 2.2 %collective-permute-start.16 = (bf16[32,2176]{1,0:T(8,128)(2,1)S(1)}, bf16[32,2176]{1,0:T(8,128)(2,1)S(1)}, u32[]{:S(2)}, u32[]{:S(2)}) collective-permute-start(bf16[32,2176]{1,0:T(8,128)(2,1)S(1)} %get-tuple-element.76), channel_id=1, source_target_pairs={{0,6},{1,7},{2,4},{3,5},{4,2},{5,3},{6,0},{7,1},{8,14},{9,15},{10,... | collective-permute-start | bytes 417800 | tf_op jit(solution)/shard_map/ppermute | solution.py:404
  48.2 1.4 %tables.1 = (bf16[144,128]{1,0:T(8,128)(2,1)S(1)}, bf16[144,128]{1,0:T(8,128)(2,1)S(1)}, f32[16,128]{1,0:T(8,128)S(1)}) custom-call(s32[3]{0:T(128)S(1)} %pad_add_fusion.refs_0_.place.refs_10_, bf16[32,2176]{1,0:T(8,128)(2,1)S(1)} %copy-done.4, bf16[32,2176]{1,0:T(8,128)(2,1)S(1)} %collective-permute-done.refs_2_.refs_1_, ...), custom_call_target="tpu_custom_call" | custom-call | bytes 1048576 | tf_op jit(solution)/shard_map/tables/pallas_call | solution.py:517
  49.7 3.2 %experts.5 = (bf16[32,2048]{1,0:T(8,128)(2,1)S(1)}, bf16[32,2048]{1,0:T(8,128)(2,1)S(1)}, bf16[32,2048]{1,0:T(8,128)(2,1)S(1)}, bf16[32,2048]{1,0:T(8,128)(2,1)S(1)}) custom-call(s32[3]{0:T(128)S(1)} %pad_add_fusion.refs_0_.place.refs_10_, bf16[32,2176]{1,0:T(8,128)(2,1)S(1)} %collective-permute-done.1.refs_6_.refs_5_.refs_1_, ...), custom_call_target="tpu_custom_call" | custom-call | flops 1207959552 | bytes 12582912 | tf_op jit(solution)/shard_map/experts/pallas_call | solution.py:488
  54.2 2.3 %collective-permute-start.24 = (bf16[32,2048]{1,0:T(8,128)(2,1)S(1)}, bf16[32,2048]{1,0:T(8,128)(2,1)S(1)}, u32[]{:S(2)}, u32[]{:S(2)}) collective-permute-start(bf16[32,2048]{1,0:T(8,128)(2,1)S(1)} %get-tuple-element.95), channel_id=1, source_target_pairs={{0,6},{1,7},{2,4},{3,5},{4,2},{5,3},{6,0},{7,1},{8,14},{9,15},{10,... | collective-permute-start | bytes 393224 | tf_op jit(solution)/shard_map/ppermute | solution.py:404
  57.8 2.6 %collective-permute-start.21 = (bf16[32,2176]{1,0:T(8,128)(2,1)S(1)}, bf16[32,2176]{1,0:T(8,128)(2,1)S(1)}, u32[]{:S(2)}, u32[]{:S(2)}) collective-permute-start(bf16[32,2176]{1,0:T(8,128)(2,1)S(1)} %get-tuple-element.91), channel_id=1, source_target_pairs={{0,24},{8,16},{16,8},{24,0},{1,25},{9,17},{17,9},{25,1},{2,26},{10... | collective-permute-start | bytes 417800 | tf_op jit(solution)/shard_map/ppermute | solution.py:407
  61.2 1.2 %collective-permute-done.24.refs_4_ = bf16[32,2048]{1,0:T(8,128)(2,1)S(1)} collective-permute-done((bf16[32,2048]{1,0:T(8,128)(2,1)S(1)}, bf16[32,2048]{1,0:T(8,128)(2,1)S(1)}, u32[]{:S(2)}, u32[]{:S(2)}) %collective-permute-start.24) | collective-permute-done | bytes 131104 | tf_op jit(solution)/shard_map/ppermute | solution.py:404
  63.8 1.0 %collective-permute-start.19 = (bf16[32,2048]{1,0:T(8,128)(2,1)S(1)}, bf16[32,2048]{1,0:T(8,128)(2,1)S(1)}, u32[]{:S(2)}, u32[]{:S(2)}) collective-permute-start(bf16[32,2048]{1,0:T(8,128)(2,1)S(1)} %get-tuple-element.87), channel_id=1, source_target_pairs={{0,4},{1,5},{2,6},{3,7},{4,0},{5,1},{6,2},{7,3},{8,12},{9,13},{10,... | collective-permute-start | bytes 393224 | tf_op jit(solution)/shard_map/ppermute | solution.py:404
  64.8 1.9 %collective-permute-start.20 = (bf16[32,2048]{1,0:T(8,128)(2,1)S(1)}, bf16[32,2048]{1,0:T(8,128)(2,1)S(1)}, u32[]{:S(2)}, u32[]{:S(2)}) collective-permute-start(bf16[32,2048]{1,0:T(8,128)(2,1)S(1)} %get-tuple-element.88), channel_id=1, source_target_pairs={{0,6},{1,7},{2,4},{3,5},{4,2},{5,3},{6,0},{7,1},{8,14},{9,15},{10,... | collective-permute-start | bytes 393224 | tf_op jit(solution)/shard_map/ppermute | solution.py:404
  66.7 4.8 %collective-permute-done.19.refs_3_ = bf16[32,2048]{1,0:T(8,128)(2,1)S(1)} collective-permute-done((bf16[32,2048]{1,0:T(8,128)(2,1)S(1)}, bf16[32,2048]{1,0:T(8,128)(2,1)S(1)}, u32[]{:S(2)}, u32[]{:S(2)}) %collective-permute-start.19) | collective-permute-done | bytes 131104 | tf_op jit(solution)/shard_map/ppermute | solution.py:404
  73.1 1.2 %collective-permute-start.28 = (bf16[32,2176]{1,0:T(8,128)(2,1)S(1)}, bf16[32,2176]{1,0:T(8,128)(2,1)S(1)}, u32[]{:S(2)}, u32[]{:S(2)}) collective-permute-start(bf16[32,2176]{1,0:T(8,128)(2,1)S(1)} %finish.1.refs_0_), channel_id=1, source_target_pairs={{0,4},{1,5},{2,6},{3,7},{4,0},{5,1},{6,2},{7,3},{8,12},{9,13},{10,... | collective-permute-start | bytes 417800 | tf_op jit(solution)/shard_map/ppermute | solution.py:404
  74.3 1.6 %collective-permute-start.29 = (bf16[32,2176]{1,0:T(8,128)(2,1)S(1)}, bf16[32,2176]{1,0:T(8,128)(2,1)S(1)}, u32[]{:S(2)}, u32[]{:S(2)}) collective-permute-start(bf16[32,2176]{1,0:T(8,128)(2,1)S(1)} %finish.1.refs_0_), channel_id=1, source_target_pairs={{0,6},{1,7},{2,4},{3,5},{4,2},{5,3},{6,0},{7,1},{8,14},{9,15},{10,... | collective-permute-start | bytes 417800 | tf_op jit(solution)/shard_map/ppermute | solution.py:404
  76.0 2.6 %collective-permute-done.27.refs_1_ = bf16[32,2176]{1,0:T(8,128)(2,1)S(1)} collective-permute-done((bf16[32,2176]{1,0:T(8,128)(2,1)S(1)}, bf16[32,2176]{1,0:T(8,128)(2,1)S(1)}, u32[]{:S(2)}, u32[]{:S(2)}) %collective-permute-start.27) | collective-permute-done | bytes 139296 | tf_op jit(solution)/shard_map/ppermute | solution.py:404
  79.1 1.3 %collective-permute-done.29.refs_3_ = bf16[32,2176]{1,0:T(8,128)(2,1)S(1)} collective-permute-done((bf16[32,2176]{1,0:T(8,128)(2,1)S(1)}, bf16[32,2176]{1,0:T(8,128)(2,1)S(1)}, u32[]{:S(2)}, u32[]{:S(2)}) %collective-permute-start.29) | collective-permute-done | bytes 139296 | tf_op jit(solution)/shard_map/ppermute | solution.py:404
  80.4 1.3 %collective-permute-done.33.refs_7_ = bf16[32,2176]{1,0:T(8,128)(2,1)S(1)} collective-permute-done((bf16[32,2176]{1,0:T(8,128)(2,1)S(1)}, bf16[32,2176]{1,0:T(8,128)(2,1)S(1)}, u32[]{:S(2)}, u32[]{:S(2)}) %collective-permute-start.33) | collective-permute-done | bytes 139296 | tf_op jit(solution)/shard_map/ppermute | solution.py:404
  81.7 4.8 %final.1 = (bf16[256,2048]{1,0:T(8,128)(2,1)}, bf16[1,2048,768]{2,1,0:T(8,128)(2,1)}, bf16[1,384,2048]{2,1,0:T(8,128)(2,1)}) custom-call(bf16[32,2176]{1,0:T(8,128)(2,1)S(1)} %finish.1.refs_0_, bf16[32,2176]{1,0:T(8,128)(2,1)S(1)} %collective-permute-done.27.refs_1_, bf16[32,2176]{1,0:T(8,128)(2,1)S(1)} %collective-permute-done.28.refs_2_, ...), custom_call_target="tpu_custom_call" | custom-call | flops 100663296 | bytes 7340032 | tf_op jit(solution)/shard_map/final/pallas_call | solution.py:594
  (61 shorter events, 13.4 us)
Async XLA Ops:
  0.6 10.3 %collective-permute-start.3 = (bf16[1,2048,768]{2,1,0:T(8,128)(2,1)}, bf16[1,2048,768]{2,1,0:T(8,128)(2,1)S(1)}, u32[]{:S(2)}, u32[]{:S(2)}) collective-permute-start(bf16[1,2048,768]{2,1,0:T(8,128)(2,1)} %refs_5_), channel_id=1, source_target_pairs={{0,1},{1,0},{2,3},{3,2},{4,5},{5,4},{6,7},{7,6},{8,9},{9,8},{10,11... | collective-permute-start | bytes 9437192 | tf_op jit(solution)/shard_map/ppermute | solution.py:404
  1.1 9.7 %collective-permute-start.4 = (bf16[1,384,2048]{2,1,0:T(8,128)(2,1)}, bf16[1,384,2048]{2,1,0:T(8,128)(2,1)}, u32[]{:S(2)}, u32[]{:S(2)}) collective-permute-start(bf16[1,384,2048]{2,1,0:T(8,128)(2,1)} %refs_14_.1), channel_id=1, source_target_pairs={{0,1},{1,0},{2,3},{3,2},{4,5},{5,4},{6,7},{7,6},{8,9},{9,8},{10,11... | collective-permute-start | bytes 4718600 | tf_op jit(solution)/shard_map/ppermute | solution.py:404
  3.6 7.3 %collective-permute-start = (bf16[32,2176]{1,0:T(8,128)(2,1)}, bf16[32,2176]{1,0:T(8,128)(2,1)S(1)}, u32[]{:S(2)}, u32[]{:S(2)}) collective-permute-start(bf16[32,2176]{1,0:T(8,128)(2,1)} %pack.1.refs_1_.refs_0_), channel_id=1, source_target_pairs={{0,8},{8,0},{16,24},{24,16},{1,9},{9,1},{17,25},{25,17},{2,10},{10... | collective-permute-start | bytes 417800 | tf_op jit(solution)/shard_map/ppermute | solution.py:407
  6.6 10.4 %collective-permute-start.2 = (bf16[32,2176]{1,0:T(8,128)(2,1)}, bf16[32,2176]{1,0:T(8,128)(2,1)}, u32[]{:S(2)}, u32[]{:S(2)}) collective-permute-start(bf16[32,2176]{1,0:T(8,128)(2,1)} %pack.1.refs_1_.refs_0_), channel_id=1, source_target_pairs={{0,24},{8,16},{16,8},{24,0},{1,25},{9,17},{17,9},{25,1},{2,26},{10... | collective-permute-start | bytes 417800 | tf_op jit(solution)/shard_map/ppermute | solution.py:407
  9.1 12.9 %collective-permute-start.1 = (bf16[32,2176]{1,0:T(8,128)(2,1)}, bf16[32,2176]{1,0:T(8,128)(2,1)S(1)}, u32[]{:S(2)}, u32[]{:S(2)}) collective-permute-start(bf16[32,2176]{1,0:T(8,128)(2,1)} %pack.1.refs_1_.refs_0_), channel_id=1, source_target_pairs={{0,16},{8,24},{16,0},{24,8},{1,17},{9,25},{17,1},{25,9},{2,18},{10... | collective-permute-start | bytes 417800 | tf_op jit(solution)/shard_map/ppermute | solution.py:407
  10.9 12.1 %collective-permute-start.5 = (bf16[32,2304]{1,0:T(8,128)(2,1)S(1)}, bf16[32,2304]{1,0:T(8,128)(2,1)S(1)}, u32[]{:S(2)}, u32[]{:S(2)}) collective-permute-start(bf16[32,2304]{1,0:T(8,128)(2,1)S(1)} %pad_maximum_fusion.1), channel_id=1, source_target_pairs={{0,2},{1,3},{2,0},{3,1},{4,6},{5,7},{6,4},{7,5},{8,10},{9,11},{10,... | collective-permute-start | bytes 442376 | tf_op jit(solution)/shard_map/ppermute | solution.py:404
  12.5 10.5 %collective-permute-start.6 = (bf16[32,2304]{1,0:T(8,128)(2,1)S(1)}, bf16[32,2304]{1,0:T(8,128)(2,1)S(1)}, u32[]{:S(2)}, u32[]{:S(2)}) collective-permute-start(bf16[32,2304]{1,0:T(8,128)(2,1)S(1)} %pad_maximum_fusion.1), channel_id=1, source_target_pairs={{0,4},{1,5},{2,6},{3,7},{4,0},{5,1},{6,2},{7,3},{8,12},{9,13},{10,... | collective-permute-start | bytes 442376 | tf_op jit(solution)/shard_map/ppermute | solution.py:404
  14.0 9.0 %collective-permute-start.7 = (bf16[32,2304]{1,0:T(8,128)(2,1)S(1)}, bf16[32,2304]{1,0:T(8,128)(2,1)S(1)}, u32[]{:S(2)}, u32[]{:S(2)}) collective-permute-start(bf16[32,2304]{1,0:T(8,128)(2,1)S(1)} %pad_maximum_fusion.1), channel_id=1, source_target_pairs={{0,6},{1,7},{2,4},{3,5},{4,2},{5,3},{6,0},{7,1},{8,14},{9,15},{10,... | collective-permute-start | bytes 442376 | tf_op jit(solution)/shard_map/ppermute | solution.py:404
  23.0 15.8 %collective-permute-start.8 = (bf16[64,2176]{1,0:T(8,128)(2,1)S(1)}, bf16[64,2176]{1,0:T(8,128)(2,1)S(1)}, u32[]{:S(2)}, u32[]{:S(2)}) collective-permute-start(bf16[64,2176]{1,0:T(8,128)(2,1)S(1)} %pad_maximum_fusion), channel_id=1, source_target_pairs={{0,2},{1,3},{2,0},{3,1},{4,6},{5,7},{6,4},{7,5},{8,10},{9,11},{10,... | collective-permute-start | bytes 835592 | tf_op jit(solution)/shard_map/ppermute | solution.py:404
  24.6 14.7 %collective-permute-start.9 = (bf16[64,2176]{1,0:T(8,128)(2,1)S(1)}, bf16[64,2176]{1,0:T(8,128)(2,1)S(1)}, u32[]{:S(2)}, u32[]{:S(2)}) collective-permute-start(bf16[64,2176]{1,0:T(8,128)(2,1)S(1)} %pad_maximum_fusion), channel_id=1, source_target_pairs={{0,4},{1,5},{2,6},{3,7},{4,0},{5,1},{6,2},{7,3},{8,12},{9,13},{10,... | collective-permute-start | bytes 835592 | tf_op jit(solution)/shard_map/ppermute | solution.py:404
  26.1 13.2 %collective-permute-start.10 = (bf16[64,2176]{1,0:T(8,128)(2,1)S(1)}, bf16[64,2176]{1,0:T(8,128)(2,1)S(1)}, u32[]{:S(2)}, u32[]{:S(2)}) collective-permute-start(bf16[64,2176]{1,0:T(8,128)(2,1)S(1)} %pad_maximum_fusion), channel_id=1, source_target_pairs={{0,6},{1,7},{2,4},{3,5},{4,2},{5,3},{6,0},{7,1},{8,14},{9,15},{10,... | collective-permute-start | bytes 835592 | tf_op jit(solution)/shard_map/ppermute | solution.py:404
  35.7 7.1 %collective-permute-start.11 = (bf16[32,2048]{1,0:T(8,128)(2,1)S(1)}, bf16[32,2048]{1,0:T(8,128)(2,1)S(1)}, u32[]{:S(2)}, u32[]{:S(2)}) collective-permute-start(bf16[32,2048]{1,0:T(8,128)(2,1)S(1)} %get-tuple-element.71), channel_id=1, source_target_pairs={{0,2},{1,3},{2,0},{3,1},{4,6},{5,7},{6,4},{7,5},{8,10},{9,11},{10,... | collective-permute-start | bytes 393224 | tf_op jit(solution)/shard_map/ppermute | solution.py:404
  37.3 5.9 %collective-permute-start.12 = (bf16[32,2048]{1,0:T(8,128)(2,1)S(1)}, bf16[32,2048]{1,0:T(8,128)(2,1)S(1)}, u32[]{:S(2)}, u32[]{:S(2)}) collective-permute-start(bf16[32,2048]{1,0:T(8,128)(2,1)S(1)} %get-tuple-element.72), channel_id=1, source_target_pairs={{0,4},{1,5},{2,6},{3,7},{4,0},{5,1},{6,2},{7,3},{8,12},{9,13},{10,... | collective-permute-start | bytes 393224 | tf_op jit(solution)/shard_map/ppermute | solution.py:404
  38.8 5.9 %collective-permute-start.13 = (bf16[32,2048]{1,0:T(8,128)(2,1)S(1)}, bf16[32,2048]{1,0:T(8,128)(2,1)S(1)}, u32[]{:S(2)}, u32[]{:S(2)}) collective-permute-start(bf16[32,2048]{1,0:T(8,128)(2,1)S(1)} %get-tuple-element.73), channel_id=1, source_target_pairs={{0,6},{1,7},{2,4},{3,5},{4,2},{5,3},{6,0},{7,1},{8,14},{9,15},{10,... | collective-permute-start | bytes 393224 | tf_op jit(solution)/shard_map/ppermute | solution.py:404
  44.7 9.5 %collective-permute-start.14 = (bf16[32,2176]{1,0:T(8,128)(2,1)S(1)}, bf16[32,2176]{1,0:T(8,128)(2,1)S(1)}, u32[]{:S(2)}, u32[]{:S(2)}) collective-permute-start(bf16[32,2176]{1,0:T(8,128)(2,1)S(1)} %get-tuple-element.74), channel_id=1, source_target_pairs={{0,2},{1,3},{2,0},{3,1},{4,6},{5,7},{6,4},{7,5},{8,10},{9,11},{10,... | collective-permute-start | bytes 417800 | tf_op jit(solution)/shard_map/ppermute | solution.py:404
  45.2 8.9 %collective-permute-start.15 = (bf16[32,2176]{1,0:T(8,128)(2,1)S(1)}, bf16[32,2176]{1,0:T(8,128)(2,1)S(1)}, u32[]{:S(2)}, u32[]{:S(2)}) collective-permute-start(bf16[32,2176]{1,0:T(8,128)(2,1)S(1)} %get-tuple-element.75), channel_id=1, source_target_pairs={{0,4},{1,5},{2,6},{3,7},{4,0},{5,1},{6,2},{7,3},{8,12},{9,13},{10,... | collective-permute-start | bytes 417800 | tf_op jit(solution)/shard_map/ppermute | solution.py:404
  45.9 8.2 %collective-permute-start.16 = (bf16[32,2176]{1,0:T(8,128)(2,1)S(1)}, bf16[32,2176]{1,0:T(8,128)(2,1)S(1)}, u32[]{:S(2)}, u32[]{:S(2)}) collective-permute-start(bf16[32,2176]{1,0:T(8,128)(2,1)S(1)} %get-tuple-element.76), channel_id=1, source_target_pairs={{0,6},{1,7},{2,4},{3,5},{4,2},{5,3},{6,0},{7,1},{8,14},{9,15},{10,... | collective-permute-start | bytes 417800 | tf_op jit(solution)/shard_map/ppermute | solution.py:404
  49.6 3.8 %collective-permute-start.17 = (bf16[144,128]{1,0:T(8,128)(2,1)S(1)}, bf16[144,128]{1,0:T(8,128)(2,1)S(1)}, u32[]{:S(2)}, u32[]{:S(2)}) collective-permute-start(bf16[144,128]{1,0:T(8,128)(2,1)S(1)} %get-tuple-element.77), channel_id=1, source_target_pairs={{0,1},{1,0},{2,3},{3,2},{4,5},{5,4},{6,7},{7,6},{8,9},{9,8},{10,11... | collective-permute-start | bytes 110600 | tf_op jit(solution)/shard_map/ppermute | solution.py:404
  52.8 8.3 %collective-permute-start.22 = (bf16[32,2048]{1,0:T(8,128)(2,1)S(1)}, bf16[32,2048]{1,0:T(8,128)(2,1)S(1)}, u32[]{:S(2)}, u32[]{:S(2)}) collective-permute-start(bf16[32,2048]{1,0:T(8,128)(2,1)S(1)} %get-tuple-element.93), channel_id=1, source_target_pairs={{0,2},{1,3},{2,0},{3,1},{4,6},{5,7},{6,4},{7,5},{8,10},{9,11},{10,... | collective-permute-start | bytes 393224 | tf_op jit(solution)/shard_map/ppermute | solution.py:404
  53.4 7.8 %collective-permute-start.23 = (bf16[32,2048]{1,0:T(8,128)(2,1)S(1)}, bf16[32,2048]{1,0:T(8,128)(2,1)S(1)}, u32[]{:S(2)}, u32[]{:S(2)}) collective-permute-start(bf16[32,2048]{1,0:T(8,128)(2,1)S(1)} %get-tuple-element.94), channel_id=1, source_target_pairs={{0,4},{1,5},{2,6},{3,7},{4,0},{5,1},{6,2},{7,3},{8,12},{9,13},{10,... | collective-permute-start | bytes 393224 | tf_op jit(solution)/shard_map/ppermute | solution.py:404
  54.2 8.2 %collective-permute-start.24 = (bf16[32,2048]{1,0:T(8,128)(2,1)S(1)}, bf16[32,2048]{1,0:T(8,128)(2,1)S(1)}, u32[]{:S(2)}, u32[]{:S(2)}) collective-permute-start(bf16[32,2048]{1,0:T(8,128)(2,1)S(1)} %get-tuple-element.95), channel_id=1, source_target_pairs={{0,6},{1,7},{2,4},{3,5},{4,2},{5,3},{6,0},{7,1},{8,14},{9,15},{10,... | collective-permute-start | bytes 393224 | tf_op jit(solution)/shard_map/ppermute | solution.py:404
  57.2 7.6 %collective-permute-start.18 = (bf16[32,2048]{1,0:T(8,128)(2,1)S(1)}, bf16[32,2048]{1,0:T(8,128)(2,1)S(1)}, u32[]{:S(2)}, u32[]{:S(2)}) collective-permute-start(bf16[32,2048]{1,0:T(8,128)(2,1)S(1)} %get-tuple-element.86), channel_id=1, source_target_pairs={{0,2},{1,3},{2,0},{3,1},{4,6},{5,7},{6,4},{7,5},{8,10},{9,11},{10,... | collective-permute-start | bytes 393224 | tf_op jit(solution)/shard_map/ppermute | solution.py:404
  57.8 14.5 %collective-permute-start.21 = (bf16[32,2176]{1,0:T(8,128)(2,1)S(1)}, bf16[32,2176]{1,0:T(8,128)(2,1)S(1)}, u32[]{:S(2)}, u32[]{:S(2)}) collective-permute-start(bf16[32,2176]{1,0:T(8,128)(2,1)S(1)} %get-tuple-element.91), channel_id=1, source_target_pairs={{0,24},{8,16},{16,8},{24,0},{1,25},{9,17},{17,9},{25,1},{2,26},{10... | collective-permute-start | bytes 417800 | tf_op jit(solution)/shard_map/ppermute | solution.py:407
  61.2 11.2 %collective-permute-start.26 = (bf16[32,2176]{1,0:T(8,128)(2,1)S(1)}, bf16[32,2176]{1,0:T(8,128)(2,1)S(1)}, u32[]{:S(2)}, u32[]{:S(2)}) collective-permute-start(bf16[32,2176]{1,0:T(8,128)(2,1)S(1)} %combine.7), channel_id=1, source_target_pairs={{0,8},{8,0},{16,24},{24,16},{1,9},{9,1},{17,25},{25,17},{2,10},{10... | collective-permute-start | bytes 417800 | tf_op jit(solution)/shard_map/ppermute | solution.py:407
  63.1 9.2 %collective-permute-start.25 = (bf16[32,2176]{1,0:T(8,128)(2,1)S(1)}, bf16[32,2176]{1,0:T(8,128)(2,1)S(1)}, u32[]{:S(2)}, u32[]{:S(2)}) collective-permute-start(bf16[32,2176]{1,0:T(8,128)(2,1)S(1)} %combine.6), channel_id=1, source_target_pairs={{0,16},{8,24},{16,0},{24,8},{1,17},{9,25},{17,1},{25,9},{2,18},{10... | collective-permute-start | bytes 417800 | tf_op jit(solution)/shard_map/ppermute | solution.py:407
  63.8 7.8 %collective-permute-start.19 = (bf16[32,2048]{1,0:T(8,128)(2,1)S(1)}, bf16[32,2048]{1,0:T(8,128)(2,1)S(1)}, u32[]{:S(2)}, u32[]{:S(2)}) collective-permute-start(bf16[32,2048]{1,0:T(8,128)(2,1)S(1)} %get-tuple-element.87), channel_id=1, source_target_pairs={{0,4},{1,5},{2,6},{3,7},{4,0},{5,1},{6,2},{7,3},{8,12},{9,13},{10,... | collective-permute-start | bytes 393224 | tf_op jit(solution)/shard_map/ppermute | solution.py:404
  64.8 6.8 %collective-permute-start.20 = (bf16[32,2048]{1,0:T(8,128)(2,1)S(1)}, bf16[32,2048]{1,0:T(8,128)(2,1)S(1)}, u32[]{:S(2)}, u32[]{:S(2)}) collective-permute-start(bf16[32,2048]{1,0:T(8,128)(2,1)S(1)} %get-tuple-element.88), channel_id=1, source_target_pairs={{0,6},{1,7},{2,4},{3,5},{4,2},{5,3},{6,0},{7,1},{8,14},{9,15},{10,... | collective-permute-start | bytes 393224 | tf_op jit(solution)/shard_map/ppermute | solution.py:404
  72.4 6.2 %collective-permute-start.27 = (bf16[32,2176]{1,0:T(8,128)(2,1)S(1)}, bf16[32,2176]{1,0:T(8,128)(2,1)S(1)}, u32[]{:S(2)}, u32[]{:S(2)}) collective-permute-start(bf16[32,2176]{1,0:T(8,128)(2,1)S(1)} %finish.1.refs_0_), channel_id=1, source_target_pairs={{0,2},{1,3},{2,0},{3,1},{4,6},{5,7},{6,4},{7,5},{8,10},{9,11},{10,... | collective-permute-start | bytes 417800 | tf_op jit(solution)/shard_map/ppermute | solution.py:404
  73.1 5.7 %collective-permute-start.28 = (bf16[32,2176]{1,0:T(8,128)(2,1)S(1)}, bf16[32,2176]{1,0:T(8,128)(2,1)S(1)}, u32[]{:S(2)}, u32[]{:S(2)}) collective-permute-start(bf16[32,2176]{1,0:T(8,128)(2,1)S(1)} %finish.1.refs_0_), channel_id=1, source_target_pairs={{0,4},{1,5},{2,6},{3,7},{4,0},{5,1},{6,2},{7,3},{8,12},{9,13},{10,... | collective-permute-start | bytes 417800 | tf_op jit(solution)/shard_map/ppermute | solution.py:404
  74.3 6.0 %collective-permute-start.29 = (bf16[32,2176]{1,0:T(8,128)(2,1)S(1)}, bf16[32,2176]{1,0:T(8,128)(2,1)S(1)}, u32[]{:S(2)}, u32[]{:S(2)}) collective-permute-start(bf16[32,2176]{1,0:T(8,128)(2,1)S(1)} %finish.1.refs_0_), channel_id=1, source_target_pairs={{0,6},{1,7},{2,4},{3,5},{4,2},{5,3},{6,0},{7,1},{8,14},{9,15},{10,... | collective-permute-start | bytes 417800 | tf_op jit(solution)/shard_map/ppermute | solution.py:404
  76.0 4.4 %collective-permute-start.30 = (bf16[32,2176]{1,0:T(8,128)(2,1)S(1)}, bf16[32,2176]{1,0:T(8,128)(2,1)S(1)}, u32[]{:S(2)}, u32[]{:S(2)}) collective-permute-start(bf16[32,2176]{1,0:T(8,128)(2,1)S(1)} %finish.1.refs_0_), channel_id=1, source_target_pairs={{0,1},{1,0},{2,3},{3,2},{4,5},{5,4},{6,7},{7,6},{8,9},{9,8},{10,11... | collective-permute-start | bytes 417800 | tf_op jit(solution)/shard_map/ppermute | solution.py:404
  78.6 1.8 %collective-permute-start.31 = (bf16[32,2176]{1,0:T(8,128)(2,1)S(1)}, bf16[32,2176]{1,0:T(8,128)(2,1)S(1)}, u32[]{:S(2)}, u32[]{:S(2)}) collective-permute-start(bf16[32,2176]{1,0:T(8,128)(2,1)S(1)} %collective-permute-done.27.refs_1_), channel_id=1, source_target_pairs={{0,1},{1,0},{2,3},{3,2},{4,5},{5,4},{6,7},{7,6},{8,9},{9,8},{10,11... | collective-permute-start | bytes 417800 | tf_op jit(solution)/shard_map/ppermute | solution.py:404
  (7 other events, 23.7 us)

commit v11 on v10

--- a/solution.py
+++ b/solution.py
@@ -202,6 +202,11 @@
     tokens = refs.pop(0) if near else None
     parts, refs = dict(zip(used, refs)), refs[len(used) :]
     weights, refs = refs[:4], refs[4:]
+    copied, sem = refs[-2:]
+    mate_copy = pltpu.make_async_copy(weights[3], copied, sem)
+    mate_copy.start()
+    weights[3] = copied
+    refs = refs[:-2]
     n_outs = chips * len(group)
     outs, refs = refs[:n_outs], refs[n_outs:]
     if with_last:
@@ -229,6 +234,7 @@
             last_projected[...] = projected[total:]
         _, up, _, activated = hidden_parts(projected)
         hidden.append((activated * up).astype(bf16))
+    mate_copy.wait()
     block = min(512, width)
     if with_last:
         each = floats.shape[0] // by_lane.shape[0]
@@ -369,8 +375,6 @@
     route_grad = (column(table, place[2]) * grad_last).astype(bf16)
     gate, up, sigmoid_gate, activated = hidden_parts(projected[...])
     hidden = (activated * up).astype(bf16)
-    made_out[...] = dot(hidden, route_grad, ((0,), (0,))).astype(bf16)
-    send(made_out, grad_out.at[0])
     grad_hidden = dot(route_grad, down[0], ((1,), (1,)))
     gate_slope = sigmoid_gate * (1.0 + gate * (1.0 - sigmoid_gate))
     slope = jnp.concatenate([grad_hidden * up * gate_slope, grad_hidden * activated], axis=1)
@@ -380,6 +384,8 @@
         spot = slice(index * block, (index + 1) * block)
         made_in[spot, :] = dot(last_all[:, spot], slope, ((0,), (0,))).astype(bf16)
         send(made_in.at[spot], grad_in.at[0, spot])
+    made_out[...] = dot(hidden, route_grad, ((0,), (0,))).astype(bf16)
+    send(made_out, grad_out.at[0])
     for copy in copies:
         copy.wait()
 
@@ -484,11 +490,14 @@
                 pltpu.VMEM((dp_count, width // lanes, -(-seq_dev // 8) * 8, lanes), f32),
             ] + scratch
         operands = [place] + [tokens] * near + parts + list(weights)
+        scratch += [pltpu.VMEM(down.shape, bf16), pltpu.SemaphoreType.DMA(())]
         layout = (tuple(group), chips, part_rows, seq_dev, where_tiles, used, with_last)
         return pl.pallas_call(
             functools.partial(expert_kernel, layout),
             out_shape=out_shape,
-            in_specs=[in_smem] + [in_vmem] * (len(operands) - 1),
+            in_specs=[in_smem]
+            + [in_vmem] * (len(operands) - 2)
+            + [pl.BlockSpec(memory_space=pl.ANY)],
             out_specs=[in_vmem] * len(out_shape),
             scratch_shapes=scratch,
             compiler_params=params(32),
@@ -499,14 +508,12 @@
     outs = {}
     after = place
     rest = list(range(dp_count - 2, 1, -1))
-    expert_groups = [[0, 1]] + [[dp_count - 1]] * (dp_count > 2)
-    expert_groups += [rest[first : first + 2] for first in range(0, len(rest), 2)]
-    for group in expert_groups:
+    for group in groups:
         with_last = dp_count - 1 in group
         out = expert(group, after, with_last)
         after, _ = lax.optimization_barrier((place, out[0]))
         for index, hop in enumerate(group):
-            outs[hop] = out[index * chips : (index + 1) * chips]
+            outs[hop] = list(out[index * chips : (index + 1) * chips])
         if with_last:
             last_all, last_projected, own_last = out[-3:]
             tables_place = after
@@ -572,10 +579,12 @@
     last_sum = None
     for hop in range(dp_count - 1, 0, -1):
         result = combine(hop, returned[hop], last_sum)
-        if last_sum is None:
-            last_sum = result[1]
-            last_sum = send_back(0, chips - 1, last_sum)
+        last_sum = result[1] if last_sum is None else last_sum
         homeward.append(to_plane(result[0], hop))
+        if hop == min(3, dp_count - 1):
+            gate = result[0]
+    outs[0][1:], gate = lax.optimization_barrier((outs[0][1:], gate))
+    send_back(0, 0, [])
     near_sum = combine(0, returned[0], last_sum)[0]
 
     own_out = pl.pallas_call(

time: 87 us -> 85.6 us (0.984)
  local copies, waits for them, and re-layouts: 5.26 us -> 3.86 us
  starting transfers between devices: 34.8 us -> 35.7 us
    unnamed x10, local copies, waits for them, and re-layouts: 4.53 us -> 3.13 us
    ppermute x6, starting transfers between devices: 9.02 us -> 10.1 us  [to_plane(): return lax.ppermute(value, 'dp', [(p, p ^ step) for p in range(dp_count)])]
    pallas_call x3 -> x2, Pallas kernels: 11.2 us -> 10.6 us  [expert(): pl.pallas_call(functools.partial(expert_kernel, layout), out_shape=out_sh...]
  transfers between devices with their start and end apart: 34 -> 34, of which waited for: 11 -> 12; matrix products, arithmetic and copies ran while one was open for 2% -> 2% of each run, Pallas kernels for 21% -> 20%
where the time goes in v11:
time: 85.6 us; the launch traced here: 85.3 us
  starting transfers between devices  35.7 us (42%)
  Pallas kernels  22 us (26%)
  waiting for transfers between devices  22 us (26%)
  local copies, waits for them, and re-layouts  3.86 us (5%)
  other arithmetic  1.01 us (1%)
    ppermute x28, starting transfers between devices, to_lane(): lax.ppermute(value, 'expert', [(j, j ^ step) for j in range(expert_count)])  25.5 us
    ppermute x28, waiting for transfers between devices, to_lane(): lax.ppermute(value, 'expert', [(j, j ^ step) for j in range(expert_count)])  13.3 us
    pallas_call x2, Pallas kernels, expert(): pl.pallas_call(functools.partial(expert_kernel, layout), out_shape=out_sh...  10.6 us
    ppermute x6, starting transfers between devices, to_plane(): return lax.ppermute(value, 'dp', [(p, p ^ step) for p in range(dp_count)])  10.1 us
    ppermute x6, waiting for transfers between devices, to_plane(): return lax.ppermute(value, 'dp', [(p, p ^ step) for p in range(dp_count)])  8.62 us
    pallas_call x1, Pallas kernels, body(): pl.pallas_call(functools.partial(final_kernel, len(pieces), n_blocks), ou...  4.73 us
    unnamed x10, local copies, waits for them, and re-layouts  3.13 us
    pallas_call x4, Pallas kernels, combine(): pl.pallas_call(functools.partial(combine_kernel, (hop, chips, with_last,...  2.89 us
  transfers between devices with their start and end apart: 34, of which 12 were waited for; matrix products, arithmetic and copies ran while one was open for 2% of the time, Pallas kernels for 20%

profile of v11, /device:TPU:0, one launch (start us, length us, event | category | flops | bytes accessed | tf_op | source)
XLA Modules:
  0.0 85.3 jit_solution(6720813975942372688)
XLA Ops:
  1.2 2.3 %pack.1.refs_1_.refs_0_ = bf16[32,2176]{1,0:T(8,128)(2,1)} custom-call(s32[4]{0:T(128)} %positives.1, s32[1,256]{1,0:T(1,128)} %bitcast.5, f32[1,256]{1,0:T(1,128)} %bitcast.6, bf16[256,2048]{1,0:T(8,128)(2,1)} %refs_1_.1), custom_call_target="tpu_custom_call" | custom-call | bytes 524288 | tf_op jit(solution)/shard_map/pack/pallas_call | solution.py:419
  3.6 3.1 %collective-permute-start = (bf16[32,2176]{1,0:T(8,128)(2,1)}, bf16[32,2176]{1,0:T(8,128)(2,1)S(1)}, u32[]{:S(2)}, u32[]{:S(2)}) collective-permute-start(bf16[32,2176]{1,0:T(8,128)(2,1)} %pack.1.refs_1_.refs_0_), channel_id=1, source_target_pairs={{0,8},{8,0},{16,24},{24,16},{1,9},{9,1},{17,25},{25,17},{2,10},{10... | collective-permute-start | bytes 417800 | tf_op jit(solution)/shard_map/ppermute | solution.py:413
  6.6 2.5 %collective-permute-start.2 = (bf16[32,2176]{1,0:T(8,128)(2,1)}, bf16[32,2176]{1,0:T(8,128)(2,1)S(1)}, u32[]{:S(2)}, u32[]{:S(2)}) collective-permute-start(bf16[32,2176]{1,0:T(8,128)(2,1)} %pack.1.refs_1_.refs_0_), channel_id=1, source_target_pairs={{0,24},{8,16},{16,8},{24,0},{1,25},{9,17},{17,9},{25,1},{2,26},{10... | collective-permute-start | bytes 417800 | tf_op jit(solution)/shard_map/ppermute | solution.py:413
  10.9 2.6 %collective-permute-start.7 = (bf16[32,2304]{1,0:T(8,128)(2,1)S(1)}, bf16[32,2304]{1,0:T(8,128)(2,1)S(1)}, u32[]{:S(2)}, u32[]{:S(2)}) collective-permute-start(bf16[32,2304]{1,0:T(8,128)(2,1)S(1)} %pad_maximum_fusion.1), channel_id=1, source_target_pairs={{0,6},{1,7},{2,4},{3,5},{4,2},{5,3},{6,0},{7,1},{8,14},{9,15},{10,... | collective-permute-start | bytes 442376 | tf_op jit(solution)/shard_map/ppermute | solution.py:410
  14.5 2.4 %collective-permute-done.2.refs_7_.refs_6_ = bf16[32,2176]{1,0:T(8,128)(2,1)S(1)} collective-permute-done((bf16[32,2176]{1,0:T(8,128)(2,1)}, bf16[32,2176]{1,0:T(8,128)(2,1)S(1)}, u32[]{:S(2)}, u32[]{:S(2)}) %collective-permute-start.2) | collective-permute-done | bytes 139296 | tf_op jit(solution)/shard_map/ppermute | solution.py:413
  16.9 5.3 %collective-permute-done.1.refs_6_.refs_5_ = bf16[32,2176]{1,0:T(8,128)(2,1)} collective-permute-done((bf16[32,2176]{1,0:T(8,128)(2,1)}, bf16[32,2176]{1,0:T(8,128)(2,1)}, u32[]{:S(2)}, u32[]{:S(2)}) %collective-permute-start.1) | collective-permute-done | bytes 139296 | tf_op jit(solution)/shard_map/ppermute | solution.py:413
  23.1 2.5 %collective-permute-start.10 = (bf16[64,2176]{1,0:T(8,128)(2,1)S(1)}, bf16[64,2176]{1,0:T(8,128)(2,1)S(1)}, u32[]{:S(2)}, u32[]{:S(2)}) collective-permute-start(bf16[64,2176]{1,0:T(8,128)(2,1)S(1)} %pad_maximum_fusion), channel_id=1, source_target_pairs={{0,6},{1,7},{2,4},{3,5},{4,2},{5,3},{6,0},{7,1},{8,14},{9,15},{10,... | collective-permute-start | bytes 835592 | tf_op jit(solution)/shard_map/ppermute | solution.py:410
  26.8 1.9 %copy-done.1 = bf16[1,2048,768]{2,1,0:T(8,128)(2,1)S(1)} copy-done((bf16[1,2048,768]{2,1,0:T(8,128)(2,1)S(1)}, bf16[1,2048,768]{2,1,0:T(8,128)(2,1)}, u32[]{:S(2)}) %copy-start.1) | copy-done | bytes 3145752
  28.6 1.2 %copy-done.3 = bf16[256,2048]{1,0:T(8,128)(2,1)S(1)} copy-done((bf16[256,2048]{1,0:T(8,128)(2,1)S(1)}, bf16[256,2048]{1,0:T(8,128)(2,1)}, u32[]{:S(2)}) %copy-start.3) | copy-done | bytes 1048600
  29.9 5.2 %experts.2 = (bf16[32,2048]{1,0:T(8,128)(2,1)S(1)}, bf16[32,2048]{1,0:T(8,128)(2,1)S(1)}, bf16[32,2048]{1,0:T(8,128)(2,1)S(1)}, bf16[32,2048]{1,0:T(8,128)(2,1)S...) custom-call(s32[3]{0:T(128)S(1)} %pad_add_fusion.refs_0_.place.refs_, ...), custom_call_target="tpu_custom_call" | custom-call | flops 2415919104 | bytes 12582912 | tf_op jit(solution)/shard_map/experts/pallas_call | solution.py:495
  35.1 1.6 %collective-permute-start.11 = (bf16[32,2048]{1,0:T(8,128)(2,1)S(1)}, bf16[32,2048]{1,0:T(8,128)(2,1)S(1)}, u32[]{:S(2)}, u32[]{:S(2)}) collective-permute-start(bf16[32,2048]{1,0:T(8,128)(2,1)S(1)} %get-tuple-element.70), channel_id=1, source_target_pairs={{0,2},{1,3},{2,0},{3,1},{4,6},{5,7},{6,4},{7,5},{8,10},{9,11},{10,... | collective-permute-start | bytes 393224 | tf_op jit(solution)/shard_map/ppermute | solution.py:410
  36.6 1.5 %collective-permute-start.12 = (bf16[32,2048]{1,0:T(8,128)(2,1)S(1)}, bf16[32,2048]{1,0:T(8,128)(2,1)S(1)}, u32[]{:S(2)}, u32[]{:S(2)}) collective-permute-start(bf16[32,2048]{1,0:T(8,128)(2,1)S(1)} %get-tuple-element.71), channel_id=1, source_target_pairs={{0,4},{1,5},{2,6},{3,7},{4,0},{5,1},{6,2},{7,3},{8,12},{9,13},{10,... | collective-permute-start | bytes 393224 | tf_op jit(solution)/shard_map/ppermute | solution.py:410
  38.7 1.1 %collective-permute-done.8.refs_8_.refs_7_ = bf16[64,2176]{1,0:T(8,128)(2,1)S(1)} collective-permute-done((bf16[64,2176]{1,0:T(8,128)(2,1)S(1)}, bf16[64,2176]{1,0:T(8,128)(2,1)S(1)}, u32[]{:S(2)}, u32[]{:S(2)}) %collective-permute-start.8) | collective-permute-done | bytes 278560 | tf_op jit(solution)/shard_map/ppermute | solution.py:410
  39.8 5.4 %experts.3 = (bf16[32,2048]{1,0:T(8,128)(2,1)S(1)}, bf16[32,2048]{1,0:T(8,128)(2,1)S(1)}, bf16[32,2048]{1,0:T(8,128)(2,1)S(1)}, bf16[32,2048]{1,0:T(8,128)(2,1)S...) custom-call(s32[3]{0:T(128)S(1)} %pad_add_fusion.refs_0_.place.refs_, ...), custom_call_target="tpu_custom_call" | custom-call | flops 2566914048 | bytes 12582912 | tf_op jit(solution)/shard_map/experts/pallas_call | solution.py:495
  45.2 1.5 %collective-permute-start.14 = (bf16[32,2176]{1,0:T(8,128)(2,1)S(1)}, bf16[32,2176]{1,0:T(8,128)(2,1)S(1)}, u32[]{:S(2)}, u32[]{:S(2)}) collective-permute-start(bf16[32,2176]{1,0:T(8,128)(2,1)S(1)} %get-tuple-element.73), channel_id=1, source_target_pairs={{0,2},{1,3},{2,0},{3,1},{4,6},{5,7},{6,4},{7,5},{8,10},{9,11},{10,... | collective-permute-start | bytes 417800 | tf_op jit(solution)/shard_map/ppermute | solution.py:410
  47.2 1.5 %collective-permute-start.16 = (bf16[32,2176]{1,0:T(8,128)(2,1)S(1)}, bf16[32,2176]{1,0:T(8,128)(2,1)S(1)}, u32[]{:S(2)}, u32[]{:S(2)}) collective-permute-start(bf16[32,2176]{1,0:T(8,128)(2,1)S(1)} %get-tuple-element.75), channel_id=1, source_target_pairs={{0,6},{1,7},{2,4},{3,5},{4,2},{5,3},{6,0},{7,1},{8,14},{9,15},{10,... | collective-permute-start | bytes 417800 | tf_op jit(solution)/shard_map/ppermute | solution.py:410
  48.7 1.4 %tables.1 = (bf16[144,128]{1,0:T(8,128)(2,1)S(1)}, bf16[144,128]{1,0:T(8,128)(2,1)S(1)}, f32[16,128]{1,0:T(8,128)S(1)}) custom-call(s32[3]{0:T(128)S(1)} %pad_add_fusion.refs_0_.place.refs_10_, bf16[32,2176]{1,0:T(8,128)(2,1)S(1)} %copy-done.4, bf16[32,2176]{1,0:T(8,128)(2,1)S(1)} %collective-permute-done.refs_2_.refs_1_, ...), custom_call_target="tpu_custom_call" | custom-call | bytes 1048576 | tf_op jit(solution)/shard_map/tables/pallas_call | solution.py:524
  50.2 1.5 %collective-permute-start.22 = (bf16[32,2048]{1,0:T(8,128)(2,1)S(1)}, bf16[32,2048]{1,0:T(8,128)(2,1)S(1)}, u32[]{:S(2)}, u32[]{:S(2)}) collective-permute-start(bf16[32,2048]{1,0:T(8,128)(2,1)S(1)} %get-tuple-element.91), channel_id=1, source_target_pairs={{0,2},{1,3},{2,0},{3,1},{4,6},{5,7},{6,4},{7,5},{8,10},{9,11},{10,... | collective-permute-start | bytes 393224 | tf_op jit(solution)/shard_map/ppermute | solution.py:410
  52.2 1.4 %collective-permute-done.15.refs_2_ = bf16[32,2176]{1,0:T(8,128)(2,1)S(1)} collective-permute-done((bf16[32,2176]{1,0:T(8,128)(2,1)S(1)}, bf16[32,2176]{1,0:T(8,128)(2,1)S(1)}, u32[]{:S(2)}, u32[]{:S(2)}) %collective-permute-start.15) | collective-permute-done | bytes 139296 | tf_op jit(solution)/shard_map/ppermute | solution.py:410
  53.6 1.0 %collective-permute-start.24 = (bf16[32,2048]{1,0:T(8,128)(2,1)S(1)}, bf16[32,2048]{1,0:T(8,128)(2,1)S(1)}, u32[]{:S(2)}, u32[]{:S(2)}) collective-permute-start(bf16[32,2048]{1,0:T(8,128)(2,1)S(1)} %get-tuple-element.93), channel_id=1, source_target_pairs={{0,6},{1,7},{2,4},{3,5},{4,2},{5,3},{6,0},{7,1},{8,14},{9,15},{10,... | collective-permute-start | bytes 393224 | tf_op jit(solution)/shard_map/ppermute | solution.py:410
  55.4 1.5 %collective-permute-start.18 = (bf16[32,2048]{1,0:T(8,128)(2,1)S(1)}, bf16[32,2048]{1,0:T(8,128)(2,1)S(1)}, u32[]{:S(2)}, u32[]{:S(2)}) collective-permute-start(bf16[32,2048]{1,0:T(8,128)(2,1)S(1)} %get-tuple-element.86), channel_id=1, source_target_pairs={{0,2},{1,3},{2,0},{3,1},{4,6},{5,7},{6,4},{7,5},{8,10},{9,11},{10,... | collective-permute-start | bytes 393224 | tf_op jit(solution)/shard_map/ppermute | solution.py:410
  56.9 2.5 %collective-permute-start.21 = (bf16[32,2176]{1,0:T(8,128)(2,1)S(1)}, bf16[32,2176]{1,0:T(8,128)(2,1)S(1)}, u32[]{:S(2)}, u32[]{:S(2)}) collective-permute-start(bf16[32,2176]{1,0:T(8,128)(2,1)S(1)} %get-tuple-element.85), channel_id=1, source_target_pairs={{0,24},{8,16},{16,8},{24,0},{1,25},{9,17},{17,9},{25,1},{2,26},{10... | collective-permute-start | bytes 417800 | tf_op jit(solution)/shard_map/ppermute | solution.py:413
  61.0 1.9 %collective-permute-start.25 = (bf16[32,2176]{1,0:T(8,128)(2,1)S(1)}, bf16[32,2176]{1,0:T(8,128)(2,1)S(1)}, u32[]{:S(2)}, u32[]{:S(2)}) collective-permute-start(bf16[32,2176]{1,0:T(8,128)(2,1)S(1)} %combine.6), channel_id=1, source_target_pairs={{0,16},{8,24},{16,0},{24,8},{1,17},{9,25},{17,1},{25,9},{2,18},{10... | collective-permute-start | bytes 417800 | tf_op jit(solution)/shard_map/ppermute | solution.py:413
  62.9 1.0 %collective-permute-start.19 = (bf16[32,2048]{1,0:T(8,128)(2,1)S(1)}, bf16[32,2048]{1,0:T(8,128)(2,1)S(1)}, u32[]{:S(2)}, u32[]{:S(2)}) collective-permute-start(bf16[32,2048]{1,0:T(8,128)(2,1)S(1)} %get-tuple-element.87), channel_id=1, source_target_pairs={{0,4},{1,5},{2,6},{3,7},{4,0},{5,1},{6,2},{7,3},{8,12},{9,13},{10,... | collective-permute-start | bytes 393224 | tf_op jit(solution)/shard_map/ppermute | solution.py:410
  63.9 1.0 %collective-permute-start.20 = (bf16[32,2048]{1,0:T(8,128)(2,1)S(1)}, bf16[32,2048]{1,0:T(8,128)(2,1)S(1)}, u32[]{:S(2)}, u32[]{:S(2)}) collective-permute-start(bf16[32,2048]{1,0:T(8,128)(2,1)S(1)} %get-tuple-element.88), channel_id=1, source_target_pairs={{0,6},{1,7},{2,4},{3,5},{4,2},{5,3},{6,0},{7,1},{8,14},{9,15},{10,... | collective-permute-start | bytes 393224 | tf_op jit(solution)/shard_map/ppermute | solution.py:410
  64.9 2.9 %collective-permute-done.19.refs_3_ = bf16[32,2048]{1,0:T(8,128)(2,1)S(1)} collective-permute-done((bf16[32,2048]{1,0:T(8,128)(2,1)S(1)}, bf16[32,2048]{1,0:T(8,128)(2,1)S(1)}, u32[]{:S(2)}, u32[]{:S(2)}) %collective-permute-start.19) | collective-permute-done | bytes 131104 | tf_op jit(solution)/shard_map/ppermute | solution.py:410
  67.8 1.9 %collective-permute-done.20.refs_4_ = bf16[32,2048]{1,0:T(8,128)(2,1)S(1)} collective-permute-done((bf16[32,2048]{1,0:T(8,128)(2,1)S(1)}, bf16[32,2048]{1,0:T(8,128)(2,1)S(1)}, u32[]{:S(2)}, u32[]{:S(2)}) %collective-permute-start.20) | collective-permute-done | bytes 131104 | tf_op jit(solution)/shard_map/ppermute | solution.py:410
  70.6 1.1 %collective-permute-start.29 = (bf16[32,2176]{1,0:T(8,128)(2,1)S(1)}, bf16[32,2176]{1,0:T(8,128)(2,1)S(1)}, u32[]{:S(2)}, u32[]{:S(2)}) collective-permute-start(bf16[32,2176]{1,0:T(8,128)(2,1)S(1)} %finish.1.refs_0_), channel_id=1, source_target_pairs={{0,6},{1,7},{2,4},{3,5},{4,2},{5,3},{6,0},{7,1},{8,14},{9,15},{10,... | collective-permute-start | bytes 417800 | tf_op jit(solution)/shard_map/ppermute | solution.py:410
  71.7 1.4 %collective-permute-start.28 = (bf16[32,2176]{1,0:T(8,128)(2,1)S(1)}, bf16[32,2176]{1,0:T(8,128)(2,1)S(1)}, u32[]{:S(2)}, u32[]{:S(2)}) collective-permute-start(bf16[32,2176]{1,0:T(8,128)(2,1)S(1)} %finish.1.refs_0_), channel_id=1, source_target_pairs={{0,4},{1,5},{2,6},{3,7},{4,0},{5,1},{6,2},{7,3},{8,12},{9,13},{10,... | collective-permute-start | bytes 417800 | tf_op jit(solution)/shard_map/ppermute | solution.py:410
  74.2 3.6 %collective-permute-done.29.refs_3_ = bf16[32,2176]{1,0:T(8,128)(2,1)S(1)} collective-permute-done((bf16[32,2176]{1,0:T(8,128)(2,1)S(1)}, bf16[32,2176]{1,0:T(8,128)(2,1)S(1)}, u32[]{:S(2)}, u32[]{:S(2)}) %collective-permute-start.29) | collective-permute-done | bytes 139296 | tf_op jit(solution)/shard_map/ppermute | solution.py:410
  77.7 1.3 %collective-permute-done.28.refs_2_ = bf16[32,2176]{1,0:T(8,128)(2,1)S(1)} collective-permute-done((bf16[32,2176]{1,0:T(8,128)(2,1)S(1)}, bf16[32,2176]{1,0:T(8,128)(2,1)S(1)}, u32[]{:S(2)}, u32[]{:S(2)}) %collective-permute-start.28) | collective-permute-done | bytes 139296 | tf_op jit(solution)/shard_map/ppermute | solution.py:410
  80.6 4.7 %final.1 = (bf16[256,2048]{1,0:T(8,128)(2,1)}, bf16[1,2048,768]{2,1,0:T(8,128)(2,1)}, bf16[1,384,2048]{2,1,0:T(8,128)(2,1)}) custom-call(bf16[32,2176]{1,0:T(8,128)(2,1)S(1)} %finish.1.refs_0_, bf16[32,2176]{1,0:T(8,128)(2,1)S(1)} %collective-permute-done.27.refs_1_, bf16[32,2176]{1,0:T(8,128)(2,1)S(1)} %collective-permute-done.28.refs_2_, ...), custom_call_target="tpu_custom_call" | custom-call | flops 100663296 | bytes 7340032 | tf_op jit(solution)/shard_map/final/pallas_call | solution.py:603
  (60 shorter events, 12.7 us)
Async XLA Ops:
  0.6 10.3 %collective-permute-start.3 = (bf16[1,2048,768]{2,1,0:T(8,128)(2,1)}, bf16[1,2048,768]{2,1,0:T(8,128)(2,1)}, u32[]{:S(2)}, u32[]{:S(2)}) collective-permute-start(bf16[1,2048,768]{2,1,0:T(8,128)(2,1)} %refs_11_), channel_id=1, source_target_pairs={{0,1},{1,0},{2,3},{3,2},{4,5},{5,4},{6,7},{7,6},{8,9},{9,8},{10,11... | collective-permute-start | bytes 9437192 | tf_op jit(solution)/shard_map/ppermute | solution.py:410
  1.2 9.7 %collective-permute-start.4 = (bf16[1,384,2048]{2,1,0:T(8,128)(2,1)}, bf16[1,384,2048]{2,1,0:T(8,128)(2,1)S(1)}, u32[]{:S(2)}, u32[]{:S(2)}) collective-permute-start(bf16[1,384,2048]{2,1,0:T(8,128)(2,1)} %refs_14_.1), channel_id=1, source_target_pairs={{0,1},{1,0},{2,3},{3,2},{4,5},{5,4},{6,7},{7,6},{8,9},{9,8},{10,11... | collective-permute-start | bytes 4718600 | tf_op jit(solution)/shard_map/ppermute | solution.py:410
  3.6 7.3 %collective-permute-start = (bf16[32,2176]{1,0:T(8,128)(2,1)}, bf16[32,2176]{1,0:T(8,128)(2,1)S(1)}, u32[]{:S(2)}, u32[]{:S(2)}) collective-permute-start(bf16[32,2176]{1,0:T(8,128)(2,1)} %pack.1.refs_1_.refs_0_), channel_id=1, source_target_pairs={{0,8},{8,0},{16,24},{24,16},{1,9},{9,1},{17,25},{25,17},{2,10},{10... | collective-permute-start | bytes 417800 | tf_op jit(solution)/shard_map/ppermute | solution.py:413
  6.6 10.3 %collective-permute-start.2 = (bf16[32,2176]{1,0:T(8,128)(2,1)}, bf16[32,2176]{1,0:T(8,128)(2,1)S(1)}, u32[]{:S(2)}, u32[]{:S(2)}) collective-permute-start(bf16[32,2176]{1,0:T(8,128)(2,1)} %pack.1.refs_1_.refs_0_), channel_id=1, source_target_pairs={{0,24},{8,16},{16,8},{24,0},{1,25},{9,17},{17,9},{25,1},{2,26},{10... | collective-permute-start | bytes 417800 | tf_op jit(solution)/shard_map/ppermute | solution.py:413
  9.1 13.1 %collective-permute-start.1 = (bf16[32,2176]{1,0:T(8,128)(2,1)}, bf16[32,2176]{1,0:T(8,128)(2,1)}, u32[]{:S(2)}, u32[]{:S(2)}) collective-permute-start(bf16[32,2176]{1,0:T(8,128)(2,1)} %pack.1.refs_1_.refs_0_), channel_id=1, source_target_pairs={{0,16},{8,24},{16,0},{24,8},{1,17},{9,25},{17,1},{25,9},{2,18},{10... | collective-permute-start | bytes 417800 | tf_op jit(solution)/shard_map/ppermute | solution.py:413
  10.9 12.2 %collective-permute-start.7 = (bf16[32,2304]{1,0:T(8,128)(2,1)S(1)}, bf16[32,2304]{1,0:T(8,128)(2,1)S(1)}, u32[]{:S(2)}, u32[]{:S(2)}) collective-permute-start(bf16[32,2304]{1,0:T(8,128)(2,1)S(1)} %pad_maximum_fusion.1), channel_id=1, source_target_pairs={{0,6},{1,7},{2,4},{3,5},{4,2},{5,3},{6,0},{7,1},{8,14},{9,15},{10,... | collective-permute-start | bytes 442376 | tf_op jit(solution)/shard_map/ppermute | solution.py:410
  13.5 9.6 %collective-permute-start.6 = (bf16[32,2304]{1,0:T(8,128)(2,1)S(1)}, bf16[32,2304]{1,0:T(8,128)(2,1)S(1)}, u32[]{:S(2)}, u32[]{:S(2)}) collective-permute-start(bf16[32,2304]{1,0:T(8,128)(2,1)S(1)} %pad_maximum_fusion.1), channel_id=1, source_target_pairs={{0,4},{1,5},{2,6},{3,7},{4,0},{5,1},{6,2},{7,3},{8,12},{9,13},{10,... | collective-permute-start | bytes 442376 | tf_op jit(solution)/shard_map/ppermute | solution.py:410
  14.0 9.1 %collective-permute-start.5 = (bf16[32,2304]{1,0:T(8,128)(2,1)S(1)}, bf16[32,2304]{1,0:T(8,128)(2,1)S(1)}, u32[]{:S(2)}, u32[]{:S(2)}) collective-permute-start(bf16[32,2304]{1,0:T(8,128)(2,1)S(1)} %pad_maximum_fusion.1), channel_id=1, source_target_pairs={{0,2},{1,3},{2,0},{3,1},{4,6},{5,7},{6,4},{7,5},{8,10},{9,11},{10,... | collective-permute-start | bytes 442376 | tf_op jit(solution)/shard_map/ppermute | solution.py:410
  23.1 15.0 %collective-permute-start.10 = (bf16[64,2176]{1,0:T(8,128)(2,1)S(1)}, bf16[64,2176]{1,0:T(8,128)(2,1)S(1)}, u32[]{:S(2)}, u32[]{:S(2)}) collective-permute-start(bf16[64,2176]{1,0:T(8,128)(2,1)S(1)} %pad_maximum_fusion), channel_id=1, source_target_pairs={{0,6},{1,7},{2,4},{3,5},{4,2},{5,3},{6,0},{7,1},{8,14},{9,15},{10,... | collective-permute-start | bytes 835592 | tf_op jit(solution)/shard_map/ppermute | solution.py:410
  25.6 13.0 %collective-permute-start.9 = (bf16[64,2176]{1,0:T(8,128)(2,1)S(1)}, bf16[64,2176]{1,0:T(8,128)(2,1)S(1)}, u32[]{:S(2)}, u32[]{:S(2)}) collective-permute-start(bf16[64,2176]{1,0:T(8,128)(2,1)S(1)} %pad_maximum_fusion), channel_id=1, source_target_pairs={{0,4},{1,5},{2,6},{3,7},{4,0},{5,1},{6,2},{7,3},{8,12},{9,13},{10,... | collective-permute-start | bytes 835592 | tf_op jit(solution)/shard_map/ppermute | solution.py:410
  26.1 13.6 %collective-permute-start.8 = (bf16[64,2176]{1,0:T(8,128)(2,1)S(1)}, bf16[64,2176]{1,0:T(8,128)(2,1)S(1)}, u32[]{:S(2)}, u32[]{:S(2)}) collective-permute-start(bf16[64,2176]{1,0:T(8,128)(2,1)S(1)} %pad_maximum_fusion), channel_id=1, source_target_pairs={{0,2},{1,3},{2,0},{3,1},{4,6},{5,7},{6,4},{7,5},{8,10},{9,11},{10,... | collective-permute-start | bytes 835592 | tf_op jit(solution)/shard_map/ppermute | solution.py:410
  35.1 10.0 %collective-permute-start.11 = (bf16[32,2048]{1,0:T(8,128)(2,1)S(1)}, bf16[32,2048]{1,0:T(8,128)(2,1)S(1)}, u32[]{:S(2)}, u32[]{:S(2)}) collective-permute-start(bf16[32,2048]{1,0:T(8,128)(2,1)S(1)} %get-tuple-element.70), channel_id=1, source_target_pairs={{0,2},{1,3},{2,0},{3,1},{4,6},{5,7},{6,4},{7,5},{8,10},{9,11},{10,... | collective-permute-start | bytes 393224 | tf_op jit(solution)/shard_map/ppermute | solution.py:410
  36.6 8.5 %collective-permute-start.12 = (bf16[32,2048]{1,0:T(8,128)(2,1)S(1)}, bf16[32,2048]{1,0:T(8,128)(2,1)S(1)}, u32[]{:S(2)}, u32[]{:S(2)}) collective-permute-start(bf16[32,2048]{1,0:T(8,128)(2,1)S(1)} %get-tuple-element.71), channel_id=1, source_target_pairs={{0,4},{1,5},{2,6},{3,7},{4,0},{5,1},{6,2},{7,3},{8,12},{9,13},{10,... | collective-permute-start | bytes 393224 | tf_op jit(solution)/shard_map/ppermute | solution.py:410
  38.2 7.0 %collective-permute-start.13 = (bf16[32,2048]{1,0:T(8,128)(2,1)S(1)}, bf16[32,2048]{1,0:T(8,128)(2,1)S(1)}, u32[]{:S(2)}, u32[]{:S(2)}) collective-permute-start(bf16[32,2048]{1,0:T(8,128)(2,1)S(1)} %get-tuple-element.72), channel_id=1, source_target_pairs={{0,6},{1,7},{2,4},{3,5},{4,2},{5,3},{6,0},{7,1},{8,14},{9,15},{10,... | collective-permute-start | bytes 393224 | tf_op jit(solution)/shard_map/ppermute | solution.py:410
  45.2 7.1 %collective-permute-start.14 = (bf16[32,2176]{1,0:T(8,128)(2,1)S(1)}, bf16[32,2176]{1,0:T(8,128)(2,1)S(1)}, u32[]{:S(2)}, u32[]{:S(2)}) collective-permute-start(bf16[32,2176]{1,0:T(8,128)(2,1)S(1)} %get-tuple-element.73), channel_id=1, source_target_pairs={{0,2},{1,3},{2,0},{3,1},{4,6},{5,7},{6,4},{7,5},{8,10},{9,11},{10,... | collective-permute-start | bytes 417800 | tf_op jit(solution)/shard_map/ppermute | solution.py:410
  46.7 7.0 %collective-permute-start.15 = (bf16[32,2176]{1,0:T(8,128)(2,1)S(1)}, bf16[32,2176]{1,0:T(8,128)(2,1)S(1)}, u32[]{:S(2)}, u32[]{:S(2)}) collective-permute-start(bf16[32,2176]{1,0:T(8,128)(2,1)S(1)} %get-tuple-element.74), channel_id=1, source_target_pairs={{0,4},{1,5},{2,6},{3,7},{4,0},{5,1},{6,2},{7,3},{8,12},{9,13},{10,... | collective-permute-start | bytes 417800 | tf_op jit(solution)/shard_map/ppermute | solution.py:410
  47.2 6.5 %collective-permute-start.16 = (bf16[32,2176]{1,0:T(8,128)(2,1)S(1)}, bf16[32,2176]{1,0:T(8,128)(2,1)S(1)}, u32[]{:S(2)}, u32[]{:S(2)}) collective-permute-start(bf16[32,2176]{1,0:T(8,128)(2,1)S(1)} %get-tuple-element.75), channel_id=1, source_target_pairs={{0,6},{1,7},{2,4},{3,5},{4,2},{5,3},{6,0},{7,1},{8,14},{9,15},{10,... | collective-permute-start | bytes 417800 | tf_op jit(solution)/shard_map/ppermute | solution.py:410
  50.1 1.6 %collective-permute-start.17 = (bf16[144,128]{1,0:T(8,128)(2,1)S(1)}, bf16[144,128]{1,0:T(8,128)(2,1)S(1)}, u32[]{:S(2)}, u32[]{:S(2)}) collective-permute-start(bf16[144,128]{1,0:T(8,128)(2,1)S(1)} %get-tuple-element.76), channel_id=1, source_target_pairs={{0,1},{1,0},{2,3},{3,2},{4,5},{5,4},{6,7},{7,6},{8,9},{9,8},{10,11... | collective-permute-start | bytes 110600 | tf_op jit(solution)/shard_map/ppermute | solution.py:410
  50.2 9.9 %collective-permute-start.22 = (bf16[32,2048]{1,0:T(8,128)(2,1)S(1)}, bf16[32,2048]{1,0:T(8,128)(2,1)S(1)}, u32[]{:S(2)}, u32[]{:S(2)}) collective-permute-start(bf16[32,2048]{1,0:T(8,128)(2,1)S(1)} %get-tuple-element.91), channel_id=1, source_target_pairs={{0,2},{1,3},{2,0},{3,1},{4,6},{5,7},{6,4},{7,5},{8,10},{9,11},{10,... | collective-permute-start | bytes 393224 | tf_op jit(solution)/shard_map/ppermute | solution.py:410
  51.7 8.5 %collective-permute-start.23 = (bf16[32,2048]{1,0:T(8,128)(2,1)S(1)}, bf16[32,2048]{1,0:T(8,128)(2,1)S(1)}, u32[]{:S(2)}, u32[]{:S(2)}) collective-permute-start(bf16[32,2048]{1,0:T(8,128)(2,1)S(1)} %get-tuple-element.92), channel_id=1, source_target_pairs={{0,4},{1,5},{2,6},{3,7},{4,0},{5,1},{6,2},{7,3},{8,12},{9,13},{10,... | collective-permute-start | bytes 393224 | tf_op jit(solution)/shard_map/ppermute | solution.py:410
  53.6 6.6 %collective-permute-start.24 = (bf16[32,2048]{1,0:T(8,128)(2,1)S(1)}, bf16[32,2048]{1,0:T(8,128)(2,1)S(1)}, u32[]{:S(2)}, u32[]{:S(2)}) collective-permute-start(bf16[32,2048]{1,0:T(8,128)(2,1)S(1)} %get-tuple-element.93), channel_id=1, source_target_pairs={{0,6},{1,7},{2,4},{3,5},{4,2},{5,3},{6,0},{7,1},{8,14},{9,15},{10,... | collective-permute-start | bytes 393224 | tf_op jit(solution)/shard_map/ppermute | solution.py:410
  55.4 8.5 %collective-permute-start.18 = (bf16[32,2048]{1,0:T(8,128)(2,1)S(1)}, bf16[32,2048]{1,0:T(8,128)(2,1)S(1)}, u32[]{:S(2)}, u32[]{:S(2)}) collective-permute-start(bf16[32,2048]{1,0:T(8,128)(2,1)S(1)} %get-tuple-element.86), channel_id=1, source_target_pairs={{0,2},{1,3},{2,0},{3,1},{4,6},{5,7},{6,4},{7,5},{8,10},{9,11},{10,... | collective-permute-start | bytes 393224 | tf_op jit(solution)/shard_map/ppermute | solution.py:410
  56.9 13.6 %collective-permute-start.21 = (bf16[32,2176]{1,0:T(8,128)(2,1)S(1)}, bf16[32,2176]{1,0:T(8,128)(2,1)S(1)}, u32[]{:S(2)}, u32[]{:S(2)}) collective-permute-start(bf16[32,2176]{1,0:T(8,128)(2,1)S(1)} %get-tuple-element.85), channel_id=1, source_target_pairs={{0,24},{8,16},{16,8},{24,0},{1,25},{9,17},{17,9},{25,1},{2,26},{10... | collective-permute-start | bytes 417800 | tf_op jit(solution)/shard_map/ppermute | solution.py:413
  60.1 10.4 %collective-permute-start.26 = (bf16[32,2176]{1,0:T(8,128)(2,1)S(1)}, bf16[32,2176]{1,0:T(8,128)(2,1)S(1)}, u32[]{:S(2)}, u32[]{:S(2)}) collective-permute-start(bf16[32,2176]{1,0:T(8,128)(2,1)S(1)} %combine.7), channel_id=1, source_target_pairs={{0,8},{8,0},{16,24},{24,16},{1,9},{9,1},{17,25},{25,17},{2,10},{10... | collective-permute-start | bytes 417800 | tf_op jit(solution)/shard_map/ppermute | solution.py:413
  61.0 9.5 %collective-permute-start.25 = (bf16[32,2176]{1,0:T(8,128)(2,1)S(1)}, bf16[32,2176]{1,0:T(8,128)(2,1)S(1)}, u32[]{:S(2)}, u32[]{:S(2)}) collective-permute-start(bf16[32,2176]{1,0:T(8,128)(2,1)S(1)} %combine.6), channel_id=1, source_target_pairs={{0,16},{8,24},{16,0},{24,8},{1,17},{9,25},{17,1},{25,9},{2,18},{10... | collective-permute-start | bytes 417800 | tf_op jit(solution)/shard_map/ppermute | solution.py:413
  62.9 5.0 %collective-permute-start.19 = (bf16[32,2048]{1,0:T(8,128)(2,1)S(1)}, bf16[32,2048]{1,0:T(8,128)(2,1)S(1)}, u32[]{:S(2)}, u32[]{:S(2)}) collective-permute-start(bf16[32,2048]{1,0:T(8,128)(2,1)S(1)} %get-tuple-element.87), channel_id=1, source_target_pairs={{0,4},{1,5},{2,6},{3,7},{4,0},{5,1},{6,2},{7,3},{8,12},{9,13},{10,... | collective-permute-start | bytes 393224 | tf_op jit(solution)/shard_map/ppermute | solution.py:410
  63.9 5.9 %collective-permute-start.20 = (bf16[32,2048]{1,0:T(8,128)(2,1)S(1)}, bf16[32,2048]{1,0:T(8,128)(2,1)S(1)}, u32[]{:S(2)}, u32[]{:S(2)}) collective-permute-start(bf16[32,2048]{1,0:T(8,128)(2,1)S(1)} %get-tuple-element.88), channel_id=1, source_target_pairs={{0,6},{1,7},{2,4},{3,5},{4,2},{5,3},{6,0},{7,1},{8,14},{9,15},{10,... | collective-permute-start | bytes 393224 | tf_op jit(solution)/shard_map/ppermute | solution.py:410
  70.6 7.1 %collective-permute-start.29 = (bf16[32,2176]{1,0:T(8,128)(2,1)S(1)}, bf16[32,2176]{1,0:T(8,128)(2,1)S(1)}, u32[]{:S(2)}, u32[]{:S(2)}) collective-permute-start(bf16[32,2176]{1,0:T(8,128)(2,1)S(1)} %finish.1.refs_0_), channel_id=1, source_target_pairs={{0,6},{1,7},{2,4},{3,5},{4,2},{5,3},{6,0},{7,1},{8,14},{9,15},{10,... | collective-permute-start | bytes 417800 | tf_op jit(solution)/shard_map/ppermute | solution.py:410
  71.7 7.3 %collective-permute-start.28 = (bf16[32,2176]{1,0:T(8,128)(2,1)S(1)}, bf16[32,2176]{1,0:T(8,128)(2,1)S(1)}, u32[]{:S(2)}, u32[]{:S(2)}) collective-permute-start(bf16[32,2176]{1,0:T(8,128)(2,1)S(1)} %finish.1.refs_0_), channel_id=1, source_target_pairs={{0,4},{1,5},{2,6},{3,7},{4,0},{5,1},{6,2},{7,3},{8,12},{9,13},{10,... | collective-permute-start | bytes 417800 | tf_op jit(solution)/shard_map/ppermute | solution.py:410
  73.2 5.9 %collective-permute-start.27 = (bf16[32,2176]{1,0:T(8,128)(2,1)S(1)}, bf16[32,2176]{1,0:T(8,128)(2,1)S(1)}, u32[]{:S(2)}, u32[]{:S(2)}) collective-permute-start(bf16[32,2176]{1,0:T(8,128)(2,1)S(1)} %finish.1.refs_0_), channel_id=1, source_target_pairs={{0,2},{1,3},{2,0},{3,1},{4,6},{5,7},{6,4},{7,5},{8,10},{9,11},{10,... | collective-permute-start | bytes 417800 | tf_op jit(solution)/shard_map/ppermute | solution.py:410
  74.2 5.4 %collective-permute-start.30 = (bf16[32,2176]{1,0:T(8,128)(2,1)S(1)}, bf16[32,2176]{1,0:T(8,128)(2,1)S(1)}, u32[]{:S(2)}, u32[]{:S(2)}) collective-permute-start(bf16[32,2176]{1,0:T(8,128)(2,1)S(1)} %finish.1.refs_0_), channel_id=1, source_target_pairs={{0,1},{1,0},{2,3},{3,2},{4,5},{5,4},{6,7},{7,6},{8,9},{9,8},{10,11... | collective-permute-start | bytes 417800 | tf_op jit(solution)/shard_map/ppermute | solution.py:410
  77.7 1.8 %collective-permute-start.33 = (bf16[32,2176]{1,0:T(8,128)(2,1)S(1)}, bf16[32,2176]{1,0:T(8,128)(2,1)S(1)}, u32[]{:S(2)}, u32[]{:S(2)}) collective-permute-start(bf16[32,2176]{1,0:T(8,128)(2,1)S(1)} %collective-permute-done.29.refs_3_), channel_id=1, source_target_pairs={{0,1},{1,0},{2,3},{3,2},{4,5},{5,4},{6,7},{7,6},{8,9},{9,8},{10,11... | collective-permute-start | bytes 417800 | tf_op jit(solution)/shard_map/ppermute | solution.py:410
  (7 other events, 51.9 us)

commit v12 on v11

--- a/solution.py
+++ b/solution.py
@@ -45,7 +45,9 @@
     return jnp.sum(jnp.where(index == wanted, table, 0.0), axis=1, keepdims=True)
 
 
-def pack_kernel(seq_dev, positives, ids_in, gates_in, tokens, out, tile, rows, ids, gates, sems):
+def pack_kernel(
+    seq_dev, partners, ids_in, gates_in, tokens, out, tile, rows, ids, gates, positives, sems
+):
     part_rows, width = out.shape[0], tokens.shape[1]
     tok_dev = tokens.shape[0]
     seq_length = tok_dev // seq_dev
@@ -67,6 +69,7 @@
     lines = [
         pltpu.make_async_copy(ids_in, ids, sems.at[seq_dev + 1]),
         pltpu.make_async_copy(gates_in, gates, sems.at[seq_dev + 2]),
+        pltpu.make_async_copy(partners, positives, sems.at[seq_dev + 3]),
     ]
     for copy in lines + [own] + copies:
         copy.start()
@@ -202,11 +205,6 @@
     tokens = refs.pop(0) if near else None
     parts, refs = dict(zip(used, refs)), refs[len(used) :]
     weights, refs = refs[:4], refs[4:]
-    copied, sem = refs[-2:]
-    mate_copy = pltpu.make_async_copy(weights[3], copied, sem)
-    mate_copy.start()
-    weights[3] = copied
-    refs = refs[:-2]
     n_outs = chips * len(group)
     outs, refs = refs[:n_outs], refs[n_outs:]
     if with_last:
@@ -234,7 +232,6 @@
             last_projected[...] = projected[total:]
         _, up, _, activated = hidden_parts(projected)
         hidden.append((activated * up).astype(bf16))
-    mate_copy.wait()
     block = min(512, width)
     if with_last:
         each = floats.shape[0] // by_lane.shape[0]
@@ -419,14 +416,15 @@
     packed = pl.pallas_call(
         functools.partial(pack_kernel, seq_dev),
         out_shape=jax.ShapeDtypeStruct((part_rows, width + lanes), bf16),
-        in_specs=[in_smem] + [in_hbm] * 3,
+        in_specs=[in_hbm] * 4,
         out_specs=in_vmem,
         scratch_shapes=[
             pltpu.VMEM((part_rows, lanes), f32),
             pltpu.VMEM((seq_dev, tail, share), bf16),
             pltpu.VMEM((1, tok_dev), jnp.int32),
             pltpu.VMEM((1, tok_dev), f32),
-            pltpu.SemaphoreType.DMA((seq_dev + 3,)),
+            pltpu.SMEM((seq_dev,), jnp.int32),
+            pltpu.SemaphoreType.DMA((seq_dev + 4,)),
         ],
         cost_estimate=cost(0, 1 << 19),
         name="pack",
@@ -490,14 +488,11 @@
                 pltpu.VMEM((dp_count, width // lanes, -(-seq_dev // 8) * 8, lanes), f32),
             ] + scratch
         operands = [place] + [tokens] * near + parts + list(weights)
-        scratch += [pltpu.VMEM(down.shape, bf16), pltpu.SemaphoreType.DMA(())]
         layout = (tuple(group), chips, part_rows, seq_dev, where_tiles, used, with_last)
         return pl.pallas_call(
             functools.partial(expert_kernel, layout),
             out_shape=out_shape,
-            in_specs=[in_smem]
-            + [in_vmem] * (len(operands) - 2)
-            + [pl.BlockSpec(memory_space=pl.ANY)],
+            in_specs=[in_smem] + [in_vmem] * (len(operands) - 1),
             out_specs=[in_vmem] * len(out_shape),
             scratch_shapes=scratch,
             compiler_params=params(32),
@@ -570,7 +565,7 @@
 
     send_back(1, 0, [])
     if dp_count > 2:
-        returned[1][1:] = send_back(dp_count - 1, chips - 1, returned[1][1:])
+        returned[1][1:-1] = send_back(dp_count - 1, chips - 1, returned[1][1:-1])
     before = dp_count - 1
     for hop in rest:
         returned[before][1:], found = send_back(hop, 1, (returned[before][1:], found))

time: 85.6 us -> 86.9 us (1.015)
  starting transfers between devices: 35.7 us -> 38.1 us
  Pallas kernels: 22 us -> 20.9 us
    ppermute x28, starting transfers between devices: 25.5 us -> 28.7 us  [to_lane(): lax.ppermute(value, 'expert', [(j, j ^ step) for j in range(expert_count)])]
  transfers between devices with their start and end apart: 34 -> 34, of which waited for: 12 -> 12; matrix products, arithmetic and copies ran while one was open for 2% -> 2% of each run, Pallas kernels for 20% -> 19%
where the time goes in v12:
time: 86.9 us; the launch traced here: 86.6 us
  starting transfers between devices  38.1 us (44%)
  waiting for transfers between devices  21.8 us (25%)
  Pallas kernels  20.9 us (24%)
  local copies, waits for them, and re-layouts  3.86 us (4%)
  other arithmetic  1.01 us (1%)
    ppermute x28, starting transfers between devices, to_lane(): lax.ppermute(value, 'expert', [(j, j ^ step) for j in range(expert_count)])  28.7 us
    ppermute x28, waiting for transfers between devices, to_lane(): lax.ppermute(value, 'expert', [(j, j ^ step) for j in range(expert_count)])  13.2 us
    pallas_call x2, Pallas kernels, expert(): pl.pallas_call(functools.partial(expert_kernel, layout), out_shape=out_sh...  10.2 us
    ppermute x6, starting transfers between devices, to_plane(): return lax.ppermute(value, 'dp', [(p, p ^ step) for p in range(dp_count)])  9.41 us
    ppermute x6, waiting for transfers between devices, to_plane(): return lax.ppermute(value, 'dp', [(p, p ^ step) for p in range(dp_count)])  8.62 us
    pallas_call x1, Pallas kernels, body(): pl.pallas_call(functools.partial(final_kernel, len(pieces), n_blocks), ou...  4.73 us
    unnamed x10, local copies, waits for them, and re-layouts  3.13 us
    pallas_call x4, Pallas kernels, combine(): pl.pallas_call(functools.partial(combine_kernel, (hop, chips, with_last,...  2.89 us
  transfers between devices with their start and end apart: 34, of which 12 were waited for; matrix products, arithmetic and copies ran while one was open for 2% of the time, Pallas kernels for 19%

profile of v12, /device:TPU:0, one launch (start us, length us, event | category | flops | bytes accessed | tf_op | source)
XLA Modules:
  0.0 86.6 jit_solution(1017582141570219146)
XLA Ops:
  1.2 1.7 %pack.1.refs_1_.refs_0_ = bf16[32,2176]{1,0:T(8,128)(2,1)} custom-call(s32[4]{0:T(128)} %partners.1, s32[1,256]{1,0:T(1,128)} %bitcast.5, f32[1,256]{1,0:T(1,128)} %bitcast.6, bf16[256,2048]{1,0:T(8,128)(2,1)} %refs_1_.1), custom_call_target="tpu_custom_call" | custom-call | bytes 524288 | tf_op jit(solution)/shard_map/pack/pallas_call | solution.py:416
  2.9 3.1 %collective-permute-start = (bf16[32,2176]{1,0:T(8,128)(2,1)}, bf16[32,2176]{1,0:T(8,128)(2,1)S(1)}, u32[]{:S(2)}, u32[]{:S(2)}) collective-permute-start(bf16[32,2176]{1,0:T(8,128)(2,1)} %pack.1.refs_1_.refs_0_), channel_id=1, source_target_pairs={{0,8},{8,0},{16,24},{24,16},{1,9},{9,1},{17,25},{25,17},{2,10},{10... | collective-permute-start | bytes 417800 | tf_op jit(solution)/shard_map/ppermute | solution.py:410
  6.0 2.5 %collective-permute-start.2 = (bf16[32,2176]{1,0:T(8,128)(2,1)}, bf16[32,2176]{1,0:T(8,128)(2,1)S(1)}, u32[]{:S(2)}, u32[]{:S(2)}) collective-permute-start(bf16[32,2176]{1,0:T(8,128)(2,1)} %pack.1.refs_1_.refs_0_), channel_id=1, source_target_pairs={{0,24},{8,16},{16,8},{24,0},{1,25},{9,17},{17,9},{25,1},{2,26},{10... | collective-permute-start | bytes 417800 | tf_op jit(solution)/shard_map/ppermute | solution.py:410
  9.3 0.9 %collective-permute-done.refs_2_.refs_1_ = bf16[32,2176]{1,0:T(8,128)(2,1)S(1)} collective-permute-done((bf16[32,2176]{1,0:T(8,128)(2,1)}, bf16[32,2176]{1,0:T(8,128)(2,1)S(1)}, u32[]{:S(2)}, u32[]{:S(2)}) %collective-permute-start) | collective-permute-done | bytes 139296 | tf_op jit(solution)/shard_map/ppermute | solution.py:410
  10.3 2.6 %collective-permute-start.7 = (bf16[32,2304]{1,0:T(8,128)(2,1)S(1)}, bf16[32,2304]{1,0:T(8,128)(2,1)S(1)}, u32[]{:S(2)}, u32[]{:S(2)}) collective-permute-start(bf16[32,2304]{1,0:T(8,128)(2,1)S(1)} %pad_maximum_fusion.1), channel_id=1, source_target_pairs={{0,6},{1,7},{2,4},{3,5},{4,2},{5,3},{6,0},{7,1},{8,14},{9,15},{10,... | collective-permute-start | bytes 442376 | tf_op jit(solution)/shard_map/ppermute | solution.py:407
  13.8 2.4 %collective-permute-done.2.refs_7_.refs_6_ = bf16[32,2176]{1,0:T(8,128)(2,1)S(1)} collective-permute-done((bf16[32,2176]{1,0:T(8,128)(2,1)}, bf16[32,2176]{1,0:T(8,128)(2,1)S(1)}, u32[]{:S(2)}, u32[]{:S(2)}) %collective-permute-start.2) | collective-permute-done | bytes 139296 | tf_op jit(solution)/shard_map/ppermute | solution.py:410
  16.2 5.3 %collective-permute-done.1.refs_6_.refs_5_ = bf16[32,2176]{1,0:T(8,128)(2,1)} collective-permute-done((bf16[32,2176]{1,0:T(8,128)(2,1)}, bf16[32,2176]{1,0:T(8,128)(2,1)}, u32[]{:S(2)}, u32[]{:S(2)}) %collective-permute-start.1) | collective-permute-done | bytes 139296 | tf_op jit(solution)/shard_map/ppermute | solution.py:410
  21.5 0.9 %pad_maximum_fusion = bf16[64,2176]{1,0:T(8,128)(2,1)S(1)} fusion(bf16[32,2176]{1,0:T(8,128)(2,1)S(1)} %collective-permute-done.2.refs_7_.refs_6_, bf16[32,2176]{1,0:T(8,128)(2,1)} %collective-permute-done.1.refs_6_.refs_5_), kind=kLoop, calls=%fused_computation | loop fusion | flops 557056 | bytes 557056 | tf_op jit(solution)/shard_map/concatenate | solution.py:446
  22.5 2.5 %collective-permute-start.10 = (bf16[64,2176]{1,0:T(8,128)(2,1)S(1)}, bf16[64,2176]{1,0:T(8,128)(2,1)S(1)}, u32[]{:S(2)}, u32[]{:S(2)}) collective-permute-start(bf16[64,2176]{1,0:T(8,128)(2,1)S(1)} %pad_maximum_fusion), channel_id=1, source_target_pairs={{0,6},{1,7},{2,4},{3,5},{4,2},{5,3},{6,0},{7,1},{8,14},{9,15},{10,... | collective-permute-start | bytes 835592 | tf_op jit(solution)/shard_map/ppermute | solution.py:407
  26.1 1.9 %copy-done.1 = bf16[1,2048,768]{2,1,0:T(8,128)(2,1)S(1)} copy-done((bf16[1,2048,768]{2,1,0:T(8,128)(2,1)S(1)}, bf16[1,2048,768]{2,1,0:T(8,128)(2,1)}, u32[]{:S(2)}) %copy-start.1) | copy-done | bytes 3145752
  28.0 1.2 %copy-done.3 = bf16[256,2048]{1,0:T(8,128)(2,1)S(1)} copy-done((bf16[256,2048]{1,0:T(8,128)(2,1)S(1)}, bf16[256,2048]{1,0:T(8,128)(2,1)}, u32[]{:S(2)}) %copy-start.3) | copy-done | bytes 1048600
  29.2 5.0 %experts.2 = (bf16[32,2048]{1,0:T(8,128)(2,1)S(1)}, bf16[32,2048]{1,0:T(8,128)(2,1)S(1)}, bf16[32,2048]{1,0:T(8,128)(2,1)S(1)}, bf16[32,2048]{1,0:T(8,128)(2,1)S...) custom-call(s32[3]{0:T(128)S(1)} %pad_add_fusion.refs_0_.place.refs_, ...), custom_call_target="tpu_custom_call" | custom-call | flops 2415919104 | bytes 12582912 | tf_op jit(solution)/shard_map/experts/pallas_call | solution.py:492
  34.2 1.6 %collective-permute-start.11 = (bf16[32,2048]{1,0:T(8,128)(2,1)S(1)}, bf16[32,2048]{1,0:T(8,128)(2,1)S(1)}, u32[]{:S(2)}, u32[]{:S(2)}) collective-permute-start(bf16[32,2048]{1,0:T(8,128)(2,1)S(1)} %get-tuple-element.69), channel_id=1, source_target_pairs={{0,2},{1,3},{2,0},{3,1},{4,6},{5,7},{6,4},{7,5},{8,10},{9,11},{10,... | collective-permute-start | bytes 393224 | tf_op jit(solution)/shard_map/ppermute | solution.py:407
  35.8 1.5 %collective-permute-start.12 = (bf16[32,2048]{1,0:T(8,128)(2,1)S(1)}, bf16[32,2048]{1,0:T(8,128)(2,1)S(1)}, u32[]{:S(2)}, u32[]{:S(2)}) collective-permute-start(bf16[32,2048]{1,0:T(8,128)(2,1)S(1)} %get-tuple-element.70), channel_id=1, source_target_pairs={{0,4},{1,5},{2,6},{3,7},{4,0},{5,1},{6,2},{7,3},{8,12},{9,13},{10,... | collective-permute-start | bytes 393224 | tf_op jit(solution)/shard_map/ppermute | solution.py:407
  37.3 1.4 %collective-permute-done.8.refs_8_.refs_7_ = bf16[64,2176]{1,0:T(8,128)(2,1)S(1)} collective-permute-done((bf16[64,2176]{1,0:T(8,128)(2,1)S(1)}, bf16[64,2176]{1,0:T(8,128)(2,1)S(1)}, u32[]{:S(2)}, u32[]{:S(2)}) %collective-permute-start.8) | collective-permute-done | bytes 278560 | tf_op jit(solution)/shard_map/ppermute | solution.py:407
  38.7 5.2 %experts.3 = (bf16[32,2048]{1,0:T(8,128)(2,1)S(1)}, bf16[32,2048]{1,0:T(8,128)(2,1)S(1)}, bf16[32,2048]{1,0:T(8,128)(2,1)S(1)}, bf16[32,2048]{1,0:T(8,128)(2,1)S...) custom-call(s32[3]{0:T(128)S(1)} %pad_add_fusion.refs_0_.place.refs_, ...), custom_call_target="tpu_custom_call" | custom-call | flops 2566914048 | bytes 12582912 | tf_op jit(solution)/shard_map/experts/pallas_call | solution.py:492
  43.9 1.6 %collective-permute-start.13 = (bf16[32,2176]{1,0:T(8,128)(2,1)S(1)}, bf16[32,2176]{1,0:T(8,128)(2,1)S(1)}, u32[]{:S(2)}, u32[]{:S(2)}) collective-permute-start(bf16[32,2176]{1,0:T(8,128)(2,1)S(1)} %get-tuple-element.71), channel_id=1, source_target_pairs={{0,2},{1,3},{2,0},{3,1},{4,6},{5,7},{6,4},{7,5},{8,10},{9,11},{10,... | collective-permute-start | bytes 417800 | tf_op jit(solution)/shard_map/ppermute | solution.py:407
  45.7 1.8 %collective-permute-start.15 = (bf16[32,2176]{1,0:T(8,128)(2,1)S(1)}, bf16[32,2176]{1,0:T(8,128)(2,1)S(1)}, u32[]{:S(2)}, u32[]{:S(2)}) collective-permute-start(bf16[32,2176]{1,0:T(8,128)(2,1)S(1)} %get-tuple-element.73), channel_id=1, source_target_pairs={{0,6},{1,7},{2,4},{3,5},{4,2},{5,3},{6,0},{7,1},{8,14},{9,15},{10,... | collective-permute-start | bytes 417800 | tf_op jit(solution)/shard_map/ppermute | solution.py:407
  47.5 1.4 %tables.1 = (bf16[144,128]{1,0:T(8,128)(2,1)S(1)}, bf16[144,128]{1,0:T(8,128)(2,1)S(1)}, f32[16,128]{1,0:T(8,128)S(1)}) custom-call(s32[3]{0:T(128)S(1)} %pad_add_fusion.refs_0_.place.refs_10_, bf16[32,2176]{1,0:T(8,128)(2,1)S(1)} %copy-done.4, bf16[32,2176]{1,0:T(8,128)(2,1)S(1)} %collective-permute-done.refs_2_.refs_1_, ...), custom_call_target="tpu_custom_call" | custom-call | bytes 1048576 | tf_op jit(solution)/shard_map/tables/pallas_call | solution.py:519
  49.0 1.2 %collective-permute-start.25 = (bf16[32,2048]{1,0:T(8,128)(2,1)S(1)}, bf16[32,2048]{1,0:T(8,128)(2,1)S(1)}, u32[]{:S(2)}, u32[]{:S(2)}) collective-permute-start(bf16[32,2048]{1,0:T(8,128)(2,1)S(1)} %get-tuple-element.95), channel_id=1, source_target_pairs={{0,6},{1,7},{2,4},{3,5},{4,2},{5,3},{6,0},{7,1},{8,14},{9,15},{10,... | collective-permute-start | bytes 393224 | tf_op jit(solution)/shard_map/ppermute | solution.py:407
  50.2 1.5 %collective-permute-start.21 = (bf16[32,2048]{1,0:T(8,128)(2,1)S(1)}, bf16[32,2048]{1,0:T(8,128)(2,1)S(1)}, u32[]{:S(2)}, u32[]{:S(2)}) collective-permute-start(bf16[32,2048]{1,0:T(8,128)(2,1)S(1)} %get-tuple-element.89), channel_id=1, source_target_pairs={{0,2},{1,3},{2,0},{3,1},{4,6},{5,7},{6,4},{7,5},{8,10},{9,11},{10,... | collective-permute-start | bytes 393224 | tf_op jit(solution)/shard_map/ppermute | solution.py:407
  51.7 0.9 %collective-permute-start.22 = (bf16[32,2048]{1,0:T(8,128)(2,1)S(1)}, bf16[32,2048]{1,0:T(8,128)(2,1)S(1)}, u32[]{:S(2)}, u32[]{:S(2)}) collective-permute-start(bf16[32,2048]{1,0:T(8,128)(2,1)S(1)} %get-tuple-element.90), channel_id=1, source_target_pairs={{0,4},{1,5},{2,6},{3,7},{4,0},{5,1},{6,2},{7,3},{8,12},{9,13},{10,... | collective-permute-start | bytes 393224 | tf_op jit(solution)/shard_map/ppermute | solution.py:407
  54.5 4.0 %collective-permute-start.17 = (bf16[32,2048]{1,0:T(8,128)(2,1)S(1)}, bf16[32,2048]{1,0:T(8,128)(2,1)S(1)}, u32[]{:S(2)}, u32[]{:S(2)}) collective-permute-start(bf16[32,2048]{1,0:T(8,128)(2,1)S(1)} %get-tuple-element.84), channel_id=1, source_target_pairs={{0,2},{1,3},{2,0},{3,1},{4,6},{5,7},{6,4},{7,5},{8,10},{9,11},{10,... | collective-permute-start | bytes 393224 | tf_op jit(solution)/shard_map/ppermute | solution.py:407
  59.4 1.6 %collective-permute-start.26 = (bf16[32,2176]{1,0:T(8,128)(2,1)S(1)}, bf16[32,2176]{1,0:T(8,128)(2,1)S(1)}, u32[]{:S(2)}, u32[]{:S(2)}) collective-permute-start(bf16[32,2176]{1,0:T(8,128)(2,1)S(1)} %combine.7), channel_id=1, source_target_pairs={{0,8},{8,0},{16,24},{24,16},{1,9},{9,1},{17,25},{25,17},{2,10},{10... | collective-permute-start | bytes 417800 | tf_op jit(solution)/shard_map/ppermute | solution.py:410
  62.6 1.9 %collective-permute-start.24 = (bf16[32,2176]{1,0:T(8,128)(2,1)S(1)}, bf16[32,2176]{1,0:T(8,128)(2,1)S(1)}, u32[]{:S(2)}, u32[]{:S(2)}) collective-permute-start(bf16[32,2176]{1,0:T(8,128)(2,1)S(1)} %combine.6), channel_id=1, source_target_pairs={{0,16},{8,24},{16,0},{24,8},{1,17},{9,25},{17,1},{25,9},{2,18},{10... | collective-permute-start | bytes 417800 | tf_op jit(solution)/shard_map/ppermute | solution.py:410
  64.9 1.5 %collective-permute-start.19 = (bf16[32,2048]{1,0:T(8,128)(2,1)S(1)}, bf16[32,2048]{1,0:T(8,128)(2,1)S(1)}, u32[]{:S(2)}, u32[]{:S(2)}) collective-permute-start(bf16[32,2048]{1,0:T(8,128)(2,1)S(1)} %get-tuple-element.86), channel_id=1, source_target_pairs={{0,6},{1,7},{2,4},{3,5},{4,2},{5,3},{6,0},{7,1},{8,14},{9,15},{10,... | collective-permute-start | bytes 393224 | tf_op jit(solution)/shard_map/ppermute | solution.py:407
  66.4 3.0 %collective-permute-done.18.refs_3_ = bf16[32,2048]{1,0:T(8,128)(2,1)S(1)} collective-permute-done((bf16[32,2048]{1,0:T(8,128)(2,1)S(1)}, bf16[32,2048]{1,0:T(8,128)(2,1)S(1)}, u32[]{:S(2)}, u32[]{:S(2)}) %collective-permute-start.18) | collective-permute-done | bytes 131104 | tf_op jit(solution)/shard_map/ppermute | solution.py:407
  69.5 1.4 %collective-permute-done.19.refs_4_ = bf16[32,2048]{1,0:T(8,128)(2,1)S(1)} collective-permute-done((bf16[32,2048]{1,0:T(8,128)(2,1)S(1)}, bf16[32,2048]{1,0:T(8,128)(2,1)S(1)}, u32[]{:S(2)}, u32[]{:S(2)}) %collective-permute-start.19) | collective-permute-done | bytes 131104 | tf_op jit(solution)/shard_map/ppermute | solution.py:407
  71.7 1.9 %collective-permute-start.29 = (bf16[32,2176]{1,0:T(8,128)(2,1)S(1)}, bf16[32,2176]{1,0:T(8,128)(2,1)S(1)}, u32[]{:S(2)}, u32[]{:S(2)}) collective-permute-start(bf16[32,2176]{1,0:T(8,128)(2,1)S(1)} %finish.1.refs_0_), channel_id=1, source_target_pairs={{0,6},{1,7},{2,4},{3,5},{4,2},{5,3},{6,0},{7,1},{8,14},{9,15},{10,... | collective-permute-start | bytes 417800 | tf_op jit(solution)/shard_map/ppermute | solution.py:407
  75.2 3.6 %collective-permute-done.29.refs_3_ = bf16[32,2176]{1,0:T(8,128)(2,1)S(1)} collective-permute-done((bf16[32,2176]{1,0:T(8,128)(2,1)S(1)}, bf16[32,2176]{1,0:T(8,128)(2,1)S(1)}, u32[]{:S(2)}, u32[]{:S(2)}) %collective-permute-start.29) | collective-permute-done | bytes 139296 | tf_op jit(solution)/shard_map/ppermute | solution.py:407
  78.8 1.4 %collective-permute-done.28.refs_2_ = bf16[32,2176]{1,0:T(8,128)(2,1)S(1)} collective-permute-done((bf16[32,2176]{1,0:T(8,128)(2,1)S(1)}, bf16[32,2176]{1,0:T(8,128)(2,1)S(1)}, u32[]{:S(2)}, u32[]{:S(2)}) %collective-permute-start.28) | collective-permute-done | bytes 139296 | tf_op jit(solution)/shard_map/ppermute | solution.py:407
  81.8 4.7 %final.1 = (bf16[256,2048]{1,0:T(8,128)(2,1)}, bf16[1,2048,768]{2,1,0:T(8,128)(2,1)}, bf16[1,384,2048]{2,1,0:T(8,128)(2,1)}) custom-call(bf16[32,2176]{1,0:T(8,128)(2,1)S(1)} %finish.1.refs_0_, bf16[32,2176]{1,0:T(8,128)(2,1)S(1)} %collective-permute-done.27.refs_1_, bf16[32,2176]{1,0:T(8,128)(2,1)S(1)} %collective-permute-done.28.refs_2_, ...), custom_call_target="tpu_custom_call" | custom-call | flops 100663296 | bytes 7340032 | tf_op jit(solution)/shard_map/final/pallas_call | solution.py:598
  (60 shorter events, 12.7 us)
Async XLA Ops:
  0.6 9.6 %collective-permute-start.3 = (bf16[1,2048,768]{2,1,0:T(8,128)(2,1)}, bf16[1,2048,768]{2,1,0:T(8,128)(2,1)}, u32[]{:S(2)}, u32[]{:S(2)}) collective-permute-start(bf16[1,2048,768]{2,1,0:T(8,128)(2,1)} %refs_11_), channel_id=1, source_target_pairs={{0,1},{1,0},{2,3},{3,2},{4,5},{5,4},{6,7},{7,6},{8,9},{9,8},{10,11... | collective-permute-start | bytes 9437192 | tf_op jit(solution)/shard_map/ppermute | solution.py:407
  1.2 9.1 %collective-permute-start.4 = (bf16[1,384,2048]{2,1,0:T(8,128)(2,1)}, bf16[1,384,2048]{2,1,0:T(8,128)(2,1)S(1)}, u32[]{:S(2)}, u32[]{:S(2)}) collective-permute-start(bf16[1,384,2048]{2,1,0:T(8,128)(2,1)} %refs_14_.1), channel_id=1, source_target_pairs={{0,1},{1,0},{2,3},{3,2},{4,5},{5,4},{6,7},{7,6},{8,9},{9,8},{10,11... | collective-permute-start | bytes 4718600 | tf_op jit(solution)/shard_map/ppermute | solution.py:407
  2.9 7.3 %collective-permute-start = (bf16[32,2176]{1,0:T(8,128)(2,1)}, bf16[32,2176]{1,0:T(8,128)(2,1)S(1)}, u32[]{:S(2)}, u32[]{:S(2)}) collective-permute-start(bf16[32,2176]{1,0:T(8,128)(2,1)} %pack.1.refs_1_.refs_0_), channel_id=1, source_target_pairs={{0,8},{8,0},{16,24},{24,16},{1,9},{9,1},{17,25},{25,17},{2,10},{10... | collective-permute-start | bytes 417800 | tf_op jit(solution)/shard_map/ppermute | solution.py:410
  6.0 10.3 %collective-permute-start.2 = (bf16[32,2176]{1,0:T(8,128)(2,1)}, bf16[32,2176]{1,0:T(8,128)(2,1)S(1)}, u32[]{:S(2)}, u32[]{:S(2)}) collective-permute-start(bf16[32,2176]{1,0:T(8,128)(2,1)} %pack.1.refs_1_.refs_0_), channel_id=1, source_target_pairs={{0,24},{8,16},{16,8},{24,0},{1,25},{9,17},{17,9},{25,1},{2,26},{10... | collective-permute-start | bytes 417800 | tf_op jit(solution)/shard_map/ppermute | solution.py:410
  8.5 13.1 %collective-permute-start.1 = (bf16[32,2176]{1,0:T(8,128)(2,1)}, bf16[32,2176]{1,0:T(8,128)(2,1)}, u32[]{:S(2)}, u32[]{:S(2)}) collective-permute-start(bf16[32,2176]{1,0:T(8,128)(2,1)} %pack.1.refs_1_.refs_0_), channel_id=1, source_target_pairs={{0,16},{8,24},{16,0},{24,8},{1,17},{9,25},{17,1},{25,9},{2,18},{10... | collective-permute-start | bytes 417800 | tf_op jit(solution)/shard_map/ppermute | solution.py:410
  10.3 12.2 %collective-permute-start.7 = (bf16[32,2304]{1,0:T(8,128)(2,1)S(1)}, bf16[32,2304]{1,0:T(8,128)(2,1)S(1)}, u32[]{:S(2)}, u32[]{:S(2)}) collective-permute-start(bf16[32,2304]{1,0:T(8,128)(2,1)S(1)} %pad_maximum_fusion.1), channel_id=1, source_target_pairs={{0,6},{1,7},{2,4},{3,5},{4,2},{5,3},{6,0},{7,1},{8,14},{9,15},{10,... | collective-permute-start | bytes 442376 | tf_op jit(solution)/shard_map/ppermute | solution.py:407
  12.9 9.6 %collective-permute-start.6 = (bf16[32,2304]{1,0:T(8,128)(2,1)S(1)}, bf16[32,2304]{1,0:T(8,128)(2,1)S(1)}, u32[]{:S(2)}, u32[]{:S(2)}) collective-permute-start(bf16[32,2304]{1,0:T(8,128)(2,1)S(1)} %pad_maximum_fusion.1), channel_id=1, source_target_pairs={{0,4},{1,5},{2,6},{3,7},{4,0},{5,1},{6,2},{7,3},{8,12},{9,13},{10,... | collective-permute-start | bytes 442376 | tf_op jit(solution)/shard_map/ppermute | solution.py:407
  13.4 9.1 %collective-permute-start.5 = (bf16[32,2304]{1,0:T(8,128)(2,1)S(1)}, bf16[32,2304]{1,0:T(8,128)(2,1)S(1)}, u32[]{:S(2)}, u32[]{:S(2)}) collective-permute-start(bf16[32,2304]{1,0:T(8,128)(2,1)S(1)} %pad_maximum_fusion.1), channel_id=1, source_target_pairs={{0,2},{1,3},{2,0},{3,1},{4,6},{5,7},{6,4},{7,5},{8,10},{9,11},{10,... | collective-permute-start | bytes 442376 | tf_op jit(solution)/shard_map/ppermute | solution.py:407
  22.5 14.8 %collective-permute-start.10 = (bf16[64,2176]{1,0:T(8,128)(2,1)S(1)}, bf16[64,2176]{1,0:T(8,128)(2,1)S(1)}, u32[]{:S(2)}, u32[]{:S(2)}) collective-permute-start(bf16[64,2176]{1,0:T(8,128)(2,1)S(1)} %pad_maximum_fusion), channel_id=1, source_target_pairs={{0,6},{1,7},{2,4},{3,5},{4,2},{5,3},{6,0},{7,1},{8,14},{9,15},{10,... | collective-permute-start | bytes 835592 | tf_op jit(solution)/shard_map/ppermute | solution.py:407
  25.0 12.3 %collective-permute-start.9 = (bf16[64,2176]{1,0:T(8,128)(2,1)S(1)}, bf16[64,2176]{1,0:T(8,128)(2,1)S(1)}, u32[]{:S(2)}, u32[]{:S(2)}) collective-permute-start(bf16[64,2176]{1,0:T(8,128)(2,1)S(1)} %pad_maximum_fusion), channel_id=1, source_target_pairs={{0,4},{1,5},{2,6},{3,7},{4,0},{5,1},{6,2},{7,3},{8,12},{9,13},{10,... | collective-permute-start | bytes 835592 | tf_op jit(solution)/shard_map/ppermute | solution.py:407
  25.5 13.2 %collective-permute-start.8 = (bf16[64,2176]{1,0:T(8,128)(2,1)S(1)}, bf16[64,2176]{1,0:T(8,128)(2,1)S(1)}, u32[]{:S(2)}, u32[]{:S(2)}) collective-permute-start(bf16[64,2176]{1,0:T(8,128)(2,1)S(1)} %pad_maximum_fusion), channel_id=1, source_target_pairs={{0,2},{1,3},{2,0},{3,1},{4,6},{5,7},{6,4},{7,5},{8,10},{9,11},{10,... | collective-permute-start | bytes 835592 | tf_op jit(solution)/shard_map/ppermute | solution.py:407
  34.2 9.7 %collective-permute-start.11 = (bf16[32,2048]{1,0:T(8,128)(2,1)S(1)}, bf16[32,2048]{1,0:T(8,128)(2,1)S(1)}, u32[]{:S(2)}, u32[]{:S(2)}) collective-permute-start(bf16[32,2048]{1,0:T(8,128)(2,1)S(1)} %get-tuple-element.69), channel_id=1, source_target_pairs={{0,2},{1,3},{2,0},{3,1},{4,6},{5,7},{6,4},{7,5},{8,10},{9,11},{10,... | collective-permute-start | bytes 393224 | tf_op jit(solution)/shard_map/ppermute | solution.py:407
  35.8 8.1 %collective-permute-start.12 = (bf16[32,2048]{1,0:T(8,128)(2,1)S(1)}, bf16[32,2048]{1,0:T(8,128)(2,1)S(1)}, u32[]{:S(2)}, u32[]{:S(2)}) collective-permute-start(bf16[32,2048]{1,0:T(8,128)(2,1)S(1)} %get-tuple-element.70), channel_id=1, source_target_pairs={{0,4},{1,5},{2,6},{3,7},{4,0},{5,1},{6,2},{7,3},{8,12},{9,13},{10,... | collective-permute-start | bytes 393224 | tf_op jit(solution)/shard_map/ppermute | solution.py:407
  43.9 7.8 %collective-permute-start.13 = (bf16[32,2176]{1,0:T(8,128)(2,1)S(1)}, bf16[32,2176]{1,0:T(8,128)(2,1)S(1)}, u32[]{:S(2)}, u32[]{:S(2)}) collective-permute-start(bf16[32,2176]{1,0:T(8,128)(2,1)S(1)} %get-tuple-element.71), channel_id=1, source_target_pairs={{0,2},{1,3},{2,0},{3,1},{4,6},{5,7},{6,4},{7,5},{8,10},{9,11},{10,... | collective-permute-start | bytes 417800 | tf_op jit(solution)/shard_map/ppermute | solution.py:407
  45.5 7.5 %collective-permute-start.14 = (bf16[32,2176]{1,0:T(8,128)(2,1)S(1)}, bf16[32,2176]{1,0:T(8,128)(2,1)S(1)}, u32[]{:S(2)}, u32[]{:S(2)}) collective-permute-start(bf16[32,2176]{1,0:T(8,128)(2,1)S(1)} %get-tuple-element.72), channel_id=1, source_target_pairs={{0,4},{1,5},{2,6},{3,7},{4,0},{5,1},{6,2},{7,3},{8,12},{9,13},{10,... | collective-permute-start | bytes 417800 | tf_op jit(solution)/shard_map/ppermute | solution.py:407
  45.7 7.3 %collective-permute-start.15 = (bf16[32,2176]{1,0:T(8,128)(2,1)S(1)}, bf16[32,2176]{1,0:T(8,128)(2,1)S(1)}, u32[]{:S(2)}, u32[]{:S(2)}) collective-permute-start(bf16[32,2176]{1,0:T(8,128)(2,1)S(1)} %get-tuple-element.73), channel_id=1, source_target_pairs={{0,6},{1,7},{2,4},{3,5},{4,2},{5,3},{6,0},{7,1},{8,14},{9,15},{10,... | collective-permute-start | bytes 417800 | tf_op jit(solution)/shard_map/ppermute | solution.py:407
  49.0 9.5 %collective-permute-start.25 = (bf16[32,2048]{1,0:T(8,128)(2,1)S(1)}, bf16[32,2048]{1,0:T(8,128)(2,1)S(1)}, u32[]{:S(2)}, u32[]{:S(2)}) collective-permute-start(bf16[32,2048]{1,0:T(8,128)(2,1)S(1)} %get-tuple-element.95), channel_id=1, source_target_pairs={{0,6},{1,7},{2,4},{3,5},{4,2},{5,3},{6,0},{7,1},{8,14},{9,15},{10,... | collective-permute-start | bytes 393224 | tf_op jit(solution)/shard_map/ppermute | solution.py:407
  50.2 9.2 %collective-permute-start.21 = (bf16[32,2048]{1,0:T(8,128)(2,1)S(1)}, bf16[32,2048]{1,0:T(8,128)(2,1)S(1)}, u32[]{:S(2)}, u32[]{:S(2)}) collective-permute-start(bf16[32,2048]{1,0:T(8,128)(2,1)S(1)} %get-tuple-element.89), channel_id=1, source_target_pairs={{0,2},{1,3},{2,0},{3,1},{4,6},{5,7},{6,4},{7,5},{8,10},{9,11},{10,... | collective-permute-start | bytes 393224 | tf_op jit(solution)/shard_map/ppermute | solution.py:407
  51.7 9.4 %collective-permute-start.22 = (bf16[32,2048]{1,0:T(8,128)(2,1)S(1)}, bf16[32,2048]{1,0:T(8,128)(2,1)S(1)}, u32[]{:S(2)}, u32[]{:S(2)}) collective-permute-start(bf16[32,2048]{1,0:T(8,128)(2,1)S(1)} %get-tuple-element.90), channel_id=1, source_target_pairs={{0,4},{1,5},{2,6},{3,7},{4,0},{5,1},{6,2},{7,3},{8,12},{9,13},{10,... | collective-permute-start | bytes 393224 | tf_op jit(solution)/shard_map/ppermute | solution.py:407
  53.0 8.8 %collective-permute-start.23 = (bf16[32,2048]{1,0:T(8,128)(2,1)S(1)}, bf16[32,2048]{1,0:T(8,128)(2,1)S(1)}, u32[]{:S(2)}, u32[]{:S(2)}) collective-permute-start(bf16[32,2048]{1,0:T(8,128)(2,1)S(1)} %get-tuple-element.91), channel_id=1, source_target_pairs={{0,6},{1,7},{2,4},{3,5},{4,2},{5,3},{6,0},{7,1},{8,14},{9,15},{10,... | collective-permute-start | bytes 393224 | tf_op jit(solution)/shard_map/ppermute | solution.py:407
  54.5 10.4 %collective-permute-start.17 = (bf16[32,2048]{1,0:T(8,128)(2,1)S(1)}, bf16[32,2048]{1,0:T(8,128)(2,1)S(1)}, u32[]{:S(2)}, u32[]{:S(2)}) collective-permute-start(bf16[32,2048]{1,0:T(8,128)(2,1)S(1)} %get-tuple-element.84), channel_id=1, source_target_pairs={{0,2},{1,3},{2,0},{3,1},{4,6},{5,7},{6,4},{7,5},{8,10},{9,11},{10,... | collective-permute-start | bytes 393224 | tf_op jit(solution)/shard_map/ppermute | solution.py:407
  58.5 13.1 %collective-permute-start.20 = (bf16[32,2176]{1,0:T(8,128)(2,1)S(1)}, bf16[32,2176]{1,0:T(8,128)(2,1)S(1)}, u32[]{:S(2)}, u32[]{:S(2)}) collective-permute-start(bf16[32,2176]{1,0:T(8,128)(2,1)S(1)} %get-tuple-element.83), channel_id=1, source_target_pairs={{0,24},{8,16},{16,8},{24,0},{1,25},{9,17},{17,9},{25,1},{2,26},{10... | collective-permute-start | bytes 417800 | tf_op jit(solution)/shard_map/ppermute | solution.py:410
  59.4 12.2 %collective-permute-start.26 = (bf16[32,2176]{1,0:T(8,128)(2,1)S(1)}, bf16[32,2176]{1,0:T(8,128)(2,1)S(1)}, u32[]{:S(2)}, u32[]{:S(2)}) collective-permute-start(bf16[32,2176]{1,0:T(8,128)(2,1)S(1)} %combine.7), channel_id=1, source_target_pairs={{0,8},{8,0},{16,24},{24,16},{1,9},{9,1},{17,25},{25,17},{2,10},{10... | collective-permute-start | bytes 417800 | tf_op jit(solution)/shard_map/ppermute | solution.py:410
  62.6 9.0 %collective-permute-start.24 = (bf16[32,2176]{1,0:T(8,128)(2,1)S(1)}, bf16[32,2176]{1,0:T(8,128)(2,1)S(1)}, u32[]{:S(2)}, u32[]{:S(2)}) collective-permute-start(bf16[32,2176]{1,0:T(8,128)(2,1)S(1)} %combine.6), channel_id=1, source_target_pairs={{0,16},{8,24},{16,0},{24,8},{1,17},{9,25},{17,1},{25,9},{2,18},{10... | collective-permute-start | bytes 417800 | tf_op jit(solution)/shard_map/ppermute | solution.py:410
  64.5 5.0 %collective-permute-start.18 = (bf16[32,2048]{1,0:T(8,128)(2,1)S(1)}, bf16[32,2048]{1,0:T(8,128)(2,1)S(1)}, u32[]{:S(2)}, u32[]{:S(2)}) collective-permute-start(bf16[32,2048]{1,0:T(8,128)(2,1)S(1)} %get-tuple-element.85), channel_id=1, source_target_pairs={{0,4},{1,5},{2,6},{3,7},{4,0},{5,1},{6,2},{7,3},{8,12},{9,13},{10,... | collective-permute-start | bytes 393224 | tf_op jit(solution)/shard_map/ppermute | solution.py:407
  64.9 5.9 %collective-permute-start.19 = (bf16[32,2048]{1,0:T(8,128)(2,1)S(1)}, bf16[32,2048]{1,0:T(8,128)(2,1)S(1)}, u32[]{:S(2)}, u32[]{:S(2)}) collective-permute-start(bf16[32,2048]{1,0:T(8,128)(2,1)S(1)} %get-tuple-element.86), channel_id=1, source_target_pairs={{0,6},{1,7},{2,4},{3,5},{4,2},{5,3},{6,0},{7,1},{8,14},{9,15},{10,... | collective-permute-start | bytes 393224 | tf_op jit(solution)/shard_map/ppermute | solution.py:407
  71.7 7.1 %collective-permute-start.29 = (bf16[32,2176]{1,0:T(8,128)(2,1)S(1)}, bf16[32,2176]{1,0:T(8,128)(2,1)S(1)}, u32[]{:S(2)}, u32[]{:S(2)}) collective-permute-start(bf16[32,2176]{1,0:T(8,128)(2,1)S(1)} %finish.1.refs_0_), channel_id=1, source_target_pairs={{0,6},{1,7},{2,4},{3,5},{4,2},{5,3},{6,0},{7,1},{8,14},{9,15},{10,... | collective-permute-start | bytes 417800 | tf_op jit(solution)/shard_map/ppermute | solution.py:407
  73.6 6.7 %collective-permute-start.28 = (bf16[32,2176]{1,0:T(8,128)(2,1)S(1)}, bf16[32,2176]{1,0:T(8,128)(2,1)S(1)}, u32[]{:S(2)}, u32[]{:S(2)}) collective-permute-start(bf16[32,2176]{1,0:T(8,128)(2,1)S(1)} %finish.1.refs_0_), channel_id=1, source_target_pairs={{0,4},{1,5},{2,6},{3,7},{4,0},{5,1},{6,2},{7,3},{8,12},{9,13},{10,... | collective-permute-start | bytes 417800 | tf_op jit(solution)/shard_map/ppermute | solution.py:407
  74.4 5.9 %collective-permute-start.27 = (bf16[32,2176]{1,0:T(8,128)(2,1)S(1)}, bf16[32,2176]{1,0:T(8,128)(2,1)S(1)}, u32[]{:S(2)}, u32[]{:S(2)}) collective-permute-start(bf16[32,2176]{1,0:T(8,128)(2,1)S(1)} %finish.1.refs_0_), channel_id=1, source_target_pairs={{0,2},{1,3},{2,0},{3,1},{4,6},{5,7},{6,4},{7,5},{8,10},{9,11},{10,... | collective-permute-start | bytes 417800 | tf_op jit(solution)/shard_map/ppermute | solution.py:407
  75.2 5.5 %collective-permute-start.30 = (bf16[32,2176]{1,0:T(8,128)(2,1)S(1)}, bf16[32,2176]{1,0:T(8,128)(2,1)S(1)}, u32[]{:S(2)}, u32[]{:S(2)}) collective-permute-start(bf16[32,2176]{1,0:T(8,128)(2,1)S(1)} %finish.1.refs_0_), channel_id=1, source_target_pairs={{0,1},{1,0},{2,3},{3,2},{4,5},{5,4},{6,7},{7,6},{8,9},{9,8},{10,11... | collective-permute-start | bytes 417800 | tf_op jit(solution)/shard_map/ppermute | solution.py:407
  78.8 2.0 %collective-permute-start.33 = (bf16[32,2176]{1,0:T(8,128)(2,1)S(1)}, bf16[32,2176]{1,0:T(8,128)(2,1)S(1)}, u32[]{:S(2)}, u32[]{:S(2)}) collective-permute-start(bf16[32,2176]{1,0:T(8,128)(2,1)S(1)} %collective-permute-done.29.refs_3_), channel_id=1, source_target_pairs={{0,1},{1,0},{2,3},{3,2},{4,5},{5,4},{6,7},{7,6},{8,9},{9,8},{10,11... | collective-permute-start | bytes 417800 | tf_op jit(solution)/shard_map/ppermute | solution.py:407
  80.3 1.5 %collective-permute-start.31 = (bf16[32,2176]{1,0:T(8,128)(2,1)S(1)}, bf16[32,2176]{1,0:T(8,128)(2,1)S(1)}, u32[]{:S(2)}, u32[]{:S(2)}) collective-permute-start(bf16[32,2176]{1,0:T(8,128)(2,1)S(1)} %collective-permute-done.27.refs_1_), channel_id=1, source_target_pairs={{0,1},{1,0},{2,3},{3,2},{4,5},{5,4},{6,7},{7,6},{8,9},{9,8},{10,11... | collective-permute-start | bytes 417800 | tf_op jit(solution)/shard_map/ppermute | solution.py:407
  (7 other events, 50.2 us)

commit v13 on v12

--- a/solution.py
+++ b/solution.py
@@ -167,13 +167,20 @@
     return gate, up, sigmoid_gate, gate * sigmoid_gate
 
 
-def spread_rows(values, rows, blocks):
-    chunks = values.shape[1] // lanes
-    for index in range(values.shape[0] * chunks):
-        row, chunk = index // chunks, index % chunks
-        spot = slice(index % rows, index % rows + 1)
-        block = slice(index // rows * lanes, (index // rows + 1) * lanes)
-        blocks[spot, block] = values[row : row + 1, chunk * lanes : (chunk + 1) * lanes]
+def spread_rows(values, flat):
+    count, chunks = values.shape[0], values.shape[1] // lanes
+    for chunk in range(chunks):
+        flat[pl.ds(chunk, count, stride=chunks), :] = values[:, chunk * lanes : (chunk + 1) * lanes]
+
+
+def share_of(flat, lane, each, part_rows, chunks):
+    size = each * chunks
+    start = lane * size
+    blocks = [
+        flat[pl.ds(pl.multiple_of(start + first, part_rows), part_rows), :]
+        for first in range(0, size, part_rows)
+    ]
+    return blocks[0] if len(blocks) == 1 else jnp.concatenate(blocks, axis=1)
 
 
 def last_tokens(place, seq_dev, where_tiles, parts, tokens):
@@ -208,7 +215,7 @@
     n_outs = chips * len(group)
     outs, refs = refs[:n_outs], refs[n_outs:]
     if with_last:
-        last_all, last_projected, own_last, by_lane, tile, seq_tokens, *refs = refs
+        last_all, last_projected, own_last, flat, seq_tokens, *refs = refs
     (rows,) = refs
     width = weights[0].shape[1]
     total = n_outs * part_rows
@@ -233,8 +240,7 @@
         _, up, _, activated = hidden_parts(projected)
         hidden.append((activated * up).astype(bf16))
     block = min(512, width)
-    if with_last:
-        each = floats.shape[0] // by_lane.shape[0]
+    chunks = width // lanes
     for first in range(0, width, block):
         columns = slice(first, first + block)
         result = dot(hidden[0], weights[1][0, :, columns]) + dot(
@@ -243,17 +249,18 @@
         for out, spot in zip(outs, spots):
             out[:, columns] = result[spot].astype(bf16)
         if with_last:
-            for lane in range(by_lane.shape[0]):
-                at = total + lane * each
-                by_lane[lane, 0:each, columns] = result[at : at + each]
+            count = result.shape[0] - total
+            for at in range(0, block, lanes):
+                flat[pl.ds((first + at) // lanes, count, stride=chunks), :] = result[
+                    total:, at : at + lanes
+                ]
     if with_last:
+        each = floats.shape[0] // (2 * chips)
         for chip in range(chips):
-            spread_rows(by_lane[place[1] ^ (2 * chip), 0:each, :], part_rows, tile)
-            outs[n_outs - chips + chip][:, width:] = tile[...].astype(bf16)
-        for lane in range(by_lane.shape[0]):
-            by_lane[lane, 0:each, :] = floats[lane * each : (lane + 1) * each]
-        spread_rows(by_lane[place[1], 0:each, :], part_rows, tile)
-        own_last[...] = tile[...]
+            share = share_of(flat, place[1] ^ (2 * chip), each, part_rows, chunks)
+            outs[n_outs - chips + chip][:, width:] = share.astype(bf16)
+        spread_rows(floats, flat)
+        own_last[...] = share_of(flat, place[1], each, part_rows, chunks)
 
 
 def combine_kernel(layout, place, kept, found, *refs):
@@ -304,21 +311,19 @@
     out[:, width:] = (own_last[...] + last).astype(bf16)
 
 
-def collect_rows(lane, pieces, by_lane, width):
+def collect_rows(lane, pieces, flat, width):
     part_rows, chunks = pieces[0].shape[0], width // lanes
     count = len(pieces)
-    each = (pieces[0].shape[1] - width) * part_rows // width
+    size = flat.shape[0] // count
     for index in range(count):
         source = lane ^ (2 * (index % (count // 2))) ^ (index // (count // 2))
-        values = pieces[index][:, width:].astype(f32)
-        for spot in range(each * chunks):
-            row, chunk = spot // chunks, spot % chunks
-            at = spot // part_rows * lanes
-            from_row = spot % part_rows
-            by_lane[source, row : row + 1, chunk * lanes : (chunk + 1) * lanes] = values[
-                from_row : from_row + 1, at : at + lanes
-            ]
-    return jnp.concatenate([by_lane[index, 0:each, :] for index in range(count)], axis=0)
+        for first in range(0, size, part_rows):
+            at = width + first // part_rows * lanes
+            start = pl.multiple_of(source * size + first, part_rows)
+            flat[pl.ds(start, part_rows), :] = pieces[index][:, at : at + lanes].astype(f32)
+    rows = flat.shape[0] // chunks
+    columns = [flat[pl.ds(chunk, rows, stride=chunks), :] for chunk in range(chunks)]
+    return jnp.concatenate(columns, axis=1)
 
 
 def both_ways(coefficient, unit, diagonal):
@@ -339,7 +344,7 @@
 def final_kernel(n_pieces, n_blocks, *refs):
     pieces, refs = refs[:n_pieces], refs[n_pieces:]
     last_all, projected, place, kept, found, partners, down, *refs = refs
-    layer_out, grad_in, grad_out, made_in, made_out, by_lane, sems = refs
+    layer_out, grad_in, grad_out, made_in, made_out, flat, sems = refs
     part_rows, width = pieces[0].shape[0], layer_out.shape[1]
     copies = []
 
@@ -351,7 +356,7 @@
         lane = place[1] ^ (2 * (index % (n_pieces // 2))) ^ (index // (n_pieces // 2))
         start = pl.multiple_of(lane * part_rows, part_rows)
         send(pieces[index].at[:, pl.ds(0, width)], layer_out.at[pl.ds(start, part_rows)])
-    values = collect_rows(place[1], pieces, by_lane, width)
+    values = collect_rows(place[1], pieces, flat, width)
     count = values.shape[0]
     last = kept.shape[0] - count
     table = kept[last:, :].astype(f32) + found[last:, :].astype(f32)
@@ -372,7 +377,7 @@
     route_grad = (column(table, place[2]) * grad_last).astype(bf16)
     gate, up, sigmoid_gate, activated = hidden_parts(projected[...])
     hidden = (activated * up).astype(bf16)
-    grad_hidden = dot(route_grad, down[0], ((1,), (1,)))
+    grad_hidden = dot(down[0], route_grad, ((1,), (1,))).T
     gate_slope = sigmoid_gate * (1.0 + gate * (1.0 - sigmoid_gate))
     slope = jnp.concatenate([grad_hidden * up * gate_slope, grad_hidden * activated], axis=1)
     slope = slope.astype(bf16)
@@ -483,8 +488,7 @@
                 jax.ShapeDtypeStruct((part_rows, extra), f32),
             ]
             scratch = [
-                pltpu.VMEM((expert_count, -(-each // 8) * 8, width), f32),
-                pltpu.VMEM((part_rows, extra), f32),
+                pltpu.VMEM((seqs * (width // lanes), lanes), f32),
                 pltpu.VMEM((dp_count, width // lanes, -(-seq_dev // 8) * 8, lanes), f32),
             ] + scratch
         operands = [place] + [tokens] * near + parts + list(weights)
@@ -565,7 +569,7 @@
 
     send_back(1, 0, [])
     if dp_count > 2:
-        returned[1][1:-1] = send_back(dp_count - 1, chips - 1, returned[1][1:-1])
+        returned[1][1:] = send_back(dp_count - 1, chips - 1, returned[1][1:])
     before = dp_count - 1
     for hop in rest:
         returned[before][1:], found = send_back(hop, 1, (returned[before][1:], found))
@@ -607,7 +611,7 @@
         scratch_shapes=[
             pltpu.VMEM((width, 2 * half_width), bf16),
             pltpu.VMEM((half_width, width), bf16),
-            pltpu.VMEM((expert_count, -(-each // 8) * 8, width), f32),
+            pltpu.VMEM((seqs * (width // lanes), lanes), f32),
             pltpu.SemaphoreType.DMA((len(pieces) + n_blocks + 1,)),
         ],
         compiler_params=params(24),

time: 86.9 us -> 85.3 us (0.982)
  starting transfers between devices: 38.1 us -> 35.4 us
    ppermute x28, starting transfers between devices: 28.7 us -> 25.2 us  [to_lane(): lax.ppermute(value, 'expert', [(j, j ^ step) for j in range(expert_count)])]
  transfers between devices with their start and end apart: 34 -> 34, of which waited for: 12 -> 11; matrix products, arithmetic and copies ran while one was open for 2% -> 2% of each run, Pallas kernels for 19% -> 19%
where the time goes in v13:
time: 85.3 us; the launch traced here: 85 us
  starting transfers between devices  35.4 us (42%)
  waiting for transfers between devices  22.4 us (26%)
  Pallas kernels  21.5 us (25%)
  local copies, waits for them, and re-layouts  3.86 us (5%)
  other arithmetic  1.01 us (1%)
    ppermute x28, starting transfers between devices, to_lane(): lax.ppermute(value, 'expert', [(j, j ^ step) for j in range(expert_count)])  25.2 us
    ppermute x28, waiting for transfers between devices, to_lane(): lax.ppermute(value, 'expert', [(j, j ^ step) for j in range(expert_count)])  13.8 us
    ppermute x6, starting transfers between devices, to_plane(): return lax.ppermute(value, 'dp', [(p, p ^ step) for p in range(dp_count)])  10.2 us
    pallas_call x2, Pallas kernels, expert(): pl.pallas_call(functools.partial(expert_kernel, layout), out_shape=out_sh...  10.1 us
    ppermute x6, waiting for transfers between devices, to_plane(): return lax.ppermute(value, 'dp', [(p, p ^ step) for p in range(dp_count)])  8.62 us
    pallas_call x1, Pallas kernels, body(): pl.pallas_call(functools.partial(final_kernel, len(pieces), n_blocks), ou...  5.3 us
    unnamed x10, local copies, waits for them, and re-layouts  3.13 us
    pallas_call x4, Pallas kernels, combine(): pl.pallas_call(functools.partial(combine_kernel, (hop, chips, with_last,...  2.89 us
  transfers between devices with their start and end apart: 34, of which 11 were waited for; matrix products, arithmetic and copies ran while one was open for 2% of the time, Pallas kernels for 19%

profile of v13, /device:TPU:0, one launch (start us, length us, event | category | flops | bytes accessed | tf_op | source)
XLA Modules:
  0.0 85.0 jit_solution(7944837587571940532)
XLA Ops:
  1.2 1.7 %pack.1.refs_1_.refs_0_ = bf16[32,2176]{1,0:T(8,128)(2,1)} custom-call(s32[4]{0:T(128)} %partners.1, s32[1,256]{1,0:T(1,128)} %bitcast.5, f32[1,256]{1,0:T(1,128)} %bitcast.6, bf16[256,2048]{1,0:T(8,128)(2,1)} %refs_1_.1), custom_call_target="tpu_custom_call" | custom-call | bytes 524288 | tf_op jit(solution)/shard_map/pack/pallas_call | solution.py:421
  2.9 3.1 %collective-permute-start = (bf16[32,2176]{1,0:T(8,128)(2,1)}, bf16[32,2176]{1,0:T(8,128)(2,1)S(1)}, u32[]{:S(2)}, u32[]{:S(2)}) collective-permute-start(bf16[32,2176]{1,0:T(8,128)(2,1)} %pack.1.refs_1_.refs_0_), channel_id=1, source_target_pairs={{0,8},{8,0},{16,24},{24,16},{1,9},{9,1},{17,25},{25,17},{2,10},{10... | collective-permute-start | bytes 417800 | tf_op jit(solution)/shard_map/ppermute | solution.py:415
  6.0 2.5 %collective-permute-start.2 = (bf16[32,2176]{1,0:T(8,128)(2,1)}, bf16[32,2176]{1,0:T(8,128)(2,1)S(1)}, u32[]{:S(2)}, u32[]{:S(2)}) collective-permute-start(bf16[32,2176]{1,0:T(8,128)(2,1)} %pack.1.refs_1_.refs_0_), channel_id=1, source_target_pairs={{0,24},{8,16},{16,8},{24,0},{1,25},{9,17},{17,9},{25,1},{2,26},{10... | collective-permute-start | bytes 417800 | tf_op jit(solution)/shard_map/ppermute | solution.py:415
  10.3 2.6 %collective-permute-start.7 = (bf16[32,2304]{1,0:T(8,128)(2,1)S(1)}, bf16[32,2304]{1,0:T(8,128)(2,1)S(1)}, u32[]{:S(2)}, u32[]{:S(2)}) collective-permute-start(bf16[32,2304]{1,0:T(8,128)(2,1)S(1)} %pad_maximum_fusion.1), channel_id=1, source_target_pairs={{0,6},{1,7},{2,4},{3,5},{4,2},{5,3},{6,0},{7,1},{8,14},{9,15},{10,... | collective-permute-start | bytes 442376 | tf_op jit(solution)/shard_map/ppermute | solution.py:412
  13.8 2.4 %collective-permute-done.2.refs_7_.refs_6_ = bf16[32,2176]{1,0:T(8,128)(2,1)S(1)} collective-permute-done((bf16[32,2176]{1,0:T(8,128)(2,1)}, bf16[32,2176]{1,0:T(8,128)(2,1)S(1)}, u32[]{:S(2)}, u32[]{:S(2)}) %collective-permute-start.2) | collective-permute-done | bytes 139296 | tf_op jit(solution)/shard_map/ppermute | solution.py:415
  16.2 5.3 %collective-permute-done.1.refs_6_.refs_5_ = bf16[32,2176]{1,0:T(8,128)(2,1)} collective-permute-done((bf16[32,2176]{1,0:T(8,128)(2,1)}, bf16[32,2176]{1,0:T(8,128)(2,1)}, u32[]{:S(2)}, u32[]{:S(2)}) %collective-permute-start.1) | collective-permute-done | bytes 139296 | tf_op jit(solution)/shard_map/ppermute | solution.py:415
  21.5 0.9 %pad_maximum_fusion = bf16[64,2176]{1,0:T(8,128)(2,1)S(1)} fusion(bf16[32,2176]{1,0:T(8,128)(2,1)S(1)} %collective-permute-done.2.refs_7_.refs_6_, bf16[32,2176]{1,0:T(8,128)(2,1)} %collective-permute-done.1.refs_6_.refs_5_), kind=kLoop, calls=%fused_computation | loop fusion | flops 557056 | bytes 557056 | tf_op jit(solution)/shard_map/concatenate | solution.py:451
  22.5 2.5 %collective-permute-start.10 = (bf16[64,2176]{1,0:T(8,128)(2,1)S(1)}, bf16[64,2176]{1,0:T(8,128)(2,1)S(1)}, u32[]{:S(2)}, u32[]{:S(2)}) collective-permute-start(bf16[64,2176]{1,0:T(8,128)(2,1)S(1)} %pad_maximum_fusion), channel_id=1, source_target_pairs={{0,6},{1,7},{2,4},{3,5},{4,2},{5,3},{6,0},{7,1},{8,14},{9,15},{10,... | collective-permute-start | bytes 835592 | tf_op jit(solution)/shard_map/ppermute | solution.py:412
  26.1 1.9 %copy-done.1 = bf16[1,2048,768]{2,1,0:T(8,128)(2,1)S(1)} copy-done((bf16[1,2048,768]{2,1,0:T(8,128)(2,1)S(1)}, bf16[1,2048,768]{2,1,0:T(8,128)(2,1)}, u32[]{:S(2)}) %copy-start.1) | copy-done | bytes 3145752
  28.0 1.2 %copy-done.3 = bf16[256,2048]{1,0:T(8,128)(2,1)S(1)} copy-done((bf16[256,2048]{1,0:T(8,128)(2,1)S(1)}, bf16[256,2048]{1,0:T(8,128)(2,1)}, u32[]{:S(2)}) %copy-start.3) | copy-done | bytes 1048600
  29.2 5.0 %experts.2 = (bf16[32,2048]{1,0:T(8,128)(2,1)S(1)}, bf16[32,2048]{1,0:T(8,128)(2,1)S(1)}, bf16[32,2048]{1,0:T(8,128)(2,1)S(1)}, bf16[32,2048]{1,0:T(8,128)(2,1)S...) custom-call(s32[3]{0:T(128)S(1)} %pad_add_fusion.refs_0_.place.refs_, ...), custom_call_target="tpu_custom_call" | custom-call | flops 2415919104 | bytes 12582912 | tf_op jit(solution)/shard_map/experts/pallas_call | solution.py:496
  34.2 1.6 %collective-permute-start.11 = (bf16[32,2048]{1,0:T(8,128)(2,1)S(1)}, bf16[32,2048]{1,0:T(8,128)(2,1)S(1)}, u32[]{:S(2)}, u32[]{:S(2)}) collective-permute-start(bf16[32,2048]{1,0:T(8,128)(2,1)S(1)} %get-tuple-element.70), channel_id=1, source_target_pairs={{0,2},{1,3},{2,0},{3,1},{4,6},{5,7},{6,4},{7,5},{8,10},{9,11},{10,... | collective-permute-start | bytes 393224 | tf_op jit(solution)/shard_map/ppermute | solution.py:412
  35.8 1.5 %collective-permute-start.12 = (bf16[32,2048]{1,0:T(8,128)(2,1)S(1)}, bf16[32,2048]{1,0:T(8,128)(2,1)S(1)}, u32[]{:S(2)}, u32[]{:S(2)}) collective-permute-start(bf16[32,2048]{1,0:T(8,128)(2,1)S(1)} %get-tuple-element.71), channel_id=1, source_target_pairs={{0,4},{1,5},{2,6},{3,7},{4,0},{5,1},{6,2},{7,3},{8,12},{9,13},{10,... | collective-permute-start | bytes 393224 | tf_op jit(solution)/shard_map/ppermute | solution.py:412
  37.8 1.3 %collective-permute-done.8.refs_8_.refs_7_ = bf16[64,2176]{1,0:T(8,128)(2,1)S(1)} collective-permute-done((bf16[64,2176]{1,0:T(8,128)(2,1)S(1)}, bf16[64,2176]{1,0:T(8,128)(2,1)S(1)}, u32[]{:S(2)}, u32[]{:S(2)}) %collective-permute-start.8) | collective-permute-done | bytes 278560 | tf_op jit(solution)/shard_map/ppermute | solution.py:412
  39.1 5.1 %experts.3 = (bf16[32,2048]{1,0:T(8,128)(2,1)S(1)}, bf16[32,2048]{1,0:T(8,128)(2,1)S(1)}, bf16[32,2048]{1,0:T(8,128)(2,1)S(1)}, bf16[32,2048]{1,0:T(8,128)(2,1)S...) custom-call(s32[3]{0:T(128)S(1)} %pad_add_fusion.refs_0_.place.refs_, ...), custom_call_target="tpu_custom_call" | custom-call | flops 2566914048 | bytes 12582912 | tf_op jit(solution)/shard_map/experts/pallas_call | solution.py:496
  44.2 1.5 %collective-permute-start.14 = (bf16[32,2176]{1,0:T(8,128)(2,1)S(1)}, bf16[32,2176]{1,0:T(8,128)(2,1)S(1)}, u32[]{:S(2)}, u32[]{:S(2)}) collective-permute-start(bf16[32,2176]{1,0:T(8,128)(2,1)S(1)} %get-tuple-element.73), channel_id=1, source_target_pairs={{0,2},{1,3},{2,0},{3,1},{4,6},{5,7},{6,4},{7,5},{8,10},{9,11},{10,... | collective-permute-start | bytes 417800 | tf_op jit(solution)/shard_map/ppermute | solution.py:412
  46.0 1.7 %collective-permute-start.16 = (bf16[32,2176]{1,0:T(8,128)(2,1)S(1)}, bf16[32,2176]{1,0:T(8,128)(2,1)S(1)}, u32[]{:S(2)}, u32[]{:S(2)}) collective-permute-start(bf16[32,2176]{1,0:T(8,128)(2,1)S(1)} %get-tuple-element.75), channel_id=1, source_target_pairs={{0,6},{1,7},{2,4},{3,5},{4,2},{5,3},{6,0},{7,1},{8,14},{9,15},{10,... | collective-permute-start | bytes 417800 | tf_op jit(solution)/shard_map/ppermute | solution.py:412
  47.8 1.4 %tables.1 = (bf16[144,128]{1,0:T(8,128)(2,1)S(1)}, bf16[144,128]{1,0:T(8,128)(2,1)S(1)}, f32[16,128]{1,0:T(8,128)S(1)}) custom-call(s32[3]{0:T(128)S(1)} %pad_add_fusion.refs_0_.place.refs_10_, bf16[32,2176]{1,0:T(8,128)(2,1)S(1)} %copy-done.4, bf16[32,2176]{1,0:T(8,128)(2,1)S(1)} %collective-permute-done.refs_2_.refs_1_, ...), custom_call_target="tpu_custom_call" | custom-call | bytes 1048576 | tf_op jit(solution)/shard_map/tables/pallas_call | solution.py:523
  49.3 1.5 %collective-permute-start.22 = (bf16[32,2048]{1,0:T(8,128)(2,1)S(1)}, bf16[32,2048]{1,0:T(8,128)(2,1)S(1)}, u32[]{:S(2)}, u32[]{:S(2)}) collective-permute-start(bf16[32,2048]{1,0:T(8,128)(2,1)S(1)} %get-tuple-element.91), channel_id=1, source_target_pairs={{0,2},{1,3},{2,0},{3,1},{4,6},{5,7},{6,4},{7,5},{8,10},{9,11},{10,... | collective-permute-start | bytes 393224 | tf_op jit(solution)/shard_map/ppermute | solution.py:412
  51.1 1.7 %collective-permute-done.15.refs_2_ = bf16[32,2176]{1,0:T(8,128)(2,1)S(1)} collective-permute-done((bf16[32,2176]{1,0:T(8,128)(2,1)S(1)}, bf16[32,2176]{1,0:T(8,128)(2,1)S(1)}, u32[]{:S(2)}, u32[]{:S(2)}) %collective-permute-start.15) | collective-permute-done | bytes 139296 | tf_op jit(solution)/shard_map/ppermute | solution.py:412
  54.5 1.5 %collective-permute-start.18 = (bf16[32,2048]{1,0:T(8,128)(2,1)S(1)}, bf16[32,2048]{1,0:T(8,128)(2,1)S(1)}, u32[]{:S(2)}, u32[]{:S(2)}) collective-permute-start(bf16[32,2048]{1,0:T(8,128)(2,1)S(1)} %get-tuple-element.86), channel_id=1, source_target_pairs={{0,2},{1,3},{2,0},{3,1},{4,6},{5,7},{6,4},{7,5},{8,10},{9,11},{10,... | collective-permute-start | bytes 393224 | tf_op jit(solution)/shard_map/ppermute | solution.py:412
  56.0 2.6 %collective-permute-start.21 = (bf16[32,2176]{1,0:T(8,128)(2,1)S(1)}, bf16[32,2176]{1,0:T(8,128)(2,1)S(1)}, u32[]{:S(2)}, u32[]{:S(2)}) collective-permute-start(bf16[32,2176]{1,0:T(8,128)(2,1)S(1)} %get-tuple-element.85), channel_id=1, source_target_pairs={{0,24},{8,16},{16,8},{24,0},{1,25},{9,17},{17,9},{25,1},{2,26},{10... | collective-permute-start | bytes 417800 | tf_op jit(solution)/shard_map/ppermute | solution.py:415
  60.2 1.8 %collective-permute-start.25 = (bf16[32,2176]{1,0:T(8,128)(2,1)S(1)}, bf16[32,2176]{1,0:T(8,128)(2,1)S(1)}, u32[]{:S(2)}, u32[]{:S(2)}) collective-permute-start(bf16[32,2176]{1,0:T(8,128)(2,1)S(1)} %combine.6), channel_id=1, source_target_pairs={{0,16},{8,24},{16,0},{24,8},{1,17},{9,25},{17,1},{25,9},{2,18},{10... | collective-permute-start | bytes 417800 | tf_op jit(solution)/shard_map/ppermute | solution.py:415
  62.0 1.1 %collective-permute-start.19 = (bf16[32,2048]{1,0:T(8,128)(2,1)S(1)}, bf16[32,2048]{1,0:T(8,128)(2,1)S(1)}, u32[]{:S(2)}, u32[]{:S(2)}) collective-permute-start(bf16[32,2048]{1,0:T(8,128)(2,1)S(1)} %get-tuple-element.87), channel_id=1, source_target_pairs={{0,4},{1,5},{2,6},{3,7},{4,0},{5,1},{6,2},{7,3},{8,12},{9,13},{10,... | collective-permute-start | bytes 393224 | tf_op jit(solution)/shard_map/ppermute | solution.py:412
  64.0 2.9 %collective-permute-done.19.refs_3_ = bf16[32,2048]{1,0:T(8,128)(2,1)S(1)} collective-permute-done((bf16[32,2048]{1,0:T(8,128)(2,1)S(1)}, bf16[32,2048]{1,0:T(8,128)(2,1)S(1)}, u32[]{:S(2)}, u32[]{:S(2)}) %collective-permute-start.19) | collective-permute-done | bytes 131104 | tf_op jit(solution)/shard_map/ppermute | solution.py:412
  66.9 2.0 %collective-permute-done.20.refs_4_ = bf16[32,2048]{1,0:T(8,128)(2,1)S(1)} collective-permute-done((bf16[32,2048]{1,0:T(8,128)(2,1)S(1)}, bf16[32,2048]{1,0:T(8,128)(2,1)S(1)}, u32[]{:S(2)}, u32[]{:S(2)}) %collective-permute-start.20) | collective-permute-done | bytes 131104 | tf_op jit(solution)/shard_map/ppermute | solution.py:412
  69.8 1.0 %collective-permute-start.29 = (bf16[32,2176]{1,0:T(8,128)(2,1)S(1)}, bf16[32,2176]{1,0:T(8,128)(2,1)S(1)}, u32[]{:S(2)}, u32[]{:S(2)}) collective-permute-start(bf16[32,2176]{1,0:T(8,128)(2,1)S(1)} %finish.1.refs_0_), channel_id=1, source_target_pairs={{0,6},{1,7},{2,4},{3,5},{4,2},{5,3},{6,0},{7,1},{8,14},{9,15},{10,... | collective-permute-start | bytes 417800 | tf_op jit(solution)/shard_map/ppermute | solution.py:412
  70.8 1.5 %collective-permute-start.28 = (bf16[32,2176]{1,0:T(8,128)(2,1)S(1)}, bf16[32,2176]{1,0:T(8,128)(2,1)S(1)}, u32[]{:S(2)}, u32[]{:S(2)}) collective-permute-start(bf16[32,2176]{1,0:T(8,128)(2,1)S(1)} %finish.1.refs_0_), channel_id=1, source_target_pairs={{0,4},{1,5},{2,6},{3,7},{4,0},{5,1},{6,2},{7,3},{8,12},{9,13},{10,... | collective-permute-start | bytes 417800 | tf_op jit(solution)/shard_map/ppermute | solution.py:412
  72.4 1.0 %collective-permute-start.27 = (bf16[32,2176]{1,0:T(8,128)(2,1)S(1)}, bf16[32,2176]{1,0:T(8,128)(2,1)S(1)}, u32[]{:S(2)}, u32[]{:S(2)}) collective-permute-start(bf16[32,2176]{1,0:T(8,128)(2,1)S(1)} %finish.1.refs_0_), channel_id=1, source_target_pairs={{0,2},{1,3},{2,0},{3,1},{4,6},{5,7},{6,4},{7,5},{8,10},{9,11},{10,... | collective-permute-start | bytes 417800 | tf_op jit(solution)/shard_map/ppermute | solution.py:412
  73.4 3.5 %collective-permute-done.29.refs_3_ = bf16[32,2176]{1,0:T(8,128)(2,1)S(1)} collective-permute-done((bf16[32,2176]{1,0:T(8,128)(2,1)S(1)}, bf16[32,2176]{1,0:T(8,128)(2,1)S(1)}, u32[]{:S(2)}, u32[]{:S(2)}) %collective-permute-start.29) | collective-permute-done | bytes 139296 | tf_op jit(solution)/shard_map/ppermute | solution.py:412
  76.9 1.2 %collective-permute-done.28.refs_2_ = bf16[32,2176]{1,0:T(8,128)(2,1)S(1)} collective-permute-done((bf16[32,2176]{1,0:T(8,128)(2,1)S(1)}, bf16[32,2176]{1,0:T(8,128)(2,1)S(1)}, u32[]{:S(2)}, u32[]{:S(2)}) %collective-permute-start.28) | collective-permute-done | bytes 139296 | tf_op jit(solution)/shard_map/ppermute | solution.py:412
  79.7 5.3 %final.1 = (bf16[256,2048]{1,0:T(8,128)(2,1)}, bf16[1,2048,768]{2,1,0:T(8,128)(2,1)}, bf16[1,384,2048]{2,1,0:T(8,128)(2,1)}) custom-call(bf16[32,2176]{1,0:T(8,128)(2,1)S(1)} %finish.1.refs_0_, bf16[32,2176]{1,0:T(8,128)(2,1)S(1)} %collective-permute-done.27.refs_1_, bf16[32,2176]{1,0:T(8,128)(2,1)S(1)} %collective-permute-done.28.refs_2_, ...), custom_call_target="tpu_custom_call" | custom-call | flops 100663296 | bytes 7340032 | tf_op jit(solution)/shard_map/final/pallas_call | solution.py:602
  (60 shorter events, 12.1 us)
Async XLA Ops:
  0.6 9.6 %collective-permute-start.3 = (bf16[1,2048,768]{2,1,0:T(8,128)(2,1)}, bf16[1,2048,768]{2,1,0:T(8,128)(2,1)}, u32[]{:S(2)}, u32[]{:S(2)}) collective-permute-start(bf16[1,2048,768]{2,1,0:T(8,128)(2,1)} %refs_11_), channel_id=1, source_target_pairs={{0,1},{1,0},{2,3},{3,2},{4,5},{5,4},{6,7},{7,6},{8,9},{9,8},{10,11... | collective-permute-start | bytes 9437192 | tf_op jit(solution)/shard_map/ppermute | solution.py:412
  1.2 9.1 %collective-permute-start.4 = (bf16[1,384,2048]{2,1,0:T(8,128)(2,1)}, bf16[1,384,2048]{2,1,0:T(8,128)(2,1)S(1)}, u32[]{:S(2)}, u32[]{:S(2)}) collective-permute-start(bf16[1,384,2048]{2,1,0:T(8,128)(2,1)} %refs_14_.1), channel_id=1, source_target_pairs={{0,1},{1,0},{2,3},{3,2},{4,5},{5,4},{6,7},{7,6},{8,9},{9,8},{10,11... | collective-permute-start | bytes 4718600 | tf_op jit(solution)/shard_map/ppermute | solution.py:412
  2.9 7.3 %collective-permute-start = (bf16[32,2176]{1,0:T(8,128)(2,1)}, bf16[32,2176]{1,0:T(8,128)(2,1)S(1)}, u32[]{:S(2)}, u32[]{:S(2)}) collective-permute-start(bf16[32,2176]{1,0:T(8,128)(2,1)} %pack.1.refs_1_.refs_0_), channel_id=1, source_target_pairs={{0,8},{8,0},{16,24},{24,16},{1,9},{9,1},{17,25},{25,17},{2,10},{10... | collective-permute-start | bytes 417800 | tf_op jit(solution)/shard_map/ppermute | solution.py:415
  6.0 10.3 %collective-permute-start.2 = (bf16[32,2176]{1,0:T(8,128)(2,1)}, bf16[32,2176]{1,0:T(8,128)(2,1)S(1)}, u32[]{:S(2)}, u32[]{:S(2)}) collective-permute-start(bf16[32,2176]{1,0:T(8,128)(2,1)} %pack.1.refs_1_.refs_0_), channel_id=1, source_target_pairs={{0,24},{8,16},{16,8},{24,0},{1,25},{9,17},{17,9},{25,1},{2,26},{10... | collective-permute-start | bytes 417800 | tf_op jit(solution)/shard_map/ppermute | solution.py:415
  8.5 13.1 %collective-permute-start.1 = (bf16[32,2176]{1,0:T(8,128)(2,1)}, bf16[32,2176]{1,0:T(8,128)(2,1)}, u32[]{:S(2)}, u32[]{:S(2)}) collective-permute-start(bf16[32,2176]{1,0:T(8,128)(2,1)} %pack.1.refs_1_.refs_0_), channel_id=1, source_target_pairs={{0,16},{8,24},{16,0},{24,8},{1,17},{9,25},{17,1},{25,9},{2,18},{10... | collective-permute-start | bytes 417800 | tf_op jit(solution)/shard_map/ppermute | solution.py:415
  10.3 12.2 %collective-permute-start.7 = (bf16[32,2304]{1,0:T(8,128)(2,1)S(1)}, bf16[32,2304]{1,0:T(8,128)(2,1)S(1)}, u32[]{:S(2)}, u32[]{:S(2)}) collective-permute-start(bf16[32,2304]{1,0:T(8,128)(2,1)S(1)} %pad_maximum_fusion.1), channel_id=1, source_target_pairs={{0,6},{1,7},{2,4},{3,5},{4,2},{5,3},{6,0},{7,1},{8,14},{9,15},{10,... | collective-permute-start | bytes 442376 | tf_op jit(solution)/shard_map/ppermute | solution.py:412
  12.9 9.6 %collective-permute-start.6 = (bf16[32,2304]{1,0:T(8,128)(2,1)S(1)}, bf16[32,2304]{1,0:T(8,128)(2,1)S(1)}, u32[]{:S(2)}, u32[]{:S(2)}) collective-permute-start(bf16[32,2304]{1,0:T(8,128)(2,1)S(1)} %pad_maximum_fusion.1), channel_id=1, source_target_pairs={{0,4},{1,5},{2,6},{3,7},{4,0},{5,1},{6,2},{7,3},{8,12},{9,13},{10,... | collective-permute-start | bytes 442376 | tf_op jit(solution)/shard_map/ppermute | solution.py:412
  13.4 9.1 %collective-permute-start.5 = (bf16[32,2304]{1,0:T(8,128)(2,1)S(1)}, bf16[32,2304]{1,0:T(8,128)(2,1)S(1)}, u32[]{:S(2)}, u32[]{:S(2)}) collective-permute-start(bf16[32,2304]{1,0:T(8,128)(2,1)S(1)} %pad_maximum_fusion.1), channel_id=1, source_target_pairs={{0,2},{1,3},{2,0},{3,1},{4,6},{5,7},{6,4},{7,5},{8,10},{9,11},{10,... | collective-permute-start | bytes 442376 | tf_op jit(solution)/shard_map/ppermute | solution.py:412
  22.5 14.8 %collective-permute-start.10 = (bf16[64,2176]{1,0:T(8,128)(2,1)S(1)}, bf16[64,2176]{1,0:T(8,128)(2,1)S(1)}, u32[]{:S(2)}, u32[]{:S(2)}) collective-permute-start(bf16[64,2176]{1,0:T(8,128)(2,1)S(1)} %pad_maximum_fusion), channel_id=1, source_target_pairs={{0,6},{1,7},{2,4},{3,5},{4,2},{5,3},{6,0},{7,1},{8,14},{9,15},{10,... | collective-permute-start | bytes 835592 | tf_op jit(solution)/shard_map/ppermute | solution.py:412
  25.0 12.8 %collective-permute-start.9 = (bf16[64,2176]{1,0:T(8,128)(2,1)S(1)}, bf16[64,2176]{1,0:T(8,128)(2,1)S(1)}, u32[]{:S(2)}, u32[]{:S(2)}) collective-permute-start(bf16[64,2176]{1,0:T(8,128)(2,1)S(1)} %pad_maximum_fusion), channel_id=1, source_target_pairs={{0,4},{1,5},{2,6},{3,7},{4,0},{5,1},{6,2},{7,3},{8,12},{9,13},{10,... | collective-permute-start | bytes 835592 | tf_op jit(solution)/shard_map/ppermute | solution.py:412
  25.5 13.6 %collective-permute-start.8 = (bf16[64,2176]{1,0:T(8,128)(2,1)S(1)}, bf16[64,2176]{1,0:T(8,128)(2,1)S(1)}, u32[]{:S(2)}, u32[]{:S(2)}) collective-permute-start(bf16[64,2176]{1,0:T(8,128)(2,1)S(1)} %pad_maximum_fusion), channel_id=1, source_target_pairs={{0,2},{1,3},{2,0},{3,1},{4,6},{5,7},{6,4},{7,5},{8,10},{9,11},{10,... | collective-permute-start | bytes 835592 | tf_op jit(solution)/shard_map/ppermute | solution.py:412
  34.2 10.0 %collective-permute-start.11 = (bf16[32,2048]{1,0:T(8,128)(2,1)S(1)}, bf16[32,2048]{1,0:T(8,128)(2,1)S(1)}, u32[]{:S(2)}, u32[]{:S(2)}) collective-permute-start(bf16[32,2048]{1,0:T(8,128)(2,1)S(1)} %get-tuple-element.70), channel_id=1, source_target_pairs={{0,2},{1,3},{2,0},{3,1},{4,6},{5,7},{6,4},{7,5},{8,10},{9,11},{10,... | collective-permute-start | bytes 393224 | tf_op jit(solution)/shard_map/ppermute | solution.py:412
  35.8 8.4 %collective-permute-start.12 = (bf16[32,2048]{1,0:T(8,128)(2,1)S(1)}, bf16[32,2048]{1,0:T(8,128)(2,1)S(1)}, u32[]{:S(2)}, u32[]{:S(2)}) collective-permute-start(bf16[32,2048]{1,0:T(8,128)(2,1)S(1)} %get-tuple-element.71), channel_id=1, source_target_pairs={{0,4},{1,5},{2,6},{3,7},{4,0},{5,1},{6,2},{7,3},{8,12},{9,13},{10,... | collective-permute-start | bytes 393224 | tf_op jit(solution)/shard_map/ppermute | solution.py:412
  37.3 6.9 %collective-permute-start.13 = (bf16[32,2048]{1,0:T(8,128)(2,1)S(1)}, bf16[32,2048]{1,0:T(8,128)(2,1)S(1)}, u32[]{:S(2)}, u32[]{:S(2)}) collective-permute-start(bf16[32,2048]{1,0:T(8,128)(2,1)S(1)} %get-tuple-element.72), channel_id=1, source_target_pairs={{0,6},{1,7},{2,4},{3,5},{4,2},{5,3},{6,0},{7,1},{8,14},{9,15},{10,... | collective-permute-start | bytes 393224 | tf_op jit(solution)/shard_map/ppermute | solution.py:412
  44.2 6.9 %collective-permute-start.14 = (bf16[32,2176]{1,0:T(8,128)(2,1)S(1)}, bf16[32,2176]{1,0:T(8,128)(2,1)S(1)}, u32[]{:S(2)}, u32[]{:S(2)}) collective-permute-start(bf16[32,2176]{1,0:T(8,128)(2,1)S(1)} %get-tuple-element.73), channel_id=1, source_target_pairs={{0,2},{1,3},{2,0},{3,1},{4,6},{5,7},{6,4},{7,5},{8,10},{9,11},{10,... | collective-permute-start | bytes 417800 | tf_op jit(solution)/shard_map/ppermute | solution.py:412
  45.8 7.1 %collective-permute-start.15 = (bf16[32,2176]{1,0:T(8,128)(2,1)S(1)}, bf16[32,2176]{1,0:T(8,128)(2,1)S(1)}, u32[]{:S(2)}, u32[]{:S(2)}) collective-permute-start(bf16[32,2176]{1,0:T(8,128)(2,1)S(1)} %get-tuple-element.74), channel_id=1, source_target_pairs={{0,4},{1,5},{2,6},{3,7},{4,0},{5,1},{6,2},{7,3},{8,12},{9,13},{10,... | collective-permute-start | bytes 417800 | tf_op jit(solution)/shard_map/ppermute | solution.py:412
  46.0 6.8 %collective-permute-start.16 = (bf16[32,2176]{1,0:T(8,128)(2,1)S(1)}, bf16[32,2176]{1,0:T(8,128)(2,1)S(1)}, u32[]{:S(2)}, u32[]{:S(2)}) collective-permute-start(bf16[32,2176]{1,0:T(8,128)(2,1)S(1)} %get-tuple-element.75), channel_id=1, source_target_pairs={{0,6},{1,7},{2,4},{3,5},{4,2},{5,3},{6,0},{7,1},{8,14},{9,15},{10,... | collective-permute-start | bytes 417800 | tf_op jit(solution)/shard_map/ppermute | solution.py:412
  49.2 1.6 %collective-permute-start.17 = (bf16[144,128]{1,0:T(8,128)(2,1)S(1)}, bf16[144,128]{1,0:T(8,128)(2,1)S(1)}, u32[]{:S(2)}, u32[]{:S(2)}) collective-permute-start(bf16[144,128]{1,0:T(8,128)(2,1)S(1)} %get-tuple-element.76), channel_id=1, source_target_pairs={{0,1},{1,0},{2,3},{3,2},{4,5},{5,4},{6,7},{7,6},{8,9},{9,8},{10,11... | collective-permute-start | bytes 110600 | tf_op jit(solution)/shard_map/ppermute | solution.py:412
  49.3 10.0 %collective-permute-start.22 = (bf16[32,2048]{1,0:T(8,128)(2,1)S(1)}, bf16[32,2048]{1,0:T(8,128)(2,1)S(1)}, u32[]{:S(2)}, u32[]{:S(2)}) collective-permute-start(bf16[32,2048]{1,0:T(8,128)(2,1)S(1)} %get-tuple-element.91), channel_id=1, source_target_pairs={{0,2},{1,3},{2,0},{3,1},{4,6},{5,7},{6,4},{7,5},{8,10},{9,11},{10,... | collective-permute-start | bytes 393224 | tf_op jit(solution)/shard_map/ppermute | solution.py:412
  50.8 8.6 %collective-permute-start.23 = (bf16[32,2048]{1,0:T(8,128)(2,1)S(1)}, bf16[32,2048]{1,0:T(8,128)(2,1)S(1)}, u32[]{:S(2)}, u32[]{:S(2)}) collective-permute-start(bf16[32,2048]{1,0:T(8,128)(2,1)S(1)} %get-tuple-element.92), channel_id=1, source_target_pairs={{0,4},{1,5},{2,6},{3,7},{4,0},{5,1},{6,2},{7,3},{8,12},{9,13},{10,... | collective-permute-start | bytes 393224 | tf_op jit(solution)/shard_map/ppermute | solution.py:412
  52.8 6.6 %collective-permute-start.24 = (bf16[32,2048]{1,0:T(8,128)(2,1)S(1)}, bf16[32,2048]{1,0:T(8,128)(2,1)S(1)}, u32[]{:S(2)}, u32[]{:S(2)}) collective-permute-start(bf16[32,2048]{1,0:T(8,128)(2,1)S(1)} %get-tuple-element.93), channel_id=1, source_target_pairs={{0,6},{1,7},{2,4},{3,5},{4,2},{5,3},{6,0},{7,1},{8,14},{9,15},{10,... | collective-permute-start | bytes 393224 | tf_op jit(solution)/shard_map/ppermute | solution.py:412
  54.5 8.6 %collective-permute-start.18 = (bf16[32,2048]{1,0:T(8,128)(2,1)S(1)}, bf16[32,2048]{1,0:T(8,128)(2,1)S(1)}, u32[]{:S(2)}, u32[]{:S(2)}) collective-permute-start(bf16[32,2048]{1,0:T(8,128)(2,1)S(1)} %get-tuple-element.86), channel_id=1, source_target_pairs={{0,2},{1,3},{2,0},{3,1},{4,6},{5,7},{6,4},{7,5},{8,10},{9,11},{10,... | collective-permute-start | bytes 393224 | tf_op jit(solution)/shard_map/ppermute | solution.py:412
  56.0 13.7 %collective-permute-start.21 = (bf16[32,2176]{1,0:T(8,128)(2,1)S(1)}, bf16[32,2176]{1,0:T(8,128)(2,1)S(1)}, u32[]{:S(2)}, u32[]{:S(2)}) collective-permute-start(bf16[32,2176]{1,0:T(8,128)(2,1)S(1)} %get-tuple-element.85), channel_id=1, source_target_pairs={{0,24},{8,16},{16,8},{24,0},{1,25},{9,17},{17,9},{25,1},{2,26},{10... | collective-permute-start | bytes 417800 | tf_op jit(solution)/shard_map/ppermute | solution.py:415
  59.3 10.4 %collective-permute-start.26 = (bf16[32,2176]{1,0:T(8,128)(2,1)S(1)}, bf16[32,2176]{1,0:T(8,128)(2,1)S(1)}, u32[]{:S(2)}, u32[]{:S(2)}) collective-permute-start(bf16[32,2176]{1,0:T(8,128)(2,1)S(1)} %combine.7), channel_id=1, source_target_pairs={{0,8},{8,0},{16,24},{24,16},{1,9},{9,1},{17,25},{25,17},{2,10},{10... | collective-permute-start | bytes 417800 | tf_op jit(solution)/shard_map/ppermute | solution.py:415
  60.2 9.6 %collective-permute-start.25 = (bf16[32,2176]{1,0:T(8,128)(2,1)S(1)}, bf16[32,2176]{1,0:T(8,128)(2,1)S(1)}, u32[]{:S(2)}, u32[]{:S(2)}) collective-permute-start(bf16[32,2176]{1,0:T(8,128)(2,1)S(1)} %combine.6), channel_id=1, source_target_pairs={{0,16},{8,24},{16,0},{24,8},{1,17},{9,25},{17,1},{25,9},{2,18},{10... | collective-permute-start | bytes 417800 | tf_op jit(solution)/shard_map/ppermute | solution.py:415
  62.0 5.0 %collective-permute-start.19 = (bf16[32,2048]{1,0:T(8,128)(2,1)S(1)}, bf16[32,2048]{1,0:T(8,128)(2,1)S(1)}, u32[]{:S(2)}, u32[]{:S(2)}) collective-permute-start(bf16[32,2048]{1,0:T(8,128)(2,1)S(1)} %get-tuple-element.87), channel_id=1, source_target_pairs={{0,4},{1,5},{2,6},{3,7},{4,0},{5,1},{6,2},{7,3},{8,12},{9,13},{10,... | collective-permute-start | bytes 393224 | tf_op jit(solution)/shard_map/ppermute | solution.py:412
  63.1 5.9 %collective-permute-start.20 = (bf16[32,2048]{1,0:T(8,128)(2,1)S(1)}, bf16[32,2048]{1,0:T(8,128)(2,1)S(1)}, u32[]{:S(2)}, u32[]{:S(2)}) collective-permute-start(bf16[32,2048]{1,0:T(8,128)(2,1)S(1)} %get-tuple-element.88), channel_id=1, source_target_pairs={{0,6},{1,7},{2,4},{3,5},{4,2},{5,3},{6,0},{7,1},{8,14},{9,15},{10,... | collective-permute-start | bytes 393224 | tf_op jit(solution)/shard_map/ppermute | solution.py:412
  69.8 7.1 %collective-permute-start.29 = (bf16[32,2176]{1,0:T(8,128)(2,1)S(1)}, bf16[32,2176]{1,0:T(8,128)(2,1)S(1)}, u32[]{:S(2)}, u32[]{:S(2)}) collective-permute-start(bf16[32,2176]{1,0:T(8,128)(2,1)S(1)} %finish.1.refs_0_), channel_id=1, source_target_pairs={{0,6},{1,7},{2,4},{3,5},{4,2},{5,3},{6,0},{7,1},{8,14},{9,15},{10,... | collective-permute-start | bytes 417800 | tf_op jit(solution)/shard_map/ppermute | solution.py:412
  70.8 7.3 %collective-permute-start.28 = (bf16[32,2176]{1,0:T(8,128)(2,1)S(1)}, bf16[32,2176]{1,0:T(8,128)(2,1)S(1)}, u32[]{:S(2)}, u32[]{:S(2)}) collective-permute-start(bf16[32,2176]{1,0:T(8,128)(2,1)S(1)} %finish.1.refs_0_), channel_id=1, source_target_pairs={{0,4},{1,5},{2,6},{3,7},{4,0},{5,1},{6,2},{7,3},{8,12},{9,13},{10,... | collective-permute-start | bytes 417800 | tf_op jit(solution)/shard_map/ppermute | solution.py:412
  72.4 5.7 %collective-permute-start.27 = (bf16[32,2176]{1,0:T(8,128)(2,1)S(1)}, bf16[32,2176]{1,0:T(8,128)(2,1)S(1)}, u32[]{:S(2)}, u32[]{:S(2)}) collective-permute-start(bf16[32,2176]{1,0:T(8,128)(2,1)S(1)} %finish.1.refs_0_), channel_id=1, source_target_pairs={{0,2},{1,3},{2,0},{3,1},{4,6},{5,7},{6,4},{7,5},{8,10},{9,11},{10,... | collective-permute-start | bytes 417800 | tf_op jit(solution)/shard_map/ppermute | solution.py:412
  73.4 5.2 %collective-permute-start.30 = (bf16[32,2176]{1,0:T(8,128)(2,1)S(1)}, bf16[32,2176]{1,0:T(8,128)(2,1)S(1)}, u32[]{:S(2)}, u32[]{:S(2)}) collective-permute-start(bf16[32,2176]{1,0:T(8,128)(2,1)S(1)} %finish.1.refs_0_), channel_id=1, source_target_pairs={{0,1},{1,0},{2,3},{3,2},{4,5},{5,4},{6,7},{7,6},{8,9},{9,8},{10,11... | collective-permute-start | bytes 417800 | tf_op jit(solution)/shard_map/ppermute | solution.py:412
  76.9 1.7 %collective-permute-start.33 = (bf16[32,2176]{1,0:T(8,128)(2,1)S(1)}, bf16[32,2176]{1,0:T(8,128)(2,1)S(1)}, u32[]{:S(2)}, u32[]{:S(2)}) collective-permute-start(bf16[32,2176]{1,0:T(8,128)(2,1)S(1)} %collective-permute-done.29.refs_3_), channel_id=1, source_target_pairs={{0,1},{1,0},{2,3},{3,2},{4,5},{5,4},{6,7},{7,6},{8,9},{9,8},{10,11... | collective-permute-start | bytes 417800 | tf_op jit(solution)/shard_map/ppermute | solution.py:412
  (7 other events, 51.3 us)

commit v14 on v13

--- a/solution.py
+++ b/solution.py
@@ -17,7 +17,6 @@
 
 in_hbm = pl.BlockSpec(memory_space=pltpu.HBM)
 in_vmem = pl.BlockSpec(memory_space=pltpu.VMEM)
-in_smem = pl.BlockSpec(memory_space=pltpu.SMEM)
 
 
 def params(mebibytes):
@@ -38,6 +37,11 @@
     steps = [1 << bit for bit in range((count - 1).bit_length())]
     assert 1 << len(steps) == count
     return steps
+
+
+def position():
+    plane, lane = lax.axis_index("dp"), lax.axis_index("expert")
+    return plane, lane, plane * (lax.axis_size("expert") // 2) + lane // 2
 
 
 def column(table, wanted):
@@ -95,8 +99,9 @@
     own.wait()
 
 
-def table_kernel(layout, place, *refs):
+def table_kernel(layout, *refs):
     seq_dev, tok_dev, where_tiles, n_parts = layout
+    place = position()
     parts = refs[:n_parts]
     kept, sent, partners, routes, marks = refs[n_parts:]
     part_rows = parts[0].shape[0]
@@ -207,7 +212,7 @@
 def expert_kernel(layout, *refs):
     group, chips, part_rows, seq_dev, where_tiles, used, with_last = layout
     refs = list(refs)
-    place = refs.pop(0)
+    place = position()
     near = 0 in group
     tokens = refs.pop(0) if near else None
     parts, refs = dict(zip(used, refs)), refs[len(used) :]
@@ -263,8 +268,9 @@
         own_last[...] = share_of(flat, place[1], each, part_rows, chunks)
 
 
-def combine_kernel(layout, place, kept, found, *refs):
+def combine_kernel(layout, kept, found, *refs):
     hop, chips, with_last, width, each = layout
+    place = position()
     own, refs = (refs[0], refs[1:]) if hop == 0 else (None, refs)
     last_in, refs = (refs[0], refs[1:]) if hop and not with_last else (None, refs)
     parts, out = refs[:chips], refs[chips]
@@ -343,7 +349,8 @@
 
 def final_kernel(n_pieces, n_blocks, *refs):
     pieces, refs = refs[:n_pieces], refs[n_pieces:]
-    last_all, projected, place, kept, found, partners, down, *refs = refs
+    last_all, projected, kept, found, partners, down, *refs = refs
+    place = position()
     layer_out, grad_in, grad_out, made_in, made_out, flat, sems = refs
     part_rows, width = pieces[0].shape[0], layer_out.shape[1]
     copies = []
@@ -377,7 +384,7 @@
     route_grad = (column(table, place[2]) * grad_last).astype(bf16)
     gate, up, sigmoid_gate, activated = hidden_parts(projected[...])
     hidden = (activated * up).astype(bf16)
-    grad_hidden = dot(down[0], route_grad, ((1,), (1,))).T
+    grad_hidden = dot(route_grad, down[0], ((1,), (1,)))
     gate_slope = sigmoid_gate * (1.0 + gate * (1.0 - sigmoid_gate))
     slope = jnp.concatenate([grad_hidden * up * gate_slope, grad_hidden * activated], axis=1)
     slope = slope.astype(bf16)
@@ -403,9 +410,6 @@
     seqs = dp_count * seq_dev
     seq_length = tok_dev // seq_dev
     part_rows = tok_dev // expert_count
-    plane = lax.axis_index("dp")
-    lane = lax.axis_index("expert")
-    place = jnp.stack([plane, lane, plane * chips + lane // 2]).astype(jnp.int32)
     assert experts <= lanes and seq_length % tail == 0
 
     def to_lane(value, step):
@@ -470,7 +474,7 @@
     extra = each * width // part_rows
     assert extra % lanes == 0 and part_rows % (width // lanes) == 0
 
-    def expert(group, place, with_last):
+    def expert(group, after, with_last):
         near = 0 in group
         wanted = range(dp_count) if with_last else [hop for hop in group if hop]
         used = sorted({spot[0] for hop in wanted for spot in where_tiles[hop]})
@@ -491,12 +495,14 @@
                 pltpu.VMEM((seqs * (width // lanes), lanes), f32),
                 pltpu.VMEM((dp_count, width // lanes, -(-seq_dev // 8) * 8, lanes), f32),
             ] + scratch
-        operands = [place] + [tokens] * near + parts + list(weights)
+        if after is not None:
+            parts[0], _ = lax.optimization_barrier((parts[0], after))
+        operands = [tokens] * near + parts + list(weights)
         layout = (tuple(group), chips, part_rows, seq_dev, where_tiles, used, with_last)
         return pl.pallas_call(
             functools.partial(expert_kernel, layout),
             out_shape=out_shape,
-            in_specs=[in_smem] + [in_vmem] * (len(operands) - 1),
+            in_specs=[in_vmem] * len(operands),
             out_specs=[in_vmem] * len(out_shape),
             scratch_shapes=scratch,
             compiler_params=params(32),
@@ -505,21 +511,22 @@
         )(*operands)
 
     outs = {}
-    after = place
+    after = None
     rest = list(range(dp_count - 2, 1, -1))
     for group in groups:
         with_last = dp_count - 1 in group
         out = expert(group, after, with_last)
-        after, _ = lax.optimization_barrier((place, out[0]))
+        after = out[0]
         for index, hop in enumerate(group):
             outs[hop] = list(out[index * chips : (index + 1) * chips])
         if with_last:
             last_all, last_projected, own_last = out[-3:]
-            tables_place = after
+            first_tile, _ = lax.optimization_barrier((tiles[0], out[0]))
 
     table_rows = dp_count * part_rows + seqs
     chunks = width // lanes
     sublanes = -(-seq_dev // 8) * 8
+    tiles[0] = first_tile
     kept, sent, partners = pl.pallas_call(
         functools.partial(table_kernel, (seq_dev, tok_dev, where_tiles, len(tiles))),
         out_shape=[
@@ -527,7 +534,7 @@
             jax.ShapeDtypeStruct((table_rows, lanes), bf16),
             jax.ShapeDtypeStruct((seqs, lanes), f32),
         ],
-        in_specs=[in_smem] + [in_vmem] * len(tiles),
+        in_specs=[in_vmem] * len(tiles),
         out_specs=[in_vmem] * 3,
         scratch_shapes=[
             pltpu.VMEM((dp_count, sublanes, lanes), f32),
@@ -536,7 +543,7 @@
         compiler_params=params(48 if dp_count > 8 else 12),
         cost_estimate=cost(0, 1 << 20),
         name="tables",
-    )(tables_place, *tiles)
+    )(*tiles)
     found = to_lane(sent, 1)
 
     def combine(hop, parts, last_sum):
@@ -546,12 +553,12 @@
             out_shape = [jax.ShapeDtypeStruct((part_rows, width + extra), bf16)]
         if with_last:
             out_shape.append(jax.ShapeDtypeStruct((part_rows, extra), bf16))
-        operands = [place, kept, found] + [packed] * (hop == 0)
+        operands = [kept, found] + [packed] * (hop == 0)
         operands += [last_sum] * (hop > 0 and not with_last) + parts
         return pl.pallas_call(
             functools.partial(combine_kernel, (hop, chips, with_last, width, each)),
             out_shape=out_shape,
-            in_specs=[in_smem] + [in_vmem] * (len(operands) - 1),
+            in_specs=[in_vmem] * len(operands),
             out_specs=[in_vmem] * len(out_shape),
             compiler_params=params(8),
             cost_estimate=cost(0, 2 << 20),
@@ -606,7 +613,7 @@
             jax.ShapeDtypeStruct(gate_up.shape, bf16),
             jax.ShapeDtypeStruct(down.shape, bf16),
         ],
-        in_specs=[in_vmem] * (len(pieces) + 2) + [in_smem] + [in_vmem] * 4,
+        in_specs=[in_vmem] * (len(pieces) + 6),
         out_specs=[in_hbm] * 3,
         scratch_shapes=[
             pltpu.VMEM((width, 2 * half_width), bf16),
@@ -617,7 +624,7 @@
         compiler_params=params(24),
         cost_estimate=cost(2 * seqs * width * 4 * half_width, 7 << 20),
         name="final",
-    )(*pieces, last_all, last_projected, place, kept, found, partners, down)
+    )(*pieces, last_all, last_projected, kept, found, partners, down)
     return (layer_out, grad_gate_up, grad_down)
 
 

time: 85.3 us -> 81.9 us (0.960)
  Pallas kernels: 21.5 us -> 16.3 us
  waiting for transfers between devices: 22.4 us -> 24.3 us
  local copies, waits for them, and re-layouts: 3.86 us -> 5.26 us
  other arithmetic: 1.01 us -> 0.03 us
    pallas_call x4, Pallas kernels: 2.89 us -> 0.78 us  [combine(): pl.pallas_call(functools.partial(combine_kernel, (hop, chips, with_last,...]
    ppermute x28, waiting for transfers between devices: 13.8 us -> 15.7 us  [to_lane(): lax.ppermute(value, 'expert', [(j, j ^ step) for j in range(expert_count)])]
    unnamed x10 -> x12, local copies, waits for them, and re-layouts: 3.13 us -> 4.53 us
    pallas_call x1, Pallas kernels: 5.3 us -> 4.12 us  [body(): pl.pallas_call(functools.partial(final_kernel, len(pieces), n_blocks), ou...]
    ppermute x6, starting transfers between devices: 10.2 us -> 9.03 us  [to_plane(): return lax.ppermute(value, 'dp', [(p, p ^ step) for p in range(dp_count)])]
    pallas_call x2, Pallas kernels: 10.1 us -> 9.17 us  [expert(): pl.pallas_call(functools.partial(expert_kernel, layout), out_shape=out_sh...]
    pallas_call x1, Pallas kernels: 1.42 us -> 0.5 us  [body(): pl.pallas_call(functools.partial(table_kernel, (seq_dev, tok_dev, where_t...]
    concatenate x1, other arithmetic: 0.93 us -> 0.02 us  [body(): joined = jnp.concatenate(own, axis=0)]
  transfers between devices with their start and end apart: 34 -> 34, of which waited for: 11 -> 15; matrix products, arithmetic and copies ran while one was open for 2% -> 1% of each run, Pallas kernels for 19% -> 15%
where the time goes in v14:
time: 81.9 us; the launch traced here: 81.6 us
  starting transfers between devices  34.9 us (43%)
  waiting for transfers between devices  24.3 us (30%)
  Pallas kernels  16.3 us (20%)
  local copies, waits for them, and re-layouts  5.26 us (6%)
  between operations  0.83 us (1%)
    ppermute x28, starting transfers between devices, to_lane(): lax.ppermute(value, 'expert', [(j, j ^ step) for j in range(expert_count)])  25.8 us
    ppermute x28, waiting for transfers between devices, to_lane(): lax.ppermute(value, 'expert', [(j, j ^ step) for j in range(expert_count)])  15.7 us
    pallas_call x2, Pallas kernels, expert(): pl.pallas_call(functools.partial(expert_kernel, layout), out_shape=out_sh...  9.17 us
    ppermute x6, starting transfers between devices, to_plane(): return lax.ppermute(value, 'dp', [(p, p ^ step) for p in range(dp_count)])  9.03 us
    ppermute x6, waiting for transfers between devices, to_plane(): return lax.ppermute(value, 'dp', [(p, p ^ step) for p in range(dp_count)])  8.64 us
    unnamed x12, local copies, waits for them, and re-layouts  4.53 us
    pallas_call x1, Pallas kernels, body(): pl.pallas_call(functools.partial(final_kernel, len(pieces), n_blocks), ou...  4.12 us
    pallas_call x1, Pallas kernels, body(): pl.pallas_call(functools.partial(pack_kernel, seq_dev), out_shape=jax.Sha...  1.66 us
  transfers between devices with their start and end apart: 34, of which 15 were waited for; matrix products, arithmetic and copies ran while one was open for 1% of the time, Pallas kernels for 15%

profile of v14, /device:TPU:0, one launch (start us, length us, event | category | flops | bytes accessed | tf_op | source)
XLA Modules:
  0.0 81.6 jit_solution(10584588640930089939)
XLA Ops:
  1.2 1.7 %pack.1.refs_0_ = bf16[32,2176]{1,0:T(8,128)(2,1)} custom-call(s32[4]{0:T(128)} %partners.1, s32[1,256]{1,0:T(1,128)} %bitcast.2, f32[1,256]{1,0:T(1,128)} %bitcast.3, bf16[256,2048]{1,0:T(8,128)(2,1)} %refs_0_.1), custom_call_target="tpu_custom_call" | custom-call | bytes 524288 | tf_op jit(solution)/shard_map/pack/pallas_call | solution.py:425
  2.9 3.1 %collective-permute-start = (bf16[32,2176]{1,0:T(8,128)(2,1)}, bf16[32,2176]{1,0:T(8,128)(2,1)S(1)}, u32[]{:S(2)}, u32[]{:S(2)}) collective-permute-start(bf16[32,2176]{1,0:T(8,128)(2,1)} %pack.1.refs_0_), channel_id=1, source_target_pairs={{0,8},{8,0},{16,24},{24,16},{1,9},{9,1},{17,25},{25,17},{2,10},{10... | collective-permute-start | bytes 417800 | tf_op jit(solution)/shard_map/ppermute | solution.py:419
  6.0 2.5 %collective-permute-start.2 = (bf16[32,2176]{1,0:T(8,128)(2,1)}, bf16[32,2176]{1,0:T(8,128)(2,1)S(1)}, u32[]{:S(2)}, u32[]{:S(2)}) collective-permute-start(bf16[32,2176]{1,0:T(8,128)(2,1)} %pack.1.refs_0_), channel_id=1, source_target_pairs={{0,24},{8,16},{16,8},{24,0},{1,25},{9,17},{17,9},{25,1},{2,26},{10... | collective-permute-start | bytes 417800 | tf_op jit(solution)/shard_map/ppermute | solution.py:419
  9.3 0.9 %collective-permute-done.refs_1_ = bf16[32,2176]{1,0:T(8,128)(2,1)S(1)} collective-permute-done((bf16[32,2176]{1,0:T(8,128)(2,1)}, bf16[32,2176]{1,0:T(8,128)(2,1)S(1)}, u32[]{:S(2)}, u32[]{:S(2)}) %collective-permute-start) | collective-permute-done | bytes 139296 | tf_op jit(solution)/shard_map/ppermute | solution.py:419
  10.2 2.6 %collective-permute-start.7 = (bf16[32,2304]{1,0:T(8,128)(2,1)S(1)}, bf16[32,2304]{1,0:T(8,128)(2,1)S(1)}, u32[]{:S(2)}, u32[]{:S(2)}) collective-permute-start(bf16[32,2304]{1,0:T(8,128)(2,1)S(1)} %pad_maximum_fusion.1), channel_id=1, source_target_pairs={{0,6},{1,7},{2,4},{3,5},{4,2},{5,3},{6,0},{7,1},{8,14},{9,15},{10,... | collective-permute-start | bytes 442376 | tf_op jit(solution)/shard_map/ppermute | solution.py:416
  13.8 2.4 %collective-permute-done.2.refs_6_ = bf16[32,2176]{1,0:T(8,128)(2,1)S(1)} collective-permute-done((bf16[32,2176]{1,0:T(8,128)(2,1)}, bf16[32,2176]{1,0:T(8,128)(2,1)S(1)}, u32[]{:S(2)}, u32[]{:S(2)}) %collective-permute-start.2) | collective-permute-done | bytes 139296 | tf_op jit(solution)/shard_map/ppermute | solution.py:419
  16.2 5.1 %collective-permute-done.1.refs_5_ = bf16[32,2176]{1,0:T(8,128)(2,1)S(1)} collective-permute-done((bf16[32,2176]{1,0:T(8,128)(2,1)}, bf16[32,2176]{1,0:T(8,128)(2,1)S(1)}, u32[]{:S(2)}, u32[]{:S(2)}) %collective-permute-start.1) | collective-permute-done | bytes 139296 | tf_op jit(solution)/shard_map/ppermute | solution.py:419
  21.4 2.5 %collective-permute-start.10 = (bf16[64,2176]{1,0:T(8,128)(2,1)S(1)}, bf16[64,2176]{1,0:T(8,128)(2,1)S(1)}, u32[]{:S(2)}, u32[]{:S(2)}) collective-permute-start(bf16[64,2176]{1,0:T(8,128)(2,1)S(1)} %pad_maximum_fusion), channel_id=1, source_target_pairs={{0,6},{1,7},{2,4},{3,5},{4,2},{5,3},{6,0},{7,1},{8,14},{9,15},{10,... | collective-permute-start | bytes 835592 | tf_op jit(solution)/shard_map/ppermute | solution.py:416
  25.0 1.4 %copy-done = bf16[1,384,2048]{2,1,0:T(8,128)(2,1)S(1)} copy-done((bf16[1,384,2048]{2,1,0:T(8,128)(2,1)S(1)}, bf16[1,384,2048]{2,1,0:T(8,128)(2,1)}, u32[]{:S(2)}) %copy-start) | copy-done | bytes 1572888
  26.4 1.9 %copy-done.2 = bf16[1,2048,768]{2,1,0:T(8,128)(2,1)S(1)} copy-done((bf16[1,2048,768]{2,1,0:T(8,128)(2,1)S(1)}, bf16[1,2048,768]{2,1,0:T(8,128)(2,1)}, u32[]{:S(2)}) %copy-start.2) | copy-done | bytes 3145752
  28.3 1.2 %copy-done.4 = bf16[256,2048]{1,0:T(8,128)(2,1)S(1)} copy-done((bf16[256,2048]{1,0:T(8,128)(2,1)S(1)}, bf16[256,2048]{1,0:T(8,128)(2,1)}, u32[]{:S(2)}) %copy-start.4) | copy-done | bytes 1048600
  29.5 4.5 %experts.2 = (bf16[32,2048]{1,0:T(8,128)(2,1)S(1)}, bf16[32,2048]{1,0:T(8,128)(2,1)S(1)}, bf16[32,2048]{1,0:T(8,128)(2,1)S(1)}, bf16[32,2048]{1,0:T(8,128)(2,1)S...) custom-call(bf16[256,2048]{1,0:T(8,128)(2,1)S(1)} %copy-done.4, ...), custom_call_target="tpu_custom_call" | custom-call | flops 2415919104 | bytes 12582912 | tf_op jit(solution)/shard_map/experts/pallas_call | solution.py:502
  34.0 1.6 %collective-permute-start.11 = (bf16[32,2048]{1,0:T(8,128)(2,1)S(1)}, bf16[32,2048]{1,0:T(8,128)(2,1)S(1)}, u32[]{:S(2)}, u32[]{:S(2)}) collective-permute-start(bf16[32,2048]{1,0:T(8,128)(2,1)S(1)} %get-tuple-element.70), channel_id=1, source_target_pairs={{0,2},{1,3},{2,0},{3,1},{4,6},{5,7},{6,4},{7,5},{8,10},{9,11},{10,... | collective-permute-start | bytes 393224 | tf_op jit(solution)/shard_map/ppermute | solution.py:416
  35.6 1.5 %collective-permute-start.12 = (bf16[32,2048]{1,0:T(8,128)(2,1)S(1)}, bf16[32,2048]{1,0:T(8,128)(2,1)S(1)}, u32[]{:S(2)}, u32[]{:S(2)}) collective-permute-start(bf16[32,2048]{1,0:T(8,128)(2,1)S(1)} %get-tuple-element.71), channel_id=1, source_target_pairs={{0,4},{1,5},{2,6},{3,7},{4,0},{5,1},{6,2},{7,3},{8,12},{9,13},{10,... | collective-permute-start | bytes 393224 | tf_op jit(solution)/shard_map/ppermute | solution.py:416
  37.6 4.7 %experts.3 = (bf16[32,2048]{1,0:T(8,128)(2,1)S(1)}, bf16[32,2048]{1,0:T(8,128)(2,1)S(1)}, bf16[32,2048]{1,0:T(8,128)(2,1)S(1)}, bf16[32,2048]{1,0:T(8,128)(2,1)S...) custom-call(bf16[32,2176]{1,0:T(8,128)(2,1)S(1)} %copy-done.5, ...), custom_call_target="tpu_custom_call" | custom-call | flops 2566914048 | bytes 12582912 | tf_op jit(solution)/shard_map/experts/pallas_call | solution.py:502
  43.9 1.5 %collective-permute-start.15 = (bf16[32,2176]{1,0:T(8,128)(2,1)S(1)}, bf16[32,2176]{1,0:T(8,128)(2,1)S(1)}, u32[]{:S(2)}, u32[]{:S(2)}) collective-permute-start(bf16[32,2176]{1,0:T(8,128)(2,1)S(1)} %get-tuple-element.74), channel_id=1, source_target_pairs={{0,4},{1,5},{2,6},{3,7},{4,0},{5,1},{6,2},{7,3},{8,12},{9,13},{10,... | collective-permute-start | bytes 417800 | tf_op jit(solution)/shard_map/ppermute | solution.py:416
  45.4 1.1 %collective-permute-start.16 = (bf16[32,2176]{1,0:T(8,128)(2,1)S(1)}, bf16[32,2176]{1,0:T(8,128)(2,1)S(1)}, u32[]{:S(2)}, u32[]{:S(2)}) collective-permute-start(bf16[32,2176]{1,0:T(8,128)(2,1)S(1)} %get-tuple-element.75), channel_id=1, source_target_pairs={{0,6},{1,7},{2,4},{3,5},{4,2},{5,3},{6,0},{7,1},{8,14},{9,15},{10,... | collective-permute-start | bytes 417800 | tf_op jit(solution)/shard_map/ppermute | solution.py:416
  47.1 1.0 %collective-permute-start.22 = (bf16[32,2048]{1,0:T(8,128)(2,1)S(1)}, bf16[32,2048]{1,0:T(8,128)(2,1)S(1)}, u32[]{:S(2)}, u32[]{:S(2)}) collective-permute-start(bf16[32,2048]{1,0:T(8,128)(2,1)S(1)} %get-tuple-element.91), channel_id=1, source_target_pairs={{0,2},{1,3},{2,0},{3,1},{4,6},{5,7},{6,4},{7,5},{8,10},{9,11},{10,... | collective-permute-start | bytes 393224 | tf_op jit(solution)/shard_map/ppermute | solution.py:416
  48.3 1.3 %collective-permute-start.23 = (bf16[32,2048]{1,0:T(8,128)(2,1)S(1)}, bf16[32,2048]{1,0:T(8,128)(2,1)S(1)}, u32[]{:S(2)}, u32[]{:S(2)}) collective-permute-start(bf16[32,2048]{1,0:T(8,128)(2,1)S(1)} %get-tuple-element.92), channel_id=1, source_target_pairs={{0,4},{1,5},{2,6},{3,7},{4,0},{5,1},{6,2},{7,3},{8,12},{9,13},{10,... | collective-permute-start | bytes 393224 | tf_op jit(solution)/shard_map/ppermute | solution.py:416
  50.0 2.1 %collective-permute-done.16.refs_3_ = bf16[32,2176]{1,0:T(8,128)(2,1)S(1)} collective-permute-done((bf16[32,2176]{1,0:T(8,128)(2,1)S(1)}, bf16[32,2176]{1,0:T(8,128)(2,1)S(1)}, u32[]{:S(2)}, u32[]{:S(2)}) %collective-permute-start.16) | collective-permute-done | bytes 139296 | tf_op jit(solution)/shard_map/ppermute | solution.py:416
  53.1 1.1 %collective-permute-start.18 = (bf16[32,2048]{1,0:T(8,128)(2,1)S(1)}, bf16[32,2048]{1,0:T(8,128)(2,1)S(1)}, u32[]{:S(2)}, u32[]{:S(2)}) collective-permute-start(bf16[32,2048]{1,0:T(8,128)(2,1)S(1)} %get-tuple-element.86), channel_id=1, source_target_pairs={{0,2},{1,3},{2,0},{3,1},{4,6},{5,7},{6,4},{7,5},{8,10},{9,11},{10,... | collective-permute-start | bytes 393224 | tf_op jit(solution)/shard_map/ppermute | solution.py:416
  54.2 2.4 %collective-permute-start.21 = (bf16[32,2176]{1,0:T(8,128)(2,1)S(1)}, bf16[32,2176]{1,0:T(8,128)(2,1)S(1)}, u32[]{:S(2)}, u32[]{:S(2)}) collective-permute-start(bf16[32,2176]{1,0:T(8,128)(2,1)S(1)} %get-tuple-element.85), channel_id=1, source_target_pairs={{0,24},{8,16},{16,8},{24,0},{1,25},{9,17},{17,9},{25,1},{2,26},{10... | collective-permute-start | bytes 417800 | tf_op jit(solution)/shard_map/ppermute | solution.py:419
  56.9 1.5 %collective-permute-done.24.refs_4_ = bf16[32,2048]{1,0:T(8,128)(2,1)S(1)} collective-permute-done((bf16[32,2048]{1,0:T(8,128)(2,1)S(1)}, bf16[32,2048]{1,0:T(8,128)(2,1)S(1)}, u32[]{:S(2)}, u32[]{:S(2)}) %collective-permute-start.24) | collective-permute-done | bytes 131104 | tf_op jit(solution)/shard_map/ppermute | solution.py:416
  59.5 1.3 %collective-permute-start.19 = (bf16[32,2048]{1,0:T(8,128)(2,1)S(1)}, bf16[32,2048]{1,0:T(8,128)(2,1)S(1)}, u32[]{:S(2)}, u32[]{:S(2)}) collective-permute-start(bf16[32,2048]{1,0:T(8,128)(2,1)S(1)} %get-tuple-element.87), channel_id=1, source_target_pairs={{0,4},{1,5},{2,6},{3,7},{4,0},{5,1},{6,2},{7,3},{8,12},{9,13},{10,... | collective-permute-start | bytes 393224 | tf_op jit(solution)/shard_map/ppermute | solution.py:416
  60.7 1.5 %collective-permute-start.20 = (bf16[32,2048]{1,0:T(8,128)(2,1)S(1)}, bf16[32,2048]{1,0:T(8,128)(2,1)S(1)}, u32[]{:S(2)}, u32[]{:S(2)}) collective-permute-start(bf16[32,2048]{1,0:T(8,128)(2,1)S(1)} %get-tuple-element.88), channel_id=1, source_target_pairs={{0,6},{1,7},{2,4},{3,5},{4,2},{5,3},{6,0},{7,1},{8,14},{9,15},{10,... | collective-permute-start | bytes 393224 | tf_op jit(solution)/shard_map/ppermute | solution.py:416
  62.2 2.2 %collective-permute-done.19.refs_3_ = bf16[32,2048]{1,0:T(8,128)(2,1)S(1)} collective-permute-done((bf16[32,2048]{1,0:T(8,128)(2,1)S(1)}, bf16[32,2048]{1,0:T(8,128)(2,1)S(1)}, u32[]{:S(2)}, u32[]{:S(2)}) %collective-permute-start.19) | collective-permute-done | bytes 131104 | tf_op jit(solution)/shard_map/ppermute | solution.py:416
  64.4 2.2 %collective-permute-done.20.refs_4_ = bf16[32,2048]{1,0:T(8,128)(2,1)S(1)} collective-permute-done((bf16[32,2048]{1,0:T(8,128)(2,1)S(1)}, bf16[32,2048]{1,0:T(8,128)(2,1)S(1)}, u32[]{:S(2)}, u32[]{:S(2)}) %collective-permute-start.20) | collective-permute-done | bytes 131104 | tf_op jit(solution)/shard_map/ppermute | solution.py:416
  67.0 1.6 %collective-permute-start.29 = (bf16[32,2176]{1,0:T(8,128)(2,1)S(1)}, bf16[32,2176]{1,0:T(8,128)(2,1)S(1)}, u32[]{:S(2)}, u32[]{:S(2)}) collective-permute-start(bf16[32,2176]{1,0:T(8,128)(2,1)S(1)} %finish.1.refs_0_), channel_id=1, source_target_pairs={{0,6},{1,7},{2,4},{3,5},{4,2},{5,3},{6,0},{7,1},{8,14},{9,15},{10,... | collective-permute-start | bytes 417800 | tf_op jit(solution)/shard_map/ppermute | solution.py:416
  69.1 1.4 %collective-permute-start.27 = (bf16[32,2176]{1,0:T(8,128)(2,1)S(1)}, bf16[32,2176]{1,0:T(8,128)(2,1)S(1)}, u32[]{:S(2)}, u32[]{:S(2)}) collective-permute-start(bf16[32,2176]{1,0:T(8,128)(2,1)S(1)} %finish.1.refs_0_), channel_id=1, source_target_pairs={{0,2},{1,3},{2,0},{3,1},{4,6},{5,7},{6,4},{7,5},{8,10},{9,11},{10,... | collective-permute-start | bytes 417800 | tf_op jit(solution)/shard_map/ppermute | solution.py:416
  70.6 3.9 %collective-permute-done.29.refs_3_ = bf16[32,2176]{1,0:T(8,128)(2,1)S(1)} collective-permute-done((bf16[32,2176]{1,0:T(8,128)(2,1)S(1)}, bf16[32,2176]{1,0:T(8,128)(2,1)S(1)}, u32[]{:S(2)}, u32[]{:S(2)}) %collective-permute-start.29) | collective-permute-done | bytes 139296 | tf_op jit(solution)/shard_map/ppermute | solution.py:416
  74.5 1.4 %collective-permute-done.28.refs_2_ = bf16[32,2176]{1,0:T(8,128)(2,1)S(1)} collective-permute-done((bf16[32,2176]{1,0:T(8,128)(2,1)S(1)}, bf16[32,2176]{1,0:T(8,128)(2,1)S(1)}, u32[]{:S(2)}, u32[]{:S(2)}) %collective-permute-start.28) | collective-permute-done | bytes 139296 | tf_op jit(solution)/shard_map/ppermute | solution.py:416
  77.5 4.1 %final.1 = (bf16[256,2048]{1,0:T(8,128)(2,1)}, bf16[1,2048,768]{2,1,0:T(8,128)(2,1)}, bf16[1,384,2048]{2,1,0:T(8,128)(2,1)}) custom-call(bf16[32,2176]{1,0:T(8,128)(2,1)S(1)} %finish.1.refs_0_, bf16[32,2176]{1,0:T(8,128)(2,1)S(1)} %collective-permute-done.27.refs_1_, bf16[32,2176]{1,0:T(8,128)(2,1)S(1)} %collective-permute-done.28.refs_2_, ...), custom_call_target="tpu_custom_call" | custom-call | flops 100663296 | bytes 7340032 | tf_op jit(solution)/shard_map/final/pallas_call | solution.py:609
  (61 shorter events, 11.8 us)
Async XLA Ops:
  0.6 9.6 %collective-permute-start.3 = (bf16[1,2048,768]{2,1,0:T(8,128)(2,1)}, bf16[1,2048,768]{2,1,0:T(8,128)(2,1)S(1)}, u32[]{:S(2)}, u32[]{:S(2)}) collective-permute-start(bf16[1,2048,768]{2,1,0:T(8,128)(2,1)} %refs_10_), channel_id=1, source_target_pairs={{0,1},{1,0},{2,3},{3,2},{4,5},{5,4},{6,7},{7,6},{8,9},{9,8},{10,11... | collective-permute-start | bytes 9437192 | tf_op jit(solution)/shard_map/ppermute | solution.py:416
  1.1 9.1 %collective-permute-start.4 = (bf16[1,384,2048]{2,1,0:T(8,128)(2,1)}, bf16[1,384,2048]{2,1,0:T(8,128)(2,1)}, u32[]{:S(2)}, u32[]{:S(2)}) collective-permute-start(bf16[1,384,2048]{2,1,0:T(8,128)(2,1)} %refs_13_.1), channel_id=1, source_target_pairs={{0,1},{1,0},{2,3},{3,2},{4,5},{5,4},{6,7},{7,6},{8,9},{9,8},{10,11... | collective-permute-start | bytes 4718600 | tf_op jit(solution)/shard_map/ppermute | solution.py:416
  2.9 7.3 %collective-permute-start = (bf16[32,2176]{1,0:T(8,128)(2,1)}, bf16[32,2176]{1,0:T(8,128)(2,1)S(1)}, u32[]{:S(2)}, u32[]{:S(2)}) collective-permute-start(bf16[32,2176]{1,0:T(8,128)(2,1)} %pack.1.refs_0_), channel_id=1, source_target_pairs={{0,8},{8,0},{16,24},{24,16},{1,9},{9,1},{17,25},{25,17},{2,10},{10... | collective-permute-start | bytes 417800 | tf_op jit(solution)/shard_map/ppermute | solution.py:419
  6.0 10.3 %collective-permute-start.2 = (bf16[32,2176]{1,0:T(8,128)(2,1)}, bf16[32,2176]{1,0:T(8,128)(2,1)S(1)}, u32[]{:S(2)}, u32[]{:S(2)}) collective-permute-start(bf16[32,2176]{1,0:T(8,128)(2,1)} %pack.1.refs_0_), channel_id=1, source_target_pairs={{0,24},{8,16},{16,8},{24,0},{1,25},{9,17},{17,9},{25,1},{2,26},{10... | collective-permute-start | bytes 417800 | tf_op jit(solution)/shard_map/ppermute | solution.py:419
  8.4 12.9 %collective-permute-start.1 = (bf16[32,2176]{1,0:T(8,128)(2,1)}, bf16[32,2176]{1,0:T(8,128)(2,1)S(1)}, u32[]{:S(2)}, u32[]{:S(2)}) collective-permute-start(bf16[32,2176]{1,0:T(8,128)(2,1)} %pack.1.refs_0_), channel_id=1, source_target_pairs={{0,16},{8,24},{16,0},{24,8},{1,17},{9,25},{17,1},{25,9},{2,18},{10... | collective-permute-start | bytes 417800 | tf_op jit(solution)/shard_map/ppermute | solution.py:419
  10.2 11.2 %collective-permute-start.7 = (bf16[32,2304]{1,0:T(8,128)(2,1)S(1)}, bf16[32,2304]{1,0:T(8,128)(2,1)S(1)}, u32[]{:S(2)}, u32[]{:S(2)}) collective-permute-start(bf16[32,2304]{1,0:T(8,128)(2,1)S(1)} %pad_maximum_fusion.1), channel_id=1, source_target_pairs={{0,6},{1,7},{2,4},{3,5},{4,2},{5,3},{6,0},{7,1},{8,14},{9,15},{10,... | collective-permute-start | bytes 442376 | tf_op jit(solution)/shard_map/ppermute | solution.py:416
  12.8 8.6 %collective-permute-start.6 = (bf16[32,2304]{1,0:T(8,128)(2,1)S(1)}, bf16[32,2304]{1,0:T(8,128)(2,1)S(1)}, u32[]{:S(2)}, u32[]{:S(2)}) collective-permute-start(bf16[32,2304]{1,0:T(8,128)(2,1)S(1)} %pad_maximum_fusion.1), channel_id=1, source_target_pairs={{0,4},{1,5},{2,6},{3,7},{4,0},{5,1},{6,2},{7,3},{8,12},{9,13},{10,... | collective-permute-start | bytes 442376 | tf_op jit(solution)/shard_map/ppermute | solution.py:416
  13.3 8.1 %collective-permute-start.5 = (bf16[32,2304]{1,0:T(8,128)(2,1)S(1)}, bf16[32,2304]{1,0:T(8,128)(2,1)S(1)}, u32[]{:S(2)}, u32[]{:S(2)}) collective-permute-start(bf16[32,2304]{1,0:T(8,128)(2,1)S(1)} %pad_maximum_fusion.1), channel_id=1, source_target_pairs={{0,2},{1,3},{2,0},{3,1},{4,6},{5,7},{6,4},{7,5},{8,10},{9,11},{10,... | collective-permute-start | bytes 442376 | tf_op jit(solution)/shard_map/ppermute | solution.py:416
  21.4 15.7 %collective-permute-start.10 = (bf16[64,2176]{1,0:T(8,128)(2,1)S(1)}, bf16[64,2176]{1,0:T(8,128)(2,1)S(1)}, u32[]{:S(2)}, u32[]{:S(2)}) collective-permute-start(bf16[64,2176]{1,0:T(8,128)(2,1)S(1)} %pad_maximum_fusion), channel_id=1, source_target_pairs={{0,6},{1,7},{2,4},{3,5},{4,2},{5,3},{6,0},{7,1},{8,14},{9,15},{10,... | collective-permute-start | bytes 835592 | tf_op jit(solution)/shard_map/ppermute | solution.py:416
  24.0 13.6 %collective-permute-start.9 = (bf16[64,2176]{1,0:T(8,128)(2,1)S(1)}, bf16[64,2176]{1,0:T(8,128)(2,1)S(1)}, u32[]{:S(2)}, u32[]{:S(2)}) collective-permute-start(bf16[64,2176]{1,0:T(8,128)(2,1)S(1)} %pad_maximum_fusion), channel_id=1, source_target_pairs={{0,4},{1,5},{2,6},{3,7},{4,0},{5,1},{6,2},{7,3},{8,12},{9,13},{10,... | collective-permute-start | bytes 835592 | tf_op jit(solution)/shard_map/ppermute | solution.py:416
  24.5 13.1 %collective-permute-start.8 = (bf16[64,2176]{1,0:T(8,128)(2,1)S(1)}, bf16[64,2176]{1,0:T(8,128)(2,1)S(1)}, u32[]{:S(2)}, u32[]{:S(2)}) collective-permute-start(bf16[64,2176]{1,0:T(8,128)(2,1)S(1)} %pad_maximum_fusion), channel_id=1, source_target_pairs={{0,2},{1,3},{2,0},{3,1},{4,6},{5,7},{6,4},{7,5},{8,10},{9,11},{10,... | collective-permute-start | bytes 835592 | tf_op jit(solution)/shard_map/ppermute | solution.py:416
  34.0 8.3 %collective-permute-start.11 = (bf16[32,2048]{1,0:T(8,128)(2,1)S(1)}, bf16[32,2048]{1,0:T(8,128)(2,1)S(1)}, u32[]{:S(2)}, u32[]{:S(2)}) collective-permute-start(bf16[32,2048]{1,0:T(8,128)(2,1)S(1)} %get-tuple-element.70), channel_id=1, source_target_pairs={{0,2},{1,3},{2,0},{3,1},{4,6},{5,7},{6,4},{7,5},{8,10},{9,11},{10,... | collective-permute-start | bytes 393224 | tf_op jit(solution)/shard_map/ppermute | solution.py:416
  35.6 6.7 %collective-permute-start.12 = (bf16[32,2048]{1,0:T(8,128)(2,1)S(1)}, bf16[32,2048]{1,0:T(8,128)(2,1)S(1)}, u32[]{:S(2)}, u32[]{:S(2)}) collective-permute-start(bf16[32,2048]{1,0:T(8,128)(2,1)S(1)} %get-tuple-element.71), channel_id=1, source_target_pairs={{0,4},{1,5},{2,6},{3,7},{4,0},{5,1},{6,2},{7,3},{8,12},{9,13},{10,... | collective-permute-start | bytes 393224 | tf_op jit(solution)/shard_map/ppermute | solution.py:416
  37.1 5.9 %collective-permute-start.13 = (bf16[32,2048]{1,0:T(8,128)(2,1)S(1)}, bf16[32,2048]{1,0:T(8,128)(2,1)S(1)}, u32[]{:S(2)}, u32[]{:S(2)}) collective-permute-start(bf16[32,2048]{1,0:T(8,128)(2,1)S(1)} %get-tuple-element.72), channel_id=1, source_target_pairs={{0,6},{1,7},{2,4},{3,5},{4,2},{5,3},{6,0},{7,1},{8,14},{9,15},{10,... | collective-permute-start | bytes 393224 | tf_op jit(solution)/shard_map/ppermute | solution.py:416
  43.0 6.6 %collective-permute-start.14 = (bf16[32,2176]{1,0:T(8,128)(2,1)S(1)}, bf16[32,2176]{1,0:T(8,128)(2,1)S(1)}, u32[]{:S(2)}, u32[]{:S(2)}) collective-permute-start(bf16[32,2176]{1,0:T(8,128)(2,1)S(1)} %get-tuple-element.73), channel_id=1, source_target_pairs={{0,2},{1,3},{2,0},{3,1},{4,6},{5,7},{6,4},{7,5},{8,10},{9,11},{10,... | collective-permute-start | bytes 417800 | tf_op jit(solution)/shard_map/ppermute | solution.py:416
  43.9 6.1 %collective-permute-start.15 = (bf16[32,2176]{1,0:T(8,128)(2,1)S(1)}, bf16[32,2176]{1,0:T(8,128)(2,1)S(1)}, u32[]{:S(2)}, u32[]{:S(2)}) collective-permute-start(bf16[32,2176]{1,0:T(8,128)(2,1)S(1)} %get-tuple-element.74), channel_id=1, source_target_pairs={{0,4},{1,5},{2,6},{3,7},{4,0},{5,1},{6,2},{7,3},{8,12},{9,13},{10,... | collective-permute-start | bytes 417800 | tf_op jit(solution)/shard_map/ppermute | solution.py:416
  45.4 6.6 %collective-permute-start.16 = (bf16[32,2176]{1,0:T(8,128)(2,1)S(1)}, bf16[32,2176]{1,0:T(8,128)(2,1)S(1)}, u32[]{:S(2)}, u32[]{:S(2)}) collective-permute-start(bf16[32,2176]{1,0:T(8,128)(2,1)S(1)} %get-tuple-element.75), channel_id=1, source_target_pairs={{0,6},{1,7},{2,4},{3,5},{4,2},{5,3},{6,0},{7,1},{8,14},{9,15},{10,... | collective-permute-start | bytes 417800 | tf_op jit(solution)/shard_map/ppermute | solution.py:416
  47.1 9.7 %collective-permute-start.22 = (bf16[32,2048]{1,0:T(8,128)(2,1)S(1)}, bf16[32,2048]{1,0:T(8,128)(2,1)S(1)}, u32[]{:S(2)}, u32[]{:S(2)}) collective-permute-start(bf16[32,2048]{1,0:T(8,128)(2,1)S(1)} %get-tuple-element.91), channel_id=1, source_target_pairs={{0,2},{1,3},{2,0},{3,1},{4,6},{5,7},{6,4},{7,5},{8,10},{9,11},{10,... | collective-permute-start | bytes 393224 | tf_op jit(solution)/shard_map/ppermute | solution.py:416
  48.3 8.6 %collective-permute-start.23 = (bf16[32,2048]{1,0:T(8,128)(2,1)S(1)}, bf16[32,2048]{1,0:T(8,128)(2,1)S(1)}, u32[]{:S(2)}, u32[]{:S(2)}) collective-permute-start(bf16[32,2048]{1,0:T(8,128)(2,1)S(1)} %get-tuple-element.92), channel_id=1, source_target_pairs={{0,4},{1,5},{2,6},{3,7},{4,0},{5,1},{6,2},{7,3},{8,12},{9,13},{10,... | collective-permute-start | bytes 393224 | tf_op jit(solution)/shard_map/ppermute | solution.py:416
  52.0 6.4 %collective-permute-start.24 = (bf16[32,2048]{1,0:T(8,128)(2,1)S(1)}, bf16[32,2048]{1,0:T(8,128)(2,1)S(1)}, u32[]{:S(2)}, u32[]{:S(2)}) collective-permute-start(bf16[32,2048]{1,0:T(8,128)(2,1)S(1)} %get-tuple-element.93), channel_id=1, source_target_pairs={{0,6},{1,7},{2,4},{3,5},{4,2},{5,3},{6,0},{7,1},{8,14},{9,15},{10,... | collective-permute-start | bytes 393224 | tf_op jit(solution)/shard_map/ppermute | solution.py:416
  53.1 7.6 %collective-permute-start.18 = (bf16[32,2048]{1,0:T(8,128)(2,1)S(1)}, bf16[32,2048]{1,0:T(8,128)(2,1)S(1)}, u32[]{:S(2)}, u32[]{:S(2)}) collective-permute-start(bf16[32,2048]{1,0:T(8,128)(2,1)S(1)} %get-tuple-element.86), channel_id=1, source_target_pairs={{0,2},{1,3},{2,0},{3,1},{4,6},{5,7},{6,4},{7,5},{8,10},{9,11},{10,... | collective-permute-start | bytes 393224 | tf_op jit(solution)/shard_map/ppermute | solution.py:416
  54.2 12.6 %collective-permute-start.21 = (bf16[32,2176]{1,0:T(8,128)(2,1)S(1)}, bf16[32,2176]{1,0:T(8,128)(2,1)S(1)}, u32[]{:S(2)}, u32[]{:S(2)}) collective-permute-start(bf16[32,2176]{1,0:T(8,128)(2,1)S(1)} %get-tuple-element.85), channel_id=1, source_target_pairs={{0,24},{8,16},{16,8},{24,0},{1,25},{9,17},{17,9},{25,1},{2,26},{10... | collective-permute-start | bytes 417800 | tf_op jit(solution)/shard_map/ppermute | solution.py:419
  56.8 10.0 %collective-permute-start.26 = (bf16[32,2176]{1,0:T(8,128)(2,1)S(1)}, bf16[32,2176]{1,0:T(8,128)(2,1)S(1)}, u32[]{:S(2)}, u32[]{:S(2)}) collective-permute-start(bf16[32,2176]{1,0:T(8,128)(2,1)S(1)} %combine.7), channel_id=1, source_target_pairs={{0,8},{8,0},{16,24},{24,16},{1,9},{9,1},{17,25},{25,17},{2,10},{10... | collective-permute-start | bytes 417800 | tf_op jit(solution)/shard_map/ppermute | solution.py:419
  58.6 8.4 %collective-permute-start.25 = (bf16[32,2176]{1,0:T(8,128)(2,1)S(1)}, bf16[32,2176]{1,0:T(8,128)(2,1)S(1)}, u32[]{:S(2)}, u32[]{:S(2)}) collective-permute-start(bf16[32,2176]{1,0:T(8,128)(2,1)S(1)} %combine.6), channel_id=1, source_target_pairs={{0,16},{8,24},{16,0},{24,8},{1,17},{9,25},{17,1},{25,9},{2,18},{10... | collective-permute-start | bytes 417800 | tf_op jit(solution)/shard_map/ppermute | solution.py:419
  59.5 5.0 %collective-permute-start.19 = (bf16[32,2048]{1,0:T(8,128)(2,1)S(1)}, bf16[32,2048]{1,0:T(8,128)(2,1)S(1)}, u32[]{:S(2)}, u32[]{:S(2)}) collective-permute-start(bf16[32,2048]{1,0:T(8,128)(2,1)S(1)} %get-tuple-element.87), channel_id=1, source_target_pairs={{0,4},{1,5},{2,6},{3,7},{4,0},{5,1},{6,2},{7,3},{8,12},{9,13},{10,... | collective-permute-start | bytes 393224 | tf_op jit(solution)/shard_map/ppermute | solution.py:416
  60.7 5.9 %collective-permute-start.20 = (bf16[32,2048]{1,0:T(8,128)(2,1)S(1)}, bf16[32,2048]{1,0:T(8,128)(2,1)S(1)}, u32[]{:S(2)}, u32[]{:S(2)}) collective-permute-start(bf16[32,2048]{1,0:T(8,128)(2,1)S(1)} %get-tuple-element.88), channel_id=1, source_target_pairs={{0,6},{1,7},{2,4},{3,5},{4,2},{5,3},{6,0},{7,1},{8,14},{9,15},{10,... | collective-permute-start | bytes 393224 | tf_op jit(solution)/shard_map/ppermute | solution.py:416
  67.0 7.5 %collective-permute-start.29 = (bf16[32,2176]{1,0:T(8,128)(2,1)S(1)}, bf16[32,2176]{1,0:T(8,128)(2,1)S(1)}, u32[]{:S(2)}, u32[]{:S(2)}) collective-permute-start(bf16[32,2176]{1,0:T(8,128)(2,1)S(1)} %finish.1.refs_0_), channel_id=1, source_target_pairs={{0,6},{1,7},{2,4},{3,5},{4,2},{5,3},{6,0},{7,1},{8,14},{9,15},{10,... | collective-permute-start | bytes 417800 | tf_op jit(solution)/shard_map/ppermute | solution.py:416
  68.6 7.4 %collective-permute-start.28 = (bf16[32,2176]{1,0:T(8,128)(2,1)S(1)}, bf16[32,2176]{1,0:T(8,128)(2,1)S(1)}, u32[]{:S(2)}, u32[]{:S(2)}) collective-permute-start(bf16[32,2176]{1,0:T(8,128)(2,1)S(1)} %finish.1.refs_0_), channel_id=1, source_target_pairs={{0,4},{1,5},{2,6},{3,7},{4,0},{5,1},{6,2},{7,3},{8,12},{9,13},{10,... | collective-permute-start | bytes 417800 | tf_op jit(solution)/shard_map/ppermute | solution.py:416
  69.1 6.8 %collective-permute-start.27 = (bf16[32,2176]{1,0:T(8,128)(2,1)S(1)}, bf16[32,2176]{1,0:T(8,128)(2,1)S(1)}, u32[]{:S(2)}, u32[]{:S(2)}) collective-permute-start(bf16[32,2176]{1,0:T(8,128)(2,1)S(1)} %finish.1.refs_0_), channel_id=1, source_target_pairs={{0,2},{1,3},{2,0},{3,1},{4,6},{5,7},{6,4},{7,5},{8,10},{9,11},{10,... | collective-permute-start | bytes 417800 | tf_op jit(solution)/shard_map/ppermute | solution.py:416
  70.6 5.9 %collective-permute-start.30 = (bf16[32,2176]{1,0:T(8,128)(2,1)S(1)}, bf16[32,2176]{1,0:T(8,128)(2,1)S(1)}, u32[]{:S(2)}, u32[]{:S(2)}) collective-permute-start(bf16[32,2176]{1,0:T(8,128)(2,1)S(1)} %finish.1.refs_0_), channel_id=1, source_target_pairs={{0,1},{1,0},{2,3},{3,2},{4,5},{5,4},{6,7},{7,6},{8,9},{9,8},{10,11... | collective-permute-start | bytes 417800 | tf_op jit(solution)/shard_map/ppermute | solution.py:416
  74.5 2.0 %collective-permute-start.33 = (bf16[32,2176]{1,0:T(8,128)(2,1)S(1)}, bf16[32,2176]{1,0:T(8,128)(2,1)S(1)}, u32[]{:S(2)}, u32[]{:S(2)}) collective-permute-start(bf16[32,2176]{1,0:T(8,128)(2,1)S(1)} %collective-permute-done.29.refs_3_), channel_id=1, source_target_pairs={{0,1},{1,0},{2,3},{3,2},{4,5},{5,4},{6,7},{7,6},{8,9},{9,8},{10,11... | collective-permute-start | bytes 417800 | tf_op jit(solution)/shard_map/ppermute | solution.py:416
  76.0 1.6 %collective-permute-start.31 = (bf16[32,2176]{1,0:T(8,128)(2,1)S(1)}, bf16[32,2176]{1,0:T(8,128)(2,1)S(1)}, u32[]{:S(2)}, u32[]{:S(2)}) collective-permute-start(bf16[32,2176]{1,0:T(8,128)(2,1)S(1)} %collective-permute-done.27.refs_1_), channel_id=1, source_target_pairs={{0,1},{1,0},{2,3},{3,2},{4,5},{5,4},{6,7},{7,6},{8,9},{9,8},{10,11... | collective-permute-start | bytes 417800 | tf_op jit(solution)/shard_map/ppermute | solution.py:416
  (8 other events, 39.6 us)

commit v15 on v14

--- a/solution.py
+++ b/solution.py
@@ -579,7 +579,7 @@
         returned[1][1:] = send_back(dp_count - 1, chips - 1, returned[1][1:])
     before = dp_count - 1
     for hop in rest:
-        returned[before][1:], found = send_back(hop, 1, (returned[before][1:], found))
+        returned[before][-1], found = send_back(hop, 1, (returned[before][-1], found))
         before = hop
     homeward = []
     last_sum = None

time: 81.9 us -> 81.3 us (level)
  waiting for transfers between devices: 24.3 us -> 22.1 us
  starting transfers between devices: 34.9 us -> 36.4 us
    ppermute x28, waiting for transfers between devices: 15.7 us -> 13.6 us  [to_lane(): lax.ppermute(value, 'expert', [(j, j ^ step) for j in range(expert_count)])]
    ppermute x28, starting transfers between devices: 25.8 us -> 26.9 us  [to_lane(): lax.ppermute(value, 'expert', [(j, j ^ step) for j in range(expert_count)])]
  transfers between devices with their start and end apart: 34 -> 34, of which waited for: 15 -> 13; matrix products, arithmetic and copies ran while one was open for 1% -> 1% of each run, Pallas kernels for 15% -> 15%
where the time goes in v15:
time: 81.3 us; the launch traced here: 81 us
  starting transfers between devices  36.4 us (45%)
  waiting for transfers between devices  22.1 us (27%)
  Pallas kernels  16.3 us (20%)
  local copies, waits for them, and re-layouts  5.26 us (6%)
  between operations  0.84 us (1%)
    ppermute x28, starting transfers between devices, to_lane(): lax.ppermute(value, 'expert', [(j, j ^ step) for j in range(expert_count)])  26.9 us
    ppermute x28, waiting for transfers between devices, to_lane(): lax.ppermute(value, 'expert', [(j, j ^ step) for j in range(expert_count)])  13.6 us
    ppermute x6, starting transfers between devices, to_plane(): return lax.ppermute(value, 'dp', [(p, p ^ step) for p in range(dp_count)])  9.43 us
    pallas_call x2, Pallas kernels, expert(): pl.pallas_call(functools.partial(expert_kernel, layout), out_shape=out_sh...  9.17 us
    ppermute x6, waiting for transfers between devices, to_plane(): return lax.ppermute(value, 'dp', [(p, p ^ step) for p in range(dp_count)])  8.51 us
    unnamed x12, local copies, waits for them, and re-layouts  4.53 us
    pallas_call x1, Pallas kernels, body(): pl.pallas_call(functools.partial(final_kernel, len(pieces), n_blocks), ou...  4.12 us
    pallas_call x1, Pallas kernels, body(): pl.pallas_call(functools.partial(pack_kernel, seq_dev), out_shape=jax.Sha...  1.66 us
  transfers between devices with their start and end apart: 34, of which 13 were waited for; matrix products, arithmetic and copies ran while one was open for 1% of the time, Pallas kernels for 15%

profile of v15, /device:TPU:0, one launch (start us, length us, event | category | flops | bytes accessed | tf_op | source)
XLA Modules:
  0.0 81.0 jit_solution(13277635166275468529)
XLA Ops:
  1.2 1.7 %pack.1.refs_0_ = bf16[32,2176]{1,0:T(8,128)(2,1)} custom-call(s32[4]{0:T(128)} %partners.1, s32[1,256]{1,0:T(1,128)} %bitcast.2, f32[1,256]{1,0:T(1,128)} %bitcast.3, bf16[256,2048]{1,0:T(8,128)(2,1)} %refs_0_.1), custom_call_target="tpu_custom_call" | custom-call | bytes 524288 | tf_op jit(solution)/shard_map/pack/pallas_call | solution.py:425
  2.9 3.1 %collective-permute-start = (bf16[32,2176]{1,0:T(8,128)(2,1)}, bf16[32,2176]{1,0:T(8,128)(2,1)S(1)}, u32[]{:S(2)}, u32[]{:S(2)}) collective-permute-start(bf16[32,2176]{1,0:T(8,128)(2,1)} %pack.1.refs_0_), channel_id=1, source_target_pairs={{0,8},{8,0},{16,24},{24,16},{1,9},{9,1},{17,25},{25,17},{2,10},{10... | collective-permute-start | bytes 417800 | tf_op jit(solution)/shard_map/ppermute | solution.py:419
  6.0 2.5 %collective-permute-start.2 = (bf16[32,2176]{1,0:T(8,128)(2,1)}, bf16[32,2176]{1,0:T(8,128)(2,1)S(1)}, u32[]{:S(2)}, u32[]{:S(2)}) collective-permute-start(bf16[32,2176]{1,0:T(8,128)(2,1)} %pack.1.refs_0_), channel_id=1, source_target_pairs={{0,24},{8,16},{16,8},{24,0},{1,25},{9,17},{17,9},{25,1},{2,26},{10... | collective-permute-start | bytes 417800 | tf_op jit(solution)/shard_map/ppermute | solution.py:419
  10.2 2.6 %collective-permute-start.7 = (bf16[32,2304]{1,0:T(8,128)(2,1)S(1)}, bf16[32,2304]{1,0:T(8,128)(2,1)S(1)}, u32[]{:S(2)}, u32[]{:S(2)}) collective-permute-start(bf16[32,2304]{1,0:T(8,128)(2,1)S(1)} %pad_maximum_fusion.1), channel_id=1, source_target_pairs={{0,6},{1,7},{2,4},{3,5},{4,2},{5,3},{6,0},{7,1},{8,14},{9,15},{10,... | collective-permute-start | bytes 442376 | tf_op jit(solution)/shard_map/ppermute | solution.py:416
  13.8 2.4 %collective-permute-done.2.refs_6_ = bf16[32,2176]{1,0:T(8,128)(2,1)S(1)} collective-permute-done((bf16[32,2176]{1,0:T(8,128)(2,1)}, bf16[32,2176]{1,0:T(8,128)(2,1)S(1)}, u32[]{:S(2)}, u32[]{:S(2)}) %collective-permute-start.2) | collective-permute-done | bytes 139296 | tf_op jit(solution)/shard_map/ppermute | solution.py:419
  16.2 5.1 %collective-permute-done.1.refs_5_ = bf16[32,2176]{1,0:T(8,128)(2,1)S(1)} collective-permute-done((bf16[32,2176]{1,0:T(8,128)(2,1)}, bf16[32,2176]{1,0:T(8,128)(2,1)S(1)}, u32[]{:S(2)}, u32[]{:S(2)}) %collective-permute-start.1) | collective-permute-done | bytes 139296 | tf_op jit(solution)/shard_map/ppermute | solution.py:419
  21.4 2.5 %collective-permute-start.10 = (bf16[64,2176]{1,0:T(8,128)(2,1)S(1)}, bf16[64,2176]{1,0:T(8,128)(2,1)S(1)}, u32[]{:S(2)}, u32[]{:S(2)}) collective-permute-start(bf16[64,2176]{1,0:T(8,128)(2,1)S(1)} %pad_maximum_fusion), channel_id=1, source_target_pairs={{0,6},{1,7},{2,4},{3,5},{4,2},{5,3},{6,0},{7,1},{8,14},{9,15},{10,... | collective-permute-start | bytes 835592 | tf_op jit(solution)/shard_map/ppermute | solution.py:416
  25.0 1.4 %copy-done = bf16[1,384,2048]{2,1,0:T(8,128)(2,1)S(1)} copy-done((bf16[1,384,2048]{2,1,0:T(8,128)(2,1)S(1)}, bf16[1,384,2048]{2,1,0:T(8,128)(2,1)}, u32[]{:S(2)}) %copy-start) | copy-done | bytes 1572888
  26.4 1.9 %copy-done.2 = bf16[1,2048,768]{2,1,0:T(8,128)(2,1)S(1)} copy-done((bf16[1,2048,768]{2,1,0:T(8,128)(2,1)S(1)}, bf16[1,2048,768]{2,1,0:T(8,128)(2,1)}, u32[]{:S(2)}) %copy-start.2) | copy-done | bytes 3145752
  28.3 1.2 %copy-done.4 = bf16[256,2048]{1,0:T(8,128)(2,1)S(1)} copy-done((bf16[256,2048]{1,0:T(8,128)(2,1)S(1)}, bf16[256,2048]{1,0:T(8,128)(2,1)}, u32[]{:S(2)}) %copy-start.4) | copy-done | bytes 1048600
  29.5 4.5 %experts.2 = (bf16[32,2048]{1,0:T(8,128)(2,1)S(1)}, bf16[32,2048]{1,0:T(8,128)(2,1)S(1)}, bf16[32,2048]{1,0:T(8,128)(2,1)S(1)}, bf16[32,2048]{1,0:T(8,128)(2,1)S...) custom-call(bf16[256,2048]{1,0:T(8,128)(2,1)S(1)} %copy-done.4, ...), custom_call_target="tpu_custom_call" | custom-call | flops 2415919104 | bytes 12582912 | tf_op jit(solution)/shard_map/experts/pallas_call | solution.py:502
  34.0 1.6 %collective-permute-start.11 = (bf16[32,2048]{1,0:T(8,128)(2,1)S(1)}, bf16[32,2048]{1,0:T(8,128)(2,1)S(1)}, u32[]{:S(2)}, u32[]{:S(2)}) collective-permute-start(bf16[32,2048]{1,0:T(8,128)(2,1)S(1)} %get-tuple-element.68), channel_id=1, source_target_pairs={{0,2},{1,3},{2,0},{3,1},{4,6},{5,7},{6,4},{7,5},{8,10},{9,11},{10,... | collective-permute-start | bytes 393224 | tf_op jit(solution)/shard_map/ppermute | solution.py:416
  35.6 1.5 %collective-permute-start.12 = (bf16[32,2048]{1,0:T(8,128)(2,1)S(1)}, bf16[32,2048]{1,0:T(8,128)(2,1)S(1)}, u32[]{:S(2)}, u32[]{:S(2)}) collective-permute-start(bf16[32,2048]{1,0:T(8,128)(2,1)S(1)} %get-tuple-element.69), channel_id=1, source_target_pairs={{0,4},{1,5},{2,6},{3,7},{4,0},{5,1},{6,2},{7,3},{8,12},{9,13},{10,... | collective-permute-start | bytes 393224 | tf_op jit(solution)/shard_map/ppermute | solution.py:416
  37.6 4.7 %experts.3 = (bf16[32,2048]{1,0:T(8,128)(2,1)S(1)}, bf16[32,2048]{1,0:T(8,128)(2,1)S(1)}, bf16[32,2048]{1,0:T(8,128)(2,1)S(1)}, bf16[32,2048]{1,0:T(8,128)(2,1)S...) custom-call(bf16[32,2176]{1,0:T(8,128)(2,1)S(1)} %copy-done.5, ...), custom_call_target="tpu_custom_call" | custom-call | flops 2566914048 | bytes 12582912 | tf_op jit(solution)/shard_map/experts/pallas_call | solution.py:502
  43.0 1.9 %collective-permute-start.14 = (bf16[32,2176]{1,0:T(8,128)(2,1)S(1)}, bf16[32,2176]{1,0:T(8,128)(2,1)S(1)}, u32[]{:S(2)}, u32[]{:S(2)}) collective-permute-start(bf16[32,2176]{1,0:T(8,128)(2,1)S(1)} %get-tuple-element.71), channel_id=1, source_target_pairs={{0,6},{1,7},{2,4},{3,5},{4,2},{5,3},{6,0},{7,1},{8,14},{9,15},{10,... | collective-permute-start | bytes 417800 | tf_op jit(solution)/shard_map/ppermute | solution.py:416
  45.6 0.9 %collective-permute-start.17 = (bf16[32,2176]{1,0:T(8,128)(2,1)S(1)}, bf16[32,2176]{1,0:T(8,128)(2,1)S(1)}, u32[]{:S(2)}, u32[]{:S(2)}) collective-permute-start(bf16[32,2176]{1,0:T(8,128)(2,1)S(1)} %get-tuple-element.79), channel_id=1, source_target_pairs={{0,4},{1,5},{2,6},{3,7},{4,0},{5,1},{6,2},{7,3},{8,12},{9,13},{10,... | collective-permute-start | bytes 417800 | tf_op jit(solution)/shard_map/ppermute | solution.py:416
  47.1 1.0 %collective-permute-start.22 = (bf16[32,2048]{1,0:T(8,128)(2,1)S(1)}, bf16[32,2048]{1,0:T(8,128)(2,1)S(1)}, u32[]{:S(2)}, u32[]{:S(2)}) collective-permute-start(bf16[32,2048]{1,0:T(8,128)(2,1)S(1)} %get-tuple-element.87), channel_id=1, source_target_pairs={{0,2},{1,3},{2,0},{3,1},{4,6},{5,7},{6,4},{7,5},{8,10},{9,11},{10,... | collective-permute-start | bytes 393224 | tf_op jit(solution)/shard_map/ppermute | solution.py:416
  48.3 1.3 %collective-permute-start.23 = (bf16[32,2048]{1,0:T(8,128)(2,1)S(1)}, bf16[32,2048]{1,0:T(8,128)(2,1)S(1)}, u32[]{:S(2)}, u32[]{:S(2)}) collective-permute-start(bf16[32,2048]{1,0:T(8,128)(2,1)S(1)} %get-tuple-element.88), channel_id=1, source_target_pairs={{0,4},{1,5},{2,6},{3,7},{4,0},{5,1},{6,2},{7,3},{8,12},{9,13},{10,... | collective-permute-start | bytes 393224 | tf_op jit(solution)/shard_map/ppermute | solution.py:416
  49.6 1.3 %collective-permute-start.24 = (bf16[32,2048]{1,0:T(8,128)(2,1)S(1)}, bf16[32,2048]{1,0:T(8,128)(2,1)S(1)}, u32[]{:S(2)}, u32[]{:S(2)}) collective-permute-start(bf16[32,2048]{1,0:T(8,128)(2,1)S(1)} %get-tuple-element.89), channel_id=1, source_target_pairs={{0,6},{1,7},{2,4},{3,5},{4,2},{5,3},{6,0},{7,1},{8,14},{9,15},{10,... | collective-permute-start | bytes 393224 | tf_op jit(solution)/shard_map/ppermute | solution.py:416
  51.1 1.2 %collective-permute-start.18 = (bf16[32,2048]{1,0:T(8,128)(2,1)S(1)}, bf16[32,2048]{1,0:T(8,128)(2,1)S(1)}, u32[]{:S(2)}, u32[]{:S(2)}) collective-permute-start(bf16[32,2048]{1,0:T(8,128)(2,1)S(1)} %get-tuple-element.82), channel_id=1, source_target_pairs={{0,2},{1,3},{2,0},{3,1},{4,6},{5,7},{6,4},{7,5},{8,10},{9,11},{10,... | collective-permute-start | bytes 393224 | tf_op jit(solution)/shard_map/ppermute | solution.py:416
  52.3 2.6 %collective-permute-start.21 = (bf16[32,2176]{1,0:T(8,128)(2,1)S(1)}, bf16[32,2176]{1,0:T(8,128)(2,1)S(1)}, u32[]{:S(2)}, u32[]{:S(2)}) collective-permute-start(bf16[32,2176]{1,0:T(8,128)(2,1)S(1)} %get-tuple-element.81), channel_id=1, source_target_pairs={{0,24},{8,16},{16,8},{24,0},{1,25},{9,17},{17,9},{25,1},{2,26},{10... | collective-permute-start | bytes 417800 | tf_op jit(solution)/shard_map/ppermute | solution.py:419
  55.1 1.3 %collective-permute-done.23.refs_3_ = bf16[32,2048]{1,0:T(8,128)(2,1)S(1)} collective-permute-done((bf16[32,2048]{1,0:T(8,128)(2,1)S(1)}, bf16[32,2048]{1,0:T(8,128)(2,1)S(1)}, u32[]{:S(2)}, u32[]{:S(2)}) %collective-permute-start.23) | collective-permute-done | bytes 131104 | tf_op jit(solution)/shard_map/ppermute | solution.py:416
  57.1 1.1 %collective-permute-start.25 = (bf16[32,2176]{1,0:T(8,128)(2,1)S(1)}, bf16[32,2176]{1,0:T(8,128)(2,1)S(1)}, u32[]{:S(2)}, u32[]{:S(2)}) collective-permute-start(bf16[32,2176]{1,0:T(8,128)(2,1)S(1)} %combine.6), channel_id=1, source_target_pairs={{0,16},{8,24},{16,0},{24,8},{1,17},{9,25},{17,1},{25,9},{2,18},{10... | collective-permute-start | bytes 417800 | tf_op jit(solution)/shard_map/ppermute | solution.py:419
  58.3 2.1 %collective-permute-start.19 = (bf16[32,2048]{1,0:T(8,128)(2,1)S(1)}, bf16[32,2048]{1,0:T(8,128)(2,1)S(1)}, u32[]{:S(2)}, u32[]{:S(2)}) collective-permute-start(bf16[32,2048]{1,0:T(8,128)(2,1)S(1)} %get-tuple-element.83), channel_id=1, source_target_pairs={{0,4},{1,5},{2,6},{3,7},{4,0},{5,1},{6,2},{7,3},{8,12},{9,13},{10,... | collective-permute-start | bytes 393224 | tf_op jit(solution)/shard_map/ppermute | solution.py:416
  60.4 1.3 %collective-permute-start.20 = (bf16[32,2048]{1,0:T(8,128)(2,1)S(1)}, bf16[32,2048]{1,0:T(8,128)(2,1)S(1)}, u32[]{:S(2)}, u32[]{:S(2)}) collective-permute-start(bf16[32,2048]{1,0:T(8,128)(2,1)S(1)} %get-tuple-element.84), channel_id=1, source_target_pairs={{0,6},{1,7},{2,4},{3,5},{4,2},{5,3},{6,0},{7,1},{8,14},{9,15},{10,... | collective-permute-start | bytes 393224 | tf_op jit(solution)/shard_map/ppermute | solution.py:416
  61.6 3.1 %collective-permute-done.19.refs_3_ = bf16[32,2048]{1,0:T(8,128)(2,1)S(1)} collective-permute-done((bf16[32,2048]{1,0:T(8,128)(2,1)S(1)}, bf16[32,2048]{1,0:T(8,128)(2,1)S(1)}, u32[]{:S(2)}, u32[]{:S(2)}) %collective-permute-start.19) | collective-permute-done | bytes 131104 | tf_op jit(solution)/shard_map/ppermute | solution.py:416
  64.7 1.5 %collective-permute-done.20.refs_4_ = bf16[32,2048]{1,0:T(8,128)(2,1)S(1)} collective-permute-done((bf16[32,2048]{1,0:T(8,128)(2,1)S(1)}, bf16[32,2048]{1,0:T(8,128)(2,1)S(1)}, u32[]{:S(2)}, u32[]{:S(2)}) %collective-permute-start.20) | collective-permute-done | bytes 131104 | tf_op jit(solution)/shard_map/ppermute | solution.py:416
  66.5 1.5 %collective-permute-start.29 = (bf16[32,2176]{1,0:T(8,128)(2,1)S(1)}, bf16[32,2176]{1,0:T(8,128)(2,1)S(1)}, u32[]{:S(2)}, u32[]{:S(2)}) collective-permute-start(bf16[32,2176]{1,0:T(8,128)(2,1)S(1)} %finish.1.refs_0_), channel_id=1, source_target_pairs={{0,6},{1,7},{2,4},{3,5},{4,2},{5,3},{6,0},{7,1},{8,14},{9,15},{10,... | collective-permute-start | bytes 417800 | tf_op jit(solution)/shard_map/ppermute | solution.py:416
  68.0 1.2 %collective-permute-start.28 = (bf16[32,2176]{1,0:T(8,128)(2,1)S(1)}, bf16[32,2176]{1,0:T(8,128)(2,1)S(1)}, u32[]{:S(2)}, u32[]{:S(2)}) collective-permute-start(bf16[32,2176]{1,0:T(8,128)(2,1)S(1)} %finish.1.refs_0_), channel_id=1, source_target_pairs={{0,4},{1,5},{2,6},{3,7},{4,0},{5,1},{6,2},{7,3},{8,12},{9,13},{10,... | collective-permute-start | bytes 417800 | tf_op jit(solution)/shard_map/ppermute | solution.py:416
  70.1 3.8 %collective-permute-done.29.refs_3_ = bf16[32,2176]{1,0:T(8,128)(2,1)S(1)} collective-permute-done((bf16[32,2176]{1,0:T(8,128)(2,1)S(1)}, bf16[32,2176]{1,0:T(8,128)(2,1)S(1)}, u32[]{:S(2)}, u32[]{:S(2)}) %collective-permute-start.29) | collective-permute-done | bytes 139296 | tf_op jit(solution)/shard_map/ppermute | solution.py:416
  73.9 1.3 %collective-permute-done.28.refs_2_ = bf16[32,2176]{1,0:T(8,128)(2,1)S(1)} collective-permute-done((bf16[32,2176]{1,0:T(8,128)(2,1)S(1)}, bf16[32,2176]{1,0:T(8,128)(2,1)S(1)}, u32[]{:S(2)}, u32[]{:S(2)}) %collective-permute-start.28) | collective-permute-done | bytes 139296 | tf_op jit(solution)/shard_map/ppermute | solution.py:416
  76.8 4.1 %final.1 = (bf16[256,2048]{1,0:T(8,128)(2,1)}, bf16[1,2048,768]{2,1,0:T(8,128)(2,1)}, bf16[1,384,2048]{2,1,0:T(8,128)(2,1)}) custom-call(bf16[32,2176]{1,0:T(8,128)(2,1)S(1)} %finish.1.refs_0_, bf16[32,2176]{1,0:T(8,128)(2,1)S(1)} %collective-permute-done.27.refs_1_, bf16[32,2176]{1,0:T(8,128)(2,1)S(1)} %collective-permute-done.28.refs_2_, ...), custom_call_target="tpu_custom_call" | custom-call | flops 100663296 | bytes 7340032 | tf_op jit(solution)/shard_map/final/pallas_call | solution.py:609
  (61 shorter events, 11.1 us)
Async XLA Ops:
  0.6 9.6 %collective-permute-start.3 = (bf16[1,2048,768]{2,1,0:T(8,128)(2,1)}, bf16[1,2048,768]{2,1,0:T(8,128)(2,1)S(1)}, u32[]{:S(2)}, u32[]{:S(2)}) collective-permute-start(bf16[1,2048,768]{2,1,0:T(8,128)(2,1)} %refs_10_), channel_id=1, source_target_pairs={{0,1},{1,0},{2,3},{3,2},{4,5},{5,4},{6,7},{7,6},{8,9},{9,8},{10,11... | collective-permute-start | bytes 9437192 | tf_op jit(solution)/shard_map/ppermute | solution.py:416
  1.1 9.1 %collective-permute-start.4 = (bf16[1,384,2048]{2,1,0:T(8,128)(2,1)}, bf16[1,384,2048]{2,1,0:T(8,128)(2,1)}, u32[]{:S(2)}, u32[]{:S(2)}) collective-permute-start(bf16[1,384,2048]{2,1,0:T(8,128)(2,1)} %refs_13_.1), channel_id=1, source_target_pairs={{0,1},{1,0},{2,3},{3,2},{4,5},{5,4},{6,7},{7,6},{8,9},{9,8},{10,11... | collective-permute-start | bytes 4718600 | tf_op jit(solution)/shard_map/ppermute | solution.py:416
  2.9 7.3 %collective-permute-start = (bf16[32,2176]{1,0:T(8,128)(2,1)}, bf16[32,2176]{1,0:T(8,128)(2,1)S(1)}, u32[]{:S(2)}, u32[]{:S(2)}) collective-permute-start(bf16[32,2176]{1,0:T(8,128)(2,1)} %pack.1.refs_0_), channel_id=1, source_target_pairs={{0,8},{8,0},{16,24},{24,16},{1,9},{9,1},{17,25},{25,17},{2,10},{10... | collective-permute-start | bytes 417800 | tf_op jit(solution)/shard_map/ppermute | solution.py:419
  6.0 10.3 %collective-permute-start.2 = (bf16[32,2176]{1,0:T(8,128)(2,1)}, bf16[32,2176]{1,0:T(8,128)(2,1)S(1)}, u32[]{:S(2)}, u32[]{:S(2)}) collective-permute-start(bf16[32,2176]{1,0:T(8,128)(2,1)} %pack.1.refs_0_), channel_id=1, source_target_pairs={{0,24},{8,16},{16,8},{24,0},{1,25},{9,17},{17,9},{25,1},{2,26},{10... | collective-permute-start | bytes 417800 | tf_op jit(solution)/shard_map/ppermute | solution.py:419
  8.4 12.9 %collective-permute-start.1 = (bf16[32,2176]{1,0:T(8,128)(2,1)}, bf16[32,2176]{1,0:T(8,128)(2,1)S(1)}, u32[]{:S(2)}, u32[]{:S(2)}) collective-permute-start(bf16[32,2176]{1,0:T(8,128)(2,1)} %pack.1.refs_0_), channel_id=1, source_target_pairs={{0,16},{8,24},{16,0},{24,8},{1,17},{9,25},{17,1},{25,9},{2,18},{10... | collective-permute-start | bytes 417800 | tf_op jit(solution)/shard_map/ppermute | solution.py:419
  10.2 11.2 %collective-permute-start.7 = (bf16[32,2304]{1,0:T(8,128)(2,1)S(1)}, bf16[32,2304]{1,0:T(8,128)(2,1)S(1)}, u32[]{:S(2)}, u32[]{:S(2)}) collective-permute-start(bf16[32,2304]{1,0:T(8,128)(2,1)S(1)} %pad_maximum_fusion.1), channel_id=1, source_target_pairs={{0,6},{1,7},{2,4},{3,5},{4,2},{5,3},{6,0},{7,1},{8,14},{9,15},{10,... | collective-permute-start | bytes 442376 | tf_op jit(solution)/shard_map/ppermute | solution.py:416
  12.8 8.6 %collective-permute-start.6 = (bf16[32,2304]{1,0:T(8,128)(2,1)S(1)}, bf16[32,2304]{1,0:T(8,128)(2,1)S(1)}, u32[]{:S(2)}, u32[]{:S(2)}) collective-permute-start(bf16[32,2304]{1,0:T(8,128)(2,1)S(1)} %pad_maximum_fusion.1), channel_id=1, source_target_pairs={{0,4},{1,5},{2,6},{3,7},{4,0},{5,1},{6,2},{7,3},{8,12},{9,13},{10,... | collective-permute-start | bytes 442376 | tf_op jit(solution)/shard_map/ppermute | solution.py:416
  13.3 8.1 %collective-permute-start.5 = (bf16[32,2304]{1,0:T(8,128)(2,1)S(1)}, bf16[32,2304]{1,0:T(8,128)(2,1)S(1)}, u32[]{:S(2)}, u32[]{:S(2)}) collective-permute-start(bf16[32,2304]{1,0:T(8,128)(2,1)S(1)} %pad_maximum_fusion.1), channel_id=1, source_target_pairs={{0,2},{1,3},{2,0},{3,1},{4,6},{5,7},{6,4},{7,5},{8,10},{9,11},{10,... | collective-permute-start | bytes 442376 | tf_op jit(solution)/shard_map/ppermute | solution.py:416
  21.4 15.7 %collective-permute-start.10 = (bf16[64,2176]{1,0:T(8,128)(2,1)S(1)}, bf16[64,2176]{1,0:T(8,128)(2,1)S(1)}, u32[]{:S(2)}, u32[]{:S(2)}) collective-permute-start(bf16[64,2176]{1,0:T(8,128)(2,1)S(1)} %pad_maximum_fusion), channel_id=1, source_target_pairs={{0,6},{1,7},{2,4},{3,5},{4,2},{5,3},{6,0},{7,1},{8,14},{9,15},{10,... | collective-permute-start | bytes 835592 | tf_op jit(solution)/shard_map/ppermute | solution.py:416
  24.0 13.6 %collective-permute-start.9 = (bf16[64,2176]{1,0:T(8,128)(2,1)S(1)}, bf16[64,2176]{1,0:T(8,128)(2,1)S(1)}, u32[]{:S(2)}, u32[]{:S(2)}) collective-permute-start(bf16[64,2176]{1,0:T(8,128)(2,1)S(1)} %pad_maximum_fusion), channel_id=1, source_target_pairs={{0,4},{1,5},{2,6},{3,7},{4,0},{5,1},{6,2},{7,3},{8,12},{9,13},{10,... | collective-permute-start | bytes 835592 | tf_op jit(solution)/shard_map/ppermute | solution.py:416
  24.5 13.1 %collective-permute-start.8 = (bf16[64,2176]{1,0:T(8,128)(2,1)S(1)}, bf16[64,2176]{1,0:T(8,128)(2,1)S(1)}, u32[]{:S(2)}, u32[]{:S(2)}) collective-permute-start(bf16[64,2176]{1,0:T(8,128)(2,1)S(1)} %pad_maximum_fusion), channel_id=1, source_target_pairs={{0,2},{1,3},{2,0},{3,1},{4,6},{5,7},{6,4},{7,5},{8,10},{9,11},{10,... | collective-permute-start | bytes 835592 | tf_op jit(solution)/shard_map/ppermute | solution.py:416
  34.0 8.3 %collective-permute-start.11 = (bf16[32,2048]{1,0:T(8,128)(2,1)S(1)}, bf16[32,2048]{1,0:T(8,128)(2,1)S(1)}, u32[]{:S(2)}, u32[]{:S(2)}) collective-permute-start(bf16[32,2048]{1,0:T(8,128)(2,1)S(1)} %get-tuple-element.68), channel_id=1, source_target_pairs={{0,2},{1,3},{2,0},{3,1},{4,6},{5,7},{6,4},{7,5},{8,10},{9,11},{10,... | collective-permute-start | bytes 393224 | tf_op jit(solution)/shard_map/ppermute | solution.py:416
  35.6 6.7 %collective-permute-start.12 = (bf16[32,2048]{1,0:T(8,128)(2,1)S(1)}, bf16[32,2048]{1,0:T(8,128)(2,1)S(1)}, u32[]{:S(2)}, u32[]{:S(2)}) collective-permute-start(bf16[32,2048]{1,0:T(8,128)(2,1)S(1)} %get-tuple-element.69), channel_id=1, source_target_pairs={{0,4},{1,5},{2,6},{3,7},{4,0},{5,1},{6,2},{7,3},{8,12},{9,13},{10,... | collective-permute-start | bytes 393224 | tf_op jit(solution)/shard_map/ppermute | solution.py:416
  37.1 5.9 %collective-permute-start.13 = (bf16[32,2048]{1,0:T(8,128)(2,1)S(1)}, bf16[32,2048]{1,0:T(8,128)(2,1)S(1)}, u32[]{:S(2)}, u32[]{:S(2)}) collective-permute-start(bf16[32,2048]{1,0:T(8,128)(2,1)S(1)} %get-tuple-element.70), channel_id=1, source_target_pairs={{0,6},{1,7},{2,4},{3,5},{4,2},{5,3},{6,0},{7,1},{8,14},{9,15},{10,... | collective-permute-start | bytes 393224 | tf_op jit(solution)/shard_map/ppermute | solution.py:416
  43.0 6.6 %collective-permute-start.14 = (bf16[32,2176]{1,0:T(8,128)(2,1)S(1)}, bf16[32,2176]{1,0:T(8,128)(2,1)S(1)}, u32[]{:S(2)}, u32[]{:S(2)}) collective-permute-start(bf16[32,2176]{1,0:T(8,128)(2,1)S(1)} %get-tuple-element.71), channel_id=1, source_target_pairs={{0,6},{1,7},{2,4},{3,5},{4,2},{5,3},{6,0},{7,1},{8,14},{9,15},{10,... | collective-permute-start | bytes 417800 | tf_op jit(solution)/shard_map/ppermute | solution.py:416
  44.9 6.0 %collective-permute-start.16 = (bf16[32,2176]{1,0:T(8,128)(2,1)S(1)}, bf16[32,2176]{1,0:T(8,128)(2,1)S(1)}, u32[]{:S(2)}, u32[]{:S(2)}) collective-permute-start(bf16[32,2176]{1,0:T(8,128)(2,1)S(1)} %get-tuple-element.78), channel_id=1, source_target_pairs={{0,2},{1,3},{2,0},{3,1},{4,6},{5,7},{6,4},{7,5},{8,10},{9,11},{10,... | collective-permute-start | bytes 417800 | tf_op jit(solution)/shard_map/ppermute | solution.py:416
  45.6 5.3 %collective-permute-start.17 = (bf16[32,2176]{1,0:T(8,128)(2,1)S(1)}, bf16[32,2176]{1,0:T(8,128)(2,1)S(1)}, u32[]{:S(2)}, u32[]{:S(2)}) collective-permute-start(bf16[32,2176]{1,0:T(8,128)(2,1)S(1)} %get-tuple-element.79), channel_id=1, source_target_pairs={{0,4},{1,5},{2,6},{3,7},{4,0},{5,1},{6,2},{7,3},{8,12},{9,13},{10,... | collective-permute-start | bytes 417800 | tf_op jit(solution)/shard_map/ppermute | solution.py:416
  47.1 7.9 %collective-permute-start.22 = (bf16[32,2048]{1,0:T(8,128)(2,1)S(1)}, bf16[32,2048]{1,0:T(8,128)(2,1)S(1)}, u32[]{:S(2)}, u32[]{:S(2)}) collective-permute-start(bf16[32,2048]{1,0:T(8,128)(2,1)S(1)} %get-tuple-element.87), channel_id=1, source_target_pairs={{0,2},{1,3},{2,0},{3,1},{4,6},{5,7},{6,4},{7,5},{8,10},{9,11},{10,... | collective-permute-start | bytes 393224 | tf_op jit(solution)/shard_map/ppermute | solution.py:416
  48.3 8.1 %collective-permute-start.23 = (bf16[32,2048]{1,0:T(8,128)(2,1)S(1)}, bf16[32,2048]{1,0:T(8,128)(2,1)S(1)}, u32[]{:S(2)}, u32[]{:S(2)}) collective-permute-start(bf16[32,2048]{1,0:T(8,128)(2,1)S(1)} %get-tuple-element.88), channel_id=1, source_target_pairs={{0,4},{1,5},{2,6},{3,7},{4,0},{5,1},{6,2},{7,3},{8,12},{9,13},{10,... | collective-permute-start | bytes 393224 | tf_op jit(solution)/shard_map/ppermute | solution.py:416
  49.6 7.4 %collective-permute-start.24 = (bf16[32,2048]{1,0:T(8,128)(2,1)S(1)}, bf16[32,2048]{1,0:T(8,128)(2,1)S(1)}, u32[]{:S(2)}, u32[]{:S(2)}) collective-permute-start(bf16[32,2048]{1,0:T(8,128)(2,1)S(1)} %get-tuple-element.89), channel_id=1, source_target_pairs={{0,6},{1,7},{2,4},{3,5},{4,2},{5,3},{6,0},{7,1},{8,14},{9,15},{10,... | collective-permute-start | bytes 393224 | tf_op jit(solution)/shard_map/ppermute | solution.py:416
  51.1 9.3 %collective-permute-start.18 = (bf16[32,2048]{1,0:T(8,128)(2,1)S(1)}, bf16[32,2048]{1,0:T(8,128)(2,1)S(1)}, u32[]{:S(2)}, u32[]{:S(2)}) collective-permute-start(bf16[32,2048]{1,0:T(8,128)(2,1)S(1)} %get-tuple-element.82), channel_id=1, source_target_pairs={{0,2},{1,3},{2,0},{3,1},{4,6},{5,7},{6,4},{7,5},{8,10},{9,11},{10,... | collective-permute-start | bytes 393224 | tf_op jit(solution)/shard_map/ppermute | solution.py:416
  52.3 14.2 %collective-permute-start.21 = (bf16[32,2176]{1,0:T(8,128)(2,1)S(1)}, bf16[32,2176]{1,0:T(8,128)(2,1)S(1)}, u32[]{:S(2)}, u32[]{:S(2)}) collective-permute-start(bf16[32,2176]{1,0:T(8,128)(2,1)S(1)} %get-tuple-element.81), channel_id=1, source_target_pairs={{0,24},{8,16},{16,8},{24,0},{1,25},{9,17},{17,9},{25,1},{2,26},{10... | collective-permute-start | bytes 417800 | tf_op jit(solution)/shard_map/ppermute | solution.py:419
  55.0 11.4 %collective-permute-start.26 = (bf16[32,2176]{1,0:T(8,128)(2,1)S(1)}, bf16[32,2176]{1,0:T(8,128)(2,1)S(1)}, u32[]{:S(2)}, u32[]{:S(2)}) collective-permute-start(bf16[32,2176]{1,0:T(8,128)(2,1)S(1)} %combine.7), channel_id=1, source_target_pairs={{0,8},{8,0},{16,24},{24,16},{1,9},{9,1},{17,25},{25,17},{2,10},{10... | collective-permute-start | bytes 417800 | tf_op jit(solution)/shard_map/ppermute | solution.py:419
  57.1 9.3 %collective-permute-start.25 = (bf16[32,2176]{1,0:T(8,128)(2,1)S(1)}, bf16[32,2176]{1,0:T(8,128)(2,1)S(1)}, u32[]{:S(2)}, u32[]{:S(2)}) collective-permute-start(bf16[32,2176]{1,0:T(8,128)(2,1)S(1)} %combine.6), channel_id=1, source_target_pairs={{0,16},{8,24},{16,0},{24,8},{1,17},{9,25},{17,1},{25,9},{2,18},{10... | collective-permute-start | bytes 417800 | tf_op jit(solution)/shard_map/ppermute | solution.py:419
  58.3 6.4 %collective-permute-start.19 = (bf16[32,2048]{1,0:T(8,128)(2,1)S(1)}, bf16[32,2048]{1,0:T(8,128)(2,1)S(1)}, u32[]{:S(2)}, u32[]{:S(2)}) collective-permute-start(bf16[32,2048]{1,0:T(8,128)(2,1)S(1)} %get-tuple-element.83), channel_id=1, source_target_pairs={{0,4},{1,5},{2,6},{3,7},{4,0},{5,1},{6,2},{7,3},{8,12},{9,13},{10,... | collective-permute-start | bytes 393224 | tf_op jit(solution)/shard_map/ppermute | solution.py:416
  60.4 5.9 %collective-permute-start.20 = (bf16[32,2048]{1,0:T(8,128)(2,1)S(1)}, bf16[32,2048]{1,0:T(8,128)(2,1)S(1)}, u32[]{:S(2)}, u32[]{:S(2)}) collective-permute-start(bf16[32,2048]{1,0:T(8,128)(2,1)S(1)} %get-tuple-element.84), channel_id=1, source_target_pairs={{0,6},{1,7},{2,4},{3,5},{4,2},{5,3},{6,0},{7,1},{8,14},{9,15},{10,... | collective-permute-start | bytes 393224 | tf_op jit(solution)/shard_map/ppermute | solution.py:416
  66.5 7.4 %collective-permute-start.29 = (bf16[32,2176]{1,0:T(8,128)(2,1)S(1)}, bf16[32,2176]{1,0:T(8,128)(2,1)S(1)}, u32[]{:S(2)}, u32[]{:S(2)}) collective-permute-start(bf16[32,2176]{1,0:T(8,128)(2,1)S(1)} %finish.1.refs_0_), channel_id=1, source_target_pairs={{0,6},{1,7},{2,4},{3,5},{4,2},{5,3},{6,0},{7,1},{8,14},{9,15},{10,... | collective-permute-start | bytes 417800 | tf_op jit(solution)/shard_map/ppermute | solution.py:416
  68.0 7.2 %collective-permute-start.28 = (bf16[32,2176]{1,0:T(8,128)(2,1)S(1)}, bf16[32,2176]{1,0:T(8,128)(2,1)S(1)}, u32[]{:S(2)}, u32[]{:S(2)}) collective-permute-start(bf16[32,2176]{1,0:T(8,128)(2,1)S(1)} %finish.1.refs_0_), channel_id=1, source_target_pairs={{0,4},{1,5},{2,6},{3,7},{4,0},{5,1},{6,2},{7,3},{8,12},{9,13},{10,... | collective-permute-start | bytes 417800 | tf_op jit(solution)/shard_map/ppermute | solution.py:416
  69.3 6.0 %collective-permute-start.27 = (bf16[32,2176]{1,0:T(8,128)(2,1)S(1)}, bf16[32,2176]{1,0:T(8,128)(2,1)S(1)}, u32[]{:S(2)}, u32[]{:S(2)}) collective-permute-start(bf16[32,2176]{1,0:T(8,128)(2,1)S(1)} %finish.1.refs_0_), channel_id=1, source_target_pairs={{0,2},{1,3},{2,0},{3,1},{4,6},{5,7},{6,4},{7,5},{8,10},{9,11},{10,... | collective-permute-start | bytes 417800 | tf_op jit(solution)/shard_map/ppermute | solution.py:416
  70.1 5.7 %collective-permute-start.30 = (bf16[32,2176]{1,0:T(8,128)(2,1)S(1)}, bf16[32,2176]{1,0:T(8,128)(2,1)S(1)}, u32[]{:S(2)}, u32[]{:S(2)}) collective-permute-start(bf16[32,2176]{1,0:T(8,128)(2,1)S(1)} %finish.1.refs_0_), channel_id=1, source_target_pairs={{0,1},{1,0},{2,3},{3,2},{4,5},{5,4},{6,7},{7,6},{8,9},{9,8},{10,11... | collective-permute-start | bytes 417800 | tf_op jit(solution)/shard_map/ppermute | solution.py:416
  73.9 1.9 %collective-permute-start.33 = (bf16[32,2176]{1,0:T(8,128)(2,1)S(1)}, bf16[32,2176]{1,0:T(8,128)(2,1)S(1)}, u32[]{:S(2)}, u32[]{:S(2)}) collective-permute-start(bf16[32,2176]{1,0:T(8,128)(2,1)S(1)} %collective-permute-done.29.refs_3_), channel_id=1, source_target_pairs={{0,1},{1,0},{2,3},{3,2},{4,5},{5,4},{6,7},{7,6},{8,9},{9,8},{10,11... | collective-permute-start | bytes 417800 | tf_op jit(solution)/shard_map/ppermute | solution.py:416
  75.3 1.6 %collective-permute-start.31 = (bf16[32,2176]{1,0:T(8,128)(2,1)S(1)}, bf16[32,2176]{1,0:T(8,128)(2,1)S(1)}, u32[]{:S(2)}, u32[]{:S(2)}) collective-permute-start(bf16[32,2176]{1,0:T(8,128)(2,1)S(1)} %collective-permute-done.27.refs_1_), channel_id=1, source_target_pairs={{0,1},{1,0},{2,3},{3,2},{4,5},{5,4},{6,7},{7,6},{8,9},{9,8},{10,11... | collective-permute-start | bytes 417800 | tf_op jit(solution)/shard_map/ppermute | solution.py:416
  (8 other events, 39.6 us)

commit v16 on v15

--- a/solution.py
+++ b/solution.py
@@ -589,7 +589,10 @@
         homeward.append(to_plane(result[0], hop))
         if hop == min(3, dp_count - 1):
             gate = result[0]
-    outs[0][1:], gate = lax.optimization_barrier((outs[0][1:], gate))
+        if hop == min(2, dp_count - 1):
+            near_gate = result[0]
+    outs[0][-1], gate = lax.optimization_barrier((outs[0][-1], gate))
+    outs[0][1:-1], near_gate = lax.optimization_barrier((outs[0][1:-1], near_gate))
     send_back(0, 0, [])
     near_sum = combine(0, returned[0], last_sum)[0]
 

time: 81.3 us -> 82.3 us (1.012)
  the two profiles are of different devices: /device:TPU:0 before, /device:TPU:13 now
where the time goes in v16:
time: 82.3 us; the launch traced here: 82 us
  starting transfers between devices  44.8 us (54%)
  Pallas kernels  16.3 us (20%)
  waiting for transfers between devices  14.8 us (18%)
  local copies, waits for them, and re-layouts  5.26 us (6%)
    ppermute x28, starting transfers between devices, to_lane(): lax.ppermute(value, 'expert', [(j, j ^ step) for j in range(expert_count)])  34.3 us
    ppermute x6, starting transfers between devices, to_plane(): return lax.ppermute(value, 'dp', [(p, p ^ step) for p in range(dp_count)])  10.5 us
    pallas_call x2, Pallas kernels, expert(): pl.pallas_call(functools.partial(expert_kernel, layout), out_shape=out_sh...  9.17 us
    ppermute x28, waiting for transfers between devices, to_lane(): lax.ppermute(value, 'expert', [(j, j ^ step) for j in range(expert_count)])  8.29 us
    ppermute x6, waiting for transfers between devices, to_plane(): return lax.ppermute(value, 'dp', [(p, p ^ step) for p in range(dp_count)])  6.5 us
    unnamed x12, local copies, waits for them, and re-layouts  4.53 us
    pallas_call x1, Pallas kernels, body(): pl.pallas_call(functools.partial(final_kernel, len(pieces), n_blocks), ou...  4.12 us
    pallas_call x1, Pallas kernels, body(): pl.pallas_call(functools.partial(pack_kernel, seq_dev), out_shape=jax.Sha...  1.66 us
  transfers between devices with their start and end apart: 34, of which 11 were waited for; matrix products, arithmetic and copies ran while one was open for 1% of the time, Pallas kernels for 15%

profile of v16, /device:TPU:13, one launch (start us, length us, event | category | flops | bytes accessed | tf_op | source)
XLA Modules:
  0.0 82.0 jit_solution(3197759706311011905)
XLA Ops:
  1.5 1.7 %pack.1.refs_0_ = bf16[32,2176]{1,0:T(8,128)(2,1)} custom-call(s32[4]{0:T(128)} %partners.1, s32[1,256]{1,0:T(1,128)} %bitcast.2, f32[1,256]{1,0:T(1,128)} %bitcast.3, bf16[256,2048]{1,0:T(8,128)(2,1)} %refs_0_.1), custom_call_target="tpu_custom_call" | custom-call | bytes 524288 | tf_op jit(solution)/shard_map/pack/pallas_call | solution.py:425
  3.4 2.4 %collective-permute-start.2 = (bf16[32,2176]{1,0:T(8,128)(2,1)}, bf16[32,2176]{1,0:T(8,128)(2,1)S(1)}, u32[]{:S(2)}, u32[]{:S(2)}) collective-permute-start(bf16[32,2176]{1,0:T(8,128)(2,1)} %pack.1.refs_0_), channel_id=1, source_target_pairs={{0,24},{8,16},{16,8},{24,0},{1,25},{9,17},{17,9},{25,1},{2,26},{10... | collective-permute-start | bytes 417800 | tf_op jit(solution)/shard_map/ppermute | solution.py:419
  5.8 1.0 %collective-permute-start.1 = (bf16[32,2176]{1,0:T(8,128)(2,1)}, bf16[32,2176]{1,0:T(8,128)(2,1)S(1)}, u32[]{:S(2)}, u32[]{:S(2)}) collective-permute-start(bf16[32,2176]{1,0:T(8,128)(2,1)} %pack.1.refs_0_), channel_id=1, source_target_pairs={{0,16},{8,24},{16,0},{24,8},{1,17},{9,25},{17,1},{25,9},{2,18},{10... | collective-permute-start | bytes 417800 | tf_op jit(solution)/shard_map/ppermute | solution.py:419
  9.1 1.2 %collective-permute-start.7 = (bf16[32,2304]{1,0:T(8,128)(2,1)S(1)}, bf16[32,2304]{1,0:T(8,128)(2,1)S(1)}, u32[]{:S(2)}, u32[]{:S(2)}) collective-permute-start(bf16[32,2304]{1,0:T(8,128)(2,1)S(1)} %pad_maximum_fusion.1), channel_id=1, source_target_pairs={{0,6},{1,7},{2,4},{3,5},{4,2},{5,3},{6,0},{7,1},{8,14},{9,15},{10,... | collective-permute-start | bytes 442376 | tf_op jit(solution)/shard_map/ppermute | solution.py:416
  10.3 1.2 %collective-permute-start.6 = (bf16[32,2304]{1,0:T(8,128)(2,1)S(1)}, bf16[32,2304]{1,0:T(8,128)(2,1)S(1)}, u32[]{:S(2)}, u32[]{:S(2)}) collective-permute-start(bf16[32,2304]{1,0:T(8,128)(2,1)S(1)} %pad_maximum_fusion.1), channel_id=1, source_target_pairs={{0,4},{1,5},{2,6},{3,7},{4,0},{5,1},{6,2},{7,3},{8,12},{9,13},{10,... | collective-permute-start | bytes 442376 | tf_op jit(solution)/shard_map/ppermute | solution.py:416
  11.8 5.7 %collective-permute-done.1.refs_5_ = bf16[32,2176]{1,0:T(8,128)(2,1)S(1)} collective-permute-done((bf16[32,2176]{1,0:T(8,128)(2,1)}, bf16[32,2176]{1,0:T(8,128)(2,1)S(1)}, u32[]{:S(2)}, u32[]{:S(2)}) %collective-permute-start.1) | collective-permute-done | bytes 139296 | tf_op jit(solution)/shard_map/ppermute | solution.py:419
  17.6 1.0 %collective-permute-done.6.refs_3_ = bf16[32,2304]{1,0:T(8,128)(2,1)S(1)} collective-permute-done((bf16[32,2304]{1,0:T(8,128)(2,1)S(1)}, bf16[32,2304]{1,0:T(8,128)(2,1)S(1)}, u32[]{:S(2)}, u32[]{:S(2)}) %collective-permute-start.6) | collective-permute-done | bytes 147488 | tf_op jit(solution)/shard_map/ppermute | solution.py:416
  18.6 1.1 %collective-permute-start.10 = (bf16[64,2176]{1,0:T(8,128)(2,1)S(1)}, bf16[64,2176]{1,0:T(8,128)(2,1)S(1)}, u32[]{:S(2)}, u32[]{:S(2)}) collective-permute-start(bf16[64,2176]{1,0:T(8,128)(2,1)S(1)} %pad_maximum_fusion), channel_id=1, source_target_pairs={{0,6},{1,7},{2,4},{3,5},{4,2},{5,3},{6,0},{7,1},{8,14},{9,15},{10,... | collective-permute-start | bytes 835592 | tf_op jit(solution)/shard_map/ppermute | solution.py:416
  20.0 1.2 %collective-permute-start.8 = (bf16[64,2176]{1,0:T(8,128)(2,1)S(1)}, bf16[64,2176]{1,0:T(8,128)(2,1)S(1)}, u32[]{:S(2)}, u32[]{:S(2)}) collective-permute-start(bf16[64,2176]{1,0:T(8,128)(2,1)S(1)} %pad_maximum_fusion), channel_id=1, source_target_pairs={{0,2},{1,3},{2,0},{3,1},{4,6},{5,7},{6,4},{7,5},{8,10},{9,11},{10,... | collective-permute-start | bytes 835592 | tf_op jit(solution)/shard_map/ppermute | solution.py:416
  21.2 1.4 %copy-done = bf16[1,384,2048]{2,1,0:T(8,128)(2,1)S(1)} copy-done((bf16[1,384,2048]{2,1,0:T(8,128)(2,1)S(1)}, bf16[1,384,2048]{2,1,0:T(8,128)(2,1)}, u32[]{:S(2)}) %copy-start) | copy-done | bytes 1572888
  22.7 1.9 %copy-done.2 = bf16[1,2048,768]{2,1,0:T(8,128)(2,1)S(1)} copy-done((bf16[1,2048,768]{2,1,0:T(8,128)(2,1)S(1)}, bf16[1,2048,768]{2,1,0:T(8,128)(2,1)}, u32[]{:S(2)}) %copy-start.2) | copy-done | bytes 3145752
  24.5 1.2 %copy-done.4 = bf16[256,2048]{1,0:T(8,128)(2,1)S(1)} copy-done((bf16[256,2048]{1,0:T(8,128)(2,1)S(1)}, bf16[256,2048]{1,0:T(8,128)(2,1)}, u32[]{:S(2)}) %copy-start.4) | copy-done | bytes 1048600
  25.8 4.5 %experts.2 = (bf16[32,2048]{1,0:T(8,128)(2,1)S(1)}, bf16[32,2048]{1,0:T(8,128)(2,1)S(1)}, bf16[32,2048]{1,0:T(8,128)(2,1)S(1)}, bf16[32,2048]{1,0:T(8,128)(2,1)S...) custom-call(bf16[256,2048]{1,0:T(8,128)(2,1)S(1)} %copy-done.4, ...), custom_call_target="tpu_custom_call" | custom-call | flops 2415919104 | bytes 12582912 | tf_op jit(solution)/shard_map/experts/pallas_call | solution.py:502
  30.6 1.2 %collective-permute-start.12 = (bf16[32,2048]{1,0:T(8,128)(2,1)S(1)}, bf16[32,2048]{1,0:T(8,128)(2,1)S(1)}, u32[]{:S(2)}, u32[]{:S(2)}) collective-permute-start(bf16[32,2048]{1,0:T(8,128)(2,1)S(1)} %get-tuple-element.69), channel_id=1, source_target_pairs={{0,4},{1,5},{2,6},{3,7},{4,0},{5,1},{6,2},{7,3},{8,12},{9,13},{10,... | collective-permute-start | bytes 393224 | tf_op jit(solution)/shard_map/ppermute | solution.py:416
  31.8 1.2 %collective-permute-start.13 = (bf16[32,2048]{1,0:T(8,128)(2,1)S(1)}, bf16[32,2048]{1,0:T(8,128)(2,1)S(1)}, u32[]{:S(2)}, u32[]{:S(2)}) collective-permute-start(bf16[32,2048]{1,0:T(8,128)(2,1)S(1)} %get-tuple-element.70), channel_id=1, source_target_pairs={{0,6},{1,7},{2,4},{3,5},{4,2},{5,3},{6,0},{7,1},{8,14},{9,15},{10,... | collective-permute-start | bytes 393224 | tf_op jit(solution)/shard_map/ppermute | solution.py:416
  33.0 1.0 %collective-permute-done.9.refs_8_ = bf16[64,2176]{1,0:T(8,128)(2,1)S(1)} collective-permute-done((bf16[64,2176]{1,0:T(8,128)(2,1)S(1)}, bf16[64,2176]{1,0:T(8,128)(2,1)S(1)}, u32[]{:S(2)}, u32[]{:S(2)}) %collective-permute-start.9) | collective-permute-done | bytes 278560 | tf_op jit(solution)/shard_map/ppermute | solution.py:416
  34.1 4.7 %experts.3 = (bf16[32,2048]{1,0:T(8,128)(2,1)S(1)}, bf16[32,2048]{1,0:T(8,128)(2,1)S(1)}, bf16[32,2048]{1,0:T(8,128)(2,1)S(1)}, bf16[32,2048]{1,0:T(8,128)(2,1)S...) custom-call(bf16[32,2176]{1,0:T(8,128)(2,1)S(1)} %copy-done.5, ...), custom_call_target="tpu_custom_call" | custom-call | flops 2566914048 | bytes 12582912 | tf_op jit(solution)/shard_map/experts/pallas_call | solution.py:502
  38.8 1.2 %collective-permute-start.14 = (bf16[32,2176]{1,0:T(8,128)(2,1)S(1)}, bf16[32,2176]{1,0:T(8,128)(2,1)S(1)}, u32[]{:S(2)}, u32[]{:S(2)}) collective-permute-start(bf16[32,2176]{1,0:T(8,128)(2,1)S(1)} %get-tuple-element.71), channel_id=1, source_target_pairs={{0,6},{1,7},{2,4},{3,5},{4,2},{5,3},{6,0},{7,1},{8,14},{9,15},{10,... | collective-permute-start | bytes 417800 | tf_op jit(solution)/shard_map/ppermute | solution.py:416
  40.1 1.3 %collective-permute-start.17 = (bf16[32,2176]{1,0:T(8,128)(2,1)S(1)}, bf16[32,2176]{1,0:T(8,128)(2,1)S(1)}, u32[]{:S(2)}, u32[]{:S(2)}) collective-permute-start(bf16[32,2176]{1,0:T(8,128)(2,1)S(1)} %get-tuple-element.78), channel_id=1, source_target_pairs={{0,4},{1,5},{2,6},{3,7},{4,0},{5,1},{6,2},{7,3},{8,12},{9,13},{10,... | collective-permute-start | bytes 417800 | tf_op jit(solution)/shard_map/ppermute | solution.py:416
  42.0 2.7 %collective-permute-start.15 = (bf16[144,128]{1,0:T(8,128)(2,1)S(1)}, bf16[144,128]{1,0:T(8,128)(2,1)S(1)}, u32[]{:S(2)}, u32[]{:S(2)}) collective-permute-start(bf16[144,128]{1,0:T(8,128)(2,1)S(1)} %get-tuple-element.72), channel_id=1, source_target_pairs={{0,1},{1,0},{2,3},{3,2},{4,5},{5,4},{6,7},{7,6},{8,9},{9,8},{10,11... | collective-permute-start | bytes 110600 | tf_op jit(solution)/shard_map/ppermute | solution.py:416
  46.0 1.4 %collective-permute-start.20 = (bf16[32,2048]{1,0:T(8,128)(2,1)S(1)}, bf16[32,2048]{1,0:T(8,128)(2,1)S(1)}, u32[]{:S(2)}, u32[]{:S(2)}) collective-permute-start(bf16[32,2048]{1,0:T(8,128)(2,1)S(1)} %get-tuple-element.83), channel_id=1, source_target_pairs={{0,6},{1,7},{2,4},{3,5},{4,2},{5,3},{6,0},{7,1},{8,14},{9,15},{10,... | collective-permute-start | bytes 393224 | tf_op jit(solution)/shard_map/ppermute | solution.py:416
  47.6 1.0 %collective-permute-start.23 = (bf16[32,2048]{1,0:T(8,128)(2,1)S(1)}, bf16[32,2048]{1,0:T(8,128)(2,1)S(1)}, u32[]{:S(2)}, u32[]{:S(2)}) collective-permute-start(bf16[32,2048]{1,0:T(8,128)(2,1)S(1)} %get-tuple-element.88), channel_id=1, source_target_pairs={{0,6},{1,7},{2,4},{3,5},{4,2},{5,3},{6,0},{7,1},{8,14},{9,15},{10,... | collective-permute-start | bytes 393224 | tf_op jit(solution)/shard_map/ppermute | solution.py:416
  48.6 1.3 %collective-permute-start.24 = (bf16[32,2176]{1,0:T(8,128)(2,1)S(1)}, bf16[32,2176]{1,0:T(8,128)(2,1)S(1)}, u32[]{:S(2)}, u32[]{:S(2)}) collective-permute-start(bf16[32,2176]{1,0:T(8,128)(2,1)S(1)} %get-tuple-element.87), channel_id=1, source_target_pairs={{0,24},{8,16},{16,8},{24,0},{1,25},{9,17},{17,9},{25,1},{2,26},{10... | collective-permute-start | bytes 417800 | tf_op jit(solution)/shard_map/ppermute | solution.py:419
  50.1 2.7 %collective-permute-start.26 = (bf16[32,2176]{1,0:T(8,128)(2,1)S(1)}, bf16[32,2176]{1,0:T(8,128)(2,1)S(1)}, u32[]{:S(2)}, u32[]{:S(2)}) collective-permute-start(bf16[32,2176]{1,0:T(8,128)(2,1)S(1)} %combine.7), channel_id=1, source_target_pairs={{0,8},{8,0},{16,24},{24,16},{1,9},{9,1},{17,25},{25,17},{2,10},{10... | collective-permute-start | bytes 417800 | tf_op jit(solution)/shard_map/ppermute | solution.py:419
  53.2 2.9 %collective-permute-start.25 = (bf16[32,2176]{1,0:T(8,128)(2,1)S(1)}, bf16[32,2176]{1,0:T(8,128)(2,1)S(1)}, u32[]{:S(2)}, u32[]{:S(2)}) collective-permute-start(bf16[32,2176]{1,0:T(8,128)(2,1)S(1)} %combine.5), channel_id=1, source_target_pairs={{0,16},{8,24},{16,0},{24,8},{1,17},{9,25},{17,1},{25,9},{2,18},{10... | collective-permute-start | bytes 417800 | tf_op jit(solution)/shard_map/ppermute | solution.py:419
  57.5 2.7 %collective-permute-done.21.refs_2_ = bf16[32,2048]{1,0:T(8,128)(2,1)S(1)} collective-permute-done((bf16[32,2048]{1,0:T(8,128)(2,1)S(1)}, bf16[32,2048]{1,0:T(8,128)(2,1)S(1)}, u32[]{:S(2)}, u32[]{:S(2)}) %collective-permute-start.21) | collective-permute-done | bytes 131104 | tf_op jit(solution)/shard_map/ppermute | solution.py:416
  61.3 1.1 %collective-permute-start.29 = (bf16[32,2176]{1,0:T(8,128)(2,1)S(1)}, bf16[32,2176]{1,0:T(8,128)(2,1)S(1)}, u32[]{:S(2)}, u32[]{:S(2)}) collective-permute-start(bf16[32,2176]{1,0:T(8,128)(2,1)S(1)} %finish.1.refs_0_), channel_id=1, source_target_pairs={{0,6},{1,7},{2,4},{3,5},{4,2},{5,3},{6,0},{7,1},{8,14},{9,15},{10,... | collective-permute-start | bytes 417800 | tf_op jit(solution)/shard_map/ppermute | solution.py:416
  64.0 8.8 %collective-permute-start.30 = (bf16[32,2176]{1,0:T(8,128)(2,1)S(1)}, bf16[32,2176]{1,0:T(8,128)(2,1)S(1)}, u32[]{:S(2)}, u32[]{:S(2)}) collective-permute-start(bf16[32,2176]{1,0:T(8,128)(2,1)S(1)} %finish.1.refs_0_), channel_id=1, source_target_pairs={{0,1},{1,0},{2,3},{3,2},{4,5},{5,4},{6,7},{7,6},{8,9},{9,8},{10,11... | collective-permute-start | bytes 417800 | tf_op jit(solution)/shard_map/ppermute | solution.py:416
  72.8 2.6 %collective-permute-start.33 = (bf16[32,2176]{1,0:T(8,128)(2,1)S(1)}, bf16[32,2176]{1,0:T(8,128)(2,1)S(1)}, u32[]{:S(2)}, u32[]{:S(2)}) collective-permute-start(bf16[32,2176]{1,0:T(8,128)(2,1)S(1)} %collective-permute-done.29.refs_3_), channel_id=1, source_target_pairs={{0,1},{1,0},{2,3},{3,2},{4,5},{5,4},{6,7},{7,6},{8,9},{9,8},{10,11... | collective-permute-start | bytes 417800 | tf_op jit(solution)/shard_map/ppermute | solution.py:416
  75.4 1.1 %collective-permute-start.32 = (bf16[32,2176]{1,0:T(8,128)(2,1)S(1)}, bf16[32,2176]{1,0:T(8,128)(2,1)S(1)}, u32[]{:S(2)}, u32[]{:S(2)}) collective-permute-start(bf16[32,2176]{1,0:T(8,128)(2,1)S(1)} %collective-permute-done.28.refs_2_), channel_id=1, source_target_pairs={{0,1},{1,0},{2,3},{3,2},{4,5},{5,4},{6,7},{7,6},{8,9},{9,8},{10,11... | collective-permute-start | bytes 417800 | tf_op jit(solution)/shard_map/ppermute | solution.py:416
  76.6 0.9 %collective-permute-done.32.refs_6_ = bf16[32,2176]{1,0:T(8,128)(2,1)S(1)} collective-permute-done((bf16[32,2176]{1,0:T(8,128)(2,1)S(1)}, bf16[32,2176]{1,0:T(8,128)(2,1)S(1)}, u32[]{:S(2)}, u32[]{:S(2)}) %collective-permute-start.32) | collective-permute-done | bytes 139296 | tf_op jit(solution)/shard_map/ppermute | solution.py:416
  77.9 4.1 %final.1 = (bf16[256,2048]{1,0:T(8,128)(2,1)}, bf16[1,2048,768]{2,1,0:T(8,128)(2,1)}, bf16[1,384,2048]{2,1,0:T(8,128)(2,1)}) custom-call(bf16[32,2176]{1,0:T(8,128)(2,1)S(1)} %finish.1.refs_0_, bf16[32,2176]{1,0:T(8,128)(2,1)S(1)} %collective-permute-done.27.refs_1_, bf16[32,2176]{1,0:T(8,128)(2,1)S(1)} %collective-permute-done.28.refs_2_, ...), custom_call_target="tpu_custom_call" | custom-call | flops 100663296 | bytes 7340032 | tf_op jit(solution)/shard_map/final/pallas_call | solution.py:612
  (61 shorter events, 11.8 us)
Async XLA Ops:
  0.6 8.5 %collective-permute-start.3 = (bf16[1,2048,768]{2,1,0:T(8,128)(2,1)}, bf16[1,2048,768]{2,1,0:T(8,128)(2,1)S(1)}, u32[]{:S(2)}, u32[]{:S(2)}) collective-permute-start(bf16[1,2048,768]{2,1,0:T(8,128)(2,1)} %refs_10_), channel_id=1, source_target_pairs={{0,1},{1,0},{2,3},{3,2},{4,5},{5,4},{6,7},{7,6},{8,9},{9,8},{10,11... | collective-permute-start | bytes 9437192 | tf_op jit(solution)/shard_map/ppermute | solution.py:416
  1.4 7.7 %collective-permute-start.4 = (bf16[1,384,2048]{2,1,0:T(8,128)(2,1)}, bf16[1,384,2048]{2,1,0:T(8,128)(2,1)}, u32[]{:S(2)}, u32[]{:S(2)}) collective-permute-start(bf16[1,384,2048]{2,1,0:T(8,128)(2,1)} %refs_13_.1), channel_id=1, source_target_pairs={{0,1},{1,0},{2,3},{3,2},{4,5},{5,4},{6,7},{7,6},{8,9},{9,8},{10,11... | collective-permute-start | bytes 4718600 | tf_op jit(solution)/shard_map/ppermute | solution.py:416
  3.1 5.1 %collective-permute-start = (bf16[32,2176]{1,0:T(8,128)(2,1)}, bf16[32,2176]{1,0:T(8,128)(2,1)S(1)}, u32[]{:S(2)}, u32[]{:S(2)}) collective-permute-start(bf16[32,2176]{1,0:T(8,128)(2,1)} %pack.1.refs_0_), channel_id=1, source_target_pairs={{0,8},{8,0},{16,24},{24,16},{1,9},{9,1},{17,25},{25,17},{2,10},{10... | collective-permute-start | bytes 417800 | tf_op jit(solution)/shard_map/ppermute | solution.py:419
  3.4 8.4 %collective-permute-start.2 = (bf16[32,2176]{1,0:T(8,128)(2,1)}, bf16[32,2176]{1,0:T(8,128)(2,1)S(1)}, u32[]{:S(2)}, u32[]{:S(2)}) collective-permute-start(bf16[32,2176]{1,0:T(8,128)(2,1)} %pack.1.refs_0_), channel_id=1, source_target_pairs={{0,24},{8,16},{16,8},{24,0},{1,25},{9,17},{17,9},{25,1},{2,26},{10... | collective-permute-start | bytes 417800 | tf_op jit(solution)/shard_map/ppermute | solution.py:419
  5.8 11.7 %collective-permute-start.1 = (bf16[32,2176]{1,0:T(8,128)(2,1)}, bf16[32,2176]{1,0:T(8,128)(2,1)S(1)}, u32[]{:S(2)}, u32[]{:S(2)}) collective-permute-start(bf16[32,2176]{1,0:T(8,128)(2,1)} %pack.1.refs_0_), channel_id=1, source_target_pairs={{0,16},{8,24},{16,0},{24,8},{1,17},{9,25},{17,1},{25,9},{2,18},{10... | collective-permute-start | bytes 417800 | tf_op jit(solution)/shard_map/ppermute | solution.py:419
  9.1 8.4 %collective-permute-start.7 = (bf16[32,2304]{1,0:T(8,128)(2,1)S(1)}, bf16[32,2304]{1,0:T(8,128)(2,1)S(1)}, u32[]{:S(2)}, u32[]{:S(2)}) collective-permute-start(bf16[32,2304]{1,0:T(8,128)(2,1)S(1)} %pad_maximum_fusion.1), channel_id=1, source_target_pairs={{0,6},{1,7},{2,4},{3,5},{4,2},{5,3},{6,0},{7,1},{8,14},{9,15},{10,... | collective-permute-start | bytes 442376 | tf_op jit(solution)/shard_map/ppermute | solution.py:416
  10.3 8.3 %collective-permute-start.6 = (bf16[32,2304]{1,0:T(8,128)(2,1)S(1)}, bf16[32,2304]{1,0:T(8,128)(2,1)S(1)}, u32[]{:S(2)}, u32[]{:S(2)}) collective-permute-start(bf16[32,2304]{1,0:T(8,128)(2,1)S(1)} %pad_maximum_fusion.1), channel_id=1, source_target_pairs={{0,4},{1,5},{2,6},{3,7},{4,0},{5,1},{6,2},{7,3},{8,12},{9,13},{10,... | collective-permute-start | bytes 442376 | tf_op jit(solution)/shard_map/ppermute | solution.py:416
  11.5 7.1 %collective-permute-start.5 = (bf16[32,2304]{1,0:T(8,128)(2,1)S(1)}, bf16[32,2304]{1,0:T(8,128)(2,1)S(1)}, u32[]{:S(2)}, u32[]{:S(2)}) collective-permute-start(bf16[32,2304]{1,0:T(8,128)(2,1)S(1)} %pad_maximum_fusion.1), channel_id=1, source_target_pairs={{0,2},{1,3},{2,0},{3,1},{4,6},{5,7},{6,4},{7,5},{8,10},{9,11},{10,... | collective-permute-start | bytes 442376 | tf_op jit(solution)/shard_map/ppermute | solution.py:416
  18.6 13.2 %collective-permute-start.10 = (bf16[64,2176]{1,0:T(8,128)(2,1)S(1)}, bf16[64,2176]{1,0:T(8,128)(2,1)S(1)}, u32[]{:S(2)}, u32[]{:S(2)}) collective-permute-start(bf16[64,2176]{1,0:T(8,128)(2,1)S(1)} %pad_maximum_fusion), channel_id=1, source_target_pairs={{0,6},{1,7},{2,4},{3,5},{4,2},{5,3},{6,0},{7,1},{8,14},{9,15},{10,... | collective-permute-start | bytes 835592 | tf_op jit(solution)/shard_map/ppermute | solution.py:416
  19.7 14.3 %collective-permute-start.9 = (bf16[64,2176]{1,0:T(8,128)(2,1)S(1)}, bf16[64,2176]{1,0:T(8,128)(2,1)S(1)}, u32[]{:S(2)}, u32[]{:S(2)}) collective-permute-start(bf16[64,2176]{1,0:T(8,128)(2,1)S(1)} %pad_maximum_fusion), channel_id=1, source_target_pairs={{0,4},{1,5},{2,6},{3,7},{4,0},{5,1},{6,2},{7,3},{8,12},{9,13},{10,... | collective-permute-start | bytes 835592 | tf_op jit(solution)/shard_map/ppermute | solution.py:416
  20.0 14.0 %collective-permute-start.8 = (bf16[64,2176]{1,0:T(8,128)(2,1)S(1)}, bf16[64,2176]{1,0:T(8,128)(2,1)S(1)}, u32[]{:S(2)}, u32[]{:S(2)}) collective-permute-start(bf16[64,2176]{1,0:T(8,128)(2,1)S(1)} %pad_maximum_fusion), channel_id=1, source_target_pairs={{0,2},{1,3},{2,0},{3,1},{4,6},{5,7},{6,4},{7,5},{8,10},{9,11},{10,... | collective-permute-start | bytes 835592 | tf_op jit(solution)/shard_map/ppermute | solution.py:416
  30.3 8.4 %collective-permute-start.11 = (bf16[32,2048]{1,0:T(8,128)(2,1)S(1)}, bf16[32,2048]{1,0:T(8,128)(2,1)S(1)}, u32[]{:S(2)}, u32[]{:S(2)}) collective-permute-start(bf16[32,2048]{1,0:T(8,128)(2,1)S(1)} %get-tuple-element.68), channel_id=1, source_target_pairs={{0,2},{1,3},{2,0},{3,1},{4,6},{5,7},{6,4},{7,5},{8,10},{9,11},{10,... | collective-permute-start | bytes 393224 | tf_op jit(solution)/shard_map/ppermute | solution.py:416
  30.6 8.1 %collective-permute-start.12 = (bf16[32,2048]{1,0:T(8,128)(2,1)S(1)}, bf16[32,2048]{1,0:T(8,128)(2,1)S(1)}, u32[]{:S(2)}, u32[]{:S(2)}) collective-permute-start(bf16[32,2048]{1,0:T(8,128)(2,1)S(1)} %get-tuple-element.69), channel_id=1, source_target_pairs={{0,4},{1,5},{2,6},{3,7},{4,0},{5,1},{6,2},{7,3},{8,12},{9,13},{10,... | collective-permute-start | bytes 393224 | tf_op jit(solution)/shard_map/ppermute | solution.py:416
  31.8 7.0 %collective-permute-start.13 = (bf16[32,2048]{1,0:T(8,128)(2,1)S(1)}, bf16[32,2048]{1,0:T(8,128)(2,1)S(1)}, u32[]{:S(2)}, u32[]{:S(2)}) collective-permute-start(bf16[32,2048]{1,0:T(8,128)(2,1)S(1)} %get-tuple-element.70), channel_id=1, source_target_pairs={{0,6},{1,7},{2,4},{3,5},{4,2},{5,3},{6,0},{7,1},{8,14},{9,15},{10,... | collective-permute-start | bytes 393224 | tf_op jit(solution)/shard_map/ppermute | solution.py:416
  38.8 7.2 %collective-permute-start.14 = (bf16[32,2176]{1,0:T(8,128)(2,1)S(1)}, bf16[32,2176]{1,0:T(8,128)(2,1)S(1)}, u32[]{:S(2)}, u32[]{:S(2)}) collective-permute-start(bf16[32,2176]{1,0:T(8,128)(2,1)S(1)} %get-tuple-element.71), channel_id=1, source_target_pairs={{0,6},{1,7},{2,4},{3,5},{4,2},{5,3},{6,0},{7,1},{8,14},{9,15},{10,... | collective-permute-start | bytes 417800 | tf_op jit(solution)/shard_map/ppermute | solution.py:416
  40.0 7.5 %collective-permute-start.16 = (bf16[32,2176]{1,0:T(8,128)(2,1)S(1)}, bf16[32,2176]{1,0:T(8,128)(2,1)S(1)}, u32[]{:S(2)}, u32[]{:S(2)}) collective-permute-start(bf16[32,2176]{1,0:T(8,128)(2,1)S(1)} %get-tuple-element.77), channel_id=1, source_target_pairs={{0,2},{1,3},{2,0},{3,1},{4,6},{5,7},{6,4},{7,5},{8,10},{9,11},{10,... | collective-permute-start | bytes 417800 | tf_op jit(solution)/shard_map/ppermute | solution.py:416
  40.1 7.3 %collective-permute-start.17 = (bf16[32,2176]{1,0:T(8,128)(2,1)S(1)}, bf16[32,2176]{1,0:T(8,128)(2,1)S(1)}, u32[]{:S(2)}, u32[]{:S(2)}) collective-permute-start(bf16[32,2176]{1,0:T(8,128)(2,1)S(1)} %get-tuple-element.78), channel_id=1, source_target_pairs={{0,4},{1,5},{2,6},{3,7},{4,0},{5,1},{6,2},{7,3},{8,12},{9,13},{10,... | collective-permute-start | bytes 417800 | tf_op jit(solution)/shard_map/ppermute | solution.py:416
  42.0 3.6 %collective-permute-start.15 = (bf16[144,128]{1,0:T(8,128)(2,1)S(1)}, bf16[144,128]{1,0:T(8,128)(2,1)S(1)}, u32[]{:S(2)}, u32[]{:S(2)}) collective-permute-start(bf16[144,128]{1,0:T(8,128)(2,1)S(1)} %get-tuple-element.72), channel_id=1, source_target_pairs={{0,1},{1,0},{2,3},{3,2},{4,5},{5,4},{6,7},{7,6},{8,9},{9,8},{10,11... | collective-permute-start | bytes 110600 | tf_op jit(solution)/shard_map/ppermute | solution.py:416
  44.7 5.4 %collective-permute-start.18 = (bf16[32,2048]{1,0:T(8,128)(2,1)S(1)}, bf16[32,2048]{1,0:T(8,128)(2,1)S(1)}, u32[]{:S(2)}, u32[]{:S(2)}) collective-permute-start(bf16[32,2048]{1,0:T(8,128)(2,1)S(1)} %get-tuple-element.81), channel_id=1, source_target_pairs={{0,2},{1,3},{2,0},{3,1},{4,6},{5,7},{6,4},{7,5},{8,10},{9,11},{10,... | collective-permute-start | bytes 393224 | tf_op jit(solution)/shard_map/ppermute | solution.py:416
  45.6 7.2 %collective-permute-start.19 = (bf16[32,2048]{1,0:T(8,128)(2,1)S(1)}, bf16[32,2048]{1,0:T(8,128)(2,1)S(1)}, u32[]{:S(2)}, u32[]{:S(2)}) collective-permute-start(bf16[32,2048]{1,0:T(8,128)(2,1)S(1)} %get-tuple-element.82), channel_id=1, source_target_pairs={{0,4},{1,5},{2,6},{3,7},{4,0},{5,1},{6,2},{7,3},{8,12},{9,13},{10,... | collective-permute-start | bytes 393224 | tf_op jit(solution)/shard_map/ppermute | solution.py:416
  46.0 7.1 %collective-permute-start.20 = (bf16[32,2048]{1,0:T(8,128)(2,1)S(1)}, bf16[32,2048]{1,0:T(8,128)(2,1)S(1)}, u32[]{:S(2)}, u32[]{:S(2)}) collective-permute-start(bf16[32,2048]{1,0:T(8,128)(2,1)S(1)} %get-tuple-element.83), channel_id=1, source_target_pairs={{0,6},{1,7},{2,4},{3,5},{4,2},{5,3},{6,0},{7,1},{8,14},{9,15},{10,... | collective-permute-start | bytes 393224 | tf_op jit(solution)/shard_map/ppermute | solution.py:416
  47.6 9.3 %collective-permute-start.23 = (bf16[32,2048]{1,0:T(8,128)(2,1)S(1)}, bf16[32,2048]{1,0:T(8,128)(2,1)S(1)}, u32[]{:S(2)}, u32[]{:S(2)}) collective-permute-start(bf16[32,2048]{1,0:T(8,128)(2,1)S(1)} %get-tuple-element.88), channel_id=1, source_target_pairs={{0,6},{1,7},{2,4},{3,5},{4,2},{5,3},{6,0},{7,1},{8,14},{9,15},{10,... | collective-permute-start | bytes 393224 | tf_op jit(solution)/shard_map/ppermute | solution.py:416
  48.6 12.6 %collective-permute-start.24 = (bf16[32,2176]{1,0:T(8,128)(2,1)S(1)}, bf16[32,2176]{1,0:T(8,128)(2,1)S(1)}, u32[]{:S(2)}, u32[]{:S(2)}) collective-permute-start(bf16[32,2176]{1,0:T(8,128)(2,1)S(1)} %get-tuple-element.87), channel_id=1, source_target_pairs={{0,24},{8,16},{16,8},{24,0},{1,25},{9,17},{17,9},{25,1},{2,26},{10... | collective-permute-start | bytes 417800 | tf_op jit(solution)/shard_map/ppermute | solution.py:419
  50.1 11.1 %collective-permute-start.26 = (bf16[32,2176]{1,0:T(8,128)(2,1)S(1)}, bf16[32,2176]{1,0:T(8,128)(2,1)S(1)}, u32[]{:S(2)}, u32[]{:S(2)}) collective-permute-start(bf16[32,2176]{1,0:T(8,128)(2,1)S(1)} %combine.7), channel_id=1, source_target_pairs={{0,8},{8,0},{16,24},{24,16},{1,9},{9,1},{17,25},{25,17},{2,10},{10... | collective-permute-start | bytes 417800 | tf_op jit(solution)/shard_map/ppermute | solution.py:419
  53.2 8.0 %collective-permute-start.25 = (bf16[32,2176]{1,0:T(8,128)(2,1)S(1)}, bf16[32,2176]{1,0:T(8,128)(2,1)S(1)}, u32[]{:S(2)}, u32[]{:S(2)}) collective-permute-start(bf16[32,2176]{1,0:T(8,128)(2,1)S(1)} %combine.5), channel_id=1, source_target_pairs={{0,16},{8,24},{16,0},{24,8},{1,17},{9,25},{17,1},{25,9},{2,18},{10... | collective-permute-start | bytes 417800 | tf_op jit(solution)/shard_map/ppermute | solution.py:419
  56.1 4.1 %collective-permute-start.21 = (bf16[32,2048]{1,0:T(8,128)(2,1)S(1)}, bf16[32,2048]{1,0:T(8,128)(2,1)S(1)}, u32[]{:S(2)}, u32[]{:S(2)}) collective-permute-start(bf16[32,2048]{1,0:T(8,128)(2,1)S(1)} %get-tuple-element.84), channel_id=1, source_target_pairs={{0,2},{1,3},{2,0},{3,1},{4,6},{5,7},{6,4},{7,5},{8,10},{9,11},{10,... | collective-permute-start | bytes 393224 | tf_op jit(solution)/shard_map/ppermute | solution.py:416
  56.9 4.1 %collective-permute-start.22 = (bf16[32,2048]{1,0:T(8,128)(2,1)S(1)}, bf16[32,2048]{1,0:T(8,128)(2,1)S(1)}, u32[]{:S(2)}, u32[]{:S(2)}) collective-permute-start(bf16[32,2048]{1,0:T(8,128)(2,1)S(1)} %get-tuple-element.85), channel_id=1, source_target_pairs={{0,4},{1,5},{2,6},{3,7},{4,0},{5,1},{6,2},{7,3},{8,12},{9,13},{10,... | collective-permute-start | bytes 393224 | tf_op jit(solution)/shard_map/ppermute | solution.py:416
  61.3 11.5 %collective-permute-start.29 = (bf16[32,2176]{1,0:T(8,128)(2,1)S(1)}, bf16[32,2176]{1,0:T(8,128)(2,1)S(1)}, u32[]{:S(2)}, u32[]{:S(2)}) collective-permute-start(bf16[32,2176]{1,0:T(8,128)(2,1)S(1)} %finish.1.refs_0_), channel_id=1, source_target_pairs={{0,6},{1,7},{2,4},{3,5},{4,2},{5,3},{6,0},{7,1},{8,14},{9,15},{10,... | collective-permute-start | bytes 417800 | tf_op jit(solution)/shard_map/ppermute | solution.py:416
  62.4 13.0 %collective-permute-start.28 = (bf16[32,2176]{1,0:T(8,128)(2,1)S(1)}, bf16[32,2176]{1,0:T(8,128)(2,1)S(1)}, u32[]{:S(2)}, u32[]{:S(2)}) collective-permute-start(bf16[32,2176]{1,0:T(8,128)(2,1)S(1)} %finish.1.refs_0_), channel_id=1, source_target_pairs={{0,4},{1,5},{2,6},{3,7},{4,0},{5,1},{6,2},{7,3},{8,12},{9,13},{10,... | collective-permute-start | bytes 417800 | tf_op jit(solution)/shard_map/ppermute | solution.py:416
  63.2 13.3 %collective-permute-start.27 = (bf16[32,2176]{1,0:T(8,128)(2,1)S(1)}, bf16[32,2176]{1,0:T(8,128)(2,1)S(1)}, u32[]{:S(2)}, u32[]{:S(2)}) collective-permute-start(bf16[32,2176]{1,0:T(8,128)(2,1)S(1)} %finish.1.refs_0_), channel_id=1, source_target_pairs={{0,2},{1,3},{2,0},{3,1},{4,6},{5,7},{6,4},{7,5},{8,10},{9,11},{10,... | collective-permute-start | bytes 417800 | tf_op jit(solution)/shard_map/ppermute | solution.py:416
  64.0 12.6 %collective-permute-start.30 = (bf16[32,2176]{1,0:T(8,128)(2,1)S(1)}, bf16[32,2176]{1,0:T(8,128)(2,1)S(1)}, u32[]{:S(2)}, u32[]{:S(2)}) collective-permute-start(bf16[32,2176]{1,0:T(8,128)(2,1)S(1)} %finish.1.refs_0_), channel_id=1, source_target_pairs={{0,1},{1,0},{2,3},{3,2},{4,5},{5,4},{6,7},{7,6},{8,9},{9,8},{10,11... | collective-permute-start | bytes 417800 | tf_op jit(solution)/shard_map/ppermute | solution.py:416
  72.8 3.8 %collective-permute-start.33 = (bf16[32,2176]{1,0:T(8,128)(2,1)S(1)}, bf16[32,2176]{1,0:T(8,128)(2,1)S(1)}, u32[]{:S(2)}, u32[]{:S(2)}) collective-permute-start(bf16[32,2176]{1,0:T(8,128)(2,1)S(1)} %collective-permute-done.29.refs_3_), channel_id=1, source_target_pairs={{0,1},{1,0},{2,3},{3,2},{4,5},{5,4},{6,7},{7,6},{8,9},{9,8},{10,11... | collective-permute-start | bytes 417800 | tf_op jit(solution)/shard_map/ppermute | solution.py:416
  (8 other events, 41.1 us)

commit v17 on v15

--- a/solution.py
+++ b/solution.py
@@ -221,9 +221,10 @@
     outs, refs = refs[:n_outs], refs[n_outs:]
     if with_last:
         last_all, last_projected, own_last, flat, seq_tokens, *refs = refs
-    (rows,) = refs
+    rows, sems = refs
     width = weights[0].shape[1]
     total = n_outs * part_rows
+    copies = []
     spots = [slice(index * part_rows, (index + 1) * part_rows) for index in range(n_outs)]
     for index, spot in enumerate(spots):
         hop, chip = group[index // chips], index % chips
@@ -232,11 +233,19 @@
             rows[spot, :] = parts[source][row : row + part_rows, :width]
         else:
             start = pl.multiple_of((place[1] ^ (2 * chip)) * part_rows, part_rows)
-            rows[spot, :] = tokens[pl.ds(start, part_rows), :]
+            copies.append(
+                pltpu.make_async_copy(
+                    tokens.at[pl.ds(start, part_rows)], rows.at[pl.ds(spot.start, part_rows)],
+                    sems.at[chip],
+                )
+            )
+            copies[-1].start()
     if with_last:
         floats = last_tokens(place, seq_dev, where_tiles, parts, seq_tokens)
         last_all[...] = floats.astype(bf16)
         rows[total:, :] = floats.astype(bf16)
+    for copy in copies:
+        copy.wait()
     hidden = []
     for half in range(2):
         projected = dot(rows[...], weights[2 * half][0])
@@ -497,12 +506,13 @@
             ] + scratch
         if after is not None:
             parts[0], _ = lax.optimization_barrier((parts[0], after))
+        scratch.append(pltpu.SemaphoreType.DMA((chips,)))
         operands = [tokens] * near + parts + list(weights)
         layout = (tuple(group), chips, part_rows, seq_dev, where_tiles, used, with_last)
         return pl.pallas_call(
             functools.partial(expert_kernel, layout),
             out_shape=out_shape,
-            in_specs=[in_vmem] * len(operands),
+            in_specs=[in_hbm] * near + [in_vmem] * (len(operands) - near),
             out_specs=[in_vmem] * len(out_shape),
             scratch_shapes=scratch,
             compiler_params=params(32),

time: 81.3 us -> 81.6 us (level)
    ppermute x28, starting transfers between devices: 26.9 us -> 26.1 us  [to_lane(): lax.ppermute(value, 'expert', [(j, j ^ step) for j in range(expert_count)])]
  transfers between devices with their start and end apart: 34 -> 34, of which waited for: 13 -> 12; matrix products, arithmetic and copies ran while one was open for 1% -> 1% of each run, Pallas kernels for 15% -> 16%
where the time goes in v17:
time: 81.6 us; the launch traced here: 81.3 us
  starting transfers between devices  35.6 us (44%)
  waiting for transfers between devices  22.5 us (28%)
  Pallas kernels  17.1 us (21%)
  local copies, waits for them, and re-layouts  5.26 us (6%)
  between operations  0.84 us (1%)
    ppermute x28, starting transfers between devices, to_lane(): lax.ppermute(value, 'expert', [(j, j ^ step) for j in range(expert_count)])  26.1 us
    ppermute x28, waiting for transfers between devices, to_lane(): lax.ppermute(value, 'expert', [(j, j ^ step) for j in range(expert_count)])  14 us
    pallas_call x2, Pallas kernels, expert(): pl.pallas_call(functools.partial(expert_kernel, layout), out_shape=out_sh...  9.93 us
    ppermute x6, starting transfers between devices, to_plane(): return lax.ppermute(value, 'dp', [(p, p ^ step) for p in range(dp_count)])  9.46 us
    ppermute x6, waiting for transfers between devices, to_plane(): return lax.ppermute(value, 'dp', [(p, p ^ step) for p in range(dp_count)])  8.51 us
    unnamed x12, local copies, waits for them, and re-layouts  4.53 us
    pallas_call x1, Pallas kernels, body(): pl.pallas_call(functools.partial(final_kernel, len(pieces), n_blocks), ou...  4.12 us
    pallas_call x1, Pallas kernels, body(): pl.pallas_call(functools.partial(pack_kernel, seq_dev), out_shape=jax.Sha...  1.66 us
  transfers between devices with their start and end apart: 34, of which 12 were waited for; matrix products, arithmetic and copies ran while one was open for 1% of the time, Pallas kernels for 16%

profile of v17, /device:TPU:0, one launch (start us, length us, event | category | flops | bytes accessed | tf_op | source)
XLA Modules:
  0.0 81.3 jit_solution(921283285925554329)
XLA Ops:
  1.2 1.7 %pack.1.refs_0_ = bf16[32,2176]{1,0:T(8,128)(2,1)} custom-call(s32[4]{0:T(128)} %partners.1, s32[1,256]{1,0:T(1,128)} %bitcast.2, f32[1,256]{1,0:T(1,128)} %bitcast.3, bf16[256,2048]{1,0:T(8,128)(2,1)} %refs_0_.1), custom_call_target="tpu_custom_call" | custom-call | bytes 524288 | tf_op jit(solution)/shard_map/pack/pallas_call | solution.py:434
  2.9 3.1 %collective-permute-start = (bf16[32,2176]{1,0:T(8,128)(2,1)}, bf16[32,2176]{1,0:T(8,128)(2,1)S(1)}, u32[]{:S(2)}, u32[]{:S(2)}) collective-permute-start(bf16[32,2176]{1,0:T(8,128)(2,1)} %pack.1.refs_0_), channel_id=1, source_target_pairs={{0,8},{8,0},{16,24},{24,16},{1,9},{9,1},{17,25},{25,17},{2,10},{10... | collective-permute-start | bytes 417800 | tf_op jit(solution)/shard_map/ppermute | solution.py:428
  6.0 2.5 %collective-permute-start.2 = (bf16[32,2176]{1,0:T(8,128)(2,1)}, bf16[32,2176]{1,0:T(8,128)(2,1)S(1)}, u32[]{:S(2)}, u32[]{:S(2)}) collective-permute-start(bf16[32,2176]{1,0:T(8,128)(2,1)} %pack.1.refs_0_), channel_id=1, source_target_pairs={{0,24},{8,16},{16,8},{24,0},{1,25},{9,17},{17,9},{25,1},{2,26},{10... | collective-permute-start | bytes 417800 | tf_op jit(solution)/shard_map/ppermute | solution.py:428
  9.3 0.9 %collective-permute-done.refs_1_ = bf16[32,2176]{1,0:T(8,128)(2,1)S(1)} collective-permute-done((bf16[32,2176]{1,0:T(8,128)(2,1)}, bf16[32,2176]{1,0:T(8,128)(2,1)S(1)}, u32[]{:S(2)}, u32[]{:S(2)}) %collective-permute-start) | collective-permute-done | bytes 139296 | tf_op jit(solution)/shard_map/ppermute | solution.py:428
  10.2 2.6 %collective-permute-start.7 = (bf16[32,2304]{1,0:T(8,128)(2,1)S(1)}, bf16[32,2304]{1,0:T(8,128)(2,1)S(1)}, u32[]{:S(2)}, u32[]{:S(2)}) collective-permute-start(bf16[32,2304]{1,0:T(8,128)(2,1)S(1)} %pad_maximum_fusion.1), channel_id=1, source_target_pairs={{0,6},{1,7},{2,4},{3,5},{4,2},{5,3},{6,0},{7,1},{8,14},{9,15},{10,... | collective-permute-start | bytes 442376 | tf_op jit(solution)/shard_map/ppermute | solution.py:425
  13.8 2.4 %collective-permute-done.2.refs_6_ = bf16[32,2176]{1,0:T(8,128)(2,1)S(1)} collective-permute-done((bf16[32,2176]{1,0:T(8,128)(2,1)}, bf16[32,2176]{1,0:T(8,128)(2,1)S(1)}, u32[]{:S(2)}, u32[]{:S(2)}) %collective-permute-start.2) | collective-permute-done | bytes 139296 | tf_op jit(solution)/shard_map/ppermute | solution.py:428
  16.2 5.1 %collective-permute-done.1.refs_5_ = bf16[32,2176]{1,0:T(8,128)(2,1)S(1)} collective-permute-done((bf16[32,2176]{1,0:T(8,128)(2,1)}, bf16[32,2176]{1,0:T(8,128)(2,1)S(1)}, u32[]{:S(2)}, u32[]{:S(2)}) %collective-permute-start.1) | collective-permute-done | bytes 139296 | tf_op jit(solution)/shard_map/ppermute | solution.py:428
  21.4 2.5 %collective-permute-start.10 = (bf16[64,2176]{1,0:T(8,128)(2,1)S(1)}, bf16[64,2176]{1,0:T(8,128)(2,1)S(1)}, u32[]{:S(2)}, u32[]{:S(2)}) collective-permute-start(bf16[64,2176]{1,0:T(8,128)(2,1)S(1)} %pad_maximum_fusion), channel_id=1, source_target_pairs={{0,6},{1,7},{2,4},{3,5},{4,2},{5,3},{6,0},{7,1},{8,14},{9,15},{10,... | collective-permute-start | bytes 835592 | tf_op jit(solution)/shard_map/ppermute | solution.py:425
  25.0 1.4 %copy-done = bf16[1,384,2048]{2,1,0:T(8,128)(2,1)S(1)} copy-done((bf16[1,384,2048]{2,1,0:T(8,128)(2,1)S(1)}, bf16[1,384,2048]{2,1,0:T(8,128)(2,1)}, u32[]{:S(2)}) %copy-start) | copy-done | bytes 1572888
  26.4 1.9 %copy-done.2 = bf16[1,2048,768]{2,1,0:T(8,128)(2,1)S(1)} copy-done((bf16[1,2048,768]{2,1,0:T(8,128)(2,1)S(1)}, bf16[1,2048,768]{2,1,0:T(8,128)(2,1)}, u32[]{:S(2)}) %copy-start.2) | copy-done | bytes 3145752
  28.3 1.2 %copy-done.4 = bf16[256,2048]{1,0:T(8,128)(2,1)S(1)} copy-done((bf16[256,2048]{1,0:T(8,128)(2,1)S(1)}, bf16[256,2048]{1,0:T(8,128)(2,1)}, u32[]{:S(2)}) %copy-start.4) | copy-done | bytes 1048600
  29.5 5.2 %experts.2 = (bf16[32,2048]{1,0:T(8,128)(2,1)S(1)}, bf16[32,2048]{1,0:T(8,128)(2,1)S(1)}, bf16[32,2048]{1,0:T(8,128)(2,1)S(1)}, bf16[32,2048]{1,0:T(8,128)(2,1)S...) custom-call(bf16[256,2048]{1,0:T(8,128)(2,1)S(1)} %copy-done.4, ...), custom_call_target="tpu_custom_call" | custom-call | flops 2415919104 | bytes 12582912 | tf_op jit(solution)/shard_map/experts/pallas_call | solution.py:512
  34.8 1.6 %collective-permute-start.11 = (bf16[32,2048]{1,0:T(8,128)(2,1)S(1)}, bf16[32,2048]{1,0:T(8,128)(2,1)S(1)}, u32[]{:S(2)}, u32[]{:S(2)}) collective-permute-start(bf16[32,2048]{1,0:T(8,128)(2,1)S(1)} %get-tuple-element.68), channel_id=1, source_target_pairs={{0,2},{1,3},{2,0},{3,1},{4,6},{5,7},{6,4},{7,5},{8,10},{9,11},{10,... | collective-permute-start | bytes 393224 | tf_op jit(solution)/shard_map/ppermute | solution.py:425
  36.3 1.5 %collective-permute-start.12 = (bf16[32,2048]{1,0:T(8,128)(2,1)S(1)}, bf16[32,2048]{1,0:T(8,128)(2,1)S(1)}, u32[]{:S(2)}, u32[]{:S(2)}) collective-permute-start(bf16[32,2048]{1,0:T(8,128)(2,1)S(1)} %get-tuple-element.69), channel_id=1, source_target_pairs={{0,4},{1,5},{2,6},{3,7},{4,0},{5,1},{6,2},{7,3},{8,12},{9,13},{10,... | collective-permute-start | bytes 393224 | tf_op jit(solution)/shard_map/ppermute | solution.py:425
  38.4 4.7 %experts.3 = (bf16[32,2048]{1,0:T(8,128)(2,1)S(1)}, bf16[32,2048]{1,0:T(8,128)(2,1)S(1)}, bf16[32,2048]{1,0:T(8,128)(2,1)S(1)}, bf16[32,2048]{1,0:T(8,128)(2,1)S...) custom-call(bf16[32,2176]{1,0:T(8,128)(2,1)S(1)} %copy-done.5, ...), custom_call_target="tpu_custom_call" | custom-call | flops 2566914048 | bytes 12582912 | tf_op jit(solution)/shard_map/experts/pallas_call | solution.py:512
  43.7 1.9 %collective-permute-start.14 = (bf16[32,2176]{1,0:T(8,128)(2,1)S(1)}, bf16[32,2176]{1,0:T(8,128)(2,1)S(1)}, u32[]{:S(2)}, u32[]{:S(2)}) collective-permute-start(bf16[32,2176]{1,0:T(8,128)(2,1)S(1)} %get-tuple-element.71), channel_id=1, source_target_pairs={{0,6},{1,7},{2,4},{3,5},{4,2},{5,3},{6,0},{7,1},{8,14},{9,15},{10,... | collective-permute-start | bytes 417800 | tf_op jit(solution)/shard_map/ppermute | solution.py:425
  46.2 1.1 %collective-permute-start.17 = (bf16[32,2176]{1,0:T(8,128)(2,1)S(1)}, bf16[32,2176]{1,0:T(8,128)(2,1)S(1)}, u32[]{:S(2)}, u32[]{:S(2)}) collective-permute-start(bf16[32,2176]{1,0:T(8,128)(2,1)S(1)} %get-tuple-element.79), channel_id=1, source_target_pairs={{0,4},{1,5},{2,6},{3,7},{4,0},{5,1},{6,2},{7,3},{8,12},{9,13},{10,... | collective-permute-start | bytes 417800 | tf_op jit(solution)/shard_map/ppermute | solution.py:425
  47.8 1.0 %collective-permute-start.22 = (bf16[32,2048]{1,0:T(8,128)(2,1)S(1)}, bf16[32,2048]{1,0:T(8,128)(2,1)S(1)}, u32[]{:S(2)}, u32[]{:S(2)}) collective-permute-start(bf16[32,2048]{1,0:T(8,128)(2,1)S(1)} %get-tuple-element.87), channel_id=1, source_target_pairs={{0,2},{1,3},{2,0},{3,1},{4,6},{5,7},{6,4},{7,5},{8,10},{9,11},{10,... | collective-permute-start | bytes 393224 | tf_op jit(solution)/shard_map/ppermute | solution.py:425
  49.0 1.3 %collective-permute-start.23 = (bf16[32,2048]{1,0:T(8,128)(2,1)S(1)}, bf16[32,2048]{1,0:T(8,128)(2,1)S(1)}, u32[]{:S(2)}, u32[]{:S(2)}) collective-permute-start(bf16[32,2048]{1,0:T(8,128)(2,1)S(1)} %get-tuple-element.88), channel_id=1, source_target_pairs={{0,4},{1,5},{2,6},{3,7},{4,0},{5,1},{6,2},{7,3},{8,12},{9,13},{10,... | collective-permute-start | bytes 393224 | tf_op jit(solution)/shard_map/ppermute | solution.py:425
  50.3 1.3 %collective-permute-start.24 = (bf16[32,2048]{1,0:T(8,128)(2,1)S(1)}, bf16[32,2048]{1,0:T(8,128)(2,1)S(1)}, u32[]{:S(2)}, u32[]{:S(2)}) collective-permute-start(bf16[32,2048]{1,0:T(8,128)(2,1)S(1)} %get-tuple-element.89), channel_id=1, source_target_pairs={{0,6},{1,7},{2,4},{3,5},{4,2},{5,3},{6,0},{7,1},{8,14},{9,15},{10,... | collective-permute-start | bytes 393224 | tf_op jit(solution)/shard_map/ppermute | solution.py:425
  51.8 1.1 %collective-permute-start.18 = (bf16[32,2048]{1,0:T(8,128)(2,1)S(1)}, bf16[32,2048]{1,0:T(8,128)(2,1)S(1)}, u32[]{:S(2)}, u32[]{:S(2)}) collective-permute-start(bf16[32,2048]{1,0:T(8,128)(2,1)S(1)} %get-tuple-element.82), channel_id=1, source_target_pairs={{0,2},{1,3},{2,0},{3,1},{4,6},{5,7},{6,4},{7,5},{8,10},{9,11},{10,... | collective-permute-start | bytes 393224 | tf_op jit(solution)/shard_map/ppermute | solution.py:425
  53.0 2.6 %collective-permute-start.21 = (bf16[32,2176]{1,0:T(8,128)(2,1)S(1)}, bf16[32,2176]{1,0:T(8,128)(2,1)S(1)}, u32[]{:S(2)}, u32[]{:S(2)}) collective-permute-start(bf16[32,2176]{1,0:T(8,128)(2,1)S(1)} %get-tuple-element.81), channel_id=1, source_target_pairs={{0,24},{8,16},{16,8},{24,0},{1,25},{9,17},{17,9},{25,1},{2,26},{10... | collective-permute-start | bytes 417800 | tf_op jit(solution)/shard_map/ppermute | solution.py:428
  55.9 1.2 %collective-permute-done.23.refs_3_ = bf16[32,2048]{1,0:T(8,128)(2,1)S(1)} collective-permute-done((bf16[32,2048]{1,0:T(8,128)(2,1)S(1)}, bf16[32,2048]{1,0:T(8,128)(2,1)S(1)}, u32[]{:S(2)}, u32[]{:S(2)}) %collective-permute-start.23) | collective-permute-done | bytes 131104 | tf_op jit(solution)/shard_map/ppermute | solution.py:425
  57.9 1.1 %collective-permute-start.25 = (bf16[32,2176]{1,0:T(8,128)(2,1)S(1)}, bf16[32,2176]{1,0:T(8,128)(2,1)S(1)}, u32[]{:S(2)}, u32[]{:S(2)}) collective-permute-start(bf16[32,2176]{1,0:T(8,128)(2,1)S(1)} %combine.6), channel_id=1, source_target_pairs={{0,16},{8,24},{16,0},{24,8},{1,17},{9,25},{17,1},{25,9},{2,18},{10... | collective-permute-start | bytes 417800 | tf_op jit(solution)/shard_map/ppermute | solution.py:428
  59.0 0.9 %collective-permute-start.19 = (bf16[32,2048]{1,0:T(8,128)(2,1)S(1)}, bf16[32,2048]{1,0:T(8,128)(2,1)S(1)}, u32[]{:S(2)}, u32[]{:S(2)}) collective-permute-start(bf16[32,2048]{1,0:T(8,128)(2,1)S(1)} %get-tuple-element.83), channel_id=1, source_target_pairs={{0,4},{1,5},{2,6},{3,7},{4,0},{5,1},{6,2},{7,3},{8,12},{9,13},{10,... | collective-permute-start | bytes 393224 | tf_op jit(solution)/shard_map/ppermute | solution.py:425
  59.9 1.5 %collective-permute-start.20 = (bf16[32,2048]{1,0:T(8,128)(2,1)S(1)}, bf16[32,2048]{1,0:T(8,128)(2,1)S(1)}, u32[]{:S(2)}, u32[]{:S(2)}) collective-permute-start(bf16[32,2048]{1,0:T(8,128)(2,1)S(1)} %get-tuple-element.84), channel_id=1, source_target_pairs={{0,6},{1,7},{2,4},{3,5},{4,2},{5,3},{6,0},{7,1},{8,14},{9,15},{10,... | collective-permute-start | bytes 393224 | tf_op jit(solution)/shard_map/ppermute | solution.py:425
  61.4 5.3 %collective-permute-done.19.refs_3_ = bf16[32,2048]{1,0:T(8,128)(2,1)S(1)} collective-permute-done((bf16[32,2048]{1,0:T(8,128)(2,1)S(1)}, bf16[32,2048]{1,0:T(8,128)(2,1)S(1)}, u32[]{:S(2)}, u32[]{:S(2)}) %collective-permute-start.19) | collective-permute-done | bytes 131104 | tf_op jit(solution)/shard_map/ppermute | solution.py:425
  67.1 1.8 %collective-permute-start.29 = (bf16[32,2176]{1,0:T(8,128)(2,1)S(1)}, bf16[32,2176]{1,0:T(8,128)(2,1)S(1)}, u32[]{:S(2)}, u32[]{:S(2)}) collective-permute-start(bf16[32,2176]{1,0:T(8,128)(2,1)S(1)} %finish.1.refs_0_), channel_id=1, source_target_pairs={{0,6},{1,7},{2,4},{3,5},{4,2},{5,3},{6,0},{7,1},{8,14},{9,15},{10,... | collective-permute-start | bytes 417800 | tf_op jit(solution)/shard_map/ppermute | solution.py:425
  69.6 1.0 %collective-permute-start.27 = (bf16[32,2176]{1,0:T(8,128)(2,1)S(1)}, bf16[32,2176]{1,0:T(8,128)(2,1)S(1)}, u32[]{:S(2)}, u32[]{:S(2)}) collective-permute-start(bf16[32,2176]{1,0:T(8,128)(2,1)S(1)} %finish.1.refs_0_), channel_id=1, source_target_pairs={{0,2},{1,3},{2,0},{3,1},{4,6},{5,7},{6,4},{7,5},{8,10},{9,11},{10,... | collective-permute-start | bytes 417800 | tf_op jit(solution)/shard_map/ppermute | solution.py:425
  70.6 3.8 %collective-permute-done.29.refs_3_ = bf16[32,2176]{1,0:T(8,128)(2,1)S(1)} collective-permute-done((bf16[32,2176]{1,0:T(8,128)(2,1)S(1)}, bf16[32,2176]{1,0:T(8,128)(2,1)S(1)}, u32[]{:S(2)}, u32[]{:S(2)}) %collective-permute-start.29) | collective-permute-done | bytes 139296 | tf_op jit(solution)/shard_map/ppermute | solution.py:425
  74.5 1.1 %collective-permute-done.28.refs_2_ = bf16[32,2176]{1,0:T(8,128)(2,1)S(1)} collective-permute-done((bf16[32,2176]{1,0:T(8,128)(2,1)S(1)}, bf16[32,2176]{1,0:T(8,128)(2,1)S(1)}, u32[]{:S(2)}, u32[]{:S(2)}) %collective-permute-start.28) | collective-permute-done | bytes 139296 | tf_op jit(solution)/shard_map/ppermute | solution.py:425
  77.2 4.1 %final.1 = (bf16[256,2048]{1,0:T(8,128)(2,1)}, bf16[1,2048,768]{2,1,0:T(8,128)(2,1)}, bf16[1,384,2048]{2,1,0:T(8,128)(2,1)}) custom-call(bf16[32,2176]{1,0:T(8,128)(2,1)S(1)} %finish.1.refs_0_, bf16[32,2176]{1,0:T(8,128)(2,1)S(1)} %collective-permute-done.27.refs_1_, bf16[32,2176]{1,0:T(8,128)(2,1)S(1)} %collective-permute-done.28.refs_2_, ...), custom_call_target="tpu_custom_call" | custom-call | flops 100663296 | bytes 7340032 | tf_op jit(solution)/shard_map/final/pallas_call | solution.py:619
  (61 shorter events, 9.8 us)
Async XLA Ops:
  0.6 9.6 %collective-permute-start.3 = (bf16[1,2048,768]{2,1,0:T(8,128)(2,1)}, bf16[1,2048,768]{2,1,0:T(8,128)(2,1)S(1)}, u32[]{:S(2)}, u32[]{:S(2)}) collective-permute-start(bf16[1,2048,768]{2,1,0:T(8,128)(2,1)} %refs_10_), channel_id=1, source_target_pairs={{0,1},{1,0},{2,3},{3,2},{4,5},{5,4},{6,7},{7,6},{8,9},{9,8},{10,11... | collective-permute-start | bytes 9437192 | tf_op jit(solution)/shard_map/ppermute | solution.py:425
  1.1 9.1 %collective-permute-start.4 = (bf16[1,384,2048]{2,1,0:T(8,128)(2,1)}, bf16[1,384,2048]{2,1,0:T(8,128)(2,1)}, u32[]{:S(2)}, u32[]{:S(2)}) collective-permute-start(bf16[1,384,2048]{2,1,0:T(8,128)(2,1)} %refs_13_.1), channel_id=1, source_target_pairs={{0,1},{1,0},{2,3},{3,2},{4,5},{5,4},{6,7},{7,6},{8,9},{9,8},{10,11... | collective-permute-start | bytes 4718600 | tf_op jit(solution)/shard_map/ppermute | solution.py:425
  2.9 7.3 %collective-permute-start = (bf16[32,2176]{1,0:T(8,128)(2,1)}, bf16[32,2176]{1,0:T(8,128)(2,1)S(1)}, u32[]{:S(2)}, u32[]{:S(2)}) collective-permute-start(bf16[32,2176]{1,0:T(8,128)(2,1)} %pack.1.refs_0_), channel_id=1, source_target_pairs={{0,8},{8,0},{16,24},{24,16},{1,9},{9,1},{17,25},{25,17},{2,10},{10... | collective-permute-start | bytes 417800 | tf_op jit(solution)/shard_map/ppermute | solution.py:428
  6.0 10.3 %collective-permute-start.2 = (bf16[32,2176]{1,0:T(8,128)(2,1)}, bf16[32,2176]{1,0:T(8,128)(2,1)S(1)}, u32[]{:S(2)}, u32[]{:S(2)}) collective-permute-start(bf16[32,2176]{1,0:T(8,128)(2,1)} %pack.1.refs_0_), channel_id=1, source_target_pairs={{0,24},{8,16},{16,8},{24,0},{1,25},{9,17},{17,9},{25,1},{2,26},{10... | collective-permute-start | bytes 417800 | tf_op jit(solution)/shard_map/ppermute | solution.py:428
  8.4 12.9 %collective-permute-start.1 = (bf16[32,2176]{1,0:T(8,128)(2,1)}, bf16[32,2176]{1,0:T(8,128)(2,1)S(1)}, u32[]{:S(2)}, u32[]{:S(2)}) collective-permute-start(bf16[32,2176]{1,0:T(8,128)(2,1)} %pack.1.refs_0_), channel_id=1, source_target_pairs={{0,16},{8,24},{16,0},{24,8},{1,17},{9,25},{17,1},{25,9},{2,18},{10... | collective-permute-start | bytes 417800 | tf_op jit(solution)/shard_map/ppermute | solution.py:428
  10.2 11.2 %collective-permute-start.7 = (bf16[32,2304]{1,0:T(8,128)(2,1)S(1)}, bf16[32,2304]{1,0:T(8,128)(2,1)S(1)}, u32[]{:S(2)}, u32[]{:S(2)}) collective-permute-start(bf16[32,2304]{1,0:T(8,128)(2,1)S(1)} %pad_maximum_fusion.1), channel_id=1, source_target_pairs={{0,6},{1,7},{2,4},{3,5},{4,2},{5,3},{6,0},{7,1},{8,14},{9,15},{10,... | collective-permute-start | bytes 442376 | tf_op jit(solution)/shard_map/ppermute | solution.py:425
  12.8 8.6 %collective-permute-start.6 = (bf16[32,2304]{1,0:T(8,128)(2,1)S(1)}, bf16[32,2304]{1,0:T(8,128)(2,1)S(1)}, u32[]{:S(2)}, u32[]{:S(2)}) collective-permute-start(bf16[32,2304]{1,0:T(8,128)(2,1)S(1)} %pad_maximum_fusion.1), channel_id=1, source_target_pairs={{0,4},{1,5},{2,6},{3,7},{4,0},{5,1},{6,2},{7,3},{8,12},{9,13},{10,... | collective-permute-start | bytes 442376 | tf_op jit(solution)/shard_map/ppermute | solution.py:425
  13.3 8.1 %collective-permute-start.5 = (bf16[32,2304]{1,0:T(8,128)(2,1)S(1)}, bf16[32,2304]{1,0:T(8,128)(2,1)S(1)}, u32[]{:S(2)}, u32[]{:S(2)}) collective-permute-start(bf16[32,2304]{1,0:T(8,128)(2,1)S(1)} %pad_maximum_fusion.1), channel_id=1, source_target_pairs={{0,2},{1,3},{2,0},{3,1},{4,6},{5,7},{6,4},{7,5},{8,10},{9,11},{10,... | collective-permute-start | bytes 442376 | tf_op jit(solution)/shard_map/ppermute | solution.py:425
  21.4 16.4 %collective-permute-start.10 = (bf16[64,2176]{1,0:T(8,128)(2,1)S(1)}, bf16[64,2176]{1,0:T(8,128)(2,1)S(1)}, u32[]{:S(2)}, u32[]{:S(2)}) collective-permute-start(bf16[64,2176]{1,0:T(8,128)(2,1)S(1)} %pad_maximum_fusion), channel_id=1, source_target_pairs={{0,6},{1,7},{2,4},{3,5},{4,2},{5,3},{6,0},{7,1},{8,14},{9,15},{10,... | collective-permute-start | bytes 835592 | tf_op jit(solution)/shard_map/ppermute | solution.py:425
  24.0 14.4 %collective-permute-start.9 = (bf16[64,2176]{1,0:T(8,128)(2,1)S(1)}, bf16[64,2176]{1,0:T(8,128)(2,1)S(1)}, u32[]{:S(2)}, u32[]{:S(2)}) collective-permute-start(bf16[64,2176]{1,0:T(8,128)(2,1)S(1)} %pad_maximum_fusion), channel_id=1, source_target_pairs={{0,4},{1,5},{2,6},{3,7},{4,0},{5,1},{6,2},{7,3},{8,12},{9,13},{10,... | collective-permute-start | bytes 835592 | tf_op jit(solution)/shard_map/ppermute | solution.py:425
  24.5 13.9 %collective-permute-start.8 = (bf16[64,2176]{1,0:T(8,128)(2,1)S(1)}, bf16[64,2176]{1,0:T(8,128)(2,1)S(1)}, u32[]{:S(2)}, u32[]{:S(2)}) collective-permute-start(bf16[64,2176]{1,0:T(8,128)(2,1)S(1)} %pad_maximum_fusion), channel_id=1, source_target_pairs={{0,2},{1,3},{2,0},{3,1},{4,6},{5,7},{6,4},{7,5},{8,10},{9,11},{10,... | collective-permute-start | bytes 835592 | tf_op jit(solution)/shard_map/ppermute | solution.py:425
  34.8 8.3 %collective-permute-start.11 = (bf16[32,2048]{1,0:T(8,128)(2,1)S(1)}, bf16[32,2048]{1,0:T(8,128)(2,1)S(1)}, u32[]{:S(2)}, u32[]{:S(2)}) collective-permute-start(bf16[32,2048]{1,0:T(8,128)(2,1)S(1)} %get-tuple-element.68), channel_id=1, source_target_pairs={{0,2},{1,3},{2,0},{3,1},{4,6},{5,7},{6,4},{7,5},{8,10},{9,11},{10,... | collective-permute-start | bytes 393224 | tf_op jit(solution)/shard_map/ppermute | solution.py:425
  36.3 6.7 %collective-permute-start.12 = (bf16[32,2048]{1,0:T(8,128)(2,1)S(1)}, bf16[32,2048]{1,0:T(8,128)(2,1)S(1)}, u32[]{:S(2)}, u32[]{:S(2)}) collective-permute-start(bf16[32,2048]{1,0:T(8,128)(2,1)S(1)} %get-tuple-element.69), channel_id=1, source_target_pairs={{0,4},{1,5},{2,6},{3,7},{4,0},{5,1},{6,2},{7,3},{8,12},{9,13},{10,... | collective-permute-start | bytes 393224 | tf_op jit(solution)/shard_map/ppermute | solution.py:425
  37.9 5.9 %collective-permute-start.13 = (bf16[32,2048]{1,0:T(8,128)(2,1)S(1)}, bf16[32,2048]{1,0:T(8,128)(2,1)S(1)}, u32[]{:S(2)}, u32[]{:S(2)}) collective-permute-start(bf16[32,2048]{1,0:T(8,128)(2,1)S(1)} %get-tuple-element.70), channel_id=1, source_target_pairs={{0,6},{1,7},{2,4},{3,5},{4,2},{5,3},{6,0},{7,1},{8,14},{9,15},{10,... | collective-permute-start | bytes 393224 | tf_op jit(solution)/shard_map/ppermute | solution.py:425
  43.7 6.6 %collective-permute-start.14 = (bf16[32,2176]{1,0:T(8,128)(2,1)S(1)}, bf16[32,2176]{1,0:T(8,128)(2,1)S(1)}, u32[]{:S(2)}, u32[]{:S(2)}) collective-permute-start(bf16[32,2176]{1,0:T(8,128)(2,1)S(1)} %get-tuple-element.71), channel_id=1, source_target_pairs={{0,6},{1,7},{2,4},{3,5},{4,2},{5,3},{6,0},{7,1},{8,14},{9,15},{10,... | collective-permute-start | bytes 417800 | tf_op jit(solution)/shard_map/ppermute | solution.py:425
  45.6 6.0 %collective-permute-start.16 = (bf16[32,2176]{1,0:T(8,128)(2,1)S(1)}, bf16[32,2176]{1,0:T(8,128)(2,1)S(1)}, u32[]{:S(2)}, u32[]{:S(2)}) collective-permute-start(bf16[32,2176]{1,0:T(8,128)(2,1)S(1)} %get-tuple-element.78), channel_id=1, source_target_pairs={{0,2},{1,3},{2,0},{3,1},{4,6},{5,7},{6,4},{7,5},{8,10},{9,11},{10,... | collective-permute-start | bytes 417800 | tf_op jit(solution)/shard_map/ppermute | solution.py:425
  46.2 5.5 %collective-permute-start.17 = (bf16[32,2176]{1,0:T(8,128)(2,1)S(1)}, bf16[32,2176]{1,0:T(8,128)(2,1)S(1)}, u32[]{:S(2)}, u32[]{:S(2)}) collective-permute-start(bf16[32,2176]{1,0:T(8,128)(2,1)S(1)} %get-tuple-element.79), channel_id=1, source_target_pairs={{0,4},{1,5},{2,6},{3,7},{4,0},{5,1},{6,2},{7,3},{8,12},{9,13},{10,... | collective-permute-start | bytes 417800 | tf_op jit(solution)/shard_map/ppermute | solution.py:425
  47.8 8.0 %collective-permute-start.22 = (bf16[32,2048]{1,0:T(8,128)(2,1)S(1)}, bf16[32,2048]{1,0:T(8,128)(2,1)S(1)}, u32[]{:S(2)}, u32[]{:S(2)}) collective-permute-start(bf16[32,2048]{1,0:T(8,128)(2,1)S(1)} %get-tuple-element.87), channel_id=1, source_target_pairs={{0,2},{1,3},{2,0},{3,1},{4,6},{5,7},{6,4},{7,5},{8,10},{9,11},{10,... | collective-permute-start | bytes 393224 | tf_op jit(solution)/shard_map/ppermute | solution.py:425
  49.0 8.1 %collective-permute-start.23 = (bf16[32,2048]{1,0:T(8,128)(2,1)S(1)}, bf16[32,2048]{1,0:T(8,128)(2,1)S(1)}, u32[]{:S(2)}, u32[]{:S(2)}) collective-permute-start(bf16[32,2048]{1,0:T(8,128)(2,1)S(1)} %get-tuple-element.88), channel_id=1, source_target_pairs={{0,4},{1,5},{2,6},{3,7},{4,0},{5,1},{6,2},{7,3},{8,12},{9,13},{10,... | collective-permute-start | bytes 393224 | tf_op jit(solution)/shard_map/ppermute | solution.py:425
  50.3 7.3 %collective-permute-start.24 = (bf16[32,2048]{1,0:T(8,128)(2,1)S(1)}, bf16[32,2048]{1,0:T(8,128)(2,1)S(1)}, u32[]{:S(2)}, u32[]{:S(2)}) collective-permute-start(bf16[32,2048]{1,0:T(8,128)(2,1)S(1)} %get-tuple-element.89), channel_id=1, source_target_pairs={{0,6},{1,7},{2,4},{3,5},{4,2},{5,3},{6,0},{7,1},{8,14},{9,15},{10,... | collective-permute-start | bytes 393224 | tf_op jit(solution)/shard_map/ppermute | solution.py:425
  51.8 8.1 %collective-permute-start.18 = (bf16[32,2048]{1,0:T(8,128)(2,1)S(1)}, bf16[32,2048]{1,0:T(8,128)(2,1)S(1)}, u32[]{:S(2)}, u32[]{:S(2)}) collective-permute-start(bf16[32,2048]{1,0:T(8,128)(2,1)S(1)} %get-tuple-element.82), channel_id=1, source_target_pairs={{0,2},{1,3},{2,0},{3,1},{4,6},{5,7},{6,4},{7,5},{8,10},{9,11},{10,... | collective-permute-start | bytes 393224 | tf_op jit(solution)/shard_map/ppermute | solution.py:425
  53.0 14.0 %collective-permute-start.21 = (bf16[32,2176]{1,0:T(8,128)(2,1)S(1)}, bf16[32,2176]{1,0:T(8,128)(2,1)S(1)}, u32[]{:S(2)}, u32[]{:S(2)}) collective-permute-start(bf16[32,2176]{1,0:T(8,128)(2,1)S(1)} %get-tuple-element.81), channel_id=1, source_target_pairs={{0,24},{8,16},{16,8},{24,0},{1,25},{9,17},{17,9},{25,1},{2,26},{10... | collective-permute-start | bytes 417800 | tf_op jit(solution)/shard_map/ppermute | solution.py:428
  55.8 11.2 %collective-permute-start.26 = (bf16[32,2176]{1,0:T(8,128)(2,1)S(1)}, bf16[32,2176]{1,0:T(8,128)(2,1)S(1)}, u32[]{:S(2)}, u32[]{:S(2)}) collective-permute-start(bf16[32,2176]{1,0:T(8,128)(2,1)S(1)} %combine.7), channel_id=1, source_target_pairs={{0,8},{8,0},{16,24},{24,16},{1,9},{9,1},{17,25},{25,17},{2,10},{10... | collective-permute-start | bytes 417800 | tf_op jit(solution)/shard_map/ppermute | solution.py:428
  57.9 9.1 %collective-permute-start.25 = (bf16[32,2176]{1,0:T(8,128)(2,1)S(1)}, bf16[32,2176]{1,0:T(8,128)(2,1)S(1)}, u32[]{:S(2)}, u32[]{:S(2)}) collective-permute-start(bf16[32,2176]{1,0:T(8,128)(2,1)S(1)} %combine.6), channel_id=1, source_target_pairs={{0,16},{8,24},{16,0},{24,8},{1,17},{9,25},{17,1},{25,9},{2,18},{10... | collective-permute-start | bytes 417800 | tf_op jit(solution)/shard_map/ppermute | solution.py:428
  59.0 7.8 %collective-permute-start.19 = (bf16[32,2048]{1,0:T(8,128)(2,1)S(1)}, bf16[32,2048]{1,0:T(8,128)(2,1)S(1)}, u32[]{:S(2)}, u32[]{:S(2)}) collective-permute-start(bf16[32,2048]{1,0:T(8,128)(2,1)S(1)} %get-tuple-element.83), channel_id=1, source_target_pairs={{0,4},{1,5},{2,6},{3,7},{4,0},{5,1},{6,2},{7,3},{8,12},{9,13},{10,... | collective-permute-start | bytes 393224 | tf_op jit(solution)/shard_map/ppermute | solution.py:425
  59.9 6.8 %collective-permute-start.20 = (bf16[32,2048]{1,0:T(8,128)(2,1)S(1)}, bf16[32,2048]{1,0:T(8,128)(2,1)S(1)}, u32[]{:S(2)}, u32[]{:S(2)}) collective-permute-start(bf16[32,2048]{1,0:T(8,128)(2,1)S(1)} %get-tuple-element.84), channel_id=1, source_target_pairs={{0,6},{1,7},{2,4},{3,5},{4,2},{5,3},{6,0},{7,1},{8,14},{9,15},{10,... | collective-permute-start | bytes 393224 | tf_op jit(solution)/shard_map/ppermute | solution.py:425
  67.1 7.4 %collective-permute-start.29 = (bf16[32,2176]{1,0:T(8,128)(2,1)S(1)}, bf16[32,2176]{1,0:T(8,128)(2,1)S(1)}, u32[]{:S(2)}, u32[]{:S(2)}) collective-permute-start(bf16[32,2176]{1,0:T(8,128)(2,1)S(1)} %finish.1.refs_0_), channel_id=1, source_target_pairs={{0,6},{1,7},{2,4},{3,5},{4,2},{5,3},{6,0},{7,1},{8,14},{9,15},{10,... | collective-permute-start | bytes 417800 | tf_op jit(solution)/shard_map/ppermute | solution.py:425
  68.8 6.8 %collective-permute-start.28 = (bf16[32,2176]{1,0:T(8,128)(2,1)S(1)}, bf16[32,2176]{1,0:T(8,128)(2,1)S(1)}, u32[]{:S(2)}, u32[]{:S(2)}) collective-permute-start(bf16[32,2176]{1,0:T(8,128)(2,1)S(1)} %finish.1.refs_0_), channel_id=1, source_target_pairs={{0,4},{1,5},{2,6},{3,7},{4,0},{5,1},{6,2},{7,3},{8,12},{9,13},{10,... | collective-permute-start | bytes 417800 | tf_op jit(solution)/shard_map/ppermute | solution.py:425
  69.6 6.0 %collective-permute-start.27 = (bf16[32,2176]{1,0:T(8,128)(2,1)S(1)}, bf16[32,2176]{1,0:T(8,128)(2,1)S(1)}, u32[]{:S(2)}, u32[]{:S(2)}) collective-permute-start(bf16[32,2176]{1,0:T(8,128)(2,1)S(1)} %finish.1.refs_0_), channel_id=1, source_target_pairs={{0,2},{1,3},{2,0},{3,1},{4,6},{5,7},{6,4},{7,5},{8,10},{9,11},{10,... | collective-permute-start | bytes 417800 | tf_op jit(solution)/shard_map/ppermute | solution.py:425
  70.6 5.5 %collective-permute-start.30 = (bf16[32,2176]{1,0:T(8,128)(2,1)S(1)}, bf16[32,2176]{1,0:T(8,128)(2,1)S(1)}, u32[]{:S(2)}, u32[]{:S(2)}) collective-permute-start(bf16[32,2176]{1,0:T(8,128)(2,1)S(1)} %finish.1.refs_0_), channel_id=1, source_target_pairs={{0,1},{1,0},{2,3},{3,2},{4,5},{5,4},{6,7},{7,6},{8,9},{9,8},{10,11... | collective-permute-start | bytes 417800 | tf_op jit(solution)/shard_map/ppermute | solution.py:425
  74.5 1.7 %collective-permute-start.33 = (bf16[32,2176]{1,0:T(8,128)(2,1)S(1)}, bf16[32,2176]{1,0:T(8,128)(2,1)S(1)}, u32[]{:S(2)}, u32[]{:S(2)}) collective-permute-start(bf16[32,2176]{1,0:T(8,128)(2,1)S(1)} %collective-permute-done.29.refs_3_), channel_id=1, source_target_pairs={{0,1},{1,0},{2,3},{3,2},{4,5},{5,4},{6,7},{7,6},{8,9},{9,8},{10,11... | collective-permute-start | bytes 417800 | tf_op jit(solution)/shard_map/ppermute | solution.py:425
  75.6 1.6 %collective-permute-start.31 = (bf16[32,2176]{1,0:T(8,128)(2,1)S(1)}, bf16[32,2176]{1,0:T(8,128)(2,1)S(1)}, u32[]{:S(2)}, u32[]{:S(2)}) collective-permute-start(bf16[32,2176]{1,0:T(8,128)(2,1)S(1)} %collective-permute-done.27.refs_1_), channel_id=1, source_target_pairs={{0,1},{1,0},{2,3},{3,2},{4,5},{5,4},{6,7},{7,6},{8,9},{9,8},{10,11... | collective-permute-start | bytes 417800 | tf_op jit(solution)/shard_map/ppermute | solution.py:425
  (8 other events, 41.7 us)

commit v18 on v15

--- a/solution.py
+++ b/solution.py
@@ -393,8 +393,9 @@
         spot = slice(index * block, (index + 1) * block)
         made_in[spot, :] = dot(last_all[:, spot], slope, ((0,), (0,))).astype(bf16)
         send(made_in.at[spot], grad_in.at[0, spot])
-    made_out[...] = dot(hidden, route_grad, ((0,), (0,))).astype(bf16)
-    send(made_out, grad_out.at[0])
+        if index == 0:
+            made_out[...] = dot(hidden, route_grad, ((0,), (0,))).astype(bf16)
+            send(made_out, grad_out.at[0])
     for copy in copies:
         copy.wait()
 

time: 81.3 us -> 81.4 us (level)
  no operation moved by 1% of the time
where the time goes in v18:
time: 81.4 us; the launch traced here: 81.1 us
  starting transfers between devices  36.4 us (45%)
  waiting for transfers between devices  22.1 us (27%)
  Pallas kernels  16.5 us (20%)
  local copies, waits for them, and re-layouts  5.26 us (6%)
  between operations  0.84 us (1%)
    ppermute x28, starting transfers between devices, to_lane(): lax.ppermute(value, 'expert', [(j, j ^ step) for j in range(expert_count)])  26.9 us
    ppermute x28, waiting for transfers between devices, to_lane(): lax.ppermute(value, 'expert', [(j, j ^ step) for j in range(expert_count)])  13.6 us
    ppermute x6, starting transfers between devices, to_plane(): return lax.ppermute(value, 'dp', [(p, p ^ step) for p in range(dp_count)])  9.43 us
    pallas_call x2, Pallas kernels, expert(): pl.pallas_call(functools.partial(expert_kernel, layout), out_shape=out_sh...  9.17 us
    ppermute x6, waiting for transfers between devices, to_plane(): return lax.ppermute(value, 'dp', [(p, p ^ step) for p in range(dp_count)])  8.51 us
    unnamed x12, local copies, waits for them, and re-layouts  4.53 us
    pallas_call x1, Pallas kernels, body(): pl.pallas_call(functools.partial(final_kernel, len(pieces), n_blocks), ou...  4.29 us
    pallas_call x1, Pallas kernels, body(): pl.pallas_call(functools.partial(pack_kernel, seq_dev), out_shape=jax.Sha...  1.66 us
  transfers between devices with their start and end apart: 34, of which 13 were waited for; matrix products, arithmetic and copies ran while one was open for 1% of the time, Pallas kernels for 15%

profile of v18, /device:TPU:0, one launch (start us, length us, event | category | flops | bytes accessed | tf_op | source)
XLA Modules:
  0.0 81.1 jit_solution(6137991943979963044)
XLA Ops:
  1.2 1.7 %pack.1.refs_0_ = bf16[32,2176]{1,0:T(8,128)(2,1)} custom-call(s32[4]{0:T(128)} %partners.1, s32[1,256]{1,0:T(1,128)} %bitcast.2, f32[1,256]{1,0:T(1,128)} %bitcast.3, bf16[256,2048]{1,0:T(8,128)(2,1)} %refs_0_.1), custom_call_target="tpu_custom_call" | custom-call | bytes 524288 | tf_op jit(solution)/shard_map/pack/pallas_call | solution.py:426
  2.9 3.1 %collective-permute-start = (bf16[32,2176]{1,0:T(8,128)(2,1)}, bf16[32,2176]{1,0:T(8,128)(2,1)S(1)}, u32[]{:S(2)}, u32[]{:S(2)}) collective-permute-start(bf16[32,2176]{1,0:T(8,128)(2,1)} %pack.1.refs_0_), channel_id=1, source_target_pairs={{0,8},{8,0},{16,24},{24,16},{1,9},{9,1},{17,25},{25,17},{2,10},{10... | collective-permute-start | bytes 417800 | tf_op jit(solution)/shard_map/ppermute | solution.py:420
  6.0 2.5 %collective-permute-start.2 = (bf16[32,2176]{1,0:T(8,128)(2,1)}, bf16[32,2176]{1,0:T(8,128)(2,1)S(1)}, u32[]{:S(2)}, u32[]{:S(2)}) collective-permute-start(bf16[32,2176]{1,0:T(8,128)(2,1)} %pack.1.refs_0_), channel_id=1, source_target_pairs={{0,24},{8,16},{16,8},{24,0},{1,25},{9,17},{17,9},{25,1},{2,26},{10... | collective-permute-start | bytes 417800 | tf_op jit(solution)/shard_map/ppermute | solution.py:420
  10.2 2.6 %collective-permute-start.7 = (bf16[32,2304]{1,0:T(8,128)(2,1)S(1)}, bf16[32,2304]{1,0:T(8,128)(2,1)S(1)}, u32[]{:S(2)}, u32[]{:S(2)}) collective-permute-start(bf16[32,2304]{1,0:T(8,128)(2,1)S(1)} %pad_maximum_fusion.1), channel_id=1, source_target_pairs={{0,6},{1,7},{2,4},{3,5},{4,2},{5,3},{6,0},{7,1},{8,14},{9,15},{10,... | collective-permute-start | bytes 442376 | tf_op jit(solution)/shard_map/ppermute | solution.py:417
  13.8 2.4 %collective-permute-done.2.refs_6_ = bf16[32,2176]{1,0:T(8,128)(2,1)S(1)} collective-permute-done((bf16[32,2176]{1,0:T(8,128)(2,1)}, bf16[32,2176]{1,0:T(8,128)(2,1)S(1)}, u32[]{:S(2)}, u32[]{:S(2)}) %collective-permute-start.2) | collective-permute-done | bytes 139296 | tf_op jit(solution)/shard_map/ppermute | solution.py:420
  16.2 5.1 %collective-permute-done.1.refs_5_ = bf16[32,2176]{1,0:T(8,128)(2,1)S(1)} collective-permute-done((bf16[32,2176]{1,0:T(8,128)(2,1)}, bf16[32,2176]{1,0:T(8,128)(2,1)S(1)}, u32[]{:S(2)}, u32[]{:S(2)}) %collective-permute-start.1) | collective-permute-done | bytes 139296 | tf_op jit(solution)/shard_map/ppermute | solution.py:420
  21.4 2.5 %collective-permute-start.10 = (bf16[64,2176]{1,0:T(8,128)(2,1)S(1)}, bf16[64,2176]{1,0:T(8,128)(2,1)S(1)}, u32[]{:S(2)}, u32[]{:S(2)}) collective-permute-start(bf16[64,2176]{1,0:T(8,128)(2,1)S(1)} %pad_maximum_fusion), channel_id=1, source_target_pairs={{0,6},{1,7},{2,4},{3,5},{4,2},{5,3},{6,0},{7,1},{8,14},{9,15},{10,... | collective-permute-start | bytes 835592 | tf_op jit(solution)/shard_map/ppermute | solution.py:417
  25.0 1.4 %copy-done = bf16[1,384,2048]{2,1,0:T(8,128)(2,1)S(1)} copy-done((bf16[1,384,2048]{2,1,0:T(8,128)(2,1)S(1)}, bf16[1,384,2048]{2,1,0:T(8,128)(2,1)}, u32[]{:S(2)}) %copy-start) | copy-done | bytes 1572888
  26.4 1.9 %copy-done.2 = bf16[1,2048,768]{2,1,0:T(8,128)(2,1)S(1)} copy-done((bf16[1,2048,768]{2,1,0:T(8,128)(2,1)S(1)}, bf16[1,2048,768]{2,1,0:T(8,128)(2,1)}, u32[]{:S(2)}) %copy-start.2) | copy-done | bytes 3145752
  28.3 1.2 %copy-done.4 = bf16[256,2048]{1,0:T(8,128)(2,1)S(1)} copy-done((bf16[256,2048]{1,0:T(8,128)(2,1)S(1)}, bf16[256,2048]{1,0:T(8,128)(2,1)}, u32[]{:S(2)}) %copy-start.4) | copy-done | bytes 1048600
  29.5 4.5 %experts.2 = (bf16[32,2048]{1,0:T(8,128)(2,1)S(1)}, bf16[32,2048]{1,0:T(8,128)(2,1)S(1)}, bf16[32,2048]{1,0:T(8,128)(2,1)S(1)}, bf16[32,2048]{1,0:T(8,128)(2,1)S...) custom-call(bf16[256,2048]{1,0:T(8,128)(2,1)S(1)} %copy-done.4, ...), custom_call_target="tpu_custom_call" | custom-call | flops 2415919104 | bytes 12582912 | tf_op jit(solution)/shard_map/experts/pallas_call | solution.py:503
  34.0 1.6 %collective-permute-start.11 = (bf16[32,2048]{1,0:T(8,128)(2,1)S(1)}, bf16[32,2048]{1,0:T(8,128)(2,1)S(1)}, u32[]{:S(2)}, u32[]{:S(2)}) collective-permute-start(bf16[32,2048]{1,0:T(8,128)(2,1)S(1)} %get-tuple-element.68), channel_id=1, source_target_pairs={{0,2},{1,3},{2,0},{3,1},{4,6},{5,7},{6,4},{7,5},{8,10},{9,11},{10,... | collective-permute-start | bytes 393224 | tf_op jit(solution)/shard_map/ppermute | solution.py:417
  35.6 1.5 %collective-permute-start.12 = (bf16[32,2048]{1,0:T(8,128)(2,1)S(1)}, bf16[32,2048]{1,0:T(8,128)(2,1)S(1)}, u32[]{:S(2)}, u32[]{:S(2)}) collective-permute-start(bf16[32,2048]{1,0:T(8,128)(2,1)S(1)} %get-tuple-element.69), channel_id=1, source_target_pairs={{0,4},{1,5},{2,6},{3,7},{4,0},{5,1},{6,2},{7,3},{8,12},{9,13},{10,... | collective-permute-start | bytes 393224 | tf_op jit(solution)/shard_map/ppermute | solution.py:417
  37.6 4.7 %experts.3 = (bf16[32,2048]{1,0:T(8,128)(2,1)S(1)}, bf16[32,2048]{1,0:T(8,128)(2,1)S(1)}, bf16[32,2048]{1,0:T(8,128)(2,1)S(1)}, bf16[32,2048]{1,0:T(8,128)(2,1)S...) custom-call(bf16[32,2176]{1,0:T(8,128)(2,1)S(1)} %copy-done.5, ...), custom_call_target="tpu_custom_call" | custom-call | flops 2566914048 | bytes 12582912 | tf_op jit(solution)/shard_map/experts/pallas_call | solution.py:503
  43.0 1.9 %collective-permute-start.14 = (bf16[32,2176]{1,0:T(8,128)(2,1)S(1)}, bf16[32,2176]{1,0:T(8,128)(2,1)S(1)}, u32[]{:S(2)}, u32[]{:S(2)}) collective-permute-start(bf16[32,2176]{1,0:T(8,128)(2,1)S(1)} %get-tuple-element.71), channel_id=1, source_target_pairs={{0,6},{1,7},{2,4},{3,5},{4,2},{5,3},{6,0},{7,1},{8,14},{9,15},{10,... | collective-permute-start | bytes 417800 | tf_op jit(solution)/shard_map/ppermute | solution.py:417
  45.6 0.9 %collective-permute-start.17 = (bf16[32,2176]{1,0:T(8,128)(2,1)S(1)}, bf16[32,2176]{1,0:T(8,128)(2,1)S(1)}, u32[]{:S(2)}, u32[]{:S(2)}) collective-permute-start(bf16[32,2176]{1,0:T(8,128)(2,1)S(1)} %get-tuple-element.79), channel_id=1, source_target_pairs={{0,4},{1,5},{2,6},{3,7},{4,0},{5,1},{6,2},{7,3},{8,12},{9,13},{10,... | collective-permute-start | bytes 417800 | tf_op jit(solution)/shard_map/ppermute | solution.py:417
  47.1 1.0 %collective-permute-start.22 = (bf16[32,2048]{1,0:T(8,128)(2,1)S(1)}, bf16[32,2048]{1,0:T(8,128)(2,1)S(1)}, u32[]{:S(2)}, u32[]{:S(2)}) collective-permute-start(bf16[32,2048]{1,0:T(8,128)(2,1)S(1)} %get-tuple-element.87), channel_id=1, source_target_pairs={{0,2},{1,3},{2,0},{3,1},{4,6},{5,7},{6,4},{7,5},{8,10},{9,11},{10,... | collective-permute-start | bytes 393224 | tf_op jit(solution)/shard_map/ppermute | solution.py:417
  48.3 1.3 %collective-permute-start.23 = (bf16[32,2048]{1,0:T(8,128)(2,1)S(1)}, bf16[32,2048]{1,0:T(8,128)(2,1)S(1)}, u32[]{:S(2)}, u32[]{:S(2)}) collective-permute-start(bf16[32,2048]{1,0:T(8,128)(2,1)S(1)} %get-tuple-element.88), channel_id=1, source_target_pairs={{0,4},{1,5},{2,6},{3,7},{4,0},{5,1},{6,2},{7,3},{8,12},{9,13},{10,... | collective-permute-start | bytes 393224 | tf_op jit(solution)/shard_map/ppermute | solution.py:417
  49.6 1.3 %collective-permute-start.24 = (bf16[32,2048]{1,0:T(8,128)(2,1)S(1)}, bf16[32,2048]{1,0:T(8,128)(2,1)S(1)}, u32[]{:S(2)}, u32[]{:S(2)}) collective-permute-start(bf16[32,2048]{1,0:T(8,128)(2,1)S(1)} %get-tuple-element.89), channel_id=1, source_target_pairs={{0,6},{1,7},{2,4},{3,5},{4,2},{5,3},{6,0},{7,1},{8,14},{9,15},{10,... | collective-permute-start | bytes 393224 | tf_op jit(solution)/shard_map/ppermute | solution.py:417
  51.1 1.2 %collective-permute-start.18 = (bf16[32,2048]{1,0:T(8,128)(2,1)S(1)}, bf16[32,2048]{1,0:T(8,128)(2,1)S(1)}, u32[]{:S(2)}, u32[]{:S(2)}) collective-permute-start(bf16[32,2048]{1,0:T(8,128)(2,1)S(1)} %get-tuple-element.82), channel_id=1, source_target_pairs={{0,2},{1,3},{2,0},{3,1},{4,6},{5,7},{6,4},{7,5},{8,10},{9,11},{10,... | collective-permute-start | bytes 393224 | tf_op jit(solution)/shard_map/ppermute | solution.py:417
  52.3 2.6 %collective-permute-start.21 = (bf16[32,2176]{1,0:T(8,128)(2,1)S(1)}, bf16[32,2176]{1,0:T(8,128)(2,1)S(1)}, u32[]{:S(2)}, u32[]{:S(2)}) collective-permute-start(bf16[32,2176]{1,0:T(8,128)(2,1)S(1)} %get-tuple-element.81), channel_id=1, source_target_pairs={{0,24},{8,16},{16,8},{24,0},{1,25},{9,17},{17,9},{25,1},{2,26},{10... | collective-permute-start | bytes 417800 | tf_op jit(solution)/shard_map/ppermute | solution.py:420
  55.1 1.3 %collective-permute-done.23.refs_3_ = bf16[32,2048]{1,0:T(8,128)(2,1)S(1)} collective-permute-done((bf16[32,2048]{1,0:T(8,128)(2,1)S(1)}, bf16[32,2048]{1,0:T(8,128)(2,1)S(1)}, u32[]{:S(2)}, u32[]{:S(2)}) %collective-permute-start.23) | collective-permute-done | bytes 131104 | tf_op jit(solution)/shard_map/ppermute | solution.py:417
  57.1 1.1 %collective-permute-start.25 = (bf16[32,2176]{1,0:T(8,128)(2,1)S(1)}, bf16[32,2176]{1,0:T(8,128)(2,1)S(1)}, u32[]{:S(2)}, u32[]{:S(2)}) collective-permute-start(bf16[32,2176]{1,0:T(8,128)(2,1)S(1)} %combine.6), channel_id=1, source_target_pairs={{0,16},{8,24},{16,0},{24,8},{1,17},{9,25},{17,1},{25,9},{2,18},{10... | collective-permute-start | bytes 417800 | tf_op jit(solution)/shard_map/ppermute | solution.py:420
  58.3 2.1 %collective-permute-start.19 = (bf16[32,2048]{1,0:T(8,128)(2,1)S(1)}, bf16[32,2048]{1,0:T(8,128)(2,1)S(1)}, u32[]{:S(2)}, u32[]{:S(2)}) collective-permute-start(bf16[32,2048]{1,0:T(8,128)(2,1)S(1)} %get-tuple-element.83), channel_id=1, source_target_pairs={{0,4},{1,5},{2,6},{3,7},{4,0},{5,1},{6,2},{7,3},{8,12},{9,13},{10,... | collective-permute-start | bytes 393224 | tf_op jit(solution)/shard_map/ppermute | solution.py:417
  60.4 1.3 %collective-permute-start.20 = (bf16[32,2048]{1,0:T(8,128)(2,1)S(1)}, bf16[32,2048]{1,0:T(8,128)(2,1)S(1)}, u32[]{:S(2)}, u32[]{:S(2)}) collective-permute-start(bf16[32,2048]{1,0:T(8,128)(2,1)S(1)} %get-tuple-element.84), channel_id=1, source_target_pairs={{0,6},{1,7},{2,4},{3,5},{4,2},{5,3},{6,0},{7,1},{8,14},{9,15},{10,... | collective-permute-start | bytes 393224 | tf_op jit(solution)/shard_map/ppermute | solution.py:417
  61.6 3.1 %collective-permute-done.19.refs_3_ = bf16[32,2048]{1,0:T(8,128)(2,1)S(1)} collective-permute-done((bf16[32,2048]{1,0:T(8,128)(2,1)S(1)}, bf16[32,2048]{1,0:T(8,128)(2,1)S(1)}, u32[]{:S(2)}, u32[]{:S(2)}) %collective-permute-start.19) | collective-permute-done | bytes 131104 | tf_op jit(solution)/shard_map/ppermute | solution.py:417
  64.7 1.5 %collective-permute-done.20.refs_4_ = bf16[32,2048]{1,0:T(8,128)(2,1)S(1)} collective-permute-done((bf16[32,2048]{1,0:T(8,128)(2,1)S(1)}, bf16[32,2048]{1,0:T(8,128)(2,1)S(1)}, u32[]{:S(2)}, u32[]{:S(2)}) %collective-permute-start.20) | collective-permute-done | bytes 131104 | tf_op jit(solution)/shard_map/ppermute | solution.py:417
  66.5 1.5 %collective-permute-start.29 = (bf16[32,2176]{1,0:T(8,128)(2,1)S(1)}, bf16[32,2176]{1,0:T(8,128)(2,1)S(1)}, u32[]{:S(2)}, u32[]{:S(2)}) collective-permute-start(bf16[32,2176]{1,0:T(8,128)(2,1)S(1)} %finish.1.refs_0_), channel_id=1, source_target_pairs={{0,6},{1,7},{2,4},{3,5},{4,2},{5,3},{6,0},{7,1},{8,14},{9,15},{10,... | collective-permute-start | bytes 417800 | tf_op jit(solution)/shard_map/ppermute | solution.py:417
  68.0 1.2 %collective-permute-start.28 = (bf16[32,2176]{1,0:T(8,128)(2,1)S(1)}, bf16[32,2176]{1,0:T(8,128)(2,1)S(1)}, u32[]{:S(2)}, u32[]{:S(2)}) collective-permute-start(bf16[32,2176]{1,0:T(8,128)(2,1)S(1)} %finish.1.refs_0_), channel_id=1, source_target_pairs={{0,4},{1,5},{2,6},{3,7},{4,0},{5,1},{6,2},{7,3},{8,12},{9,13},{10,... | collective-permute-start | bytes 417800 | tf_op jit(solution)/shard_map/ppermute | solution.py:417
  70.1 3.8 %collective-permute-done.29.refs_3_ = bf16[32,2176]{1,0:T(8,128)(2,1)S(1)} collective-permute-done((bf16[32,2176]{1,0:T(8,128)(2,1)S(1)}, bf16[32,2176]{1,0:T(8,128)(2,1)S(1)}, u32[]{:S(2)}, u32[]{:S(2)}) %collective-permute-start.29) | collective-permute-done | bytes 139296 | tf_op jit(solution)/shard_map/ppermute | solution.py:417
  73.9 1.3 %collective-permute-done.28.refs_2_ = bf16[32,2176]{1,0:T(8,128)(2,1)S(1)} collective-permute-done((bf16[32,2176]{1,0:T(8,128)(2,1)S(1)}, bf16[32,2176]{1,0:T(8,128)(2,1)S(1)}, u32[]{:S(2)}, u32[]{:S(2)}) %collective-permute-start.28) | collective-permute-done | bytes 139296 | tf_op jit(solution)/shard_map/ppermute | solution.py:417
  76.8 4.3 %final.1 = (bf16[256,2048]{1,0:T(8,128)(2,1)}, bf16[1,2048,768]{2,1,0:T(8,128)(2,1)}, bf16[1,384,2048]{2,1,0:T(8,128)(2,1)}) custom-call(bf16[32,2176]{1,0:T(8,128)(2,1)S(1)} %finish.1.refs_0_, bf16[32,2176]{1,0:T(8,128)(2,1)S(1)} %collective-permute-done.27.refs_1_, bf16[32,2176]{1,0:T(8,128)(2,1)S(1)} %collective-permute-done.28.refs_2_, ...), custom_call_target="tpu_custom_call" | custom-call | flops 100663296 | bytes 7340032 | tf_op jit(solution)/shard_map/final/pallas_call | solution.py:610
  (61 shorter events, 11.1 us)
Async XLA Ops:
  0.6 9.6 %collective-permute-start.3 = (bf16[1,2048,768]{2,1,0:T(8,128)(2,1)}, bf16[1,2048,768]{2,1,0:T(8,128)(2,1)S(1)}, u32[]{:S(2)}, u32[]{:S(2)}) collective-permute-start(bf16[1,2048,768]{2,1,0:T(8,128)(2,1)} %refs_10_), channel_id=1, source_target_pairs={{0,1},{1,0},{2,3},{3,2},{4,5},{5,4},{6,7},{7,6},{8,9},{9,8},{10,11... | collective-permute-start | bytes 9437192 | tf_op jit(solution)/shard_map/ppermute | solution.py:417
  1.1 9.1 %collective-permute-start.4 = (bf16[1,384,2048]{2,1,0:T(8,128)(2,1)}, bf16[1,384,2048]{2,1,0:T(8,128)(2,1)}, u32[]{:S(2)}, u32[]{:S(2)}) collective-permute-start(bf16[1,384,2048]{2,1,0:T(8,128)(2,1)} %refs_13_.1), channel_id=1, source_target_pairs={{0,1},{1,0},{2,3},{3,2},{4,5},{5,4},{6,7},{7,6},{8,9},{9,8},{10,11... | collective-permute-start | bytes 4718600 | tf_op jit(solution)/shard_map/ppermute | solution.py:417
  2.9 7.3 %collective-permute-start = (bf16[32,2176]{1,0:T(8,128)(2,1)}, bf16[32,2176]{1,0:T(8,128)(2,1)S(1)}, u32[]{:S(2)}, u32[]{:S(2)}) collective-permute-start(bf16[32,2176]{1,0:T(8,128)(2,1)} %pack.1.refs_0_), channel_id=1, source_target_pairs={{0,8},{8,0},{16,24},{24,16},{1,9},{9,1},{17,25},{25,17},{2,10},{10... | collective-permute-start | bytes 417800 | tf_op jit(solution)/shard_map/ppermute | solution.py:420
  6.0 10.3 %collective-permute-start.2 = (bf16[32,2176]{1,0:T(8,128)(2,1)}, bf16[32,2176]{1,0:T(8,128)(2,1)S(1)}, u32[]{:S(2)}, u32[]{:S(2)}) collective-permute-start(bf16[32,2176]{1,0:T(8,128)(2,1)} %pack.1.refs_0_), channel_id=1, source_target_pairs={{0,24},{8,16},{16,8},{24,0},{1,25},{9,17},{17,9},{25,1},{2,26},{10... | collective-permute-start | bytes 417800 | tf_op jit(solution)/shard_map/ppermute | solution.py:420
  8.4 12.9 %collective-permute-start.1 = (bf16[32,2176]{1,0:T(8,128)(2,1)}, bf16[32,2176]{1,0:T(8,128)(2,1)S(1)}, u32[]{:S(2)}, u32[]{:S(2)}) collective-permute-start(bf16[32,2176]{1,0:T(8,128)(2,1)} %pack.1.refs_0_), channel_id=1, source_target_pairs={{0,16},{8,24},{16,0},{24,8},{1,17},{9,25},{17,1},{25,9},{2,18},{10... | collective-permute-start | bytes 417800 | tf_op jit(solution)/shard_map/ppermute | solution.py:420
  10.2 11.2 %collective-permute-start.7 = (bf16[32,2304]{1,0:T(8,128)(2,1)S(1)}, bf16[32,2304]{1,0:T(8,128)(2,1)S(1)}, u32[]{:S(2)}, u32[]{:S(2)}) collective-permute-start(bf16[32,2304]{1,0:T(8,128)(2,1)S(1)} %pad_maximum_fusion.1), channel_id=1, source_target_pairs={{0,6},{1,7},{2,4},{3,5},{4,2},{5,3},{6,0},{7,1},{8,14},{9,15},{10,... | collective-permute-start | bytes 442376 | tf_op jit(solution)/shard_map/ppermute | solution.py:417
  12.8 8.6 %collective-permute-start.6 = (bf16[32,2304]{1,0:T(8,128)(2,1)S(1)}, bf16[32,2304]{1,0:T(8,128)(2,1)S(1)}, u32[]{:S(2)}, u32[]{:S(2)}) collective-permute-start(bf16[32,2304]{1,0:T(8,128)(2,1)S(1)} %pad_maximum_fusion.1), channel_id=1, source_target_pairs={{0,4},{1,5},{2,6},{3,7},{4,0},{5,1},{6,2},{7,3},{8,12},{9,13},{10,... | collective-permute-start | bytes 442376 | tf_op jit(solution)/shard_map/ppermute | solution.py:417
  13.3 8.1 %collective-permute-start.5 = (bf16[32,2304]{1,0:T(8,128)(2,1)S(1)}, bf16[32,2304]{1,0:T(8,128)(2,1)S(1)}, u32[]{:S(2)}, u32[]{:S(2)}) collective-permute-start(bf16[32,2304]{1,0:T(8,128)(2,1)S(1)} %pad_maximum_fusion.1), channel_id=1, source_target_pairs={{0,2},{1,3},{2,0},{3,1},{4,6},{5,7},{6,4},{7,5},{8,10},{9,11},{10,... | collective-permute-start | bytes 442376 | tf_op jit(solution)/shard_map/ppermute | solution.py:417
  21.4 15.7 %collective-permute-start.10 = (bf16[64,2176]{1,0:T(8,128)(2,1)S(1)}, bf16[64,2176]{1,0:T(8,128)(2,1)S(1)}, u32[]{:S(2)}, u32[]{:S(2)}) collective-permute-start(bf16[64,2176]{1,0:T(8,128)(2,1)S(1)} %pad_maximum_fusion), channel_id=1, source_target_pairs={{0,6},{1,7},{2,4},{3,5},{4,2},{5,3},{6,0},{7,1},{8,14},{9,15},{10,... | collective-permute-start | bytes 835592 | tf_op jit(solution)/shard_map/ppermute | solution.py:417
  24.0 13.6 %collective-permute-start.9 = (bf16[64,2176]{1,0:T(8,128)(2,1)S(1)}, bf16[64,2176]{1,0:T(8,128)(2,1)S(1)}, u32[]{:S(2)}, u32[]{:S(2)}) collective-permute-start(bf16[64,2176]{1,0:T(8,128)(2,1)S(1)} %pad_maximum_fusion), channel_id=1, source_target_pairs={{0,4},{1,5},{2,6},{3,7},{4,0},{5,1},{6,2},{7,3},{8,12},{9,13},{10,... | collective-permute-start | bytes 835592 | tf_op jit(solution)/shard_map/ppermute | solution.py:417
  24.5 13.1 %collective-permute-start.8 = (bf16[64,2176]{1,0:T(8,128)(2,1)S(1)}, bf16[64,2176]{1,0:T(8,128)(2,1)S(1)}, u32[]{:S(2)}, u32[]{:S(2)}) collective-permute-start(bf16[64,2176]{1,0:T(8,128)(2,1)S(1)} %pad_maximum_fusion), channel_id=1, source_target_pairs={{0,2},{1,3},{2,0},{3,1},{4,6},{5,7},{6,4},{7,5},{8,10},{9,11},{10,... | collective-permute-start | bytes 835592 | tf_op jit(solution)/shard_map/ppermute | solution.py:417
  34.0 8.3 %collective-permute-start.11 = (bf16[32,2048]{1,0:T(8,128)(2,1)S(1)}, bf16[32,2048]{1,0:T(8,128)(2,1)S(1)}, u32[]{:S(2)}, u32[]{:S(2)}) collective-permute-start(bf16[32,2048]{1,0:T(8,128)(2,1)S(1)} %get-tuple-element.68), channel_id=1, source_target_pairs={{0,2},{1,3},{2,0},{3,1},{4,6},{5,7},{6,4},{7,5},{8,10},{9,11},{10,... | collective-permute-start | bytes 393224 | tf_op jit(solution)/shard_map/ppermute | solution.py:417
  35.6 6.7 %collective-permute-start.12 = (bf16[32,2048]{1,0:T(8,128)(2,1)S(1)}, bf16[32,2048]{1,0:T(8,128)(2,1)S(1)}, u32[]{:S(2)}, u32[]{:S(2)}) collective-permute-start(bf16[32,2048]{1,0:T(8,128)(2,1)S(1)} %get-tuple-element.69), channel_id=1, source_target_pairs={{0,4},{1,5},{2,6},{3,7},{4,0},{5,1},{6,2},{7,3},{8,12},{9,13},{10,... | collective-permute-start | bytes 393224 | tf_op jit(solution)/shard_map/ppermute | solution.py:417
  37.1 5.9 %collective-permute-start.13 = (bf16[32,2048]{1,0:T(8,128)(2,1)S(1)}, bf16[32,2048]{1,0:T(8,128)(2,1)S(1)}, u32[]{:S(2)}, u32[]{:S(2)}) collective-permute-start(bf16[32,2048]{1,0:T(8,128)(2,1)S(1)} %get-tuple-element.70), channel_id=1, source_target_pairs={{0,6},{1,7},{2,4},{3,5},{4,2},{5,3},{6,0},{7,1},{8,14},{9,15},{10,... | collective-permute-start | bytes 393224 | tf_op jit(solution)/shard_map/ppermute | solution.py:417
  43.0 6.6 %collective-permute-start.14 = (bf16[32,2176]{1,0:T(8,128)(2,1)S(1)}, bf16[32,2176]{1,0:T(8,128)(2,1)S(1)}, u32[]{:S(2)}, u32[]{:S(2)}) collective-permute-start(bf16[32,2176]{1,0:T(8,128)(2,1)S(1)} %get-tuple-element.71), channel_id=1, source_target_pairs={{0,6},{1,7},{2,4},{3,5},{4,2},{5,3},{6,0},{7,1},{8,14},{9,15},{10,... | collective-permute-start | bytes 417800 | tf_op jit(solution)/shard_map/ppermute | solution.py:417
  44.9 6.0 %collective-permute-start.16 = (bf16[32,2176]{1,0:T(8,128)(2,1)S(1)}, bf16[32,2176]{1,0:T(8,128)(2,1)S(1)}, u32[]{:S(2)}, u32[]{:S(2)}) collective-permute-start(bf16[32,2176]{1,0:T(8,128)(2,1)S(1)} %get-tuple-element.78), channel_id=1, source_target_pairs={{0,2},{1,3},{2,0},{3,1},{4,6},{5,7},{6,4},{7,5},{8,10},{9,11},{10,... | collective-permute-start | bytes 417800 | tf_op jit(solution)/shard_map/ppermute | solution.py:417
  45.6 5.3 %collective-permute-start.17 = (bf16[32,2176]{1,0:T(8,128)(2,1)S(1)}, bf16[32,2176]{1,0:T(8,128)(2,1)S(1)}, u32[]{:S(2)}, u32[]{:S(2)}) collective-permute-start(bf16[32,2176]{1,0:T(8,128)(2,1)S(1)} %get-tuple-element.79), channel_id=1, source_target_pairs={{0,4},{1,5},{2,6},{3,7},{4,0},{5,1},{6,2},{7,3},{8,12},{9,13},{10,... | collective-permute-start | bytes 417800 | tf_op jit(solution)/shard_map/ppermute | solution.py:417
  47.1 7.9 %collective-permute-start.22 = (bf16[32,2048]{1,0:T(8,128)(2,1)S(1)}, bf16[32,2048]{1,0:T(8,128)(2,1)S(1)}, u32[]{:S(2)}, u32[]{:S(2)}) collective-permute-start(bf16[32,2048]{1,0:T(8,128)(2,1)S(1)} %get-tuple-element.87), channel_id=1, source_target_pairs={{0,2},{1,3},{2,0},{3,1},{4,6},{5,7},{6,4},{7,5},{8,10},{9,11},{10,... | collective-permute-start | bytes 393224 | tf_op jit(solution)/shard_map/ppermute | solution.py:417
  48.3 8.1 %collective-permute-start.23 = (bf16[32,2048]{1,0:T(8,128)(2,1)S(1)}, bf16[32,2048]{1,0:T(8,128)(2,1)S(1)}, u32[]{:S(2)}, u32[]{:S(2)}) collective-permute-start(bf16[32,2048]{1,0:T(8,128)(2,1)S(1)} %get-tuple-element.88), channel_id=1, source_target_pairs={{0,4},{1,5},{2,6},{3,7},{4,0},{5,1},{6,2},{7,3},{8,12},{9,13},{10,... | collective-permute-start | bytes 393224 | tf_op jit(solution)/shard_map/ppermute | solution.py:417
  49.6 7.4 %collective-permute-start.24 = (bf16[32,2048]{1,0:T(8,128)(2,1)S(1)}, bf16[32,2048]{1,0:T(8,128)(2,1)S(1)}, u32[]{:S(2)}, u32[]{:S(2)}) collective-permute-start(bf16[32,2048]{1,0:T(8,128)(2,1)S(1)} %get-tuple-element.89), channel_id=1, source_target_pairs={{0,6},{1,7},{2,4},{3,5},{4,2},{5,3},{6,0},{7,1},{8,14},{9,15},{10,... | collective-permute-start | bytes 393224 | tf_op jit(solution)/shard_map/ppermute | solution.py:417
  51.1 9.3 %collective-permute-start.18 = (bf16[32,2048]{1,0:T(8,128)(2,1)S(1)}, bf16[32,2048]{1,0:T(8,128)(2,1)S(1)}, u32[]{:S(2)}, u32[]{:S(2)}) collective-permute-start(bf16[32,2048]{1,0:T(8,128)(2,1)S(1)} %get-tuple-element.82), channel_id=1, source_target_pairs={{0,2},{1,3},{2,0},{3,1},{4,6},{5,7},{6,4},{7,5},{8,10},{9,11},{10,... | collective-permute-start | bytes 393224 | tf_op jit(solution)/shard_map/ppermute | solution.py:417
  52.3 14.2 %collective-permute-start.21 = (bf16[32,2176]{1,0:T(8,128)(2,1)S(1)}, bf16[32,2176]{1,0:T(8,128)(2,1)S(1)}, u32[]{:S(2)}, u32[]{:S(2)}) collective-permute-start(bf16[32,2176]{1,0:T(8,128)(2,1)S(1)} %get-tuple-element.81), channel_id=1, source_target_pairs={{0,24},{8,16},{16,8},{24,0},{1,25},{9,17},{17,9},{25,1},{2,26},{10... | collective-permute-start | bytes 417800 | tf_op jit(solution)/shard_map/ppermute | solution.py:420
  55.0 11.4 %collective-permute-start.26 = (bf16[32,2176]{1,0:T(8,128)(2,1)S(1)}, bf16[32,2176]{1,0:T(8,128)(2,1)S(1)}, u32[]{:S(2)}, u32[]{:S(2)}) collective-permute-start(bf16[32,2176]{1,0:T(8,128)(2,1)S(1)} %combine.7), channel_id=1, source_target_pairs={{0,8},{8,0},{16,24},{24,16},{1,9},{9,1},{17,25},{25,17},{2,10},{10... | collective-permute-start | bytes 417800 | tf_op jit(solution)/shard_map/ppermute | solution.py:420
  57.1 9.3 %collective-permute-start.25 = (bf16[32,2176]{1,0:T(8,128)(2,1)S(1)}, bf16[32,2176]{1,0:T(8,128)(2,1)S(1)}, u32[]{:S(2)}, u32[]{:S(2)}) collective-permute-start(bf16[32,2176]{1,0:T(8,128)(2,1)S(1)} %combine.6), channel_id=1, source_target_pairs={{0,16},{8,24},{16,0},{24,8},{1,17},{9,25},{17,1},{25,9},{2,18},{10... | collective-permute-start | bytes 417800 | tf_op jit(solution)/shard_map/ppermute | solution.py:420
  58.3 6.4 %collective-permute-start.19 = (bf16[32,2048]{1,0:T(8,128)(2,1)S(1)}, bf16[32,2048]{1,0:T(8,128)(2,1)S(1)}, u32[]{:S(2)}, u32[]{:S(2)}) collective-permute-start(bf16[32,2048]{1,0:T(8,128)(2,1)S(1)} %get-tuple-element.83), channel_id=1, source_target_pairs={{0,4},{1,5},{2,6},{3,7},{4,0},{5,1},{6,2},{7,3},{8,12},{9,13},{10,... | collective-permute-start | bytes 393224 | tf_op jit(solution)/shard_map/ppermute | solution.py:417
  60.4 5.9 %collective-permute-start.20 = (bf16[32,2048]{1,0:T(8,128)(2,1)S(1)}, bf16[32,2048]{1,0:T(8,128)(2,1)S(1)}, u32[]{:S(2)}, u32[]{:S(2)}) collective-permute-start(bf16[32,2048]{1,0:T(8,128)(2,1)S(1)} %get-tuple-element.84), channel_id=1, source_target_pairs={{0,6},{1,7},{2,4},{3,5},{4,2},{5,3},{6,0},{7,1},{8,14},{9,15},{10,... | collective-permute-start | bytes 393224 | tf_op jit(solution)/shard_map/ppermute | solution.py:417
  66.5 7.4 %collective-permute-start.29 = (bf16[32,2176]{1,0:T(8,128)(2,1)S(1)}, bf16[32,2176]{1,0:T(8,128)(2,1)S(1)}, u32[]{:S(2)}, u32[]{:S(2)}) collective-permute-start(bf16[32,2176]{1,0:T(8,128)(2,1)S(1)} %finish.1.refs_0_), channel_id=1, source_target_pairs={{0,6},{1,7},{2,4},{3,5},{4,2},{5,3},{6,0},{7,1},{8,14},{9,15},{10,... | collective-permute-start | bytes 417800 | tf_op jit(solution)/shard_map/ppermute | solution.py:417
  68.0 7.2 %collective-permute-start.28 = (bf16[32,2176]{1,0:T(8,128)(2,1)S(1)}, bf16[32,2176]{1,0:T(8,128)(2,1)S(1)}, u32[]{:S(2)}, u32[]{:S(2)}) collective-permute-start(bf16[32,2176]{1,0:T(8,128)(2,1)S(1)} %finish.1.refs_0_), channel_id=1, source_target_pairs={{0,4},{1,5},{2,6},{3,7},{4,0},{5,1},{6,2},{7,3},{8,12},{9,13},{10,... | collective-permute-start | bytes 417800 | tf_op jit(solution)/shard_map/ppermute | solution.py:417
  69.3 6.0 %collective-permute-start.27 = (bf16[32,2176]{1,0:T(8,128)(2,1)S(1)}, bf16[32,2176]{1,0:T(8,128)(2,1)S(1)}, u32[]{:S(2)}, u32[]{:S(2)}) collective-permute-start(bf16[32,2176]{1,0:T(8,128)(2,1)S(1)} %finish.1.refs_0_), channel_id=1, source_target_pairs={{0,2},{1,3},{2,0},{3,1},{4,6},{5,7},{6,4},{7,5},{8,10},{9,11},{10,... | collective-permute-start | bytes 417800 | tf_op jit(solution)/shard_map/ppermute | solution.py:417
  70.1 5.7 %collective-permute-start.30 = (bf16[32,2176]{1,0:T(8,128)(2,1)S(1)}, bf16[32,2176]{1,0:T(8,128)(2,1)S(1)}, u32[]{:S(2)}, u32[]{:S(2)}) collective-permute-start(bf16[32,2176]{1,0:T(8,128)(2,1)S(1)} %finish.1.refs_0_), channel_id=1, source_target_pairs={{0,1},{1,0},{2,3},{3,2},{4,5},{5,4},{6,7},{7,6},{8,9},{9,8},{10,11... | collective-permute-start | bytes 417800 | tf_op jit(solution)/shard_map/ppermute | solution.py:417
  73.9 1.9 %collective-permute-start.33 = (bf16[32,2176]{1,0:T(8,128)(2,1)S(1)}, bf16[32,2176]{1,0:T(8,128)(2,1)S(1)}, u32[]{:S(2)}, u32[]{:S(2)}) collective-permute-start(bf16[32,2176]{1,0:T(8,128)(2,1)S(1)} %collective-permute-done.29.refs_3_), channel_id=1, source_target_pairs={{0,1},{1,0},{2,3},{3,2},{4,5},{5,4},{6,7},{7,6},{8,9},{9,8},{10,11... | collective-permute-start | bytes 417800 | tf_op jit(solution)/shard_map/ppermute | solution.py:417
  75.3 1.6 %collective-permute-start.31 = (bf16[32,2176]{1,0:T(8,128)(2,1)S(1)}, bf16[32,2176]{1,0:T(8,128)(2,1)S(1)}, u32[]{:S(2)}, u32[]{:S(2)}) collective-permute-start(bf16[32,2176]{1,0:T(8,128)(2,1)S(1)} %collective-permute-done.27.refs_1_), channel_id=1, source_target_pairs={{0,1},{1,0},{2,3},{3,2},{4,5},{5,4},{6,7},{7,6},{8,9},{9,8},{10,11... | collective-permute-start | bytes 417800 | tf_op jit(solution)/shard_map/ppermute | solution.py:417
  (8 other events, 39.6 us)
